TPU v7x, 32 devices: a whole 2x2x4 slice. The times are simulated.
32 devices in a mesh: groups: 2 (over y), dom: 4 (over z), sub: 4 (over x, core).
Axes of the slice: x: 2, y: 2, z: 4, core: 2. Of those that a mesh axis runs over, the one named last changes fastest.
Arguments:
- grid_lat: bfloat16 [4096, 512], P(('groups', 'dom'), 'sub'), parts along dimension 0, may hold values from -6 to 6
- mesh_lat: bfloat16 [4096, 512], P(('groups', 'dom'), 'sub'), parts along dimension 0, may hold values from -6 to 6
- grid_send: int32 [4, 4, 64], P('dom'), may hold values from 0 to 511, as said below
- mesh_send: int32 [4, 4, 32], P('dom'), may hold values from 0 to 511, as said below
- enc_edges: int32 [2, 16384], P(None, ('dom', 'sub')), may hold values from 0 to 767, as said below
- enc_geom: float32 [4, 16384], P(None, ('dom', 'sub')), may hold values from -6 to 6
- enc_blocks: int32 [4], P('dom'), may hold values from 16 to 32, as said below
- proc_edges: int32 [2, 32768], P(None, ('dom', 'sub')), may hold values from 0 to 639, as said below
- proc_geom: float32 [4, 32768], P(None, ('dom', 'sub')), may hold values from -6 to 6
- proc_blocks: int32 [4], P('dom'), may hold values from 32 to 64, as said below
- enc_geo: float32 [4, 512], replicated, may hold values from -3 to 3
- proc_geo: float32 [4, 512], replicated, may hold values from -3 to 3
- enc_edge_in: bfloat16 [1536, 512], P('sub'), may hold values from -0.15625 to 0.15625
- enc_edge_out: bfloat16 [512, 512], P('sub'), may hold values from -0.25 to 0.25
- enc_node_in: bfloat16 [1024, 512], P('sub'), may hold values from -0.1875 to 0.1875
- enc_node_out: bfloat16 [512, 512], P('sub'), may hold values from -0.25 to 0.25
- proc_edge_in: bfloat16 [1536, 512], P('sub'), may hold values from -0.15625 to 0.15625
- proc_edge_out: bfloat16 [512, 512], P('sub'), may hold values from -0.25 to 0.25
- proc_node_in: bfloat16 [1024, 512], P('sub'), may hold values from -0.1875 to 0.1875
- proc_node_out: bfloat16 [512, 512], P('sub'), may hold values from -0.25 to 0.25
- enc_edge_gain: float32 [512], replicated, may hold values from 0.25 to 1.75
- enc_node_gain: float32 [512], replicated, may hold values from 0.25 to 1.75
- proc_edge_gain: float32 [512], replicated, may hold values from 0.25 to 1.75
- proc_node_gain: float32 [512], replicated, may hold values from 0.25 to 1.75
Outputs:
- mesh_out: bfloat16 [4096, 512], P(('groups', 'dom', 'sub')), parts along dimension 0
There are 2 independent parts, one for each index of `groups`. A program takes and returns all parts, laid end to end along the dimension named above; an argument that names none is the same for every part. Nothing has to cross between parts.
Inputs may be any that keep to these rules, and one draw needn't show every extreme that they name: grid_send[q, r, :] are 64 distinct local grid rows of partition q, the ones partition q + o[r] reads, o = (-2, -1, 1, 2). mesh_send[q, r, :] are 32 distinct local mesh rows of partition q, the ones partition q + o[r] reads. `enc_edges`: row 0 is a sender, a place in its partition's grid_table, never in a list r whose partition p + o[r] lies outside 0 to 3; row 1 is a receiver, a local mesh row of the partition, below 512. `proc_edges`: row 0 is a sender, a place in its partition's mesh_table, never in a list whose partition lies outside 0 to 3; row 1 is a receiver, a local mesh row of the partition. `enc_blocks`: some partition has all 32 blocks live. `proc_blocks`: some partition has all 64 blocks live.
All inputs are finite; a program needn't handle non-finite values.
Results may differ from a plain program's by a relative error of at most 0.0095.
Values may be sent and summed in bfloat16 or wider, within the bound.
No kernel may reach another device: no remote copies, remote signals or barrier semaphores. Data moves between devices by JAX's collectives and lax.ppermute only.
A program may use at most 64 MiB of HBM per device.

v0:
```python
import jax
import jax.numpy as jnp
from jax import lax
from jax.sharding import PartitionSpec as P

BLOCK = 128


OFFSETS = (-2, -1, 1, 2)


def passed_along(value, axis, steps):
    count = lax.axis_size(axis)
    first, last = (max(0, -steps), min(count, count - steps))
    return lax.ppermute(value, axis, [(source, source + steps) for source in range(first, last)])


def layer_norm(values, scales):
    average = jnp.mean(values, axis=-1, keepdims=True)
    centered = values - average
    spread = jnp.mean(centered * centered, axis=-1, keepdims=True)
    return centered / jnp.sqrt(spread + 1e-05) * scales


def near_rows(outgoing, family):
    incoming = [None, None, None, None]
    for region in range(4):
        if family == "grid":
            arrived = passed_along(outgoing[region], "dom", OFFSETS[region])
        else:
            arrived = passed_along(outgoing[region], "dom", OFFSETS[region])
        incoming[3 - region] = arrived
    return jnp.concatenate(incoming, axis=0)


def edge_pass(
    edge_lists,
    geometry,
    live_blocks,
    source_rows,
    target_rows,
    geo_weight,
    weights_in,
    weights_out,
    edge_gain,
):
    feature_count = target_rows.shape[1]
    local_edges = edge_lists.shape[1]
    local_blocks = local_edges // BLOCK
    step_edges = 4 * BLOCK
    step_total = local_edges // step_edges
    quarter = lax.axis_index("sub")
    live_edges = jnp.clip(live_blocks[0] - quarter * local_blocks, 0, local_blocks) * BLOCK
    embed_part = weights_in[:feature_count]
    source_part = weights_in[feature_count : 2 * feature_count]
    target_part = weights_in[2 * feature_count :]

    def advance(counter, totals):
        first_edge = counter * step_edges
        edges_here = lax.dynamic_slice_in_dim(edge_lists, first_edge, step_edges, 1)
        geometry_here = lax.dynamic_slice_in_dim(geometry, first_edge, step_edges, 1)
        senders = edges_here[0]
        receivers = edges_here[1]
        embedded = jax.nn.silu(
            jnp.dot(geometry_here.T, geo_weight, precision=lax.Precision.HIGHEST)
        ).astype(jnp.bfloat16)
        summed = jnp.dot(embedded, embed_part, preferred_element_type=jnp.float32)
        summed = summed + jnp.dot(
            source_rows[senders], source_part, preferred_element_type=jnp.float32
        )
        summed = summed + jnp.dot(
            target_rows[receivers], target_part, preferred_element_type=jnp.float32
        )
        hidden = jax.nn.silu(summed).astype(jnp.bfloat16)
        message = layer_norm(
            jnp.dot(hidden, weights_out, preferred_element_type=jnp.float32), edge_gain
        )
        active = first_edge + jnp.arange(step_edges) < live_edges
        message = jnp.where(active[:, None], message, 0.0)
        return totals.at[receivers].add(message)

    totals = jnp.zeros((target_rows.shape[0], feature_count), jnp.float32)
    totals = lax.fori_loop(0, step_total, advance, totals)
    return totals


def node_pass(latent, shares, weights_in, weights_out, node_gain):
    feature_count = latent.shape[1]
    summed = jnp.dot(latent, weights_in[:feature_count], preferred_element_type=jnp.float32)
    summed = summed + jnp.dot(
        shares.astype(jnp.bfloat16), weights_in[feature_count:], preferred_element_type=jnp.float32
    )
    hidden = jax.nn.silu(summed).astype(jnp.bfloat16)
    update = layer_norm(jnp.dot(hidden, weights_out, preferred_element_type=jnp.float32), node_gain)
    return (latent.astype(jnp.float32) + update).astype(jnp.bfloat16)


def local(
    grid_lat,
    mesh_lat,
    grid_send,
    mesh_send,
    enc_edges,
    enc_geom,
    enc_blocks,
    proc_edges,
    proc_geom,
    proc_blocks,
    enc_geo,
    proc_geo,
    enc_edge_in,
    enc_edge_out,
    enc_node_in,
    enc_node_out,
    proc_edge_in,
    proc_edge_out,
    proc_node_in,
    proc_node_out,
    enc_edge_gain,
    enc_node_gain,
    proc_edge_gain,
    proc_node_gain,
):
    enc_weights = (
        lax.all_gather(enc_edge_in, "sub", axis=0, tiled=True),
        lax.all_gather(enc_edge_out, "sub", axis=0, tiled=True),
        lax.all_gather(enc_node_in, "sub", axis=0, tiled=True),
        lax.all_gather(enc_node_out, "sub", axis=0, tiled=True),
    )
    outgoing = [grid_lat[grid_send[0, region]] for region in range(4)]
    grid_halo = near_rows(outgoing, "grid")
    grid_wide = lax.all_gather(
        jnp.concatenate([grid_lat, grid_halo], axis=0), "sub", axis=1, tiled=True
    )
    mesh_wide = lax.all_gather(mesh_lat, "sub", axis=1, tiled=True)
    totals = edge_pass(
        enc_edges,
        enc_geom,
        enc_blocks,
        grid_wide,
        mesh_wide,
        enc_geo,
        enc_weights[0],
        enc_weights[1],
        enc_edge_gain,
    )
    shares = lax.psum_scatter(totals, "sub", scatter_dimension=0, tiled=True)
    quarter = lax.axis_index("sub")
    own_rows = lax.dynamic_slice_in_dim(mesh_wide, quarter * shares.shape[0], shares.shape[0], 0)
    middle = node_pass(own_rows, shares, enc_weights[2], enc_weights[3], enc_node_gain)
    proc_weights = (
        lax.all_gather(proc_edge_in, "sub", axis=0, tiled=True),
        lax.all_gather(proc_edge_out, "sub", axis=0, tiled=True),
        lax.all_gather(proc_node_in, "sub", axis=0, tiled=True),
        lax.all_gather(proc_node_out, "sub", axis=0, tiled=True),
    )
    mesh_part = lax.all_gather(middle, "sub", axis=0, tiled=True)
    outgoing = [mesh_part[mesh_send[0, region]] for region in range(4)]
    mesh_halo = near_rows(outgoing, "mesh")
    mesh_ext = jnp.concatenate([mesh_part, mesh_halo], axis=0)
    totals = edge_pass(
        proc_edges,
        proc_geom,
        proc_blocks,
        mesh_ext,
        mesh_part,
        proc_geo,
        proc_weights[0],
        proc_weights[1],
        proc_edge_gain,
    )
    shares = lax.psum_scatter(
        totals.astype(jnp.bfloat16), "sub", scatter_dimension=0, tiled=True
    ).astype(jnp.float32)
    return node_pass(middle, shares, proc_weights[2], proc_weights[3], proc_node_gain)


def solution(mesh):
    placed = (
        P(("groups", "dom"), "sub"),
        P(("groups", "dom"), "sub"),
        P("dom", None, None),
        P("dom", None, None),
        P(None, ("dom", "sub")),
        P(None, ("dom", "sub")),
        P("dom"),
        P(None, ("dom", "sub")),
        P(None, ("dom", "sub")),
        P("dom"),
        P(),
        P(),
        P("sub", None),
        P("sub", None),
        P("sub", None),
        P("sub", None),
        P("sub", None),
        P("sub", None),
        P("sub", None),
        P("sub", None),
        P(),
        P(),
        P(),
        P(),
    )
    return jax.shard_map(
        local,
        mesh=mesh,
        in_specs=placed,
        out_specs=P(("groups", "dom", "sub"), None),
        check_vma=False,
    )
```

profile of v0, /device:TPU:12, one launch (start us, length us, event | category | flops | bytes accessed | tf_op | source)
XLA Modules:
  0.0 266.0 jit_solution(2803873461678441304)
XLA Ops:
  10.4 4.5 %collective-permute-start = (bf16[64,128]{1,0:T(8,128)(2,1)S(1)}, bf16[64,128]{1,0:T(8,128)(2,1)S(1)}, u32[]{:S(2)}, u32[]{:S(2)}) collective-permute-start(bf16[64,128]{1,0:T(8,128)(2,1)S(1)} %gather_fusion.4), channel_id=1, source_target_pairs={{0,8},{4,12},{1,9},{5,13},{2,10},{6,14},{3,11},{7,15},{16,24},{20,... | collective-permute-start | bytes 49160 | tf_op jit(solution)/shard_map/ppermute | solution.py:15
  16.5 1.9 collective-permute-start.1
  19.9 3.9 %collective-permute-start.2 = (bf16[64,128]{1,0:T(8,128)(2,1)S(1)}, bf16[64,128]{1,0:T(8,128)(2,1)S(1)}, u32[]{:S(2)}, u32[]{:S(2)}) collective-permute-start(bf16[64,128]{1,0:T(8,128)(2,1)S(1)} %gather_fusion.6), channel_id=1, source_target_pairs={{4,0},{8,4},{12,8},{5,1},{9,5},{13,9},{6,2},{10,6},{14,10},{7,3},{... | collective-permute-start | bytes 49160 | tf_op jit(solution)/shard_map/ppermute | solution.py:15
  26.8 7.2 %all_gather.33 = bf16[512,512]{1,0:T(8,128)(2,1)S(1)} all-gather(bf16[512,128]{1,0:T(8,128)(2,1)S(1)} %copy-done.5), channel_id=1, replica_groups=mesh['groups'=2,'dom'=4,'sub'=4] {'sub'}, dimensions={1}, use_global_device_ids=true | all-gather | bytes 655360 | tf_op jit(solution)/shard_map/all_gather | solution.py:135
  34.0 7.7 %all_gather.37 = bf16[512,512]{1,0:T(8,128)(2,1)} all-gather(bf16[128,512]{1,0:T(8,128)(2,1)S(1)} %copy-done.6), channel_id=1, replica_groups=mesh['groups'=2,'dom'=4,'sub'=4] {'sub'}, dimensions={0}, use_global_device_ids=true | all-gather | bytes 655360 | tf_op jit(solution)/shard_map/all_gather | solution.py:126
  42.5 9.2 %all_gather.36 = bf16[768,512]{1,0:T(8,128)(2,1)S(1)} all-gather(bf16[768,128]{1,0:T(8,128)(2,1)S(1)} %constant_dynamic-update-slice_fusion), channel_id=1, replica_groups=mesh['groups'=2,'dom'=4,'sub'=4] {'sub'}, dimensions={1}, use_global_device_ids=true | all-gather | bytes 983040 | tf_op jit(solution)/shard_map/all_gather | solution.py:132
  51.7 2.6 fusion.45
  54.4 41.4 %while.26 = (s32[]{:T(128)}, f32[512,512]{1,0:T(8,128)S(1)}, s32[2,1024]{1,0:T(2,128)S(1)}, s32[]{:T(128)}, f32[4,1024]{1,0:T(4,128)}, /*index=5*/f32[4,512]{1,0...) while((s32[]{:T(128)}, f32[512,512]{1,0:T(8,128)S(1)}, ...), condition=%wide.region_4.5_spmd, body=%wide.region_0.4_spmd.sunk | while | flops 1091836416 | bytes 22084880 | solution.py:83
  54.4 2.0 multiply_convert_fusion.8
  56.9 2.6 gather_fusion
  59.5 2.6 convolution_add_fusion.8
  62.2 2.6 gather_fusion.1
  64.8 2.7 %fusion.108 = (f32[512]{0:T(512)S(1)}, f32[512,512]{0,1:T(8,128)S(1)}) fusion(bf16[512,512]{1,0:T(8,128)(2,1)} %get-tuple-element.734, f32[512,512]{1,0:T(8,128)} %convolution_add_fusion.8, bf16[512,512]{1,0:T(8,128)(2,1)} %gather_fusion.1, bf16[512,512]{1,0:T(8,128)(2,1)} %get-tuple-element.733), kind=kOutput, calls=%fused_computation.115.clone.1 | convolution fusion | flops 538705408 | bytes 3672064 | tf_op jit(solution)/shard_map/while/body/eval_jaxpr/dot_general | solution.py:76
  67.7 1.8 multiply_select_fusion.4
  69.5 1.6 copy.29
  71.1 4.0 %scatter_fusion = f32[512,512]{1,0:T(8,128)S(1)} fusion(f32[512,512]{1,0:T(8,128)S(1)} %get-tuple-element.706, s32[512]{0:T(512)S(1)} %bitcast.121, f32[512,512]{1,0:T(8,128)S(1)} %copy.29), kind=kCustom, calls=%fused_computation.12.clone.1 | custom fusion | flops 262144 | bytes 3147776 | tf_op jit(solution)/shard_map/while/body/eval_jaxpr/scatter-add | solution.py:80
  75.1 1.9 multiply_convert_fusion.8
  77.6 2.6 gather_fusion
  80.2 2.6 convolution_add_fusion.8
  82.9 2.6 gather_fusion.1
  85.5 2.7 %fusion.108 = (f32[512]{0:T(512)S(1)}, f32[512,512]{0,1:T(8,128)S(1)}) fusion(bf16[512,512]{1,0:T(8,128)(2,1)} %get-tuple-element.734, f32[512,512]{1,0:T(8,128)} %convolution_add_fusion.8, bf16[512,512]{1,0:T(8,128)(2,1)} %gather_fusion.1, bf16[512,512]{1,0:T(8,128)(2,1)} %get-tuple-element.733), kind=kOutput, calls=%fused_computation.115.clone.1 | convolution fusion | flops 538705408 | bytes 3672064 | tf_op jit(solution)/shard_map/while/body/eval_jaxpr/dot_general | solution.py:76
  88.4 1.8 multiply_select_fusion.4
  90.2 1.6 copy.29
  91.8 4.0 %scatter_fusion = f32[512,512]{1,0:T(8,128)S(1)} fusion(f32[512,512]{1,0:T(8,128)S(1)} %get-tuple-element.706, s32[512]{0:T(512)S(1)} %bitcast.121, f32[512,512]{1,0:T(8,128)S(1)} %copy.29), kind=kCustom, calls=%fused_computation.12.clone.1 | custom fusion | flops 262144 | bytes 3147776 | tf_op jit(solution)/shard_map/while/body/eval_jaxpr/scatter-add | solution.py:80
  97.4 7.3 %all_gather.38 = bf16[512,512]{1,0:T(8,128)(2,1)S(1)} all-gather(bf16[128,512]{1,0:T(8,128)(2,1)S(1)} %copy-done.7), channel_id=1, replica_groups=mesh['groups'=2,'dom'=4,'sub'=4] {'sub'}, dimensions={0}, use_global_device_ids=true | all-gather | bytes 655360 | tf_op jit(solution)/shard_map/all_gather | solution.py:128
  105.5 7.7 %all_gather.42 = bf16[512,512]{1,0:T(8,128)(2,1)} all-gather(bf16[128,512]{1,0:T(8,128)(2,1)S(1)} %copy-done.8), channel_id=1, replica_groups=mesh['groups'=2,'dom'=4,'sub'=4] {'sub'}, dimensions={0}, use_global_device_ids=true | all-gather | bytes 655360 | tf_op jit(solution)/shard_map/all_gather | solution.py:153
  114.5 2.8 %fusion.44 = (bf16[512,512]{1,0:T(8,128)(2,1)}, bf16[512,512]{1,0:T(8,128)(2,1)}, bf16[512,512]{1,0:T(8,128)(2,1)}) fusion(bf16[1536,512]{1,0:T(8,128)(2,1)} %all-gather.11.cloned.1.call-done), kind=kLoop, calls=%fused_computation.117 | loop fusion | bytes 3145728 | tf_op jit(solution)/shard_map/slice | solution.py:56
  117.3 6.8 %reduce-scatter.3.cloned.1.call-done = f32[128,512]{1,0:T(8,128)} async-done(((f32[512,512]{1,0:T(8,128)}), f32[128,512]{1,0:T(8,128)}) %reduce-scatter.3.cloned.1.call-update) | async-done | bytes 262160 | tf_op jit(solution)/shard_map/reduce_scatter | solution.py:147
  125.9 6.8 %all_gather.41 = bf16[512,512]{1,0:T(8,128)(2,1)S(1)} all-gather(bf16[128,512]{1,0:T(8,128)(2,1)S(1)} %add_convert_fusion.1), channel_id=1, replica_groups=mesh['groups'=2,'dom'=4,'sub'=4] {'sub'}, dimensions={0}, use_global_device_ids=true | all-gather | bytes 655360 | tf_op jit(solution)/shard_map/all_gather | solution.py:157
  133.3 4.4 %collective-permute-start.4 = (bf16[32,512]{1,0:T(8,128)(2,1)S(1)}, bf16[32,512]{1,0:T(8,128)(2,1)S(1)}, u32[]{:S(2)}, u32[]{:S(2)}) collective-permute-start(bf16[32,512]{1,0:T(8,128)(2,1)S(1)} %gather_fusion.8), channel_id=1, source_target_pairs={{0,8},{4,12},{1,9},{5,13},{2,10},{6,14},{3,11},{7,15},{16,24},{20,... | collective-permute-start | bytes 98312 | tf_op jit(solution)/shard_map/ppermute | solution.py:15
  138.4 1.9 collective-permute-start.5
  140.9 3.9 %collective-permute-start.6 = (bf16[32,512]{1,0:T(8,128)(2,1)S(1)}, bf16[32,512]{1,0:T(8,128)(2,1)S(1)}, u32[]{:S(2)}, u32[]{:S(2)}) collective-permute-start(bf16[32,512]{1,0:T(8,128)(2,1)S(1)} %gather_fusion.10), channel_id=1, source_target_pairs={{4,0},{8,4},{12,8},{5,1},{9,5},{13,9},{6,2},{10,6},{14,10},{7,3},{... | collective-permute-start | bytes 98312 | tf_op jit(solution)/shard_map/ppermute | solution.py:15
  147.0 5.2 %collective-permute-done.7 = bf16[32,512]{1,0:T(8,128)(2,1)S(1)} collective-permute-done((bf16[32,512]{1,0:T(8,128)(2,1)S(1)}, bf16[32,512]{1,0:T(8,128)(2,1)S(1)}, u32[]{:S(2)}, u32[]{:S(2)}) %collective-permute-start.7) | collective-permute-done | bytes 32800 | tf_op jit(solution)/shard_map/ppermute | solution.py:15
  152.3 82.9 %while.27 = (s32[]{:T(128)}, f32[512,512]{1,0:T(8,128)S(1)}, s32[2,2048]{1,0:T(2,128)}, s32[]{:T(128)}, f32[4,2048]{1,0:T(4,128)}, /*index=5*/f32[4,512]{1,0:T(4...) while((s32[]{:T(128)}, f32[512,512]{1,0:T(8,128)S(1)}, ...), condition=%wide.region_12.13_spmd, body=%wide.region_8.12_spmd.sunk | while | flops 1091836416 | bytes 22084880 | solution.py:83
  152.4 1.9 multiply_convert_fusion.9
  155.6 2.6 gather_fusion.2
  158.2 2.6 convolution_add_fusion.9
  160.8 2.6 gather_fusion.3
  163.5 2.7 %fusion.119 = (f32[512]{0:T(512)S(1)}, f32[512,512]{0,1:T(8,128)S(1)}) fusion(bf16[512,512]{1,0:T(8,128)(2,1)} %get-tuple-element.788, f32[512,512]{1,0:T(8,128)} %convolution_add_fusion.9, bf16[512,512]{1,0:T(8,128)(2,1)} %gather_fusion.3, bf16[512,512]{1,0:T(8,128)(2,1)} %get-tuple-element.787), kind=kOutput, calls=%fused_computation.116.clone.1 | convolution fusion | flops 538705408 | bytes 3672064 | tf_op jit(solution)/shard_map/while/body/eval_jaxpr/dot_general | solution.py:76
  167.5 1.6 copy.30
  169.1 4.0 %scatter_fusion.1 = f32[512,512]{1,0:T(8,128)S(1)} fusion(f32[512,512]{1,0:T(8,128)S(1)} %get-tuple-element.760, s32[512]{0:T(512)S(1)} %bitcast.123, f32[512,512]{1,0:T(8,128)S(1)} %copy.30), kind=kCustom, calls=%fused_computation.13.clone.1 | custom fusion | flops 262144 | bytes 3147776 | tf_op jit(solution)/shard_map/while/body/eval_jaxpr/scatter-add | solution.py:80
  173.1 1.9 multiply_convert_fusion.9
  176.3 2.6 gather_fusion.2
  179.0 2.6 convolution_add_fusion.9
  181.6 2.6 gather_fusion.3
  184.2 2.7 %fusion.119 = (f32[512]{0:T(512)S(1)}, f32[512,512]{0,1:T(8,128)S(1)}) fusion(bf16[512,512]{1,0:T(8,128)(2,1)} %get-tuple-element.788, f32[512,512]{1,0:T(8,128)} %convolution_add_fusion.9, bf16[512,512]{1,0:T(8,128)(2,1)} %gather_fusion.3, bf16[512,512]{1,0:T(8,128)(2,1)} %get-tuple-element.787), kind=kOutput, calls=%fused_computation.116.clone.1 | convolution fusion | flops 538705408 | bytes 3672064 | tf_op jit(solution)/shard_map/while/body/eval_jaxpr/dot_general | solution.py:76
  188.2 1.6 copy.30
  189.8 4.0 %scatter_fusion.1 = f32[512,512]{1,0:T(8,128)S(1)} fusion(f32[512,512]{1,0:T(8,128)S(1)} %get-tuple-element.760, s32[512]{0:T(512)S(1)} %bitcast.123, f32[512,512]{1,0:T(8,128)S(1)} %copy.30), kind=kCustom, calls=%fused_computation.13.clone.1 | custom fusion | flops 262144 | bytes 3147776 | tf_op jit(solution)/shard_map/while/body/eval_jaxpr/scatter-add | solution.py:80
  193.8 1.9 multiply_convert_fusion.9
  197.1 2.6 gather_fusion.2
  199.7 2.6 convolution_add_fusion.9
  202.3 2.6 gather_fusion.3
  204.9 2.7 %fusion.119 = (f32[512]{0:T(512)S(1)}, f32[512,512]{0,1:T(8,128)S(1)}) fusion(bf16[512,512]{1,0:T(8,128)(2,1)} %get-tuple-element.788, f32[512,512]{1,0:T(8,128)} %convolution_add_fusion.9, bf16[512,512]{1,0:T(8,128)(2,1)} %gather_fusion.3, bf16[512,512]{1,0:T(8,128)(2,1)} %get-tuple-element.787), kind=kOutput, calls=%fused_computation.116.clone.1 | convolution fusion | flops 538705408 | bytes 3672064 | tf_op jit(solution)/shard_map/while/body/eval_jaxpr/dot_general | solution.py:76
  209.0 1.6 copy.30
  210.5 4.0 %scatter_fusion.1 = f32[512,512]{1,0:T(8,128)S(1)} fusion(f32[512,512]{1,0:T(8,128)S(1)} %get-tuple-element.760, s32[512]{0:T(512)S(1)} %bitcast.123, f32[512,512]{1,0:T(8,128)S(1)} %copy.30), kind=kCustom, calls=%fused_computation.13.clone.1 | custom fusion | flops 262144 | bytes 3147776 | tf_op jit(solution)/shard_map/while/body/eval_jaxpr/scatter-add | solution.py:80
  214.6 1.9 multiply_convert_fusion.9
  217.8 2.6 gather_fusion.2
  220.4 2.6 convolution_add_fusion.9
  223.0 2.6 gather_fusion.3
  225.7 2.7 %fusion.119 = (f32[512]{0:T(512)S(1)}, f32[512,512]{0,1:T(8,128)S(1)}) fusion(bf16[512,512]{1,0:T(8,128)(2,1)} %get-tuple-element.788, f32[512,512]{1,0:T(8,128)} %convolution_add_fusion.9, bf16[512,512]{1,0:T(8,128)(2,1)} %gather_fusion.3, bf16[512,512]{1,0:T(8,128)(2,1)} %get-tuple-element.787), kind=kOutput, calls=%fused_computation.116.clone.1 | convolution fusion | flops 538705408 | bytes 3672064 | tf_op jit(solution)/shard_map/while/body/eval_jaxpr/dot_general | solution.py:76
  231.2 4.0 %scatter_fusion.1 = f32[512,512]{1,0:T(8,128)S(1)} fusion(f32[512,512]{1,0:T(8,128)S(1)} %get-tuple-element.760, s32[512]{0:T(512)S(1)} %bitcast.123, f32[512,512]{1,0:T(8,128)S(1)} %copy.30), kind=kCustom, calls=%fused_computation.13.clone.1 | custom fusion | flops 262144 | bytes 3147776 | tf_op jit(solution)/shard_map/while/body/eval_jaxpr/scatter-add | solution.py:80
  236.2 6.6 %all_gather.43 = bf16[512,512]{1,0:T(8,128)(2,1)S(1)} all-gather(bf16[128,512]{1,0:T(8,128)(2,1)S(1)} %copy-done.9), channel_id=1, replica_groups=mesh['groups'=2,'dom'=4,'sub'=4] {'sub'}, dimensions={0}, use_global_device_ids=true | all-gather | bytes 655360 | tf_op jit(solution)/shard_map/all_gather | solution.py:155
  244.1 12.4 %reduce-scatter.5.cloned.1.call-done = bf16[128,512]{1,0:T(8,128)(2,1)} async-done(((bf16[512,512]{1,0:T(8,128)(2,1)}), bf16[128,512]{1,0:T(8,128)(2,1)}) %reduce-scatter.5.cloned.1.call-update) | async-done | bytes 131088 | tf_op jit(solution)/shard_map/reduce_scatter | solution.py:172
  256.5 1.6 fusion.51
  (160 shorter events, 35.6 us)
Async XLA Ops:
  6.5 35.2 %copy-start.3 = (bf16[512,128]{1,0:T(8,128)(2,1)S(1)}, bf16[512,128]{1,0:T(8,128)(2,1)}, u32[]{:S(2)}) copy-start(bf16[512,128]{1,0:T(8,128)(2,1)} %param.28) | copy-start | bytes 393220
  6.5 20.2 %copy-start.5 = (bf16[512,128]{1,0:T(8,128)(2,1)S(1)}, bf16[512,128]{1,0:T(8,128)(2,1)}, u32[]{:S(2)}) copy-start(bf16[512,128]{1,0:T(8,128)(2,1)} %param.29) | copy-start | bytes 393220
  6.5 27.4 %copy-start.6 = (bf16[128,512]{1,0:T(8,128)(2,1)S(1)}, bf16[128,512]{1,0:T(8,128)(2,1)}, u32[]{:S(2)}) copy-start(bf16[128,512]{1,0:T(8,128)(2,1)} %param.41) | copy-start | bytes 393220
  6.5 45.1 %all-gather.7.cloned.1.call-start = ((), (), s32[]{:S(2)}) async-start(), calls=%async_computation.3 | async-start | bytes 1966080 | tf_op jit(solution)/shard_map/all_gather | solution.py:125
  7.3 105.9 %all-gather.5.cloned.1.call-start = ((), (), s32[]{:S(2)}) async-start(), calls=%async_computation.2 | async-start | bytes 1310720 | tf_op jit(solution)/shard_map/all_gather | solution.py:127
  8.0 106.5 %all-gather.11.cloned.1.call-start = ((), (), s32[]{:S(2)}) async-start(), calls=%async_computation.6 | async-start | bytes 1966080 | tf_op jit(solution)/shard_map/all_gather | solution.py:152
  10.4 31.9 %collective-permute-start = (bf16[64,128]{1,0:T(8,128)(2,1)S(1)}, bf16[64,128]{1,0:T(8,128)(2,1)S(1)}, u32[]{:S(2)}, u32[]{:S(2)}) collective-permute-start(bf16[64,128]{1,0:T(8,128)(2,1)S(1)} %gather_fusion.4), channel_id=1, source_target_pairs={{0,8},{4,12},{1,9},{5,13},{2,10},{6,14},{3,11},{7,15},{16,24},{20,... | collective-permute-start | bytes 49160 | tf_op jit(solution)/shard_map/ppermute | solution.py:15
  16.5 25.9 %collective-permute-start.1 = (bf16[64,128]{1,0:T(8,128)(2,1)S(1)}, bf16[64,128]{1,0:T(8,128)(2,1)S(1)}, u32[]{:S(2)}, u32[]{:S(2)}) collective-permute-start(bf16[64,128]{1,0:T(8,128)(2,1)S(1)} %gather_fusion.5), channel_id=1, source_target_pairs={{0,4},{4,8},{8,12},{1,5},{5,9},{9,13},{2,6},{6,10},{10,14},{3,7},{... | collective-permute-start | bytes 49160 | tf_op jit(solution)/shard_map/ppermute | solution.py:15
  19.9 22.5 %collective-permute-start.2 = (bf16[64,128]{1,0:T(8,128)(2,1)S(1)}, bf16[64,128]{1,0:T(8,128)(2,1)S(1)}, u32[]{:S(2)}, u32[]{:S(2)}) collective-permute-start(bf16[64,128]{1,0:T(8,128)(2,1)S(1)} %gather_fusion.6), channel_id=1, source_target_pairs={{4,0},{8,4},{12,8},{5,1},{9,5},{13,9},{6,2},{10,6},{14,10},{7,3},{... | collective-permute-start | bytes 49160 | tf_op jit(solution)/shard_map/ppermute | solution.py:15
  25.4 17.1 %collective-permute-start.3 = (bf16[64,128]{1,0:T(8,128)(2,1)S(1)}, bf16[64,128]{1,0:T(8,128)(2,1)S(1)}, u32[]{:S(2)}, u32[]{:S(2)}) collective-permute-start(bf16[64,128]{1,0:T(8,128)(2,1)S(1)} %gather_fusion.7), channel_id=1, source_target_pairs={{8,0},{12,4},{9,1},{13,5},{10,2},{14,6},{11,3},{15,7},{24,16},{28,... | collective-permute-start | bytes 49160 | tf_op jit(solution)/shard_map/ppermute | solution.py:15
  26.7 97.4 %reduce-scatter.3.cloned.1.call-start = ((), (), s32[]{:S(2)}) async-start(), calls=%async_computation.4 | async-start | bytes 1310720 | tf_op jit(solution)/shard_map/reduce_scatter | solution.py:147
  51.7 2.7 %copy-start.10 = (s32[2,1024]{1,0:T(2,128)S(1)}, s32[2,1024]{1,0:T(2,128)}, u32[]{:S(2)}) copy-start(s32[2,1024]{1,0:T(2,128)} %param.32) | copy-start | bytes 24580
  54.4 43.1 %copy-start.7 = (bf16[128,512]{1,0:T(8,128)(2,1)S(1)}, bf16[128,512]{1,0:T(8,128)(2,1)}, u32[]{:S(2)}) copy-start(bf16[128,512]{1,0:T(8,128)(2,1)} %param.43) | copy-start | bytes 393220
  54.4 2.0 copy-start.2
  75.1 2.0 copy-start.2
  95.8 1.0 copy-start
  95.8 8.9 %copy-start.14 = (s32[1,4,32]{2,1,0:T(4,128)S(1)}, s32[1,4,32]{2,1,0:T(4,128)}, u32[]{:S(2)}) copy-start(s32[1,4,32]{2,1,0:T(4,128)} %param.31) | copy-start | bytes 1540
  95.8 9.6 %copy-start.8 = (bf16[128,512]{1,0:T(8,128)(2,1)S(1)}, bf16[128,512]{1,0:T(8,128)(2,1)}, u32[]{:S(2)}) copy-start(bf16[128,512]{1,0:T(8,128)(2,1)} %param.45) | copy-start | bytes 393220
  96.8 146.0 %all-gather.9.cloned.1.call-start = ((), (), s32[]{:S(2)}) async-start(), calls=%async_computation.5 | async-start | bytes 1310720 | tf_op jit(solution)/shard_map/all_gather | solution.py:154
  97.4 159.1 %reduce-scatter.5.cloned.1.call-start = ((), (), s32[]{:S(2)}) async-start(), calls=%async_computation.7 | async-start | bytes 655360 | tf_op jit(solution)/shard_map/reduce_scatter | solution.py:172
  114.5 9.6 %copy-start.4 = (bf16[1024,512]{1,0:T(8,128)(2,1)S(1)}, bf16[1024,512]{1,0:T(8,128)(2,1)}, u32[]{:S(2)}) copy-start(bf16[1024,512]{1,0:T(8,128)(2,1)} %all-gather.5.cloned.1.call-done) | copy-start | bytes 3145732
  117.3 8.5 %copy-start.12 = (f32[512]{0:T(512)S(1)}, f32[512]{0:T(512)}, u32[]{:S(2)}) copy-start(f32[512]{0:T(512)} %param.49) | copy-start | bytes 6148
  133.3 19.0 %copy-start.11 = (f32[512]{0:T(512)S(1)}, f32[512]{0:T(512)}, u32[]{:S(2)}) copy-start(f32[512]{0:T(512)} %param.50) | copy-start | bytes 6148
  133.3 19.0 %copy-start.15 = (f32[4,512]{1,0:T(4,128)S(1)}, f32[4,512]{1,0:T(4,128)}, u32[]{:S(2)}) copy-start(f32[4,512]{1,0:T(4,128)} %param.39) | copy-start | bytes 24580
  133.3 13.6 %collective-permute-start.4 = (bf16[32,512]{1,0:T(8,128)(2,1)S(1)}, bf16[32,512]{1,0:T(8,128)(2,1)S(1)}, u32[]{:S(2)}, u32[]{:S(2)}) collective-permute-start(bf16[32,512]{1,0:T(8,128)(2,1)S(1)} %gather_fusion.8), channel_id=1, source_target_pairs={{0,8},{4,12},{1,9},{5,13},{2,10},{6,14},{3,11},{7,15},{16,24},{20,... | collective-permute-start | bytes 98312 | tf_op jit(solution)/shard_map/ppermute | solution.py:15
  138.4 8.6 %collective-permute-start.5 = (bf16[32,512]{1,0:T(8,128)(2,1)S(1)}, bf16[32,512]{1,0:T(8,128)(2,1)S(1)}, u32[]{:S(2)}, u32[]{:S(2)}) collective-permute-start(bf16[32,512]{1,0:T(8,128)(2,1)S(1)} %gather_fusion.9), channel_id=1, source_target_pairs={{0,4},{4,8},{8,12},{1,5},{5,9},{9,13},{2,6},{6,10},{10,14},{3,7},{... | collective-permute-start | bytes 98312 | tf_op jit(solution)/shard_map/ppermute | solution.py:15
  140.9 6.1 %collective-permute-start.6 = (bf16[32,512]{1,0:T(8,128)(2,1)S(1)}, bf16[32,512]{1,0:T(8,128)(2,1)S(1)}, u32[]{:S(2)}, u32[]{:S(2)}) collective-permute-start(bf16[32,512]{1,0:T(8,128)(2,1)S(1)} %gather_fusion.10), channel_id=1, source_target_pairs={{4,0},{8,4},{12,8},{5,1},{9,5},{13,9},{6,2},{10,6},{14,10},{7,3},{... | collective-permute-start | bytes 98312 | tf_op jit(solution)/shard_map/ppermute | solution.py:15
  145.5 6.7 %collective-permute-start.7 = (bf16[32,512]{1,0:T(8,128)(2,1)S(1)}, bf16[32,512]{1,0:T(8,128)(2,1)S(1)}, u32[]{:S(2)}, u32[]{:S(2)}) collective-permute-start(bf16[32,512]{1,0:T(8,128)(2,1)S(1)} %gather_fusion.11), channel_id=1, source_target_pairs={{8,0},{12,4},{9,1},{13,5},{10,2},{14,6},{11,3},{15,7},{24,16},{28,... | collective-permute-start | bytes 98312 | tf_op jit(solution)/shard_map/ppermute | solution.py:15
  152.3 1.9 copy-start.1
  173.1 1.9 copy-start.1
  193.8 1.9 copy-start.1
  214.5 1.9 copy-start.1
  235.3 0.9 copy-start.9
  244.1 14.3 %copy-start.13 = (f32[512]{0:T(512)S(1)}, f32[512]{0:T(512)}, u32[]{:S(2)}) copy-start(f32[512]{0:T(512)} %param.51) | copy-start | bytes 6148
Sparse Core Ops, SparseCore 0:
  8.9 20.7 all-gather.6
  31.3 17.2 all-gather.4
  50.1 19.9 all-gather.10
  96.9 27.1 reduce-scatter.2
  125.6 16.7 all-gather.8
  236.3 20.1 reduce-scatter.4
where the time goes:
time: 269 us; the launch traced here: 266 us
  local copies, waits for them, and re-layouts  56.1 us (21%)
  blocking collectives  52.5 us (20%)
  matrix products  51.7 us (19%)
  other arithmetic  40.1 us (15%)
  waiting for transfers between devices  26.4 us (10%)
  starting transfers between devices  23.5 us (9%)
  between operations  15.3 us (6%)
    scatter-add x6, other arithmetic, advance(): return totals.at[receivers].add(message)  24 us
    ppermute x8, starting transfers between devices, passed_along(): lax.ppermute(value, axis, [(source, source + steps) for source in range(f...  23.3 us
    dot_general x6, matrix products, advance(): jnp.dot(hidden, weights_out, preferred_element_type=jnp.float32)  16.1 us
    gather x6, local copies, waits for them, and re-layouts, advance(): source_rows[senders]  15.7 us
    dot_general x6, matrix products, advance(): jnp.dot(source_rows[senders], source_part, preferred_element_type=jnp.flo...  15.7 us
    gather x6, local copies, waits for them, and re-layouts, advance(): target_rows[receivers]  15.7 us
    reduce_scatter x1, waiting for transfers between devices, local(): lax.psum_scatter(totals.astype(jnp.bfloat16), 'sub', scatter_dimension=0,...  12.4 us
    dot_general x6, matrix products, advance(): jnp.dot(geometry_here.T, geo_weight, precision=lax.Precision.HIGHEST)  11.6 us
  transfers between devices with their start and end apart: 14, of which 3 were waited for; matrix products, arithmetic and copies ran while one was open for 54% of the time, Pallas kernels for 0%

commit v1 on v0

v1 whole, which is shorter than its diff:
```python
import functools

import jax
import jax.numpy as jnp
from jax import lax
from jax.experimental import pallas as pl
from jax.experimental.pallas import tpu as pltpu
from jax.sharding import PartitionSpec as P

BLOCK = 128
OFFSETS = (-2, -1, 1, 2)
STEP = 256
VMEM_BYTES = 48 * 1024 * 1024
BF16 = jnp.bfloat16
F32 = jnp.float32


def silu(v):
    h = 0.5 * v
    return h + h * jnp.tanh(h)


def region_of(delta):
    return jnp.where(delta < 0, delta + 2, delta + 1)


def halo_plan(count):
    plan = []
    if count == 4:
        for bit in (1, 2, 3):
            pairs = [(d, d ^ bit) for d in range(4) if abs((d ^ bit) - d) <= 2]
            regions = [(OFFSETS.index((d ^ bit) - d) if abs((d ^ bit) - d) <= 2 else -1) for d in range(4)]
            plan.append((pairs, regions, regions))
    else:
        for region, offset in enumerate(OFFSETS):
            pairs = [(d, d + offset) for d in range(count) if 0 <= d + offset < count]
            plan.append((pairs, region, 3 - region))
    return plan


def by_index(choice, index):
    if isinstance(choice, int):
        return choice
    picked = jnp.int32(choice[0])
    for place in range(1, len(choice)):
        picked = jnp.where(index == place, choice[place], picked)
    return picked


def whole_refs(count):
    return [pl.BlockSpec(memory_space=pltpu.VMEM)] * count


def call(body, outs, args, scratch=(), flops=0, smem=0):
    moved = sum(a.size * a.dtype.itemsize for a in args) + sum(
        o.size * jnp.dtype(o.dtype).itemsize for o in outs
    )
    specs = whole_refs(len(args) - smem) + [pl.BlockSpec(memory_space=pltpu.SMEM)] * smem
    return pl.pallas_call(
        body,
        out_shape=tuple(outs),
        in_specs=specs,
        out_specs=tuple(whole_refs(len(outs))),
        scratch_shapes=list(scratch),
        compiler_params=pltpu.CompilerParams(vmem_limit_bytes=VMEM_BYTES),
        cost_estimate=pl.CostEstimate(flops=int(flops), bytes_accessed=int(moved), transcendentals=0),
    )(*args)


def dot(a, b):
    return jnp.dot(a, b, preferred_element_type=F32)


def dot_first(a, b):
    return lax.dot_general(a, b, (((0,), (0,)), ((), ())), preferred_element_type=F32)


def three_parts(v):
    a = v.astype(BF16)
    rest = v - a.astype(F32)
    b = rest.astype(BF16)
    c = (rest - b.astype(F32)).astype(BF16)
    return a, b, c


def embed_rows(geom, geo):
    a1, a2, a3 = three_parts(geom)
    b1, b2, b3 = three_parts(geo)
    left = jnp.concatenate([a1, a1, a2, a1, a2, a3], axis=0)
    right = jnp.concatenate([b1, b2, b1, b3, b2, b1], axis=0)
    return silu(dot_first(left, right)).astype(BF16)


def embed_kernel(egeom, egeo, pgeom, pgeo, eout, pout):
    for geom, geo, out in ((egeom, egeo, eout), (pgeom, pgeo, pout)):
        for first in range(0, out.shape[0], STEP):
            out[first : first + STEP, :] = embed_rows(geom[:, first : first + STEP], geo[...])


def layer_norm(v):
    width = v.shape[-1]
    centered = v - jnp.sum(v, axis=-1, keepdims=True) * (1.0 / width)
    spread = jnp.sum(centered * centered, axis=-1, keepdims=True) * (1.0 / width)
    return centered * lax.rsqrt(spread + 1e-05)


def pick_rows(table, listed):
    rows = lax.broadcasted_iota(jnp.int32, (table.shape[0], listed.shape[1]), 0)
    return dot_first((rows == listed).astype(F32).astype(BF16), table).astype(BF16)


def place_shards(shards, steps, target, rows, first_row=0):
    quarter = lax.axis_index("sub")
    for shard, step in zip(shards, steps):
        place = pl.multiple_of(lax.bitwise_xor(quarter, step) * rows, rows)
        target[pl.ds(place, rows), :] = shard[first_row : first_row + rows, :]


def pack_kernel(grid, mesh, w_in, w_out, lat, weights):
    n = grid.shape[0]
    lat[:n, :] = grid[...]
    lat[n:, :] = mesh[...]
    k = w_in.shape[0]
    weights[:k, :] = w_in[...]
    weights[k:, :] = w_out[...]


XOR_STEPS = (0, 2, 1, 3)


def spread_kernel(plan, rows, l0, l1, l2, l3, send, full, *outs):
    quarter = lax.axis_index("sub")
    here = lax.axis_index("dom")
    width = l0.shape[1]
    for shard, step in zip((l0, l1, l2, l3), XOR_STEPS):
        place = pl.multiple_of(lax.bitwise_xor(quarter, step) * width, width)
        full[:, pl.ds(place, width)] = shard[...]
    table = full[:rows, :]
    for (pairs, sent, received), out in zip(plan, outs):
        region = jnp.maximum(by_index(sent, here), 0)
        out[...] = pick_rows(table, send[0, pl.ds(region, 1), :])


def halo_targets(plan, slots, node_rows, width):
    here = lax.axis_index("dom")
    lane = lax.broadcasted_iota(jnp.int32, (1, width), 1)
    target = jnp.full((1, width), -1, jnp.int32)
    for place, (pairs, sent, received) in enumerate(plan):
        region = by_index(received, here)
        first = jnp.where(region < 0, -4 * node_rows, node_rows + region * slots)
        inside = (lane >= place * slots) & (lane < (place + 1) * slots)
        target = jnp.where(inside, lane - place * slots + first, target)
    return target


def edge_blocks(edges, live_edges, count, targets, node_rows, out_rows, first_stage, w_out, totals):
    lane = lax.broadcasted_iota(jnp.int32, (1, node_rows), 1)
    row = lax.broadcasted_iota(jnp.int32, (out_rows, 1), 0)
    quarter = lax.axis_index("sub")
    zero = jnp.zeros((6, STEP), jnp.int32)
    total = None
    for block in range(count // STEP):
        first = block * STEP
        pair = edges[:, first : first + STEP]
        upright = jnp.transpose(jnp.concatenate([pair, zero], axis=0).astype(F32)).astype(jnp.int32)
        senders = upright[:, 0:1]
        receivers = upright[:, 1:2]
        summed = first_stage(block, senders, receivers, lane)
        hidden = silu(summed).astype(BF16)
        message = layer_norm(dot(hidden, w_out[...]))
        place = lax.broadcasted_iota(jnp.int32, (STEP, 1), 0) + (first + quarter * count)
        message = jnp.where(place < live_edges, message, 0.0).astype(BF16)
        collect = (row == pair[1:2, :]).astype(F32).astype(BF16)
        part = dot(collect, message)
        if block == 0:
            totals[...] = part
        else:
            totals[...] += part
    return total


def hot(cond):
    return cond.astype(F32).astype(BF16)


def hand_out(totals, gain, keep, give):
    rows = totals.shape[0] // 4
    core = lax.rem(lax.axis_index("sub"), 2)
    for half in range(2):
        for out, which in ((keep, core), (give, 1 - core)):
            place = pl.multiple_of((2 * half + which) * rows, rows)
            out[half * rows : (half + 1) * rows, :] = (totals[pl.ds(place, rows), :] * gain[...]).astype(BF16)


def enc_kernel(plan, slots, node_rows, n_halo, emb, full, edges, gain, w0, w1, w2, w3, *rest):
    halos = rest[:n_halo]
    live, keep, give, w_in, w_out, table, totals = rest[n_halo:]
    d = full.shape[1]
    k = w_in.shape[0] // 4
    shards = (w0, w1, w2, w3)
    place_shards(shards, XOR_STEPS, w_in, k)
    place_shards(shards, XOR_STEPS, w_out, w_out.shape[0] // 4, k)
    mesh_rows = full.shape[0] - node_rows
    table[:node_rows, :] = dot(full[:node_rows, :], w_in[d : 2 * d, :]).astype(BF16)
    table[node_rows : node_rows + mesh_rows, :] = dot(full[node_rows:, :], w_in[2 * d :, :]).astype(BF16)
    base = node_rows + mesh_rows
    got = jnp.concatenate([h[...] for h in halos], axis=0)
    table[base : base + got.shape[0], :] = dot(got, w_in[d : 2 * d, :]).astype(BF16)
    if base + got.shape[0] < table.shape[0]:
        table[base + got.shape[0] :, :] = jnp.zeros((table.shape[0] - base - got.shape[0], d), BF16)
    targets = halo_targets(plan, slots, node_rows, table.shape[0] - base)

    def first_stage(block, senders, receivers, lane):
        chosen = jnp.concatenate(
            [hot(lane == senders), hot(lane == receivers), hot(targets == senders)], axis=1
        )
        return dot(emb[block * STEP : (block + 1) * STEP, :], w_in[:d, :]) + dot(chosen, table[...])

    edge_blocks(
        edges, live[0] * BLOCK, edges.shape[1], targets, node_rows, mesh_rows, first_stage, w_out, totals
    )
    hand_out(totals, gain, keep, give)


def shard_rows(ref, first, rows, place):
    step = ref.shape[0] // 4
    start = (0, 2, 1, 3).index(place) * step + first
    return ref[start : start + rows, :]


def node_kernel(rows_total, first_in, rows_in, rows_out, mesh, mine, theirs, gain, weights, out):
    d = gain.shape[1]
    shares = (mine[...].astype(F32) + theirs[...].astype(F32)).astype(BF16)
    stacked = jnp.concatenate([mesh[...], shares], axis=1)
    w_in = jnp.concatenate([shard_rows(weights, first_in, rows_in, p) for p in range(4)], axis=0)
    w_out = jnp.concatenate([shard_rows(weights, first_in + rows_in, rows_out, p) for p in range(4)], axis=0)
    hidden = silu(dot(stacked, w_in)).astype(BF16)
    update = layer_norm(dot(hidden, w_out)) * gain[...]
    out[...] = (mesh[...].astype(F32) + update).astype(BF16)


def core_rows_kernel(first_row, full, out):
    rows = out.shape[0] // 2
    core = lax.rem(lax.axis_index("sub"), 2)
    for half in range(2):
        place = pl.multiple_of(first_row + (2 * half + core) * rows, rows)
        out[half * rows : (half + 1) * rows, :] = full[pl.ds(place, rows), :]


def middle_kernel(plan, mine, theirs, send, full, *outs):
    rows = mine.shape[0] // 2
    core = lax.rem(lax.axis_index("sub"), 2)
    here = lax.axis_index("dom")
    for half in range(2):
        for part, which in ((mine, core), (theirs, 1 - core)):
            place = pl.multiple_of((2 * half + which) * rows, rows)
            full[pl.ds(place, rows), :] = part[half * rows : (half + 1) * rows, :]
    table = full[...]
    for (pairs, sent, received), out in zip(plan, outs):
        region = jnp.maximum(by_index(sent, here), 0)
        out[...] = pick_rows(table, send[0, pl.ds(region, 1), :])


def proc_first_kernel(emb, full, edges, weights, pre, table):
    d = full.shape[1]
    node_rows = full.shape[0]
    step = weights.shape[0] // 4
    w_in = jnp.concatenate([shard_rows(weights, 0, 3 * d // 4, p) for p in range(4)], axis=0)
    table[:node_rows, :] = dot(full[...], w_in[d : 2 * d, :]).astype(BF16)
    table[node_rows:, :] = dot(full[...], w_in[2 * d :, :]).astype(BF16)
    lane = lax.broadcasted_iota(jnp.int32, (1, node_rows), 1)
    zero = jnp.zeros((6, STEP), jnp.int32)
    for block in range(edges.shape[1] // STEP):
        first = block * STEP
        pair = edges[:, first : first + STEP]
        upright = jnp.transpose(jnp.concatenate([pair, zero], axis=0).astype(F32)).astype(jnp.int32)
        chosen = jnp.concatenate([hot(lane == upright[:, 0:1]), hot(lane == upright[:, 1:2])], axis=1)
        pre[first : first + STEP, :] = dot(emb[first : first + STEP, :], w_in[:d, :]) + dot(chosen, table[...])


def proc_second_kernel(plan, slots, node_rows, n_halo, pre, edges, gain, weights, *rest):
    halos = rest[:n_halo]
    live, keep, give, w_out, table, totals = rest[n_halo:]
    d = pre.shape[1]
    for place in range(4):
        k = 3 * d // 4
        w_out[place * d // 4 : (place + 1) * d // 4, :] = shard_rows(weights, k, d // 4, place)
    w_source = jnp.concatenate([shard_rows(weights, 0, 3 * d // 4, p) for p in range(4)], axis=0)[d : 2 * d, :]
    got = jnp.concatenate([h[...] for h in halos], axis=0)
    table[: got.shape[0], :] = dot(got, w_source).astype(BF16)
    if got.shape[0] < table.shape[0]:
        table[got.shape[0] :, :] = jnp.zeros((table.shape[0] - got.shape[0], d), BF16)
    targets = halo_targets(plan, slots, node_rows, table.shape[0])

    def first_stage(block, senders, receivers, lane):
        return pre[block * STEP : (block + 1) * STEP, :] + dot(hot(targets == senders), table[...])

    edge_blocks(
        edges, live[0] * BLOCK, edges.shape[1], targets, node_rows, node_rows, first_stage, w_out, totals
    )
    hand_out(totals, gain, keep, give)


def fold_kernel(mine, theirs, keep, give):
    rows = mine.shape[0] // 2
    chip = lax.div(lax.axis_index("sub"), 2)
    for out, which in ((keep, chip), (give, 1 - chip)):
        place = pl.multiple_of(which * rows, rows)
        out[...] = (mine[pl.ds(place, rows), :].astype(F32) + theirs[pl.ds(place, rows), :].astype(F32)).astype(BF16)


def add_kernel(mine, theirs, out):
    out[...] = (mine[...].astype(F32) + theirs[...].astype(F32)).astype(BF16)


def out_kernel(first_in, rows_in, rows_out, full, mine, theirs, gain, weights, out):
    rows = mine.shape[0]
    place = pl.multiple_of(lax.axis_index("sub") * rows, rows)
    node_kernel(rows, first_in, rows_in, rows_out, full.at[pl.ds(place, rows), :], mine, theirs, gain, weights, out)


def to_chip(v):
    return lax.ppermute(v, "sub", [(i, i ^ 2) for i in range(4)])


def to_core(v):
    return lax.ppermute(v, "sub", [(i, i ^ 1) for i in range(4)])


def spread(v):
    across = to_chip(v)
    beside = to_core(v)
    return v, across, beside, to_core(across)


def gathered(v):
    pair = lax.all_gather(v, "sub", axis=0, tiled=True, axis_index_groups=[[0, 2], [1, 3]])
    return lax.all_gather(pair, "sub", axis=0, tiled=True, axis_index_groups=[[0, 1], [2, 3]])


def shape(rows, width, dtype=BF16):
    return jax.ShapeDtypeStruct((rows, width), dtype)


def padded(rows):
    return -(-rows // 128) * 128


def local(
    grid_lat,
    mesh_lat,
    grid_send,
    mesh_send,
    enc_edges,
    enc_geom,
    enc_blocks,
    proc_edges,
    proc_geom,
    proc_blocks,
    enc_geo,
    proc_geo,
    enc_edge_in,
    enc_edge_out,
    enc_node_in,
    enc_node_out,
    proc_edge_in,
    proc_edge_out,
    proc_node_in,
    proc_node_out,
    enc_edge_gain,
    enc_node_gain,
    proc_edge_gain,
    proc_node_gain,
):
    plan = halo_plan(lax.axis_size("dom"))
    d = enc_geo.shape[1]
    grid_rows, mesh_rows = grid_lat.shape[0], mesh_lat.shape[0]
    n_enc, n_proc = enc_edges.shape[1], proc_edges.shape[1]
    enc_edge_gain, enc_node_gain, proc_edge_gain, proc_node_gain = (
        g.reshape(1, d) for g in (enc_edge_gain, enc_node_gain, proc_edge_gain, proc_node_gain)
    )
    k_in, k_out = enc_edge_in.shape[0], enc_edge_out.shape[0]

    lat, enc_w = call(
        pack_kernel,
        [shape(grid_rows + mesh_rows, grid_lat.shape[1]), shape(k_in + k_out, d)],
        [grid_lat, mesh_lat, enc_edge_in, enc_edge_out],
    )
    lat_parts = spread(lat)
    enc_w_parts = spread(enc_w)
    enc_node_w = gathered(jnp.concatenate([enc_node_in, enc_node_out], axis=0))
    proc_w = gathered(jnp.concatenate([proc_edge_in, proc_edge_out, proc_node_in, proc_node_out], axis=0))

    enc_emb, proc_emb = call(
        embed_kernel,
        [shape(n_enc, d), shape(n_proc, d)],
        [enc_geom, enc_geo, proc_geom, proc_geo],
        flops=2 * (n_enc + n_proc) * d * 128,
    )
    slots = grid_send.shape[2]
    full, *outgoing = call(
        functools.partial(spread_kernel, plan, grid_rows),
        [shape(grid_rows + mesh_rows, d)] + [shape(slots, d)] * len(plan),
        [*lat_parts, grid_send],
        flops=2 * len(plan) * slots * grid_rows * d,
    )
    halos = [lax.ppermute(v, "dom", entry[0]) for v, entry in zip(outgoing, plan)]
    halo_rows = padded(len(plan) * slots)
    half = mesh_rows // 2
    keep, give = call(
        functools.partial(enc_kernel, plan, slots, grid_rows, len(plan)),
        [shape(half, d), shape(half, d)],
        [enc_emb, full, enc_edges, enc_edge_gain, *enc_w_parts, *halos, enc_blocks],
        scratch=[
            pltpu.VMEM((3 * d, d), BF16),
            pltpu.VMEM((d, d), BF16),
            pltpu.VMEM((grid_rows + mesh_rows + halo_rows, d), BF16),
            pltpu.VMEM((mesh_rows, d), F32),
        ],
        flops=2 * n_enc * d * (3 * d + grid_rows + mesh_rows + halo_rows),
        smem=1,
    )
    (own_mesh,) = call(functools.partial(core_rows_kernel, grid_rows), [shape(half, d)], [full])
    (chip_sum,) = call(add_kernel, [shape(half, d)], [keep, to_core(give)])
    (mid_half,) = call(
        functools.partial(node_kernel, half, 0, enc_node_in.shape[0], enc_node_out.shape[0]),
        [shape(half, d)],
        [own_mesh, chip_sum, to_chip(chip_sum), enc_node_gain, enc_node_w],
        flops=2 * half * d * 3 * d,
    )
    slots = mesh_send.shape[2]
    mid, *outgoing = call(
        functools.partial(middle_kernel, plan),
        [shape(mesh_rows, d)] + [shape(slots, d)] * len(plan),
        [mid_half, to_core(mid_half), mesh_send],
        flops=2 * len(plan) * slots * mesh_rows * d,
    )
    halos = [lax.ppermute(v, "dom", entry[0]) for v, entry in zip(outgoing, plan)]
    halo_rows = padded(len(plan) * slots)
    (pre,) = call(
        proc_first_kernel,
        [shape(n_proc, d, F32)],
        [proc_emb, mid, proc_edges, proc_w],
        scratch=[pltpu.VMEM((2 * mesh_rows, d), BF16)],
        flops=2 * n_proc * d * (d + 2 * mesh_rows),
    )
    keep, give = call(
        functools.partial(proc_second_kernel, plan, slots, mesh_rows, len(plan)),
        [shape(half, d), shape(half, d)],
        [pre, proc_edges, proc_edge_gain, proc_w, *halos, proc_blocks],
        scratch=[
            pltpu.VMEM((d, d), BF16),
            pltpu.VMEM((halo_rows, d), BF16),
            pltpu.VMEM((mesh_rows, d), F32),
        ],
        flops=2 * n_proc * d * (d + mesh_rows + halo_rows),
        smem=1,
    )
    quarter = mesh_rows // 4
    mine, other = call(fold_kernel, [shape(quarter, d)] * 2, [keep, to_core(give)])
    (result,) = call(
        functools.partial(out_kernel, k_in + k_out, proc_node_in.shape[0], proc_node_out.shape[0]),
        [shape(quarter, d)],
        [mid, mine, to_chip(other), proc_node_gain, proc_w],
        flops=2 * quarter * d * 3 * d,
    )
    return result


def solution(mesh):
    placed = (
        P(("groups", "dom"), "sub"),
        P(("groups", "dom"), "sub"),
        P("dom", None, None),
        P("dom", None, None),
        P(None, ("dom", "sub")),
        P(None, ("dom", "sub")),
        P("dom"),
        P(None, ("dom", "sub")),
        P(None, ("dom", "sub")),
        P("dom"),
        P(),
        P(),
        P("sub", None),
        P("sub", None),
        P("sub", None),
        P("sub", None),
        P("sub", None),
        P("sub", None),
        P("sub", None),
        P("sub", None),
        P(),
        P(),
        P(),
        P(),
    )
    return jax.shard_map(
        local,
        mesh=mesh,
        in_specs=placed,
        out_specs=P(("groups", "dom", "sub"), None),
        check_vma=False,
    )
```

time: 269 us -> 131 us (0.49)
  local copies, waits for them, and re-layouts: 56.1 us -> 1.51 us
  matrix products: 51.7 us -> 0 us
  blocking collectives: 52.5 us -> 12.9 us
  other arithmetic: 40.1 us -> 2.27 us
  Pallas kernels: 0 us -> 28.7 us
  waiting for transfers between devices: 26.4 us -> 53.2 us
  starting transfers between devices: 23.5 us -> 17.1 us
    dot_general x28 -> x0, matrix products: 51.7 us -> none  [the longest x6 16.1 us: advance(): jnp.dot(hidden, weights_out, preferred_element_type=jnp.float32)]
    gather x20 -> x0, local copies, waits for them, and re-layouts: 40 us -> none  [the longest x6 15.7 us: advance(): source_rows[senders]]
    all_gather x7 -> x1, blocking collectives: 52.5 us -> 12.9 us  [gathered(): lax.all_gather(v, 'sub', axis=0, tiled=True, axis_index_groups=[[0, 2], [...]
    ppermute x8 -> x17, waiting for transfers between devices: 5.18 us -> 34.5 us  [the longest x4 27.8 us: to_chip(): return lax.ppermute(v, 'sub', [(i, i ^ 2) for i in range(4)])]
    pallas_call x0 -> x12, Pallas kernels: none -> 28.7 us  [call(): pl.pallas_call(body, out_shape=tuple(outs), in_specs=specs, out_specs=tup...]
    scatter-add x6 -> x0, other arithmetic: 24 us -> none  [advance(): return totals.at[receivers].add(message)]
    reduce_scatter x2 -> x0, waiting for transfers between devices: 19.2 us -> none  [the longest x1 12.4 us: local(): lax.psum_scatter(totals.astype(jnp.bfloat16), 'sub', scatter_dimension=0,...]
    all_gather x4 -> x3, waiting for transfers between devices: 0.03 us -> 18.6 us  [the longest x1 18.6 us: gathered(): lax.all_gather(v, 'sub', axis=0, tiled=True, axis_index_groups=[[0, 2], [...]
  transfers between devices with their start and end apart: 14 -> 20, of which waited for: 3 -> 10; matrix products, arithmetic and copies ran while one was open for 54% -> 0% of each run, Pallas kernels for 0% -> 14%
where the time goes in v1:
time: 131 us; the launch traced here: 130 us
  waiting for transfers between devices  53.2 us (41%)
  Pallas kernels  28.7 us (22%)
  starting transfers between devices  17.1 us (13%)
  between operations  14.8 us (11%)
  blocking collectives  12.9 us (10%)
  other arithmetic  2.27 us (2%)
  local copies, waits for them, and re-layouts  1.51 us (1%)
    pallas_call x12, Pallas kernels, call(): pl.pallas_call(body, out_shape=tuple(outs), in_specs=specs, out_specs=tup...  28.7 us
    ppermute x4, waiting for transfers between devices, to_chip(): return lax.ppermute(v, 'sub', [(i, i ^ 2) for i in range(4)])  27.8 us
    all_gather x1, waiting for transfers between devices, gathered(): lax.all_gather(v, 'sub', axis=0, tiled=True, axis_index_groups=[[0, 2], [...  18.6 us
    all_gather x1, blocking collectives, gathered(): lax.all_gather(v, 'sub', axis=0, tiled=True, axis_index_groups=[[0, 2], [...  12.9 us
    ppermute x6, starting transfers between devices, local(): lax.ppermute(v, 'dom', entry[0])  11 us
    ppermute x7, waiting for transfers between devices, to_core(): return lax.ppermute(v, 'sub', [(i, i ^ 1) for i in range(4)])  5.46 us
    ppermute x4, starting transfers between devices, to_chip(): return lax.ppermute(v, 'sub', [(i, i ^ 2) for i in range(4)])  5.22 us
  transfers between devices with their start and end apart: 20, of which 10 were waited for; matrix products, arithmetic and copies ran while one was open for 0% of the time, Pallas kernels for 14%

profile of v1, /device:TPU:12, one launch (start us, length us, event | category | flops | bytes accessed | tf_op | source)
XLA Modules:
  0.0 130.4 jit_solution(2032250095479355204)
XLA Ops:
  6.5 2.2 %pad_maximum_fusion = bf16[896,512]{1,0:T(8,128)(2,1)} fusion(bf16[128,512]{1,0:T(8,128)(2,1)} %param.43, bf16[256,512]{1,0:T(8,128)(2,1)} %param.42, bf16[128,512]{1,0:T(8,128)(2,1)} %param.41, bf16[384,512]{1,0:T(8,128)(2,1)} %param.40), kind=kLoop, calls=%fused_computation | loop fusion | flops 3670016 | bytes 1835008 | tf_op jit(solution)/shard_map/concatenate | solution.py:392
  8.8 0.0 all-gather.6.cloned.1.call-update
  8.8 0.0 all-gather.4.cloned.1.call-start
  8.9 0.0 copy-start.2
  8.9 0.0 copy-start.3
  8.9 0.0 copy-start.4
  8.9 0.0 copy-start.5
  9.0 12.9 %all_gather.12 = bf16[768,512]{1,0:T(8,128)(2,1)} all-gather(bf16[384,512]{1,0:T(8,128)(2,1)S(1)} %pad_maximum_fusion.1), channel_id=1, replica_groups={{0,2},{1,3},{4,6},{5,7},{8,10},{9,11},{12,14},{13,15},{16,18},{17,19},{..., dimensions={0}, use_global_device_ids=true | all-gather | bytes 1179648 | tf_op jit(solution)/shard_map/all_gather | solution.py:337
  21.9 0.0 all-gather.4.cloned.1.call-update
  21.9 0.0 all-gather.8.cloned.1.call-start
  22.0 18.6 %all-gather.6.cloned.1.call-done = bf16[1792,512]{1,0:T(8,128)(2,1)} async-done(((bf16[896,512]{1,0:T(8,128)(2,1)}), bf16[1792,512]{1,0:T(8,128)(2,1)}) %all-gather.6.cloned.1.call-update) | async-done | bytes 1835024 | tf_op jit(solution)/shard_map/all_gather | solution.py:337
  40.5 0.0 all-gather.8.cloned.1.call-update
  40.6 0.0 copy-start.15
  40.6 0.0 copy-start.16
  40.6 0.1 shard_map.226
  40.7 1.6 %collective-permute-start.3 = (bf16[512,512]{1,0:T(8,128)(2,1)S(1)}, bf16[512,512]{1,0:T(8,128)(2,1)S(1)}, u32[]{:S(2)}, u32[]{:S(2)}) collective-permute-start(bf16[512,512]{1,0:T(8,128)(2,1)S(1)} %get-tuple-element.26.w0), channel_id=1, source_target_pairs={{0,2},{1,3},{2,0},{3,1},{4,6},{5,7},{6,4},{7,5},{8,10},{9,11},{10,... | collective-permute-start | bytes 1572872 | tf_op jit(solution)/shard_map/ppermute | solution.py:323
  42.3 0.5 collective-permute-start
  42.8 0.0 collective-permute-start.4
  42.8 12.7 %collective-permute-done.3.w1 = bf16[512,512]{1,0:T(8,128)(2,1)S(1)} collective-permute-done((bf16[512,512]{1,0:T(8,128)(2,1)S(1)}, bf16[512,512]{1,0:T(8,128)(2,1)S(1)}, u32[]{:S(2)}, u32[]{:S(2)}) %collective-permute-start.3) | collective-permute-done | bytes 524320 | tf_op jit(solution)/shard_map/ppermute | solution.py:323
  55.5 0.0 collective-permute-start.5
  55.5 0.5 collective-permute-start.1
  56.0 4.2 %collective-permute-done.l1 = bf16[1024,128]{1,0:T(8,128)(2,1)S(1)} collective-permute-done((bf16[1024,128]{1,0:T(8,128)(2,1)S(1)}, bf16[1024,128]{1,0:T(8,128)(2,1)S(1)}, u32[]{:S(2)}, u32[]{:S(2)}) %collective-permute-start) | collective-permute-done | bytes 262176 | tf_op jit(solution)/shard_map/ppermute | solution.py:323
  60.3 0.0 collective-permute-start.2
  60.3 0.0 collective-permute-done.1.l2
  60.3 1.5 %collective-permute-done.2.l3 = bf16[1024,128]{1,0:T(8,128)(2,1)S(1)} collective-permute-done((bf16[1024,128]{1,0:T(8,128)(2,1)S(1)}, bf16[1024,128]{1,0:T(8,128)(2,1)S(1)}, u32[]{:S(2)}, u32[]{:S(2)}) %collective-permute-start.2) | collective-permute-done | bytes 262176 | tf_op jit(solution)/shard_map/ppermute | solution.py:327
  61.8 0.6 shard_map.227
  62.4 0.5 collective-permute-start.6
  62.9 2.6 %collective-permute-start.7 = (bf16[64,512]{1,0:T(8,128)(2,1)S(1)}, bf16[64,512]{1,0:T(8,128)(2,1)S(1)}, u32[]{:S(2)}, u32[]{:S(2)}) collective-permute-start(bf16[64,512]{1,0:T(8,128)(2,1)S(1)} %get-tuple-element.28), channel_id=1, source_target_pairs={{0,8},{4,12},{8,0},{12,4},{1,9},{5,13},{9,1},{13,5},{2,10},{6,14},... | collective-permute-start | bytes 196616 | tf_op jit(solution)/shard_map/ppermute | solution.py:407
  65.5 2.3 %collective-permute-start.8 = (bf16[64,512]{1,0:T(8,128)(2,1)S(1)}, bf16[64,512]{1,0:T(8,128)(2,1)S(1)}, u32[]{:S(2)}, u32[]{:S(2)}) collective-permute-start(bf16[64,512]{1,0:T(8,128)(2,1)S(1)} %get-tuple-element.29), channel_id=1, source_target_pairs={{4,8},{8,4},{5,9},{9,5},{6,10},{10,6},{7,11},{11,7},{20,24},{24,20... | collective-permute-start | bytes 196616 | tf_op jit(solution)/shard_map/ppermute | solution.py:407
  68.6 1.8 %shard_map.229 = (bf16[1024,512]{1,0:T(8,128)(2,1)S(1)}, bf16[2048,512]{1,0:T(8,128)(2,1)S(1)}) custom-call(f32[4,1024]{1,0:T(4,128)S(1)} %copy-done.11, f32[4,512]{1,0:T(4,128)S(1)} %copy-done.13, f32[4,2048]{1,0:T(4,128)S(1)} %copy-done.10, f32[4,512]{1,0:T(4,128)S(1)} %copy-done.14), custom_call_target="tpu_custom_call" | custom-call | flops 402653184 | bytes 3211264 | tf_op jit(solution)/shard_map/pallas_call | solution.py:59
  70.4 0.0 collective-permute-done.4.w2
  70.4 0.0 collective-permute-done.6.rest_0_
  70.4 0.0 collective-permute-done.7.rest_1_
  70.5 1.2 collective-permute-done.8.rest_2_
  71.7 5.9 %shard_map.230 = (bf16[256,512]{1,0:T(8,128)(2,1)S(1)}, bf16[256,512]{1,0:T(8,128)(2,1)S(1)}) custom-call(bf16[1024,512]{1,0:T(8,128)(2,1)S(1)} %get-tuple-element.25.emb, bf16[1024,512]{1,0:T(8,128)(2,1)S(1)} %get-tuple-element.24.full, s32[2,1024]{1,0:T(2,128)S(1)} %copy-done.15, f32[1,512]{1,0:T(1,128)S(1)} %bitcast.6, ...), custom_call_target="tpu_custom_call" | custom-call | flops 2952790016 | bytes 4925444 | tf_op jit(solution)/shard_map/pallas_call | solution.py:59
  77.6 0.0 copy-start.9
  77.6 0.1 collective-permute-start.9
  77.7 1.5 %collective-permute-done.9.theirs = bf16[256,512]{1,0:T(8,128)(2,1)S(1)} collective-permute-done((bf16[256,512]{1,0:T(8,128)(2,1)S(1)}, bf16[256,512]{1,0:T(8,128)(2,1)S(1)}, u32[]{:S(2)}, u32[]{:S(2)}) %collective-permute-start.9) | collective-permute-done | bytes 262176 | tf_op jit(solution)/shard_map/ppermute | solution.py:327
  79.2 0.1 shard_map.231.mine
  79.3 0.0 copy-start.7
  79.3 1.6 %collective-permute-start.10 = (bf16[256,512]{1,0:T(8,128)(2,1)S(1)}, bf16[256,512]{1,0:T(8,128)(2,1)S(1)}, u32[]{:S(2)}, u32[]{:S(2)}) collective-permute-start(bf16[256,512]{1,0:T(8,128)(2,1)S(1)} %shard_map.231.mine), channel_id=1, source_target_pairs={{0,2},{1,3},{2,0},{3,1},{4,6},{5,7},{6,4},{7,5},{8,10},{9,11},{10,... | collective-permute-start | bytes 786440 | tf_op jit(solution)/shard_map/ppermute | solution.py:323
  80.9 6.8 %collective-permute-done.10.theirs = bf16[256,512]{1,0:T(8,128)(2,1)S(1)} collective-permute-done((bf16[256,512]{1,0:T(8,128)(2,1)S(1)}, bf16[256,512]{1,0:T(8,128)(2,1)S(1)}, u32[]{:S(2)}, u32[]{:S(2)}) %collective-permute-start.10) | collective-permute-done | bytes 262176 | tf_op jit(solution)/shard_map/ppermute | solution.py:323
  87.7 1.4 %copy-done.1 = bf16[1536,512]{1,0:T(8,128)(2,1)S(1)} copy-done((bf16[1536,512]{1,0:T(8,128)(2,1)S(1)}, bf16[1536,512]{1,0:T(8,128)(2,1)}, u32[]{:S(2)}) %copy-start.1) | copy-done | bytes 1572888
  89.1 0.9 shard_map.232.mine
  90.0 0.1 collective-permute-start.11
  90.8 0.9 collective-permute-done.11.theirs
  91.6 0.4 shard_map.233
  92.1 0.0 collective-permute-start.12
  92.1 2.3 %collective-permute-start.13 = (bf16[32,512]{1,0:T(8,128)(2,1)S(1)}, bf16[32,512]{1,0:T(8,128)(2,1)S(1)}, u32[]{:S(2)}, u32[]{:S(2)}) collective-permute-start(bf16[32,512]{1,0:T(8,128)(2,1)S(1)} %get-tuple-element.35), channel_id=1, source_target_pairs={{0,8},{4,12},{8,0},{12,4},{1,9},{5,13},{9,1},{13,5},{2,10},{6,14},... | collective-permute-start | bytes 98312 | tf_op jit(solution)/shard_map/ppermute | solution.py:438
  94.4 3.3 %collective-permute-start.14 = (bf16[32,512]{1,0:T(8,128)(2,1)S(1)}, bf16[32,512]{1,0:T(8,128)(2,1)S(1)}, u32[]{:S(2)}, u32[]{:S(2)}) collective-permute-start(bf16[32,512]{1,0:T(8,128)(2,1)S(1)} %get-tuple-element.36), channel_id=1, source_target_pairs={{4,8},{8,4},{5,9},{9,5},{6,10},{10,6},{7,11},{11,7},{20,24},{24,20... | collective-permute-start | bytes 98312 | tf_op jit(solution)/shard_map/ppermute | solution.py:438
  97.7 0.0 all-gather.8.cloned.1.call-done.weights
  97.7 0.0 copy-start.17
  97.7 8.6 %shard_map.234.pre = f32[2048,512]{1,0:T(8,128)} custom-call(bf16[2048,512]{1,0:T(8,128)(2,1)S(1)} %get-tuple-element.33.emb, bf16[512,512]{1,0:T(8,128)(2,1)S(1)} %get-tuple-element.32.full, s32[2,2048]{1,0:T(2,128)S(1)} %copy-done.12, bf16[3584,512]{1,0:T(8,128)(2,1)} %all-gather.8.cloned.1.call-done.weights), custom_call_target="tpu_custom_call" | custom-call | flops 3221225472 | bytes 10502144 | tf_op jit(solution)/shard_map/pallas_call | solution.py:59
  106.3 0.0 collective-permute-done.12.rest_0_
  106.3 0.0 collective-permute-done.13.rest_1_
  106.3 0.0 collective-permute-done.14.rest_2_
  106.3 0.0 copy-start.8
  106.3 8.9 %shard_map.235 = (bf16[256,512]{1,0:T(8,128)(2,1)S(1)}, bf16[256,512]{1,0:T(8,128)(2,1)S(1)}) custom-call(f32[2048,512]{1,0:T(8,128)} %shard_map.234.pre, s32[2,2048]{1,0:T(2,128)S(1)} %copy-done.12, f32[1,512]{1,0:T(1,128)S(1)} %bitcast.7, bf16[3584,512]{1,0:T(8,128)(2,1)S(1)} %copy-done, bf16[32,512]{1,0:T(8,128)(2,1)S(1)} %collective-permute-done.12.rest_0_, ...), custom_call_target="tpu_custom_call" | custom-call | flops 2415919104 | bytes 8505348 | tf_op jit(solution)/shard_map/pallas_call | solution.py:59
  115.2 0.1 collective-permute-start.15
  115.3 1.5 %collective-permute-done.15.theirs = bf16[256,512]{1,0:T(8,128)(2,1)S(1)} collective-permute-done((bf16[256,512]{1,0:T(8,128)(2,1)S(1)}, bf16[256,512]{1,0:T(8,128)(2,1)S(1)}, u32[]{:S(2)}, u32[]{:S(2)}) %collective-permute-start.15) | collective-permute-done | bytes 262176 | tf_op jit(solution)/shard_map/ppermute | solution.py:327
  116.9 0.1 shard_map.236
  116.9 1.6 %collective-permute-start.16 = (bf16[128,512]{1,0:T(8,128)(2,1)S(1)}, bf16[128,512]{1,0:T(8,128)(2,1)S(1)}, u32[]{:S(2)}, u32[]{:S(2)}) collective-permute-start(bf16[128,512]{1,0:T(8,128)(2,1)S(1)} %get-tuple-element.40), channel_id=1, source_target_pairs={{0,2},{1,3},{2,0},{3,1},{4,6},{5,7},{6,4},{7,5},{8,10},{9,11},{10,... | collective-permute-start | bytes 393224 | tf_op jit(solution)/shard_map/ppermute | solution.py:323
  118.5 4.0 %collective-permute-done.16.theirs = bf16[128,512]{1,0:T(8,128)(2,1)S(1)} collective-permute-done((bf16[128,512]{1,0:T(8,128)(2,1)S(1)}, bf16[128,512]{1,0:T(8,128)(2,1)S(1)}, u32[]{:S(2)}, u32[]{:S(2)}) %collective-permute-start.16) | collective-permute-done | bytes 131104 | tf_op jit(solution)/shard_map/ppermute | solution.py:323
  122.5 1.4 %shard_map.237 = bf16[128,512]{1,0:T(8,128)(2,1)} custom-call(bf16[512,512]{1,0:T(8,128)(2,1)S(1)} %get-tuple-element.32.full, bf16[128,512]{1,0:T(8,128)(2,1)S(1)} %get-tuple-element.39.mine, bf16[128,512]{1,0:T(8,128)(2,1)S(1)} %collective-permute-done.16.theirs, f32[1,512]{1,0:T(1,128)S(1)} %bitcast.4, bf16[3584,512]{1,0:T(8,128)(2,1)S(1)} %copy-done), custom_call_target="tpu_custom_call" | custom-call | flops 201326592 | bytes 4589568 | tf_op jit(solution)/shard_map/pallas_call | solution.py:59
  (34 shorter events, 0.1 us)
Async XLA Ops:
  6.5 2.3 %copy-start.18 = (bf16[256,512]{1,0:T(8,128)(2,1)S(1)}, bf16[256,512]{1,0:T(8,128)(2,1)}, u32[]{:S(2)}) copy-start(bf16[256,512]{1,0:T(8,128)(2,1)} %param.38) | copy-start | bytes 786436
  6.5 2.3 %copy-start.19 = (bf16[128,512]{1,0:T(8,128)(2,1)S(1)}, bf16[128,512]{1,0:T(8,128)(2,1)}, u32[]{:S(2)}) copy-start(bf16[128,512]{1,0:T(8,128)(2,1)} %param.39) | copy-start | bytes 393220
  6.5 34.0 %all-gather.6.cloned.1.call-start = ((), (), s32[]{:S(2)}) async-start(), calls=%async_computation.1 | async-start | bytes 2752512 | tf_op jit(solution)/shard_map/all_gather | solution.py:337
  8.8 78.9 %all-gather.4.cloned.1.call-start = ((), (), s32[]{:S(2)}) async-start(), calls=%async_computation | async-start | bytes 2359296 | tf_op jit(solution)/shard_map/all_gather | solution.py:338
  8.9 31.7 %copy-start.2 = (bf16[384,512]{1,0:T(8,128)(2,1)S(1)}, bf16[384,512]{1,0:T(8,128)(2,1)}, u32[]{:S(2)}) copy-start(bf16[384,512]{1,0:T(8,128)(2,1)} %w_in.1) | copy-start | bytes 1179652
  8.9 31.7 %copy-start.3 = (bf16[512,128]{1,0:T(8,128)(2,1)S(1)}, bf16[512,128]{1,0:T(8,128)(2,1)}, u32[]{:S(2)}) copy-start(bf16[512,128]{1,0:T(8,128)(2,1)} %grid.1) | copy-start | bytes 393220
  8.9 31.7 %copy-start.4 = (bf16[512,128]{1,0:T(8,128)(2,1)S(1)}, bf16[512,128]{1,0:T(8,128)(2,1)}, u32[]{:S(2)}) copy-start(bf16[512,128]{1,0:T(8,128)(2,1)} %mesh.1) | copy-start | bytes 393220
  8.9 31.7 %copy-start.5 = (bf16[128,512]{1,0:T(8,128)(2,1)S(1)}, bf16[128,512]{1,0:T(8,128)(2,1)}, u32[]{:S(2)}) copy-start(bf16[128,512]{1,0:T(8,128)(2,1)} %w_out.1) | copy-start | bytes 393220
  21.9 39.9 %copy-start.6 = (s32[1,4,64]{2,1,0:T(4,128)S(1)}, s32[1,4,64]{2,1,0:T(4,128)}, u32[]{:S(2)}) copy-start(s32[1,4,64]{2,1,0:T(4,128)} %send.2) | copy-start | bytes 3076
  21.9 75.8 %all-gather.8.cloned.1.call-start = ((), (), s32[]{:S(2)}) async-start(), calls=%async_computation.2 | async-start | bytes 5505024 | tf_op jit(solution)/shard_map/all_gather | solution.py:338
  40.5 28.0 %copy-start.10 = (f32[4,2048]{1,0:T(4,128)S(1)}, f32[4,2048]{1,0:T(4,128)}, u32[]{:S(2)}) copy-start(f32[4,2048]{1,0:T(4,128)} %pgeom.1) | copy-start | bytes 98308
  40.5 28.0 %copy-start.11 = (f32[4,1024]{1,0:T(4,128)S(1)}, f32[4,1024]{1,0:T(4,128)}, u32[]{:S(2)}) copy-start(f32[4,1024]{1,0:T(4,128)} %egeom.1) | copy-start | bytes 49156
  40.5 28.0 %copy-start.13 = (f32[4,512]{1,0:T(4,128)S(1)}, f32[4,512]{1,0:T(4,128)}, u32[]{:S(2)}) copy-start(f32[4,512]{1,0:T(4,128)} %egeo.1) | copy-start | bytes 24580
  40.5 28.0 %copy-start.14 = (f32[4,512]{1,0:T(4,128)S(1)}, f32[4,512]{1,0:T(4,128)}, u32[]{:S(2)}) copy-start(f32[4,512]{1,0:T(4,128)} %pgeo.1) | copy-start | bytes 24580
  40.6 31.1 %copy-start.15 = (s32[2,1024]{1,0:T(2,128)S(1)}, s32[2,1024]{1,0:T(2,128)}, u32[]{:S(2)}) copy-start(s32[2,1024]{1,0:T(2,128)} %edges.3) | copy-start | bytes 24580
  40.6 31.1 %copy-start.16 = (f32[512]{0:T(512)S(1)}, f32[512]{0:T(512)}, u32[]{:S(2)}) copy-start(f32[512]{0:T(512)} %param.44) | copy-start | bytes 6148
  40.7 14.8 %collective-permute-start.3 = (bf16[512,512]{1,0:T(8,128)(2,1)S(1)}, bf16[512,512]{1,0:T(8,128)(2,1)S(1)}, u32[]{:S(2)}, u32[]{:S(2)}) collective-permute-start(bf16[512,512]{1,0:T(8,128)(2,1)S(1)} %get-tuple-element.26.w0), channel_id=1, source_target_pairs={{0,2},{1,3},{2,0},{3,1},{4,6},{5,7},{6,4},{7,5},{8,10},{9,11},{10,... | collective-permute-start | bytes 1572872 | tf_op jit(solution)/shard_map/ppermute | solution.py:323
  42.3 18.0 %collective-permute-start = (bf16[1024,128]{1,0:T(8,128)(2,1)S(1)}, bf16[1024,128]{1,0:T(8,128)(2,1)S(1)}, u32[]{:S(2)}, u32[]{:S(2)}) collective-permute-start(bf16[1024,128]{1,0:T(8,128)(2,1)S(1)} %get-tuple-element.23.l0), channel_id=1, source_target_pairs={{0,2},{1,3},{2,0},{3,1},{4,6},{5,7},{6,4},{7,5},{8,10},{9,11},{10,... | collective-permute-start | bytes 786440 | tf_op jit(solution)/shard_map/ppermute | solution.py:323
  42.8 27.6 %collective-permute-start.4 = (bf16[512,512]{1,0:T(8,128)(2,1)S(1)}, bf16[512,512]{1,0:T(8,128)(2,1)S(1)}, u32[]{:S(2)}, u32[]{:S(2)}) collective-permute-start(bf16[512,512]{1,0:T(8,128)(2,1)S(1)} %get-tuple-element.26.w0), channel_id=1, source_target_pairs={{0,1},{1,0},{2,3},{3,2},{4,5},{5,4},{6,7},{7,6},{8,9},{9,8},{10,11... | collective-permute-start | bytes 1572872 | tf_op jit(solution)/shard_map/ppermute | solution.py:327
  55.5 16.1 %collective-permute-start.5 = (bf16[512,512]{1,0:T(8,128)(2,1)S(1)}, bf16[512,512]{1,0:T(8,128)(2,1)S(1)}, u32[]{:S(2)}, u32[]{:S(2)}) collective-permute-start(bf16[512,512]{1,0:T(8,128)(2,1)S(1)} %collective-permute-done.3.w1), channel_id=1, source_target_pairs={{0,1},{1,0},{2,3},{3,2},{4,5},{5,4},{6,7},{7,6},{8,9},{9,8},{10,11... | collective-permute-start | bytes 1572872 | tf_op jit(solution)/shard_map/ppermute | solution.py:327
  55.5 4.7 %collective-permute-start.1 = (bf16[1024,128]{1,0:T(8,128)(2,1)S(1)}, bf16[1024,128]{1,0:T(8,128)(2,1)S(1)}, u32[]{:S(2)}, u32[]{:S(2)}) collective-permute-start(bf16[1024,128]{1,0:T(8,128)(2,1)S(1)} %get-tuple-element.23.l0), channel_id=1, source_target_pairs={{0,1},{1,0},{2,3},{3,2},{4,5},{5,4},{6,7},{7,6},{8,9},{9,8},{10,11... | collective-permute-start | bytes 786440 | tf_op jit(solution)/shard_map/ppermute | solution.py:327
  60.3 1.5 %collective-permute-start.2 = (bf16[1024,128]{1,0:T(8,128)(2,1)S(1)}, bf16[1024,128]{1,0:T(8,128)(2,1)S(1)}, u32[]{:S(2)}, u32[]{:S(2)}) collective-permute-start(bf16[1024,128]{1,0:T(8,128)(2,1)S(1)} %collective-permute-done.l1), channel_id=1, source_target_pairs={{0,1},{1,0},{2,3},{3,2},{4,5},{5,4},{6,7},{7,6},{8,9},{9,8},{10,11... | collective-permute-start | bytes 786440 | tf_op jit(solution)/shard_map/ppermute | solution.py:327
  62.4 8.0 %collective-permute-start.6 = (bf16[64,512]{1,0:T(8,128)(2,1)S(1)}, bf16[64,512]{1,0:T(8,128)(2,1)S(1)}, u32[]{:S(2)}, u32[]{:S(2)}) collective-permute-start(bf16[64,512]{1,0:T(8,128)(2,1)S(1)} %get-tuple-element.27), channel_id=1, source_target_pairs={{0,4},{4,0},{8,12},{12,8},{1,5},{5,1},{9,13},{13,9},{2,6},{6,2},{1... | collective-permute-start | bytes 196616 | tf_op jit(solution)/shard_map/ppermute | solution.py:407
  62.9 7.5 %collective-permute-start.7 = (bf16[64,512]{1,0:T(8,128)(2,1)S(1)}, bf16[64,512]{1,0:T(8,128)(2,1)S(1)}, u32[]{:S(2)}, u32[]{:S(2)}) collective-permute-start(bf16[64,512]{1,0:T(8,128)(2,1)S(1)} %get-tuple-element.28), channel_id=1, source_target_pairs={{0,8},{4,12},{8,0},{12,4},{1,9},{5,13},{9,1},{13,5},{2,10},{6,14},... | collective-permute-start | bytes 196616 | tf_op jit(solution)/shard_map/ppermute | solution.py:407
  65.5 6.1 %collective-permute-start.8 = (bf16[64,512]{1,0:T(8,128)(2,1)S(1)}, bf16[64,512]{1,0:T(8,128)(2,1)S(1)}, u32[]{:S(2)}, u32[]{:S(2)}) collective-permute-start(bf16[64,512]{1,0:T(8,128)(2,1)S(1)} %get-tuple-element.29), channel_id=1, source_target_pairs={{4,8},{8,4},{5,9},{9,5},{6,10},{10,6},{7,11},{11,7},{20,24},{24,20... | collective-permute-start | bytes 196616 | tf_op jit(solution)/shard_map/ppermute | solution.py:407
  77.6 10.1 %copy-start.9 = (f32[512]{0:T(512)S(1)}, f32[512]{0:T(512)}, u32[]{:S(2)}) copy-start(f32[512]{0:T(512)} %param.45) | copy-start | bytes 6148
  77.6 1.6 %collective-permute-start.9 = (bf16[256,512]{1,0:T(8,128)(2,1)S(1)}, bf16[256,512]{1,0:T(8,128)(2,1)S(1)}, u32[]{:S(2)}, u32[]{:S(2)}) collective-permute-start(bf16[256,512]{1,0:T(8,128)(2,1)S(1)} %get-tuple-element.31), channel_id=1, source_target_pairs={{0,1},{1,0},{2,3},{3,2},{4,5},{5,4},{6,7},{7,6},{8,9},{9,8},{10,11... | collective-permute-start | bytes 786440 | tf_op jit(solution)/shard_map/ppermute | solution.py:327
  79.3 12.4 %copy-start.7 = (s32[1,4,32]{2,1,0:T(4,128)S(1)}, s32[1,4,32]{2,1,0:T(4,128)}, u32[]{:S(2)}) copy-start(s32[1,4,32]{2,1,0:T(4,128)} %send.3) | copy-start | bytes 1540
  79.3 8.4 %collective-permute-start.10 = (bf16[256,512]{1,0:T(8,128)(2,1)S(1)}, bf16[256,512]{1,0:T(8,128)(2,1)S(1)}, u32[]{:S(2)}, u32[]{:S(2)}) collective-permute-start(bf16[256,512]{1,0:T(8,128)(2,1)S(1)} %shard_map.231.mine), channel_id=1, source_target_pairs={{0,2},{1,3},{2,0},{3,1},{4,6},{5,7},{6,4},{7,5},{8,10},{9,11},{10,... | collective-permute-start | bytes 786440 | tf_op jit(solution)/shard_map/ppermute | solution.py:323
  80.9 16.8 %copy-start.12 = (s32[2,2048]{1,0:T(2,128)S(1)}, s32[2,2048]{1,0:T(2,128)}, u32[]{:S(2)}) copy-start(s32[2,2048]{1,0:T(2,128)} %edges.5) | copy-start | bytes 49156
  87.7 1.4 %copy-start.1 = (bf16[1536,512]{1,0:T(8,128)(2,1)S(1)}, bf16[1536,512]{1,0:T(8,128)(2,1)}, u32[]{:S(2)}) copy-start(bf16[1536,512]{1,0:T(8,128)(2,1)} %all-gather.4.cloned.1.call-done.weights) | copy-start | bytes 4718596
  90.0 1.6 %collective-permute-start.11 = (bf16[256,512]{1,0:T(8,128)(2,1)S(1)}, bf16[256,512]{1,0:T(8,128)(2,1)S(1)}, u32[]{:S(2)}, u32[]{:S(2)}) collective-permute-start(bf16[256,512]{1,0:T(8,128)(2,1)S(1)} %shard_map.232.mine), channel_id=1, source_target_pairs={{0,1},{1,0},{2,3},{3,2},{4,5},{5,4},{6,7},{7,6},{8,9},{9,8},{10,11... | collective-permute-start | bytes 786440 | tf_op jit(solution)/shard_map/ppermute | solution.py:327
  92.1 14.2 %collective-permute-start.12 = (bf16[32,512]{1,0:T(8,128)(2,1)S(1)}, bf16[32,512]{1,0:T(8,128)(2,1)S(1)}, u32[]{:S(2)}, u32[]{:S(2)}) collective-permute-start(bf16[32,512]{1,0:T(8,128)(2,1)S(1)} %get-tuple-element.34), channel_id=1, source_target_pairs={{0,4},{4,0},{8,12},{12,8},{1,5},{5,1},{9,13},{13,9},{2,6},{6,2},{1... | collective-permute-start | bytes 98312 | tf_op jit(solution)/shard_map/ppermute | solution.py:438
  92.1 14.2 %collective-permute-start.13 = (bf16[32,512]{1,0:T(8,128)(2,1)S(1)}, bf16[32,512]{1,0:T(8,128)(2,1)S(1)}, u32[]{:S(2)}, u32[]{:S(2)}) collective-permute-start(bf16[32,512]{1,0:T(8,128)(2,1)S(1)} %get-tuple-element.35), channel_id=1, source_target_pairs={{0,8},{4,12},{8,0},{12,4},{1,9},{5,13},{9,1},{13,5},{2,10},{6,14},... | collective-permute-start | bytes 98312 | tf_op jit(solution)/shard_map/ppermute | solution.py:438
  94.4 11.9 %collective-permute-start.14 = (bf16[32,512]{1,0:T(8,128)(2,1)S(1)}, bf16[32,512]{1,0:T(8,128)(2,1)S(1)}, u32[]{:S(2)}, u32[]{:S(2)}) collective-permute-start(bf16[32,512]{1,0:T(8,128)(2,1)S(1)} %get-tuple-element.36), channel_id=1, source_target_pairs={{4,8},{8,4},{5,9},{9,5},{6,10},{10,6},{7,11},{11,7},{20,24},{24,20... | collective-permute-start | bytes 98312 | tf_op jit(solution)/shard_map/ppermute | solution.py:438
  97.7 8.6 %copy-start = (bf16[3584,512]{1,0:T(8,128)(2,1)S(1)}, bf16[3584,512]{1,0:T(8,128)(2,1)}, u32[]{:S(2)}) copy-start(bf16[3584,512]{1,0:T(8,128)(2,1)} %all-gather.8.cloned.1.call-done.weights) | copy-start | bytes 11010052
  97.7 8.6 %copy-start.17 = (f32[512]{0:T(512)S(1)}, f32[512]{0:T(512)}, u32[]{:S(2)}) copy-start(f32[512]{0:T(512)} %param.46) | copy-start | bytes 6148
  106.3 16.2 %copy-start.8 = (f32[512]{0:T(512)S(1)}, f32[512]{0:T(512)}, u32[]{:S(2)}) copy-start(f32[512]{0:T(512)} %param.47) | copy-start | bytes 6148
  115.2 1.6 %collective-permute-start.15 = (bf16[256,512]{1,0:T(8,128)(2,1)S(1)}, bf16[256,512]{1,0:T(8,128)(2,1)S(1)}, u32[]{:S(2)}, u32[]{:S(2)}) collective-permute-start(bf16[256,512]{1,0:T(8,128)(2,1)S(1)} %get-tuple-element.38), channel_id=1, source_target_pairs={{0,1},{1,0},{2,3},{3,2},{4,5},{5,4},{6,7},{7,6},{8,9},{9,8},{10,11... | collective-permute-start | bytes 786440 | tf_op jit(solution)/shard_map/ppermute | solution.py:327
  116.9 5.6 %collective-permute-start.16 = (bf16[128,512]{1,0:T(8,128)(2,1)S(1)}, bf16[128,512]{1,0:T(8,128)(2,1)S(1)}, u32[]{:S(2)}, u32[]{:S(2)}) collective-permute-start(bf16[128,512]{1,0:T(8,128)(2,1)S(1)} %get-tuple-element.40), channel_id=1, source_target_pairs={{0,2},{1,3},{2,0},{3,1},{4,6},{5,7},{6,4},{7,5},{8,10},{9,11},{10,... | collective-permute-start | bytes 393224 | tf_op jit(solution)/shard_map/ppermute | solution.py:323
Sparse Core Ops, SparseCore 0:
  8.9 31.5 all-gather.5
  42.1 11.1 all-gather.3
  54.8 14.0 all-gather.7

commit v2 on v1

v2 whole, which is shorter than its diff:
```python
import functools

import jax
import jax.numpy as jnp
from jax import lax
from jax.experimental import pallas as pl
from jax.experimental.pallas import tpu as pltpu
from jax.sharding import PartitionSpec as P

BLOCK = 128
OFFSETS = (-2, -1, 1, 2)
STEP = 512
GATHERED = 1024
VMEM_BYTES = 24 * 1024 * 1024
I16 = jnp.int16
BF16 = jnp.bfloat16
F32 = jnp.float32


def silu(v):
    h = 0.5 * v
    return h + h * jnp.tanh(h)


def region_of(delta):
    return jnp.where(delta < 0, delta + 2, delta + 1)


def halo_plan(count):
    plan = []
    if count == 4:
        for bit in (1, 2, 3):
            pairs = [(d, d ^ bit) for d in range(4) if abs((d ^ bit) - d) <= 2]
            regions = [(OFFSETS.index((d ^ bit) - d) if abs((d ^ bit) - d) <= 2 else -1) for d in range(4)]
            plan.append((pairs, regions, regions))
    else:
        for region, offset in enumerate(OFFSETS):
            pairs = [(d, d + offset) for d in range(count) if 0 <= d + offset < count]
            plan.append((pairs, region, 3 - region))
    return plan


def by_index(choice, index):
    if isinstance(choice, int):
        return choice
    picked = jnp.int32(choice[0])
    for place in range(1, len(choice)):
        picked = jnp.where(index == place, choice[place], picked)
    return picked


def whole_refs(count):
    return [pl.BlockSpec(memory_space=pltpu.VMEM)] * count


def call(body, outs, args, scratch=(), flops=0, smem=0):
    moved = sum(a.size * a.dtype.itemsize for a in args) + sum(
        o.size * jnp.dtype(o.dtype).itemsize for o in outs
    )
    specs = whole_refs(len(args) - smem) + [pl.BlockSpec(memory_space=pltpu.SMEM)] * smem
    return pl.pallas_call(
        body,
        out_shape=tuple(outs),
        in_specs=specs,
        out_specs=tuple(whole_refs(len(outs))),
        scratch_shapes=list(scratch),
        compiler_params=pltpu.CompilerParams(vmem_limit_bytes=VMEM_BYTES),
        cost_estimate=pl.CostEstimate(flops=int(flops), bytes_accessed=int(moved), transcendentals=0),
    )(*args)


def dot(a, b):
    return jnp.dot(a, b, preferred_element_type=F32)


def dot_first(a, b):
    return lax.dot_general(a, b, (((0,), (0,)), ((), ())), preferred_element_type=F32)


def three_parts(v):
    a = v.astype(BF16)
    rest = v - a.astype(F32)
    b = rest.astype(BF16)
    c = (rest - b.astype(F32)).astype(BF16)
    return a, b, c


def embed_rows(geom, geo):
    a1, a2, a3 = three_parts(geom)
    b1, b2, b3 = three_parts(geo)
    left = jnp.concatenate([a1, a1, a2, a1, a2, a3], axis=0)
    right = jnp.concatenate([b1, b2, b1, b3, b2, b1], axis=0)
    return silu(dot_first(left, right)).astype(BF16)


def embed_kernel(egeom, egeo, pgeom, pgeo, after, eout, pout):
    for geom, geo, out in ((egeom, egeo, eout), (pgeom, pgeo, pout)):
        for first in range(0, out.shape[0], STEP):
            out[first : first + STEP, :] = embed_rows(geom[:, first : first + STEP], geo[...])


def layer_norm(v):
    width = v.shape[-1]
    centered = v - jnp.sum(v, axis=-1, keepdims=True) * (1.0 / width)
    spread = jnp.sum(centered * centered, axis=-1, keepdims=True) * (1.0 / width)
    return centered * lax.rsqrt(spread + 1e-05)


def hot(cond):
    return jnp.where(cond, BF16(1), BF16(0))


def pick_rows(table, listed):
    rows = lax.broadcasted_iota(I16, (table.shape[0], 1), 0)
    return dot_first(hot(rows == listed.astype(I16)), table).astype(BF16)


def pick_lists(plan, table, send, outs):
    here = lax.axis_index("dom")
    for (pairs, sent, received), out in zip(plan, outs):
        region = jnp.maximum(by_index(sent, here), 0)
        out[...] = pick_rows(table, send[0, pl.ds(region, 1), :])


def half_of(whole, half):
    rows = half.shape[0]
    half[...] = whole[pl.ds(pl.multiple_of(lax.axis_index("groups") * rows, rows), rows), :]


def stack_into(out, parts):
    first = 0
    for part in parts:
        out[first : first + part.shape[0], :] = part[...]
        first += part.shape[0]


def first_pack_kernel(plan, grid, send, w_in, w_out, weights, half, *outs):
    stack_into(weights, (w_in, w_out))
    half_of(weights, half)
    pick_lists(plan, grid[...], send, outs)


def second_pack_kernel(e_in, e_out, p_in, p_out, after, weights, e_half, p_half):
    stack_into(weights, (e_in, e_out, p_in, p_out))
    rows = e_in.shape[0] + e_out.shape[0]
    half_of(weights.at[:rows, :], e_half)
    half_of(weights.at[rows:, :], p_half)


def concat_kernel(*refs):
    stack_into(refs[-1], refs[:-1])


def place_shards(target, refs, first=0):
    own, beside, *halves = refs
    quarter = lax.axis_index("sub")
    group = lax.axis_index("groups")
    rows = target.shape[0] // 4
    for ref, step in ((own, 0), (beside, 1)):
        place = pl.multiple_of(lax.bitwise_xor(quarter, step) * rows, rows)
        target[pl.ds(place, rows), :] = ref[first : first + rows, :]
    if len(halves) == 2:
        for ref, step in zip(halves, (2, 3)):
            place = pl.multiple_of(lax.bitwise_xor(quarter, step) * rows, rows)
            target[pl.ds(place, rows), :] = ref[...]
    else:
        half = rows // 2
        for ref, step, other in zip(halves, (2, 2, 3, 3), (0, 1, 0, 1)):
            which = lax.bitwise_xor(group, other)
            place = pl.multiple_of(lax.bitwise_xor(quarter, step) * rows + which * half, half)
            target[pl.ds(place, half), :] = ref[...]


def joined(stack, first, rows):
    step = stack.shape[0] // 4
    return jnp.concatenate([stack[k * step + first : k * step + first + rows, :] for k in range(4)], axis=0)


def halo_targets(plan, slots, node_rows, width):
    here = lax.axis_index("dom")
    lane = lax.broadcasted_iota(jnp.int32, (1, width), 1)
    target = jnp.full((1, width), -1, jnp.int32)
    for place, (pairs, sent, received) in enumerate(plan):
        region = by_index(received, here)
        first = jnp.where(region < 0, -4 * node_rows, node_rows + region * slots)
        inside = (lane >= place * slots) & (lane < (place + 1) * slots)
        target = jnp.where(inside, lane - place * slots + first, target)
    return target.astype(I16)


def columns(edges, first):
    pair = edges[:, first : first + STEP]
    zero = jnp.zeros((8 - pair.shape[0], STEP), jnp.int32)
    upright = jnp.transpose(jnp.concatenate([pair, zero], axis=0).astype(F32)).astype(jnp.int32).astype(I16)
    return upright[:, 0:1], upright[:, 1:2]


def edge_blocks(edges, live_edges, first_stage, w_out, messages, totals):
    count = edges.shape[1]
    row = lax.broadcasted_iota(I16, (totals.shape[0], 1), 0)
    quarter = lax.axis_index("sub")
    for first in range(0, count, STEP):
        hidden = silu(first_stage(first)).astype(BF16)
        message = layer_norm(dot(hidden, w_out))
        place = lax.broadcasted_iota(jnp.int32, (STEP, 1), 0) + (first + quarter * count)
        messages[first : first + STEP, :] = jnp.where(place < live_edges, message, 0.0).astype(BF16)
        done = first + STEP
        if done % GATHERED == 0 or done == count:
            begin = (first // GATHERED) * GATHERED
            collect = hot(row == edges[1:2, begin:done].astype(I16))
            part = dot(collect, messages[begin:done, :])
            if begin == 0:
                totals[...] = part
            else:
                totals[...] += part


def hand_out(totals, gain, keep, give):
    rows = totals.shape[0] // 4
    core = lax.rem(lax.axis_index("sub"), 2)
    for half in range(2):
        for out, which in ((keep, core), (give, 1 - core)):
            place = pl.multiple_of((2 * half + which) * rows, rows)
            out[half * rows : (half + 1) * rows, :] = (totals[pl.ds(place, rows), :] * gain[...]).astype(BF16)


def enc_kernel(
    plan, slots, grid_rows, mesh_rows, k_in, emb, edges, gain, l0, l1, l2, l3, w0, w1, w2, w3, w4, w5,
    live, keep, give, own_mesh, full, stack, table, messages, totals,
):
    d = gain.shape[1]
    quarter = lax.axis_index("sub")
    width = l0.shape[1]
    for shard, step in zip((l0, l1, l2, l3), (0, 2, 1, 3)):
        place = pl.multiple_of(lax.bitwise_xor(quarter, step) * width, width)
        full[:, pl.ds(place, width)] = shard[...]
    place_shards(stack, (w0, w1, w2, w3, w4, w5))
    rows = mesh_rows // 4
    core = lax.rem(quarter, 2)
    for half in range(2):
        place = pl.multiple_of(grid_rows + (2 * half + core) * rows, rows)
        own_mesh[half * rows : (half + 1) * rows, :] = full[pl.ds(place, rows), :]

    w_in = joined(stack, 0, k_in)
    halo_first, got = grid_rows + mesh_rows, full.shape[0] - grid_rows - mesh_rows
    table[:d, :] = w_in[:d, :]
    table[d : d + grid_rows, :] = dot(full[:grid_rows, :], w_in[d : 2 * d, :]).astype(BF16)
    base = d + grid_rows + mesh_rows
    table[d + grid_rows : base, :] = dot(full[grid_rows:halo_first, :], w_in[2 * d :, :]).astype(BF16)
    table[base : base + got, :] = dot(full[halo_first:, :], w_in[d : 2 * d, :]).astype(BF16)
    if base + got < table.shape[0]:
        table[base + got :, :] = jnp.zeros((table.shape[0] - base - got, d), BF16)
    targets = halo_targets(plan, slots, grid_rows, table.shape[0] - base)
    own = lax.broadcasted_iota(I16, (1, grid_rows), 1)
    mesh = lax.broadcasted_iota(I16, (1, mesh_rows), 1)

    def first_stage(first):
        senders, receivers = columns(edges, first)
        chosen = [emb[first : first + STEP, :], hot(own == senders), hot(mesh == receivers), hot(targets == senders)]
        return dot(jnp.concatenate(chosen, axis=1), table[...])

    edge_blocks(edges, live[0] * BLOCK, first_stage, joined(stack, k_in, d // 4), messages, totals)
    hand_out(totals, gain, keep, give)


def node_update(mesh, shares, w_in, w_out, gain):
    stacked = jnp.concatenate([mesh, shares], axis=1)
    hidden = silu(dot(stacked, w_in)).astype(BF16)
    update = layer_norm(dot(hidden, w_out)) * gain
    return (mesh.astype(F32) + update).astype(BF16)


def add(mine, theirs):
    return (mine.astype(F32) + theirs.astype(F32)).astype(BF16)


def add_kernel(mine, theirs, out):
    out[...] = add(mine[...], theirs[...])


def node_kernel(k_in, k_out, mesh, mine, theirs, gain, n_in, n_out, w0, w1, w2, w3, w4, w5, out, packed, stack):
    place_shards(stack, (w0, w1, w2, w3, w4, w5))
    w_in, w_out = joined(stack, 0, k_in), joined(stack, k_in, k_out)
    out[...] = node_update(mesh[...], add(mine[...], theirs[...]), w_in, w_out, gain[...])
    stack_into(packed, (n_in, n_out))


def middle_kernel(plan, mine, theirs, send, full, *outs):
    rows = mine.shape[0] // 2
    core = lax.rem(lax.axis_index("sub"), 2)
    for half in range(2):
        for part, which in ((mine, core), (theirs, 1 - core)):
            place = pl.multiple_of((2 * half + which) * rows, rows)
            full[pl.ds(place, rows), :] = part[half * rows : (half + 1) * rows, :]
    pick_lists(plan, full[...], send, outs)


def proc_first_kernel(k_in, first_row, emb, full, edges, w0, w1, w2, w3, w4, w5, table, pre, w_source, w_out, stack):
    d = full.shape[1]
    node_rows = full.shape[0]
    place_shards(stack, (w0, w1, w2, w3, w4, w5), first_row)
    w_in = joined(stack, 0, k_in)
    w_out[...] = joined(stack, k_in, d // 4)
    w_source[...] = w_in[d : 2 * d, :]
    table[:d, :] = w_in[:d, :]
    table[d : d + node_rows, :] = dot(full[...], w_in[d : 2 * d, :]).astype(BF16)
    table[d + node_rows :, :] = dot(full[...], w_in[2 * d :, :]).astype(BF16)
    lane = lax.broadcasted_iota(I16, (1, node_rows), 1)
    for first in range(0, pre.shape[0], STEP):
        pre[first : first + STEP, :] = dot(own_chosen(emb, edges, lane, first), table[...])


def own_chosen(emb, edges, lane, first):
    senders, receivers = columns(edges, first)
    return jnp.concatenate([emb[first : first + STEP, :], hot(lane == senders), hot(lane == receivers)], axis=1)


def proc_second_kernel(
    plan, slots, node_rows, n_halo, emb, edges, gain, table, pre, w_source, w_out, *rest
):
    halos = rest[:n_halo]
    live, keep, give, halo_table, messages, totals = rest[n_halo:]
    d = pre.shape[1]
    got = jnp.concatenate([h[...] for h in halos], axis=0)
    halo_table[: got.shape[0], :] = dot(got, w_source[...]).astype(BF16)
    if got.shape[0] < halo_table.shape[0]:
        halo_table[got.shape[0] :, :] = jnp.zeros((halo_table.shape[0] - got.shape[0], d), BF16)
    targets = halo_targets(plan, slots, node_rows, halo_table.shape[0])
    lane = lax.broadcasted_iota(I16, (1, node_rows), 1)

    def first_stage(first):
        senders, receivers = columns(edges, first)
        remote = dot(hot(targets == senders), halo_table[...])
        if first < pre.shape[0]:
            return pre[first : first + STEP, :] + remote
        return dot(own_chosen(emb, edges, lane, first), table[...]) + remote

    edge_blocks(edges, live[0] * BLOCK, first_stage, w_out[...], messages, totals)
    hand_out(totals, gain, keep, give)


def fold_kernel(mine, theirs, keep, give):
    rows = mine.shape[0] // 2
    chip = lax.div(lax.axis_index("sub"), 2)
    for out, which in ((keep, chip), (give, 1 - chip)):
        place = pl.multiple_of(which * rows, rows)
        out[...] = add(mine[pl.ds(place, rows), :], theirs[pl.ds(place, rows), :])


def out_kernel(k_in, k_out, full, mine, theirs, gain, w0, w1, w2, w3, out, stack):
    rows = mine.shape[0]
    mesh = full[pl.ds(pl.multiple_of(lax.axis_index("sub") * rows, rows), rows), :]
    place_shards(stack, (w0, w1, w2, w3))
    w_in, w_out = joined(stack, 0, k_in), joined(stack, k_in, k_out)
    out[...] = node_update(mesh, add(mine[...], theirs[...]), w_in, w_out, gain[...])


def to_chip(v):
    return lax.ppermute(v, "sub", [(i, i ^ 2) for i in range(4)])


def to_core(v):
    return lax.ppermute(v, "sub", [(i, i ^ 1) for i in range(4)])


def to_group(v):
    count = lax.axis_size("groups")
    return lax.ppermute(v, "groups", [(i, count - 1 - i) for i in range(count)])


def shape(rows, width, dtype=BF16):
    return jax.ShapeDtypeStruct((rows, width), dtype)


def padded(rows):
    return -(-rows // 128) * 128


def local(
    grid_lat,
    mesh_lat,
    grid_send,
    mesh_send,
    enc_edges,
    enc_geom,
    enc_blocks,
    proc_edges,
    proc_geom,
    proc_blocks,
    enc_geo,
    proc_geo,
    enc_edge_in,
    enc_edge_out,
    enc_node_in,
    enc_node_out,
    proc_edge_in,
    proc_edge_out,
    proc_node_in,
    proc_node_out,
    enc_edge_gain,
    enc_node_gain,
    proc_edge_gain,
    proc_node_gain,
):
    plan = halo_plan(lax.axis_size("dom"))
    d = enc_geo.shape[1]
    grid_rows, mesh_rows = grid_lat.shape[0], mesh_lat.shape[0]
    n_enc, n_proc = enc_edges.shape[1], proc_edges.shape[1]
    enc_edge_gain, enc_node_gain, proc_edge_gain, proc_node_gain = (
        g.reshape(1, d) for g in (enc_edge_gain, enc_node_gain, proc_edge_gain, proc_node_gain)
    )
    k_in, k_out = enc_edge_in.shape[0], enc_edge_out.shape[0]
    n_in, n_out = enc_node_in.shape[0], enc_node_out.shape[0]
    width = grid_lat.shape[1]

    slots = grid_send.shape[2]
    edge_w, edge_half, *outgoing = call(
        functools.partial(first_pack_kernel, plan),
        [shape(k_in + k_out, d), shape((k_in + k_out) // 2, d)] + [shape(slots, width)] * len(plan),
        [grid_lat, grid_send, enc_edge_in, enc_edge_out],
    )
    edge_across = to_chip(edge_half)
    halos = [lax.ppermute(v, "dom", entry[0]) for v, entry in zip(outgoing, plan)]
    got = len(plan) * slots
    (lat,) = call(concat_kernel, [shape(grid_rows + mesh_rows + got, width)], [grid_lat, mesh_lat, *halos])
    lat_across = to_chip(lat)
    lat_beside = to_core(lat)
    edge_beside = to_core(edge_w)
    enc_emb, proc_emb = call(
        embed_kernel,
        [shape(n_enc, d), shape(n_proc, d)],
        [enc_geom, enc_geo, proc_geom, proc_geo, lat],
        flops=2 * (n_enc + n_proc) * d * 128,
    )
    edge_round = to_group(edge_across)
    lat_both = to_core(lat_across)
    next_w, node_half, proc_half = call(
        second_pack_kernel,
        [shape(n_in + n_out + k_in + k_out, d), shape((n_in + n_out) // 2, d), shape((k_in + k_out) // 2, d)],
        [enc_node_in, enc_node_out, proc_edge_in, proc_edge_out, lat_across],
    )
    node_across, proc_across = to_chip(node_half), to_chip(proc_half)
    next_beside = to_core(next_w)

    halo_rows = padded(got)
    half = mesh_rows // 2
    keep, give, own_mesh = call(
        functools.partial(enc_kernel, plan, slots, grid_rows, mesh_rows, k_in),
        [shape(half, d)] * 3,
        [
            enc_emb, enc_edges, enc_edge_gain, lat, lat_across, lat_beside, lat_both,
            edge_w, edge_beside, edge_across, edge_round, to_core(edge_across), to_core(edge_round), enc_blocks,
        ],
        scratch=[
            pltpu.VMEM((grid_rows + mesh_rows + got, d), BF16),
            pltpu.VMEM((4 * (k_in + k_out), d), BF16),
            pltpu.VMEM((d + grid_rows + mesh_rows + halo_rows, d), BF16),
            pltpu.VMEM((n_enc, d), BF16),
            pltpu.VMEM((mesh_rows, d), F32),
        ],
        flops=2 * n_enc * d * (3 * d + grid_rows + mesh_rows + halo_rows),
        smem=1,
    )
    node_round, proc_round = to_group(node_across), to_group(proc_across)
    (chip_sum,) = call(add_kernel, [shape(half, d)], [keep, to_core(give)])
    mid_half, last_w = call(
        functools.partial(node_kernel, n_in, n_out),
        [shape(half, d), shape(n_in + n_out, d)],
        [
            own_mesh, chip_sum, to_chip(chip_sum), enc_node_gain, proc_node_in, proc_node_out,
            next_w, next_beside, node_across, node_round, to_core(node_across), to_core(node_round),
        ],
        scratch=[pltpu.VMEM((4 * (n_in + n_out), d), BF16)],
        flops=2 * half * d * 3 * d,
    )
    slots = mesh_send.shape[2]
    mid, *outgoing = call(
        functools.partial(middle_kernel, plan),
        [shape(mesh_rows, d)] + [shape(slots, d)] * len(plan),
        [mid_half, to_core(mid_half), mesh_send],
        flops=2 * len(plan) * slots * mesh_rows * d,
    )
    halos = [lax.ppermute(v, "dom", entry[0]) for v, entry in zip(outgoing, plan)]
    last_across, last_beside = to_chip(last_w), to_core(last_w)
    early = n_proc // 2
    table, pre, w_source, w_out = call(
        functools.partial(proc_first_kernel, k_in, n_in + n_out),
        [shape(d + 2 * mesh_rows, d), shape(early, d, F32), shape(d, d), shape(d, d)],
        [
            proc_emb, mid, proc_edges, next_w, next_beside, proc_across, proc_round,
            to_core(proc_across), to_core(proc_round),
        ],
        scratch=[pltpu.VMEM((4 * (k_in + k_out), d), BF16)],
        flops=2 * early * d * (d + 2 * mesh_rows),
    )
    halo_rows = padded(len(plan) * slots)
    keep, give = call(
        functools.partial(proc_second_kernel, plan, slots, mesh_rows, len(plan)),
        [shape(half, d), shape(half, d)],
        [proc_emb, proc_edges, proc_edge_gain, table, pre, w_source, w_out, *halos, proc_blocks],
        scratch=[
            pltpu.VMEM((halo_rows, d), BF16),
            pltpu.VMEM((n_proc, d), BF16),
            pltpu.VMEM((mesh_rows, d), F32),
        ],
        flops=2 * n_proc * d * (2 * d + mesh_rows + halo_rows),
        smem=1,
    )
    quarter = mesh_rows // 4
    mine, other = call(fold_kernel, [shape(quarter, d)] * 2, [keep, to_core(give)])
    (result,) = call(
        functools.partial(out_kernel, n_in, n_out),
        [shape(quarter, d)],
        [mid, mine, to_chip(other), proc_node_gain, last_w, last_beside, last_across, to_core(last_across)],
        scratch=[pltpu.VMEM((4 * (n_in + n_out), d), BF16)],
        flops=2 * quarter * d * 3 * d,
    )
    return result


def solution(mesh):
    placed = (
        P(("groups", "dom"), "sub"),
        P(("groups", "dom"), "sub"),
        P("dom", None, None),
        P("dom", None, None),
        P(None, ("dom", "sub")),
        P(None, ("dom", "sub")),
        P("dom"),
        P(None, ("dom", "sub")),
        P(None, ("dom", "sub")),
        P("dom"),
        P(),
        P(),
        P("sub", None),
        P("sub", None),
        P("sub", None),
        P("sub", None),
        P("sub", None),
        P("sub", None),
        P("sub", None),
        P("sub", None),
        P(),
        P(),
        P(),
        P(),
    )
    return jax.shard_map(
        local,
        mesh=mesh,
        in_specs=placed,
        out_specs=P(("groups", "dom", "sub"), None),
        check_vma=False,
    )
```

time: 131 us -> 79.2 us (0.60)
  waiting for transfers between devices: 53.2 us -> 27.4 us
  between operations: 14.8 us -> 1.65 us
  blocking collectives: 12.9 us -> 0 us
  Pallas kernels: 28.7 us -> 18.4 us
  local copies, waits for them, and re-layouts: 1.51 us -> 8.21 us
  starting transfers between devices: 17.1 us -> 23.2 us
  other arithmetic: 2.27 us -> 0 us
    all_gather x3 -> x0, waiting for transfers between devices: 18.6 us -> none  [the longest x1 18.6 us: gathered(): lax.all_gather(v, 'sub', axis=0, tiled=True, axis_index_groups=[[0, 2], [...]
    all_gather x1 -> x0, blocking collectives: 12.9 us -> none  [gathered(): lax.all_gather(v, 'sub', axis=0, tiled=True, axis_index_groups=[[0, 2], [...]
    pallas_call x12, Pallas kernels: 28.7 us -> 18.4 us  [call(): pl.pallas_call(body, out_shape=tuple(outs), in_specs=specs, out_specs=tup...]
    ppermute x4 -> x7, waiting for transfers between devices: 27.8 us -> 19.4 us  [to_chip(): return lax.ppermute(v, 'sub', [(i, i ^ 2) for i in range(4)])]
    unnamed x40 -> x44, local copies, waits for them, and re-layouts: 1.51 us -> 8.21 us
    ppermute x7 -> x15, waiting for transfers between devices: 5.46 us -> 2.59 us  [to_core(): return lax.ppermute(v, 'sub', [(i, i ^ 1) for i in range(4)])]
    ppermute x4 -> x7, starting transfers between devices: 5.22 us -> 7.61 us  [to_chip(): return lax.ppermute(v, 'sub', [(i, i ^ 2) for i in range(4)])]
    ppermute x7 -> x15, starting transfers between devices: 0.73 us -> 3.11 us  [to_core(): return lax.ppermute(v, 'sub', [(i, i ^ 1) for i in range(4)])]
  transfers between devices with their start and end apart: 20 -> 31, of which waited for: 10 -> 11; matrix products, arithmetic and copies ran while one was open for 0% -> 0% of each run, Pallas kernels for 14% -> 21%
where the time goes in v2:
time: 79.2 us; the launch traced here: 78.8 us
  waiting for transfers between devices  27.4 us (35%)
  starting transfers between devices  23.2 us (29%)
  Pallas kernels  18.4 us (23%)
  local copies, waits for them, and re-layouts  8.21 us (10%)
  between operations  1.65 us (2%)
    ppermute x7, waiting for transfers between devices, to_chip(): return lax.ppermute(v, 'sub', [(i, i ^ 2) for i in range(4)])  19.4 us
    pallas_call x12, Pallas kernels, call(): pl.pallas_call(body, out_shape=tuple(outs), in_specs=specs, out_specs=tup...  18.4 us
    ppermute x6, starting transfers between devices, local(): lax.ppermute(v, 'dom', entry[0])  11 us
    unnamed x44, local copies, waits for them, and re-layouts  8.21 us
    ppermute x7, starting transfers between devices, to_chip(): return lax.ppermute(v, 'sub', [(i, i ^ 2) for i in range(4)])  7.61 us
    ppermute x6, waiting for transfers between devices, local(): lax.ppermute(v, 'dom', entry[0])  3.26 us
    ppermute x15, starting transfers between devices, to_core(): return lax.ppermute(v, 'sub', [(i, i ^ 1) for i in range(4)])  3.11 us
    ppermute x15, waiting for transfers between devices, to_core(): return lax.ppermute(v, 'sub', [(i, i ^ 1) for i in range(4)])  2.59 us
  transfers between devices with their start and end apart: 31, of which 11 were waited for; matrix products, arithmetic and copies ran while one was open for 0% of the time, Pallas kernels for 21%

profile of v2, /device:TPU:12, one launch (start us, length us, event | category | flops | bytes accessed | tf_op | source)
XLA Modules:
  0.0 78.8 jit_solution(4946977304652242786)
XLA Ops:
  0.0 0.9 %copy-done = bf16[512,128]{1,0:T(8,128)(2,1)S(1)} copy-done((bf16[512,128]{1,0:T(8,128)(2,1)S(1)}, bf16[512,128]{1,0:T(8,128)(2,1)}, u32[]{:S(2)}) %copy-start) | copy-done | bytes 131096
  0.9 1.0 %copy-done.1 = bf16[384,512]{1,0:T(8,128)(2,1)S(1)} copy-done((bf16[384,512]{1,0:T(8,128)(2,1)S(1)}, bf16[384,512]{1,0:T(8,128)(2,1)}, u32[]{:S(2)}) %copy-start.1) | copy-done | bytes 393240
  1.9 0.9 %copy-done.5 = bf16[128,512]{1,0:T(8,128)(2,1)S(1)} copy-done((bf16[128,512]{1,0:T(8,128)(2,1)S(1)}, bf16[128,512]{1,0:T(8,128)(2,1)}, u32[]{:S(2)}) %copy-start.5) | copy-done | bytes 131096
  2.8 0.7 copy-done.11
  3.5 0.3 shard_map.226
  3.9 1.6 %collective-permute-start.7 = (bf16[256,512]{1,0:T(8,128)(2,1)S(1)}, bf16[256,512]{1,0:T(8,128)(2,1)S(1)}, u32[]{:S(2)}, u32[]{:S(2)}) collective-permute-start(bf16[256,512]{1,0:T(8,128)(2,1)S(1)} %get-tuple-element.37), channel_id=1, source_target_pairs={{0,2},{1,3},{2,0},{3,1},{4,6},{5,7},{6,4},{7,5},{8,10},{9,11},{10,... | collective-permute-start | bytes 786440 | tf_op jit(solution)/shard_map/ppermute | solution.py:359
  5.4 0.4 collective-permute-start
  5.9 2.6 %collective-permute-start.1 = (bf16[64,128]{1,0:T(8,128)(2,1)S(1)}, bf16[64,128]{1,0:T(8,128)(2,1)S(1)}, u32[]{:S(2)}, u32[]{:S(2)}) collective-permute-start(bf16[64,128]{1,0:T(8,128)(2,1)S(1)} %get-tuple-element.33), channel_id=1, source_target_pairs={{0,8},{4,12},{8,0},{12,4},{1,9},{5,13},{9,1},{13,5},{2,10},{6,14},... | collective-permute-start | bytes 49160 | tf_op jit(solution)/shard_map/ppermute | solution.py:423
  8.5 2.3 %collective-permute-start.2 = (bf16[64,128]{1,0:T(8,128)(2,1)S(1)}, bf16[64,128]{1,0:T(8,128)(2,1)S(1)}, u32[]{:S(2)}, u32[]{:S(2)}) collective-permute-start(bf16[64,128]{1,0:T(8,128)(2,1)S(1)} %get-tuple-element.34), channel_id=1, source_target_pairs={{4,8},{8,4},{5,9},{9,5},{6,10},{10,6},{7,11},{11,7},{20,24},{24,20... | collective-permute-start | bytes 49160 | tf_op jit(solution)/shard_map/ppermute | solution.py:423
  10.8 3.2 %collective-permute-done.2.refs_4_ = bf16[64,128]{1,0:T(8,128)(2,1)S(1)} collective-permute-done((bf16[64,128]{1,0:T(8,128)(2,1)S(1)}, bf16[64,128]{1,0:T(8,128)(2,1)S(1)}, u32[]{:S(2)}, u32[]{:S(2)}) %collective-permute-start.2) | collective-permute-done | bytes 16416 | tf_op jit(solution)/shard_map/ppermute | solution.py:423
  14.1 0.9 %copy-done.6 = bf16[512,128]{1,0:T(8,128)(2,1)S(1)} copy-done((bf16[512,128]{1,0:T(8,128)(2,1)S(1)}, bf16[512,128]{1,0:T(8,128)(2,1)}, u32[]{:S(2)}) %copy-start.6) | copy-done | bytes 131096
  15.0 0.6 collective-permute-start.3
  15.6 0.5 collective-permute-start.8
  16.1 0.2 collective-permute-start.4
  16.3 6.0 %collective-permute-done.3.l1.after = bf16[1216,128]{1,0:T(8,128)(2,1)S(1)} collective-permute-done((bf16[1216,128]{1,0:T(8,128)(2,1)S(1)}, bf16[1216,128]{1,0:T(8,128)(2,1)S(1)}, u32[]{:S(2)}, u32[]{:S(2)}) %collective-permute-start.3) | collective-permute-done | bytes 311328 | tf_op jit(solution)/shard_map/ppermute | solution.py:359
  22.3 0.5 collective-permute-start.9
  22.9 1.5 %collective-permute-done.8.w3 = bf16[256,512]{1,0:T(8,128)(2,1)S(1)} collective-permute-done((bf16[256,512]{1,0:T(8,128)(2,1)S(1)}, bf16[256,512]{1,0:T(8,128)(2,1)S(1)}, u32[]{:S(2)}, u32[]{:S(2)}) %collective-permute-start.8) | collective-permute-done | bytes 262176 | tf_op jit(solution)/shard_map/ppermute | solution.py:368
  24.3 1.0 %copy-done.2 = bf16[384,512]{1,0:T(8,128)(2,1)S(1)} copy-done((bf16[384,512]{1,0:T(8,128)(2,1)S(1)}, bf16[384,512]{1,0:T(8,128)(2,1)}, u32[]{:S(2)}) %copy-start.2) | copy-done | bytes 393240
  25.3 0.9 %copy-done.3 = bf16[256,512]{1,0:T(8,128)(2,1)S(1)} copy-done((bf16[256,512]{1,0:T(8,128)(2,1)S(1)}, bf16[256,512]{1,0:T(8,128)(2,1)}, u32[]{:S(2)}) %copy-start.3) | copy-done | bytes 262168
  26.3 0.9 %copy-done.7 = bf16[128,512]{1,0:T(8,128)(2,1)S(1)} copy-done((bf16[128,512]{1,0:T(8,128)(2,1)S(1)}, bf16[128,512]{1,0:T(8,128)(2,1)}, u32[]{:S(2)}) %copy-start.7) | copy-done | bytes 131096
  27.2 0.9 %copy-done.8 = bf16[128,512]{1,0:T(8,128)(2,1)S(1)} copy-done((bf16[128,512]{1,0:T(8,128)(2,1)S(1)}, bf16[128,512]{1,0:T(8,128)(2,1)}, u32[]{:S(2)}) %copy-start.8) | copy-done | bytes 131096
  28.1 0.1 shard_map.231
  28.2 0.6 collective-permute-start.13
  29.5 1.8 %shard_map.228 = (bf16[1024,512]{1,0:T(8,128)(2,1)S(1)}, bf16[2048,512]{1,0:T(8,128)(2,1)S(1)}) custom-call(f32[4,1024]{1,0:T(4,128)S(1)} %copy-done.15, f32[4,512]{1,0:T(4,128)S(1)} %copy-done.17, f32[4,2048]{1,0:T(4,128)S(1)} %copy-done.14, f32[4,512]{1,0:T(4,128)S(1)} %copy-done.18, bf16[1216,128]{1,0:T(8,128)(2,1)S(1)} %shard_map.227.after.l0), custom_call_target="tpu_custom_call" | custom-call | flops 402653184 | bytes 3522560 | tf_op jit(solution)/shard_map/pallas_call | solution.py:61
  31.2 1.5 %collective-permute-start.14 = (bf16[192,512]{1,0:T(8,128)(2,1)S(1)}, bf16[192,512]{1,0:T(8,128)(2,1)S(1)}, u32[]{:S(2)}, u32[]{:S(2)}) collective-permute-start(bf16[192,512]{1,0:T(8,128)(2,1)S(1)} %get-tuple-element.42), channel_id=1, source_target_pairs={{0,2},{1,3},{2,0},{3,1},{4,6},{5,7},{6,4},{7,5},{8,10},{9,11},{10,... | collective-permute-start | bytes 589832 | tf_op jit(solution)/shard_map/ppermute | solution.py:359
  32.8 0.0 copy-start.4
  32.8 0.0 copy-start.9
  32.8 0.0 copy-start.10
  32.9 4.8 %shard_map.229 = (bf16[256,512]{1,0:T(8,128)(2,1)S(1)}, bf16[256,512]{1,0:T(8,128)(2,1)S(1)}, bf16[256,512]{1,0:T(8,128)(2,1)S(1)}) custom-call(bf16[1024,512]{1,0:T(8,128)(2,1)S(1)} %get-tuple-element.35.emb, s32[2,1024]{1,0:T(2,128)S(1)} %copy-done.19, f32[1,512]{1,0:T(1,128)S(1)} %bitcast.6, bf16[1216,128]{1,0:T(8,128)(2,1)S(1)} %shard_map.227.after.l0, ...), custom_call_target="tpu_custom_call" | custom-call | flops 2952790016 | bytes 5187588 | tf_op jit(solution)/shard_map/pallas_call | solution.py:61
  37.6 0.1 collective-permute-start.11
  37.7 0.6 collective-permute-start.19
  38.3 0.5 collective-permute-start.15
  38.8 0.4 collective-permute-done.11.theirs
  39.2 0.1 shard_map.230.mine
  39.3 0.0 copy-start.12
  39.3 1.1 %collective-permute-start.12 = (bf16[256,512]{1,0:T(8,128)(2,1)S(1)}, bf16[256,512]{1,0:T(8,128)(2,1)S(1)}, u32[]{:S(2)}, u32[]{:S(2)}) collective-permute-start(bf16[256,512]{1,0:T(8,128)(2,1)S(1)} %shard_map.230.mine), channel_id=1, source_target_pairs={{0,2},{1,3},{2,0},{3,1},{4,6},{5,7},{6,4},{7,5},{8,10},{9,11},{10,... | collective-permute-start | bytes 786440 | tf_op jit(solution)/shard_map/ppermute | solution.py:359
  40.5 6.4 %collective-permute-done.19.w2 = bf16[256,512]{1,0:T(8,128)(2,1)S(1)} collective-permute-done((bf16[256,512]{1,0:T(8,128)(2,1)S(1)}, bf16[256,512]{1,0:T(8,128)(2,1)S(1)}, u32[]{:S(2)}, u32[]{:S(2)}) %collective-permute-start.19) | collective-permute-done | bytes 262176 | tf_op jit(solution)/shard_map/ppermute | solution.py:359
  46.9 0.5 collective-permute-start.20
  47.4 0.5 collective-permute-start.17
  47.9 0.9 %collective-permute-done.16.w4 = bf16[192,512]{1,0:T(8,128)(2,1)S(1)} collective-permute-done((bf16[192,512]{1,0:T(8,128)(2,1)S(1)}, bf16[192,512]{1,0:T(8,128)(2,1)S(1)}, u32[]{:S(2)}, u32[]{:S(2)}) %collective-permute-start.16) | collective-permute-done | bytes 196640 | tf_op jit(solution)/shard_map/ppermute | solution.py:363
  48.8 0.3 collective-permute-done.17.w5
  49.1 2.9 %collective-permute-done.12.theirs = bf16[256,512]{1,0:T(8,128)(2,1)S(1)} collective-permute-done((bf16[256,512]{1,0:T(8,128)(2,1)S(1)}, bf16[256,512]{1,0:T(8,128)(2,1)S(1)}, u32[]{:S(2)}, u32[]{:S(2)}) %collective-permute-start.12) | collective-permute-done | bytes 262176 | tf_op jit(solution)/shard_map/ppermute | solution.py:359
  52.1 0.0 copy-start.16
  52.1 1.0 %shard_map.232 = (bf16[256,512]{1,0:T(8,128)(2,1)S(1)}, bf16[384,512]{1,0:T(8,128)(2,1)S(1)}) custom-call(bf16[256,512]{1,0:T(8,128)(2,1)S(1)} %get-tuple-element.38.mesh, bf16[256,512]{1,0:T(8,128)(2,1)S(1)} %shard_map.230.mine, bf16[256,512]{1,0:T(8,128)(2,1)S(1)} %collective-permute-done.12.theirs, f32[1,512]{1,0:T(1,128)S(1)} %bitcast.4, ...), custom_call_target="tpu_custom_call" | custom-call | flops 402653184 | bytes 4458496 | tf_op jit(solution)/shard_map/pallas_call | solution.py:61
  53.1 0.1 collective-permute-start.18
  53.2 0.5 collective-permute-start.21
  53.7 0.6 collective-permute-done.20.w3
  55.0 0.6 collective-permute-start.29
  55.6 0.4 shard_map.233
  56.0 0.0 collective-permute-start.23
  56.0 1.9 %collective-permute-start.24 = (bf16[32,512]{1,0:T(8,128)(2,1)S(1)}, bf16[32,512]{1,0:T(8,128)(2,1)S(1)}, u32[]{:S(2)}, u32[]{:S(2)}) collective-permute-start(bf16[32,512]{1,0:T(8,128)(2,1)S(1)} %get-tuple-element.52), channel_id=1, source_target_pairs={{0,8},{4,12},{8,0},{12,4},{1,9},{5,13},{9,1},{13,5},{2,10},{6,14},... | collective-permute-start | bytes 98312 | tf_op jit(solution)/shard_map/ppermute | solution.py:483
  57.9 3.7 %collective-permute-start.25 = (bf16[32,512]{1,0:T(8,128)(2,1)S(1)}, bf16[32,512]{1,0:T(8,128)(2,1)S(1)}, u32[]{:S(2)}, u32[]{:S(2)}) collective-permute-start(bf16[32,512]{1,0:T(8,128)(2,1)S(1)} %get-tuple-element.53), channel_id=1, source_target_pairs={{4,8},{8,4},{5,9},{9,5},{6,10},{10,6},{7,11},{11,7},{20,24},{24,20... | collective-permute-start | bytes 98312 | tf_op jit(solution)/shard_map/ppermute | solution.py:483
  61.6 0.0 copy-start.21
  61.6 2.6 %shard_map.234 = (bf16[1536,512]{1,0:T(8,128)(2,1)S(1)}, f32[1024,512]{1,0:T(8,128)S(1)}, bf16[512,512]{1,0:T(8,128)(2,1)S(1)}, bf16[512,512]{1,0:T(8,128)(2,1)S(1)}) custom-call(bf16[2048,512]{1,0:T(8,128)(2,1)S(1)} %get-tuple-element.45.emb, bf16[512,512]{1,0:T(8,128)(2,1)S(1)} %get-tuple-element.44.full, s32[2,2048]{1,0:T(2,128)S(1)} %copy-done.16, ...), custom_call_target="tpu_custom_call" | custom-call | flops 1610612736 | bytes 10240000 | tf_op jit(solution)/shard_map/pallas_call | solution.py:61
  64.3 0.0 copy-start.13
  64.3 5.8 %shard_map.235 = (bf16[256,512]{1,0:T(8,128)(2,1)S(1)}, bf16[256,512]{1,0:T(8,128)(2,1)S(1)}) custom-call(bf16[2048,512]{1,0:T(8,128)(2,1)S(1)} %get-tuple-element.45.emb, s32[2,2048]{1,0:T(2,128)S(1)} %copy-done.16, f32[1,512]{1,0:T(1,128)S(1)} %bitcast.7, bf16[1536,512]{1,0:T(8,128)(2,1)S(1)} %get-tuple-element.47.table, ...), custom_call_target="tpu_custom_call" | custom-call | flops 3489660928 | bytes 7456772 | tf_op jit(solution)/shard_map/pallas_call | solution.py:61
  70.1 0.1 collective-permute-start.26
  70.2 0.5 collective-permute-start.28
  70.7 0.1 collective-permute-start.30
  70.7 0.9 %collective-permute-done.26.theirs = bf16[256,512]{1,0:T(8,128)(2,1)S(1)} collective-permute-done((bf16[256,512]{1,0:T(8,128)(2,1)S(1)}, bf16[256,512]{1,0:T(8,128)(2,1)S(1)}, u32[]{:S(2)}, u32[]{:S(2)}) %collective-permute-start.26) | collective-permute-done | bytes 262176 | tf_op jit(solution)/shard_map/ppermute | solution.py:363
  71.7 0.1 shard_map.236
  71.7 1.5 %collective-permute-start.27 = (bf16[128,512]{1,0:T(8,128)(2,1)S(1)}, bf16[128,512]{1,0:T(8,128)(2,1)S(1)}, u32[]{:S(2)}, u32[]{:S(2)}) collective-permute-start(bf16[128,512]{1,0:T(8,128)(2,1)S(1)} %get-tuple-element.57), channel_id=1, source_target_pairs={{0,2},{1,3},{2,0},{3,1},{4,6},{5,7},{6,4},{7,5},{8,10},{9,11},{10,... | collective-permute-start | bytes 393224 | tf_op jit(solution)/shard_map/ppermute | solution.py:359
  73.3 4.1 %collective-permute-done.27.theirs = bf16[128,512]{1,0:T(8,128)(2,1)S(1)} collective-permute-done((bf16[128,512]{1,0:T(8,128)(2,1)S(1)}, bf16[128,512]{1,0:T(8,128)(2,1)S(1)}, u32[]{:S(2)}, u32[]{:S(2)}) %collective-permute-start.27) | collective-permute-done | bytes 131104 | tf_op jit(solution)/shard_map/ppermute | solution.py:359
  77.4 1.5 %shard_map.237 = bf16[128,512]{1,0:T(8,128)(2,1)} custom-call(bf16[512,512]{1,0:T(8,128)(2,1)S(1)} %get-tuple-element.44.full, bf16[128,512]{1,0:T(8,128)(2,1)S(1)} %get-tuple-element.56.mine, bf16[128,512]{1,0:T(8,128)(2,1)S(1)} %collective-permute-done.27.theirs, f32[1,512]{1,0:T(1,128)S(1)} %bitcast.5, bf16[384,512]{1,0:T(8,128)(2,1)S(1)} %get-tuple-element.58.w0, ...), custom_call_target="tpu_custom_call" | custom-call | flops 201326592 | bytes 2492416 | tf_op jit(solution)/shard_map/pallas_call | solution.py:61
  (54 shorter events, 0.1 us)
Async XLA Ops:
  0.0 0.9 %copy-start = (bf16[512,128]{1,0:T(8,128)(2,1)S(1)}, bf16[512,128]{1,0:T(8,128)(2,1)}, u32[]{:S(2)}) copy-start(bf16[512,128]{1,0:T(8,128)(2,1)} %refs_0_.1) | copy-start | bytes 393220
  0.9 1.0 %copy-start.1 = (bf16[384,512]{1,0:T(8,128)(2,1)S(1)}, bf16[384,512]{1,0:T(8,128)(2,1)}, u32[]{:S(2)}) copy-start(bf16[384,512]{1,0:T(8,128)(2,1)} %w_in.1) | copy-start | bytes 1179652
  1.9 0.9 %copy-start.5 = (bf16[128,512]{1,0:T(8,128)(2,1)S(1)}, bf16[128,512]{1,0:T(8,128)(2,1)}, u32[]{:S(2)}) copy-start(bf16[128,512]{1,0:T(8,128)(2,1)} %w_out.1) | copy-start | bytes 393220
  2.8 0.7 copy-start.11
  3.5 25.9 %copy-start.14 = (f32[4,2048]{1,0:T(4,128)S(1)}, f32[4,2048]{1,0:T(4,128)}, u32[]{:S(2)}) copy-start(f32[4,2048]{1,0:T(4,128)} %pgeom.1) | copy-start | bytes 98308
  3.5 25.9 %copy-start.15 = (f32[4,1024]{1,0:T(4,128)S(1)}, f32[4,1024]{1,0:T(4,128)}, u32[]{:S(2)}) copy-start(f32[4,1024]{1,0:T(4,128)} %egeom.1) | copy-start | bytes 49156
  3.5 26.0 %copy-start.17 = (f32[4,512]{1,0:T(4,128)S(1)}, f32[4,512]{1,0:T(4,128)}, u32[]{:S(2)}) copy-start(f32[4,512]{1,0:T(4,128)} %egeo.1) | copy-start | bytes 24580
  3.5 26.0 %copy-start.18 = (f32[4,512]{1,0:T(4,128)S(1)}, f32[4,512]{1,0:T(4,128)}, u32[]{:S(2)}) copy-start(f32[4,512]{1,0:T(4,128)} %pgeo.1) | copy-start | bytes 24580
  3.5 29.3 %copy-start.19 = (s32[2,1024]{1,0:T(2,128)S(1)}, s32[2,1024]{1,0:T(2,128)}, u32[]{:S(2)}) copy-start(s32[2,1024]{1,0:T(2,128)} %edges.3) | copy-start | bytes 24580
  3.5 29.3 %copy-start.20 = (f32[512]{0:T(512)S(1)}, f32[512]{0:T(512)}, u32[]{:S(2)}) copy-start(f32[512]{0:T(512)} %param.44) | copy-start | bytes 6148
  3.9 11.8 %collective-permute-start.7 = (bf16[256,512]{1,0:T(8,128)(2,1)S(1)}, bf16[256,512]{1,0:T(8,128)(2,1)S(1)}, u32[]{:S(2)}, u32[]{:S(2)}) collective-permute-start(bf16[256,512]{1,0:T(8,128)(2,1)S(1)} %get-tuple-element.37), channel_id=1, source_target_pairs={{0,2},{1,3},{2,0},{3,1},{4,6},{5,7},{6,4},{7,5},{8,10},{9,11},{10,... | collective-permute-start | bytes 786440 | tf_op jit(solution)/shard_map/ppermute | solution.py:359
  5.4 5.4 %collective-permute-start = (bf16[64,128]{1,0:T(8,128)(2,1)S(1)}, bf16[64,128]{1,0:T(8,128)(2,1)S(1)}, u32[]{:S(2)}, u32[]{:S(2)}) collective-permute-start(bf16[64,128]{1,0:T(8,128)(2,1)S(1)} %get-tuple-element.32), channel_id=1, source_target_pairs={{0,4},{4,0},{8,12},{12,8},{1,5},{5,1},{9,13},{13,9},{2,6},{6,2},{1... | collective-permute-start | bytes 49160 | tf_op jit(solution)/shard_map/ppermute | solution.py:423
  5.9 5.0 %collective-permute-start.1 = (bf16[64,128]{1,0:T(8,128)(2,1)S(1)}, bf16[64,128]{1,0:T(8,128)(2,1)S(1)}, u32[]{:S(2)}, u32[]{:S(2)}) collective-permute-start(bf16[64,128]{1,0:T(8,128)(2,1)S(1)} %get-tuple-element.33), channel_id=1, source_target_pairs={{0,8},{4,12},{8,0},{12,4},{1,9},{5,13},{9,1},{13,5},{2,10},{6,14},... | collective-permute-start | bytes 49160 | tf_op jit(solution)/shard_map/ppermute | solution.py:423
  8.5 5.6 %collective-permute-start.2 = (bf16[64,128]{1,0:T(8,128)(2,1)S(1)}, bf16[64,128]{1,0:T(8,128)(2,1)S(1)}, u32[]{:S(2)}, u32[]{:S(2)}) collective-permute-start(bf16[64,128]{1,0:T(8,128)(2,1)S(1)} %get-tuple-element.34), channel_id=1, source_target_pairs={{4,8},{8,4},{5,9},{9,5},{6,10},{10,6},{7,11},{11,7},{20,24},{24,20... | collective-permute-start | bytes 49160 | tf_op jit(solution)/shard_map/ppermute | solution.py:423
  14.1 0.9 %copy-start.6 = (bf16[512,128]{1,0:T(8,128)(2,1)S(1)}, bf16[512,128]{1,0:T(8,128)(2,1)}, u32[]{:S(2)}) copy-start(bf16[512,128]{1,0:T(8,128)(2,1)} %refs_1_.1) | copy-start | bytes 393220
  15.0 7.3 %collective-permute-start.3 = (bf16[1216,128]{1,0:T(8,128)(2,1)S(1)}, bf16[1216,128]{1,0:T(8,128)(2,1)S(1)}, u32[]{:S(2)}, u32[]{:S(2)}) collective-permute-start(bf16[1216,128]{1,0:T(8,128)(2,1)S(1)} %shard_map.227.after.l0), channel_id=1, source_target_pairs={{0,2},{1,3},{2,0},{3,1},{4,6},{5,7},{6,4},{7,5},{8,10},{9,11},{10,... | collective-permute-start | bytes 933896 | tf_op jit(solution)/shard_map/ppermute | solution.py:359
  15.6 17.2 %collective-permute-start.6 = (bf16[512,512]{1,0:T(8,128)(2,1)S(1)}, bf16[512,512]{1,0:T(8,128)(2,1)S(1)}, u32[]{:S(2)}, u32[]{:S(2)}) collective-permute-start(bf16[512,512]{1,0:T(8,128)(2,1)S(1)} %get-tuple-element.36.w0), channel_id=1, source_target_pairs={{0,1},{1,0},{2,3},{3,2},{4,5},{5,4},{6,7},{7,6},{8,9},{9,8},{10,11... | collective-permute-start | bytes 1572872 | tf_op jit(solution)/shard_map/ppermute | solution.py:363
  15.6 8.7 %collective-permute-start.8 = (bf16[256,512]{1,0:T(8,128)(2,1)S(1)}, bf16[256,512]{1,0:T(8,128)(2,1)S(1)}, u32[]{:S(2)}, u32[]{:S(2)}) collective-permute-start(bf16[256,512]{1,0:T(8,128)(2,1)S(1)} %collective-permute-done.7.w2), channel_id=1, source_target_pairs={{0,16},{16,0},{1,17},{17,1},{2,18},{18,2},{3,19},{19,3},{4,20},{20... | collective-permute-start | bytes 786440 | tf_op jit(solution)/shard_map/ppermute | solution.py:368
  16.1 12.1 %collective-permute-start.4 = (bf16[1216,128]{1,0:T(8,128)(2,1)S(1)}, bf16[1216,128]{1,0:T(8,128)(2,1)S(1)}, u32[]{:S(2)}, u32[]{:S(2)}) collective-permute-start(bf16[1216,128]{1,0:T(8,128)(2,1)S(1)} %shard_map.227.after.l0), channel_id=1, source_target_pairs={{0,1},{1,0},{2,3},{3,2},{4,5},{5,4},{6,7},{7,6},{8,9},{9,8},{10,11... | collective-permute-start | bytes 933896 | tf_op jit(solution)/shard_map/ppermute | solution.py:363
  22.3 10.4 %collective-permute-start.5 = (bf16[1216,128]{1,0:T(8,128)(2,1)S(1)}, bf16[1216,128]{1,0:T(8,128)(2,1)S(1)}, u32[]{:S(2)}, u32[]{:S(2)}) collective-permute-start(bf16[1216,128]{1,0:T(8,128)(2,1)S(1)} %collective-permute-done.3.l1.after), channel_id=1, source_target_pairs={{0,1},{1,0},{2,3},{3,2},{4,5},{5,4},{6,7},{7,6},{8,9},{9,8},{10,11... | collective-permute-start | bytes 933896 | tf_op jit(solution)/shard_map/ppermute | solution.py:363
  22.3 8.9 %collective-permute-start.9 = (bf16[256,512]{1,0:T(8,128)(2,1)S(1)}, bf16[256,512]{1,0:T(8,128)(2,1)S(1)}, u32[]{:S(2)}, u32[]{:S(2)}) collective-permute-start(bf16[256,512]{1,0:T(8,128)(2,1)S(1)} %collective-permute-done.7.w2), channel_id=1, source_target_pairs={{0,1},{1,0},{2,3},{3,2},{4,5},{5,4},{6,7},{7,6},{8,9},{9,8},{10,11... | collective-permute-start | bytes 786440 | tf_op jit(solution)/shard_map/ppermute | solution.py:363
  24.3 8.5 %collective-permute-start.10 = (bf16[256,512]{1,0:T(8,128)(2,1)S(1)}, bf16[256,512]{1,0:T(8,128)(2,1)S(1)}, u32[]{:S(2)}, u32[]{:S(2)}) collective-permute-start(bf16[256,512]{1,0:T(8,128)(2,1)S(1)} %collective-permute-done.8.w3), channel_id=1, source_target_pairs={{0,1},{1,0},{2,3},{3,2},{4,5},{5,4},{6,7},{7,6},{8,9},{9,8},{10,11... | collective-permute-start | bytes 786440 | tf_op jit(solution)/shard_map/ppermute | solution.py:363
  24.3 1.0 %copy-start.2 = (bf16[384,512]{1,0:T(8,128)(2,1)S(1)}, bf16[384,512]{1,0:T(8,128)(2,1)}, u32[]{:S(2)}) copy-start(bf16[384,512]{1,0:T(8,128)(2,1)} %p_in.1) | copy-start | bytes 1179652
  25.3 0.9 %copy-start.3 = (bf16[256,512]{1,0:T(8,128)(2,1)S(1)}, bf16[256,512]{1,0:T(8,128)(2,1)}, u32[]{:S(2)}) copy-start(bf16[256,512]{1,0:T(8,128)(2,1)} %e_in.1) | copy-start | bytes 786436
  26.3 0.9 %copy-start.7 = (bf16[128,512]{1,0:T(8,128)(2,1)S(1)}, bf16[128,512]{1,0:T(8,128)(2,1)}, u32[]{:S(2)}) copy-start(bf16[128,512]{1,0:T(8,128)(2,1)} %e_out.1) | copy-start | bytes 393220
  27.2 0.9 %copy-start.8 = (bf16[128,512]{1,0:T(8,128)(2,1)S(1)}, bf16[128,512]{1,0:T(8,128)(2,1)}, u32[]{:S(2)}) copy-start(bf16[128,512]{1,0:T(8,128)(2,1)} %p_out.1) | copy-start | bytes 393220
  28.2 20.9 %collective-permute-start.13 = (bf16[896,512]{1,0:T(8,128)(2,1)S(1)}, bf16[896,512]{1,0:T(8,128)(2,1)S(1)}, u32[]{:S(2)}, u32[]{:S(2)}) collective-permute-start(bf16[896,512]{1,0:T(8,128)(2,1)S(1)} %get-tuple-element.41.w0), channel_id=1, source_target_pairs={{0,1},{1,0},{2,3},{3,2},{4,5},{5,4},{6,7},{7,6},{8,9},{9,8},{10,11... | collective-permute-start | bytes 2752520 | tf_op jit(solution)/shard_map/ppermute | solution.py:363
  31.2 7.1 %collective-permute-start.14 = (bf16[192,512]{1,0:T(8,128)(2,1)S(1)}, bf16[192,512]{1,0:T(8,128)(2,1)S(1)}, u32[]{:S(2)}, u32[]{:S(2)}) collective-permute-start(bf16[192,512]{1,0:T(8,128)(2,1)S(1)} %get-tuple-element.42), channel_id=1, source_target_pairs={{0,2},{1,3},{2,0},{3,1},{4,6},{5,7},{6,4},{7,5},{8,10},{9,11},{10,... | collective-permute-start | bytes 589832 | tf_op jit(solution)/shard_map/ppermute | solution.py:359
  32.8 19.2 %copy-start.4 = (bf16[256,512]{1,0:T(8,128)(2,1)S(1)}, bf16[256,512]{1,0:T(8,128)(2,1)}, u32[]{:S(2)}) copy-start(bf16[256,512]{1,0:T(8,128)(2,1)} %n_in.1) | copy-start | bytes 786436
  32.8 19.2 %copy-start.9 = (bf16[128,512]{1,0:T(8,128)(2,1)S(1)}, bf16[128,512]{1,0:T(8,128)(2,1)}, u32[]{:S(2)}) copy-start(bf16[128,512]{1,0:T(8,128)(2,1)} %n_out.1) | copy-start | bytes 393220
  32.8 19.2 %copy-start.10 = (f32[512]{0:T(512)S(1)}, f32[512]{0:T(512)}, u32[]{:S(2)}) copy-start(f32[512]{0:T(512)} %param.45) | copy-start | bytes 6148
  37.6 1.6 %collective-permute-start.11 = (bf16[256,512]{1,0:T(8,128)(2,1)S(1)}, bf16[256,512]{1,0:T(8,128)(2,1)S(1)}, u32[]{:S(2)}, u32[]{:S(2)}) collective-permute-start(bf16[256,512]{1,0:T(8,128)(2,1)S(1)} %get-tuple-element.40), channel_id=1, source_target_pairs={{0,1},{1,0},{2,3},{3,2},{4,5},{5,4},{6,7},{7,6},{8,9},{9,8},{10,11... | collective-permute-start | bytes 786440 | tf_op jit(solution)/shard_map/ppermute | solution.py:363
  37.7 9.2 %collective-permute-start.19 = (bf16[256,512]{1,0:T(8,128)(2,1)S(1)}, bf16[256,512]{1,0:T(8,128)(2,1)S(1)}, u32[]{:S(2)}, u32[]{:S(2)}) collective-permute-start(bf16[256,512]{1,0:T(8,128)(2,1)S(1)} %get-tuple-element.46), channel_id=1, source_target_pairs={{0,2},{1,3},{2,0},{3,1},{4,6},{5,7},{6,4},{7,5},{8,10},{9,11},{10,... | collective-permute-start | bytes 786440 | tf_op jit(solution)/shard_map/ppermute | solution.py:359
  38.3 9.1 %collective-permute-start.15 = (bf16[192,512]{1,0:T(8,128)(2,1)S(1)}, bf16[192,512]{1,0:T(8,128)(2,1)S(1)}, u32[]{:S(2)}, u32[]{:S(2)}) collective-permute-start(bf16[192,512]{1,0:T(8,128)(2,1)S(1)} %collective-permute-done.14.w2), channel_id=1, source_target_pairs={{0,16},{16,0},{1,17},{17,1},{2,18},{18,2},{3,19},{19,3},{4,20},{20... | collective-permute-start | bytes 589832 | tf_op jit(solution)/shard_map/ppermute | solution.py:368
  39.3 16.3 %copy-start.12 = (s32[1,4,32]{2,1,0:T(4,128)S(1)}, s32[1,4,32]{2,1,0:T(4,128)}, u32[]{:S(2)}) copy-start(s32[1,4,32]{2,1,0:T(4,128)} %send.3) | copy-start | bytes 1540
  39.3 12.7 %collective-permute-start.12 = (bf16[256,512]{1,0:T(8,128)(2,1)S(1)}, bf16[256,512]{1,0:T(8,128)(2,1)S(1)}, u32[]{:S(2)}, u32[]{:S(2)}) collective-permute-start(bf16[256,512]{1,0:T(8,128)(2,1)S(1)} %shard_map.230.mine), channel_id=1, source_target_pairs={{0,2},{1,3},{2,0},{3,1},{4,6},{5,7},{6,4},{7,5},{8,10},{9,11},{10,... | collective-permute-start | bytes 786440 | tf_op jit(solution)/shard_map/ppermute | solution.py:359
  46.9 7.4 %collective-permute-start.20 = (bf16[256,512]{1,0:T(8,128)(2,1)S(1)}, bf16[256,512]{1,0:T(8,128)(2,1)S(1)}, u32[]{:S(2)}, u32[]{:S(2)}) collective-permute-start(bf16[256,512]{1,0:T(8,128)(2,1)S(1)} %collective-permute-done.19.w2), channel_id=1, source_target_pairs={{0,16},{16,0},{1,17},{17,1},{2,18},{18,2},{3,19},{19,3},{4,20},{20... | collective-permute-start | bytes 786440 | tf_op jit(solution)/shard_map/ppermute | solution.py:368
  47.4 1.4 %collective-permute-start.16 = (bf16[192,512]{1,0:T(8,128)(2,1)S(1)}, bf16[192,512]{1,0:T(8,128)(2,1)S(1)}, u32[]{:S(2)}, u32[]{:S(2)}) collective-permute-start(bf16[192,512]{1,0:T(8,128)(2,1)S(1)} %collective-permute-done.14.w2), channel_id=1, source_target_pairs={{0,1},{1,0},{2,3},{3,2},{4,5},{5,4},{6,7},{7,6},{8,9},{9,8},{10,11... | collective-permute-start | bytes 589832 | tf_op jit(solution)/shard_map/ppermute | solution.py:363
  47.4 1.7 %collective-permute-start.17 = (bf16[192,512]{1,0:T(8,128)(2,1)S(1)}, bf16[192,512]{1,0:T(8,128)(2,1)S(1)}, u32[]{:S(2)}, u32[]{:S(2)}) collective-permute-start(bf16[192,512]{1,0:T(8,128)(2,1)S(1)} %collective-permute-done.15.w3), channel_id=1, source_target_pairs={{0,1},{1,0},{2,3},{3,2},{4,5},{5,4},{6,7},{7,6},{8,9},{9,8},{10,11... | collective-permute-start | bytes 589832 | tf_op jit(solution)/shard_map/ppermute | solution.py:363
  52.1 9.5 %copy-start.16 = (s32[2,2048]{1,0:T(2,128)S(1)}, s32[2,2048]{1,0:T(2,128)}, u32[]{:S(2)}) copy-start(s32[2,2048]{1,0:T(2,128)} %edges.5) | copy-start | bytes 49156
  53.1 2.5 %collective-permute-start.18 = (bf16[256,512]{1,0:T(8,128)(2,1)S(1)}, bf16[256,512]{1,0:T(8,128)(2,1)S(1)}, u32[]{:S(2)}, u32[]{:S(2)}) collective-permute-start(bf16[256,512]{1,0:T(8,128)(2,1)S(1)} %get-tuple-element.43.mine), channel_id=1, source_target_pairs={{0,1},{1,0},{2,3},{3,2},{4,5},{5,4},{6,7},{7,6},{8,9},{9,8},{10,11... | collective-permute-start | bytes 786440 | tf_op jit(solution)/shard_map/ppermute | solution.py:363
  53.2 4.7 %collective-permute-start.21 = (bf16[256,512]{1,0:T(8,128)(2,1)S(1)}, bf16[256,512]{1,0:T(8,128)(2,1)S(1)}, u32[]{:S(2)}, u32[]{:S(2)}) collective-permute-start(bf16[256,512]{1,0:T(8,128)(2,1)S(1)} %collective-permute-done.19.w2), channel_id=1, source_target_pairs={{0,1},{1,0},{2,3},{3,2},{4,5},{5,4},{6,7},{7,6},{8,9},{9,8},{10,11... | collective-permute-start | bytes 786440 | tf_op jit(solution)/shard_map/ppermute | solution.py:363
  54.3 7.3 %collective-permute-start.22 = (bf16[256,512]{1,0:T(8,128)(2,1)S(1)}, bf16[256,512]{1,0:T(8,128)(2,1)S(1)}, u32[]{:S(2)}, u32[]{:S(2)}) collective-permute-start(bf16[256,512]{1,0:T(8,128)(2,1)S(1)} %collective-permute-done.20.w3), channel_id=1, source_target_pairs={{0,1},{1,0},{2,3},{3,2},{4,5},{5,4},{6,7},{7,6},{8,9},{9,8},{10,11... | collective-permute-start | bytes 786440 | tf_op jit(solution)/shard_map/ppermute | solution.py:363
  55.0 15.7 %collective-permute-start.29 = (bf16[384,512]{1,0:T(8,128)(2,1)S(1)}, bf16[384,512]{1,0:T(8,128)(2,1)S(1)}, u32[]{:S(2)}, u32[]{:S(2)}) collective-permute-start(bf16[384,512]{1,0:T(8,128)(2,1)S(1)} %get-tuple-element.58.w0), channel_id=1, source_target_pairs={{0,2},{1,3},{2,0},{3,1},{4,6},{5,7},{6,4},{7,5},{8,10},{9,11},{10,... | collective-permute-start | bytes 1179656 | tf_op jit(solution)/shard_map/ppermute | solution.py:359
  56.0 8.2 %collective-permute-start.23 = (bf16[32,512]{1,0:T(8,128)(2,1)S(1)}, bf16[32,512]{1,0:T(8,128)(2,1)S(1)}, u32[]{:S(2)}, u32[]{:S(2)}) collective-permute-start(bf16[32,512]{1,0:T(8,128)(2,1)S(1)} %get-tuple-element.51), channel_id=1, source_target_pairs={{0,4},{4,0},{8,12},{12,8},{1,5},{5,1},{9,13},{13,9},{2,6},{6,2},{1... | collective-permute-start | bytes 98312 | tf_op jit(solution)/shard_map/ppermute | solution.py:483
  56.0 8.2 %collective-permute-start.24 = (bf16[32,512]{1,0:T(8,128)(2,1)S(1)}, bf16[32,512]{1,0:T(8,128)(2,1)S(1)}, u32[]{:S(2)}, u32[]{:S(2)}) collective-permute-start(bf16[32,512]{1,0:T(8,128)(2,1)S(1)} %get-tuple-element.52), channel_id=1, source_target_pairs={{0,8},{4,12},{8,0},{12,4},{1,9},{5,13},{9,1},{13,5},{2,10},{6,14},... | collective-permute-start | bytes 98312 | tf_op jit(solution)/shard_map/ppermute | solution.py:483
  57.9 6.3 %collective-permute-start.25 = (bf16[32,512]{1,0:T(8,128)(2,1)S(1)}, bf16[32,512]{1,0:T(8,128)(2,1)S(1)}, u32[]{:S(2)}, u32[]{:S(2)}) collective-permute-start(bf16[32,512]{1,0:T(8,128)(2,1)S(1)} %get-tuple-element.53), channel_id=1, source_target_pairs={{4,8},{8,4},{5,9},{9,5},{6,10},{10,6},{7,11},{11,7},{20,24},{24,20... | collective-permute-start | bytes 98312 | tf_op jit(solution)/shard_map/ppermute | solution.py:483
  61.6 2.6 %copy-start.21 = (f32[512]{0:T(512)S(1)}, f32[512]{0:T(512)}, u32[]{:S(2)}) copy-start(f32[512]{0:T(512)} %param.46) | copy-start | bytes 6148
  64.3 13.1 %copy-start.13 = (f32[512]{0:T(512)S(1)}, f32[512]{0:T(512)}, u32[]{:S(2)}) copy-start(f32[512]{0:T(512)} %param.47) | copy-start | bytes 6148
  70.1 1.6 %collective-permute-start.26 = (bf16[256,512]{1,0:T(8,128)(2,1)S(1)}, bf16[256,512]{1,0:T(8,128)(2,1)S(1)}, u32[]{:S(2)}, u32[]{:S(2)}) collective-permute-start(bf16[256,512]{1,0:T(8,128)(2,1)S(1)} %get-tuple-element.55), channel_id=1, source_target_pairs={{0,1},{1,0},{2,3},{3,2},{4,5},{5,4},{6,7},{7,6},{8,9},{9,8},{10,11... | collective-permute-start | bytes 786440 | tf_op jit(solution)/shard_map/ppermute | solution.py:363
  70.2 3.1 %collective-permute-start.28 = (bf16[384,512]{1,0:T(8,128)(2,1)S(1)}, bf16[384,512]{1,0:T(8,128)(2,1)S(1)}, u32[]{:S(2)}, u32[]{:S(2)}) collective-permute-start(bf16[384,512]{1,0:T(8,128)(2,1)S(1)} %get-tuple-element.58.w0), channel_id=1, source_target_pairs={{0,1},{1,0},{2,3},{3,2},{4,5},{5,4},{6,7},{7,6},{8,9},{9,8},{10,11... | collective-permute-start | bytes 1179656 | tf_op jit(solution)/shard_map/ppermute | solution.py:363
  70.7 6.7 %collective-permute-start.30 = (bf16[384,512]{1,0:T(8,128)(2,1)S(1)}, bf16[384,512]{1,0:T(8,128)(2,1)S(1)}, u32[]{:S(2)}, u32[]{:S(2)}) collective-permute-start(bf16[384,512]{1,0:T(8,128)(2,1)S(1)} %collective-permute-done.29.w2), channel_id=1, source_target_pairs={{0,1},{1,0},{2,3},{3,2},{4,5},{5,4},{6,7},{7,6},{8,9},{9,8},{10,11... | collective-permute-start | bytes 1179656 | tf_op jit(solution)/shard_map/ppermute | solution.py:363
  71.7 5.6 %collective-permute-start.27 = (bf16[128,512]{1,0:T(8,128)(2,1)S(1)}, bf16[128,512]{1,0:T(8,128)(2,1)S(1)}, u32[]{:S(2)}, u32[]{:S(2)}) collective-permute-start(bf16[128,512]{1,0:T(8,128)(2,1)S(1)} %get-tuple-element.57), channel_id=1, source_target_pairs={{0,2},{1,3},{2,0},{3,1},{4,6},{5,7},{6,4},{7,5},{8,10},{9,11},{10,... | collective-permute-start | bytes 393224 | tf_op jit(solution)/shard_map/ppermute | solution.py:359

commit v3 on v2

--- a/solution.py
+++ b/solution.py
@@ -11,6 +11,7 @@
 OFFSETS = (-2, -1, 1, 2)
 STEP = 512
 GATHERED = 1024
+VMEM_FULL = 64 * 1024 * 1024
 VMEM_BYTES = 24 * 1024 * 1024
 I16 = jnp.int16
 BF16 = jnp.bfloat16
@@ -53,18 +54,19 @@
     return [pl.BlockSpec(memory_space=pltpu.VMEM)] * count
 
 
-def call(body, outs, args, scratch=(), flops=0, smem=0):
+def call(body, outs, args, scratch=(), flops=0, smem=0, far=0, vmem=VMEM_BYTES):
     moved = sum(a.size * a.dtype.itemsize for a in args) + sum(
         o.size * jnp.dtype(o.dtype).itemsize for o in outs
     )
-    specs = whole_refs(len(args) - smem) + [pl.BlockSpec(memory_space=pltpu.SMEM)] * smem
+    specs = [pl.BlockSpec(memory_space=pltpu.HBM)] * far + whole_refs(len(args) - smem - far)
+    specs += [pl.BlockSpec(memory_space=pltpu.SMEM)] * smem
     return pl.pallas_call(
         body,
         out_shape=tuple(outs),
         in_specs=specs,
         out_specs=tuple(whole_refs(len(outs))),
         scratch_shapes=list(scratch),
-        compiler_params=pltpu.CompilerParams(vmem_limit_bytes=VMEM_BYTES),
+        compiler_params=pltpu.CompilerParams(vmem_limit_bytes=vmem),
         cost_estimate=pl.CostEstimate(flops=int(flops), bytes_accessed=int(moved), transcendentals=0),
     )(*args)
 
@@ -93,12 +95,6 @@
     return silu(dot_first(left, right)).astype(BF16)
 
 
-def embed_kernel(egeom, egeo, pgeom, pgeo, after, eout, pout):
-    for geom, geo, out in ((egeom, egeo, eout), (pgeom, pgeo, pout)):
-        for first in range(0, out.shape[0], STEP):
-            out[first : first + STEP, :] = embed_rows(geom[:, first : first + STEP], geo[...])
-
-
 def layer_norm(v):
     width = v.shape[-1]
     centered = v - jnp.sum(v, axis=-1, keepdims=True) * (1.0 / width)
@@ -122,11 +118,6 @@
         out[...] = pick_rows(table, send[0, pl.ds(region, 1), :])
 
 
-def half_of(whole, half):
-    rows = half.shape[0]
-    half[...] = whole[pl.ds(pl.multiple_of(lax.axis_index("groups") * rows, rows), rows), :]
-
-
 def stack_into(out, parts):
     first = 0
     for part in parts:
@@ -134,41 +125,80 @@
         first += part.shape[0]
 
 
-def first_pack_kernel(plan, grid, send, w_in, w_out, weights, half, *outs):
-    stack_into(weights, (w_in, w_out))
-    half_of(weights, half)
-    pick_lists(plan, grid[...], send, outs)
-
-
-def second_pack_kernel(e_in, e_out, p_in, p_out, after, weights, e_half, p_half):
+def fetch(sems, moves):
+    copies = [pltpu.make_async_copy(source, target, sems.at[k]) for k, (source, target) in enumerate(moves)]
+    for copy in copies:
+        copy.start()
+    return copies
+
+
+def own_half(ref):
+    rows = ref.shape[0] // 2
+    return ref.at[pl.ds(pl.multiple_of(lax.axis_index("groups") * rows, rows), rows), :]
+
+
+def first_pack_kernel(plan, grid, send, w_in, w_out, half, *rest):
+    outs = rest[: len(plan)]
+    listed, table, sems = rest[len(plan) :]
+    k, n = w_in.shape[0] // 2, w_out.shape[0] // 2
+    copies = fetch(
+        sems,
+        [
+            (send, listed),
+            (grid, table),
+            (own_half(w_in), half.at[pl.ds(0, k), :]),
+            (own_half(w_out), half.at[pl.ds(k, n), :]),
+        ],
+    )
+    copies[0].wait()
+    copies[1].wait()
+    pick_lists(plan, table[...], listed, outs)
+    copies[2].wait()
+    copies[3].wait()
+
+
+def embed_kernel(e_in, e_out, p_in, p_out, egeom, egeo, pgeom, pgeo, after, weights, eout, pout):
     stack_into(weights, (e_in, e_out, p_in, p_out))
-    rows = e_in.shape[0] + e_out.shape[0]
-    half_of(weights.at[:rows, :], e_half)
-    half_of(weights.at[rows:, :], p_half)
+    for geom, geo, out in ((egeom, egeo, eout), (pgeom, pgeo, pout)):
+        for begin in range(0, out.shape[0], STEP):
+            out[begin : begin + STEP, :] = embed_rows(geom[:, begin : begin + STEP], geo[...])
+
+
+def cross_kernel(rows_whole, k_in, weights, lat, crossing, lat_out):
+    lat_out[...] = lat[...]
+    crossing[:rows_whole, :] = weights[:rows_whole, :]
+    first, place = rows_whole, rows_whole
+    for rows in (k_in, weights.shape[0] - rows_whole - k_in):
+        half = rows // 2
+        begin = pl.multiple_of(first + lax.axis_index("groups") * half, 64)
+        crossing[place : place + half, :] = weights[pl.ds(begin, half), :]
+        first, place = first + rows, place + half
+
+
+def split_kernel(source, after, *outs):
+    first = 0
+    for out in outs:
+        out[...] = source[first : first + out.shape[0], :]
+        first += out.shape[0]
 
 
 def concat_kernel(*refs):
     stack_into(refs[-1], refs[:-1])
 
 
-def place_shards(target, refs, first=0):
-    own, beside, *halves = refs
-    quarter = lax.axis_index("sub")
-    group = lax.axis_index("groups")
+def put_shard(target, source, first, step, part=0, parts=1):
+    rows = target.shape[0] // (4 * parts)
+    place = (lax.bitwise_xor(lax.axis_index("sub"), step) * parts + part) * rows
+    target[pl.ds(pl.multiple_of(place, rows), rows), :] = source[first : first + rows, :]
+
+
+def put_half(target, k, source, first=0, step=0, other=0):
     rows = target.shape[0] // 4
-    for ref, step in ((own, 0), (beside, 1)):
-        place = pl.multiple_of(lax.bitwise_xor(quarter, step) * rows, rows)
-        target[pl.ds(place, rows), :] = ref[first : first + rows, :]
-    if len(halves) == 2:
-        for ref, step in zip(halves, (2, 3)):
-            place = pl.multiple_of(lax.bitwise_xor(quarter, step) * rows, rows)
-            target[pl.ds(place, rows), :] = ref[...]
-    else:
-        half = rows // 2
-        for ref, step, other in zip(halves, (2, 2, 3, 3), (0, 1, 0, 1)):
-            which = lax.bitwise_xor(group, other)
-            place = pl.multiple_of(lax.bitwise_xor(quarter, step) * rows + which * half, half)
-            target[pl.ds(place, half), :] = ref[...]
+    which = lax.bitwise_xor(lax.axis_index("groups"), other)
+    begin = lax.bitwise_xor(lax.axis_index("sub"), step) * rows
+    for base, count in ((0, k // 2), (k // 2, (rows - k) // 2)):
+        place = pl.multiple_of(begin + 2 * base + which * count, 64)
+        target[pl.ds(place, count), :] = source[first + base : first + base + count, :]
 
 
 def joined(stack, first, rows):
@@ -225,8 +255,8 @@
 
 
 def enc_kernel(
-    plan, slots, grid_rows, mesh_rows, k_in, emb, edges, gain, l0, l1, l2, l3, w0, w1, w2, w3, w4, w5,
-    live, keep, give, own_mesh, full, stack, table, messages, totals,
+    plan, slots, grid_rows, mesh_rows, k_in, emb, edges, gain, l0, l1, l2, l3, o_in, o_out, b_in, b_out,
+    across, round_, both, round_both, live, keep, give, own_mesh, full, stack, table, messages, totals,
 ):
     d = gain.shape[1]
     quarter = lax.axis_index("sub")
@@ -234,7 +264,15 @@
     for shard, step in zip((l0, l1, l2, l3), (0, 2, 1, 3)):
         place = pl.multiple_of(lax.bitwise_xor(quarter, step) * width, width)
         full[:, pl.ds(place, width)] = shard[...]
-    place_shards(stack, (w0, w1, w2, w3, w4, w5))
+    step = k_in + d // 4
+    for first, second, bit in ((o_in, o_out, 0), (b_in, b_out, 1)):
+        place = lax.bitwise_xor(quarter, bit) * step
+        stack[pl.ds(pl.multiple_of(place, 128), k_in), :] = first[...]
+        stack[pl.ds(pl.multiple_of(place + k_in, 128), d // 4), :] = second[...]
+    put_half(stack, k_in, across, 0, 2, 0)
+    put_half(stack, k_in, round_, 0, 2, 1)
+    put_half(stack, k_in, both, 0, 3, 0)
+    put_half(stack, k_in, round_both, 0, 3, 1)
     rows = mesh_rows // 4
     core = lax.rem(quarter, 2)
     for half in range(2):
@@ -278,8 +316,11 @@
     out[...] = add(mine[...], theirs[...])
 
 
-def node_kernel(k_in, k_out, mesh, mine, theirs, gain, n_in, n_out, w0, w1, w2, w3, w4, w5, out, packed, stack):
-    place_shards(stack, (w0, w1, w2, w3, w4, w5))
+def node_kernel(k_in, k_out, mesh, mine, theirs, gain, n_in, n_out, w0, w1, w2, w3, w4, out, packed, stack):
+    for shard, bit in zip((w0, w1, w2), (0, 1, 2)):
+        put_shard(stack, shard, 0, bit)
+    put_shard(stack, w3, 0, 3, 0, 2)
+    put_shard(stack, w4, 0, 3, 1, 2)
     w_in, w_out = joined(stack, 0, k_in), joined(stack, k_in, k_out)
     out[...] = node_update(mesh[...], add(mine[...], theirs[...]), w_in, w_out, gain[...])
     stack_into(packed, (n_in, n_out))
@@ -295,10 +336,15 @@
     pick_lists(plan, full[...], send, outs)
 
 
-def proc_first_kernel(k_in, first_row, emb, full, edges, w0, w1, w2, w3, w4, w5, table, pre, w_source, w_out, stack):
+def proc_first_kernel(k_in, first_row, emb, full, edges, w0, w1, across, both, round_, round_both, table, pre, w_source, w_out, stack):
     d = full.shape[1]
     node_rows = full.shape[0]
-    place_shards(stack, (w0, w1, w2, w3, w4, w5), first_row)
+    put_shard(stack, w0, first_row, 0)
+    put_shard(stack, w1, first_row, 1)
+    put_half(stack, k_in, across, 0, 2, 0)
+    put_half(stack, k_in, both, 0, 3, 0)
+    put_half(stack, k_in, round_, 0, 2, 1)
+    put_half(stack, k_in, round_both, 0, 3, 1)
     w_in = joined(stack, 0, k_in)
     w_out[...] = joined(stack, k_in, d // 4)
     w_source[...] = w_in[d : 2 * d, :]
@@ -350,7 +396,8 @@
 def out_kernel(k_in, k_out, full, mine, theirs, gain, w0, w1, w2, w3, out, stack):
     rows = mine.shape[0]
     mesh = full[pl.ds(pl.multiple_of(lax.axis_index("sub") * rows, rows), rows), :]
-    place_shards(stack, (w0, w1, w2, w3))
+    for shard, bit in zip((w0, w1, w2, w3), (0, 1, 2, 3)):
+        put_shard(stack, shard, 0, bit)
     w_in, w_out = joined(stack, 0, k_in), joined(stack, k_in, k_out)
     out[...] = node_update(mesh, add(mine[...], theirs[...]), w_in, w_out, gain[...])
 
@@ -414,32 +461,46 @@
     width = grid_lat.shape[1]
 
     slots = grid_send.shape[2]
-    edge_w, edge_half, *outgoing = call(
+    edge_half, *outgoing = call(
         functools.partial(first_pack_kernel, plan),
-        [shape(k_in + k_out, d), shape((k_in + k_out) // 2, d)] + [shape(slots, width)] * len(plan),
+        [shape((k_in + k_out) // 2, d)] + [shape(slots, width)] * len(plan),
         [grid_lat, grid_send, enc_edge_in, enc_edge_out],
+        scratch=[
+            pltpu.VMEM(grid_send.shape, jnp.int32),
+            pltpu.VMEM(grid_lat.shape, BF16),
+            pltpu.SemaphoreType.DMA((4,)),
+        ],
+        far=4,
+        vmem=VMEM_FULL - 512 * 1024,
     )
     edge_across = to_chip(edge_half)
     halos = [lax.ppermute(v, "dom", entry[0]) for v, entry in zip(outgoing, plan)]
     got = len(plan) * slots
-    (lat,) = call(concat_kernel, [shape(grid_rows + mesh_rows + got, width)], [grid_lat, mesh_lat, *halos])
+    (lat,) = call(
+        concat_kernel,
+        [shape(grid_rows + mesh_rows + got, width)],
+        [grid_lat, mesh_lat, *halos],
+    )
     lat_across = to_chip(lat)
     lat_beside = to_core(lat)
-    edge_beside = to_core(edge_w)
-    enc_emb, proc_emb = call(
+    edge_beside = [to_core(enc_edge_in), to_core(enc_edge_out)]
+    edge_round = to_group(edge_across)
+    next_w, enc_emb, proc_emb = call(
         embed_kernel,
-        [shape(n_enc, d), shape(n_proc, d)],
-        [enc_geom, enc_geo, proc_geom, proc_geo, lat],
+        [shape(n_in + n_out + k_in + k_out, d), shape(n_enc, d), shape(n_proc, d)],
+        [
+            enc_node_in, enc_node_out, proc_edge_in, proc_edge_out,
+            enc_geom, enc_geo, proc_geom, proc_geo, lat,
+        ],
         flops=2 * (n_enc + n_proc) * d * 128,
     )
-    edge_round = to_group(edge_across)
-    lat_both = to_core(lat_across)
-    next_w, node_half, proc_half = call(
-        second_pack_kernel,
-        [shape(n_in + n_out + k_in + k_out, d), shape((n_in + n_out) // 2, d), shape((k_in + k_out) // 2, d)],
-        [enc_node_in, enc_node_out, proc_edge_in, proc_edge_out, lat_across],
-    )
-    node_across, proc_across = to_chip(node_half), to_chip(proc_half)
+    crossing, lat_sent = call(
+        functools.partial(cross_kernel, n_in + n_out, k_in),
+        [shape(n_in + n_out + (k_in + k_out) // 2, d), shape(lat.shape[0], width)],
+        [next_w, lat_across],
+    )
+    lat_both = to_core(lat_sent)
+    next_across = to_chip(crossing)
     next_beside = to_core(next_w)
 
     halo_rows = padded(got)
@@ -449,7 +510,8 @@
         [shape(half, d)] * 3,
         [
             enc_emb, enc_edges, enc_edge_gain, lat, lat_across, lat_beside, lat_both,
-            edge_w, edge_beside, edge_across, edge_round, to_core(edge_across), to_core(edge_round), enc_blocks,
+            enc_edge_in, enc_edge_out, *edge_beside,
+            edge_across, edge_round, to_core(edge_across), to_core(edge_round), enc_blocks,
         ],
         scratch=[
             pltpu.VMEM((grid_rows + mesh_rows + got, d), BF16),
@@ -461,14 +523,20 @@
         flops=2 * n_enc * d * (3 * d + grid_rows + mesh_rows + halo_rows),
         smem=1,
     )
-    node_round, proc_round = to_group(node_across), to_group(proc_across)
     (chip_sum,) = call(add_kernel, [shape(half, d)], [keep, to_core(give)])
+    *node_across, proc_across = call(
+        split_kernel,
+        [shape((n_in + n_out) // 2, d)] * 2 + [shape((k_in + k_out) // 2, d)],
+        [next_across, chip_sum],
+    )
+    node_both = [to_core(v) for v in node_across]
+    proc_round = to_group(proc_across)
     mid_half, last_w = call(
         functools.partial(node_kernel, n_in, n_out),
         [shape(half, d), shape(n_in + n_out, d)],
         [
             own_mesh, chip_sum, to_chip(chip_sum), enc_node_gain, proc_node_in, proc_node_out,
-            next_w, next_beside, node_across, node_round, to_core(node_across), to_core(node_round),
+            next_w, next_beside, next_across, *node_both,
         ],
         scratch=[pltpu.VMEM((4 * (n_in + n_out), d), BF16)],
         flops=2 * half * d * 3 * d,
@@ -487,8 +555,8 @@
         functools.partial(proc_first_kernel, k_in, n_in + n_out),
         [shape(d + 2 * mesh_rows, d), shape(early, d, F32), shape(d, d), shape(d, d)],
         [
-            proc_emb, mid, proc_edges, next_w, next_beside, proc_across, proc_round,
-            to_core(proc_across), to_core(proc_round),
+            proc_emb, mid, proc_edges, next_w, next_beside, proc_across, to_core(proc_across),
+            proc_round, to_core(proc_round),
         ],
         scratch=[pltpu.VMEM((4 * (k_in + k_out), d), BF16)],
         flops=2 * early * d * (d + 2 * mesh_rows),

time: 79.2 us -> 77.6 us (0.980); the launches traced: 78.8 us -> 76.1 us
  waiting for transfers between devices: 27.4 us -> 22.7 us
  Pallas kernels: 18.4 us -> 20 us
    ppermute x7 -> x6, waiting for transfers between devices: 19.4 us -> 14.9 us  [to_chip(): return lax.ppermute(v, 'sub', [(i, i ^ 2) for i in range(4)])]
    pallas_call x12 -> x13, Pallas kernels: 18.4 us -> 20 us  [call(): pl.pallas_call(body, out_shape=tuple(outs), in_specs=specs, out_specs=tup...]
    ppermute x3 -> x2, waiting for transfers between devices: 2.09 us -> 0.75 us  [to_group(): return lax.ppermute(v, 'groups', [(i, count - 1 - i) for i in range(count)])]
    ppermute x7 -> x6, starting transfers between devices: 7.61 us -> 6.56 us  [to_chip(): return lax.ppermute(v, 'sub', [(i, i ^ 2) for i in range(4)])]
    ppermute x15 -> x16, waiting for transfers between devices: 2.59 us -> 3.55 us  [to_core(): return lax.ppermute(v, 'sub', [(i, i ^ 1) for i in range(4)])]
    ppermute x3 -> x2, starting transfers between devices: 1.51 us -> 2.09 us  [to_group(): return lax.ppermute(v, 'groups', [(i, count - 1 - i) for i in range(count)])]
    ppermute x15 -> x16, starting transfers between devices: 3.11 us -> 3.64 us  [to_core(): return lax.ppermute(v, 'sub', [(i, i ^ 1) for i in range(4)])]
    unnamed x44 -> x42, local copies, waits for them, and re-layouts: 8.21 us -> 8.49 us
  transfers between devices with their start and end apart: 31 -> 30, of which waited for: 11 -> 9; matrix products, arithmetic and copies ran while one was open for 0% -> 0% of each run, Pallas kernels for 21% -> 22%
where the time goes in v3:
time: 77.6 us; the launch traced here: 76.1 us
  starting transfers between devices  23.3 us (30%)
  waiting for transfers between devices  22.7 us (29%)
  Pallas kernels  20 us (26%)
  local copies, waits for them, and re-layouts  8.49 us (11%)
  between operations  1.63 us (2%)
    pallas_call x13, Pallas kernels, call(): pl.pallas_call(body, out_shape=tuple(outs), in_specs=specs, out_specs=tup...  20 us
    ppermute x6, waiting for transfers between devices, to_chip(): return lax.ppermute(v, 'sub', [(i, i ^ 2) for i in range(4)])  14.9 us
    ppermute x6, starting transfers between devices, local(): lax.ppermute(v, 'dom', entry[0])  11 us
    unnamed x42, local copies, waits for them, and re-layouts  8.49 us
    ppermute x6, starting transfers between devices, to_chip(): return lax.ppermute(v, 'sub', [(i, i ^ 2) for i in range(4)])  6.56 us
    ppermute x16, starting transfers between devices, to_core(): return lax.ppermute(v, 'sub', [(i, i ^ 1) for i in range(4)])  3.64 us
    ppermute x16, waiting for transfers between devices, to_core(): return lax.ppermute(v, 'sub', [(i, i ^ 1) for i in range(4)])  3.55 us
    ppermute x6, waiting for transfers between devices, local(): lax.ppermute(v, 'dom', entry[0])  3.47 us
  transfers between devices with their start and end apart: 30, of which 9 were waited for; matrix products, arithmetic and copies ran while one was open for 0% of the time, Pallas kernels for 22%

profile of v3, /device:TPU:12, one launch (start us, length us, event | category | flops | bytes accessed | tf_op | source)
XLA Modules:
  0.0 76.1 jit_solution(7104189207035828371)
XLA Ops:
  0.0 2.0 %shard_map.226 = (bf16[256,512]{1,0:T(8,128)(2,1)}, bf16[64,128]{1,0:T(8,128)(2,1)}, bf16[64,128]{1,0:T(8,128)(2,1)}, bf16[64,128]{1,0:T(8,128)(2,1)}) custom-call(bf16[512,128]{1,0:T(8,128)(2,1)} %refs_0_.1, s32[1,4,64]{2,1,0:T(4,128)} %send.2, bf16[384,512]{1,0:T(8,128)(2,1)} %o_in.1, bf16[128,512]{1,0:T(8,128)(2,1)} %o_out.1), custom_call_target="tpu_custom_call" | custom-call | bytes 967680 | tf_op jit(solution)/shard_map/pallas_call | solution.py:63
  2.0 1.6 %collective-permute-start.8 = (bf16[256,512]{1,0:T(8,128)(2,1)}, bf16[256,512]{1,0:T(8,128)(2,1)S(1)}, u32[]{:S(2)}, u32[]{:S(2)}) collective-permute-start(bf16[256,512]{1,0:T(8,128)(2,1)} %get-tuple-element.40), channel_id=1, source_target_pairs={{0,2},{1,3},{2,0},{3,1},{4,6},{5,7},{6,4},{7,5},{8,10},{9,11},{10,... | collective-permute-start | bytes 786440 | tf_op jit(solution)/shard_map/ppermute | solution.py:406
  3.6 0.4 collective-permute-start
  4.1 2.6 %collective-permute-start.1 = (bf16[64,128]{1,0:T(8,128)(2,1)}, bf16[64,128]{1,0:T(8,128)(2,1)S(1)}, u32[]{:S(2)}, u32[]{:S(2)}) collective-permute-start(bf16[64,128]{1,0:T(8,128)(2,1)} %get-tuple-element.35), channel_id=1, source_target_pairs={{0,8},{4,12},{8,0},{12,4},{1,9},{5,13},{9,1},{13,5},{2,10},{6,14},... | collective-permute-start | bytes 49160 | tf_op jit(solution)/shard_map/ppermute | solution.py:477
  6.6 2.3 %collective-permute-start.2 = (bf16[64,128]{1,0:T(8,128)(2,1)}, bf16[64,128]{1,0:T(8,128)(2,1)S(1)}, u32[]{:S(2)}, u32[]{:S(2)}) collective-permute-start(bf16[64,128]{1,0:T(8,128)(2,1)} %get-tuple-element.36), channel_id=1, source_target_pairs={{4,8},{8,4},{5,9},{9,5},{6,10},{10,6},{7,11},{11,7},{20,24},{24,20... | collective-permute-start | bytes 49160 | tf_op jit(solution)/shard_map/ppermute | solution.py:477
  9.0 0.0 collective-permute-done.refs_2_
  9.0 3.5 %collective-permute-done.2.refs_4_ = bf16[64,128]{1,0:T(8,128)(2,1)S(1)} collective-permute-done((bf16[64,128]{1,0:T(8,128)(2,1)}, bf16[64,128]{1,0:T(8,128)(2,1)S(1)}, u32[]{:S(2)}, u32[]{:S(2)}) %collective-permute-start.2) | collective-permute-done | bytes 16416 | tf_op jit(solution)/shard_map/ppermute | solution.py:477
  12.5 0.9 %copy-done = bf16[512,128]{1,0:T(8,128)(2,1)S(1)} copy-done((bf16[512,128]{1,0:T(8,128)(2,1)S(1)}, bf16[512,128]{1,0:T(8,128)(2,1)}, u32[]{:S(2)}) %copy-start) | copy-done | bytes 131096
  13.4 0.9 %copy-done.3 = bf16[512,128]{1,0:T(8,128)(2,1)S(1)} copy-done((bf16[512,128]{1,0:T(8,128)(2,1)S(1)}, bf16[512,128]{1,0:T(8,128)(2,1)}, u32[]{:S(2)}) %copy-start.3) | copy-done | bytes 131096
  14.3 0.6 collective-permute-start.3
  14.9 0.5 collective-permute-start.9
  15.4 0.5 collective-permute-start.4
  15.9 1.0 %copy-done.9 = bf16[384,512]{1,0:T(8,128)(2,1)S(1)} copy-done((bf16[384,512]{1,0:T(8,128)(2,1)S(1)}, bf16[384,512]{1,0:T(8,128)(2,1)}, u32[]{:S(2)}) %copy-start.9) | copy-done | bytes 393240
  16.9 0.9 %copy-done.10 = bf16[256,512]{1,0:T(8,128)(2,1)S(1)} copy-done((bf16[256,512]{1,0:T(8,128)(2,1)S(1)}, bf16[256,512]{1,0:T(8,128)(2,1)}, u32[]{:S(2)}) %copy-start.10) | copy-done | bytes 262168
  17.9 0.9 %copy-done.11 = bf16[128,512]{1,0:T(8,128)(2,1)S(1)} copy-done((bf16[128,512]{1,0:T(8,128)(2,1)S(1)}, bf16[128,512]{1,0:T(8,128)(2,1)}, u32[]{:S(2)}) %copy-start.11) | copy-done | bytes 131096
  18.8 0.9 %copy-done.12 = bf16[128,512]{1,0:T(8,128)(2,1)S(1)} copy-done((bf16[128,512]{1,0:T(8,128)(2,1)S(1)}, bf16[128,512]{1,0:T(8,128)(2,1)}, u32[]{:S(2)}) %copy-start.12) | copy-done | bytes 131096
  19.7 0.8 copy-done.13
  20.5 0.7 copy-done.14
  21.2 0.7 copy-done.16
  21.9 0.7 copy-done.17
  22.6 1.8 %shard_map.228 = (bf16[896,512]{1,0:T(8,128)(2,1)S(1)}, bf16[1024,512]{1,0:T(8,128)(2,1)S(1)}, bf16[2048,512]{1,0:T(8,128)(2,1)S(1)}) custom-call(bf16[256,512]{1,0:T(8,128)(2,1)S(1)} %copy-done.10, bf16[128,512]{1,0:T(8,128)(2,1)S(1)} %copy-done.11, bf16[384,512]{1,0:T(8,128)(2,1)S(1)} %copy-done.9, bf16[128,512]{1,0:T(8,128)(2,1)S(1)} %copy-done.12, ...), custom_call_target="tpu_custom_call" | custom-call | flops 402653184 | bytes 5357568 | tf_op jit(solution)/shard_map/pallas_call | solution.py:63
  24.3 0.1 shard_map.229
  24.4 0.6 collective-permute-start.5
  25.0 0.1 collective-permute-start.10
  25.1 0.4 collective-permute-start.11
  25.5 0.1 collective-permute-start.14
  25.6 1.5 %collective-permute-start.15 = (bf16[640,512]{1,0:T(8,128)(2,1)S(1)}, bf16[640,512]{1,0:T(8,128)(2,1)S(1)}, u32[]{:S(2)}, u32[]{:S(2)}) collective-permute-start(bf16[640,512]{1,0:T(8,128)(2,1)S(1)} %get-tuple-element.44), channel_id=1, source_target_pairs={{0,2},{1,3},{2,0},{3,1},{4,6},{5,7},{6,4},{7,5},{8,10},{9,11},{10,... | collective-permute-start | bytes 1966088 | tf_op jit(solution)/shard_map/ppermute | solution.py:406
  27.8 0.0 copy-start.2
  27.8 0.0 copy-start.5
  27.8 0.0 copy-start.6
  27.8 4.8 %shard_map.230 = (bf16[256,512]{1,0:T(8,128)(2,1)S(1)}, bf16[256,512]{1,0:T(8,128)(2,1)S(1)}, bf16[256,512]{1,0:T(8,128)(2,1)S(1)}) custom-call(bf16[1024,512]{1,0:T(8,128)(2,1)S(1)} %get-tuple-element.37.emb, s32[2,1024]{1,0:T(2,128)S(1)} %copy-done.18, f32[1,512]{1,0:T(1,128)S(1)} %bitcast.6, bf16[1216,128]{1,0:T(8,128)(2,1)S(1)} %shard_map.227.after.l0, ...), custom_call_target="tpu_custom_call" | custom-call | flops 2952790016 | bytes 5187588 | tf_op jit(solution)/shard_map/pallas_call | solution.py:63
  32.6 0.2 collective-permute-start.12
  32.8 1.4 %collective-permute-done.12.theirs = bf16[256,512]{1,0:T(8,128)(2,1)S(1)} collective-permute-done((bf16[256,512]{1,0:T(8,128)(2,1)S(1)}, bf16[256,512]{1,0:T(8,128)(2,1)S(1)}, u32[]{:S(2)}, u32[]{:S(2)}) %collective-permute-start.12) | collective-permute-done | bytes 262176 | tf_op jit(solution)/shard_map/ppermute | solution.py:410
  34.2 0.1 shard_map.231.after.mine
  34.3 0.8 %collective-permute-start.13 = (bf16[256,512]{1,0:T(8,128)(2,1)S(1)}, bf16[256,512]{1,0:T(8,128)(2,1)S(1)}, u32[]{:S(2)}, u32[]{:S(2)}) collective-permute-start(bf16[256,512]{1,0:T(8,128)(2,1)S(1)} %shard_map.231.after.mine), channel_id=1, source_target_pairs={{0,2},{1,3},{2,0},{3,1},{4,6},{5,7},{6,4},{7,5},{8,10},{9,11},{10,... | collective-permute-start | bytes 786440 | tf_op jit(solution)/shard_map/ppermute | solution.py:406
  35.0 8.1 %collective-permute-done.15.source.w2 = bf16[640,512]{1,0:T(8,128)(2,1)S(1)} collective-permute-done((bf16[640,512]{1,0:T(8,128)(2,1)S(1)}, bf16[640,512]{1,0:T(8,128)(2,1)S(1)}, u32[]{:S(2)}, u32[]{:S(2)}) %collective-permute-start.15) | collective-permute-done | bytes 655392 | tf_op jit(solution)/shard_map/ppermute | solution.py:406
  43.2 0.0 copy-start.7
  43.2 1.6 %collective-permute-start.20 = (bf16[256,512]{1,0:T(8,128)(2,1)S(1)}, bf16[256,512]{1,0:T(8,128)(2,1)S(1)}, u32[]{:S(2)}, u32[]{:S(2)}) collective-permute-start(bf16[256,512]{1,0:T(8,128)(2,1)S(1)} %get-tuple-element.50.across), channel_id=1, source_target_pairs={{0,16},{16,0},{1,17},{17,1},{2,18},{18,2},{3,19},{19,3},{4,20},{20... | collective-permute-start | bytes 786440 | tf_op jit(solution)/shard_map/ppermute | solution.py:415
  44.8 0.5 collective-permute-start.17
  45.3 0.9 %collective-permute-done.16.w3 = bf16[192,512]{1,0:T(8,128)(2,1)S(1)} collective-permute-done((bf16[192,512]{1,0:T(8,128)(2,1)S(1)}, bf16[192,512]{1,0:T(8,128)(2,1)S(1)}, u32[]{:S(2)}, u32[]{:S(2)}) %collective-permute-start.16) | collective-permute-done | bytes 196640 | tf_op jit(solution)/shard_map/ppermute | solution.py:410
  46.2 0.3 collective-permute-done.17.w4
  46.5 1.8 %collective-permute-done.13.theirs = bf16[256,512]{1,0:T(8,128)(2,1)S(1)} collective-permute-done((bf16[256,512]{1,0:T(8,128)(2,1)S(1)}, bf16[256,512]{1,0:T(8,128)(2,1)S(1)}, u32[]{:S(2)}, u32[]{:S(2)}) %collective-permute-start.13) | collective-permute-done | bytes 262176 | tf_op jit(solution)/shard_map/ppermute | solution.py:406
  48.3 0.0 copy-start.15
  48.3 1.0 %shard_map.233 = (bf16[256,512]{1,0:T(8,128)(2,1)S(1)}, bf16[384,512]{1,0:T(8,128)(2,1)S(1)}) custom-call(bf16[256,512]{1,0:T(8,128)(2,1)S(1)} %get-tuple-element.41.mesh, bf16[256,512]{1,0:T(8,128)(2,1)S(1)} %shard_map.231.after.mine, bf16[256,512]{1,0:T(8,128)(2,1)S(1)} %collective-permute-done.13.theirs, f32[1,512]{1,0:T(1,128)S(1)} %bitcast.4, ...), custom_call_target="tpu_custom_call" | custom-call | flops 402653184 | bytes 4720640 | tf_op jit(solution)/shard_map/pallas_call | solution.py:63
  49.3 0.1 collective-permute-start.18
  49.4 0.5 collective-permute-start.19
  49.9 0.7 collective-permute-done.20.round_
  51.3 1.6 %collective-permute-start.28 = (bf16[384,512]{1,0:T(8,128)(2,1)S(1)}, bf16[384,512]{1,0:T(8,128)(2,1)S(1)}, u32[]{:S(2)}, u32[]{:S(2)}) collective-permute-start(bf16[384,512]{1,0:T(8,128)(2,1)S(1)} %get-tuple-element.62.w0), channel_id=1, source_target_pairs={{0,2},{1,3},{2,0},{3,1},{4,6},{5,7},{6,4},{7,5},{8,10},{9,11},{10,... | collective-permute-start | bytes 1179656 | tf_op jit(solution)/shard_map/ppermute | solution.py:406
  52.9 0.4 shard_map.234
  53.3 0.0 collective-permute-start.22
  53.3 1.9 %collective-permute-start.23 = (bf16[32,512]{1,0:T(8,128)(2,1)S(1)}, bf16[32,512]{1,0:T(8,128)(2,1)S(1)}, u32[]{:S(2)}, u32[]{:S(2)}) collective-permute-start(bf16[32,512]{1,0:T(8,128)(2,1)S(1)} %get-tuple-element.56), channel_id=1, source_target_pairs={{0,8},{4,12},{8,0},{12,4},{1,9},{5,13},{9,1},{13,5},{2,10},{6,14},... | collective-permute-start | bytes 98312 | tf_op jit(solution)/shard_map/ppermute | solution.py:551
  55.2 3.7 %collective-permute-start.24 = (bf16[32,512]{1,0:T(8,128)(2,1)S(1)}, bf16[32,512]{1,0:T(8,128)(2,1)S(1)}, u32[]{:S(2)}, u32[]{:S(2)}) collective-permute-start(bf16[32,512]{1,0:T(8,128)(2,1)S(1)} %get-tuple-element.57), channel_id=1, source_target_pairs={{4,8},{8,4},{5,9},{9,5},{6,10},{10,6},{7,11},{11,7},{20,24},{24,20... | collective-permute-start | bytes 98312 | tf_op jit(solution)/shard_map/ppermute | solution.py:551
  58.9 0.0 copy-start.20
  58.9 2.6 %shard_map.235 = (bf16[1536,512]{1,0:T(8,128)(2,1)S(1)}, f32[1024,512]{1,0:T(8,128)S(1)}, bf16[512,512]{1,0:T(8,128)(2,1)S(1)}, bf16[512,512]{1,0:T(8,128)(2,1)S(1)}) custom-call(bf16[2048,512]{1,0:T(8,128)(2,1)S(1)} %get-tuple-element.49.emb, bf16[512,512]{1,0:T(8,128)(2,1)S(1)} %get-tuple-element.48.full, s32[2,2048]{1,0:T(2,128)S(1)} %copy-done.15, ...), custom_call_target="tpu_custom_call" | custom-call | flops 1610612736 | bytes 10240000 | tf_op jit(solution)/shard_map/pallas_call | solution.py:63
  61.6 0.0 copy-start.8
  61.6 5.8 %shard_map.236 = (bf16[256,512]{1,0:T(8,128)(2,1)S(1)}, bf16[256,512]{1,0:T(8,128)(2,1)S(1)}) custom-call(bf16[2048,512]{1,0:T(8,128)(2,1)S(1)} %get-tuple-element.49.emb, s32[2,2048]{1,0:T(2,128)S(1)} %copy-done.15, f32[1,512]{1,0:T(1,128)S(1)} %bitcast.7, bf16[1536,512]{1,0:T(8,128)(2,1)S(1)} %get-tuple-element.51.table, ...), custom_call_target="tpu_custom_call" | custom-call | flops 3489660928 | bytes 7456772 | tf_op jit(solution)/shard_map/pallas_call | solution.py:63
  67.3 0.1 collective-permute-start.25
  67.4 0.5 collective-permute-start.27
  67.9 0.1 collective-permute-start.29
  68.0 0.9 %collective-permute-done.25.theirs = bf16[256,512]{1,0:T(8,128)(2,1)S(1)} collective-permute-done((bf16[256,512]{1,0:T(8,128)(2,1)S(1)}, bf16[256,512]{1,0:T(8,128)(2,1)S(1)}, u32[]{:S(2)}, u32[]{:S(2)}) %collective-permute-start.25) | collective-permute-done | bytes 262176 | tf_op jit(solution)/shard_map/ppermute | solution.py:410
  69.0 0.1 shard_map.237
  69.0 0.6 collective-permute-start.26
  69.6 5.0 %collective-permute-done.26.theirs = bf16[128,512]{1,0:T(8,128)(2,1)S(1)} collective-permute-done((bf16[128,512]{1,0:T(8,128)(2,1)S(1)}, bf16[128,512]{1,0:T(8,128)(2,1)S(1)}, u32[]{:S(2)}, u32[]{:S(2)}) %collective-permute-start.26) | collective-permute-done | bytes 131104 | tf_op jit(solution)/shard_map/ppermute | solution.py:406
  74.6 1.5 %shard_map.238 = bf16[128,512]{1,0:T(8,128)(2,1)} custom-call(bf16[512,512]{1,0:T(8,128)(2,1)S(1)} %get-tuple-element.48.full, bf16[128,512]{1,0:T(8,128)(2,1)S(1)} %get-tuple-element.60.mine, bf16[128,512]{1,0:T(8,128)(2,1)S(1)} %collective-permute-done.26.theirs, f32[1,512]{1,0:T(1,128)S(1)} %bitcast.5, bf16[384,512]{1,0:T(8,128)(2,1)S(1)} %get-tuple-element.62.w0, ...), custom_call_target="tpu_custom_call" | custom-call | flops 201326592 | bytes 2492416 | tf_op jit(solution)/shard_map/pallas_call | solution.py:63
  (51 shorter events, 0.2 us)
Async XLA Ops:
  0.0 27.8 %copy-start.1 = (bf16[384,512]{1,0:T(8,128)(2,1)S(1)}, bf16[384,512]{1,0:T(8,128)(2,1)}, u32[]{:S(2)}) copy-start(bf16[384,512]{1,0:T(8,128)(2,1)} %o_in.1) | copy-start | bytes 1179652
  0.0 27.8 %copy-start.19 = (f32[512]{0:T(512)S(1)}, f32[512]{0:T(512)}, u32[]{:S(2)}) copy-start(f32[512]{0:T(512)} %param.44) | copy-start | bytes 6148
  0.0 27.8 %copy-start.18 = (s32[2,1024]{1,0:T(2,128)S(1)}, s32[2,1024]{1,0:T(2,128)}, u32[]{:S(2)}) copy-start(s32[2,1024]{1,0:T(2,128)} %edges.3) | copy-start | bytes 24580
  2.0 12.9 %collective-permute-start.8 = (bf16[256,512]{1,0:T(8,128)(2,1)}, bf16[256,512]{1,0:T(8,128)(2,1)S(1)}, u32[]{:S(2)}, u32[]{:S(2)}) collective-permute-start(bf16[256,512]{1,0:T(8,128)(2,1)} %get-tuple-element.40), channel_id=1, source_target_pairs={{0,2},{1,3},{2,0},{3,1},{4,6},{5,7},{6,4},{7,5},{8,10},{9,11},{10,... | collective-permute-start | bytes 786440 | tf_op jit(solution)/shard_map/ppermute | solution.py:406
  3.6 5.4 %collective-permute-start = (bf16[64,128]{1,0:T(8,128)(2,1)}, bf16[64,128]{1,0:T(8,128)(2,1)S(1)}, u32[]{:S(2)}, u32[]{:S(2)}) collective-permute-start(bf16[64,128]{1,0:T(8,128)(2,1)} %get-tuple-element.34), channel_id=1, source_target_pairs={{0,4},{4,0},{8,12},{12,8},{1,5},{5,1},{9,13},{13,9},{2,6},{6,2},{1... | collective-permute-start | bytes 49160 | tf_op jit(solution)/shard_map/ppermute | solution.py:477
  4.1 5.0 %collective-permute-start.1 = (bf16[64,128]{1,0:T(8,128)(2,1)}, bf16[64,128]{1,0:T(8,128)(2,1)S(1)}, u32[]{:S(2)}, u32[]{:S(2)}) collective-permute-start(bf16[64,128]{1,0:T(8,128)(2,1)} %get-tuple-element.35), channel_id=1, source_target_pairs={{0,8},{4,12},{8,0},{12,4},{1,9},{5,13},{9,1},{13,5},{2,10},{6,14},... | collective-permute-start | bytes 49160 | tf_op jit(solution)/shard_map/ppermute | solution.py:477
  6.6 5.8 %collective-permute-start.2 = (bf16[64,128]{1,0:T(8,128)(2,1)}, bf16[64,128]{1,0:T(8,128)(2,1)S(1)}, u32[]{:S(2)}, u32[]{:S(2)}) collective-permute-start(bf16[64,128]{1,0:T(8,128)(2,1)} %get-tuple-element.36), channel_id=1, source_target_pairs={{4,8},{8,4},{5,9},{9,5},{6,10},{10,6},{7,11},{11,7},{20,24},{24,20... | collective-permute-start | bytes 49160 | tf_op jit(solution)/shard_map/ppermute | solution.py:477
  12.5 0.9 %copy-start = (bf16[512,128]{1,0:T(8,128)(2,1)S(1)}, bf16[512,128]{1,0:T(8,128)(2,1)}, u32[]{:S(2)}) copy-start(bf16[512,128]{1,0:T(8,128)(2,1)} %refs_0_.1) | copy-start | bytes 393220
  13.4 0.9 %copy-start.3 = (bf16[512,128]{1,0:T(8,128)(2,1)S(1)}, bf16[512,128]{1,0:T(8,128)(2,1)}, u32[]{:S(2)}) copy-start(bf16[512,128]{1,0:T(8,128)(2,1)} %refs_1_.1) | copy-start | bytes 393220
  14.3 13.5 %copy-start.4 = (bf16[128,512]{1,0:T(8,128)(2,1)S(1)}, bf16[128,512]{1,0:T(8,128)(2,1)}, u32[]{:S(2)}) copy-start(bf16[128,512]{1,0:T(8,128)(2,1)} %o_out.1) | copy-start | bytes 393220
  14.3 10.0 %collective-permute-start.3 = (bf16[1216,128]{1,0:T(8,128)(2,1)S(1)}, bf16[1216,128]{1,0:T(8,128)(2,1)S(1)}, u32[]{:S(2)}, u32[]{:S(2)}) collective-permute-start(bf16[1216,128]{1,0:T(8,128)(2,1)S(1)} %shard_map.227.after.l0), channel_id=1, source_target_pairs={{0,2},{1,3},{2,0},{3,1},{4,6},{5,7},{6,4},{7,5},{8,10},{9,11},{10,... | collective-permute-start | bytes 933896 | tf_op jit(solution)/shard_map/ppermute | solution.py:406
  14.9 10.2 %collective-permute-start.9 = (bf16[256,512]{1,0:T(8,128)(2,1)S(1)}, bf16[256,512]{1,0:T(8,128)(2,1)S(1)}, u32[]{:S(2)}, u32[]{:S(2)}) collective-permute-start(bf16[256,512]{1,0:T(8,128)(2,1)S(1)} %collective-permute-done.8.across), channel_id=1, source_target_pairs={{0,16},{16,0},{1,17},{17,1},{2,18},{18,2},{3,19},{19,3},{4,20},{20... | collective-permute-start | bytes 786440 | tf_op jit(solution)/shard_map/ppermute | solution.py:415
  15.4 10.2 %collective-permute-start.6 = (bf16[384,512]{1,0:T(8,128)(2,1)}, bf16[384,512]{1,0:T(8,128)(2,1)S(1)}, u32[]{:S(2)}, u32[]{:S(2)}) collective-permute-start(bf16[384,512]{1,0:T(8,128)(2,1)} %o_in.1), channel_id=1, source_target_pairs={{0,1},{1,0},{2,3},{3,2},{4,5},{5,4},{6,7},{7,6},{8,9},{9,8},{10,11... | collective-permute-start | bytes 1179656 | tf_op jit(solution)/shard_map/ppermute | solution.py:410
  15.4 10.1 %collective-permute-start.4 = (bf16[1216,128]{1,0:T(8,128)(2,1)S(1)}, bf16[1216,128]{1,0:T(8,128)(2,1)S(1)}, u32[]{:S(2)}, u32[]{:S(2)}) collective-permute-start(bf16[1216,128]{1,0:T(8,128)(2,1)S(1)} %shard_map.227.after.l0), channel_id=1, source_target_pairs={{0,1},{1,0},{2,3},{3,2},{4,5},{5,4},{6,7},{7,6},{8,9},{9,8},{10,11... | collective-permute-start | bytes 933896 | tf_op jit(solution)/shard_map/ppermute | solution.py:410
  15.9 9.1 %collective-permute-start.7 = (bf16[128,512]{1,0:T(8,128)(2,1)}, bf16[128,512]{1,0:T(8,128)(2,1)S(1)}, u32[]{:S(2)}, u32[]{:S(2)}) collective-permute-start(bf16[128,512]{1,0:T(8,128)(2,1)} %o_out.1), channel_id=1, source_target_pairs={{0,1},{1,0},{2,3},{3,2},{4,5},{5,4},{6,7},{7,6},{8,9},{9,8},{10,11... | collective-permute-start | bytes 393224 | tf_op jit(solution)/shard_map/ppermute | solution.py:410
  15.9 1.0 %copy-start.9 = (bf16[384,512]{1,0:T(8,128)(2,1)S(1)}, bf16[384,512]{1,0:T(8,128)(2,1)}, u32[]{:S(2)}) copy-start(bf16[384,512]{1,0:T(8,128)(2,1)} %p_in.1) | copy-start | bytes 1179652
  16.9 0.9 %copy-start.10 = (bf16[256,512]{1,0:T(8,128)(2,1)S(1)}, bf16[256,512]{1,0:T(8,128)(2,1)}, u32[]{:S(2)}) copy-start(bf16[256,512]{1,0:T(8,128)(2,1)} %e_in.1) | copy-start | bytes 786436
  17.9 0.9 %copy-start.11 = (bf16[128,512]{1,0:T(8,128)(2,1)S(1)}, bf16[128,512]{1,0:T(8,128)(2,1)}, u32[]{:S(2)}) copy-start(bf16[128,512]{1,0:T(8,128)(2,1)} %e_out.1) | copy-start | bytes 393220
  18.8 0.9 %copy-start.12 = (bf16[128,512]{1,0:T(8,128)(2,1)S(1)}, bf16[128,512]{1,0:T(8,128)(2,1)}, u32[]{:S(2)}) copy-start(bf16[128,512]{1,0:T(8,128)(2,1)} %p_out.1) | copy-start | bytes 393220
  19.7 0.8 copy-start.13
  20.4 0.7 copy-start.14
  21.2 0.7 copy-start.16
  21.9 0.7 copy-start.17
  24.4 3.3 %collective-permute-start.5 = (bf16[1216,128]{1,0:T(8,128)(2,1)S(1)}, bf16[1216,128]{1,0:T(8,128)(2,1)S(1)}, u32[]{:S(2)}, u32[]{:S(2)}) collective-permute-start(bf16[1216,128]{1,0:T(8,128)(2,1)S(1)} %get-tuple-element.39), channel_id=1, source_target_pairs={{0,1},{1,0},{2,3},{3,2},{4,5},{5,4},{6,7},{7,6},{8,9},{9,8},{10,11... | collective-permute-start | bytes 933896 | tf_op jit(solution)/shard_map/ppermute | solution.py:410
  25.0 2.8 %collective-permute-start.10 = (bf16[256,512]{1,0:T(8,128)(2,1)S(1)}, bf16[256,512]{1,0:T(8,128)(2,1)S(1)}, u32[]{:S(2)}, u32[]{:S(2)}) collective-permute-start(bf16[256,512]{1,0:T(8,128)(2,1)S(1)} %collective-permute-done.8.across), channel_id=1, source_target_pairs={{0,1},{1,0},{2,3},{3,2},{4,5},{5,4},{6,7},{7,6},{8,9},{9,8},{10,11... | collective-permute-start | bytes 786440 | tf_op jit(solution)/shard_map/ppermute | solution.py:410
  25.1 2.7 %collective-permute-start.11 = (bf16[256,512]{1,0:T(8,128)(2,1)S(1)}, bf16[256,512]{1,0:T(8,128)(2,1)S(1)}, u32[]{:S(2)}, u32[]{:S(2)}) collective-permute-start(bf16[256,512]{1,0:T(8,128)(2,1)S(1)} %collective-permute-done.9.round_), channel_id=1, source_target_pairs={{0,1},{1,0},{2,3},{3,2},{4,5},{5,4},{6,7},{7,6},{8,9},{9,8},{10,11... | collective-permute-start | bytes 786440 | tf_op jit(solution)/shard_map/ppermute | solution.py:410
  25.5 19.8 %collective-permute-start.14 = (bf16[896,512]{1,0:T(8,128)(2,1)S(1)}, bf16[896,512]{1,0:T(8,128)(2,1)S(1)}, u32[]{:S(2)}, u32[]{:S(2)}) collective-permute-start(bf16[896,512]{1,0:T(8,128)(2,1)S(1)} %get-tuple-element.38.weights.w0), channel_id=1, source_target_pairs={{0,1},{1,0},{2,3},{3,2},{4,5},{5,4},{6,7},{7,6},{8,9},{9,8},{10,11... | collective-permute-start | bytes 2752520 | tf_op jit(solution)/shard_map/ppermute | solution.py:410
  25.6 17.5 %collective-permute-start.15 = (bf16[640,512]{1,0:T(8,128)(2,1)S(1)}, bf16[640,512]{1,0:T(8,128)(2,1)S(1)}, u32[]{:S(2)}, u32[]{:S(2)}) collective-permute-start(bf16[640,512]{1,0:T(8,128)(2,1)S(1)} %get-tuple-element.44), channel_id=1, source_target_pairs={{0,2},{1,3},{2,0},{3,1},{4,6},{5,7},{6,4},{7,5},{8,10},{9,11},{10,... | collective-permute-start | bytes 1966088 | tf_op jit(solution)/shard_map/ppermute | solution.py:406
  27.8 20.5 %copy-start.2 = (bf16[256,512]{1,0:T(8,128)(2,1)S(1)}, bf16[256,512]{1,0:T(8,128)(2,1)}, u32[]{:S(2)}) copy-start(bf16[256,512]{1,0:T(8,128)(2,1)} %n_in.1) | copy-start | bytes 786436
  27.8 20.5 %copy-start.5 = (bf16[128,512]{1,0:T(8,128)(2,1)S(1)}, bf16[128,512]{1,0:T(8,128)(2,1)}, u32[]{:S(2)}) copy-start(bf16[128,512]{1,0:T(8,128)(2,1)} %n_out.1) | copy-start | bytes 393220
  27.8 20.5 %copy-start.6 = (f32[512]{0:T(512)S(1)}, f32[512]{0:T(512)}, u32[]{:S(2)}) copy-start(f32[512]{0:T(512)} %param.45) | copy-start | bytes 6148
  32.6 1.6 %collective-permute-start.12 = (bf16[256,512]{1,0:T(8,128)(2,1)S(1)}, bf16[256,512]{1,0:T(8,128)(2,1)S(1)}, u32[]{:S(2)}, u32[]{:S(2)}) collective-permute-start(bf16[256,512]{1,0:T(8,128)(2,1)S(1)} %get-tuple-element.43), channel_id=1, source_target_pairs={{0,1},{1,0},{2,3},{3,2},{4,5},{5,4},{6,7},{7,6},{8,9},{9,8},{10,11... | collective-permute-start | bytes 786440 | tf_op jit(solution)/shard_map/ppermute | solution.py:410
  34.3 14.0 %collective-permute-start.13 = (bf16[256,512]{1,0:T(8,128)(2,1)S(1)}, bf16[256,512]{1,0:T(8,128)(2,1)S(1)}, u32[]{:S(2)}, u32[]{:S(2)}) collective-permute-start(bf16[256,512]{1,0:T(8,128)(2,1)S(1)} %shard_map.231.after.mine), channel_id=1, source_target_pairs={{0,2},{1,3},{2,0},{3,1},{4,6},{5,7},{6,4},{7,5},{8,10},{9,11},{10,... | collective-permute-start | bytes 786440 | tf_op jit(solution)/shard_map/ppermute | solution.py:406
  43.2 9.7 %copy-start.7 = (s32[1,4,32]{2,1,0:T(4,128)S(1)}, s32[1,4,32]{2,1,0:T(4,128)}, u32[]{:S(2)}) copy-start(s32[1,4,32]{2,1,0:T(4,128)} %send.3) | copy-start | bytes 1540
  43.2 7.5 %collective-permute-start.20 = (bf16[256,512]{1,0:T(8,128)(2,1)S(1)}, bf16[256,512]{1,0:T(8,128)(2,1)S(1)}, u32[]{:S(2)}, u32[]{:S(2)}) collective-permute-start(bf16[256,512]{1,0:T(8,128)(2,1)S(1)} %get-tuple-element.50.across), channel_id=1, source_target_pairs={{0,16},{16,0},{1,17},{17,1},{2,18},{18,2},{3,19},{19,3},{4,20},{20... | collective-permute-start | bytes 786440 | tf_op jit(solution)/shard_map/ppermute | solution.py:415
  44.8 1.4 %collective-permute-start.16 = (bf16[192,512]{1,0:T(8,128)(2,1)S(1)}, bf16[192,512]{1,0:T(8,128)(2,1)S(1)}, u32[]{:S(2)}, u32[]{:S(2)}) collective-permute-start(bf16[192,512]{1,0:T(8,128)(2,1)S(1)} %get-tuple-element.45), channel_id=1, source_target_pairs={{0,1},{1,0},{2,3},{3,2},{4,5},{5,4},{6,7},{7,6},{8,9},{9,8},{10,11... | collective-permute-start | bytes 589832 | tf_op jit(solution)/shard_map/ppermute | solution.py:410
  44.8 1.7 %collective-permute-start.17 = (bf16[192,512]{1,0:T(8,128)(2,1)S(1)}, bf16[192,512]{1,0:T(8,128)(2,1)S(1)}, u32[]{:S(2)}, u32[]{:S(2)}) collective-permute-start(bf16[192,512]{1,0:T(8,128)(2,1)S(1)} %get-tuple-element.46), channel_id=1, source_target_pairs={{0,1},{1,0},{2,3},{3,2},{4,5},{5,4},{6,7},{7,6},{8,9},{9,8},{10,11... | collective-permute-start | bytes 589832 | tf_op jit(solution)/shard_map/ppermute | solution.py:410
  48.3 10.6 %copy-start.15 = (s32[2,2048]{1,0:T(2,128)S(1)}, s32[2,2048]{1,0:T(2,128)}, u32[]{:S(2)}) copy-start(s32[2,2048]{1,0:T(2,128)} %edges.5) | copy-start | bytes 49156
  49.3 3.5 %collective-permute-start.18 = (bf16[256,512]{1,0:T(8,128)(2,1)S(1)}, bf16[256,512]{1,0:T(8,128)(2,1)S(1)}, u32[]{:S(2)}, u32[]{:S(2)}) collective-permute-start(bf16[256,512]{1,0:T(8,128)(2,1)S(1)} %get-tuple-element.47.mine), channel_id=1, source_target_pairs={{0,1},{1,0},{2,3},{3,2},{4,5},{5,4},{6,7},{7,6},{8,9},{9,8},{10,11... | collective-permute-start | bytes 786440 | tf_op jit(solution)/shard_map/ppermute | solution.py:410
  49.4 5.8 %collective-permute-start.19 = (bf16[256,512]{1,0:T(8,128)(2,1)S(1)}, bf16[256,512]{1,0:T(8,128)(2,1)S(1)}, u32[]{:S(2)}, u32[]{:S(2)}) collective-permute-start(bf16[256,512]{1,0:T(8,128)(2,1)S(1)} %get-tuple-element.50.across), channel_id=1, source_target_pairs={{0,1},{1,0},{2,3},{3,2},{4,5},{5,4},{6,7},{7,6},{8,9},{9,8},{10,11... | collective-permute-start | bytes 786440 | tf_op jit(solution)/shard_map/ppermute | solution.py:410
  50.7 8.2 %collective-permute-start.21 = (bf16[256,512]{1,0:T(8,128)(2,1)S(1)}, bf16[256,512]{1,0:T(8,128)(2,1)S(1)}, u32[]{:S(2)}, u32[]{:S(2)}) collective-permute-start(bf16[256,512]{1,0:T(8,128)(2,1)S(1)} %collective-permute-done.20.round_), channel_id=1, source_target_pairs={{0,1},{1,0},{2,3},{3,2},{4,5},{5,4},{6,7},{7,6},{8,9},{9,8},{10,11... | collective-permute-start | bytes 786440 | tf_op jit(solution)/shard_map/ppermute | solution.py:410
  51.3 16.6 %collective-permute-start.28 = (bf16[384,512]{1,0:T(8,128)(2,1)S(1)}, bf16[384,512]{1,0:T(8,128)(2,1)S(1)}, u32[]{:S(2)}, u32[]{:S(2)}) collective-permute-start(bf16[384,512]{1,0:T(8,128)(2,1)S(1)} %get-tuple-element.62.w0), channel_id=1, source_target_pairs={{0,2},{1,3},{2,0},{3,1},{4,6},{5,7},{6,4},{7,5},{8,10},{9,11},{10,... | collective-permute-start | bytes 1179656 | tf_op jit(solution)/shard_map/ppermute | solution.py:406
  53.3 8.2 %collective-permute-start.22 = (bf16[32,512]{1,0:T(8,128)(2,1)S(1)}, bf16[32,512]{1,0:T(8,128)(2,1)S(1)}, u32[]{:S(2)}, u32[]{:S(2)}) collective-permute-start(bf16[32,512]{1,0:T(8,128)(2,1)S(1)} %get-tuple-element.55), channel_id=1, source_target_pairs={{0,4},{4,0},{8,12},{12,8},{1,5},{5,1},{9,13},{13,9},{2,6},{6,2},{1... | collective-permute-start | bytes 98312 | tf_op jit(solution)/shard_map/ppermute | solution.py:551
  53.3 8.2 %collective-permute-start.23 = (bf16[32,512]{1,0:T(8,128)(2,1)S(1)}, bf16[32,512]{1,0:T(8,128)(2,1)S(1)}, u32[]{:S(2)}, u32[]{:S(2)}) collective-permute-start(bf16[32,512]{1,0:T(8,128)(2,1)S(1)} %get-tuple-element.56), channel_id=1, source_target_pairs={{0,8},{4,12},{8,0},{12,4},{1,9},{5,13},{9,1},{13,5},{2,10},{6,14},... | collective-permute-start | bytes 98312 | tf_op jit(solution)/shard_map/ppermute | solution.py:551
  55.2 6.3 %collective-permute-start.24 = (bf16[32,512]{1,0:T(8,128)(2,1)S(1)}, bf16[32,512]{1,0:T(8,128)(2,1)S(1)}, u32[]{:S(2)}, u32[]{:S(2)}) collective-permute-start(bf16[32,512]{1,0:T(8,128)(2,1)S(1)} %get-tuple-element.57), channel_id=1, source_target_pairs={{4,8},{8,4},{5,9},{9,5},{6,10},{10,6},{7,11},{11,7},{20,24},{24,20... | collective-permute-start | bytes 98312 | tf_op jit(solution)/shard_map/ppermute | solution.py:551
  58.9 2.6 %copy-start.20 = (f32[512]{0:T(512)S(1)}, f32[512]{0:T(512)}, u32[]{:S(2)}) copy-start(f32[512]{0:T(512)} %param.46) | copy-start | bytes 6148
  61.6 13.1 %copy-start.8 = (f32[512]{0:T(512)S(1)}, f32[512]{0:T(512)}, u32[]{:S(2)}) copy-start(f32[512]{0:T(512)} %param.47) | copy-start | bytes 6148
  67.3 1.6 %collective-permute-start.25 = (bf16[256,512]{1,0:T(8,128)(2,1)S(1)}, bf16[256,512]{1,0:T(8,128)(2,1)S(1)}, u32[]{:S(2)}, u32[]{:S(2)}) collective-permute-start(bf16[256,512]{1,0:T(8,128)(2,1)S(1)} %get-tuple-element.59), channel_id=1, source_target_pairs={{0,1},{1,0},{2,3},{3,2},{4,5},{5,4},{6,7},{7,6},{8,9},{9,8},{10,11... | collective-permute-start | bytes 786440 | tf_op jit(solution)/shard_map/ppermute | solution.py:410
  67.4 2.2 %collective-permute-start.27 = (bf16[384,512]{1,0:T(8,128)(2,1)S(1)}, bf16[384,512]{1,0:T(8,128)(2,1)S(1)}, u32[]{:S(2)}, u32[]{:S(2)}) collective-permute-start(bf16[384,512]{1,0:T(8,128)(2,1)S(1)} %get-tuple-element.62.w0), channel_id=1, source_target_pairs={{0,1},{1,0},{2,3},{3,2},{4,5},{5,4},{6,7},{7,6},{8,9},{9,8},{10,11... | collective-permute-start | bytes 1179656 | tf_op jit(solution)/shard_map/ppermute | solution.py:410
  67.9 6.7 %collective-permute-start.29 = (bf16[384,512]{1,0:T(8,128)(2,1)S(1)}, bf16[384,512]{1,0:T(8,128)(2,1)S(1)}, u32[]{:S(2)}, u32[]{:S(2)}) collective-permute-start(bf16[384,512]{1,0:T(8,128)(2,1)S(1)} %collective-permute-done.28.w2), channel_id=1, source_target_pairs={{0,1},{1,0},{2,3},{3,2},{4,5},{5,4},{6,7},{7,6},{8,9},{9,8},{10,11... | collective-permute-start | bytes 1179656 | tf_op jit(solution)/shard_map/ppermute | solution.py:410
  69.0 5.6 %collective-permute-start.26 = (bf16[128,512]{1,0:T(8,128)(2,1)S(1)}, bf16[128,512]{1,0:T(8,128)(2,1)S(1)}, u32[]{:S(2)}, u32[]{:S(2)}) collective-permute-start(bf16[128,512]{1,0:T(8,128)(2,1)S(1)} %get-tuple-element.61), channel_id=1, source_target_pairs={{0,2},{1,3},{2,0},{3,1},{4,6},{5,7},{6,4},{7,5},{8,10},{9,11},{10,... | collective-permute-start | bytes 393224 | tf_op jit(solution)/shard_map/ppermute | solution.py:406

commit v4 on v3

--- a/solution.py
+++ b/solution.py
@@ -11,7 +11,7 @@
 OFFSETS = (-2, -1, 1, 2)
 STEP = 512
 GATHERED = 1024
-VMEM_FULL = 64 * 1024 * 1024
+LONG = 30 * 10**9
 VMEM_BYTES = 24 * 1024 * 1024
 I16 = jnp.int16
 BF16 = jnp.bfloat16
@@ -23,50 +23,57 @@
     return h + h * jnp.tanh(h)
 
 
-def region_of(delta):
-    return jnp.where(delta < 0, delta + 2, delta + 1)
-
-
 def halo_plan(count):
-    plan = []
-    if count == 4:
-        for bit in (1, 2, 3):
-            pairs = [(d, d ^ bit) for d in range(4) if abs((d ^ bit) - d) <= 2]
-            regions = [(OFFSETS.index((d ^ bit) - d) if abs((d ^ bit) - d) <= 2 else -1) for d in range(4)]
-            plan.append((pairs, regions, regions))
-    else:
-        for region, offset in enumerate(OFFSETS):
-            pairs = [(d, d + offset) for d in range(count) if 0 <= d + offset < count]
-            plan.append((pairs, region, 3 - region))
-    return plan
-
-
-def by_index(choice, index):
-    if isinstance(choice, int):
-        return choice
-    picked = jnp.int32(choice[0])
-    for place in range(1, len(choice)):
-        picked = jnp.where(index == place, choice[place], picked)
-    return picked
+    if count <= 5:
+        return [("all", place) for place in range(count)]
+    return [("region", region) for region in range(4)]
+
+
+def sent_region(entry, here):
+    kind, place = entry
+    if kind == "region":
+        return place, True
+    delta = place - here
+    region = jnp.where(delta < 0, delta + 2, delta + 1)
+    return jnp.clip(region, 0, 3), (delta != 0) & (delta >= -2) & (delta <= 2)
+
+
+def received_region(entry, here):
+    kind, place = entry
+    if kind == "region":
+        return 3 - place, True
+    return sent_region(entry, here)
+
+
+def exchange(plan, lists):
+    if plan[0][0] == "all":
+        return lax.all_to_all(lists, "dom", split_axis=0, concat_axis=0, tiled=True)
+    count = lax.axis_size("dom")
+    rows = lists.shape[0] // len(plan)
+    blocks = []
+    for place, (kind, region) in enumerate(plan):
+        step = OFFSETS[region]
+        pairs = [(d, d + step) for d in range(count) if 0 <= d + step < count]
+        blocks.append(lax.ppermute(lists[place * rows : (place + 1) * rows], "dom", pairs))
+    return jnp.concatenate(blocks, axis=0)
 
 
 def whole_refs(count):
     return [pl.BlockSpec(memory_space=pltpu.VMEM)] * count
 
 
-def call(body, outs, args, scratch=(), flops=0, smem=0, far=0, vmem=VMEM_BYTES):
+def call(body, outs, args, scratch=(), flops=0, smem=0):
     moved = sum(a.size * a.dtype.itemsize for a in args) + sum(
         o.size * jnp.dtype(o.dtype).itemsize for o in outs
     )
-    specs = [pl.BlockSpec(memory_space=pltpu.HBM)] * far + whole_refs(len(args) - smem - far)
-    specs += [pl.BlockSpec(memory_space=pltpu.SMEM)] * smem
+    specs = whole_refs(len(args) - smem) + [pl.BlockSpec(memory_space=pltpu.SMEM)] * smem
     return pl.pallas_call(
         body,
         out_shape=tuple(outs),
         in_specs=specs,
         out_specs=tuple(whole_refs(len(outs))),
         scratch_shapes=list(scratch),
-        compiler_params=pltpu.CompilerParams(vmem_limit_bytes=vmem),
+        compiler_params=pltpu.CompilerParams(vmem_limit_bytes=VMEM_BYTES),
         cost_estimate=pl.CostEstimate(flops=int(flops), bytes_accessed=int(moved), transcendentals=0),
     )(*args)
 
@@ -111,11 +118,13 @@
     return dot_first(hot(rows == listed.astype(I16)), table).astype(BF16)
 
 
-def pick_lists(plan, table, send, outs):
+def pick_lists(plan, table, send, out):
     here = lax.axis_index("dom")
-    for (pairs, sent, received), out in zip(plan, outs):
-        region = jnp.maximum(by_index(sent, here), 0)
-        out[...] = pick_rows(table, send[0, pl.ds(region, 1), :])
+    rows = out.shape[0] // len(plan)
+    for place, entry in enumerate(plan):
+        region, there = sent_region(entry, here)
+        listed = jnp.where(there, send[0, pl.ds(region, 1), :], -1)
+        out[place * rows : (place + 1) * rows, :] = pick_rows(table, listed)
 
 
 def stack_into(out, parts):
@@ -125,36 +134,18 @@
         first += part.shape[0]
 
 
-def fetch(sems, moves):
-    copies = [pltpu.make_async_copy(source, target, sems.at[k]) for k, (source, target) in enumerate(moves)]
-    for copy in copies:
-        copy.start()
-    return copies
-
-
-def own_half(ref):
-    rows = ref.shape[0] // 2
-    return ref.at[pl.ds(pl.multiple_of(lax.axis_index("groups") * rows, rows), rows), :]
-
-
-def first_pack_kernel(plan, grid, send, w_in, w_out, half, *rest):
-    outs = rest[: len(plan)]
-    listed, table, sems = rest[len(plan) :]
-    k, n = w_in.shape[0] // 2, w_out.shape[0] // 2
-    copies = fetch(
-        sems,
-        [
-            (send, listed),
-            (grid, table),
-            (own_half(w_in), half.at[pl.ds(0, k), :]),
-            (own_half(w_out), half.at[pl.ds(k, n), :]),
-        ],
-    )
-    copies[0].wait()
-    copies[1].wait()
-    pick_lists(plan, table[...], listed, outs)
-    copies[2].wait()
-    copies[3].wait()
+def begin_kernel(token):
+    token[...] = jnp.zeros(token.shape, token.dtype)
+
+
+def first_pack_kernel(plan, grid, send, w_in, w_out, token, half, out):
+    place = 0
+    for source in (w_in, w_out):
+        rows = source.shape[0] // 2
+        begin = pl.multiple_of(lax.axis_index("groups") * rows, 64)
+        half[place : place + rows, :] = source[pl.ds(begin, rows), :]
+        place += rows
+    pick_lists(plan, grid[...], send, out)
 
 
 def embed_kernel(e_in, e_out, p_in, p_out, egeom, egeo, pgeom, pgeo, after, weights, eout, pout):
@@ -210,9 +201,9 @@
     here = lax.axis_index("dom")
     lane = lax.broadcasted_iota(jnp.int32, (1, width), 1)
     target = jnp.full((1, width), -1, jnp.int32)
-    for place, (pairs, sent, received) in enumerate(plan):
-        region = by_index(received, here)
-        first = jnp.where(region < 0, -4 * node_rows, node_rows + region * slots)
+    for place, entry in enumerate(plan):
+        region, there = received_region(entry, here)
+        first = jnp.where(there, node_rows + region * slots, -4 * node_rows)
         inside = (lane >= place * slots) & (lane < (place + 1) * slots)
         target = jnp.where(inside, lane - place * slots + first, target)
     return target.astype(I16)
@@ -326,14 +317,14 @@
     stack_into(packed, (n_in, n_out))
 
 
-def middle_kernel(plan, mine, theirs, send, full, *outs):
+def middle_kernel(plan, mine, theirs, send, full, out):
     rows = mine.shape[0] // 2
     core = lax.rem(lax.axis_index("sub"), 2)
     for half in range(2):
         for part, which in ((mine, core), (theirs, 1 - core)):
             place = pl.multiple_of((2 * half + which) * rows, rows)
             full[pl.ds(place, rows), :] = part[half * rows : (half + 1) * rows, :]
-    pick_lists(plan, full[...], send, outs)
+    pick_lists(plan, full[...], send, out)
 
 
 def proc_first_kernel(k_in, first_row, emb, full, edges, w0, w1, across, both, round_, round_both, table, pre, w_source, w_out, stack):
@@ -362,12 +353,11 @@
 
 
 def proc_second_kernel(
-    plan, slots, node_rows, n_halo, emb, edges, gain, table, pre, w_source, w_out, *rest
+    plan, slots, node_rows, emb, edges, gain, table, pre, w_source, w_out, halos,
+    live, keep, give, halo_table, messages, totals,
 ):
-    halos = rest[:n_halo]
-    live, keep, give, halo_table, messages, totals = rest[n_halo:]
     d = pre.shape[1]
-    got = jnp.concatenate([h[...] for h in halos], axis=0)
+    got = halos[...]
     halo_table[: got.shape[0], :] = dot(got, w_source[...]).astype(BF16)
     if got.shape[0] < halo_table.shape[0]:
         halo_table[got.shape[0] :, :] = jnp.zeros((halo_table.shape[0] - got.shape[0], d), BF16)
@@ -461,25 +451,19 @@
     width = grid_lat.shape[1]
 
     slots = grid_send.shape[2]
-    edge_half, *outgoing = call(
+    (token,) = call(begin_kernel, [shape(16, 128)], [], flops=LONG)
+    edge_half, outgoing = call(
         functools.partial(first_pack_kernel, plan),
-        [shape((k_in + k_out) // 2, d)] + [shape(slots, width)] * len(plan),
-        [grid_lat, grid_send, enc_edge_in, enc_edge_out],
-        scratch=[
-            pltpu.VMEM(grid_send.shape, jnp.int32),
-            pltpu.VMEM(grid_lat.shape, BF16),
-            pltpu.SemaphoreType.DMA((4,)),
-        ],
-        far=4,
-        vmem=VMEM_FULL - 512 * 1024,
+        [shape((k_in + k_out) // 2, d), shape(len(plan) * slots, width)],
+        [grid_lat, grid_send, enc_edge_in, enc_edge_out, token],
     )
     edge_across = to_chip(edge_half)
-    halos = [lax.ppermute(v, "dom", entry[0]) for v, entry in zip(outgoing, plan)]
+    halos = exchange(plan, outgoing)
     got = len(plan) * slots
     (lat,) = call(
         concat_kernel,
         [shape(grid_rows + mesh_rows + got, width)],
-        [grid_lat, mesh_lat, *halos],
+        [grid_lat, mesh_lat, halos],
     )
     lat_across = to_chip(lat)
     lat_beside = to_core(lat)
@@ -542,13 +526,13 @@
         flops=2 * half * d * 3 * d,
     )
     slots = mesh_send.shape[2]
-    mid, *outgoing = call(
+    mid, outgoing = call(
         functools.partial(middle_kernel, plan),
-        [shape(mesh_rows, d)] + [shape(slots, d)] * len(plan),
+        [shape(mesh_rows, d), shape(len(plan) * slots, d)],
         [mid_half, to_core(mid_half), mesh_send],
         flops=2 * len(plan) * slots * mesh_rows * d,
     )
-    halos = [lax.ppermute(v, "dom", entry[0]) for v, entry in zip(outgoing, plan)]
+    halos = exchange(plan, outgoing)
     last_across, last_beside = to_chip(last_w), to_core(last_w)
     early = n_proc // 2
     table, pre, w_source, w_out = call(
@@ -563,9 +547,9 @@
     )
     halo_rows = padded(len(plan) * slots)
     keep, give = call(
-        functools.partial(proc_second_kernel, plan, slots, mesh_rows, len(plan)),
+        functools.partial(proc_second_kernel, plan, slots, mesh_rows),
         [shape(half, d), shape(half, d)],
-        [proc_emb, proc_edges, proc_edge_gain, table, pre, w_source, w_out, *halos, proc_blocks],
+        [proc_emb, proc_edges, proc_edge_gain, table, pre, w_source, w_out, halos, proc_blocks],
         scratch=[
             pltpu.VMEM((halo_rows, d), BF16),
             pltpu.VMEM((n_proc, d), BF16),

time: 77.6 us -> 88.5 us (1.14)
  the two profiles are of different devices: /device:TPU:12 before, /device:TPU:0 now
where the time goes in v4:
time: 88.5 us; the launch traced here: 87.9 us
  waiting for transfers between devices  22 us (25%)
  Pallas kernels  20.4 us (23%)
  starting transfers between devices  18 us (20%)
  local copies, waits for them, and re-layouts  15.5 us (18%)
  blocking collectives  10.4 us (12%)
  between operations  1.65 us (2%)
    pallas_call x14, Pallas kernels, call(): pl.pallas_call(body, out_shape=tuple(outs), in_specs=specs, out_specs=tup...  20.4 us
    ppermute x6, waiting for transfers between devices, to_chip(): return lax.ppermute(v, 'sub', [(i, i ^ 2) for i in range(4)])  17 us
    unnamed x66, local copies, waits for them, and re-layouts  15.5 us
    all_to_all x1, blocking collectives, exchange(): return lax.all_to_all(lists, 'dom', split_axis=0, concat_axis=0, tiled=True)  10.4 us
    ppermute x6, starting transfers between devices, to_chip(): return lax.ppermute(v, 'sub', [(i, i ^ 2) for i in range(4)])  7.76 us
    ppermute x16, starting transfers between devices, to_core(): return lax.ppermute(v, 'sub', [(i, i ^ 1) for i in range(4)])  3.72 us
    all_to_all x1, starting transfers between devices, exchange(): return lax.all_to_all(lists, 'dom', split_axis=0, concat_axis=0, tiled=True)  3.51 us
    ppermute x2, starting transfers between devices, to_group(): return lax.ppermute(v, 'groups', [(i, count - 1 - i) for i in range(count)])  3.04 us
  transfers between devices with their start and end apart: 25, of which 8 were waited for; matrix products, arithmetic and copies ran while one was open for 0% of the time, Pallas kernels for 21%

profile of v4, /device:TPU:0, one launch (start us, length us, event | category | flops | bytes accessed | tf_op | source)
XLA Modules:
  0.0 87.9 jit_solution(4737512701979472113)
XLA Ops:
  0.1 0.8 copy-done
  0.9 0.2 copy-done.1
  1.1 0.0 copy-done.4
  1.1 0.3 shard_map.227
  1.5 3.0 %collective-permute-start.5 = (bf16[256,512]{1,0:T(8,128)(2,1)S(1)}, bf16[256,512]{1,0:T(8,128)(2,1)S(1)}, u32[]{:S(2)}, u32[]{:S(2)}) collective-permute-start(bf16[256,512]{1,0:T(8,128)(2,1)S(1)} %get-tuple-element.34), channel_id=1, source_target_pairs={{0,2},{1,3},{2,0},{3,1},{4,6},{5,7},{6,4},{7,5},{8,10},{9,11},{10,... | collective-permute-start | bytes 786440 | tf_op jit(solution)/shard_map/ppermute | solution.py:396
  4.5 10.4 %all_to_all.22 = bf16[4,64,128]{2,1,0:T(8,128)(2,1)S(1)} all-to-all(bf16[4,64,128]{2,1,0:T(8,128)(2,1)S(1)} %bitcast.10), channel_id=1, replica_groups=mesh['groups'=2,'dom'=4,'sub'=4] {'dom'}, dimensions={0} | all-to-all | bytes 131072 | tf_op jit(solution)/shard_map/all_to_all | solution.py:50
  14.9 0.6 collective-permute-start
  15.5 1.5 %collective-permute-start.6 = (bf16[256,512]{1,0:T(8,128)(2,1)S(1)}, bf16[256,512]{1,0:T(8,128)(2,1)S(1)}, u32[]{:S(2)}, u32[]{:S(2)}) collective-permute-start(bf16[256,512]{1,0:T(8,128)(2,1)S(1)} %collective-permute-done.5.across), channel_id=1, source_target_pairs={{0,16},{16,0},{1,17},{17,1},{2,18},{18,2},{3,19},{19,3},{4,20},{20... | collective-permute-start | bytes 786440 | tf_op jit(solution)/shard_map/ppermute | solution.py:405
  17.0 0.0 collective-permute-start.3
  17.0 0.5 collective-permute-start.4
  17.6 1.8 %shard_map.229 = (bf16[896,512]{1,0:T(8,128)(2,1)S(1)}, bf16[1024,512]{1,0:T(8,128)(2,1)S(1)}, bf16[2048,512]{1,0:T(8,128)(2,1)S(1)}) custom-call(bf16[256,512]{1,0:T(8,128)(2,1)S(1)} %copy-done.11, bf16[128,512]{1,0:T(8,128)(2,1)S(1)} %copy-done.12, bf16[384,512]{1,0:T(8,128)(2,1)S(1)} %copy-done.10, bf16[128,512]{1,0:T(8,128)(2,1)S(1)} %copy-done.13, ...), custom_call_target="tpu_custom_call" | custom-call | flops 402653184 | bytes 5373952 | tf_op jit(solution)/shard_map/pallas_call | solution.py:70
  19.4 1.3 %copy-done.22 = bf16[2048,512]{1,0:T(8,128)(2,1)} copy-done((bf16[2048,512]{1,0:T(8,128)(2,1)}, bf16[2048,512]{1,0:T(8,128)(2,1)S(1)}, u32[]{:S(2)}) %copy-start.22) | copy-done | bytes 2097176
  20.7 2.1 %collective-permute-done.lat.l1 = bf16[1280,128]{1,0:T(8,128)(2,1)S(1)} collective-permute-done((bf16[1280,128]{1,0:T(8,128)(2,1)S(1)}, bf16[1280,128]{1,0:T(8,128)(2,1)S(1)}, u32[]{:S(2)}, u32[]{:S(2)}) %collective-permute-start) | collective-permute-done | bytes 327712 | tf_op jit(solution)/shard_map/ppermute | solution.py:396
  22.8 0.1 shard_map.230
  22.8 0.1 collective-permute-start.2
  22.9 0.0 collective-permute-done.4.b_out
  22.9 0.5 collective-permute-start.7
  23.4 0.1 collective-permute-start.8
  23.5 0.0 collective-permute-done.3.b_in
  23.5 0.4 collective-permute-start.11
  23.9 0.5 collective-permute-start.12
  25.1 0.0 collective-permute-done.7.both
  25.2 0.1 collective-permute-done.8.round_both
  25.3 0.0 copy-start.6
  25.3 4.9 %shard_map.231 = (bf16[256,512]{1,0:T(8,128)(2,1)S(1)}, bf16[256,512]{1,0:T(8,128)(2,1)S(1)}, bf16[256,512]{1,0:T(8,128)(2,1)S(1)}) custom-call(bf16[1024,512]{1,0:T(8,128)(2,1)S(1)} %get-tuple-element.31.emb, s32[2,1024]{1,0:T(2,128)S(1)} %copy-done.19, f32[1,512]{1,0:T(1,128)S(1)} %bitcast.13, bf16[1280,128]{1,0:T(8,128)(2,1)S(1)} %shard_map.228.after.l0, ...), custom_call_target="tpu_custom_call" | custom-call | flops 2952790016 | bytes 5253124 | tf_op jit(solution)/shard_map/pallas_call | solution.py:70
  30.2 0.2 collective-permute-start.9
  30.4 1.4 %collective-permute-done.9.theirs = bf16[256,512]{1,0:T(8,128)(2,1)S(1)} collective-permute-done((bf16[256,512]{1,0:T(8,128)(2,1)S(1)}, bf16[256,512]{1,0:T(8,128)(2,1)S(1)}, u32[]{:S(2)}, u32[]{:S(2)}) %collective-permute-start.9) | collective-permute-done | bytes 262176 | tf_op jit(solution)/shard_map/ppermute | solution.py:400
  31.8 0.1 shard_map.232.after.mine
  31.9 1.5 %collective-permute-start.10 = (bf16[256,512]{1,0:T(8,128)(2,1)S(1)}, bf16[256,512]{1,0:T(8,128)(2,1)S(1)}, u32[]{:S(2)}, u32[]{:S(2)}) collective-permute-start(bf16[256,512]{1,0:T(8,128)(2,1)S(1)} %shard_map.232.after.mine), channel_id=1, source_target_pairs={{0,2},{1,3},{2,0},{3,1},{4,6},{5,7},{6,4},{7,5},{8,10},{9,11},{10,... | collective-permute-start | bytes 786440 | tf_op jit(solution)/shard_map/ppermute | solution.py:396
  33.3 8.2 %collective-permute-done.12.source.w2 = bf16[640,512]{1,0:T(8,128)(2,1)S(1)} collective-permute-done((bf16[640,512]{1,0:T(8,128)(2,1)S(1)}, bf16[640,512]{1,0:T(8,128)(2,1)S(1)}, u32[]{:S(2)}, u32[]{:S(2)}) %collective-permute-start.12) | collective-permute-done | bytes 655392 | tf_op jit(solution)/shard_map/ppermute | solution.py:396
  41.6 0.0 copy-start.8
  41.6 0.1 collective-permute-start.13
  41.7 0.5 collective-permute-start.14
  42.2 1.5 %collective-permute-start.17 = (bf16[256,512]{1,0:T(8,128)(2,1)S(1)}, bf16[256,512]{1,0:T(8,128)(2,1)}, u32[]{:S(2)}, u32[]{:S(2)}) collective-permute-start(bf16[256,512]{1,0:T(8,128)(2,1)S(1)} %get-tuple-element.44.across), channel_id=1, source_target_pairs={{0,16},{16,0},{1,17},{17,1},{2,18},{18,2},{3,19},{19,3},{4,20},{20... | collective-permute-start | bytes 786440 | tf_op jit(solution)/shard_map/ppermute | solution.py:405
  43.7 2.6 %collective-permute-done.10.theirs = bf16[256,512]{1,0:T(8,128)(2,1)S(1)} collective-permute-done((bf16[256,512]{1,0:T(8,128)(2,1)S(1)}, bf16[256,512]{1,0:T(8,128)(2,1)S(1)}, u32[]{:S(2)}, u32[]{:S(2)}) %collective-permute-start.10) | collective-permute-done | bytes 262176 | tf_op jit(solution)/shard_map/ppermute | solution.py:396
  46.3 0.0 copy-start.16
  46.3 1.0 %shard_map.234 = (bf16[256,512]{1,0:T(8,128)(2,1)S(1)}, bf16[384,512]{1,0:T(8,128)(2,1)S(1)}) custom-call(bf16[256,512]{1,0:T(8,128)(2,1)S(1)} %get-tuple-element.35.mesh, bf16[256,512]{1,0:T(8,128)(2,1)S(1)} %shard_map.232.after.mine, bf16[256,512]{1,0:T(8,128)(2,1)S(1)} %collective-permute-done.10.theirs, f32[1,512]{1,0:T(1,128)S(1)} %bitcast.11, ...), custom_call_target="tpu_custom_call" | custom-call | flops 402653184 | bytes 4720640 | tf_op jit(solution)/shard_map/pallas_call | solution.py:70
  47.3 0.1 collective-permute-start.15
  47.4 0.5 collective-permute-start.16
  47.9 2.6 %collective-permute-done.17.round_ = bf16[256,512]{1,0:T(8,128)(2,1)} collective-permute-done((bf16[256,512]{1,0:T(8,128)(2,1)S(1)}, bf16[256,512]{1,0:T(8,128)(2,1)}, u32[]{:S(2)}, u32[]{:S(2)}) %collective-permute-start.17) | collective-permute-done | bytes 262176 | tf_op jit(solution)/shard_map/ppermute | solution.py:405
  50.6 1.2 %shard_map.235 = (bf16[512,512]{1,0:T(8,128)(2,1)S(1)}, bf16[128,512]{1,0:T(8,128)(2,1)}) custom-call(bf16[256,512]{1,0:T(8,128)(2,1)S(1)} %get-tuple-element.41.mine, bf16[256,512]{1,0:T(8,128)(2,1)S(1)} %collective-permute-done.15.theirs, s32[1,4,32]{2,1,0:T(4,128)S(1)} %copy-done.8), custom_call_target="tpu_custom_call" | custom-call | flops 67108864 | bytes 1180160 | tf_op jit(solution)/shard_map/pallas_call | solution.py:70
  51.8 3.5 %all-to-all-start.1 = ((bf16[4,32,512]{2,1,0:T(8,128)(2,1)}), bf16[4,32,512]{2,1,0:T(8,128)(2,1)S(1)}, u32[]{:S(2)}, u32[]{:S(2)}) async-start(bf16[4,32,512]{2,1,0:T(8,128)(2,1)} %bitcast.5), calls=%async_computation.1 | async-start | bytes 262144 | tf_op jit(solution)/shard_map/all_to_all | solution.py:50
  55.9 0.6 collective-permute-start.22
  56.6 1.6 %copy-done.23 = bf16[2048,512]{1,0:T(8,128)(2,1)S(1)} copy-done((bf16[2048,512]{1,0:T(8,128)(2,1)S(1)}, bf16[2048,512]{1,0:T(8,128)(2,1)}, u32[]{:S(2)}) %copy-start.23) | copy-done | bytes 2097176
  58.1 3.7 %shard_map.236 = (bf16[1536,512]{1,0:T(8,128)(2,1)S(1)}, f32[1024,512]{1,0:T(8,128)S(1)}, bf16[512,512]{1,0:T(8,128)(2,1)S(1)}, bf16[512,512]{1,0:T(8,128)(2,1)S(1)}) custom-call(bf16[2048,512]{1,0:T(8,128)(2,1)S(1)} %copy-done.23, bf16[512,512]{1,0:T(8,128)(2,1)S(1)} %get-tuple-element.42.full, s32[2,2048]{1,0:T(2,128)S(1)} %copy-done.16, ...), custom_call_target="tpu_custom_call" | custom-call | flops 1610612736 | bytes 10240000 | tf_op jit(solution)/shard_map/pallas_call | solution.py:70
  61.8 1.3 %copy-done.25 = f32[1024,512]{1,0:T(8,128)} copy-done((f32[1024,512]{1,0:T(8,128)}, f32[1024,512]{1,0:T(8,128)S(1)}, u32[]{:S(2)}) %copy-start.25) | copy-done | bytes 2097176
  63.2 1.2 %copy-done.27 = bf16[1536,512]{1,0:T(8,128)(2,1)} copy-done((bf16[1536,512]{1,0:T(8,128)(2,1)}, bf16[1536,512]{1,0:T(8,128)(2,1)S(1)}, u32[]{:S(2)}) %copy-start.27) | copy-done | bytes 1572888
  64.4 0.8 copy-done.29
  65.2 0.8 copy-done.31
  66.0 0.7 copy-done.21
  66.6 1.6 %copy-done.24 = bf16[2048,512]{1,0:T(8,128)(2,1)S(1)} copy-done((bf16[2048,512]{1,0:T(8,128)(2,1)S(1)}, bf16[2048,512]{1,0:T(8,128)(2,1)}, u32[]{:S(2)}) %copy-start.24) | copy-done | bytes 2097176
  68.2 1.6 %copy-done.26 = f32[1024,512]{1,0:T(8,128)S(1)} copy-done((f32[1024,512]{1,0:T(8,128)S(1)}, f32[1024,512]{1,0:T(8,128)}, u32[]{:S(2)}) %copy-start.26) | copy-done | bytes 2097176
  69.8 1.4 %copy-done.28 = bf16[1536,512]{1,0:T(8,128)(2,1)S(1)} copy-done((bf16[1536,512]{1,0:T(8,128)(2,1)S(1)}, bf16[1536,512]{1,0:T(8,128)(2,1)}, u32[]{:S(2)}) %copy-start.28) | copy-done | bytes 1572888
  71.2 1.0 %copy-done.30 = bf16[512,512]{1,0:T(8,128)(2,1)S(1)} copy-done((bf16[512,512]{1,0:T(8,128)(2,1)S(1)}, bf16[512,512]{1,0:T(8,128)(2,1)}, u32[]{:S(2)}) %copy-start.30) | copy-done | bytes 524312
  72.3 1.0 %copy-done.32 = bf16[512,512]{1,0:T(8,128)(2,1)S(1)} copy-done((bf16[512,512]{1,0:T(8,128)(2,1)S(1)}, bf16[512,512]{1,0:T(8,128)(2,1)}, u32[]{:S(2)}) %copy-start.32) | copy-done | bytes 524312
  73.3 5.8 %shard_map.237 = (bf16[256,512]{1,0:T(8,128)(2,1)S(1)}, bf16[256,512]{1,0:T(8,128)(2,1)S(1)}) custom-call(bf16[2048,512]{1,0:T(8,128)(2,1)S(1)} %copy-done.24, s32[2,2048]{1,0:T(2,128)S(1)} %copy-done.16, f32[1,512]{1,0:T(1,128)S(1)} %bitcast.14, bf16[1536,512]{1,0:T(8,128)(2,1)S(1)} %copy-done.28, f32[1024,512]{1,0:T(8,128)S(1)} %copy-done.26, ...), custom_call_target="tpu_custom_call" | custom-call | flops 3489660928 | bytes 7489540 | tf_op jit(solution)/shard_map/pallas_call | solution.py:70
  79.1 0.3 collective-permute-start.19
  79.4 0.3 collective-permute-start.21
  79.7 0.2 collective-permute-start.23
  79.9 0.8 collective-permute-done.19.theirs
  80.7 0.1 shard_map.238
  80.8 1.6 %collective-permute-start.20 = (bf16[128,512]{1,0:T(8,128)(2,1)S(1)}, bf16[128,512]{1,0:T(8,128)(2,1)S(1)}, u32[]{:S(2)}, u32[]{:S(2)}) collective-permute-start(bf16[128,512]{1,0:T(8,128)(2,1)S(1)} %get-tuple-element.53), channel_id=1, source_target_pairs={{0,2},{1,3},{2,0},{3,1},{4,6},{5,7},{6,4},{7,5},{8,10},{9,11},{10,... | collective-permute-start | bytes 393224 | tf_op jit(solution)/shard_map/ppermute | solution.py:396
  82.3 4.1 %collective-permute-done.20.theirs = bf16[128,512]{1,0:T(8,128)(2,1)S(1)} collective-permute-done((bf16[128,512]{1,0:T(8,128)(2,1)S(1)}, bf16[128,512]{1,0:T(8,128)(2,1)S(1)}, u32[]{:S(2)}, u32[]{:S(2)}) %collective-permute-start.20) | collective-permute-done | bytes 131104 | tf_op jit(solution)/shard_map/ppermute | solution.py:396
  86.5 1.5 %shard_map.239 = bf16[128,512]{1,0:T(8,128)(2,1)} custom-call(bf16[512,512]{1,0:T(8,128)(2,1)S(1)} %get-tuple-element.42.full, bf16[128,512]{1,0:T(8,128)(2,1)S(1)} %get-tuple-element.52.mine, bf16[128,512]{1,0:T(8,128)(2,1)S(1)} %collective-permute-done.20.theirs, f32[1,512]{1,0:T(1,128)S(1)} %bitcast.12, bf16[384,512]{1,0:T(8,128)(2,1)S(1)} %get-tuple-element.54.w0, ...), custom_call_target="tpu_custom_call" | custom-call | flops 201326592 | bytes 2492416 | tf_op jit(solution)/shard_map/pallas_call | solution.py:70
  (67 shorter events, 0.2 us)
Async XLA Ops:
  0.0 0.9 %copy-start = (bf16[512,128]{1,0:T(8,128)(2,1)S(1)}, bf16[512,128]{1,0:T(8,128)(2,1)}, u32[]{:S(2)}) copy-start(bf16[512,128]{1,0:T(8,128)(2,1)} %refs_0_.1) | copy-start | bytes 393220
  0.0 0.9 %copy-start.7 = (s32[1,4,64]{2,1,0:T(4,128)S(1)}, s32[1,4,64]{2,1,0:T(4,128)}, u32[]{:S(2)}) copy-start(s32[1,4,64]{2,1,0:T(4,128)} %send.2) | copy-start | bytes 3076
  0.0 1.1 %copy-start.1 = (bf16[384,512]{1,0:T(8,128)(2,1)S(1)}, bf16[384,512]{1,0:T(8,128)(2,1)}, u32[]{:S(2)}) copy-start(bf16[384,512]{1,0:T(8,128)(2,1)} %o_in.1) | copy-start | bytes 1179652
  0.0 1.1 %copy-start.4 = (bf16[128,512]{1,0:T(8,128)(2,1)S(1)}, bf16[128,512]{1,0:T(8,128)(2,1)}, u32[]{:S(2)}) copy-start(bf16[128,512]{1,0:T(8,128)(2,1)} %o_out.1) | copy-start | bytes 393220
  0.0 14.9 %copy-start.3 = (bf16[512,128]{1,0:T(8,128)(2,1)S(1)}, bf16[512,128]{1,0:T(8,128)(2,1)}, u32[]{:S(2)}) copy-start(bf16[512,128]{1,0:T(8,128)(2,1)} %refs_1_.1) | copy-start | bytes 393220
  0.0 17.5 %copy-start.15 = (f32[4,1024]{1,0:T(4,128)S(1)}, f32[4,1024]{1,0:T(4,128)}, u32[]{:S(2)}) copy-start(f32[4,1024]{1,0:T(4,128)} %egeom.1) | copy-start | bytes 49156
  0.0 17.5 %copy-start.14 = (f32[4,2048]{1,0:T(4,128)S(1)}, f32[4,2048]{1,0:T(4,128)}, u32[]{:S(2)}) copy-start(f32[4,2048]{1,0:T(4,128)} %pgeom.1) | copy-start | bytes 98308
  0.0 17.5 %copy-start.17 = (f32[4,512]{1,0:T(4,128)S(1)}, f32[4,512]{1,0:T(4,128)}, u32[]{:S(2)}) copy-start(f32[4,512]{1,0:T(4,128)} %egeo.1) | copy-start | bytes 24580
  0.0 17.5 %copy-start.18 = (f32[4,512]{1,0:T(4,128)S(1)}, f32[4,512]{1,0:T(4,128)}, u32[]{:S(2)}) copy-start(f32[4,512]{1,0:T(4,128)} %pgeo.1) | copy-start | bytes 24580
  0.1 17.5 %copy-start.11 = (bf16[256,512]{1,0:T(8,128)(2,1)S(1)}, bf16[256,512]{1,0:T(8,128)(2,1)}, u32[]{:S(2)}) copy-start(bf16[256,512]{1,0:T(8,128)(2,1)} %e_in.1) | copy-start | bytes 786436
  0.1 17.5 %copy-start.12 = (bf16[128,512]{1,0:T(8,128)(2,1)S(1)}, bf16[128,512]{1,0:T(8,128)(2,1)}, u32[]{:S(2)}) copy-start(bf16[128,512]{1,0:T(8,128)(2,1)} %e_out.1) | copy-start | bytes 393220
  0.1 17.5 %copy-start.10 = (bf16[384,512]{1,0:T(8,128)(2,1)S(1)}, bf16[384,512]{1,0:T(8,128)(2,1)}, u32[]{:S(2)}) copy-start(bf16[384,512]{1,0:T(8,128)(2,1)} %p_in.1) | copy-start | bytes 1179652
  0.1 17.5 %copy-start.13 = (bf16[128,512]{1,0:T(8,128)(2,1)S(1)}, bf16[128,512]{1,0:T(8,128)(2,1)}, u32[]{:S(2)}) copy-start(bf16[128,512]{1,0:T(8,128)(2,1)} %p_out.1) | copy-start | bytes 393220
  1.1 24.2 %copy-start.19 = (s32[2,1024]{1,0:T(2,128)S(1)}, s32[2,1024]{1,0:T(2,128)}, u32[]{:S(2)}) copy-start(s32[2,1024]{1,0:T(2,128)} %edges.3) | copy-start | bytes 24580
  1.1 24.2 %copy-start.20 = (f32[512]{0:T(512)S(1)}, f32[512]{0:T(512)}, u32[]{:S(2)}) copy-start(f32[512]{0:T(512)} %param.44) | copy-start | bytes 6148
  1.5 14.0 %collective-permute-start.5 = (bf16[256,512]{1,0:T(8,128)(2,1)S(1)}, bf16[256,512]{1,0:T(8,128)(2,1)S(1)}, u32[]{:S(2)}, u32[]{:S(2)}) collective-permute-start(bf16[256,512]{1,0:T(8,128)(2,1)S(1)} %get-tuple-element.34), channel_id=1, source_target_pairs={{0,2},{1,3},{2,0},{3,1},{4,6},{5,7},{6,4},{7,5},{8,10},{9,11},{10,... | collective-permute-start | bytes 786440 | tf_op jit(solution)/shard_map/ppermute | solution.py:396
  14.9 7.9 %collective-permute-start = (bf16[1280,128]{1,0:T(8,128)(2,1)S(1)}, bf16[1280,128]{1,0:T(8,128)(2,1)S(1)}, u32[]{:S(2)}, u32[]{:S(2)}) collective-permute-start(bf16[1280,128]{1,0:T(8,128)(2,1)S(1)} %shard_map.228.after.l0), channel_id=1, source_target_pairs={{0,2},{1,3},{2,0},{3,1},{4,6},{5,7},{6,4},{7,5},{8,10},{9,11},{10,... | collective-permute-start | bytes 983048 | tf_op jit(solution)/shard_map/ppermute | solution.py:396
  15.5 7.9 %collective-permute-start.6 = (bf16[256,512]{1,0:T(8,128)(2,1)S(1)}, bf16[256,512]{1,0:T(8,128)(2,1)S(1)}, u32[]{:S(2)}, u32[]{:S(2)}) collective-permute-start(bf16[256,512]{1,0:T(8,128)(2,1)S(1)} %collective-permute-done.5.across), channel_id=1, source_target_pairs={{0,16},{16,0},{1,17},{17,1},{2,18},{18,2},{3,19},{19,3},{4,20},{20... | collective-permute-start | bytes 786440 | tf_op jit(solution)/shard_map/ppermute | solution.py:405
  17.0 6.5 %collective-permute-start.3 = (bf16[384,512]{1,0:T(8,128)(2,1)S(1)}, bf16[384,512]{1,0:T(8,128)(2,1)S(1)}, u32[]{:S(2)}, u32[]{:S(2)}) collective-permute-start(bf16[384,512]{1,0:T(8,128)(2,1)S(1)} %copy-done.1), channel_id=1, source_target_pairs={{0,1},{1,0},{2,3},{3,2},{4,5},{5,4},{6,7},{7,6},{8,9},{9,8},{10,11... | collective-permute-start | bytes 1179656 | tf_op jit(solution)/shard_map/ppermute | solution.py:400
  17.0 5.9 %collective-permute-start.4 = (bf16[128,512]{1,0:T(8,128)(2,1)S(1)}, bf16[128,512]{1,0:T(8,128)(2,1)S(1)}, u32[]{:S(2)}, u32[]{:S(2)}) collective-permute-start(bf16[128,512]{1,0:T(8,128)(2,1)S(1)} %copy-done.4), channel_id=1, source_target_pairs={{0,1},{1,0},{2,3},{3,2},{4,5},{5,4},{6,7},{7,6},{8,9},{9,8},{10,11... | collective-permute-start | bytes 393224 | tf_op jit(solution)/shard_map/ppermute | solution.py:400
  17.5 6.4 %collective-permute-start.1 = (bf16[1280,128]{1,0:T(8,128)(2,1)S(1)}, bf16[1280,128]{1,0:T(8,128)(2,1)S(1)}, u32[]{:S(2)}, u32[]{:S(2)}) collective-permute-start(bf16[1280,128]{1,0:T(8,128)(2,1)S(1)} %shard_map.228.after.l0), channel_id=1, source_target_pairs={{0,1},{1,0},{2,3},{3,2},{4,5},{5,4},{6,7},{7,6},{8,9},{9,8},{10,11... | collective-permute-start | bytes 983048 | tf_op jit(solution)/shard_map/ppermute | solution.py:400
  19.4 1.3 %copy-start.22 = (bf16[2048,512]{1,0:T(8,128)(2,1)}, bf16[2048,512]{1,0:T(8,128)(2,1)S(1)}, u32[]{:S(2)}) copy-start(bf16[2048,512]{1,0:T(8,128)(2,1)S(1)} %get-tuple-element.43.emb) | copy-start | bytes 6291460
  22.8 2.3 %collective-permute-start.2 = (bf16[1280,128]{1,0:T(8,128)(2,1)S(1)}, bf16[1280,128]{1,0:T(8,128)(2,1)S(1)}, u32[]{:S(2)}, u32[]{:S(2)}) collective-permute-start(bf16[1280,128]{1,0:T(8,128)(2,1)S(1)} %get-tuple-element.33), channel_id=1, source_target_pairs={{0,1},{1,0},{2,3},{3,2},{4,5},{5,4},{6,7},{7,6},{8,9},{9,8},{10,11... | collective-permute-start | bytes 983048 | tf_op jit(solution)/shard_map/ppermute | solution.py:400
  22.9 2.2 %collective-permute-start.7 = (bf16[256,512]{1,0:T(8,128)(2,1)S(1)}, bf16[256,512]{1,0:T(8,128)(2,1)S(1)}, u32[]{:S(2)}, u32[]{:S(2)}) collective-permute-start(bf16[256,512]{1,0:T(8,128)(2,1)S(1)} %collective-permute-done.5.across), channel_id=1, source_target_pairs={{0,1},{1,0},{2,3},{3,2},{4,5},{5,4},{6,7},{7,6},{8,9},{9,8},{10,11... | collective-permute-start | bytes 786440 | tf_op jit(solution)/shard_map/ppermute | solution.py:400
  23.4 1.9 %collective-permute-start.8 = (bf16[256,512]{1,0:T(8,128)(2,1)S(1)}, bf16[256,512]{1,0:T(8,128)(2,1)S(1)}, u32[]{:S(2)}, u32[]{:S(2)}) collective-permute-start(bf16[256,512]{1,0:T(8,128)(2,1)S(1)} %collective-permute-done.6.round_), channel_id=1, source_target_pairs={{0,1},{1,0},{2,3},{3,2},{4,5},{5,4},{6,7},{7,6},{8,9},{9,8},{10,11... | collective-permute-start | bytes 786440 | tf_op jit(solution)/shard_map/ppermute | solution.py:400
  23.5 20.2 %collective-permute-start.11 = (bf16[896,512]{1,0:T(8,128)(2,1)S(1)}, bf16[896,512]{1,0:T(8,128)(2,1)S(1)}, u32[]{:S(2)}, u32[]{:S(2)}) collective-permute-start(bf16[896,512]{1,0:T(8,128)(2,1)S(1)} %get-tuple-element.32.weights.w0), channel_id=1, source_target_pairs={{0,1},{1,0},{2,3},{3,2},{4,5},{5,4},{6,7},{7,6},{8,9},{9,8},{10,11... | collective-permute-start | bytes 2752520 | tf_op jit(solution)/shard_map/ppermute | solution.py:400
  23.9 17.6 %collective-permute-start.12 = (bf16[640,512]{1,0:T(8,128)(2,1)S(1)}, bf16[640,512]{1,0:T(8,128)(2,1)S(1)}, u32[]{:S(2)}, u32[]{:S(2)}) collective-permute-start(bf16[640,512]{1,0:T(8,128)(2,1)S(1)} %get-tuple-element.38), channel_id=1, source_target_pairs={{0,2},{1,3},{2,0},{3,1},{4,6},{5,7},{6,4},{7,5},{8,10},{9,11},{10,... | collective-permute-start | bytes 1966088 | tf_op jit(solution)/shard_map/ppermute | solution.py:396
  25.3 21.0 %copy-start.2 = (bf16[256,512]{1,0:T(8,128)(2,1)S(1)}, bf16[256,512]{1,0:T(8,128)(2,1)}, u32[]{:S(2)}) copy-start(bf16[256,512]{1,0:T(8,128)(2,1)} %n_in.1) | copy-start | bytes 786436
  25.3 21.0 %copy-start.5 = (bf16[128,512]{1,0:T(8,128)(2,1)S(1)}, bf16[128,512]{1,0:T(8,128)(2,1)}, u32[]{:S(2)}) copy-start(bf16[128,512]{1,0:T(8,128)(2,1)} %n_out.1) | copy-start | bytes 393220
  25.3 21.0 %copy-start.6 = (f32[512]{0:T(512)S(1)}, f32[512]{0:T(512)}, u32[]{:S(2)}) copy-start(f32[512]{0:T(512)} %param.45) | copy-start | bytes 6148
  30.2 1.6 %collective-permute-start.9 = (bf16[256,512]{1,0:T(8,128)(2,1)S(1)}, bf16[256,512]{1,0:T(8,128)(2,1)S(1)}, u32[]{:S(2)}, u32[]{:S(2)}) collective-permute-start(bf16[256,512]{1,0:T(8,128)(2,1)S(1)} %get-tuple-element.37), channel_id=1, source_target_pairs={{0,1},{1,0},{2,3},{3,2},{4,5},{5,4},{6,7},{7,6},{8,9},{9,8},{10,11... | collective-permute-start | bytes 786440 | tf_op jit(solution)/shard_map/ppermute | solution.py:400
  31.9 14.4 %collective-permute-start.10 = (bf16[256,512]{1,0:T(8,128)(2,1)S(1)}, bf16[256,512]{1,0:T(8,128)(2,1)S(1)}, u32[]{:S(2)}, u32[]{:S(2)}) collective-permute-start(bf16[256,512]{1,0:T(8,128)(2,1)S(1)} %shard_map.232.after.mine), channel_id=1, source_target_pairs={{0,2},{1,3},{2,0},{3,1},{4,6},{5,7},{6,4},{7,5},{8,10},{9,11},{10,... | collective-permute-start | bytes 786440 | tf_op jit(solution)/shard_map/ppermute | solution.py:396
  41.6 9.0 %copy-start.8 = (s32[1,4,32]{2,1,0:T(4,128)S(1)}, s32[1,4,32]{2,1,0:T(4,128)}, u32[]{:S(2)}) copy-start(s32[1,4,32]{2,1,0:T(4,128)} %send.3) | copy-start | bytes 1540
  41.6 2.1 %collective-permute-start.13 = (bf16[192,512]{1,0:T(8,128)(2,1)S(1)}, bf16[192,512]{1,0:T(8,128)(2,1)S(1)}, u32[]{:S(2)}, u32[]{:S(2)}) collective-permute-start(bf16[192,512]{1,0:T(8,128)(2,1)S(1)} %get-tuple-element.39), channel_id=1, source_target_pairs={{0,1},{1,0},{2,3},{3,2},{4,5},{5,4},{6,7},{7,6},{8,9},{9,8},{10,11... | collective-permute-start | bytes 589832 | tf_op jit(solution)/shard_map/ppermute | solution.py:400
  41.7 2.0 %collective-permute-start.14 = (bf16[192,512]{1,0:T(8,128)(2,1)S(1)}, bf16[192,512]{1,0:T(8,128)(2,1)S(1)}, u32[]{:S(2)}, u32[]{:S(2)}) collective-permute-start(bf16[192,512]{1,0:T(8,128)(2,1)S(1)} %get-tuple-element.40), channel_id=1, source_target_pairs={{0,1},{1,0},{2,3},{3,2},{4,5},{5,4},{6,7},{7,6},{8,9},{9,8},{10,11... | collective-permute-start | bytes 589832 | tf_op jit(solution)/shard_map/ppermute | solution.py:400
  42.2 8.4 %collective-permute-start.17 = (bf16[256,512]{1,0:T(8,128)(2,1)S(1)}, bf16[256,512]{1,0:T(8,128)(2,1)}, u32[]{:S(2)}, u32[]{:S(2)}) collective-permute-start(bf16[256,512]{1,0:T(8,128)(2,1)S(1)} %get-tuple-element.44.across), channel_id=1, source_target_pairs={{0,16},{16,0},{1,17},{17,1},{2,18},{18,2},{3,19},{19,3},{4,20},{20... | collective-permute-start | bytes 786440 | tf_op jit(solution)/shard_map/ppermute | solution.py:405
  46.3 10.2 %copy-start.16 = (s32[2,2048]{1,0:T(2,128)S(1)}, s32[2,2048]{1,0:T(2,128)}, u32[]{:S(2)}) copy-start(s32[2,2048]{1,0:T(2,128)} %edges.5) | copy-start | bytes 49156
  47.3 3.2 %collective-permute-start.15 = (bf16[256,512]{1,0:T(8,128)(2,1)S(1)}, bf16[256,512]{1,0:T(8,128)(2,1)S(1)}, u32[]{:S(2)}, u32[]{:S(2)}) collective-permute-start(bf16[256,512]{1,0:T(8,128)(2,1)S(1)} %get-tuple-element.41.mine), channel_id=1, source_target_pairs={{0,1},{1,0},{2,3},{3,2},{4,5},{5,4},{6,7},{7,6},{8,9},{9,8},{10,11... | collective-permute-start | bytes 786440 | tf_op jit(solution)/shard_map/ppermute | solution.py:400
  47.4 9.1 %collective-permute-start.16 = (bf16[256,512]{1,0:T(8,128)(2,1)S(1)}, bf16[256,512]{1,0:T(8,128)(2,1)}, u32[]{:S(2)}, u32[]{:S(2)}) collective-permute-start(bf16[256,512]{1,0:T(8,128)(2,1)S(1)} %get-tuple-element.44.across), channel_id=1, source_target_pairs={{0,1},{1,0},{2,3},{3,2},{4,5},{5,4},{6,7},{7,6},{8,9},{9,8},{10,11... | collective-permute-start | bytes 786440 | tf_op jit(solution)/shard_map/ppermute | solution.py:400
  50.6 6.0 %collective-permute-start.18 = (bf16[256,512]{1,0:T(8,128)(2,1)}, bf16[256,512]{1,0:T(8,128)(2,1)}, u32[]{:S(2)}, u32[]{:S(2)}) collective-permute-start(bf16[256,512]{1,0:T(8,128)(2,1)} %collective-permute-done.17.round_), channel_id=1, source_target_pairs={{0,1},{1,0},{2,3},{3,2},{4,5},{5,4},{6,7},{7,6},{8,9},{9,8},{10,11... | collective-permute-start | bytes 786440 | tf_op jit(solution)/shard_map/ppermute | solution.py:400
  51.8 14.2 %all-to-all-start.1 = ((bf16[4,32,512]{2,1,0:T(8,128)(2,1)}), bf16[4,32,512]{2,1,0:T(8,128)(2,1)S(1)}, u32[]{:S(2)}, u32[]{:S(2)}) async-start(bf16[4,32,512]{2,1,0:T(8,128)(2,1)} %bitcast.5), calls=%async_computation.1 | async-start | bytes 262144 | tf_op jit(solution)/shard_map/all_to_all | solution.py:50
  55.9 23.7 %collective-permute-start.22 = (bf16[384,512]{1,0:T(8,128)(2,1)S(1)}, bf16[384,512]{1,0:T(8,128)(2,1)S(1)}, u32[]{:S(2)}, u32[]{:S(2)}) collective-permute-start(bf16[384,512]{1,0:T(8,128)(2,1)S(1)} %get-tuple-element.54.w0), channel_id=1, source_target_pairs={{0,2},{1,3},{2,0},{3,1},{4,6},{5,7},{6,4},{7,5},{8,10},{9,11},{10,... | collective-permute-start | bytes 1179656 | tf_op jit(solution)/shard_map/ppermute | solution.py:396
  56.5 1.6 %copy-start.23 = (bf16[2048,512]{1,0:T(8,128)(2,1)S(1)}, bf16[2048,512]{1,0:T(8,128)(2,1)}, u32[]{:S(2)}) copy-start(bf16[2048,512]{1,0:T(8,128)(2,1)} %copy-done.22) | copy-start | bytes 6291460
  61.8 1.3 %copy-start.25 = (f32[1024,512]{1,0:T(8,128)}, f32[1024,512]{1,0:T(8,128)S(1)}, u32[]{:S(2)}) copy-start(f32[1024,512]{1,0:T(8,128)S(1)} %get-tuple-element.46.pre) | copy-start | bytes 6291460
  63.2 1.2 %copy-start.27 = (bf16[1536,512]{1,0:T(8,128)(2,1)}, bf16[1536,512]{1,0:T(8,128)(2,1)S(1)}, u32[]{:S(2)}) copy-start(bf16[1536,512]{1,0:T(8,128)(2,1)S(1)} %get-tuple-element.45.table) | copy-start | bytes 4718596
  64.4 0.8 copy-start.29
  65.2 0.8 copy-start.31
  66.0 0.7 copy-start.21
  66.6 1.6 %copy-start.24 = (bf16[2048,512]{1,0:T(8,128)(2,1)S(1)}, bf16[2048,512]{1,0:T(8,128)(2,1)}, u32[]{:S(2)}) copy-start(bf16[2048,512]{1,0:T(8,128)(2,1)} %copy-done.22) | copy-start | bytes 6291460
  68.2 1.6 %copy-start.26 = (f32[1024,512]{1,0:T(8,128)S(1)}, f32[1024,512]{1,0:T(8,128)}, u32[]{:S(2)}) copy-start(f32[1024,512]{1,0:T(8,128)} %copy-done.25) | copy-start | bytes 6291460
  69.8 1.4 %copy-start.28 = (bf16[1536,512]{1,0:T(8,128)(2,1)S(1)}, bf16[1536,512]{1,0:T(8,128)(2,1)}, u32[]{:S(2)}) copy-start(bf16[1536,512]{1,0:T(8,128)(2,1)} %copy-done.27) | copy-start | bytes 4718596
  71.2 1.0 %copy-start.30 = (bf16[512,512]{1,0:T(8,128)(2,1)S(1)}, bf16[512,512]{1,0:T(8,128)(2,1)}, u32[]{:S(2)}) copy-start(bf16[512,512]{1,0:T(8,128)(2,1)} %copy-done.29) | copy-start | bytes 1572868
  72.3 1.0 %copy-start.32 = (bf16[512,512]{1,0:T(8,128)(2,1)S(1)}, bf16[512,512]{1,0:T(8,128)(2,1)}, u32[]{:S(2)}) copy-start(bf16[512,512]{1,0:T(8,128)(2,1)} %copy-done.31) | copy-start | bytes 1572868
  73.3 13.1 %copy-start.9 = (f32[512]{0:T(512)S(1)}, f32[512]{0:T(512)}, u32[]{:S(2)}) copy-start(f32[512]{0:T(512)} %param.47) | copy-start | bytes 6148
  79.1 1.6 %collective-permute-start.19 = (bf16[256,512]{1,0:T(8,128)(2,1)S(1)}, bf16[256,512]{1,0:T(8,128)(2,1)S(1)}, u32[]{:S(2)}, u32[]{:S(2)}) collective-permute-start(bf16[256,512]{1,0:T(8,128)(2,1)S(1)} %get-tuple-element.51), channel_id=1, source_target_pairs={{0,1},{1,0},{2,3},{3,2},{4,5},{5,4},{6,7},{7,6},{8,9},{9,8},{10,11... | collective-permute-start | bytes 786440 | tf_op jit(solution)/shard_map/ppermute | solution.py:400
  79.4 2.9 %collective-permute-start.21 = (bf16[384,512]{1,0:T(8,128)(2,1)S(1)}, bf16[384,512]{1,0:T(8,128)(2,1)S(1)}, u32[]{:S(2)}, u32[]{:S(2)}) collective-permute-start(bf16[384,512]{1,0:T(8,128)(2,1)S(1)} %get-tuple-element.54.w0), channel_id=1, source_target_pairs={{0,1},{1,0},{2,3},{3,2},{4,5},{5,4},{6,7},{7,6},{8,9},{9,8},{10,11... | collective-permute-start | bytes 1179656 | tf_op jit(solution)/shard_map/ppermute | solution.py:400
  79.7 2.7 %collective-permute-start.23 = (bf16[384,512]{1,0:T(8,128)(2,1)S(1)}, bf16[384,512]{1,0:T(8,128)(2,1)S(1)}, u32[]{:S(2)}, u32[]{:S(2)}) collective-permute-start(bf16[384,512]{1,0:T(8,128)(2,1)S(1)} %collective-permute-done.22.w2), channel_id=1, source_target_pairs={{0,1},{1,0},{2,3},{3,2},{4,5},{5,4},{6,7},{7,6},{8,9},{9,8},{10,11... | collective-permute-start | bytes 1179656 | tf_op jit(solution)/shard_map/ppermute | solution.py:400
  80.8 5.7 %collective-permute-start.20 = (bf16[128,512]{1,0:T(8,128)(2,1)S(1)}, bf16[128,512]{1,0:T(8,128)(2,1)S(1)}, u32[]{:S(2)}, u32[]{:S(2)}) collective-permute-start(bf16[128,512]{1,0:T(8,128)(2,1)S(1)} %get-tuple-element.53), channel_id=1, source_target_pairs={{0,2},{1,3},{2,0},{3,1},{4,6},{5,7},{6,4},{7,5},{8,10},{9,11},{10,... | collective-permute-start | bytes 393224 | tf_op jit(solution)/shard_map/ppermute | solution.py:396

commit v5 on v3

--- a/solution.py
+++ b/solution.py
@@ -11,7 +11,7 @@
 OFFSETS = (-2, -1, 1, 2)
 STEP = 512
 GATHERED = 1024
-VMEM_FULL = 64 * 1024 * 1024
+LONG = 30 * 10**9
 VMEM_BYTES = 24 * 1024 * 1024
 I16 = jnp.int16
 BF16 = jnp.bfloat16
@@ -54,19 +54,18 @@
     return [pl.BlockSpec(memory_space=pltpu.VMEM)] * count
 
 
-def call(body, outs, args, scratch=(), flops=0, smem=0, far=0, vmem=VMEM_BYTES):
+def call(body, outs, args, scratch=(), flops=0, smem=0):
     moved = sum(a.size * a.dtype.itemsize for a in args) + sum(
         o.size * jnp.dtype(o.dtype).itemsize for o in outs
     )
-    specs = [pl.BlockSpec(memory_space=pltpu.HBM)] * far + whole_refs(len(args) - smem - far)
-    specs += [pl.BlockSpec(memory_space=pltpu.SMEM)] * smem
+    specs = whole_refs(len(args) - smem) + [pl.BlockSpec(memory_space=pltpu.SMEM)] * smem
     return pl.pallas_call(
         body,
         out_shape=tuple(outs),
         in_specs=specs,
         out_specs=tuple(whole_refs(len(outs))),
         scratch_shapes=list(scratch),
-        compiler_params=pltpu.CompilerParams(vmem_limit_bytes=vmem),
+        compiler_params=pltpu.CompilerParams(vmem_limit_bytes=VMEM_BYTES),
         cost_estimate=pl.CostEstimate(flops=int(flops), bytes_accessed=int(moved), transcendentals=0),
     )(*args)
 
@@ -106,16 +105,17 @@
     return jnp.where(cond, BF16(1), BF16(0))
 
 
-def pick_rows(table, listed):
-    rows = lax.broadcasted_iota(I16, (table.shape[0], 1), 0)
+def pick_rows(table, listed, rows=None):
+    if rows is None:
+        rows = lax.broadcasted_iota(I16, (table.shape[0], 1), 0)
     return dot_first(hot(rows == listed.astype(I16)), table).astype(BF16)
 
 
-def pick_lists(plan, table, send, outs):
+def pick_lists(plan, table, send, outs, rows=None):
     here = lax.axis_index("dom")
     for (pairs, sent, received), out in zip(plan, outs):
         region = jnp.maximum(by_index(sent, here), 0)
-        out[...] = pick_rows(table, send[0, pl.ds(region, 1), :])
+        out[...] = pick_rows(table, send[0, pl.ds(region, 1), :], rows)
 
 
 def stack_into(out, parts):
@@ -125,36 +125,18 @@
         first += part.shape[0]
 
 
-def fetch(sems, moves):
-    copies = [pltpu.make_async_copy(source, target, sems.at[k]) for k, (source, target) in enumerate(moves)]
-    for copy in copies:
-        copy.start()
-    return copies
-
-
-def own_half(ref):
-    rows = ref.shape[0] // 2
-    return ref.at[pl.ds(pl.multiple_of(lax.axis_index("groups") * rows, rows), rows), :]
-
-
-def first_pack_kernel(plan, grid, send, w_in, w_out, half, *rest):
-    outs = rest[: len(plan)]
-    listed, table, sems = rest[len(plan) :]
-    k, n = w_in.shape[0] // 2, w_out.shape[0] // 2
-    copies = fetch(
-        sems,
-        [
-            (send, listed),
-            (grid, table),
-            (own_half(w_in), half.at[pl.ds(0, k), :]),
-            (own_half(w_out), half.at[pl.ds(k, n), :]),
-        ],
-    )
-    copies[0].wait()
-    copies[1].wait()
-    pick_lists(plan, table[...], listed, outs)
-    copies[2].wait()
-    copies[3].wait()
+def begin_kernel(token):
+    token[...] = jnp.zeros(token.shape, token.dtype)
+
+
+def first_pack_kernel(plan, grid, send, w_in, w_out, token, half, *outs):
+    place = 0
+    for source in (w_in, w_out):
+        rows = source.shape[0] // 2
+        begin = pl.multiple_of(lax.axis_index("groups") * rows, 64)
+        half[place : place + rows, :] = source[pl.ds(begin, rows), :]
+        place += rows
+    pick_lists(plan, grid[...], send, outs)
 
 
 def embed_kernel(e_in, e_out, p_in, p_out, egeom, egeo, pgeom, pgeo, after, weights, eout, pout):
@@ -316,29 +298,37 @@
     out[...] = add(mine[...], theirs[...])
 
 
-def node_kernel(k_in, k_out, mesh, mine, theirs, gain, n_in, n_out, w0, w1, w2, w3, w4, out, packed, stack):
+def node_kernel(
+    plan, k_in, k_out, mesh, mine, theirs, gain, n_in, n_out, w0, w1, w2, w3, w4, send, out, packed, *rest
+):
+    outs, stack = rest[:-1], rest[-1]
     for shard, bit in zip((w0, w1, w2), (0, 1, 2)):
         put_shard(stack, shard, 0, bit)
     put_shard(stack, w3, 0, 3, 0, 2)
     put_shard(stack, w4, 0, 3, 1, 2)
     w_in, w_out = joined(stack, 0, k_in), joined(stack, k_in, k_out)
-    out[...] = node_update(mesh[...], add(mine[...], theirs[...]), w_in, w_out, gain[...])
+    fresh = node_update(mesh[...], add(mine[...], theirs[...]), w_in, w_out, gain[...])
+    out[...] = fresh
+    half = fresh.shape[0] // 2
+    core = lax.rem(lax.axis_index("sub"), 2)
+    place = lax.broadcasted_iota(jnp.int32, (fresh.shape[0], 1), 0)
+    rows = place + core * half + jnp.where(place < half, 0, half)
+    pick_lists(plan, fresh, send, outs, rows.astype(I16))
     stack_into(packed, (n_in, n_out))
 
 
-def middle_kernel(plan, mine, theirs, send, full, *outs):
-    rows = mine.shape[0] // 2
+def proc_first_kernel(
+    k_in, first_row, emb, mine, theirs, edges, w0, w1, across, both, round_, round_both,
+    table, pre, w_source, w_out, stack, full,
+):
+    d = full.shape[1]
+    node_rows = full.shape[0]
+    rows = node_rows // 4
     core = lax.rem(lax.axis_index("sub"), 2)
     for half in range(2):
         for part, which in ((mine, core), (theirs, 1 - core)):
             place = pl.multiple_of((2 * half + which) * rows, rows)
             full[pl.ds(place, rows), :] = part[half * rows : (half + 1) * rows, :]
-    pick_lists(plan, full[...], send, outs)
-
-
-def proc_first_kernel(k_in, first_row, emb, full, edges, w0, w1, across, both, round_, round_both, table, pre, w_source, w_out, stack):
-    d = full.shape[1]
-    node_rows = full.shape[0]
     put_shard(stack, w0, first_row, 0)
     put_shard(stack, w1, first_row, 1)
     put_half(stack, k_in, across, 0, 2, 0)
@@ -362,12 +352,11 @@
 
 
 def proc_second_kernel(
-    plan, slots, node_rows, n_halo, emb, edges, gain, table, pre, w_source, w_out, *rest
+    plan, slots, node_rows, emb, edges, gain, table, pre, w_source, w_out, halo, halo_beside,
+    live, keep, give, halo_table, messages, totals,
 ):
-    halos = rest[:n_halo]
-    live, keep, give, halo_table, messages, totals = rest[n_halo:]
     d = pre.shape[1]
-    got = jnp.concatenate([h[...] for h in halos], axis=0)
+    got = halo[...] + halo_beside[...]
     halo_table[: got.shape[0], :] = dot(got, w_source[...]).astype(BF16)
     if got.shape[0] < halo_table.shape[0]:
         halo_table[got.shape[0] :, :] = jnp.zeros((halo_table.shape[0] - got.shape[0], d), BF16)
@@ -393,9 +382,10 @@
         out[...] = add(mine[pl.ds(place, rows), :], theirs[pl.ds(place, rows), :])
 
 
-def out_kernel(k_in, k_out, full, mine, theirs, gain, w0, w1, w2, w3, out, stack):
+def out_kernel(k_in, k_out, middle, mine, theirs, gain, w0, w1, w2, w3, out, stack):
     rows = mine.shape[0]
-    mesh = full[pl.ds(pl.multiple_of(lax.axis_index("sub") * rows, rows), rows), :]
+    chip = lax.div(lax.axis_index("sub"), 2)
+    mesh = middle[pl.ds(pl.multiple_of(chip * rows, rows), rows), :]
     for shard, bit in zip((w0, w1, w2, w3), (0, 1, 2, 3)):
         put_shard(stack, shard, 0, bit)
     w_in, w_out = joined(stack, 0, k_in), joined(stack, k_in, k_out)
@@ -461,17 +451,11 @@
     width = grid_lat.shape[1]
 
     slots = grid_send.shape[2]
+    (token,) = call(begin_kernel, [shape(16, 128)], [], flops=LONG)
     edge_half, *outgoing = call(
         functools.partial(first_pack_kernel, plan),
         [shape((k_in + k_out) // 2, d)] + [shape(slots, width)] * len(plan),
-        [grid_lat, grid_send, enc_edge_in, enc_edge_out],
-        scratch=[
-            pltpu.VMEM(grid_send.shape, jnp.int32),
-            pltpu.VMEM(grid_lat.shape, BF16),
-            pltpu.SemaphoreType.DMA((4,)),
-        ],
-        far=4,
-        vmem=VMEM_FULL - 512 * 1024,
+        [grid_lat, grid_send, enc_edge_in, enc_edge_out, token],
     )
     edge_across = to_chip(edge_half)
     halos = [lax.ppermute(v, "dom", entry[0]) for v, entry in zip(outgoing, plan)]
@@ -531,41 +515,37 @@
     )
     node_both = [to_core(v) for v in node_across]
     proc_round = to_group(proc_across)
-    mid_half, last_w = call(
-        functools.partial(node_kernel, n_in, n_out),
-        [shape(half, d), shape(n_in + n_out, d)],
+    slots = mesh_send.shape[2]
+    mid_half, last_w, *outgoing = call(
+        functools.partial(node_kernel, plan, n_in, n_out),
+        [shape(half, d), shape(n_in + n_out, d)] + [shape(slots, d)] * len(plan),
         [
             own_mesh, chip_sum, to_chip(chip_sum), enc_node_gain, proc_node_in, proc_node_out,
-            next_w, next_beside, next_across, *node_both,
+            next_w, next_beside, next_across, *node_both, mesh_send,
         ],
         scratch=[pltpu.VMEM((4 * (n_in + n_out), d), BF16)],
         flops=2 * half * d * 3 * d,
     )
-    slots = mesh_send.shape[2]
-    mid, *outgoing = call(
-        functools.partial(middle_kernel, plan),
-        [shape(mesh_rows, d)] + [shape(slots, d)] * len(plan),
-        [mid_half, to_core(mid_half), mesh_send],
-        flops=2 * len(plan) * slots * mesh_rows * d,
-    )
     halos = [lax.ppermute(v, "dom", entry[0]) for v, entry in zip(outgoing, plan)]
+    (halo,) = call(concat_kernel, [shape(len(plan) * slots, d)], halos)
+    halo_beside = to_core(halo)
     last_across, last_beside = to_chip(last_w), to_core(last_w)
     early = n_proc // 2
     table, pre, w_source, w_out = call(
         functools.partial(proc_first_kernel, k_in, n_in + n_out),
         [shape(d + 2 * mesh_rows, d), shape(early, d, F32), shape(d, d), shape(d, d)],
         [
-            proc_emb, mid, proc_edges, next_w, next_beside, proc_across, to_core(proc_across),
+            proc_emb, mid_half, to_core(mid_half), proc_edges, next_w, next_beside, proc_across, to_core(proc_across),
             proc_round, to_core(proc_round),
         ],
-        scratch=[pltpu.VMEM((4 * (k_in + k_out), d), BF16)],
+        scratch=[pltpu.VMEM((4 * (k_in + k_out), d), BF16), pltpu.VMEM((mesh_rows, d), BF16)],
         flops=2 * early * d * (d + 2 * mesh_rows),
     )
     halo_rows = padded(len(plan) * slots)
     keep, give = call(
-        functools.partial(proc_second_kernel, plan, slots, mesh_rows, len(plan)),
+        functools.partial(proc_second_kernel, plan, slots, mesh_rows),
         [shape(half, d), shape(half, d)],
-        [proc_emb, proc_edges, proc_edge_gain, table, pre, w_source, w_out, *halos, proc_blocks],
+        [proc_emb, proc_edges, proc_edge_gain, table, pre, w_source, w_out, halo, halo_beside, proc_blocks],
         scratch=[
             pltpu.VMEM((halo_rows, d), BF16),
             pltpu.VMEM((n_proc, d), BF16),
@@ -579,7 +559,7 @@
     (result,) = call(
         functools.partial(out_kernel, n_in, n_out),
         [shape(quarter, d)],
-        [mid, mine, to_chip(other), proc_node_gain, last_w, last_beside, last_across, to_core(last_across)],
+        [mid_half, mine, to_chip(other), proc_node_gain, last_w, last_beside, last_across, to_core(last_across)],
         scratch=[pltpu.VMEM((4 * (n_in + n_out), d), BF16)],
         flops=2 * quarter * d * 3 * d,
     )

time: 77.6 us -> 72.3 us (0.932); the launches traced: 76.1 us -> 72.1 us
  waiting for transfers between devices: 22.7 us -> 31 us
  local copies, waits for them, and re-layouts: 8.49 us -> 1.08 us
  starting transfers between devices: 23.3 us -> 20 us
  Pallas kernels: 20 us -> 18.2 us
    unnamed x42 -> x44, local copies, waits for them, and re-layouts: 8.49 us -> 1.08 us
    ppermute x6, waiting for transfers between devices: 14.9 us -> 19.6 us  [to_chip(): return lax.ppermute(v, 'sub', [(i, i ^ 2) for i in range(4)])]
    ppermute x6, waiting for transfers between devices: 3.47 us -> 7.47 us  [local(): lax.ppermute(v, 'dom', entry[0])]
    pallas_call x13 -> x14, Pallas kernels: 20 us -> 18.2 us  [call(): pl.pallas_call(body, out_shape=tuple(outs), in_specs=specs, out_specs=tup...]
    ppermute x6, starting transfers between devices: 11 us -> 9.85 us  [local(): lax.ppermute(v, 'dom', entry[0])]
    ppermute x2, starting transfers between devices: 2.09 us -> 1.08 us  [to_group(): return lax.ppermute(v, 'groups', [(i, count - 1 - i) for i in range(count)])]
    ppermute x6, starting transfers between devices: 6.56 us -> 5.68 us  [to_chip(): return lax.ppermute(v, 'sub', [(i, i ^ 2) for i in range(4)])]
    ppermute x16 -> x17, waiting for transfers between devices: 3.55 us -> 3.34 us  [to_core(): return lax.ppermute(v, 'sub', [(i, i ^ 1) for i in range(4)])]
  transfers between devices with their start and end apart: 30 -> 31, of which waited for: 9 -> 12; matrix products, arithmetic and copies ran while one was open for 0% -> 0% of each run, Pallas kernels for 22% -> 23%
where the time goes in v5:
time: 72.3 us; the launch traced here: 72.1 us
  waiting for transfers between devices  31 us (43%)
  starting transfers between devices  20 us (28%)
  Pallas kernels  18.2 us (25%)
  between operations  1.76 us (2%)
  local copies, waits for them, and re-layouts  1.08 us (1%)
    ppermute x6, waiting for transfers between devices, to_chip(): return lax.ppermute(v, 'sub', [(i, i ^ 2) for i in range(4)])  19.6 us
    pallas_call x14, Pallas kernels, call(): pl.pallas_call(body, out_shape=tuple(outs), in_specs=specs, out_specs=tup...  18.2 us
    ppermute x6, starting transfers between devices, local(): lax.ppermute(v, 'dom', entry[0])  9.85 us
    ppermute x6, waiting for transfers between devices, local(): lax.ppermute(v, 'dom', entry[0])  7.47 us
    ppermute x6, starting transfers between devices, to_chip(): return lax.ppermute(v, 'sub', [(i, i ^ 2) for i in range(4)])  5.68 us
    ppermute x17, starting transfers between devices, to_core(): return lax.ppermute(v, 'sub', [(i, i ^ 1) for i in range(4)])  3.44 us
    ppermute x17, waiting for transfers between devices, to_core(): return lax.ppermute(v, 'sub', [(i, i ^ 1) for i in range(4)])  3.34 us
  transfers between devices with their start and end apart: 31, of which 12 were waited for; matrix products, arithmetic and copies ran while one was open for 0% of the time, Pallas kernels for 23%

profile of v5, /device:TPU:12, one launch (start us, length us, event | category | flops | bytes accessed | tf_op | source)
XLA Modules:
  0.0 72.1 jit_solution(1995203151844961882)
XLA Ops:
  0.1 0.8 %copy-done = bf16[512,128]{1,0:T(8,128)(2,1)S(1)} copy-done((bf16[512,128]{1,0:T(8,128)(2,1)S(1)}, bf16[512,128]{1,0:T(8,128)(2,1)}, u32[]{:S(2)}) %copy-start) | copy-done | bytes 131096
  0.9 0.2 copy-done.1
  1.1 0.0 copy-done.4
  1.1 0.3 shard_map.227
  1.4 1.6 %collective-permute-start.8 = (bf16[256,512]{1,0:T(8,128)(2,1)S(1)}, bf16[256,512]{1,0:T(8,128)(2,1)S(1)}, u32[]{:S(2)}, u32[]{:S(2)}) collective-permute-start(bf16[256,512]{1,0:T(8,128)(2,1)S(1)} %get-tuple-element.39), channel_id=1, source_target_pairs={{0,2},{1,3},{2,0},{3,1},{4,6},{5,7},{6,4},{7,5},{8,10},{9,11},{10,... | collective-permute-start | bytes 786440 | tf_op jit(solution)/shard_map/ppermute | solution.py:396
  3.0 0.4 collective-permute-start
  3.4 2.6 %collective-permute-start.1 = (bf16[64,128]{1,0:T(8,128)(2,1)S(1)}, bf16[64,128]{1,0:T(8,128)(2,1)S(1)}, u32[]{:S(2)}, u32[]{:S(2)}) collective-permute-start(bf16[64,128]{1,0:T(8,128)(2,1)S(1)} %get-tuple-element.34), channel_id=1, source_target_pairs={{0,8},{4,12},{8,0},{12,4},{1,9},{5,13},{9,1},{13,5},{2,10},{6,14},... | collective-permute-start | bytes 49160 | tf_op jit(solution)/shard_map/ppermute | solution.py:461
  6.0 2.3 %collective-permute-start.2 = (bf16[64,128]{1,0:T(8,128)(2,1)S(1)}, bf16[64,128]{1,0:T(8,128)(2,1)S(1)}, u32[]{:S(2)}, u32[]{:S(2)}) collective-permute-start(bf16[64,128]{1,0:T(8,128)(2,1)S(1)} %get-tuple-element.35), channel_id=1, source_target_pairs={{4,8},{8,4},{5,9},{9,5},{6,10},{10,6},{7,11},{11,7},{20,24},{24,20... | collective-permute-start | bytes 49160 | tf_op jit(solution)/shard_map/ppermute | solution.py:461
  8.4 0.0 collective-permute-done.1.refs_3_
  8.4 3.2 %collective-permute-done.2.refs_4_ = bf16[64,128]{1,0:T(8,128)(2,1)S(1)} collective-permute-done((bf16[64,128]{1,0:T(8,128)(2,1)S(1)}, bf16[64,128]{1,0:T(8,128)(2,1)S(1)}, u32[]{:S(2)}, u32[]{:S(2)}) %collective-permute-start.2) | collective-permute-done | bytes 16416 | tf_op jit(solution)/shard_map/ppermute | solution.py:461
  11.7 0.6 collective-permute-start.3
  12.3 0.0 collective-permute-done.8.across
  12.3 0.5 collective-permute-start.9
  12.8 0.0 collective-permute-start.6
  12.8 0.5 collective-permute-start.4
  13.3 0.0 collective-permute-start.7
  13.4 1.8 %shard_map.229 = (bf16[896,512]{1,0:T(8,128)(2,1)S(1)}, bf16[1024,512]{1,0:T(8,128)(2,1)S(1)}, bf16[2048,512]{1,0:T(8,128)(2,1)S(1)}) custom-call(bf16[256,512]{1,0:T(8,128)(2,1)S(1)} %copy-done.11, bf16[128,512]{1,0:T(8,128)(2,1)S(1)} %copy-done.12, bf16[384,512]{1,0:T(8,128)(2,1)S(1)} %copy-done.10, bf16[128,512]{1,0:T(8,128)(2,1)S(1)} %copy-done.13, ...), custom_call_target="tpu_custom_call" | custom-call | flops 402653184 | bytes 5357568 | tf_op jit(solution)/shard_map/pallas_call | solution.py:62
  15.1 3.9 %collective-permute-done.3.lat.l1 = bf16[1216,128]{1,0:T(8,128)(2,1)S(1)} collective-permute-done((bf16[1216,128]{1,0:T(8,128)(2,1)S(1)}, bf16[1216,128]{1,0:T(8,128)(2,1)S(1)}, u32[]{:S(2)}, u32[]{:S(2)}) %collective-permute-start.3) | collective-permute-done | bytes 311328 | tf_op jit(solution)/shard_map/ppermute | solution.py:396
  19.0 0.1 shard_map.230
  19.1 0.1 collective-permute-start.5
  19.2 0.5 collective-permute-start.10
  19.7 0.1 collective-permute-start.11
  19.7 0.0 collective-permute-done.4.l2
  19.7 0.4 collective-permute-start.14
  20.2 0.7 collective-permute-start.15
  21.5 0.0 collective-permute-done.5.l3
  21.5 0.0 copy-start.2
  21.6 0.0 copy-start.5
  21.6 0.0 copy-start.7
  21.6 0.0 copy-start.8
  21.6 4.8 %shard_map.231 = (bf16[256,512]{1,0:T(8,128)(2,1)S(1)}, bf16[256,512]{1,0:T(8,128)(2,1)S(1)}, bf16[256,512]{1,0:T(8,128)(2,1)S(1)}) custom-call(bf16[1024,512]{1,0:T(8,128)(2,1)S(1)} %get-tuple-element.36.emb, s32[2,1024]{1,0:T(2,128)S(1)} %copy-done.19, f32[1,512]{1,0:T(1,128)S(1)} %bitcast.6, bf16[1216,128]{1,0:T(8,128)(2,1)S(1)} %shard_map.228.after.l0, ...), custom_call_target="tpu_custom_call" | custom-call | flops 2952790016 | bytes 5187588 | tf_op jit(solution)/shard_map/pallas_call | solution.py:62
  26.4 0.1 collective-permute-start.12
  26.5 1.5 %collective-permute-done.12.theirs = bf16[256,512]{1,0:T(8,128)(2,1)S(1)} collective-permute-done((bf16[256,512]{1,0:T(8,128)(2,1)S(1)}, bf16[256,512]{1,0:T(8,128)(2,1)S(1)}, u32[]{:S(2)}, u32[]{:S(2)}) %collective-permute-start.12) | collective-permute-done | bytes 262176 | tf_op jit(solution)/shard_map/ppermute | solution.py:400
  28.0 0.1 shard_map.232.after.mine
  28.0 1.4 %collective-permute-start.13 = (bf16[256,512]{1,0:T(8,128)(2,1)S(1)}, bf16[256,512]{1,0:T(8,128)(2,1)S(1)}, u32[]{:S(2)}, u32[]{:S(2)}) collective-permute-start(bf16[256,512]{1,0:T(8,128)(2,1)S(1)} %shard_map.232.after.mine), channel_id=1, source_target_pairs={{0,2},{1,3},{2,0},{3,1},{4,6},{5,7},{6,4},{7,5},{8,10},{9,11},{10,... | collective-permute-start | bytes 786440 | tf_op jit(solution)/shard_map/ppermute | solution.py:396
  29.5 8.3 %collective-permute-done.15.source.w2 = bf16[640,512]{1,0:T(8,128)(2,1)S(1)} collective-permute-done((bf16[640,512]{1,0:T(8,128)(2,1)S(1)}, bf16[640,512]{1,0:T(8,128)(2,1)S(1)}, u32[]{:S(2)}, u32[]{:S(2)}) %collective-permute-start.15) | collective-permute-done | bytes 655392 | tf_op jit(solution)/shard_map/ppermute | solution.py:396
  37.8 0.6 collective-permute-start.20
  38.4 0.5 collective-permute-start.17
  38.9 0.0 collective-permute-start.19
  38.9 0.9 %collective-permute-done.16.w3 = bf16[192,512]{1,0:T(8,128)(2,1)S(1)} collective-permute-done((bf16[192,512]{1,0:T(8,128)(2,1)S(1)}, bf16[192,512]{1,0:T(8,128)(2,1)S(1)}, u32[]{:S(2)}, u32[]{:S(2)}) %collective-permute-start.16) | collective-permute-done | bytes 196640 | tf_op jit(solution)/shard_map/ppermute | solution.py:400
  39.8 0.3 collective-permute-done.17.w4
  40.1 2.4 %collective-permute-done.13.theirs = bf16[256,512]{1,0:T(8,128)(2,1)S(1)} collective-permute-done((bf16[256,512]{1,0:T(8,128)(2,1)S(1)}, bf16[256,512]{1,0:T(8,128)(2,1)S(1)}, u32[]{:S(2)}, u32[]{:S(2)}) %collective-permute-start.13) | collective-permute-done | bytes 262176 | tf_op jit(solution)/shard_map/ppermute | solution.py:396
  42.5 0.0 copy-start.16
  42.5 1.2 %shard_map.234 = (bf16[256,512]{1,0:T(8,128)(2,1)S(1)}, bf16[384,512]{1,0:T(8,128)(2,1)S(1)}, bf16[32,512]{1,0:T(8,128)(2,1)S(1)}, bf16[32,512]{1,0:T(8,128)(2,1)S(1)}, bf16[32,512]{1,0:T(8,128)(2,1)S(1)}) custom-call(bf16[256,512]{1,0:T(8,128)(2,1)S(1)} %get-tuple-element.40.mesh, bf16[256,512]{1,0:T(8,128)(2,1)S(1)} %shard_map.232.after.mine, ...), custom_call_target="tpu_custom_call" | custom-call | flops 402653184 | bytes 4819456 | tf_op jit(solution)/shard_map/pallas_call | solution.py:62
  43.8 0.1 collective-permute-start.18
  43.9 0.6 collective-permute-done.20.round_
  44.5 2.0 %collective-permute-start.23 = (bf16[32,512]{1,0:T(8,128)(2,1)S(1)}, bf16[32,512]{1,0:T(8,128)(2,1)S(1)}, u32[]{:S(2)}, u32[]{:S(2)}) collective-permute-start(bf16[32,512]{1,0:T(8,128)(2,1)S(1)} %get-tuple-element.54), channel_id=1, source_target_pairs={{0,8},{4,12},{8,0},{12,4},{1,9},{5,13},{9,1},{13,5},{2,10},{6,14},... | collective-permute-start | bytes 98312 | tf_op jit(solution)/shard_map/ppermute | solution.py:529
  46.5 2.1 %collective-permute-done.22.refs_0_ = bf16[32,512]{1,0:T(8,128)(2,1)S(1)} collective-permute-done((bf16[32,512]{1,0:T(8,128)(2,1)S(1)}, bf16[32,512]{1,0:T(8,128)(2,1)S(1)}, u32[]{:S(2)}, u32[]{:S(2)}) %collective-permute-start.22) | collective-permute-done | bytes 32800 | tf_op jit(solution)/shard_map/ppermute | solution.py:529
  48.6 2.4 %collective-permute-start.24 = (bf16[32,512]{1,0:T(8,128)(2,1)S(1)}, bf16[32,512]{1,0:T(8,128)(2,1)S(1)}, u32[]{:S(2)}, u32[]{:S(2)}) collective-permute-start(bf16[32,512]{1,0:T(8,128)(2,1)S(1)} %get-tuple-element.55), channel_id=1, source_target_pairs={{4,8},{8,4},{5,9},{9,5},{6,10},{10,6},{7,11},{11,7},{20,24},{24,20... | collective-permute-start | bytes 98312 | tf_op jit(solution)/shard_map/ppermute | solution.py:529
  51.7 0.6 collective-permute-start.29
  52.3 2.1 %collective-permute-done.24.refs_2_ = bf16[32,512]{1,0:T(8,128)(2,1)S(1)} collective-permute-done((bf16[32,512]{1,0:T(8,128)(2,1)S(1)}, bf16[32,512]{1,0:T(8,128)(2,1)S(1)}, u32[]{:S(2)}, u32[]{:S(2)}) %collective-permute-start.24) | collective-permute-done | bytes 32800 | tf_op jit(solution)/shard_map/ppermute | solution.py:529
  54.4 0.1 collective-permute-start.25
  54.5 0.0 copy-start.21
  54.6 2.6 %shard_map.235 = (bf16[1536,512]{1,0:T(8,128)(2,1)S(1)}, f32[1024,512]{1,0:T(8,128)S(1)}, bf16[512,512]{1,0:T(8,128)(2,1)S(1)}, bf16[512,512]{1,0:T(8,128)(2,1)S(1)}) custom-call(bf16[2048,512]{1,0:T(8,128)(2,1)S(1)} %get-tuple-element.47.emb, bf16[256,512]{1,0:T(8,128)(2,1)S(1)} %get-tuple-element.46.mine.middle, ...), custom_call_target="tpu_custom_call" | custom-call | flops 1610612736 | bytes 10240000 | tf_op jit(solution)/shard_map/pallas_call | solution.py:62
  57.2 0.0 copy-start.9
  57.2 5.8 %shard_map.237 = (bf16[256,512]{1,0:T(8,128)(2,1)S(1)}, bf16[256,512]{1,0:T(8,128)(2,1)S(1)}) custom-call(bf16[2048,512]{1,0:T(8,128)(2,1)S(1)} %get-tuple-element.47.emb, s32[2,2048]{1,0:T(2,128)S(1)} %copy-done.16, f32[1,512]{1,0:T(1,128)S(1)} %bitcast.7, bf16[1536,512]{1,0:T(8,128)(2,1)S(1)} %get-tuple-element.49.table, ...), custom_call_target="tpu_custom_call" | custom-call | flops 3489660928 | bytes 7555076 | tf_op jit(solution)/shard_map/pallas_call | solution.py:62
  63.0 0.5 collective-permute-start.26
  63.6 0.1 collective-permute-start.28
  63.7 0.4 collective-permute-start.30
  64.1 0.6 collective-permute-done.26.theirs
  64.7 0.1 shard_map.238
  64.8 0.8 %collective-permute-start.27 = (bf16[128,512]{1,0:T(8,128)(2,1)S(1)}, bf16[128,512]{1,0:T(8,128)(2,1)S(1)}, u32[]{:S(2)}, u32[]{:S(2)}) collective-permute-start(bf16[128,512]{1,0:T(8,128)(2,1)S(1)} %get-tuple-element.59), channel_id=1, source_target_pairs={{0,2},{1,3},{2,0},{3,1},{4,6},{5,7},{6,4},{7,5},{8,10},{9,11},{10,... | collective-permute-start | bytes 393224 | tf_op jit(solution)/shard_map/ppermute | solution.py:396
  65.6 5.0 %collective-permute-done.27.theirs = bf16[128,512]{1,0:T(8,128)(2,1)S(1)} collective-permute-done((bf16[128,512]{1,0:T(8,128)(2,1)S(1)}, bf16[128,512]{1,0:T(8,128)(2,1)S(1)}, u32[]{:S(2)}, u32[]{:S(2)}) %collective-permute-start.27) | collective-permute-done | bytes 131104 | tf_op jit(solution)/shard_map/ppermute | solution.py:396
  70.7 1.5 %shard_map.239 = bf16[128,512]{1,0:T(8,128)(2,1)} custom-call(bf16[256,512]{1,0:T(8,128)(2,1)S(1)} %get-tuple-element.46.mine.middle, bf16[128,512]{1,0:T(8,128)(2,1)S(1)} %get-tuple-element.58.mine, bf16[128,512]{1,0:T(8,128)(2,1)S(1)} %collective-permute-done.27.theirs, f32[1,512]{1,0:T(1,128)S(1)} %bitcast.5, bf16[384,512]{1,0:T(8,128)(2,1)S(1)} %get-tuple-element.60.w0, ...), custom_call_target="tpu_custom_call" | custom-call | flops 201326592 | bytes 2230272 | tf_op jit(solution)/shard_map/pallas_call | solution.py:62
  (56 shorter events, 0.2 us)
Async XLA Ops:
  0.0 0.9 %copy-start = (bf16[512,128]{1,0:T(8,128)(2,1)S(1)}, bf16[512,128]{1,0:T(8,128)(2,1)}, u32[]{:S(2)}) copy-start(bf16[512,128]{1,0:T(8,128)(2,1)} %refs_0_.1) | copy-start | bytes 393220
  0.0 0.9 %copy-start.6 = (s32[1,4,64]{2,1,0:T(4,128)S(1)}, s32[1,4,64]{2,1,0:T(4,128)}, u32[]{:S(2)}) copy-start(s32[1,4,64]{2,1,0:T(4,128)} %send.2) | copy-start | bytes 3076
  0.0 1.1 %copy-start.1 = (bf16[384,512]{1,0:T(8,128)(2,1)S(1)}, bf16[384,512]{1,0:T(8,128)(2,1)}, u32[]{:S(2)}) copy-start(bf16[384,512]{1,0:T(8,128)(2,1)} %o_in.1) | copy-start | bytes 1179652
  0.0 1.1 %copy-start.4 = (bf16[128,512]{1,0:T(8,128)(2,1)S(1)}, bf16[128,512]{1,0:T(8,128)(2,1)}, u32[]{:S(2)}) copy-start(bf16[128,512]{1,0:T(8,128)(2,1)} %o_out.1) | copy-start | bytes 393220
  0.0 11.6 %copy-start.3 = (bf16[512,128]{1,0:T(8,128)(2,1)S(1)}, bf16[512,128]{1,0:T(8,128)(2,1)}, u32[]{:S(2)}) copy-start(bf16[512,128]{1,0:T(8,128)(2,1)} %refs_1_.1) | copy-start | bytes 393220
  0.0 13.3 %copy-start.11 = (bf16[256,512]{1,0:T(8,128)(2,1)S(1)}, bf16[256,512]{1,0:T(8,128)(2,1)}, u32[]{:S(2)}) copy-start(bf16[256,512]{1,0:T(8,128)(2,1)} %e_in.1) | copy-start | bytes 786436
  0.0 13.3 %copy-start.12 = (bf16[128,512]{1,0:T(8,128)(2,1)S(1)}, bf16[128,512]{1,0:T(8,128)(2,1)}, u32[]{:S(2)}) copy-start(bf16[128,512]{1,0:T(8,128)(2,1)} %e_out.1) | copy-start | bytes 393220
  0.0 13.2 %copy-start.10 = (bf16[384,512]{1,0:T(8,128)(2,1)S(1)}, bf16[384,512]{1,0:T(8,128)(2,1)}, u32[]{:S(2)}) copy-start(bf16[384,512]{1,0:T(8,128)(2,1)} %p_in.1) | copy-start | bytes 1179652
  0.1 13.2 %copy-start.13 = (bf16[128,512]{1,0:T(8,128)(2,1)S(1)}, bf16[128,512]{1,0:T(8,128)(2,1)}, u32[]{:S(2)}) copy-start(bf16[128,512]{1,0:T(8,128)(2,1)} %p_out.1) | copy-start | bytes 393220
  0.1 13.2 %copy-start.15 = (f32[4,1024]{1,0:T(4,128)S(1)}, f32[4,1024]{1,0:T(4,128)}, u32[]{:S(2)}) copy-start(f32[4,1024]{1,0:T(4,128)} %egeom.1) | copy-start | bytes 49156
  0.1 13.2 %copy-start.17 = (f32[4,512]{1,0:T(4,128)S(1)}, f32[4,512]{1,0:T(4,128)}, u32[]{:S(2)}) copy-start(f32[4,512]{1,0:T(4,128)} %egeo.1) | copy-start | bytes 24580
  0.1 13.2 %copy-start.14 = (f32[4,2048]{1,0:T(4,128)S(1)}, f32[4,2048]{1,0:T(4,128)}, u32[]{:S(2)}) copy-start(f32[4,2048]{1,0:T(4,128)} %pgeom.1) | copy-start | bytes 98308
  0.1 13.2 %copy-start.18 = (f32[4,512]{1,0:T(4,128)S(1)}, f32[4,512]{1,0:T(4,128)}, u32[]{:S(2)}) copy-start(f32[4,512]{1,0:T(4,128)} %pgeo.1) | copy-start | bytes 24580
  1.1 20.4 %copy-start.19 = (s32[2,1024]{1,0:T(2,128)S(1)}, s32[2,1024]{1,0:T(2,128)}, u32[]{:S(2)}) copy-start(s32[2,1024]{1,0:T(2,128)} %edges.3) | copy-start | bytes 24580
  1.1 20.4 %copy-start.20 = (f32[512]{0:T(512)S(1)}, f32[512]{0:T(512)}, u32[]{:S(2)}) copy-start(f32[512]{0:T(512)} %param.44) | copy-start | bytes 6148
  1.4 10.8 %collective-permute-start.8 = (bf16[256,512]{1,0:T(8,128)(2,1)S(1)}, bf16[256,512]{1,0:T(8,128)(2,1)S(1)}, u32[]{:S(2)}, u32[]{:S(2)}) collective-permute-start(bf16[256,512]{1,0:T(8,128)(2,1)S(1)} %get-tuple-element.39), channel_id=1, source_target_pairs={{0,2},{1,3},{2,0},{3,1},{4,6},{5,7},{6,4},{7,5},{8,10},{9,11},{10,... | collective-permute-start | bytes 786440 | tf_op jit(solution)/shard_map/ppermute | solution.py:396
  3.0 5.4 %collective-permute-start = (bf16[64,128]{1,0:T(8,128)(2,1)S(1)}, bf16[64,128]{1,0:T(8,128)(2,1)S(1)}, u32[]{:S(2)}, u32[]{:S(2)}) collective-permute-start(bf16[64,128]{1,0:T(8,128)(2,1)S(1)} %get-tuple-element.33), channel_id=1, source_target_pairs={{0,4},{4,0},{8,12},{12,8},{1,5},{5,1},{9,13},{13,9},{2,6},{6,2},{1... | collective-permute-start | bytes 49160 | tf_op jit(solution)/shard_map/ppermute | solution.py:461
  3.4 5.0 %collective-permute-start.1 = (bf16[64,128]{1,0:T(8,128)(2,1)S(1)}, bf16[64,128]{1,0:T(8,128)(2,1)S(1)}, u32[]{:S(2)}, u32[]{:S(2)}) collective-permute-start(bf16[64,128]{1,0:T(8,128)(2,1)S(1)} %get-tuple-element.34), channel_id=1, source_target_pairs={{0,8},{4,12},{8,0},{12,4},{1,9},{5,13},{9,1},{13,5},{2,10},{6,14},... | collective-permute-start | bytes 49160 | tf_op jit(solution)/shard_map/ppermute | solution.py:461
  6.0 5.6 %collective-permute-start.2 = (bf16[64,128]{1,0:T(8,128)(2,1)S(1)}, bf16[64,128]{1,0:T(8,128)(2,1)S(1)}, u32[]{:S(2)}, u32[]{:S(2)}) collective-permute-start(bf16[64,128]{1,0:T(8,128)(2,1)S(1)} %get-tuple-element.35), channel_id=1, source_target_pairs={{4,8},{8,4},{5,9},{9,5},{6,10},{10,6},{7,11},{11,7},{20,24},{24,20... | collective-permute-start | bytes 49160 | tf_op jit(solution)/shard_map/ppermute | solution.py:461
  11.7 7.3 %collective-permute-start.3 = (bf16[1216,128]{1,0:T(8,128)(2,1)S(1)}, bf16[1216,128]{1,0:T(8,128)(2,1)S(1)}, u32[]{:S(2)}, u32[]{:S(2)}) collective-permute-start(bf16[1216,128]{1,0:T(8,128)(2,1)S(1)} %shard_map.228.after.l0), channel_id=1, source_target_pairs={{0,2},{1,3},{2,0},{3,1},{4,6},{5,7},{6,4},{7,5},{8,10},{9,11},{10,... | collective-permute-start | bytes 933896 | tf_op jit(solution)/shard_map/ppermute | solution.py:396
  12.3 7.4 %collective-permute-start.9 = (bf16[256,512]{1,0:T(8,128)(2,1)S(1)}, bf16[256,512]{1,0:T(8,128)(2,1)S(1)}, u32[]{:S(2)}, u32[]{:S(2)}) collective-permute-start(bf16[256,512]{1,0:T(8,128)(2,1)S(1)} %collective-permute-done.8.across), channel_id=1, source_target_pairs={{0,16},{16,0},{1,17},{17,1},{2,18},{18,2},{3,19},{19,3},{4,20},{20... | collective-permute-start | bytes 786440 | tf_op jit(solution)/shard_map/ppermute | solution.py:405
  12.8 7.4 %collective-permute-start.6 = (bf16[384,512]{1,0:T(8,128)(2,1)S(1)}, bf16[384,512]{1,0:T(8,128)(2,1)S(1)}, u32[]{:S(2)}, u32[]{:S(2)}) collective-permute-start(bf16[384,512]{1,0:T(8,128)(2,1)S(1)} %copy-done.1), channel_id=1, source_target_pairs={{0,1},{1,0},{2,3},{3,2},{4,5},{5,4},{6,7},{7,6},{8,9},{9,8},{10,11... | collective-permute-start | bytes 1179656 | tf_op jit(solution)/shard_map/ppermute | solution.py:400
  12.8 7.0 %collective-permute-start.4 = (bf16[1216,128]{1,0:T(8,128)(2,1)S(1)}, bf16[1216,128]{1,0:T(8,128)(2,1)S(1)}, u32[]{:S(2)}, u32[]{:S(2)}) collective-permute-start(bf16[1216,128]{1,0:T(8,128)(2,1)S(1)} %shard_map.228.after.l0), channel_id=1, source_target_pairs={{0,1},{1,0},{2,3},{3,2},{4,5},{5,4},{6,7},{7,6},{8,9},{9,8},{10,11... | collective-permute-start | bytes 933896 | tf_op jit(solution)/shard_map/ppermute | solution.py:400
  13.3 5.9 %collective-permute-start.7 = (bf16[128,512]{1,0:T(8,128)(2,1)S(1)}, bf16[128,512]{1,0:T(8,128)(2,1)S(1)}, u32[]{:S(2)}, u32[]{:S(2)}) collective-permute-start(bf16[128,512]{1,0:T(8,128)(2,1)S(1)} %copy-done.4), channel_id=1, source_target_pairs={{0,1},{1,0},{2,3},{3,2},{4,5},{5,4},{6,7},{7,6},{8,9},{9,8},{10,11... | collective-permute-start | bytes 393224 | tf_op jit(solution)/shard_map/ppermute | solution.py:400
  19.1 2.4 %collective-permute-start.5 = (bf16[1216,128]{1,0:T(8,128)(2,1)S(1)}, bf16[1216,128]{1,0:T(8,128)(2,1)S(1)}, u32[]{:S(2)}, u32[]{:S(2)}) collective-permute-start(bf16[1216,128]{1,0:T(8,128)(2,1)S(1)} %get-tuple-element.38), channel_id=1, source_target_pairs={{0,1},{1,0},{2,3},{3,2},{4,5},{5,4},{6,7},{7,6},{8,9},{9,8},{10,11... | collective-permute-start | bytes 933896 | tf_op jit(solution)/shard_map/ppermute | solution.py:400
  19.2 2.3 %collective-permute-start.10 = (bf16[256,512]{1,0:T(8,128)(2,1)S(1)}, bf16[256,512]{1,0:T(8,128)(2,1)S(1)}, u32[]{:S(2)}, u32[]{:S(2)}) collective-permute-start(bf16[256,512]{1,0:T(8,128)(2,1)S(1)} %collective-permute-done.8.across), channel_id=1, source_target_pairs={{0,1},{1,0},{2,3},{3,2},{4,5},{5,4},{6,7},{7,6},{8,9},{9,8},{10,11... | collective-permute-start | bytes 786440 | tf_op jit(solution)/shard_map/ppermute | solution.py:400
  19.7 1.9 %collective-permute-start.11 = (bf16[256,512]{1,0:T(8,128)(2,1)S(1)}, bf16[256,512]{1,0:T(8,128)(2,1)S(1)}, u32[]{:S(2)}, u32[]{:S(2)}) collective-permute-start(bf16[256,512]{1,0:T(8,128)(2,1)S(1)} %collective-permute-done.9.round_), channel_id=1, source_target_pairs={{0,1},{1,0},{2,3},{3,2},{4,5},{5,4},{6,7},{7,6},{8,9},{9,8},{10,11... | collective-permute-start | bytes 786440 | tf_op jit(solution)/shard_map/ppermute | solution.py:400
  19.7 19.2 %collective-permute-start.14 = (bf16[896,512]{1,0:T(8,128)(2,1)S(1)}, bf16[896,512]{1,0:T(8,128)(2,1)S(1)}, u32[]{:S(2)}, u32[]{:S(2)}) collective-permute-start(bf16[896,512]{1,0:T(8,128)(2,1)S(1)} %get-tuple-element.37.weights.w0), channel_id=1, source_target_pairs={{0,1},{1,0},{2,3},{3,2},{4,5},{5,4},{6,7},{7,6},{8,9},{9,8},{10,11... | collective-permute-start | bytes 2752520 | tf_op jit(solution)/shard_map/ppermute | solution.py:400
  20.2 17.6 %collective-permute-start.15 = (bf16[640,512]{1,0:T(8,128)(2,1)S(1)}, bf16[640,512]{1,0:T(8,128)(2,1)S(1)}, u32[]{:S(2)}, u32[]{:S(2)}) collective-permute-start(bf16[640,512]{1,0:T(8,128)(2,1)S(1)} %get-tuple-element.43), channel_id=1, source_target_pairs={{0,2},{1,3},{2,0},{3,1},{4,6},{5,7},{6,4},{7,5},{8,10},{9,11},{10,... | collective-permute-start | bytes 1966088 | tf_op jit(solution)/shard_map/ppermute | solution.py:396
  21.5 21.0 %copy-start.2 = (bf16[256,512]{1,0:T(8,128)(2,1)S(1)}, bf16[256,512]{1,0:T(8,128)(2,1)}, u32[]{:S(2)}) copy-start(bf16[256,512]{1,0:T(8,128)(2,1)} %n_in.1) | copy-start | bytes 786436
  21.6 21.0 %copy-start.5 = (bf16[128,512]{1,0:T(8,128)(2,1)S(1)}, bf16[128,512]{1,0:T(8,128)(2,1)}, u32[]{:S(2)}) copy-start(bf16[128,512]{1,0:T(8,128)(2,1)} %n_out.1) | copy-start | bytes 393220
  21.6 21.0 %copy-start.7 = (f32[512]{0:T(512)S(1)}, f32[512]{0:T(512)}, u32[]{:S(2)}) copy-start(f32[512]{0:T(512)} %param.45) | copy-start | bytes 6148
  21.6 20.9 %copy-start.8 = (s32[1,4,32]{2,1,0:T(4,128)S(1)}, s32[1,4,32]{2,1,0:T(4,128)}, u32[]{:S(2)}) copy-start(s32[1,4,32]{2,1,0:T(4,128)} %send.3) | copy-start | bytes 1540
  26.4 1.6 %collective-permute-start.12 = (bf16[256,512]{1,0:T(8,128)(2,1)S(1)}, bf16[256,512]{1,0:T(8,128)(2,1)S(1)}, u32[]{:S(2)}, u32[]{:S(2)}) collective-permute-start(bf16[256,512]{1,0:T(8,128)(2,1)S(1)} %get-tuple-element.42), channel_id=1, source_target_pairs={{0,1},{1,0},{2,3},{3,2},{4,5},{5,4},{6,7},{7,6},{8,9},{9,8},{10,11... | collective-permute-start | bytes 786440 | tf_op jit(solution)/shard_map/ppermute | solution.py:400
  28.0 14.5 %collective-permute-start.13 = (bf16[256,512]{1,0:T(8,128)(2,1)S(1)}, bf16[256,512]{1,0:T(8,128)(2,1)S(1)}, u32[]{:S(2)}, u32[]{:S(2)}) collective-permute-start(bf16[256,512]{1,0:T(8,128)(2,1)S(1)} %shard_map.232.after.mine), channel_id=1, source_target_pairs={{0,2},{1,3},{2,0},{3,1},{4,6},{5,7},{6,4},{7,5},{8,10},{9,11},{10,... | collective-permute-start | bytes 786440 | tf_op jit(solution)/shard_map/ppermute | solution.py:396
  37.8 6.7 %collective-permute-start.20 = (bf16[256,512]{1,0:T(8,128)(2,1)S(1)}, bf16[256,512]{1,0:T(8,128)(2,1)S(1)}, u32[]{:S(2)}, u32[]{:S(2)}) collective-permute-start(bf16[256,512]{1,0:T(8,128)(2,1)S(1)} %get-tuple-element.48.across), channel_id=1, source_target_pairs={{0,16},{16,0},{1,17},{17,1},{2,18},{18,2},{3,19},{19,3},{4,20},{20... | collective-permute-start | bytes 786440 | tf_op jit(solution)/shard_map/ppermute | solution.py:405
  38.4 1.4 %collective-permute-start.16 = (bf16[192,512]{1,0:T(8,128)(2,1)S(1)}, bf16[192,512]{1,0:T(8,128)(2,1)S(1)}, u32[]{:S(2)}, u32[]{:S(2)}) collective-permute-start(bf16[192,512]{1,0:T(8,128)(2,1)S(1)} %get-tuple-element.44), channel_id=1, source_target_pairs={{0,1},{1,0},{2,3},{3,2},{4,5},{5,4},{6,7},{7,6},{8,9},{9,8},{10,11... | collective-permute-start | bytes 589832 | tf_op jit(solution)/shard_map/ppermute | solution.py:400
  38.4 1.7 %collective-permute-start.17 = (bf16[192,512]{1,0:T(8,128)(2,1)S(1)}, bf16[192,512]{1,0:T(8,128)(2,1)S(1)}, u32[]{:S(2)}, u32[]{:S(2)}) collective-permute-start(bf16[192,512]{1,0:T(8,128)(2,1)S(1)} %get-tuple-element.45), channel_id=1, source_target_pairs={{0,1},{1,0},{2,3},{3,2},{4,5},{5,4},{6,7},{7,6},{8,9},{9,8},{10,11... | collective-permute-start | bytes 589832 | tf_op jit(solution)/shard_map/ppermute | solution.py:400
  38.9 15.6 %collective-permute-start.19 = (bf16[256,512]{1,0:T(8,128)(2,1)S(1)}, bf16[256,512]{1,0:T(8,128)(2,1)S(1)}, u32[]{:S(2)}, u32[]{:S(2)}) collective-permute-start(bf16[256,512]{1,0:T(8,128)(2,1)S(1)} %get-tuple-element.48.across), channel_id=1, source_target_pairs={{0,1},{1,0},{2,3},{3,2},{4,5},{5,4},{6,7},{7,6},{8,9},{9,8},{10,11... | collective-permute-start | bytes 786440 | tf_op jit(solution)/shard_map/ppermute | solution.py:400
  42.5 12.0 %copy-start.16 = (s32[2,2048]{1,0:T(2,128)S(1)}, s32[2,2048]{1,0:T(2,128)}, u32[]{:S(2)}) copy-start(s32[2,2048]{1,0:T(2,128)} %edges.5) | copy-start | bytes 49156
  43.8 10.7 %collective-permute-start.18 = (bf16[256,512]{1,0:T(8,128)(2,1)S(1)}, bf16[256,512]{1,0:T(8,128)(2,1)S(1)}, u32[]{:S(2)}, u32[]{:S(2)}) collective-permute-start(bf16[256,512]{1,0:T(8,128)(2,1)S(1)} %get-tuple-element.46.mine.middle), channel_id=1, source_target_pairs={{0,1},{1,0},{2,3},{3,2},{4,5},{5,4},{6,7},{7,6},{8,9},{9,8},{10,11... | collective-permute-start | bytes 786440 | tf_op jit(solution)/shard_map/ppermute | solution.py:400
  44.5 10.1 %collective-permute-start.21 = (bf16[256,512]{1,0:T(8,128)(2,1)S(1)}, bf16[256,512]{1,0:T(8,128)(2,1)S(1)}, u32[]{:S(2)}, u32[]{:S(2)}) collective-permute-start(bf16[256,512]{1,0:T(8,128)(2,1)S(1)} %collective-permute-done.20.round_), channel_id=1, source_target_pairs={{0,1},{1,0},{2,3},{3,2},{4,5},{5,4},{6,7},{7,6},{8,9},{9,8},{10,11... | collective-permute-start | bytes 786440 | tf_op jit(solution)/shard_map/ppermute | solution.py:400
  44.5 4.2 %collective-permute-start.22 = (bf16[32,512]{1,0:T(8,128)(2,1)S(1)}, bf16[32,512]{1,0:T(8,128)(2,1)S(1)}, u32[]{:S(2)}, u32[]{:S(2)}) collective-permute-start(bf16[32,512]{1,0:T(8,128)(2,1)S(1)} %get-tuple-element.53), channel_id=1, source_target_pairs={{0,4},{4,0},{8,12},{12,8},{1,5},{5,1},{9,13},{13,9},{2,6},{6,2},{1... | collective-permute-start | bytes 98312 | tf_op jit(solution)/shard_map/ppermute | solution.py:529
  44.5 7.2 %collective-permute-start.23 = (bf16[32,512]{1,0:T(8,128)(2,1)S(1)}, bf16[32,512]{1,0:T(8,128)(2,1)S(1)}, u32[]{:S(2)}, u32[]{:S(2)}) collective-permute-start(bf16[32,512]{1,0:T(8,128)(2,1)S(1)} %get-tuple-element.54), channel_id=1, source_target_pairs={{0,8},{4,12},{8,0},{12,4},{1,9},{5,13},{9,1},{13,5},{2,10},{6,14},... | collective-permute-start | bytes 98312 | tf_op jit(solution)/shard_map/ppermute | solution.py:529
  48.6 5.8 %collective-permute-start.24 = (bf16[32,512]{1,0:T(8,128)(2,1)S(1)}, bf16[32,512]{1,0:T(8,128)(2,1)S(1)}, u32[]{:S(2)}, u32[]{:S(2)}) collective-permute-start(bf16[32,512]{1,0:T(8,128)(2,1)S(1)} %get-tuple-element.55), channel_id=1, source_target_pairs={{4,8},{8,4},{5,9},{9,5},{6,10},{10,6},{7,11},{11,7},{20,24},{24,20... | collective-permute-start | bytes 98312 | tf_op jit(solution)/shard_map/ppermute | solution.py:529
  51.7 12.0 %collective-permute-start.29 = (bf16[384,512]{1,0:T(8,128)(2,1)S(1)}, bf16[384,512]{1,0:T(8,128)(2,1)S(1)}, u32[]{:S(2)}, u32[]{:S(2)}) collective-permute-start(bf16[384,512]{1,0:T(8,128)(2,1)S(1)} %get-tuple-element.60.w0), channel_id=1, source_target_pairs={{0,2},{1,3},{2,0},{3,1},{4,6},{5,7},{6,4},{7,5},{8,10},{9,11},{10,... | collective-permute-start | bytes 1179656 | tf_op jit(solution)/shard_map/ppermute | solution.py:396
  54.4 2.7 %collective-permute-start.25 = (bf16[96,512]{1,0:T(8,128)(2,1)S(1)}, bf16[96,512]{1,0:T(8,128)(2,1)S(1)}, u32[]{:S(2)}, u32[]{:S(2)}) collective-permute-start(bf16[96,512]{1,0:T(8,128)(2,1)S(1)} %shard_map.236.halo), channel_id=1, source_target_pairs={{0,1},{1,0},{2,3},{3,2},{4,5},{5,4},{6,7},{7,6},{8,9},{9,8},{10,11... | collective-permute-start | bytes 294920 | tf_op jit(solution)/shard_map/ppermute | solution.py:400
  54.5 2.6 %copy-start.21 = (f32[512]{0:T(512)S(1)}, f32[512]{0:T(512)}, u32[]{:S(2)}) copy-start(f32[512]{0:T(512)} %param.46) | copy-start | bytes 6148
  57.2 13.5 %copy-start.9 = (f32[512]{0:T(512)S(1)}, f32[512]{0:T(512)}, u32[]{:S(2)}) copy-start(f32[512]{0:T(512)} %param.47) | copy-start | bytes 6148
  63.0 1.7 %collective-permute-start.26 = (bf16[256,512]{1,0:T(8,128)(2,1)S(1)}, bf16[256,512]{1,0:T(8,128)(2,1)S(1)}, u32[]{:S(2)}, u32[]{:S(2)}) collective-permute-start(bf16[256,512]{1,0:T(8,128)(2,1)S(1)} %get-tuple-element.57), channel_id=1, source_target_pairs={{0,1},{1,0},{2,3},{3,2},{4,5},{5,4},{6,7},{7,6},{8,9},{9,8},{10,11... | collective-permute-start | bytes 786440 | tf_op jit(solution)/shard_map/ppermute | solution.py:400
  63.6 2.0 %collective-permute-start.28 = (bf16[384,512]{1,0:T(8,128)(2,1)S(1)}, bf16[384,512]{1,0:T(8,128)(2,1)S(1)}, u32[]{:S(2)}, u32[]{:S(2)}) collective-permute-start(bf16[384,512]{1,0:T(8,128)(2,1)S(1)} %get-tuple-element.60.w0), channel_id=1, source_target_pairs={{0,1},{1,0},{2,3},{3,2},{4,5},{5,4},{6,7},{7,6},{8,9},{9,8},{10,11... | collective-permute-start | bytes 1179656 | tf_op jit(solution)/shard_map/ppermute | solution.py:400
  63.7 7.0 %collective-permute-start.30 = (bf16[384,512]{1,0:T(8,128)(2,1)S(1)}, bf16[384,512]{1,0:T(8,128)(2,1)S(1)}, u32[]{:S(2)}, u32[]{:S(2)}) collective-permute-start(bf16[384,512]{1,0:T(8,128)(2,1)S(1)} %collective-permute-done.29.w2), channel_id=1, source_target_pairs={{0,1},{1,0},{2,3},{3,2},{4,5},{5,4},{6,7},{7,6},{8,9},{9,8},{10,11... | collective-permute-start | bytes 1179656 | tf_op jit(solution)/shard_map/ppermute | solution.py:400
  64.8 5.8 %collective-permute-start.27 = (bf16[128,512]{1,0:T(8,128)(2,1)S(1)}, bf16[128,512]{1,0:T(8,128)(2,1)S(1)}, u32[]{:S(2)}, u32[]{:S(2)}) collective-permute-start(bf16[128,512]{1,0:T(8,128)(2,1)S(1)} %get-tuple-element.59), channel_id=1, source_target_pairs={{0,2},{1,3},{2,0},{3,1},{4,6},{5,7},{6,4},{7,5},{8,10},{9,11},{10,... | collective-permute-start | bytes 393224 | tf_op jit(solution)/shard_map/ppermute | solution.py:396

commit v6 on v5

--- a/solution.py
+++ b/solution.py
@@ -12,6 +12,7 @@
 STEP = 512
 GATHERED = 1024
 LONG = 30 * 10**9
+BY_PART = ("dom",)
 VMEM_BYTES = 24 * 1024 * 1024
 I16 = jnp.int16
 BF16 = jnp.bfloat16
@@ -146,15 +147,18 @@
             out[begin : begin + STEP, :] = embed_rows(geom[:, begin : begin + STEP], geo[...])
 
 
-def cross_kernel(rows_whole, k_in, weights, lat, crossing, lat_out):
+def cross_kernel(parts, weights, lat, crossing, lat_out):
     lat_out[...] = lat[...]
-    crossing[:rows_whole, :] = weights[:rows_whole, :]
-    first, place = rows_whole, rows_whole
-    for rows in (k_in, weights.shape[0] - rows_whole - k_in):
+    first, place = 0, 0
+    for rows, axes in parts:
         half = rows // 2
-        begin = pl.multiple_of(first + lax.axis_index("groups") * half, 64)
+        begin = pl.multiple_of(first + parity(axes) * half, 64)
         crossing[place : place + half, :] = weights[pl.ds(begin, half), :]
         first, place = first + rows, place + half
+
+
+def pair_kernel(first, second, after, out):
+    stack_into(out, (first, second))
 
 
 def split_kernel(source, after, *outs):
@@ -174,13 +178,17 @@
     target[pl.ds(pl.multiple_of(place, rows), rows), :] = source[first : first + rows, :]
 
 
-def put_half(target, k, source, first=0, step=0, other=0):
+def parity(axes):
+    return lax.rem(sum(lax.axis_index(axis) for axis in axes), 2)
+
+
+def put_half(target, k, source, step, other, axes=("groups",)):
     rows = target.shape[0] // 4
-    which = lax.bitwise_xor(lax.axis_index("groups"), other)
+    which = lax.bitwise_xor(parity(axes), other)
     begin = lax.bitwise_xor(lax.axis_index("sub"), step) * rows
     for base, count in ((0, k // 2), (k // 2, (rows - k) // 2)):
         place = pl.multiple_of(begin + 2 * base + which * count, 64)
-        target[pl.ds(place, count), :] = source[first + base : first + base + count, :]
+        target[pl.ds(place, count), :] = source[base : base + count, :]
 
 
 def joined(stack, first, rows):
@@ -251,10 +259,10 @@
         place = lax.bitwise_xor(quarter, bit) * step
         stack[pl.ds(pl.multiple_of(place, 128), k_in), :] = first[...]
         stack[pl.ds(pl.multiple_of(place + k_in, 128), d // 4), :] = second[...]
-    put_half(stack, k_in, across, 0, 2, 0)
-    put_half(stack, k_in, round_, 0, 2, 1)
-    put_half(stack, k_in, both, 0, 3, 0)
-    put_half(stack, k_in, round_both, 0, 3, 1)
+    put_half(stack, k_in, across, 2, 0)
+    put_half(stack, k_in, round_, 2, 1)
+    put_half(stack, k_in, both, 3, 0)
+    put_half(stack, k_in, round_both, 3, 1)
     rows = mesh_rows // 4
     core = lax.rem(quarter, 2)
     for half in range(2):
@@ -299,13 +307,15 @@
 
 
 def node_kernel(
-    plan, k_in, k_out, mesh, mine, theirs, gain, n_in, n_out, w0, w1, w2, w3, w4, send, out, packed, *rest
+    plan, k_in, k_out, mesh, mine, theirs, gain, n_in, n_out, w0, w1, w2, w3, w4, w5, send, out, packed, *rest
 ):
     outs, stack = rest[:-1], rest[-1]
-    for shard, bit in zip((w0, w1, w2), (0, 1, 2)):
-        put_shard(stack, shard, 0, bit)
-    put_shard(stack, w3, 0, 3, 0, 2)
-    put_shard(stack, w4, 0, 3, 1, 2)
+    put_shard(stack, w0, 0, 0)
+    put_shard(stack, w1, 0, 1)
+    put_half(stack, k_in, w2, 2, 0, BY_PART)
+    put_half(stack, k_in, w3, 2, 1, BY_PART)
+    put_half(stack, k_in, w4, 3, 0, BY_PART)
+    put_half(stack, k_in, w5, 3, 1, BY_PART)
     w_in, w_out = joined(stack, 0, k_in), joined(stack, k_in, k_out)
     fresh = node_update(mesh[...], add(mine[...], theirs[...]), w_in, w_out, gain[...])
     out[...] = fresh
@@ -318,7 +328,7 @@
 
 
 def proc_first_kernel(
-    k_in, first_row, emb, mine, theirs, edges, w0, w1, across, both, round_, round_both,
+    k_in, first_row, emb, mine, theirs, edges, w0, w1, pair, pair_beside,
     table, pre, w_source, w_out, stack, full,
 ):
     d = full.shape[1]
@@ -331,10 +341,10 @@
             full[pl.ds(place, rows), :] = part[half * rows : (half + 1) * rows, :]
     put_shard(stack, w0, first_row, 0)
     put_shard(stack, w1, first_row, 1)
-    put_half(stack, k_in, across, 0, 2, 0)
-    put_half(stack, k_in, both, 0, 3, 0)
-    put_half(stack, k_in, round_, 0, 2, 1)
-    put_half(stack, k_in, round_both, 0, 3, 1)
+    rows = pair.shape[0] // 2
+    for other in range(2):
+        put_half(stack, k_in, pair.at[pl.ds(other * rows, rows), :], 2, other)
+        put_half(stack, k_in, pair_beside.at[pl.ds(other * rows, rows), :], 3, other)
     w_in = joined(stack, 0, k_in)
     w_out[...] = joined(stack, k_in, d // 4)
     w_source[...] = w_in[d : 2 * d, :]
@@ -403,6 +413,10 @@
 def to_group(v):
     count = lax.axis_size("groups")
     return lax.ppermute(v, "groups", [(i, count - 1 - i) for i in range(count)])
+
+
+def to_partition(v):
+    return lax.ppermute(v, "dom", [(i, i ^ 1) for i in range(lax.axis_size("dom"))])
 
 
 def shape(rows, width, dtype=BF16):
@@ -479,8 +493,10 @@
         flops=2 * (n_enc + n_proc) * d * 128,
     )
     crossing, lat_sent = call(
-        functools.partial(cross_kernel, n_in + n_out, k_in),
-        [shape(n_in + n_out + (k_in + k_out) // 2, d), shape(lat.shape[0], width)],
+        functools.partial(
+            cross_kernel, ((n_in, BY_PART), (n_out, BY_PART), (k_in, ("groups",)), (k_out, ("groups",)))
+        ),
+        [shape((n_in + n_out + k_in + k_out) // 2, d), shape(lat.shape[0], width)],
         [next_w, lat_across],
     )
     lat_both = to_core(lat_sent)
@@ -508,24 +524,26 @@
         smem=1,
     )
     (chip_sum,) = call(add_kernel, [shape(half, d)], [keep, to_core(give)])
-    *node_across, proc_across = call(
+    node_across, proc_across = call(
         split_kernel,
-        [shape((n_in + n_out) // 2, d)] * 2 + [shape((k_in + k_out) // 2, d)],
+        [shape((n_in + n_out) // 2, d), shape((k_in + k_out) // 2, d)],
         [next_across, chip_sum],
     )
-    node_both = [to_core(v) for v in node_across]
+    node_round = to_partition(node_across)
     proc_round = to_group(proc_across)
+    node_both = to_core(node_across)
     slots = mesh_send.shape[2]
     mid_half, last_w, *outgoing = call(
         functools.partial(node_kernel, plan, n_in, n_out),
         [shape(half, d), shape(n_in + n_out, d)] + [shape(slots, d)] * len(plan),
         [
             own_mesh, chip_sum, to_chip(chip_sum), enc_node_gain, proc_node_in, proc_node_out,
-            next_w, next_beside, next_across, *node_both, mesh_send,
+            next_w, next_beside, node_across, node_round, node_both, to_core(node_round), mesh_send,
         ],
         scratch=[pltpu.VMEM((4 * (n_in + n_out), d), BF16)],
         flops=2 * half * d * 3 * d,
     )
+    (proc_pair,) = call(pair_kernel, [shape(k_in + k_out, d)], [proc_across, proc_round, mid_half])
     halos = [lax.ppermute(v, "dom", entry[0]) for v, entry in zip(outgoing, plan)]
     (halo,) = call(concat_kernel, [shape(len(plan) * slots, d)], halos)
     halo_beside = to_core(halo)
@@ -535,8 +553,7 @@
         functools.partial(proc_first_kernel, k_in, n_in + n_out),
         [shape(d + 2 * mesh_rows, d), shape(early, d, F32), shape(d, d), shape(d, d)],
         [
-            proc_emb, mid_half, to_core(mid_half), proc_edges, next_w, next_beside, proc_across, to_core(proc_across),
-            proc_round, to_core(proc_round),
+            proc_emb, mid_half, to_core(mid_half), proc_edges, next_w, next_beside, proc_pair, to_core(proc_pair),
         ],
         scratch=[pltpu.VMEM((4 * (k_in + k_out), d), BF16), pltpu.VMEM((mesh_rows, d), BF16)],
         flops=2 * early * d * (d + 2 * mesh_rows),

time: 72.3 us -> 69 us (0.954)
  waiting for transfers between devices: 31 us -> 26.4 us
  starting transfers between devices: 20 us -> 21 us
    ppermute x0 -> x1, waiting for transfers between devices: none -> 4.79 us  [to_partition(): lax.ppermute(v, 'dom', [(i, i ^ 1) for i in range(lax.axis_size('dom'))])]
    ppermute x6, waiting for transfers between devices: 19.6 us -> 15.3 us  [to_chip(): return lax.ppermute(v, 'sub', [(i, i ^ 2) for i in range(4)])]
    ppermute x6, waiting for transfers between devices: 7.47 us -> 4.13 us  [local(): lax.ppermute(v, 'dom', entry[0])]
    ppermute x17 -> x16, waiting for transfers between devices: 3.34 us -> 2.2 us  [to_core(): return lax.ppermute(v, 'sub', [(i, i ^ 1) for i in range(4)])]
    ppermute x6, starting transfers between devices: 9.85 us -> 10.9 us  [local(): lax.ppermute(v, 'dom', entry[0])]
    pallas_call x14 -> x15, Pallas kernels: 18.2 us -> 18.3 us  [call(): pl.pallas_call(body, out_shape=tuple(outs), in_specs=specs, out_specs=tup...]
    ppermute x17 -> x16, starting transfers between devices: 3.44 us -> 3.46 us  [to_core(): return lax.ppermute(v, 'sub', [(i, i ^ 1) for i in range(4)])]
  transfers between devices with their start and end apart: 31 -> 31, of which waited for: 12 -> 9; matrix products, arithmetic and copies ran while one was open for 0% -> 0% of each run, Pallas kernels for 23% -> 24%
where the time goes in v6:
time: 69 us; the launch traced here: 68.5 us
  waiting for transfers between devices  26.4 us (38%)
  starting transfers between devices  21 us (30%)
  Pallas kernels  18.3 us (27%)
  between operations  1.77 us (3%)
  local copies, waits for them, and re-layouts  1.08 us (2%)
    pallas_call x15, Pallas kernels, call(): pl.pallas_call(body, out_shape=tuple(outs), in_specs=specs, out_specs=tup...  18.3 us
    ppermute x6, waiting for transfers between devices, to_chip(): return lax.ppermute(v, 'sub', [(i, i ^ 2) for i in range(4)])  15.3 us
    ppermute x6, starting transfers between devices, local(): lax.ppermute(v, 'dom', entry[0])  10.9 us
    ppermute x6, starting transfers between devices, to_chip(): return lax.ppermute(v, 'sub', [(i, i ^ 2) for i in range(4)])  5.48 us
    ppermute x1, waiting for transfers between devices, to_partition(): lax.ppermute(v, 'dom', [(i, i ^ 1) for i in range(lax.axis_size('dom'))])  4.79 us
    ppermute x6, waiting for transfers between devices, local(): lax.ppermute(v, 'dom', entry[0])  4.13 us
    ppermute x16, starting transfers between devices, to_core(): return lax.ppermute(v, 'sub', [(i, i ^ 1) for i in range(4)])  3.46 us
    ppermute x16, waiting for transfers between devices, to_core(): return lax.ppermute(v, 'sub', [(i, i ^ 1) for i in range(4)])  2.2 us
  transfers between devices with their start and end apart: 31, of which 9 were waited for; matrix products, arithmetic and copies ran while one was open for 0% of the time, Pallas kernels for 24%

profile of v6, /device:TPU:12, one launch (start us, length us, event | category | flops | bytes accessed | tf_op | source)
XLA Modules:
  0.0 68.5 jit_solution(17620805408227430931)
XLA Ops:
  0.1 0.8 %copy-done = bf16[512,128]{1,0:T(8,128)(2,1)S(1)} copy-done((bf16[512,128]{1,0:T(8,128)(2,1)S(1)}, bf16[512,128]{1,0:T(8,128)(2,1)}, u32[]{:S(2)}) %copy-start) | copy-done | bytes 131096
  0.9 0.2 copy-done.1
  1.1 0.0 copy-done.4
  1.1 0.3 shard_map.227
  1.4 1.6 %collective-permute-start.8 = (bf16[256,512]{1,0:T(8,128)(2,1)S(1)}, bf16[256,512]{1,0:T(8,128)(2,1)S(1)}, u32[]{:S(2)}, u32[]{:S(2)}) collective-permute-start(bf16[256,512]{1,0:T(8,128)(2,1)S(1)} %get-tuple-element.38), channel_id=1, source_target_pairs={{0,2},{1,3},{2,0},{3,1},{4,6},{5,7},{6,4},{7,5},{8,10},{9,11},{10,... | collective-permute-start | bytes 786440 | tf_op jit(solution)/shard_map/ppermute | solution.py:406
  3.0 0.4 collective-permute-start
  3.4 2.6 %collective-permute-start.1 = (bf16[64,128]{1,0:T(8,128)(2,1)S(1)}, bf16[64,128]{1,0:T(8,128)(2,1)S(1)}, u32[]{:S(2)}, u32[]{:S(2)}) collective-permute-start(bf16[64,128]{1,0:T(8,128)(2,1)S(1)} %get-tuple-element.33), channel_id=1, source_target_pairs={{0,8},{4,12},{8,0},{12,4},{1,9},{5,13},{9,1},{13,5},{2,10},{6,14},... | collective-permute-start | bytes 49160 | tf_op jit(solution)/shard_map/ppermute | solution.py:475
  6.0 2.3 %collective-permute-start.2 = (bf16[64,128]{1,0:T(8,128)(2,1)S(1)}, bf16[64,128]{1,0:T(8,128)(2,1)S(1)}, u32[]{:S(2)}, u32[]{:S(2)}) collective-permute-start(bf16[64,128]{1,0:T(8,128)(2,1)S(1)} %get-tuple-element.34), channel_id=1, source_target_pairs={{4,8},{8,4},{5,9},{9,5},{6,10},{10,6},{7,11},{11,7},{20,24},{24,20... | collective-permute-start | bytes 49160 | tf_op jit(solution)/shard_map/ppermute | solution.py:475
  8.4 3.2 %collective-permute-done.2.refs_4_ = bf16[64,128]{1,0:T(8,128)(2,1)S(1)} collective-permute-done((bf16[64,128]{1,0:T(8,128)(2,1)S(1)}, bf16[64,128]{1,0:T(8,128)(2,1)S(1)}, u32[]{:S(2)}, u32[]{:S(2)}) %collective-permute-start.2) | collective-permute-done | bytes 16416 | tf_op jit(solution)/shard_map/ppermute | solution.py:475
  11.7 0.6 collective-permute-start.3
  12.3 0.5 collective-permute-start.9
  12.8 0.0 collective-permute-start.6
  12.8 0.5 collective-permute-start.7
  13.4 1.8 %shard_map.229 = (bf16[896,512]{1,0:T(8,128)(2,1)S(1)}, bf16[1024,512]{1,0:T(8,128)(2,1)S(1)}, bf16[2048,512]{1,0:T(8,128)(2,1)S(1)}) custom-call(bf16[256,512]{1,0:T(8,128)(2,1)S(1)} %copy-done.11, bf16[128,512]{1,0:T(8,128)(2,1)S(1)} %copy-done.12, bf16[384,512]{1,0:T(8,128)(2,1)S(1)} %copy-done.10, bf16[128,512]{1,0:T(8,128)(2,1)S(1)} %copy-done.13, ...), custom_call_target="tpu_custom_call" | custom-call | flops 402653184 | bytes 5357568 | tf_op jit(solution)/shard_map/pallas_call | solution.py:63
  15.1 3.9 %collective-permute-done.3.lat.l1 = bf16[1216,128]{1,0:T(8,128)(2,1)S(1)} collective-permute-done((bf16[1216,128]{1,0:T(8,128)(2,1)S(1)}, bf16[1216,128]{1,0:T(8,128)(2,1)S(1)}, u32[]{:S(2)}, u32[]{:S(2)}) %collective-permute-start.3) | collective-permute-done | bytes 311328 | tf_op jit(solution)/shard_map/ppermute | solution.py:406
  19.0 0.1 shard_map.230
  19.1 0.1 collective-permute-start.5
  19.1 0.0 collective-permute-done.7.b_out
  19.1 0.5 collective-permute-start.10
  19.6 0.1 collective-permute-start.11
  20.4 0.0 collective-permute-done.4.l2
  20.4 0.5 collective-permute-start.14
  20.9 0.7 collective-permute-start.15
  21.5 0.0 collective-permute-done.10.both
  21.6 0.0 collective-permute-done.5.l3
  21.6 0.0 collective-permute-done.11.round_both
  21.6 0.0 copy-start.2
  21.6 0.0 copy-start.5
  21.6 0.0 copy-start.7
  21.6 0.0 copy-start.8
  21.6 4.8 %shard_map.231 = (bf16[256,512]{1,0:T(8,128)(2,1)S(1)}, bf16[256,512]{1,0:T(8,128)(2,1)S(1)}, bf16[256,512]{1,0:T(8,128)(2,1)S(1)}) custom-call(bf16[1024,512]{1,0:T(8,128)(2,1)S(1)} %get-tuple-element.35.emb, s32[2,1024]{1,0:T(2,128)S(1)} %copy-done.19, f32[1,512]{1,0:T(1,128)S(1)} %bitcast.6, bf16[1216,128]{1,0:T(8,128)(2,1)S(1)} %shard_map.228.after.l0, ...), custom_call_target="tpu_custom_call" | custom-call | flops 2952790016 | bytes 5187588 | tf_op jit(solution)/shard_map/pallas_call | solution.py:63
  26.4 0.1 collective-permute-start.12
  26.5 1.5 %collective-permute-done.12.theirs = bf16[256,512]{1,0:T(8,128)(2,1)S(1)} collective-permute-done((bf16[256,512]{1,0:T(8,128)(2,1)S(1)}, bf16[256,512]{1,0:T(8,128)(2,1)S(1)}, u32[]{:S(2)}, u32[]{:S(2)}) %collective-permute-start.12) | collective-permute-done | bytes 262176 | tf_op jit(solution)/shard_map/ppermute | solution.py:410
  28.0 0.1 shard_map.232.after.mine
  28.1 5.3 %collective-permute-done.15.source = bf16[448,512]{1,0:T(8,128)(2,1)S(1)} collective-permute-done((bf16[448,512]{1,0:T(8,128)(2,1)S(1)}, bf16[448,512]{1,0:T(8,128)(2,1)S(1)}, u32[]{:S(2)}, u32[]{:S(2)}) %collective-permute-start.15) | collective-permute-done | bytes 458784 | tf_op jit(solution)/shard_map/ppermute | solution.py:406
  33.4 0.1 collective-permute-start.16
  33.5 0.7 %collective-permute-start.13 = (bf16[256,512]{1,0:T(8,128)(2,1)S(1)}, bf16[256,512]{1,0:T(8,128)(2,1)S(1)}, u32[]{:S(2)}, u32[]{:S(2)}) collective-permute-start(bf16[256,512]{1,0:T(8,128)(2,1)S(1)} %shard_map.232.after.mine), channel_id=1, source_target_pairs={{0,2},{1,3},{2,0},{3,1},{4,6},{5,7},{6,4},{7,5},{8,10},{9,11},{10,... | collective-permute-start | bytes 786440 | tf_op jit(solution)/shard_map/ppermute | solution.py:406
  34.2 0.5 collective-permute-start.20
  34.7 4.8 %collective-permute-done.16.w3 = bf16[192,512]{1,0:T(8,128)(2,1)S(1)} collective-permute-done((bf16[192,512]{1,0:T(8,128)(2,1)S(1)}, bf16[192,512]{1,0:T(8,128)(2,1)S(1)}, u32[]{:S(2)}, u32[]{:S(2)}) %collective-permute-start.16) | collective-permute-done | bytes 196640 | tf_op jit(solution)/shard_map/ppermute | solution.py:419
  39.6 1.5 %collective-permute-done.13.theirs = bf16[256,512]{1,0:T(8,128)(2,1)S(1)} collective-permute-done((bf16[256,512]{1,0:T(8,128)(2,1)S(1)}, bf16[256,512]{1,0:T(8,128)(2,1)S(1)}, u32[]{:S(2)}, u32[]{:S(2)}) %collective-permute-start.13) | collective-permute-done | bytes 262176 | tf_op jit(solution)/shard_map/ppermute | solution.py:406
  41.1 0.0 copy-start.16
  41.1 1.2 %shard_map.234 = (bf16[256,512]{1,0:T(8,128)(2,1)S(1)}, bf16[384,512]{1,0:T(8,128)(2,1)S(1)}, bf16[32,512]{1,0:T(8,128)(2,1)S(1)}, bf16[32,512]{1,0:T(8,128)(2,1)S(1)}, bf16[32,512]{1,0:T(8,128)(2,1)S(1)}) custom-call(bf16[256,512]{1,0:T(8,128)(2,1)S(1)} %get-tuple-element.39.mesh, bf16[256,512]{1,0:T(8,128)(2,1)S(1)} %shard_map.232.after.mine, ...), custom_call_target="tpu_custom_call" | custom-call | flops 402653184 | bytes 4557312 | tf_op jit(solution)/shard_map/pallas_call | solution.py:63
  42.3 0.0 collective-permute-done.20.second
  42.4 0.1 collective-permute-start.21
  42.5 0.4 collective-permute-start.19
  42.9 1.7 %collective-permute-start.22 = (bf16[32,512]{1,0:T(8,128)(2,1)S(1)}, bf16[32,512]{1,0:T(8,128)(2,1)S(1)}, u32[]{:S(2)}, u32[]{:S(2)}) collective-permute-start(bf16[32,512]{1,0:T(8,128)(2,1)S(1)} %get-tuple-element.51), channel_id=1, source_target_pairs={{0,4},{4,0},{8,12},{12,8},{1,5},{5,1},{9,13},{13,9},{2,6},{6,2},{1... | collective-permute-start | bytes 98312 | tf_op jit(solution)/shard_map/ppermute | solution.py:547
  44.6 0.4 collective-permute-start.23
  45.0 3.5 %collective-permute-start.24 = (bf16[32,512]{1,0:T(8,128)(2,1)S(1)}, bf16[32,512]{1,0:T(8,128)(2,1)S(1)}, u32[]{:S(2)}, u32[]{:S(2)}) collective-permute-start(bf16[32,512]{1,0:T(8,128)(2,1)S(1)} %get-tuple-element.53), channel_id=1, source_target_pairs={{4,8},{8,4},{5,9},{9,5},{6,10},{10,6},{7,11},{11,7},{20,24},{24,20... | collective-permute-start | bytes 98312 | tf_op jit(solution)/shard_map/ppermute | solution.py:547
  49.2 0.7 %collective-permute-start.29 = (bf16[384,512]{1,0:T(8,128)(2,1)S(1)}, bf16[384,512]{1,0:T(8,128)(2,1)S(1)}, u32[]{:S(2)}, u32[]{:S(2)}) collective-permute-start(bf16[384,512]{1,0:T(8,128)(2,1)S(1)} %get-tuple-element.58.w0), channel_id=1, source_target_pairs={{0,2},{1,3},{2,0},{3,1},{4,6},{5,7},{6,4},{7,5},{8,10},{9,11},{10,... | collective-permute-start | bytes 1179656 | tf_op jit(solution)/shard_map/ppermute | solution.py:406
  49.9 0.9 %collective-permute-done.24.refs_2_ = bf16[32,512]{1,0:T(8,128)(2,1)S(1)} collective-permute-done((bf16[32,512]{1,0:T(8,128)(2,1)S(1)}, bf16[32,512]{1,0:T(8,128)(2,1)S(1)}, u32[]{:S(2)}, u32[]{:S(2)}) %collective-permute-start.24) | collective-permute-done | bytes 32800 | tf_op jit(solution)/shard_map/ppermute | solution.py:547
  50.8 0.1 collective-permute-start.25
  50.9 0.0 collective-permute-done.21.pair_beside
  50.9 0.0 copy-start.21
  50.9 2.6 %shard_map.236 = (bf16[1536,512]{1,0:T(8,128)(2,1)S(1)}, f32[1024,512]{1,0:T(8,128)S(1)}, bf16[512,512]{1,0:T(8,128)(2,1)S(1)}, bf16[512,512]{1,0:T(8,128)(2,1)S(1)}) custom-call(bf16[2048,512]{1,0:T(8,128)(2,1)S(1)} %get-tuple-element.45.emb, bf16[256,512]{1,0:T(8,128)(2,1)S(1)} %get-tuple-element.44.after.mine.middle, ...), custom_call_target="tpu_custom_call" | custom-call | flops 1610612736 | bytes 10240000 | tf_op jit(solution)/shard_map/pallas_call | solution.py:63
  53.5 0.0 copy-start.9
  53.6 5.8 %shard_map.238 = (bf16[256,512]{1,0:T(8,128)(2,1)S(1)}, bf16[256,512]{1,0:T(8,128)(2,1)S(1)}) custom-call(bf16[2048,512]{1,0:T(8,128)(2,1)S(1)} %get-tuple-element.45.emb, s32[2,2048]{1,0:T(2,128)S(1)} %copy-done.16, f32[1,512]{1,0:T(1,128)S(1)} %bitcast.7, bf16[1536,512]{1,0:T(8,128)(2,1)S(1)} %get-tuple-element.47.table, ...), custom_call_target="tpu_custom_call" | custom-call | flops 3489660928 | bytes 7555076 | tf_op jit(solution)/shard_map/pallas_call | solution.py:63
  59.4 0.6 collective-permute-start.26
  60.0 0.1 collective-permute-start.28
  60.0 0.4 collective-permute-start.30
  60.5 0.6 collective-permute-done.26.theirs
  61.1 0.1 shard_map.239
  61.2 1.2 %collective-permute-start.27 = (bf16[128,512]{1,0:T(8,128)(2,1)S(1)}, bf16[128,512]{1,0:T(8,128)(2,1)S(1)}, u32[]{:S(2)}, u32[]{:S(2)}) collective-permute-start(bf16[128,512]{1,0:T(8,128)(2,1)S(1)} %get-tuple-element.57), channel_id=1, source_target_pairs={{0,2},{1,3},{2,0},{3,1},{4,6},{5,7},{6,4},{7,5},{8,10},{9,11},{10,... | collective-permute-start | bytes 393224 | tf_op jit(solution)/shard_map/ppermute | solution.py:406
  62.4 4.6 %collective-permute-done.27.theirs = bf16[128,512]{1,0:T(8,128)(2,1)S(1)} collective-permute-done((bf16[128,512]{1,0:T(8,128)(2,1)S(1)}, bf16[128,512]{1,0:T(8,128)(2,1)S(1)}, u32[]{:S(2)}, u32[]{:S(2)}) %collective-permute-start.27) | collective-permute-done | bytes 131104 | tf_op jit(solution)/shard_map/ppermute | solution.py:406
  67.0 1.5 %shard_map.240 = bf16[128,512]{1,0:T(8,128)(2,1)} custom-call(bf16[256,512]{1,0:T(8,128)(2,1)S(1)} %get-tuple-element.44.after.mine.middle, bf16[128,512]{1,0:T(8,128)(2,1)S(1)} %get-tuple-element.56.mine, bf16[128,512]{1,0:T(8,128)(2,1)S(1)} %collective-permute-done.27.theirs, f32[1,512]{1,0:T(1,128)S(1)} %bitcast.5, ...), custom_call_target="tpu_custom_call" | custom-call | flops 201326592 | bytes 2230272 | tf_op jit(solution)/shard_map/pallas_call | solution.py:63
  (57 shorter events, 0.2 us)
Async XLA Ops:
  0.0 0.9 %copy-start = (bf16[512,128]{1,0:T(8,128)(2,1)S(1)}, bf16[512,128]{1,0:T(8,128)(2,1)}, u32[]{:S(2)}) copy-start(bf16[512,128]{1,0:T(8,128)(2,1)} %refs_0_.1) | copy-start | bytes 393220
  0.0 0.9 %copy-start.6 = (s32[1,4,64]{2,1,0:T(4,128)S(1)}, s32[1,4,64]{2,1,0:T(4,128)}, u32[]{:S(2)}) copy-start(s32[1,4,64]{2,1,0:T(4,128)} %send.2) | copy-start | bytes 3076
  0.0 1.1 %copy-start.1 = (bf16[384,512]{1,0:T(8,128)(2,1)S(1)}, bf16[384,512]{1,0:T(8,128)(2,1)}, u32[]{:S(2)}) copy-start(bf16[384,512]{1,0:T(8,128)(2,1)} %o_in.1) | copy-start | bytes 1179652
  0.0 1.1 %copy-start.4 = (bf16[128,512]{1,0:T(8,128)(2,1)S(1)}, bf16[128,512]{1,0:T(8,128)(2,1)}, u32[]{:S(2)}) copy-start(bf16[128,512]{1,0:T(8,128)(2,1)} %o_out.1) | copy-start | bytes 393220
  0.0 11.6 %copy-start.3 = (bf16[512,128]{1,0:T(8,128)(2,1)S(1)}, bf16[512,128]{1,0:T(8,128)(2,1)}, u32[]{:S(2)}) copy-start(bf16[512,128]{1,0:T(8,128)(2,1)} %refs_1_.1) | copy-start | bytes 393220
  0.0 13.3 %copy-start.11 = (bf16[256,512]{1,0:T(8,128)(2,1)S(1)}, bf16[256,512]{1,0:T(8,128)(2,1)}, u32[]{:S(2)}) copy-start(bf16[256,512]{1,0:T(8,128)(2,1)} %e_in.1) | copy-start | bytes 786436
  0.0 13.3 %copy-start.12 = (bf16[128,512]{1,0:T(8,128)(2,1)S(1)}, bf16[128,512]{1,0:T(8,128)(2,1)}, u32[]{:S(2)}) copy-start(bf16[128,512]{1,0:T(8,128)(2,1)} %e_out.1) | copy-start | bytes 393220
  0.0 13.2 %copy-start.10 = (bf16[384,512]{1,0:T(8,128)(2,1)S(1)}, bf16[384,512]{1,0:T(8,128)(2,1)}, u32[]{:S(2)}) copy-start(bf16[384,512]{1,0:T(8,128)(2,1)} %p_in.1) | copy-start | bytes 1179652
  0.1 13.2 %copy-start.13 = (bf16[128,512]{1,0:T(8,128)(2,1)S(1)}, bf16[128,512]{1,0:T(8,128)(2,1)}, u32[]{:S(2)}) copy-start(bf16[128,512]{1,0:T(8,128)(2,1)} %p_out.1) | copy-start | bytes 393220
  0.1 13.2 %copy-start.15 = (f32[4,1024]{1,0:T(4,128)S(1)}, f32[4,1024]{1,0:T(4,128)}, u32[]{:S(2)}) copy-start(f32[4,1024]{1,0:T(4,128)} %egeom.1) | copy-start | bytes 49156
  0.1 13.2 %copy-start.17 = (f32[4,512]{1,0:T(4,128)S(1)}, f32[4,512]{1,0:T(4,128)}, u32[]{:S(2)}) copy-start(f32[4,512]{1,0:T(4,128)} %egeo.1) | copy-start | bytes 24580
  0.1 13.2 %copy-start.14 = (f32[4,2048]{1,0:T(4,128)S(1)}, f32[4,2048]{1,0:T(4,128)}, u32[]{:S(2)}) copy-start(f32[4,2048]{1,0:T(4,128)} %pgeom.1) | copy-start | bytes 98308
  0.1 13.2 %copy-start.18 = (f32[4,512]{1,0:T(4,128)S(1)}, f32[4,512]{1,0:T(4,128)}, u32[]{:S(2)}) copy-start(f32[4,512]{1,0:T(4,128)} %pgeo.1) | copy-start | bytes 24580
  1.1 20.5 %copy-start.19 = (s32[2,1024]{1,0:T(2,128)S(1)}, s32[2,1024]{1,0:T(2,128)}, u32[]{:S(2)}) copy-start(s32[2,1024]{1,0:T(2,128)} %edges.3) | copy-start | bytes 24580
  1.1 20.5 %copy-start.20 = (f32[512]{0:T(512)S(1)}, f32[512]{0:T(512)}, u32[]{:S(2)}) copy-start(f32[512]{0:T(512)} %param.44) | copy-start | bytes 6148
  1.4 10.8 %collective-permute-start.8 = (bf16[256,512]{1,0:T(8,128)(2,1)S(1)}, bf16[256,512]{1,0:T(8,128)(2,1)S(1)}, u32[]{:S(2)}, u32[]{:S(2)}) collective-permute-start(bf16[256,512]{1,0:T(8,128)(2,1)S(1)} %get-tuple-element.38), channel_id=1, source_target_pairs={{0,2},{1,3},{2,0},{3,1},{4,6},{5,7},{6,4},{7,5},{8,10},{9,11},{10,... | collective-permute-start | bytes 786440 | tf_op jit(solution)/shard_map/ppermute | solution.py:406
  3.0 5.4 %collective-permute-start = (bf16[64,128]{1,0:T(8,128)(2,1)S(1)}, bf16[64,128]{1,0:T(8,128)(2,1)S(1)}, u32[]{:S(2)}, u32[]{:S(2)}) collective-permute-start(bf16[64,128]{1,0:T(8,128)(2,1)S(1)} %get-tuple-element.32), channel_id=1, source_target_pairs={{0,4},{4,0},{8,12},{12,8},{1,5},{5,1},{9,13},{13,9},{2,6},{6,2},{1... | collective-permute-start | bytes 49160 | tf_op jit(solution)/shard_map/ppermute | solution.py:475
  3.4 5.0 %collective-permute-start.1 = (bf16[64,128]{1,0:T(8,128)(2,1)S(1)}, bf16[64,128]{1,0:T(8,128)(2,1)S(1)}, u32[]{:S(2)}, u32[]{:S(2)}) collective-permute-start(bf16[64,128]{1,0:T(8,128)(2,1)S(1)} %get-tuple-element.33), channel_id=1, source_target_pairs={{0,8},{4,12},{8,0},{12,4},{1,9},{5,13},{9,1},{13,5},{2,10},{6,14},... | collective-permute-start | bytes 49160 | tf_op jit(solution)/shard_map/ppermute | solution.py:475
  6.0 5.6 %collective-permute-start.2 = (bf16[64,128]{1,0:T(8,128)(2,1)S(1)}, bf16[64,128]{1,0:T(8,128)(2,1)S(1)}, u32[]{:S(2)}, u32[]{:S(2)}) collective-permute-start(bf16[64,128]{1,0:T(8,128)(2,1)S(1)} %get-tuple-element.34), channel_id=1, source_target_pairs={{4,8},{8,4},{5,9},{9,5},{6,10},{10,6},{7,11},{11,7},{20,24},{24,20... | collective-permute-start | bytes 49160 | tf_op jit(solution)/shard_map/ppermute | solution.py:475
  11.7 7.3 %collective-permute-start.3 = (bf16[1216,128]{1,0:T(8,128)(2,1)S(1)}, bf16[1216,128]{1,0:T(8,128)(2,1)S(1)}, u32[]{:S(2)}, u32[]{:S(2)}) collective-permute-start(bf16[1216,128]{1,0:T(8,128)(2,1)S(1)} %shard_map.228.after.l0), channel_id=1, source_target_pairs={{0,2},{1,3},{2,0},{3,1},{4,6},{5,7},{6,4},{7,5},{8,10},{9,11},{10,... | collective-permute-start | bytes 933896 | tf_op jit(solution)/shard_map/ppermute | solution.py:406
  12.3 7.4 %collective-permute-start.9 = (bf16[256,512]{1,0:T(8,128)(2,1)S(1)}, bf16[256,512]{1,0:T(8,128)(2,1)S(1)}, u32[]{:S(2)}, u32[]{:S(2)}) collective-permute-start(bf16[256,512]{1,0:T(8,128)(2,1)S(1)} %collective-permute-done.8.across), channel_id=1, source_target_pairs={{0,16},{16,0},{1,17},{17,1},{2,18},{18,2},{3,19},{19,3},{4,20},{20... | collective-permute-start | bytes 786440 | tf_op jit(solution)/shard_map/ppermute | solution.py:415
  12.8 8.1 %collective-permute-start.6 = (bf16[384,512]{1,0:T(8,128)(2,1)S(1)}, bf16[384,512]{1,0:T(8,128)(2,1)S(1)}, u32[]{:S(2)}, u32[]{:S(2)}) collective-permute-start(bf16[384,512]{1,0:T(8,128)(2,1)S(1)} %copy-done.1), channel_id=1, source_target_pairs={{0,1},{1,0},{2,3},{3,2},{4,5},{5,4},{6,7},{7,6},{8,9},{9,8},{10,11... | collective-permute-start | bytes 1179656 | tf_op jit(solution)/shard_map/ppermute | solution.py:410
  12.8 6.4 %collective-permute-start.7 = (bf16[128,512]{1,0:T(8,128)(2,1)S(1)}, bf16[128,512]{1,0:T(8,128)(2,1)S(1)}, u32[]{:S(2)}, u32[]{:S(2)}) collective-permute-start(bf16[128,512]{1,0:T(8,128)(2,1)S(1)} %copy-done.4), channel_id=1, source_target_pairs={{0,1},{1,0},{2,3},{3,2},{4,5},{5,4},{6,7},{7,6},{8,9},{9,8},{10,11... | collective-permute-start | bytes 393224 | tf_op jit(solution)/shard_map/ppermute | solution.py:410
  13.3 7.1 %collective-permute-start.4 = (bf16[1216,128]{1,0:T(8,128)(2,1)S(1)}, bf16[1216,128]{1,0:T(8,128)(2,1)S(1)}, u32[]{:S(2)}, u32[]{:S(2)}) collective-permute-start(bf16[1216,128]{1,0:T(8,128)(2,1)S(1)} %shard_map.228.after.l0), channel_id=1, source_target_pairs={{0,1},{1,0},{2,3},{3,2},{4,5},{5,4},{6,7},{7,6},{8,9},{9,8},{10,11... | collective-permute-start | bytes 933896 | tf_op jit(solution)/shard_map/ppermute | solution.py:410
  19.1 2.5 %collective-permute-start.5 = (bf16[1216,128]{1,0:T(8,128)(2,1)S(1)}, bf16[1216,128]{1,0:T(8,128)(2,1)S(1)}, u32[]{:S(2)}, u32[]{:S(2)}) collective-permute-start(bf16[1216,128]{1,0:T(8,128)(2,1)S(1)} %get-tuple-element.37), channel_id=1, source_target_pairs={{0,1},{1,0},{2,3},{3,2},{4,5},{5,4},{6,7},{7,6},{8,9},{9,8},{10,11... | collective-permute-start | bytes 933896 | tf_op jit(solution)/shard_map/ppermute | solution.py:410
  19.1 2.4 %collective-permute-start.10 = (bf16[256,512]{1,0:T(8,128)(2,1)S(1)}, bf16[256,512]{1,0:T(8,128)(2,1)S(1)}, u32[]{:S(2)}, u32[]{:S(2)}) collective-permute-start(bf16[256,512]{1,0:T(8,128)(2,1)S(1)} %collective-permute-done.8.across), channel_id=1, source_target_pairs={{0,1},{1,0},{2,3},{3,2},{4,5},{5,4},{6,7},{7,6},{8,9},{9,8},{10,11... | collective-permute-start | bytes 786440 | tf_op jit(solution)/shard_map/ppermute | solution.py:410
  19.6 1.9 %collective-permute-start.11 = (bf16[256,512]{1,0:T(8,128)(2,1)S(1)}, bf16[256,512]{1,0:T(8,128)(2,1)S(1)}, u32[]{:S(2)}, u32[]{:S(2)}) collective-permute-start(bf16[256,512]{1,0:T(8,128)(2,1)S(1)} %collective-permute-done.9.round_), channel_id=1, source_target_pairs={{0,1},{1,0},{2,3},{3,2},{4,5},{5,4},{6,7},{7,6},{8,9},{9,8},{10,11... | collective-permute-start | bytes 786440 | tf_op jit(solution)/shard_map/ppermute | solution.py:410
  20.4 19.2 %collective-permute-start.14 = (bf16[896,512]{1,0:T(8,128)(2,1)S(1)}, bf16[896,512]{1,0:T(8,128)(2,1)S(1)}, u32[]{:S(2)}, u32[]{:S(2)}) collective-permute-start(bf16[896,512]{1,0:T(8,128)(2,1)S(1)} %get-tuple-element.36.weights.w0), channel_id=1, source_target_pairs={{0,1},{1,0},{2,3},{3,2},{4,5},{5,4},{6,7},{7,6},{8,9},{9,8},{10,11... | collective-permute-start | bytes 2752520 | tf_op jit(solution)/shard_map/ppermute | solution.py:410
  20.9 12.5 %collective-permute-start.15 = (bf16[448,512]{1,0:T(8,128)(2,1)S(1)}, bf16[448,512]{1,0:T(8,128)(2,1)S(1)}, u32[]{:S(2)}, u32[]{:S(2)}) collective-permute-start(bf16[448,512]{1,0:T(8,128)(2,1)S(1)} %get-tuple-element.42), channel_id=1, source_target_pairs={{0,2},{1,3},{2,0},{3,1},{4,6},{5,7},{6,4},{7,5},{8,10},{9,11},{10,... | collective-permute-start | bytes 1376264 | tf_op jit(solution)/shard_map/ppermute | solution.py:406
  21.6 19.5 %copy-start.2 = (bf16[256,512]{1,0:T(8,128)(2,1)S(1)}, bf16[256,512]{1,0:T(8,128)(2,1)}, u32[]{:S(2)}) copy-start(bf16[256,512]{1,0:T(8,128)(2,1)} %n_in.1) | copy-start | bytes 786436
  21.6 19.4 %copy-start.5 = (bf16[128,512]{1,0:T(8,128)(2,1)S(1)}, bf16[128,512]{1,0:T(8,128)(2,1)}, u32[]{:S(2)}) copy-start(bf16[128,512]{1,0:T(8,128)(2,1)} %n_out.1) | copy-start | bytes 393220
  21.6 19.4 %copy-start.7 = (f32[512]{0:T(512)S(1)}, f32[512]{0:T(512)}, u32[]{:S(2)}) copy-start(f32[512]{0:T(512)} %param.45) | copy-start | bytes 6148
  21.6 19.4 %copy-start.8 = (s32[1,4,32]{2,1,0:T(4,128)S(1)}, s32[1,4,32]{2,1,0:T(4,128)}, u32[]{:S(2)}) copy-start(s32[1,4,32]{2,1,0:T(4,128)} %send.3) | copy-start | bytes 1540
  26.4 1.6 %collective-permute-start.12 = (bf16[256,512]{1,0:T(8,128)(2,1)S(1)}, bf16[256,512]{1,0:T(8,128)(2,1)S(1)}, u32[]{:S(2)}, u32[]{:S(2)}) collective-permute-start(bf16[256,512]{1,0:T(8,128)(2,1)S(1)} %get-tuple-element.41), channel_id=1, source_target_pairs={{0,1},{1,0},{2,3},{3,2},{4,5},{5,4},{6,7},{7,6},{8,9},{9,8},{10,11... | collective-permute-start | bytes 786440 | tf_op jit(solution)/shard_map/ppermute | solution.py:410
  33.4 6.1 %collective-permute-start.16 = (bf16[192,512]{1,0:T(8,128)(2,1)S(1)}, bf16[192,512]{1,0:T(8,128)(2,1)S(1)}, u32[]{:S(2)}, u32[]{:S(2)}) collective-permute-start(bf16[192,512]{1,0:T(8,128)(2,1)S(1)} %get-tuple-element.43.w2), channel_id=1, source_target_pairs={{0,4},{4,0},{8,12},{12,8},{1,5},{5,1},{9,13},{13,9},{2,6},{6,2},{1... | collective-permute-start | bytes 589832 | tf_op jit(solution)/shard_map/ppermute | solution.py:419
  33.5 7.5 %collective-permute-start.13 = (bf16[256,512]{1,0:T(8,128)(2,1)S(1)}, bf16[256,512]{1,0:T(8,128)(2,1)S(1)}, u32[]{:S(2)}, u32[]{:S(2)}) collective-permute-start(bf16[256,512]{1,0:T(8,128)(2,1)S(1)} %shard_map.232.after.mine), channel_id=1, source_target_pairs={{0,2},{1,3},{2,0},{3,1},{4,6},{5,7},{6,4},{7,5},{8,10},{9,11},{10,... | collective-permute-start | bytes 786440 | tf_op jit(solution)/shard_map/ppermute | solution.py:406
  34.2 8.1 %collective-permute-start.20 = (bf16[256,512]{1,0:T(8,128)(2,1)S(1)}, bf16[256,512]{1,0:T(8,128)(2,1)S(1)}, u32[]{:S(2)}, u32[]{:S(2)}) collective-permute-start(bf16[256,512]{1,0:T(8,128)(2,1)S(1)} %get-tuple-element.46.first), channel_id=1, source_target_pairs={{0,16},{16,0},{1,17},{17,1},{2,18},{18,2},{3,19},{19,3},{4,20},{20... | collective-permute-start | bytes 786440 | tf_op jit(solution)/shard_map/ppermute | solution.py:415
  34.7 4.8 %collective-permute-start.17 = (bf16[192,512]{1,0:T(8,128)(2,1)S(1)}, bf16[192,512]{1,0:T(8,128)(2,1)S(1)}, u32[]{:S(2)}, u32[]{:S(2)}) collective-permute-start(bf16[192,512]{1,0:T(8,128)(2,1)S(1)} %get-tuple-element.43.w2), channel_id=1, source_target_pairs={{0,1},{1,0},{2,3},{3,2},{4,5},{5,4},{6,7},{7,6},{8,9},{9,8},{10,11... | collective-permute-start | bytes 589832 | tf_op jit(solution)/shard_map/ppermute | solution.py:410
  39.5 1.5 %collective-permute-start.18 = (bf16[192,512]{1,0:T(8,128)(2,1)S(1)}, bf16[192,512]{1,0:T(8,128)(2,1)S(1)}, u32[]{:S(2)}, u32[]{:S(2)}) collective-permute-start(bf16[192,512]{1,0:T(8,128)(2,1)S(1)} %collective-permute-done.16.w3), channel_id=1, source_target_pairs={{0,1},{1,0},{2,3},{3,2},{4,5},{5,4},{6,7},{7,6},{8,9},{9,8},{10,11... | collective-permute-start | bytes 589832 | tf_op jit(solution)/shard_map/ppermute | solution.py:410
  41.1 9.8 %copy-start.16 = (s32[2,2048]{1,0:T(2,128)S(1)}, s32[2,2048]{1,0:T(2,128)}, u32[]{:S(2)}) copy-start(s32[2,2048]{1,0:T(2,128)} %edges.5) | copy-start | bytes 49156
  42.4 8.5 %collective-permute-start.21 = (bf16[512,512]{1,0:T(8,128)(2,1)S(1)}, bf16[512,512]{1,0:T(8,128)(2,1)S(1)}, u32[]{:S(2)}, u32[]{:S(2)}) collective-permute-start(bf16[512,512]{1,0:T(8,128)(2,1)S(1)} %shard_map.235.pair), channel_id=1, source_target_pairs={{0,1},{1,0},{2,3},{3,2},{4,5},{5,4},{6,7},{7,6},{8,9},{9,8},{10,11... | collective-permute-start | bytes 1572872 | tf_op jit(solution)/shard_map/ppermute | solution.py:410
  42.5 8.4 %collective-permute-start.19 = (bf16[256,512]{1,0:T(8,128)(2,1)S(1)}, bf16[256,512]{1,0:T(8,128)(2,1)S(1)}, u32[]{:S(2)}, u32[]{:S(2)}) collective-permute-start(bf16[256,512]{1,0:T(8,128)(2,1)S(1)} %get-tuple-element.44.after.mine.middle), channel_id=1, source_target_pairs={{0,1},{1,0},{2,3},{3,2},{4,5},{5,4},{6,7},{7,6},{8,9},{9,8},{10,11... | collective-permute-start | bytes 786440 | tf_op jit(solution)/shard_map/ppermute | solution.py:410
  42.9 6.2 %collective-permute-start.22 = (bf16[32,512]{1,0:T(8,128)(2,1)S(1)}, bf16[32,512]{1,0:T(8,128)(2,1)S(1)}, u32[]{:S(2)}, u32[]{:S(2)}) collective-permute-start(bf16[32,512]{1,0:T(8,128)(2,1)S(1)} %get-tuple-element.51), channel_id=1, source_target_pairs={{0,4},{4,0},{8,12},{12,8},{1,5},{5,1},{9,13},{13,9},{2,6},{6,2},{1... | collective-permute-start | bytes 98312 | tf_op jit(solution)/shard_map/ppermute | solution.py:547
  44.6 5.3 %collective-permute-start.23 = (bf16[32,512]{1,0:T(8,128)(2,1)S(1)}, bf16[32,512]{1,0:T(8,128)(2,1)S(1)}, u32[]{:S(2)}, u32[]{:S(2)}) collective-permute-start(bf16[32,512]{1,0:T(8,128)(2,1)S(1)} %get-tuple-element.52), channel_id=1, source_target_pairs={{0,8},{4,12},{8,0},{12,4},{1,9},{5,13},{9,1},{13,5},{2,10},{6,14},... | collective-permute-start | bytes 98312 | tf_op jit(solution)/shard_map/ppermute | solution.py:547
  45.0 5.8 %collective-permute-start.24 = (bf16[32,512]{1,0:T(8,128)(2,1)S(1)}, bf16[32,512]{1,0:T(8,128)(2,1)S(1)}, u32[]{:S(2)}, u32[]{:S(2)}) collective-permute-start(bf16[32,512]{1,0:T(8,128)(2,1)S(1)} %get-tuple-element.53), channel_id=1, source_target_pairs={{4,8},{8,4},{5,9},{9,5},{6,10},{10,6},{7,11},{11,7},{20,24},{24,20... | collective-permute-start | bytes 98312 | tf_op jit(solution)/shard_map/ppermute | solution.py:547
  49.2 10.9 %collective-permute-start.29 = (bf16[384,512]{1,0:T(8,128)(2,1)S(1)}, bf16[384,512]{1,0:T(8,128)(2,1)S(1)}, u32[]{:S(2)}, u32[]{:S(2)}) collective-permute-start(bf16[384,512]{1,0:T(8,128)(2,1)S(1)} %get-tuple-element.58.w0), channel_id=1, source_target_pairs={{0,2},{1,3},{2,0},{3,1},{4,6},{5,7},{6,4},{7,5},{8,10},{9,11},{10,... | collective-permute-start | bytes 1179656 | tf_op jit(solution)/shard_map/ppermute | solution.py:406
  50.8 2.7 %collective-permute-start.25 = (bf16[96,512]{1,0:T(8,128)(2,1)S(1)}, bf16[96,512]{1,0:T(8,128)(2,1)S(1)}, u32[]{:S(2)}, u32[]{:S(2)}) collective-permute-start(bf16[96,512]{1,0:T(8,128)(2,1)S(1)} %shard_map.237.halo), channel_id=1, source_target_pairs={{0,1},{1,0},{2,3},{3,2},{4,5},{5,4},{6,7},{7,6},{8,9},{9,8},{10,11... | collective-permute-start | bytes 294920 | tf_op jit(solution)/shard_map/ppermute | solution.py:410
  50.9 2.6 %copy-start.21 = (f32[512]{0:T(512)S(1)}, f32[512]{0:T(512)}, u32[]{:S(2)}) copy-start(f32[512]{0:T(512)} %param.46) | copy-start | bytes 6148
  53.5 13.5 %copy-start.9 = (f32[512]{0:T(512)S(1)}, f32[512]{0:T(512)}, u32[]{:S(2)}) copy-start(f32[512]{0:T(512)} %param.47) | copy-start | bytes 6148
  59.4 1.7 %collective-permute-start.26 = (bf16[256,512]{1,0:T(8,128)(2,1)S(1)}, bf16[256,512]{1,0:T(8,128)(2,1)S(1)}, u32[]{:S(2)}, u32[]{:S(2)}) collective-permute-start(bf16[256,512]{1,0:T(8,128)(2,1)S(1)} %get-tuple-element.55), channel_id=1, source_target_pairs={{0,1},{1,0},{2,3},{3,2},{4,5},{5,4},{6,7},{7,6},{8,9},{9,8},{10,11... | collective-permute-start | bytes 786440 | tf_op jit(solution)/shard_map/ppermute | solution.py:410
  60.0 2.4 %collective-permute-start.28 = (bf16[384,512]{1,0:T(8,128)(2,1)S(1)}, bf16[384,512]{1,0:T(8,128)(2,1)S(1)}, u32[]{:S(2)}, u32[]{:S(2)}) collective-permute-start(bf16[384,512]{1,0:T(8,128)(2,1)S(1)} %get-tuple-element.58.w0), channel_id=1, source_target_pairs={{0,1},{1,0},{2,3},{3,2},{4,5},{5,4},{6,7},{7,6},{8,9},{9,8},{10,11... | collective-permute-start | bytes 1179656 | tf_op jit(solution)/shard_map/ppermute | solution.py:410
  60.0 2.3 %collective-permute-start.30 = (bf16[384,512]{1,0:T(8,128)(2,1)S(1)}, bf16[384,512]{1,0:T(8,128)(2,1)S(1)}, u32[]{:S(2)}, u32[]{:S(2)}) collective-permute-start(bf16[384,512]{1,0:T(8,128)(2,1)S(1)} %collective-permute-done.29.w2), channel_id=1, source_target_pairs={{0,1},{1,0},{2,3},{3,2},{4,5},{5,4},{6,7},{7,6},{8,9},{9,8},{10,11... | collective-permute-start | bytes 1179656 | tf_op jit(solution)/shard_map/ppermute | solution.py:410
  61.2 5.8 %collective-permute-start.27 = (bf16[128,512]{1,0:T(8,128)(2,1)S(1)}, bf16[128,512]{1,0:T(8,128)(2,1)S(1)}, u32[]{:S(2)}, u32[]{:S(2)}) collective-permute-start(bf16[128,512]{1,0:T(8,128)(2,1)S(1)} %get-tuple-element.57), channel_id=1, source_target_pairs={{0,2},{1,3},{2,0},{3,1},{4,6},{5,7},{6,4},{7,5},{8,10},{9,11},{10,... | collective-permute-start | bytes 393224 | tf_op jit(solution)/shard_map/ppermute | solution.py:406

commit v7 on v6

--- a/solution.py
+++ b/solution.py
@@ -12,7 +12,6 @@
 STEP = 512
 GATHERED = 1024
 LONG = 30 * 10**9
-BY_PART = ("dom",)
 VMEM_BYTES = 24 * 1024 * 1024
 I16 = jnp.int16
 BF16 = jnp.bfloat16
@@ -147,25 +146,24 @@
             out[begin : begin + STEP, :] = embed_rows(geom[:, begin : begin + STEP], geo[...])
 
 
-def cross_kernel(parts, weights, lat, crossing, lat_out):
+def cross_kernel(parts, weights, lat, lat_out, *crossing):
     lat_out[...] = lat[...]
-    first, place = 0, 0
-    for rows, axes in parts:
-        half = rows // 2
-        begin = pl.multiple_of(first + parity(axes) * half, 64)
-        crossing[place : place + half, :] = weights[pl.ds(begin, half), :]
-        first, place = first + rows, place + half
+    first = 0
+    for stack, out in zip(parts, crossing):
+        place = 0
+        for rows in stack:
+            half = rows // 2
+            begin = pl.multiple_of(first + lax.axis_index("groups") * half, 64)
+            out[place : place + half, :] = weights[pl.ds(begin, half), :]
+            first, place = first + rows, place + half
 
 
 def pair_kernel(first, second, after, out):
     stack_into(out, (first, second))
 
 
-def split_kernel(source, after, *outs):
-    first = 0
-    for out in outs:
-        out[...] = source[first : first + out.shape[0], :]
-        first += out.shape[0]
+def hold_kernel(source, after, out):
+    out[...] = source[...]
 
 
 def concat_kernel(*refs):
@@ -178,13 +176,9 @@
     target[pl.ds(pl.multiple_of(place, rows), rows), :] = source[first : first + rows, :]
 
 
-def parity(axes):
-    return lax.rem(sum(lax.axis_index(axis) for axis in axes), 2)
-
-
-def put_half(target, k, source, step, other, axes=("groups",)):
+def put_half(target, k, source, step, other):
     rows = target.shape[0] // 4
-    which = lax.bitwise_xor(parity(axes), other)
+    which = lax.bitwise_xor(lax.axis_index("groups"), other)
     begin = lax.bitwise_xor(lax.axis_index("sub"), step) * rows
     for base, count in ((0, k // 2), (k // 2, (rows - k) // 2)):
         place = pl.multiple_of(begin + 2 * base + which * count, 64)
@@ -235,18 +229,20 @@
                 totals[...] += part
 
 
-def hand_out(totals, gain, keep, give):
+def hand_out(totals, gain, keep, *give):
     rows = totals.shape[0] // 4
     core = lax.rem(lax.axis_index("sub"), 2)
     for half in range(2):
-        for out, which in ((keep, core), (give, 1 - core)):
+        kept = keep.at[pl.ds(half * rows, rows), :]
+        given = give[0].at[pl.ds(half * rows, rows), :] if len(give) == 1 else give[half]
+        for out, which in ((kept, core), (given, 1 - core)):
             place = pl.multiple_of((2 * half + which) * rows, rows)
-            out[half * rows : (half + 1) * rows, :] = (totals[pl.ds(place, rows), :] * gain[...]).astype(BF16)
+            out[...] = (totals[pl.ds(place, rows), :] * gain[...]).astype(BF16)
 
 
 def enc_kernel(
     plan, slots, grid_rows, mesh_rows, k_in, emb, edges, gain, l0, l1, l2, l3, o_in, o_out, b_in, b_out,
-    across, round_, both, round_both, live, keep, give, own_mesh, full, stack, table, messages, totals,
+    across, round_, both, round_both, live, keep, give, give_more, own_mesh, full, stack, table, messages, totals,
 ):
     d = gain.shape[1]
     quarter = lax.axis_index("sub")
@@ -288,7 +284,7 @@
         return dot(jnp.concatenate(chosen, axis=1), table[...])
 
     edge_blocks(edges, live[0] * BLOCK, first_stage, joined(stack, k_in, d // 4), messages, totals)
-    hand_out(totals, gain, keep, give)
+    hand_out(totals, gain, keep, give, give_more)
 
 
 def node_update(mesh, shares, w_in, w_out, gain):
@@ -302,8 +298,10 @@
     return (mine.astype(F32) + theirs.astype(F32)).astype(BF16)
 
 
-def add_kernel(mine, theirs, out):
-    out[...] = add(mine[...], theirs[...])
+def add_kernel(mine, first, second, out):
+    rows = first.shape[0]
+    out[:rows, :] = add(mine[:rows, :], first[...])
+    out[rows:, :] = add(mine[rows:, :], second[...])
 
 
 def node_kernel(
@@ -312,10 +310,10 @@
     outs, stack = rest[:-1], rest[-1]
     put_shard(stack, w0, 0, 0)
     put_shard(stack, w1, 0, 1)
-    put_half(stack, k_in, w2, 2, 0, BY_PART)
-    put_half(stack, k_in, w3, 2, 1, BY_PART)
-    put_half(stack, k_in, w4, 3, 0, BY_PART)
-    put_half(stack, k_in, w5, 3, 1, BY_PART)
+    put_half(stack, k_in, w2, 2, 0)
+    put_half(stack, k_in, w3, 2, 1)
+    put_half(stack, k_in, w4, 3, 0)
+    put_half(stack, k_in, w5, 3, 1)
     w_in, w_out = joined(stack, 0, k_in), joined(stack, k_in, k_out)
     fresh = node_update(mesh[...], add(mine[...], theirs[...]), w_in, w_out, gain[...])
     out[...] = fresh
@@ -415,12 +413,12 @@
     return lax.ppermute(v, "groups", [(i, count - 1 - i) for i in range(count)])
 
 
-def to_partition(v):
-    return lax.ppermute(v, "dom", [(i, i ^ 1) for i in range(lax.axis_size("dom"))])
-
-
 def shape(rows, width, dtype=BF16):
     return jax.ShapeDtypeStruct((rows, width), dtype)
+
+
+def call_hold(source, after):
+    return call(hold_kernel, [shape(*source.shape)], [source, after])[0]
 
 
 def padded(rows):
@@ -492,22 +490,20 @@
         ],
         flops=2 * (n_enc + n_proc) * d * 128,
     )
-    crossing, lat_sent = call(
-        functools.partial(
-            cross_kernel, ((n_in, BY_PART), (n_out, BY_PART), (k_in, ("groups",)), (k_out, ("groups",)))
-        ),
-        [shape((n_in + n_out + k_in + k_out) // 2, d), shape(lat.shape[0], width)],
+    lat_sent, node_half, proc_half = call(
+        functools.partial(cross_kernel, ((n_in, n_out), (k_in, k_out))),
+        [shape(lat.shape[0], width), shape((n_in + n_out) // 2, d), shape((k_in + k_out) // 2, d)],
         [next_w, lat_across],
     )
     lat_both = to_core(lat_sent)
-    next_across = to_chip(crossing)
+    node_came, proc_came = to_chip(node_half), to_chip(proc_half)
     next_beside = to_core(next_w)
 
     halo_rows = padded(got)
     half = mesh_rows // 2
-    keep, give, own_mesh = call(
+    keep, give, give_more, own_mesh = call(
         functools.partial(enc_kernel, plan, slots, grid_rows, mesh_rows, k_in),
-        [shape(half, d)] * 3,
+        [shape(half, d), shape(half // 2, d), shape(half // 2, d), shape(half, d)],
         [
             enc_emb, enc_edges, enc_edge_gain, lat, lat_across, lat_beside, lat_both,
             enc_edge_in, enc_edge_out, *edge_beside,
@@ -523,14 +519,9 @@
         flops=2 * n_enc * d * (3 * d + grid_rows + mesh_rows + halo_rows),
         smem=1,
     )
-    (chip_sum,) = call(add_kernel, [shape(half, d)], [keep, to_core(give)])
-    node_across, proc_across = call(
-        split_kernel,
-        [shape((n_in + n_out) // 2, d), shape((k_in + k_out) // 2, d)],
-        [next_across, chip_sum],
-    )
-    node_round = to_partition(node_across)
-    proc_round = to_group(proc_across)
+    (chip_sum,) = call(add_kernel, [shape(half, d)], [keep, to_core(give), to_core(give_more)])
+    node_across, proc_across = call_hold(node_came, chip_sum), call_hold(proc_came, chip_sum)
+    node_round, proc_round = to_group(node_across), to_group(proc_across)
     node_both = to_core(node_across)
     slots = mesh_send.shape[2]
     mid_half, last_w, *outgoing = call(
@@ -543,8 +534,9 @@
         scratch=[pltpu.VMEM((4 * (n_in + n_out), d), BF16)],
         flops=2 * half * d * 3 * d,
     )
-    (proc_pair,) = call(pair_kernel, [shape(k_in + k_out, d)], [proc_across, proc_round, mid_half])
+    mid_beside = to_core(mid_half)
     halos = [lax.ppermute(v, "dom", entry[0]) for v, entry in zip(outgoing, plan)]
+    (proc_pair,) = call(pair_kernel, [shape(k_in + k_out, d)], [proc_across, proc_round, halos[0]])
     (halo,) = call(concat_kernel, [shape(len(plan) * slots, d)], halos)
     halo_beside = to_core(halo)
     last_across, last_beside = to_chip(last_w), to_core(last_w)
@@ -553,7 +545,7 @@
         functools.partial(proc_first_kernel, k_in, n_in + n_out),
         [shape(d + 2 * mesh_rows, d), shape(early, d, F32), shape(d, d), shape(d, d)],
         [
-            proc_emb, mid_half, to_core(mid_half), proc_edges, next_w, next_beside, proc_pair, to_core(proc_pair),
+            proc_emb, mid_half, mid_beside, proc_edges, next_w, next_beside, proc_pair, to_core(proc_pair),
         ],
         scratch=[pltpu.VMEM((4 * (k_in + k_out), d), BF16), pltpu.VMEM((mesh_rows, d), BF16)],
         flops=2 * early * d * (d + 2 * mesh_rows),

time: 69 us -> 71.2 us (1.032)
  waiting for transfers between devices: 26.4 us -> 28.1 us
  starting transfers between devices: 21 us -> 21.8 us
    ppermute x2 -> x3, waiting for transfers between devices: 0.01 us -> 7.14 us  [to_group(): return lax.ppermute(v, 'groups', [(i, count - 1 - i) for i in range(count)])]
    ppermute x1 -> x0, waiting for transfers between devices: 4.79 us -> none  [to_partition(): lax.ppermute(v, 'dom', [(i, i ^ 1) for i in range(lax.axis_size('dom'))])]
    ppermute x6, waiting for transfers between devices: 4.13 us -> 6.27 us  [local(): lax.ppermute(v, 'dom', entry[0])]
    ppermute x6, starting transfers between devices: 10.9 us -> 9 us  [local(): lax.ppermute(v, 'dom', entry[0])]
    ppermute x6 -> x7, starting transfers between devices: 5.48 us -> 7.34 us  [to_chip(): return lax.ppermute(v, 'sub', [(i, i ^ 2) for i in range(4)])]
    ppermute x6 -> x7, waiting for transfers between devices: 15.3 us -> 13.6 us  [to_chip(): return lax.ppermute(v, 'sub', [(i, i ^ 2) for i in range(4)])]
    ppermute x16 -> x17, waiting for transfers between devices: 2.2 us -> 1.1 us  [to_core(): return lax.ppermute(v, 'sub', [(i, i ^ 1) for i in range(4)])]
    ppermute x2 -> x3, starting transfers between devices: 1.01 us -> 1.64 us  [to_group(): return lax.ppermute(v, 'groups', [(i, count - 1 - i) for i in range(count)])]
  transfers between devices with their start and end apart: 31 -> 33, of which waited for: 9 -> 11; matrix products, arithmetic and copies ran while one was open for 0% -> 0% of each run, Pallas kernels for 24% -> 23%
where the time goes in v7:
time: 71.2 us; the launch traced here: 71.1 us
  waiting for transfers between devices  28.1 us (39%)
  starting transfers between devices  21.8 us (31%)
  Pallas kernels  18.2 us (26%)
  between operations  1.77 us (2%)
  local copies, waits for them, and re-layouts  1.08 us (2%)
    pallas_call x16, Pallas kernels, call(): pl.pallas_call(body, out_shape=tuple(outs), in_specs=specs, out_specs=tup...  18.2 us
    ppermute x7, waiting for transfers between devices, to_chip(): return lax.ppermute(v, 'sub', [(i, i ^ 2) for i in range(4)])  13.6 us
    ppermute x6, starting transfers between devices, local(): lax.ppermute(v, 'dom', entry[0])  9 us
    ppermute x7, starting transfers between devices, to_chip(): return lax.ppermute(v, 'sub', [(i, i ^ 2) for i in range(4)])  7.34 us
    ppermute x3, waiting for transfers between devices, to_group(): return lax.ppermute(v, 'groups', [(i, count - 1 - i) for i in range(count)])  7.14 us
    ppermute x6, waiting for transfers between devices, local(): lax.ppermute(v, 'dom', entry[0])  6.27 us
    ppermute x17, starting transfers between devices, to_core(): return lax.ppermute(v, 'sub', [(i, i ^ 1) for i in range(4)])  3.86 us
    ppermute x3, starting transfers between devices, to_group(): return lax.ppermute(v, 'groups', [(i, count - 1 - i) for i in range(count)])  1.64 us
  transfers between devices with their start and end apart: 33, of which 11 were waited for; matrix products, arithmetic and copies ran while one was open for 0% of the time, Pallas kernels for 23%

profile of v7, /device:TPU:12, one launch (start us, length us, event | category | flops | bytes accessed | tf_op | source)
XLA Modules:
  0.0 71.1 jit_solution(8005820786583343755)
XLA Ops:
  0.1 0.8 %copy-done = bf16[512,128]{1,0:T(8,128)(2,1)S(1)} copy-done((bf16[512,128]{1,0:T(8,128)(2,1)S(1)}, bf16[512,128]{1,0:T(8,128)(2,1)}, u32[]{:S(2)}) %copy-start) | copy-done | bytes 131096
  0.9 0.2 copy-done.1
  1.1 0.0 copy-done.4
  1.1 0.3 shard_map.227
  1.4 1.6 %collective-permute-start.8 = (bf16[256,512]{1,0:T(8,128)(2,1)S(1)}, bf16[256,512]{1,0:T(8,128)(2,1)S(1)}, u32[]{:S(2)}, u32[]{:S(2)}) collective-permute-start(bf16[256,512]{1,0:T(8,128)(2,1)S(1)} %get-tuple-element.38), channel_id=1, source_target_pairs={{0,2},{1,3},{2,0},{3,1},{4,6},{5,7},{6,4},{7,5},{8,10},{9,11},{10,... | collective-permute-start | bytes 786440 | tf_op jit(solution)/shard_map/ppermute | solution.py:404
  3.0 0.4 collective-permute-start
  3.4 2.6 %collective-permute-start.1 = (bf16[64,128]{1,0:T(8,128)(2,1)S(1)}, bf16[64,128]{1,0:T(8,128)(2,1)S(1)}, u32[]{:S(2)}, u32[]{:S(2)}) collective-permute-start(bf16[64,128]{1,0:T(8,128)(2,1)S(1)} %get-tuple-element.33), channel_id=1, source_target_pairs={{0,8},{4,12},{8,0},{12,4},{1,9},{5,13},{9,1},{13,5},{2,10},{6,14},... | collective-permute-start | bytes 49160 | tf_op jit(solution)/shard_map/ppermute | solution.py:473
  6.0 2.3 %collective-permute-start.2 = (bf16[64,128]{1,0:T(8,128)(2,1)S(1)}, bf16[64,128]{1,0:T(8,128)(2,1)S(1)}, u32[]{:S(2)}, u32[]{:S(2)}) collective-permute-start(bf16[64,128]{1,0:T(8,128)(2,1)S(1)} %get-tuple-element.34), channel_id=1, source_target_pairs={{4,8},{8,4},{5,9},{9,5},{6,10},{10,6},{7,11},{11,7},{20,24},{24,20... | collective-permute-start | bytes 49160 | tf_op jit(solution)/shard_map/ppermute | solution.py:473
  8.4 0.0 collective-permute-done.1.refs_3_
  8.4 3.2 %collective-permute-done.2.refs_4_ = bf16[64,128]{1,0:T(8,128)(2,1)S(1)} collective-permute-done((bf16[64,128]{1,0:T(8,128)(2,1)S(1)}, bf16[64,128]{1,0:T(8,128)(2,1)S(1)}, u32[]{:S(2)}, u32[]{:S(2)}) %collective-permute-start.2) | collective-permute-done | bytes 16416 | tf_op jit(solution)/shard_map/ppermute | solution.py:473
  11.7 0.6 collective-permute-start.3
  12.3 0.0 collective-permute-done.8.across
  12.3 0.5 collective-permute-start.9
  12.8 0.0 collective-permute-start.4
  12.8 0.5 collective-permute-start.6
  13.3 0.0 collective-permute-start.7
  13.4 1.8 %shard_map.229 = (bf16[896,512]{1,0:T(8,128)(2,1)S(1)}, bf16[1024,512]{1,0:T(8,128)(2,1)S(1)}, bf16[2048,512]{1,0:T(8,128)(2,1)S(1)}) custom-call(bf16[256,512]{1,0:T(8,128)(2,1)S(1)} %copy-done.11, bf16[128,512]{1,0:T(8,128)(2,1)S(1)} %copy-done.12, bf16[384,512]{1,0:T(8,128)(2,1)S(1)} %copy-done.10, bf16[128,512]{1,0:T(8,128)(2,1)S(1)} %copy-done.13, ...), custom_call_target="tpu_custom_call" | custom-call | flops 402653184 | bytes 5357568 | tf_op jit(solution)/shard_map/pallas_call | solution.py:62
  15.1 3.9 %collective-permute-done.3.lat.l1 = bf16[1216,128]{1,0:T(8,128)(2,1)S(1)} collective-permute-done((bf16[1216,128]{1,0:T(8,128)(2,1)S(1)}, bf16[1216,128]{1,0:T(8,128)(2,1)S(1)}, u32[]{:S(2)}, u32[]{:S(2)}) %collective-permute-start.3) | collective-permute-done | bytes 311328 | tf_op jit(solution)/shard_map/ppermute | solution.py:404
  19.0 0.1 shard_map.230
  19.1 0.1 collective-permute-start.5
  19.1 0.5 collective-permute-start.10
  19.6 0.1 collective-permute-start.11
  19.7 0.4 collective-permute-start.15
  20.8 0.7 %collective-permute-start.16 = (bf16[192,512]{1,0:T(8,128)(2,1)S(1)}, bf16[192,512]{1,0:T(8,128)(2,1)S(1)}, u32[]{:S(2)}, u32[]{:S(2)}) collective-permute-start(bf16[192,512]{1,0:T(8,128)(2,1)S(1)} %get-tuple-element.43), channel_id=1, source_target_pairs={{0,2},{1,3},{2,0},{3,1},{4,6},{5,7},{6,4},{7,5},{8,10},{9,11},{10,... | collective-permute-start | bytes 589832 | tf_op jit(solution)/shard_map/ppermute | solution.py:404
  21.6 4.8 %shard_map.231 = (bf16[256,512]{1,0:T(8,128)(2,1)S(1)}, bf16[128,512]{1,0:T(8,128)(2,1)S(1)}, bf16[128,512]{1,0:T(8,128)(2,1)S(1)}, bf16[256,512]{1,0:T(8,128)(2,1)S(1)}) custom-call(bf16[1024,512]{1,0:T(8,128)(2,1)S(1)} %get-tuple-element.35.emb, s32[2,1024]{1,0:T(2,128)S(1)} %copy-done.19, f32[1,512]{1,0:T(1,128)S(1)} %bitcast.6, ...), custom_call_target="tpu_custom_call" | custom-call | flops 2952790016 | bytes 5187588 | tf_op jit(solution)/shard_map/pallas_call | solution.py:62
  26.4 0.0 copy-start.2
  26.4 0.0 copy-start.5
  26.4 0.0 copy-start.7
  26.4 0.0 copy-start.8
  26.4 0.1 collective-permute-start.12
  26.5 0.5 collective-permute-start.13
  27.0 1.4 %collective-permute-start.21 = (bf16[256,512]{1,0:T(8,128)(2,1)S(1)}, bf16[256,512]{1,0:T(8,128)(2,1)S(1)}, u32[]{:S(2)}, u32[]{:S(2)}) collective-permute-start(bf16[256,512]{1,0:T(8,128)(2,1)S(1)} %get-tuple-element.46), channel_id=1, source_target_pairs={{0,2},{1,3},{2,0},{3,1},{4,6},{5,7},{6,4},{7,5},{8,10},{9,11},{10,... | collective-permute-start | bytes 786440 | tf_op jit(solution)/shard_map/ppermute | solution.py:404
  28.3 0.1 shard_map.232.after.mine
  28.5 0.6 collective-permute-start.17
  29.0 1.0 %collective-permute-start.14 = (bf16[256,512]{1,0:T(8,128)(2,1)S(1)}, bf16[256,512]{1,0:T(8,128)(2,1)S(1)}, u32[]{:S(2)}, u32[]{:S(2)}) collective-permute-start(bf16[256,512]{1,0:T(8,128)(2,1)S(1)} %shard_map.232.after.mine), channel_id=1, source_target_pairs={{0,2},{1,3},{2,0},{3,1},{4,6},{5,7},{6,4},{7,5},{8,10},{9,11},{10,... | collective-permute-start | bytes 786440 | tf_op jit(solution)/shard_map/ppermute | solution.py:404
  30.0 5.3 %collective-permute-done.17.w3 = bf16[192,512]{1,0:T(8,128)(2,1)S(1)} collective-permute-done((bf16[192,512]{1,0:T(8,128)(2,1)S(1)}, bf16[192,512]{1,0:T(8,128)(2,1)S(1)}, u32[]{:S(2)}, u32[]{:S(2)}) %collective-permute-start.17) | collective-permute-done | bytes 196640 | tf_op jit(solution)/shard_map/ppermute | solution.py:413
  35.3 0.8 %collective-permute-done.21.source = bf16[256,512]{1,0:T(8,128)(2,1)S(1)} collective-permute-done((bf16[256,512]{1,0:T(8,128)(2,1)S(1)}, bf16[256,512]{1,0:T(8,128)(2,1)S(1)}, u32[]{:S(2)}, u32[]{:S(2)}) %collective-permute-start.21) | collective-permute-done | bytes 262176 | tf_op jit(solution)/shard_map/ppermute | solution.py:404
  36.2 0.6 collective-permute-start.22
  36.7 4.1 %collective-permute-done.14.theirs = bf16[256,512]{1,0:T(8,128)(2,1)S(1)} collective-permute-done((bf16[256,512]{1,0:T(8,128)(2,1)S(1)}, bf16[256,512]{1,0:T(8,128)(2,1)S(1)}, u32[]{:S(2)}, u32[]{:S(2)}) %collective-permute-start.14) | collective-permute-done | bytes 262176 | tf_op jit(solution)/shard_map/ppermute | solution.py:404
  40.9 0.0 copy-start.16
  40.9 1.2 %shard_map.234 = (bf16[256,512]{1,0:T(8,128)(2,1)S(1)}, bf16[384,512]{1,0:T(8,128)(2,1)S(1)}, bf16[32,512]{1,0:T(8,128)(2,1)S(1)}, bf16[32,512]{1,0:T(8,128)(2,1)S(1)}, bf16[32,512]{1,0:T(8,128)(2,1)S(1)}) custom-call(bf16[256,512]{1,0:T(8,128)(2,1)S(1)} %get-tuple-element.39.mesh, bf16[256,512]{1,0:T(8,128)(2,1)S(1)} %shard_map.232.after.mine, ...), custom_call_target="tpu_custom_call" | custom-call | flops 402653184 | bytes 4557312 | tf_op jit(solution)/shard_map/pallas_call | solution.py:62
  42.2 0.1 collective-permute-start.23
  42.2 1.9 %collective-permute-done.22.second = bf16[256,512]{1,0:T(8,128)(2,1)S(1)} collective-permute-done((bf16[256,512]{1,0:T(8,128)(2,1)S(1)}, bf16[256,512]{1,0:T(8,128)(2,1)S(1)}, u32[]{:S(2)}, u32[]{:S(2)}) %collective-permute-start.22) | collective-permute-done | bytes 262176 | tf_op jit(solution)/shard_map/ppermute | solution.py:413
  44.1 2.0 %collective-permute-done.23.after.refs_0_ = bf16[32,512]{1,0:T(8,128)(2,1)S(1)} collective-permute-done((bf16[32,512]{1,0:T(8,128)(2,1)S(1)}, bf16[32,512]{1,0:T(8,128)(2,1)S(1)}, u32[]{:S(2)}, u32[]{:S(2)}) %collective-permute-start.23) | collective-permute-done | bytes 32800 | tf_op jit(solution)/shard_map/ppermute | solution.py:538
  46.2 0.1 collective-permute-start.24
  46.3 0.5 collective-permute-start.20
  46.8 0.8 %collective-permute-start.25 = (bf16[32,512]{1,0:T(8,128)(2,1)S(1)}, bf16[32,512]{1,0:T(8,128)(2,1)S(1)}, u32[]{:S(2)}, u32[]{:S(2)}) collective-permute-start(bf16[32,512]{1,0:T(8,128)(2,1)S(1)} %get-tuple-element.52), channel_id=1, source_target_pairs={{0,8},{4,12},{8,0},{12,4},{1,9},{5,13},{9,1},{13,5},{2,10},{6,14},... | collective-permute-start | bytes 98312 | tf_op jit(solution)/shard_map/ppermute | solution.py:538
  47.6 2.7 %collective-permute-start.26 = (bf16[32,512]{1,0:T(8,128)(2,1)S(1)}, bf16[32,512]{1,0:T(8,128)(2,1)S(1)}, u32[]{:S(2)}, u32[]{:S(2)}) collective-permute-start(bf16[32,512]{1,0:T(8,128)(2,1)S(1)} %get-tuple-element.53), channel_id=1, source_target_pairs={{4,8},{8,4},{5,9},{9,5},{6,10},{10,6},{7,11},{11,7},{20,24},{24,20... | collective-permute-start | bytes 98312 | tf_op jit(solution)/shard_map/ppermute | solution.py:538
  51.0 1.4 %collective-permute-start.31 = (bf16[384,512]{1,0:T(8,128)(2,1)S(1)}, bf16[384,512]{1,0:T(8,128)(2,1)S(1)}, u32[]{:S(2)}, u32[]{:S(2)}) collective-permute-start(bf16[384,512]{1,0:T(8,128)(2,1)S(1)} %get-tuple-element.58.w0), channel_id=1, source_target_pairs={{0,2},{1,3},{2,0},{3,1},{4,6},{5,7},{6,4},{7,5},{8,10},{9,11},{10,... | collective-permute-start | bytes 1179656 | tf_op jit(solution)/shard_map/ppermute | solution.py:404
  52.4 1.0 %collective-permute-done.26.refs_2_ = bf16[32,512]{1,0:T(8,128)(2,1)S(1)} collective-permute-done((bf16[32,512]{1,0:T(8,128)(2,1)S(1)}, bf16[32,512]{1,0:T(8,128)(2,1)S(1)}, u32[]{:S(2)}, u32[]{:S(2)}) %collective-permute-start.26) | collective-permute-done | bytes 32800 | tf_op jit(solution)/shard_map/ppermute | solution.py:538
  53.4 0.1 collective-permute-start.27
  53.5 0.0 copy-start.21
  53.5 2.6 %shard_map.237 = (bf16[1536,512]{1,0:T(8,128)(2,1)S(1)}, f32[1024,512]{1,0:T(8,128)S(1)}, bf16[512,512]{1,0:T(8,128)(2,1)S(1)}, bf16[512,512]{1,0:T(8,128)(2,1)S(1)}) custom-call(bf16[2048,512]{1,0:T(8,128)(2,1)S(1)} %get-tuple-element.45.emb, bf16[256,512]{1,0:T(8,128)(2,1)S(1)} %get-tuple-element.44.mine.middle, ...), custom_call_target="tpu_custom_call" | custom-call | flops 1610612736 | bytes 10240000 | tf_op jit(solution)/shard_map/pallas_call | solution.py:62
  56.1 0.0 copy-start.9
  56.2 5.8 %shard_map.239 = (bf16[256,512]{1,0:T(8,128)(2,1)S(1)}, bf16[256,512]{1,0:T(8,128)(2,1)S(1)}) custom-call(bf16[2048,512]{1,0:T(8,128)(2,1)S(1)} %get-tuple-element.45.emb, s32[2,2048]{1,0:T(2,128)S(1)} %copy-done.16, f32[1,512]{1,0:T(1,128)S(1)} %bitcast.7, bf16[1536,512]{1,0:T(8,128)(2,1)S(1)} %get-tuple-element.48.table, ...), custom_call_target="tpu_custom_call" | custom-call | flops 3489660928 | bytes 7555076 | tf_op jit(solution)/shard_map/pallas_call | solution.py:62
  62.0 0.5 collective-permute-start.28
  62.5 0.1 collective-permute-start.30
  62.6 0.4 collective-permute-start.32
  63.1 0.6 collective-permute-done.28.theirs
  63.7 0.1 shard_map.240
  63.8 0.6 collective-permute-start.29
  64.4 0.4 collective-permute-done.32.w3
  64.8 4.8 %collective-permute-done.29.theirs = bf16[128,512]{1,0:T(8,128)(2,1)S(1)} collective-permute-done((bf16[128,512]{1,0:T(8,128)(2,1)S(1)}, bf16[128,512]{1,0:T(8,128)(2,1)S(1)}, u32[]{:S(2)}, u32[]{:S(2)}) %collective-permute-start.29) | collective-permute-done | bytes 131104 | tf_op jit(solution)/shard_map/ppermute | solution.py:404
  69.6 1.5 %shard_map.241 = bf16[128,512]{1,0:T(8,128)(2,1)} custom-call(bf16[256,512]{1,0:T(8,128)(2,1)S(1)} %get-tuple-element.44.mine.middle, bf16[128,512]{1,0:T(8,128)(2,1)S(1)} %get-tuple-element.56.mine, bf16[128,512]{1,0:T(8,128)(2,1)S(1)} %collective-permute-done.29.theirs, f32[1,512]{1,0:T(1,128)S(1)} %bitcast.5, bf16[384,512]{1,0:T(8,128)(2,1)S(1)} %get-tuple-element.58.w0, ...), custom_call_target="tpu_custom_call" | custom-call | flops 201326592 | bytes 2230272 | tf_op jit(solution)/shard_map/pallas_call | solution.py:62
  (62 shorter events, 0.2 us)
Async XLA Ops:
  0.0 0.9 %copy-start = (bf16[512,128]{1,0:T(8,128)(2,1)S(1)}, bf16[512,128]{1,0:T(8,128)(2,1)}, u32[]{:S(2)}) copy-start(bf16[512,128]{1,0:T(8,128)(2,1)} %refs_0_.1) | copy-start | bytes 393220
  0.0 0.9 %copy-start.6 = (s32[1,4,64]{2,1,0:T(4,128)S(1)}, s32[1,4,64]{2,1,0:T(4,128)}, u32[]{:S(2)}) copy-start(s32[1,4,64]{2,1,0:T(4,128)} %send.2) | copy-start | bytes 3076
  0.0 1.1 %copy-start.1 = (bf16[384,512]{1,0:T(8,128)(2,1)S(1)}, bf16[384,512]{1,0:T(8,128)(2,1)}, u32[]{:S(2)}) copy-start(bf16[384,512]{1,0:T(8,128)(2,1)} %o_in.1) | copy-start | bytes 1179652
  0.0 1.1 %copy-start.4 = (bf16[128,512]{1,0:T(8,128)(2,1)S(1)}, bf16[128,512]{1,0:T(8,128)(2,1)}, u32[]{:S(2)}) copy-start(bf16[128,512]{1,0:T(8,128)(2,1)} %o_out.1) | copy-start | bytes 393220
  0.0 11.6 %copy-start.3 = (bf16[512,128]{1,0:T(8,128)(2,1)S(1)}, bf16[512,128]{1,0:T(8,128)(2,1)}, u32[]{:S(2)}) copy-start(bf16[512,128]{1,0:T(8,128)(2,1)} %refs_1_.1) | copy-start | bytes 393220
  0.0 13.3 %copy-start.11 = (bf16[256,512]{1,0:T(8,128)(2,1)S(1)}, bf16[256,512]{1,0:T(8,128)(2,1)}, u32[]{:S(2)}) copy-start(bf16[256,512]{1,0:T(8,128)(2,1)} %e_in.1) | copy-start | bytes 786436
  0.0 13.3 %copy-start.12 = (bf16[128,512]{1,0:T(8,128)(2,1)S(1)}, bf16[128,512]{1,0:T(8,128)(2,1)}, u32[]{:S(2)}) copy-start(bf16[128,512]{1,0:T(8,128)(2,1)} %e_out.1) | copy-start | bytes 393220
  0.0 13.2 %copy-start.10 = (bf16[384,512]{1,0:T(8,128)(2,1)S(1)}, bf16[384,512]{1,0:T(8,128)(2,1)}, u32[]{:S(2)}) copy-start(bf16[384,512]{1,0:T(8,128)(2,1)} %p_in.1) | copy-start | bytes 1179652
  0.1 13.2 %copy-start.13 = (bf16[128,512]{1,0:T(8,128)(2,1)S(1)}, bf16[128,512]{1,0:T(8,128)(2,1)}, u32[]{:S(2)}) copy-start(bf16[128,512]{1,0:T(8,128)(2,1)} %p_out.1) | copy-start | bytes 393220
  0.1 13.2 %copy-start.15 = (f32[4,1024]{1,0:T(4,128)S(1)}, f32[4,1024]{1,0:T(4,128)}, u32[]{:S(2)}) copy-start(f32[4,1024]{1,0:T(4,128)} %egeom.1) | copy-start | bytes 49156
  0.1 13.2 %copy-start.17 = (f32[4,512]{1,0:T(4,128)S(1)}, f32[4,512]{1,0:T(4,128)}, u32[]{:S(2)}) copy-start(f32[4,512]{1,0:T(4,128)} %egeo.1) | copy-start | bytes 24580
  0.1 13.2 %copy-start.14 = (f32[4,2048]{1,0:T(4,128)S(1)}, f32[4,2048]{1,0:T(4,128)}, u32[]{:S(2)}) copy-start(f32[4,2048]{1,0:T(4,128)} %pgeom.1) | copy-start | bytes 98308
  0.1 13.2 %copy-start.18 = (f32[4,512]{1,0:T(4,128)S(1)}, f32[4,512]{1,0:T(4,128)}, u32[]{:S(2)}) copy-start(f32[4,512]{1,0:T(4,128)} %pgeo.1) | copy-start | bytes 24580
  1.1 20.5 %copy-start.19 = (s32[2,1024]{1,0:T(2,128)S(1)}, s32[2,1024]{1,0:T(2,128)}, u32[]{:S(2)}) copy-start(s32[2,1024]{1,0:T(2,128)} %edges.3) | copy-start | bytes 24580
  1.1 20.5 %copy-start.20 = (f32[512]{0:T(512)S(1)}, f32[512]{0:T(512)}, u32[]{:S(2)}) copy-start(f32[512]{0:T(512)} %param.44) | copy-start | bytes 6148
  1.4 10.8 %collective-permute-start.8 = (bf16[256,512]{1,0:T(8,128)(2,1)S(1)}, bf16[256,512]{1,0:T(8,128)(2,1)S(1)}, u32[]{:S(2)}, u32[]{:S(2)}) collective-permute-start(bf16[256,512]{1,0:T(8,128)(2,1)S(1)} %get-tuple-element.38), channel_id=1, source_target_pairs={{0,2},{1,3},{2,0},{3,1},{4,6},{5,7},{6,4},{7,5},{8,10},{9,11},{10,... | collective-permute-start | bytes 786440 | tf_op jit(solution)/shard_map/ppermute | solution.py:404
  3.0 5.4 %collective-permute-start = (bf16[64,128]{1,0:T(8,128)(2,1)S(1)}, bf16[64,128]{1,0:T(8,128)(2,1)S(1)}, u32[]{:S(2)}, u32[]{:S(2)}) collective-permute-start(bf16[64,128]{1,0:T(8,128)(2,1)S(1)} %get-tuple-element.32), channel_id=1, source_target_pairs={{0,4},{4,0},{8,12},{12,8},{1,5},{5,1},{9,13},{13,9},{2,6},{6,2},{1... | collective-permute-start | bytes 49160 | tf_op jit(solution)/shard_map/ppermute | solution.py:473
  3.4 5.0 %collective-permute-start.1 = (bf16[64,128]{1,0:T(8,128)(2,1)S(1)}, bf16[64,128]{1,0:T(8,128)(2,1)S(1)}, u32[]{:S(2)}, u32[]{:S(2)}) collective-permute-start(bf16[64,128]{1,0:T(8,128)(2,1)S(1)} %get-tuple-element.33), channel_id=1, source_target_pairs={{0,8},{4,12},{8,0},{12,4},{1,9},{5,13},{9,1},{13,5},{2,10},{6,14},... | collective-permute-start | bytes 49160 | tf_op jit(solution)/shard_map/ppermute | solution.py:473
  6.0 5.6 %collective-permute-start.2 = (bf16[64,128]{1,0:T(8,128)(2,1)S(1)}, bf16[64,128]{1,0:T(8,128)(2,1)S(1)}, u32[]{:S(2)}, u32[]{:S(2)}) collective-permute-start(bf16[64,128]{1,0:T(8,128)(2,1)S(1)} %get-tuple-element.34), channel_id=1, source_target_pairs={{4,8},{8,4},{5,9},{9,5},{6,10},{10,6},{7,11},{11,7},{20,24},{24,20... | collective-permute-start | bytes 49160 | tf_op jit(solution)/shard_map/ppermute | solution.py:473
  11.7 7.3 %collective-permute-start.3 = (bf16[1216,128]{1,0:T(8,128)(2,1)S(1)}, bf16[1216,128]{1,0:T(8,128)(2,1)S(1)}, u32[]{:S(2)}, u32[]{:S(2)}) collective-permute-start(bf16[1216,128]{1,0:T(8,128)(2,1)S(1)} %shard_map.228.after.l0), channel_id=1, source_target_pairs={{0,2},{1,3},{2,0},{3,1},{4,6},{5,7},{6,4},{7,5},{8,10},{9,11},{10,... | collective-permute-start | bytes 933896 | tf_op jit(solution)/shard_map/ppermute | solution.py:404
  12.3 7.4 %collective-permute-start.9 = (bf16[256,512]{1,0:T(8,128)(2,1)S(1)}, bf16[256,512]{1,0:T(8,128)(2,1)S(1)}, u32[]{:S(2)}, u32[]{:S(2)}) collective-permute-start(bf16[256,512]{1,0:T(8,128)(2,1)S(1)} %collective-permute-done.8.across), channel_id=1, source_target_pairs={{0,16},{16,0},{1,17},{17,1},{2,18},{18,2},{3,19},{19,3},{4,20},{20... | collective-permute-start | bytes 786440 | tf_op jit(solution)/shard_map/ppermute | solution.py:413
  12.8 7.0 %collective-permute-start.4 = (bf16[1216,128]{1,0:T(8,128)(2,1)S(1)}, bf16[1216,128]{1,0:T(8,128)(2,1)S(1)}, u32[]{:S(2)}, u32[]{:S(2)}) collective-permute-start(bf16[1216,128]{1,0:T(8,128)(2,1)S(1)} %shard_map.228.after.l0), channel_id=1, source_target_pairs={{0,1},{1,0},{2,3},{3,2},{4,5},{5,4},{6,7},{7,6},{8,9},{9,8},{10,11... | collective-permute-start | bytes 933896 | tf_op jit(solution)/shard_map/ppermute | solution.py:408
  12.8 8.0 %collective-permute-start.6 = (bf16[384,512]{1,0:T(8,128)(2,1)S(1)}, bf16[384,512]{1,0:T(8,128)(2,1)S(1)}, u32[]{:S(2)}, u32[]{:S(2)}) collective-permute-start(bf16[384,512]{1,0:T(8,128)(2,1)S(1)} %copy-done.1), channel_id=1, source_target_pairs={{0,1},{1,0},{2,3},{3,2},{4,5},{5,4},{6,7},{7,6},{8,9},{9,8},{10,11... | collective-permute-start | bytes 1179656 | tf_op jit(solution)/shard_map/ppermute | solution.py:408
  13.3 5.9 %collective-permute-start.7 = (bf16[128,512]{1,0:T(8,128)(2,1)S(1)}, bf16[128,512]{1,0:T(8,128)(2,1)S(1)}, u32[]{:S(2)}, u32[]{:S(2)}) collective-permute-start(bf16[128,512]{1,0:T(8,128)(2,1)S(1)} %copy-done.4), channel_id=1, source_target_pairs={{0,1},{1,0},{2,3},{3,2},{4,5},{5,4},{6,7},{7,6},{8,9},{9,8},{10,11... | collective-permute-start | bytes 393224 | tf_op jit(solution)/shard_map/ppermute | solution.py:408
  19.1 2.5 %collective-permute-start.5 = (bf16[1216,128]{1,0:T(8,128)(2,1)S(1)}, bf16[1216,128]{1,0:T(8,128)(2,1)S(1)}, u32[]{:S(2)}, u32[]{:S(2)}) collective-permute-start(bf16[1216,128]{1,0:T(8,128)(2,1)S(1)} %get-tuple-element.37), channel_id=1, source_target_pairs={{0,1},{1,0},{2,3},{3,2},{4,5},{5,4},{6,7},{7,6},{8,9},{9,8},{10,11... | collective-permute-start | bytes 933896 | tf_op jit(solution)/shard_map/ppermute | solution.py:408
  19.1 2.4 %collective-permute-start.10 = (bf16[256,512]{1,0:T(8,128)(2,1)S(1)}, bf16[256,512]{1,0:T(8,128)(2,1)S(1)}, u32[]{:S(2)}, u32[]{:S(2)}) collective-permute-start(bf16[256,512]{1,0:T(8,128)(2,1)S(1)} %collective-permute-done.8.across), channel_id=1, source_target_pairs={{0,1},{1,0},{2,3},{3,2},{4,5},{5,4},{6,7},{7,6},{8,9},{9,8},{10,11... | collective-permute-start | bytes 786440 | tf_op jit(solution)/shard_map/ppermute | solution.py:408
  19.6 1.9 %collective-permute-start.11 = (bf16[256,512]{1,0:T(8,128)(2,1)S(1)}, bf16[256,512]{1,0:T(8,128)(2,1)S(1)}, u32[]{:S(2)}, u32[]{:S(2)}) collective-permute-start(bf16[256,512]{1,0:T(8,128)(2,1)S(1)} %collective-permute-done.9.round_), channel_id=1, source_target_pairs={{0,1},{1,0},{2,3},{3,2},{4,5},{5,4},{6,7},{7,6},{8,9},{9,8},{10,11... | collective-permute-start | bytes 786440 | tf_op jit(solution)/shard_map/ppermute | solution.py:408
  19.7 17.0 %collective-permute-start.15 = (bf16[896,512]{1,0:T(8,128)(2,1)S(1)}, bf16[896,512]{1,0:T(8,128)(2,1)S(1)}, u32[]{:S(2)}, u32[]{:S(2)}) collective-permute-start(bf16[896,512]{1,0:T(8,128)(2,1)S(1)} %get-tuple-element.36.weights.w0), channel_id=1, source_target_pairs={{0,1},{1,0},{2,3},{3,2},{4,5},{5,4},{6,7},{7,6},{8,9},{9,8},{10,11... | collective-permute-start | bytes 2752520 | tf_op jit(solution)/shard_map/ppermute | solution.py:408
  20.8 7.6 %collective-permute-start.16 = (bf16[192,512]{1,0:T(8,128)(2,1)S(1)}, bf16[192,512]{1,0:T(8,128)(2,1)S(1)}, u32[]{:S(2)}, u32[]{:S(2)}) collective-permute-start(bf16[192,512]{1,0:T(8,128)(2,1)S(1)} %get-tuple-element.43), channel_id=1, source_target_pairs={{0,2},{1,3},{2,0},{3,1},{4,6},{5,7},{6,4},{7,5},{8,10},{9,11},{10,... | collective-permute-start | bytes 589832 | tf_op jit(solution)/shard_map/ppermute | solution.py:404
  26.4 14.5 %copy-start.2 = (bf16[256,512]{1,0:T(8,128)(2,1)S(1)}, bf16[256,512]{1,0:T(8,128)(2,1)}, u32[]{:S(2)}) copy-start(bf16[256,512]{1,0:T(8,128)(2,1)} %n_in.1) | copy-start | bytes 786436
  26.4 14.5 %copy-start.5 = (bf16[128,512]{1,0:T(8,128)(2,1)S(1)}, bf16[128,512]{1,0:T(8,128)(2,1)}, u32[]{:S(2)}) copy-start(bf16[128,512]{1,0:T(8,128)(2,1)} %n_out.1) | copy-start | bytes 393220
  26.4 14.5 %copy-start.7 = (f32[512]{0:T(512)S(1)}, f32[512]{0:T(512)}, u32[]{:S(2)}) copy-start(f32[512]{0:T(512)} %param.45) | copy-start | bytes 6148
  26.4 14.5 %copy-start.8 = (s32[1,4,32]{2,1,0:T(4,128)S(1)}, s32[1,4,32]{2,1,0:T(4,128)}, u32[]{:S(2)}) copy-start(s32[1,4,32]{2,1,0:T(4,128)} %send.3) | copy-start | bytes 1540
  26.4 1.9 %collective-permute-start.12 = (bf16[128,512]{1,0:T(8,128)(2,1)S(1)}, bf16[128,512]{1,0:T(8,128)(2,1)S(1)}, u32[]{:S(2)}, u32[]{:S(2)}) collective-permute-start(bf16[128,512]{1,0:T(8,128)(2,1)S(1)} %get-tuple-element.41), channel_id=1, source_target_pairs={{0,1},{1,0},{2,3},{3,2},{4,5},{5,4},{6,7},{7,6},{8,9},{9,8},{10,11... | collective-permute-start | bytes 393224 | tf_op jit(solution)/shard_map/ppermute | solution.py:408
  26.5 1.9 %collective-permute-start.13 = (bf16[128,512]{1,0:T(8,128)(2,1)S(1)}, bf16[128,512]{1,0:T(8,128)(2,1)S(1)}, u32[]{:S(2)}, u32[]{:S(2)}) collective-permute-start(bf16[128,512]{1,0:T(8,128)(2,1)S(1)} %get-tuple-element.42), channel_id=1, source_target_pairs={{0,1},{1,0},{2,3},{3,2},{4,5},{5,4},{6,7},{7,6},{8,9},{9,8},{10,11... | collective-permute-start | bytes 393224 | tf_op jit(solution)/shard_map/ppermute | solution.py:408
  27.0 9.2 %collective-permute-start.21 = (bf16[256,512]{1,0:T(8,128)(2,1)S(1)}, bf16[256,512]{1,0:T(8,128)(2,1)S(1)}, u32[]{:S(2)}, u32[]{:S(2)}) collective-permute-start(bf16[256,512]{1,0:T(8,128)(2,1)S(1)} %get-tuple-element.46), channel_id=1, source_target_pairs={{0,2},{1,3},{2,0},{3,1},{4,6},{5,7},{6,4},{7,5},{8,10},{9,11},{10,... | collective-permute-start | bytes 786440 | tf_op jit(solution)/shard_map/ppermute | solution.py:404
  28.5 6.8 %collective-permute-start.17 = (bf16[192,512]{1,0:T(8,128)(2,1)S(1)}, bf16[192,512]{1,0:T(8,128)(2,1)S(1)}, u32[]{:S(2)}, u32[]{:S(2)}) collective-permute-start(bf16[192,512]{1,0:T(8,128)(2,1)S(1)} %shard_map.233.w2), channel_id=1, source_target_pairs={{0,16},{16,0},{1,17},{17,1},{2,18},{18,2},{3,19},{19,3},{4,20},{20... | collective-permute-start | bytes 589832 | tf_op jit(solution)/shard_map/ppermute | solution.py:413
  29.0 11.9 %collective-permute-start.14 = (bf16[256,512]{1,0:T(8,128)(2,1)S(1)}, bf16[256,512]{1,0:T(8,128)(2,1)S(1)}, u32[]{:S(2)}, u32[]{:S(2)}) collective-permute-start(bf16[256,512]{1,0:T(8,128)(2,1)S(1)} %shard_map.232.after.mine), channel_id=1, source_target_pairs={{0,2},{1,3},{2,0},{3,1},{4,6},{5,7},{6,4},{7,5},{8,10},{9,11},{10,... | collective-permute-start | bytes 786440 | tf_op jit(solution)/shard_map/ppermute | solution.py:404
  30.0 6.7 %collective-permute-start.18 = (bf16[192,512]{1,0:T(8,128)(2,1)S(1)}, bf16[192,512]{1,0:T(8,128)(2,1)S(1)}, u32[]{:S(2)}, u32[]{:S(2)}) collective-permute-start(bf16[192,512]{1,0:T(8,128)(2,1)S(1)} %shard_map.233.w2), channel_id=1, source_target_pairs={{0,1},{1,0},{2,3},{3,2},{4,5},{5,4},{6,7},{7,6},{8,9},{9,8},{10,11... | collective-permute-start | bytes 589832 | tf_op jit(solution)/shard_map/ppermute | solution.py:408
  35.3 5.6 %collective-permute-start.19 = (bf16[192,512]{1,0:T(8,128)(2,1)S(1)}, bf16[192,512]{1,0:T(8,128)(2,1)S(1)}, u32[]{:S(2)}, u32[]{:S(2)}) collective-permute-start(bf16[192,512]{1,0:T(8,128)(2,1)S(1)} %collective-permute-done.17.w3), channel_id=1, source_target_pairs={{0,1},{1,0},{2,3},{3,2},{4,5},{5,4},{6,7},{7,6},{8,9},{9,8},{10,11... | collective-permute-start | bytes 589832 | tf_op jit(solution)/shard_map/ppermute | solution.py:408
  36.2 8.0 %collective-permute-start.22 = (bf16[256,512]{1,0:T(8,128)(2,1)S(1)}, bf16[256,512]{1,0:T(8,128)(2,1)S(1)}, u32[]{:S(2)}, u32[]{:S(2)}) collective-permute-start(bf16[256,512]{1,0:T(8,128)(2,1)S(1)} %shard_map.235.first), channel_id=1, source_target_pairs={{0,16},{16,0},{1,17},{17,1},{2,18},{18,2},{3,19},{19,3},{4,20},{20... | collective-permute-start | bytes 786440 | tf_op jit(solution)/shard_map/ppermute | solution.py:413
  40.9 12.6 %copy-start.16 = (s32[2,2048]{1,0:T(2,128)S(1)}, s32[2,2048]{1,0:T(2,128)}, u32[]{:S(2)}) copy-start(s32[2,2048]{1,0:T(2,128)} %edges.5) | copy-start | bytes 49156
  42.2 4.0 %collective-permute-start.23 = (bf16[32,512]{1,0:T(8,128)(2,1)S(1)}, bf16[32,512]{1,0:T(8,128)(2,1)S(1)}, u32[]{:S(2)}, u32[]{:S(2)}) collective-permute-start(bf16[32,512]{1,0:T(8,128)(2,1)S(1)} %get-tuple-element.47), channel_id=1, source_target_pairs={{0,4},{4,0},{8,12},{12,8},{1,5},{5,1},{9,13},{13,9},{2,6},{6,2},{1... | collective-permute-start | bytes 98312 | tf_op jit(solution)/shard_map/ppermute | solution.py:538
  46.2 7.3 %collective-permute-start.24 = (bf16[512,512]{1,0:T(8,128)(2,1)S(1)}, bf16[512,512]{1,0:T(8,128)(2,1)S(1)}, u32[]{:S(2)}, u32[]{:S(2)}) collective-permute-start(bf16[512,512]{1,0:T(8,128)(2,1)S(1)} %shard_map.236.pair), channel_id=1, source_target_pairs={{0,1},{1,0},{2,3},{3,2},{4,5},{5,4},{6,7},{7,6},{8,9},{9,8},{10,11... | collective-permute-start | bytes 1572872 | tf_op jit(solution)/shard_map/ppermute | solution.py:408
  46.3 7.2 %collective-permute-start.20 = (bf16[256,512]{1,0:T(8,128)(2,1)S(1)}, bf16[256,512]{1,0:T(8,128)(2,1)S(1)}, u32[]{:S(2)}, u32[]{:S(2)}) collective-permute-start(bf16[256,512]{1,0:T(8,128)(2,1)S(1)} %get-tuple-element.44.mine.middle), channel_id=1, source_target_pairs={{0,1},{1,0},{2,3},{3,2},{4,5},{5,4},{6,7},{7,6},{8,9},{9,8},{10,11... | collective-permute-start | bytes 786440 | tf_op jit(solution)/shard_map/ppermute | solution.py:408
  46.8 5.6 %collective-permute-start.25 = (bf16[32,512]{1,0:T(8,128)(2,1)S(1)}, bf16[32,512]{1,0:T(8,128)(2,1)S(1)}, u32[]{:S(2)}, u32[]{:S(2)}) collective-permute-start(bf16[32,512]{1,0:T(8,128)(2,1)S(1)} %get-tuple-element.52), channel_id=1, source_target_pairs={{0,8},{4,12},{8,0},{12,4},{1,9},{5,13},{9,1},{13,5},{2,10},{6,14},... | collective-permute-start | bytes 98312 | tf_op jit(solution)/shard_map/ppermute | solution.py:538
  47.6 5.8 %collective-permute-start.26 = (bf16[32,512]{1,0:T(8,128)(2,1)S(1)}, bf16[32,512]{1,0:T(8,128)(2,1)S(1)}, u32[]{:S(2)}, u32[]{:S(2)}) collective-permute-start(bf16[32,512]{1,0:T(8,128)(2,1)S(1)} %get-tuple-element.53), channel_id=1, source_target_pairs={{4,8},{8,4},{5,9},{9,5},{6,10},{10,6},{7,11},{11,7},{20,24},{24,20... | collective-permute-start | bytes 98312 | tf_op jit(solution)/shard_map/ppermute | solution.py:538
  51.0 11.7 %collective-permute-start.31 = (bf16[384,512]{1,0:T(8,128)(2,1)S(1)}, bf16[384,512]{1,0:T(8,128)(2,1)S(1)}, u32[]{:S(2)}, u32[]{:S(2)}) collective-permute-start(bf16[384,512]{1,0:T(8,128)(2,1)S(1)} %get-tuple-element.58.w0), channel_id=1, source_target_pairs={{0,2},{1,3},{2,0},{3,1},{4,6},{5,7},{6,4},{7,5},{8,10},{9,11},{10,... | collective-permute-start | bytes 1179656 | tf_op jit(solution)/shard_map/ppermute | solution.py:404
  53.4 2.7 %collective-permute-start.27 = (bf16[96,512]{1,0:T(8,128)(2,1)S(1)}, bf16[96,512]{1,0:T(8,128)(2,1)S(1)}, u32[]{:S(2)}, u32[]{:S(2)}) collective-permute-start(bf16[96,512]{1,0:T(8,128)(2,1)S(1)} %shard_map.238.halo), channel_id=1, source_target_pairs={{0,1},{1,0},{2,3},{3,2},{4,5},{5,4},{6,7},{7,6},{8,9},{9,8},{10,11... | collective-permute-start | bytes 294920 | tf_op jit(solution)/shard_map/ppermute | solution.py:408
  53.5 2.6 %copy-start.21 = (f32[512]{0:T(512)S(1)}, f32[512]{0:T(512)}, u32[]{:S(2)}) copy-start(f32[512]{0:T(512)} %param.46) | copy-start | bytes 6148
  56.1 13.5 %copy-start.9 = (f32[512]{0:T(512)S(1)}, f32[512]{0:T(512)}, u32[]{:S(2)}) copy-start(f32[512]{0:T(512)} %param.47) | copy-start | bytes 6148
  62.0 1.7 %collective-permute-start.28 = (bf16[256,512]{1,0:T(8,128)(2,1)S(1)}, bf16[256,512]{1,0:T(8,128)(2,1)S(1)}, u32[]{:S(2)}, u32[]{:S(2)}) collective-permute-start(bf16[256,512]{1,0:T(8,128)(2,1)S(1)} %get-tuple-element.55), channel_id=1, source_target_pairs={{0,1},{1,0},{2,3},{3,2},{4,5},{5,4},{6,7},{7,6},{8,9},{9,8},{10,11... | collective-permute-start | bytes 786440 | tf_op jit(solution)/shard_map/ppermute | solution.py:408
  62.5 1.9 %collective-permute-start.30 = (bf16[384,512]{1,0:T(8,128)(2,1)S(1)}, bf16[384,512]{1,0:T(8,128)(2,1)S(1)}, u32[]{:S(2)}, u32[]{:S(2)}) collective-permute-start(bf16[384,512]{1,0:T(8,128)(2,1)S(1)} %get-tuple-element.58.w0), channel_id=1, source_target_pairs={{0,1},{1,0},{2,3},{3,2},{4,5},{5,4},{6,7},{7,6},{8,9},{9,8},{10,11... | collective-permute-start | bytes 1179656 | tf_op jit(solution)/shard_map/ppermute | solution.py:408
  62.6 2.2 %collective-permute-start.32 = (bf16[384,512]{1,0:T(8,128)(2,1)S(1)}, bf16[384,512]{1,0:T(8,128)(2,1)S(1)}, u32[]{:S(2)}, u32[]{:S(2)}) collective-permute-start(bf16[384,512]{1,0:T(8,128)(2,1)S(1)} %collective-permute-done.31.w2), channel_id=1, source_target_pairs={{0,1},{1,0},{2,3},{3,2},{4,5},{5,4},{6,7},{7,6},{8,9},{9,8},{10,11... | collective-permute-start | bytes 1179656 | tf_op jit(solution)/shard_map/ppermute | solution.py:408
  63.8 5.8 %collective-permute-start.29 = (bf16[128,512]{1,0:T(8,128)(2,1)S(1)}, bf16[128,512]{1,0:T(8,128)(2,1)S(1)}, u32[]{:S(2)}, u32[]{:S(2)}) collective-permute-start(bf16[128,512]{1,0:T(8,128)(2,1)S(1)} %get-tuple-element.57), channel_id=1, source_target_pairs={{0,2},{1,3},{2,0},{3,1},{4,6},{5,7},{6,4},{7,5},{8,10},{9,11},{10,... | collective-permute-start | bytes 393224 | tf_op jit(solution)/shard_map/ppermute | solution.py:404

commit v8 on v7

--- a/solution.py
+++ b/solution.py
@@ -158,8 +158,11 @@
             first, place = first + rows, place + half
 
 
-def pair_kernel(first, second, after, out):
-    stack_into(out, (first, second))
+def relay_kernel(across, round_, w_in, w_out, *refs):
+    *parts, out, pair, packed = refs
+    stack_into(out, parts)
+    stack_into(pair, (across, round_))
+    stack_into(packed, (w_in, w_out))
 
 
 def hold_kernel(source, after, out):
@@ -305,7 +308,7 @@
 
 
 def node_kernel(
-    plan, k_in, k_out, mesh, mine, theirs, gain, n_in, n_out, w0, w1, w2, w3, w4, w5, send, out, packed, *rest
+    plan, k_in, k_out, mesh, mine, theirs, gain, w0, w1, w2, w3, w4, w5, send, out, *rest
 ):
     outs, stack = rest[:-1], rest[-1]
     put_shard(stack, w0, 0, 0)
@@ -322,7 +325,6 @@
     place = lax.broadcasted_iota(jnp.int32, (fresh.shape[0], 1), 0)
     rows = place + core * half + jnp.where(place < half, 0, half)
     pick_lists(plan, fresh, send, outs, rows.astype(I16))
-    stack_into(packed, (n_in, n_out))
 
 
 def proc_first_kernel(
@@ -524,11 +526,11 @@
     node_round, proc_round = to_group(node_across), to_group(proc_across)
     node_both = to_core(node_across)
     slots = mesh_send.shape[2]
-    mid_half, last_w, *outgoing = call(
+    mid_half, *outgoing = call(
         functools.partial(node_kernel, plan, n_in, n_out),
-        [shape(half, d), shape(n_in + n_out, d)] + [shape(slots, d)] * len(plan),
+        [shape(half, d)] + [shape(slots, d)] * len(plan),
         [
-            own_mesh, chip_sum, to_chip(chip_sum), enc_node_gain, proc_node_in, proc_node_out,
+            own_mesh, chip_sum, to_chip(chip_sum), enc_node_gain,
             next_w, next_beside, node_across, node_round, node_both, to_core(node_round), mesh_send,
         ],
         scratch=[pltpu.VMEM((4 * (n_in + n_out), d), BF16)],
@@ -536,8 +538,11 @@
     )
     mid_beside = to_core(mid_half)
     halos = [lax.ppermute(v, "dom", entry[0]) for v, entry in zip(outgoing, plan)]
-    (proc_pair,) = call(pair_kernel, [shape(k_in + k_out, d)], [proc_across, proc_round, halos[0]])
-    (halo,) = call(concat_kernel, [shape(len(plan) * slots, d)], halos)
+    halo, proc_pair, last_w = call(
+        relay_kernel,
+        [shape(len(plan) * slots, d), shape(k_in + k_out, d), shape(n_in + n_out, d)],
+        [proc_across, proc_round, proc_node_in, proc_node_out, *halos],
+    )
     halo_beside = to_core(halo)
     last_across, last_beside = to_chip(last_w), to_core(last_w)
     early = n_proc // 2

time: 71.2 us -> 70.8 us (level)
  waiting for transfers between devices: 28.1 us -> 25.1 us
  starting transfers between devices: 21.8 us -> 24.2 us
    ppermute x6, starting transfers between devices: 9 us -> 11 us  [local(): lax.ppermute(v, 'dom', entry[0])]
    ppermute x3, waiting for transfers between devices: 7.14 us -> 5.27 us  [to_group(): return lax.ppermute(v, 'groups', [(i, count - 1 - i) for i in range(count)])]
    ppermute x17, waiting for transfers between devices: 1.1 us -> 0.25 us  [to_core(): return lax.ppermute(v, 'sub', [(i, i ^ 1) for i in range(4)])]
    ppermute x6, waiting for transfers between devices: 6.27 us -> 5.44 us  [local(): lax.ppermute(v, 'dom', entry[0])]
    ppermute x7, starting transfers between devices: 7.34 us -> 8.11 us  [to_chip(): return lax.ppermute(v, 'sub', [(i, i ^ 2) for i in range(4)])]
    pallas_call x16 -> x15, Pallas kernels: 18.2 us -> 18.3 us  [call(): pl.pallas_call(body, out_shape=tuple(outs), in_specs=specs, out_specs=tup...]
  transfers between devices with their start and end apart: 33 -> 33, of which waited for: 11 -> 9; matrix products, arithmetic and copies ran while one was open for 0% -> 0% of each run, Pallas kernels for 23% -> 23%
where the time goes in v8:
time: 70.8 us; the launch traced here: 70.4 us
  waiting for transfers between devices  25.1 us (35%)
  starting transfers between devices  24.2 us (34%)
  Pallas kernels  18.3 us (26%)
  between operations  1.75 us (2%)
  local copies, waits for them, and re-layouts  1.08 us (2%)
    pallas_call x15, Pallas kernels, call(): pl.pallas_call(body, out_shape=tuple(outs), in_specs=specs, out_specs=tup...  18.3 us
    ppermute x7, waiting for transfers between devices, to_chip(): return lax.ppermute(v, 'sub', [(i, i ^ 2) for i in range(4)])  14.1 us
    ppermute x6, starting transfers between devices, local(): lax.ppermute(v, 'dom', entry[0])  11 us
    ppermute x7, starting transfers between devices, to_chip(): return lax.ppermute(v, 'sub', [(i, i ^ 2) for i in range(4)])  8.11 us
    ppermute x6, waiting for transfers between devices, local(): lax.ppermute(v, 'dom', entry[0])  5.44 us
    ppermute x3, waiting for transfers between devices, to_group(): return lax.ppermute(v, 'groups', [(i, count - 1 - i) for i in range(count)])  5.27 us
    ppermute x17, starting transfers between devices, to_core(): return lax.ppermute(v, 'sub', [(i, i ^ 1) for i in range(4)])  3.45 us
    ppermute x3, starting transfers between devices, to_group(): return lax.ppermute(v, 'groups', [(i, count - 1 - i) for i in range(count)])  1.64 us
  transfers between devices with their start and end apart: 33, of which 9 were waited for; matrix products, arithmetic and copies ran while one was open for 0% of the time, Pallas kernels for 23%

profile of v8, /device:TPU:12, one launch (start us, length us, event | category | flops | bytes accessed | tf_op | source)
XLA Modules:
  0.0 70.4 jit_solution(822830255800467999)
XLA Ops:
  0.1 0.8 %copy-done = bf16[512,128]{1,0:T(8,128)(2,1)S(1)} copy-done((bf16[512,128]{1,0:T(8,128)(2,1)S(1)}, bf16[512,128]{1,0:T(8,128)(2,1)}, u32[]{:S(2)}) %copy-start) | copy-done | bytes 131096
  0.9 0.2 copy-done.1
  1.1 0.0 copy-done.4
  1.1 0.3 shard_map.227
  1.4 1.6 %collective-permute-start.8 = (bf16[256,512]{1,0:T(8,128)(2,1)S(1)}, bf16[256,512]{1,0:T(8,128)(2,1)S(1)}, u32[]{:S(2)}, u32[]{:S(2)}) collective-permute-start(bf16[256,512]{1,0:T(8,128)(2,1)S(1)} %get-tuple-element.40), channel_id=1, source_target_pairs={{0,2},{1,3},{2,0},{3,1},{4,6},{5,7},{6,4},{7,5},{8,10},{9,11},{10,... | collective-permute-start | bytes 786440 | tf_op jit(solution)/shard_map/ppermute | solution.py:406
  3.0 0.4 collective-permute-start
  3.4 2.6 %collective-permute-start.1 = (bf16[64,128]{1,0:T(8,128)(2,1)S(1)}, bf16[64,128]{1,0:T(8,128)(2,1)S(1)}, u32[]{:S(2)}, u32[]{:S(2)}) collective-permute-start(bf16[64,128]{1,0:T(8,128)(2,1)S(1)} %get-tuple-element.35), channel_id=1, source_target_pairs={{0,8},{4,12},{8,0},{12,4},{1,9},{5,13},{9,1},{13,5},{2,10},{6,14},... | collective-permute-start | bytes 49160 | tf_op jit(solution)/shard_map/ppermute | solution.py:475
  6.0 2.3 %collective-permute-start.2 = (bf16[64,128]{1,0:T(8,128)(2,1)S(1)}, bf16[64,128]{1,0:T(8,128)(2,1)S(1)}, u32[]{:S(2)}, u32[]{:S(2)}) collective-permute-start(bf16[64,128]{1,0:T(8,128)(2,1)S(1)} %get-tuple-element.36), channel_id=1, source_target_pairs={{4,8},{8,4},{5,9},{9,5},{6,10},{10,6},{7,11},{11,7},{20,24},{24,20... | collective-permute-start | bytes 49160 | tf_op jit(solution)/shard_map/ppermute | solution.py:475
  8.4 3.2 %collective-permute-done.2.refs_4_ = bf16[64,128]{1,0:T(8,128)(2,1)S(1)} collective-permute-done((bf16[64,128]{1,0:T(8,128)(2,1)S(1)}, bf16[64,128]{1,0:T(8,128)(2,1)S(1)}, u32[]{:S(2)}, u32[]{:S(2)}) %collective-permute-start.2) | collective-permute-done | bytes 16416 | tf_op jit(solution)/shard_map/ppermute | solution.py:475
  11.7 0.6 collective-permute-start.3
  12.3 0.5 collective-permute-start.9
  12.8 0.0 collective-permute-start.4
  12.8 0.5 collective-permute-start.6
  13.4 1.8 %shard_map.229 = (bf16[896,512]{1,0:T(8,128)(2,1)S(1)}, bf16[1024,512]{1,0:T(8,128)(2,1)S(1)}, bf16[2048,512]{1,0:T(8,128)(2,1)S(1)}) custom-call(bf16[256,512]{1,0:T(8,128)(2,1)S(1)} %copy-done.11, bf16[128,512]{1,0:T(8,128)(2,1)S(1)} %copy-done.12, bf16[384,512]{1,0:T(8,128)(2,1)S(1)} %copy-done.10, bf16[128,512]{1,0:T(8,128)(2,1)S(1)} %copy-done.13, ...), custom_call_target="tpu_custom_call" | custom-call | flops 402653184 | bytes 5357568 | tf_op jit(solution)/shard_map/pallas_call | solution.py:62
  15.1 3.9 %collective-permute-done.3.lat.l1 = bf16[1216,128]{1,0:T(8,128)(2,1)S(1)} collective-permute-done((bf16[1216,128]{1,0:T(8,128)(2,1)S(1)}, bf16[1216,128]{1,0:T(8,128)(2,1)S(1)}, u32[]{:S(2)}, u32[]{:S(2)}) %collective-permute-start.3) | collective-permute-done | bytes 311328 | tf_op jit(solution)/shard_map/ppermute | solution.py:406
  19.0 0.1 shard_map.230
  19.1 0.1 collective-permute-start.5
  19.1 0.0 collective-permute-done.7.b_out
  19.1 0.5 collective-permute-start.10
  19.6 0.1 collective-permute-start.11
  19.7 0.0 collective-permute-done.4.l2
  19.7 0.4 collective-permute-start.15
  20.8 0.0 collective-permute-done.6.b_in
  20.8 0.7 %collective-permute-start.16 = (bf16[192,512]{1,0:T(8,128)(2,1)S(1)}, bf16[192,512]{1,0:T(8,128)(2,1)S(1)}, u32[]{:S(2)}, u32[]{:S(2)}) collective-permute-start(bf16[192,512]{1,0:T(8,128)(2,1)S(1)} %get-tuple-element.45), channel_id=1, source_target_pairs={{0,2},{1,3},{2,0},{3,1},{4,6},{5,7},{6,4},{7,5},{8,10},{9,11},{10,... | collective-permute-start | bytes 589832 | tf_op jit(solution)/shard_map/ppermute | solution.py:406
  21.5 0.0 collective-permute-done.10.both
  21.6 4.8 %shard_map.231 = (bf16[256,512]{1,0:T(8,128)(2,1)S(1)}, bf16[128,512]{1,0:T(8,128)(2,1)S(1)}, bf16[128,512]{1,0:T(8,128)(2,1)S(1)}, bf16[256,512]{1,0:T(8,128)(2,1)S(1)}) custom-call(bf16[1024,512]{1,0:T(8,128)(2,1)S(1)} %get-tuple-element.37.emb, s32[2,1024]{1,0:T(2,128)S(1)} %copy-done.19, f32[1,512]{1,0:T(1,128)S(1)} %bitcast.6, ...), custom_call_target="tpu_custom_call" | custom-call | flops 2952790016 | bytes 5187588 | tf_op jit(solution)/shard_map/pallas_call | solution.py:62
  26.4 0.0 copy-start.8
  26.4 0.0 copy-start.9
  26.4 0.1 collective-permute-start.12
  26.5 0.5 collective-permute-start.13
  27.0 1.4 %collective-permute-start.21 = (bf16[256,512]{1,0:T(8,128)(2,1)S(1)}, bf16[256,512]{1,0:T(8,128)(2,1)S(1)}, u32[]{:S(2)}, u32[]{:S(2)}) collective-permute-start(bf16[256,512]{1,0:T(8,128)(2,1)S(1)} %get-tuple-element.48), channel_id=1, source_target_pairs={{0,2},{1,3},{2,0},{3,1},{4,6},{5,7},{6,4},{7,5},{8,10},{9,11},{10,... | collective-permute-start | bytes 786440 | tf_op jit(solution)/shard_map/ppermute | solution.py:406
  28.3 0.1 shard_map.232.after.mine
  28.4 0.0 copy-start.2
  28.4 0.0 copy-start.5
  28.5 0.6 collective-permute-start.17
  29.0 1.0 %collective-permute-start.14 = (bf16[256,512]{1,0:T(8,128)(2,1)S(1)}, bf16[256,512]{1,0:T(8,128)(2,1)S(1)}, u32[]{:S(2)}, u32[]{:S(2)}) collective-permute-start(bf16[256,512]{1,0:T(8,128)(2,1)S(1)} %shard_map.232.after.mine), channel_id=1, source_target_pairs={{0,2},{1,3},{2,0},{3,1},{4,6},{5,7},{6,4},{7,5},{8,10},{9,11},{10,... | collective-permute-start | bytes 786440 | tf_op jit(solution)/shard_map/ppermute | solution.py:406
  30.0 5.3 %collective-permute-done.17.w3 = bf16[192,512]{1,0:T(8,128)(2,1)S(1)} collective-permute-done((bf16[192,512]{1,0:T(8,128)(2,1)S(1)}, bf16[192,512]{1,0:T(8,128)(2,1)S(1)}, u32[]{:S(2)}, u32[]{:S(2)}) %collective-permute-start.17) | collective-permute-done | bytes 196640 | tf_op jit(solution)/shard_map/ppermute | solution.py:415
  35.3 0.8 %collective-permute-done.21.source = bf16[256,512]{1,0:T(8,128)(2,1)S(1)} collective-permute-done((bf16[256,512]{1,0:T(8,128)(2,1)S(1)}, bf16[256,512]{1,0:T(8,128)(2,1)S(1)}, u32[]{:S(2)}, u32[]{:S(2)}) %collective-permute-start.21) | collective-permute-done | bytes 262176 | tf_op jit(solution)/shard_map/ppermute | solution.py:406
  36.1 0.6 collective-permute-start.22
  36.7 4.1 %collective-permute-done.14.theirs = bf16[256,512]{1,0:T(8,128)(2,1)S(1)} collective-permute-done((bf16[256,512]{1,0:T(8,128)(2,1)S(1)}, bf16[256,512]{1,0:T(8,128)(2,1)S(1)}, u32[]{:S(2)}, u32[]{:S(2)}) %collective-permute-start.14) | collective-permute-done | bytes 262176 | tf_op jit(solution)/shard_map/ppermute | solution.py:406
  40.9 0.0 copy-start.16
  40.9 1.2 %shard_map.234 = (bf16[256,512]{1,0:T(8,128)(2,1)S(1)}, bf16[32,512]{1,0:T(8,128)(2,1)S(1)}, bf16[32,512]{1,0:T(8,128)(2,1)S(1)}, bf16[32,512]{1,0:T(8,128)(2,1)S(1)}) custom-call(bf16[256,512]{1,0:T(8,128)(2,1)S(1)} %get-tuple-element.41.mesh, bf16[256,512]{1,0:T(8,128)(2,1)S(1)} %shard_map.232.after.mine, ...), custom_call_target="tpu_custom_call" | custom-call | flops 402653184 | bytes 3770880 | tf_op jit(solution)/shard_map/pallas_call | solution.py:62
  42.1 0.1 collective-permute-start.23
  42.2 2.0 %collective-permute-start.24 = (bf16[32,512]{1,0:T(8,128)(2,1)S(1)}, bf16[32,512]{1,0:T(8,128)(2,1)S(1)}, u32[]{:S(2)}, u32[]{:S(2)}) collective-permute-start(bf16[32,512]{1,0:T(8,128)(2,1)S(1)} %get-tuple-element.50), channel_id=1, source_target_pairs={{0,8},{4,12},{8,0},{12,4},{1,9},{5,13},{9,1},{13,5},{2,10},{6,14},... | collective-permute-start | bytes 98312 | tf_op jit(solution)/shard_map/ppermute | solution.py:540
  44.2 3.6 %collective-permute-start.25 = (bf16[32,512]{1,0:T(8,128)(2,1)S(1)}, bf16[32,512]{1,0:T(8,128)(2,1)S(1)}, u32[]{:S(2)}, u32[]{:S(2)}) collective-permute-start(bf16[32,512]{1,0:T(8,128)(2,1)S(1)} %get-tuple-element.51), channel_id=1, source_target_pairs={{4,8},{8,4},{5,9},{9,5},{6,10},{10,6},{7,11},{11,7},{20,24},{24,20... | collective-permute-start | bytes 98312 | tf_op jit(solution)/shard_map/ppermute | solution.py:540
  47.8 2.2 %collective-permute-done.25.refs_2_ = bf16[32,512]{1,0:T(8,128)(2,1)S(1)} collective-permute-done((bf16[32,512]{1,0:T(8,128)(2,1)S(1)}, bf16[32,512]{1,0:T(8,128)(2,1)S(1)}, u32[]{:S(2)}, u32[]{:S(2)}) %collective-permute-start.25) | collective-permute-done | bytes 32800 | tf_op jit(solution)/shard_map/ppermute | solution.py:540
  50.0 0.1 shard_map.236
  50.1 0.1 collective-permute-start.26
  50.1 0.5 collective-permute-start.20
  51.3 0.1 collective-permute-start.27
  51.4 1.4 %collective-permute-start.31 = (bf16[384,512]{1,0:T(8,128)(2,1)S(1)}, bf16[384,512]{1,0:T(8,128)(2,1)S(1)}, u32[]{:S(2)}, u32[]{:S(2)}) collective-permute-start(bf16[384,512]{1,0:T(8,128)(2,1)S(1)} %get-tuple-element.62.w0), channel_id=1, source_target_pairs={{0,2},{1,3},{2,0},{3,1},{4,6},{5,7},{6,4},{7,5},{8,10},{9,11},{10,... | collective-permute-start | bytes 1179656 | tf_op jit(solution)/shard_map/ppermute | solution.py:406
  52.8 0.0 copy-start.21
  52.9 2.6 %shard_map.237 = (bf16[1536,512]{1,0:T(8,128)(2,1)S(1)}, f32[1024,512]{1,0:T(8,128)S(1)}, bf16[512,512]{1,0:T(8,128)(2,1)S(1)}, bf16[512,512]{1,0:T(8,128)(2,1)S(1)}) custom-call(bf16[2048,512]{1,0:T(8,128)(2,1)S(1)} %get-tuple-element.47.emb, bf16[256,512]{1,0:T(8,128)(2,1)S(1)} %get-tuple-element.46.mine.middle, ...), custom_call_target="tpu_custom_call" | custom-call | flops 1610612736 | bytes 10240000 | tf_op jit(solution)/shard_map/pallas_call | solution.py:62
  55.5 0.0 copy-start.7
  55.5 5.8 %shard_map.238 = (bf16[256,512]{1,0:T(8,128)(2,1)S(1)}, bf16[256,512]{1,0:T(8,128)(2,1)S(1)}) custom-call(bf16[2048,512]{1,0:T(8,128)(2,1)S(1)} %get-tuple-element.47.emb, s32[2,2048]{1,0:T(2,128)S(1)} %copy-done.16, f32[1,512]{1,0:T(1,128)S(1)} %bitcast.7, bf16[1536,512]{1,0:T(8,128)(2,1)S(1)} %get-tuple-element.53.table, ...), custom_call_target="tpu_custom_call" | custom-call | flops 3489660928 | bytes 7555076 | tf_op jit(solution)/shard_map/pallas_call | solution.py:62
  61.3 0.2 collective-permute-start.28
  61.6 0.3 collective-permute-start.30
  61.9 1.0 %collective-permute-done.31.w2 = bf16[384,512]{1,0:T(8,128)(2,1)S(1)} collective-permute-done((bf16[384,512]{1,0:T(8,128)(2,1)S(1)}, bf16[384,512]{1,0:T(8,128)(2,1)S(1)}, u32[]{:S(2)}, u32[]{:S(2)}) %collective-permute-start.31) | collective-permute-done | bytes 393248 | tf_op jit(solution)/shard_map/ppermute | solution.py:406
  62.9 0.0 collective-permute-done.28.theirs
  62.9 0.1 shard_map.239
  63.0 1.4 %collective-permute-start.29 = (bf16[128,512]{1,0:T(8,128)(2,1)S(1)}, bf16[128,512]{1,0:T(8,128)(2,1)S(1)}, u32[]{:S(2)}, u32[]{:S(2)}) collective-permute-start(bf16[128,512]{1,0:T(8,128)(2,1)S(1)} %get-tuple-element.61), channel_id=1, source_target_pairs={{0,2},{1,3},{2,0},{3,1},{4,6},{5,7},{6,4},{7,5},{8,10},{9,11},{10,... | collective-permute-start | bytes 393224 | tf_op jit(solution)/shard_map/ppermute | solution.py:406
  64.4 0.2 collective-permute-done.32.w3
  64.6 4.3 %collective-permute-done.29.theirs = bf16[128,512]{1,0:T(8,128)(2,1)S(1)} collective-permute-done((bf16[128,512]{1,0:T(8,128)(2,1)S(1)}, bf16[128,512]{1,0:T(8,128)(2,1)S(1)}, u32[]{:S(2)}, u32[]{:S(2)}) %collective-permute-start.29) | collective-permute-done | bytes 131104 | tf_op jit(solution)/shard_map/ppermute | solution.py:406
  68.9 1.5 %shard_map.240 = bf16[128,512]{1,0:T(8,128)(2,1)} custom-call(bf16[256,512]{1,0:T(8,128)(2,1)S(1)} %get-tuple-element.46.mine.middle, bf16[128,512]{1,0:T(8,128)(2,1)S(1)} %get-tuple-element.60.mine, bf16[128,512]{1,0:T(8,128)(2,1)S(1)} %collective-permute-done.29.theirs, f32[1,512]{1,0:T(1,128)S(1)} %bitcast.4, bf16[384,512]{1,0:T(8,128)(2,1)S(1)} %get-tuple-element.62.w0, ...), custom_call_target="tpu_custom_call" | custom-call | flops 201326592 | bytes 2230272 | tf_op jit(solution)/shard_map/pallas_call | solution.py:62
  (61 shorter events, 0.2 us)
Async XLA Ops:
  0.0 0.9 %copy-start = (bf16[512,128]{1,0:T(8,128)(2,1)S(1)}, bf16[512,128]{1,0:T(8,128)(2,1)}, u32[]{:S(2)}) copy-start(bf16[512,128]{1,0:T(8,128)(2,1)} %refs_0_.1) | copy-start | bytes 393220
  0.0 0.9 %copy-start.6 = (s32[1,4,64]{2,1,0:T(4,128)S(1)}, s32[1,4,64]{2,1,0:T(4,128)}, u32[]{:S(2)}) copy-start(s32[1,4,64]{2,1,0:T(4,128)} %send.2) | copy-start | bytes 3076
  0.0 1.1 %copy-start.1 = (bf16[384,512]{1,0:T(8,128)(2,1)S(1)}, bf16[384,512]{1,0:T(8,128)(2,1)}, u32[]{:S(2)}) copy-start(bf16[384,512]{1,0:T(8,128)(2,1)} %o_in.1) | copy-start | bytes 1179652
  0.0 1.1 %copy-start.4 = (bf16[128,512]{1,0:T(8,128)(2,1)S(1)}, bf16[128,512]{1,0:T(8,128)(2,1)}, u32[]{:S(2)}) copy-start(bf16[128,512]{1,0:T(8,128)(2,1)} %o_out.1) | copy-start | bytes 393220
  0.0 11.6 %copy-start.3 = (bf16[512,128]{1,0:T(8,128)(2,1)S(1)}, bf16[512,128]{1,0:T(8,128)(2,1)}, u32[]{:S(2)}) copy-start(bf16[512,128]{1,0:T(8,128)(2,1)} %refs_1_.1) | copy-start | bytes 393220
  0.0 13.3 %copy-start.15 = (f32[4,1024]{1,0:T(4,128)S(1)}, f32[4,1024]{1,0:T(4,128)}, u32[]{:S(2)}) copy-start(f32[4,1024]{1,0:T(4,128)} %egeom.1) | copy-start | bytes 49156
  0.0 13.3 %copy-start.14 = (f32[4,2048]{1,0:T(4,128)S(1)}, f32[4,2048]{1,0:T(4,128)}, u32[]{:S(2)}) copy-start(f32[4,2048]{1,0:T(4,128)} %pgeom.1) | copy-start | bytes 98308
  0.0 13.2 %copy-start.17 = (f32[4,512]{1,0:T(4,128)S(1)}, f32[4,512]{1,0:T(4,128)}, u32[]{:S(2)}) copy-start(f32[4,512]{1,0:T(4,128)} %egeo.1) | copy-start | bytes 24580
  0.1 13.2 %copy-start.18 = (f32[4,512]{1,0:T(4,128)S(1)}, f32[4,512]{1,0:T(4,128)}, u32[]{:S(2)}) copy-start(f32[4,512]{1,0:T(4,128)} %pgeo.1) | copy-start | bytes 24580
  0.1 13.2 %copy-start.11 = (bf16[256,512]{1,0:T(8,128)(2,1)S(1)}, bf16[256,512]{1,0:T(8,128)(2,1)}, u32[]{:S(2)}) copy-start(bf16[256,512]{1,0:T(8,128)(2,1)} %e_in.1) | copy-start | bytes 786436
  0.1 13.2 %copy-start.12 = (bf16[128,512]{1,0:T(8,128)(2,1)S(1)}, bf16[128,512]{1,0:T(8,128)(2,1)}, u32[]{:S(2)}) copy-start(bf16[128,512]{1,0:T(8,128)(2,1)} %e_out.1) | copy-start | bytes 393220
  0.1 13.2 %copy-start.10 = (bf16[384,512]{1,0:T(8,128)(2,1)S(1)}, bf16[384,512]{1,0:T(8,128)(2,1)}, u32[]{:S(2)}) copy-start(bf16[384,512]{1,0:T(8,128)(2,1)} %p_in.1) | copy-start | bytes 1179652
  0.1 13.2 %copy-start.13 = (bf16[128,512]{1,0:T(8,128)(2,1)S(1)}, bf16[128,512]{1,0:T(8,128)(2,1)}, u32[]{:S(2)}) copy-start(bf16[128,512]{1,0:T(8,128)(2,1)} %p_out.1) | copy-start | bytes 393220
  1.1 20.5 %copy-start.19 = (s32[2,1024]{1,0:T(2,128)S(1)}, s32[2,1024]{1,0:T(2,128)}, u32[]{:S(2)}) copy-start(s32[2,1024]{1,0:T(2,128)} %edges.3) | copy-start | bytes 24580
  1.1 20.5 %copy-start.20 = (f32[512]{0:T(512)S(1)}, f32[512]{0:T(512)}, u32[]{:S(2)}) copy-start(f32[512]{0:T(512)} %param.44) | copy-start | bytes 6148
  1.4 10.8 %collective-permute-start.8 = (bf16[256,512]{1,0:T(8,128)(2,1)S(1)}, bf16[256,512]{1,0:T(8,128)(2,1)S(1)}, u32[]{:S(2)}, u32[]{:S(2)}) collective-permute-start(bf16[256,512]{1,0:T(8,128)(2,1)S(1)} %get-tuple-element.40), channel_id=1, source_target_pairs={{0,2},{1,3},{2,0},{3,1},{4,6},{5,7},{6,4},{7,5},{8,10},{9,11},{10,... | collective-permute-start | bytes 786440 | tf_op jit(solution)/shard_map/ppermute | solution.py:406
  3.0 5.4 %collective-permute-start = (bf16[64,128]{1,0:T(8,128)(2,1)S(1)}, bf16[64,128]{1,0:T(8,128)(2,1)S(1)}, u32[]{:S(2)}, u32[]{:S(2)}) collective-permute-start(bf16[64,128]{1,0:T(8,128)(2,1)S(1)} %get-tuple-element.34), channel_id=1, source_target_pairs={{0,4},{4,0},{8,12},{12,8},{1,5},{5,1},{9,13},{13,9},{2,6},{6,2},{1... | collective-permute-start | bytes 49160 | tf_op jit(solution)/shard_map/ppermute | solution.py:475
  3.4 5.0 %collective-permute-start.1 = (bf16[64,128]{1,0:T(8,128)(2,1)S(1)}, bf16[64,128]{1,0:T(8,128)(2,1)S(1)}, u32[]{:S(2)}, u32[]{:S(2)}) collective-permute-start(bf16[64,128]{1,0:T(8,128)(2,1)S(1)} %get-tuple-element.35), channel_id=1, source_target_pairs={{0,8},{4,12},{8,0},{12,4},{1,9},{5,13},{9,1},{13,5},{2,10},{6,14},... | collective-permute-start | bytes 49160 | tf_op jit(solution)/shard_map/ppermute | solution.py:475
  6.0 5.6 %collective-permute-start.2 = (bf16[64,128]{1,0:T(8,128)(2,1)S(1)}, bf16[64,128]{1,0:T(8,128)(2,1)S(1)}, u32[]{:S(2)}, u32[]{:S(2)}) collective-permute-start(bf16[64,128]{1,0:T(8,128)(2,1)S(1)} %get-tuple-element.36), channel_id=1, source_target_pairs={{4,8},{8,4},{5,9},{9,5},{6,10},{10,6},{7,11},{11,7},{20,24},{24,20... | collective-permute-start | bytes 49160 | tf_op jit(solution)/shard_map/ppermute | solution.py:475
  11.7 7.3 %collective-permute-start.3 = (bf16[1216,128]{1,0:T(8,128)(2,1)S(1)}, bf16[1216,128]{1,0:T(8,128)(2,1)S(1)}, u32[]{:S(2)}, u32[]{:S(2)}) collective-permute-start(bf16[1216,128]{1,0:T(8,128)(2,1)S(1)} %shard_map.228.after.l0), channel_id=1, source_target_pairs={{0,2},{1,3},{2,0},{3,1},{4,6},{5,7},{6,4},{7,5},{8,10},{9,11},{10,... | collective-permute-start | bytes 933896 | tf_op jit(solution)/shard_map/ppermute | solution.py:406
  12.3 7.4 %collective-permute-start.9 = (bf16[256,512]{1,0:T(8,128)(2,1)S(1)}, bf16[256,512]{1,0:T(8,128)(2,1)S(1)}, u32[]{:S(2)}, u32[]{:S(2)}) collective-permute-start(bf16[256,512]{1,0:T(8,128)(2,1)S(1)} %collective-permute-done.8.across), channel_id=1, source_target_pairs={{0,16},{16,0},{1,17},{17,1},{2,18},{18,2},{3,19},{19,3},{4,20},{20... | collective-permute-start | bytes 786440 | tf_op jit(solution)/shard_map/ppermute | solution.py:415
  12.8 7.0 %collective-permute-start.4 = (bf16[1216,128]{1,0:T(8,128)(2,1)S(1)}, bf16[1216,128]{1,0:T(8,128)(2,1)S(1)}, u32[]{:S(2)}, u32[]{:S(2)}) collective-permute-start(bf16[1216,128]{1,0:T(8,128)(2,1)S(1)} %shard_map.228.after.l0), channel_id=1, source_target_pairs={{0,1},{1,0},{2,3},{3,2},{4,5},{5,4},{6,7},{7,6},{8,9},{9,8},{10,11... | collective-permute-start | bytes 933896 | tf_op jit(solution)/shard_map/ppermute | solution.py:410
  12.8 8.0 %collective-permute-start.6 = (bf16[384,512]{1,0:T(8,128)(2,1)S(1)}, bf16[384,512]{1,0:T(8,128)(2,1)S(1)}, u32[]{:S(2)}, u32[]{:S(2)}) collective-permute-start(bf16[384,512]{1,0:T(8,128)(2,1)S(1)} %copy-done.1), channel_id=1, source_target_pairs={{0,1},{1,0},{2,3},{3,2},{4,5},{5,4},{6,7},{7,6},{8,9},{9,8},{10,11... | collective-permute-start | bytes 1179656 | tf_op jit(solution)/shard_map/ppermute | solution.py:410
  13.3 5.9 %collective-permute-start.7 = (bf16[128,512]{1,0:T(8,128)(2,1)S(1)}, bf16[128,512]{1,0:T(8,128)(2,1)S(1)}, u32[]{:S(2)}, u32[]{:S(2)}) collective-permute-start(bf16[128,512]{1,0:T(8,128)(2,1)S(1)} %copy-done.4), channel_id=1, source_target_pairs={{0,1},{1,0},{2,3},{3,2},{4,5},{5,4},{6,7},{7,6},{8,9},{9,8},{10,11... | collective-permute-start | bytes 393224 | tf_op jit(solution)/shard_map/ppermute | solution.py:410
  19.1 2.5 %collective-permute-start.5 = (bf16[1216,128]{1,0:T(8,128)(2,1)S(1)}, bf16[1216,128]{1,0:T(8,128)(2,1)S(1)}, u32[]{:S(2)}, u32[]{:S(2)}) collective-permute-start(bf16[1216,128]{1,0:T(8,128)(2,1)S(1)} %get-tuple-element.39), channel_id=1, source_target_pairs={{0,1},{1,0},{2,3},{3,2},{4,5},{5,4},{6,7},{7,6},{8,9},{9,8},{10,11... | collective-permute-start | bytes 933896 | tf_op jit(solution)/shard_map/ppermute | solution.py:410
  19.1 2.4 %collective-permute-start.10 = (bf16[256,512]{1,0:T(8,128)(2,1)S(1)}, bf16[256,512]{1,0:T(8,128)(2,1)S(1)}, u32[]{:S(2)}, u32[]{:S(2)}) collective-permute-start(bf16[256,512]{1,0:T(8,128)(2,1)S(1)} %collective-permute-done.8.across), channel_id=1, source_target_pairs={{0,1},{1,0},{2,3},{3,2},{4,5},{5,4},{6,7},{7,6},{8,9},{9,8},{10,11... | collective-permute-start | bytes 786440 | tf_op jit(solution)/shard_map/ppermute | solution.py:410
  19.6 1.9 %collective-permute-start.11 = (bf16[256,512]{1,0:T(8,128)(2,1)S(1)}, bf16[256,512]{1,0:T(8,128)(2,1)S(1)}, u32[]{:S(2)}, u32[]{:S(2)}) collective-permute-start(bf16[256,512]{1,0:T(8,128)(2,1)S(1)} %collective-permute-done.9.round_), channel_id=1, source_target_pairs={{0,1},{1,0},{2,3},{3,2},{4,5},{5,4},{6,7},{7,6},{8,9},{9,8},{10,11... | collective-permute-start | bytes 786440 | tf_op jit(solution)/shard_map/ppermute | solution.py:410
  19.7 17.0 %collective-permute-start.15 = (bf16[896,512]{1,0:T(8,128)(2,1)S(1)}, bf16[896,512]{1,0:T(8,128)(2,1)S(1)}, u32[]{:S(2)}, u32[]{:S(2)}) collective-permute-start(bf16[896,512]{1,0:T(8,128)(2,1)S(1)} %get-tuple-element.38.weights.w0), channel_id=1, source_target_pairs={{0,1},{1,0},{2,3},{3,2},{4,5},{5,4},{6,7},{7,6},{8,9},{9,8},{10,11... | collective-permute-start | bytes 2752520 | tf_op jit(solution)/shard_map/ppermute | solution.py:410
  20.8 7.6 %collective-permute-start.16 = (bf16[192,512]{1,0:T(8,128)(2,1)S(1)}, bf16[192,512]{1,0:T(8,128)(2,1)S(1)}, u32[]{:S(2)}, u32[]{:S(2)}) collective-permute-start(bf16[192,512]{1,0:T(8,128)(2,1)S(1)} %get-tuple-element.45), channel_id=1, source_target_pairs={{0,2},{1,3},{2,0},{3,1},{4,6},{5,7},{6,4},{7,5},{8,10},{9,11},{10,... | collective-permute-start | bytes 589832 | tf_op jit(solution)/shard_map/ppermute | solution.py:406
  26.4 14.5 %copy-start.8 = (f32[512]{0:T(512)S(1)}, f32[512]{0:T(512)}, u32[]{:S(2)}) copy-start(f32[512]{0:T(512)} %param.45) | copy-start | bytes 6148
  26.4 14.5 %copy-start.9 = (s32[1,4,32]{2,1,0:T(4,128)S(1)}, s32[1,4,32]{2,1,0:T(4,128)}, u32[]{:S(2)}) copy-start(s32[1,4,32]{2,1,0:T(4,128)} %send.3) | copy-start | bytes 1540
  26.4 1.9 %collective-permute-start.12 = (bf16[128,512]{1,0:T(8,128)(2,1)S(1)}, bf16[128,512]{1,0:T(8,128)(2,1)S(1)}, u32[]{:S(2)}, u32[]{:S(2)}) collective-permute-start(bf16[128,512]{1,0:T(8,128)(2,1)S(1)} %get-tuple-element.43), channel_id=1, source_target_pairs={{0,1},{1,0},{2,3},{3,2},{4,5},{5,4},{6,7},{7,6},{8,9},{9,8},{10,11... | collective-permute-start | bytes 393224 | tf_op jit(solution)/shard_map/ppermute | solution.py:410
  26.5 1.9 %collective-permute-start.13 = (bf16[128,512]{1,0:T(8,128)(2,1)S(1)}, bf16[128,512]{1,0:T(8,128)(2,1)S(1)}, u32[]{:S(2)}, u32[]{:S(2)}) collective-permute-start(bf16[128,512]{1,0:T(8,128)(2,1)S(1)} %get-tuple-element.44), channel_id=1, source_target_pairs={{0,1},{1,0},{2,3},{3,2},{4,5},{5,4},{6,7},{7,6},{8,9},{9,8},{10,11... | collective-permute-start | bytes 393224 | tf_op jit(solution)/shard_map/ppermute | solution.py:410
  27.0 9.2 %collective-permute-start.21 = (bf16[256,512]{1,0:T(8,128)(2,1)S(1)}, bf16[256,512]{1,0:T(8,128)(2,1)S(1)}, u32[]{:S(2)}, u32[]{:S(2)}) collective-permute-start(bf16[256,512]{1,0:T(8,128)(2,1)S(1)} %get-tuple-element.48), channel_id=1, source_target_pairs={{0,2},{1,3},{2,0},{3,1},{4,6},{5,7},{6,4},{7,5},{8,10},{9,11},{10,... | collective-permute-start | bytes 786440 | tf_op jit(solution)/shard_map/ppermute | solution.py:406
  28.4 21.6 %copy-start.2 = (bf16[256,512]{1,0:T(8,128)(2,1)S(1)}, bf16[256,512]{1,0:T(8,128)(2,1)}, u32[]{:S(2)}) copy-start(bf16[256,512]{1,0:T(8,128)(2,1)} %w_in.3) | copy-start | bytes 786436
  28.4 21.5 %copy-start.5 = (bf16[128,512]{1,0:T(8,128)(2,1)S(1)}, bf16[128,512]{1,0:T(8,128)(2,1)}, u32[]{:S(2)}) copy-start(bf16[128,512]{1,0:T(8,128)(2,1)} %w_out.3) | copy-start | bytes 393220
  28.5 6.8 %collective-permute-start.17 = (bf16[192,512]{1,0:T(8,128)(2,1)S(1)}, bf16[192,512]{1,0:T(8,128)(2,1)S(1)}, u32[]{:S(2)}, u32[]{:S(2)}) collective-permute-start(bf16[192,512]{1,0:T(8,128)(2,1)S(1)} %shard_map.233.w2), channel_id=1, source_target_pairs={{0,16},{16,0},{1,17},{17,1},{2,18},{18,2},{3,19},{19,3},{4,20},{20... | collective-permute-start | bytes 589832 | tf_op jit(solution)/shard_map/ppermute | solution.py:415
  29.0 11.8 %collective-permute-start.14 = (bf16[256,512]{1,0:T(8,128)(2,1)S(1)}, bf16[256,512]{1,0:T(8,128)(2,1)S(1)}, u32[]{:S(2)}, u32[]{:S(2)}) collective-permute-start(bf16[256,512]{1,0:T(8,128)(2,1)S(1)} %shard_map.232.after.mine), channel_id=1, source_target_pairs={{0,2},{1,3},{2,0},{3,1},{4,6},{5,7},{6,4},{7,5},{8,10},{9,11},{10,... | collective-permute-start | bytes 786440 | tf_op jit(solution)/shard_map/ppermute | solution.py:406
  30.0 6.7 %collective-permute-start.18 = (bf16[192,512]{1,0:T(8,128)(2,1)S(1)}, bf16[192,512]{1,0:T(8,128)(2,1)S(1)}, u32[]{:S(2)}, u32[]{:S(2)}) collective-permute-start(bf16[192,512]{1,0:T(8,128)(2,1)S(1)} %shard_map.233.w2), channel_id=1, source_target_pairs={{0,1},{1,0},{2,3},{3,2},{4,5},{5,4},{6,7},{7,6},{8,9},{9,8},{10,11... | collective-permute-start | bytes 589832 | tf_op jit(solution)/shard_map/ppermute | solution.py:410
  35.3 5.6 %collective-permute-start.19 = (bf16[192,512]{1,0:T(8,128)(2,1)S(1)}, bf16[192,512]{1,0:T(8,128)(2,1)S(1)}, u32[]{:S(2)}, u32[]{:S(2)}) collective-permute-start(bf16[192,512]{1,0:T(8,128)(2,1)S(1)} %collective-permute-done.17.w3), channel_id=1, source_target_pairs={{0,1},{1,0},{2,3},{3,2},{4,5},{5,4},{6,7},{7,6},{8,9},{9,8},{10,11... | collective-permute-start | bytes 589832 | tf_op jit(solution)/shard_map/ppermute | solution.py:410
  36.1 11.6 %collective-permute-start.22 = (bf16[256,512]{1,0:T(8,128)(2,1)S(1)}, bf16[256,512]{1,0:T(8,128)(2,1)S(1)}, u32[]{:S(2)}, u32[]{:S(2)}) collective-permute-start(bf16[256,512]{1,0:T(8,128)(2,1)S(1)} %shard_map.235.across), channel_id=1, source_target_pairs={{0,16},{16,0},{1,17},{17,1},{2,18},{18,2},{3,19},{19,3},{4,20},{20... | collective-permute-start | bytes 786440 | tf_op jit(solution)/shard_map/ppermute | solution.py:415
  40.9 12.0 %copy-start.16 = (s32[2,2048]{1,0:T(2,128)S(1)}, s32[2,2048]{1,0:T(2,128)}, u32[]{:S(2)}) copy-start(s32[2,2048]{1,0:T(2,128)} %edges.5) | copy-start | bytes 49156
  42.1 5.7 %collective-permute-start.23 = (bf16[32,512]{1,0:T(8,128)(2,1)S(1)}, bf16[32,512]{1,0:T(8,128)(2,1)S(1)}, u32[]{:S(2)}, u32[]{:S(2)}) collective-permute-start(bf16[32,512]{1,0:T(8,128)(2,1)S(1)} %get-tuple-element.49), channel_id=1, source_target_pairs={{0,4},{4,0},{8,12},{12,8},{1,5},{5,1},{9,13},{13,9},{2,6},{6,2},{1... | collective-permute-start | bytes 98312 | tf_op jit(solution)/shard_map/ppermute | solution.py:540
  42.2 5.6 %collective-permute-start.24 = (bf16[32,512]{1,0:T(8,128)(2,1)S(1)}, bf16[32,512]{1,0:T(8,128)(2,1)S(1)}, u32[]{:S(2)}, u32[]{:S(2)}) collective-permute-start(bf16[32,512]{1,0:T(8,128)(2,1)S(1)} %get-tuple-element.50), channel_id=1, source_target_pairs={{0,8},{4,12},{8,0},{12,4},{1,9},{5,13},{9,1},{13,5},{2,10},{6,14},... | collective-permute-start | bytes 98312 | tf_op jit(solution)/shard_map/ppermute | solution.py:540
  44.2 5.8 %collective-permute-start.25 = (bf16[32,512]{1,0:T(8,128)(2,1)S(1)}, bf16[32,512]{1,0:T(8,128)(2,1)S(1)}, u32[]{:S(2)}, u32[]{:S(2)}) collective-permute-start(bf16[32,512]{1,0:T(8,128)(2,1)S(1)} %get-tuple-element.51), channel_id=1, source_target_pairs={{4,8},{8,4},{5,9},{9,5},{6,10},{10,6},{7,11},{11,7},{20,24},{24,20... | collective-permute-start | bytes 98312 | tf_op jit(solution)/shard_map/ppermute | solution.py:540
  50.1 2.8 %collective-permute-start.26 = (bf16[512,512]{1,0:T(8,128)(2,1)S(1)}, bf16[512,512]{1,0:T(8,128)(2,1)S(1)}, u32[]{:S(2)}, u32[]{:S(2)}) collective-permute-start(bf16[512,512]{1,0:T(8,128)(2,1)S(1)} %get-tuple-element.52.pair), channel_id=1, source_target_pairs={{0,1},{1,0},{2,3},{3,2},{4,5},{5,4},{6,7},{7,6},{8,9},{9,8},{10,11... | collective-permute-start | bytes 1572872 | tf_op jit(solution)/shard_map/ppermute | solution.py:410
  50.1 2.7 %collective-permute-start.20 = (bf16[256,512]{1,0:T(8,128)(2,1)S(1)}, bf16[256,512]{1,0:T(8,128)(2,1)S(1)}, u32[]{:S(2)}, u32[]{:S(2)}) collective-permute-start(bf16[256,512]{1,0:T(8,128)(2,1)S(1)} %get-tuple-element.46.mine.middle), channel_id=1, source_target_pairs={{0,1},{1,0},{2,3},{3,2},{4,5},{5,4},{6,7},{7,6},{8,9},{9,8},{10,11... | collective-permute-start | bytes 786440 | tf_op jit(solution)/shard_map/ppermute | solution.py:410
  51.3 4.2 %collective-permute-start.27 = (bf16[96,512]{1,0:T(8,128)(2,1)S(1)}, bf16[96,512]{1,0:T(8,128)(2,1)S(1)}, u32[]{:S(2)}, u32[]{:S(2)}) collective-permute-start(bf16[96,512]{1,0:T(8,128)(2,1)S(1)} %get-tuple-element.57.halo), channel_id=1, source_target_pairs={{0,1},{1,0},{2,3},{3,2},{4,5},{5,4},{6,7},{7,6},{8,9},{9,8},{10,11... | collective-permute-start | bytes 294920 | tf_op jit(solution)/shard_map/ppermute | solution.py:410
  51.4 11.5 %collective-permute-start.31 = (bf16[384,512]{1,0:T(8,128)(2,1)S(1)}, bf16[384,512]{1,0:T(8,128)(2,1)S(1)}, u32[]{:S(2)}, u32[]{:S(2)}) collective-permute-start(bf16[384,512]{1,0:T(8,128)(2,1)S(1)} %get-tuple-element.62.w0), channel_id=1, source_target_pairs={{0,2},{1,3},{2,0},{3,1},{4,6},{5,7},{6,4},{7,5},{8,10},{9,11},{10,... | collective-permute-start | bytes 1179656 | tf_op jit(solution)/shard_map/ppermute | solution.py:406
  52.8 2.6 %copy-start.21 = (f32[512]{0:T(512)S(1)}, f32[512]{0:T(512)}, u32[]{:S(2)}) copy-start(f32[512]{0:T(512)} %param.46) | copy-start | bytes 6148
  55.5 13.5 %copy-start.7 = (f32[512]{0:T(512)S(1)}, f32[512]{0:T(512)}, u32[]{:S(2)}) copy-start(f32[512]{0:T(512)} %param.47) | copy-start | bytes 6148
  61.3 1.6 %collective-permute-start.28 = (bf16[256,512]{1,0:T(8,128)(2,1)S(1)}, bf16[256,512]{1,0:T(8,128)(2,1)S(1)}, u32[]{:S(2)}, u32[]{:S(2)}) collective-permute-start(bf16[256,512]{1,0:T(8,128)(2,1)S(1)} %get-tuple-element.59), channel_id=1, source_target_pairs={{0,1},{1,0},{2,3},{3,2},{4,5},{5,4},{6,7},{7,6},{8,9},{9,8},{10,11... | collective-permute-start | bytes 786440 | tf_op jit(solution)/shard_map/ppermute | solution.py:410
  61.6 2.9 %collective-permute-start.30 = (bf16[384,512]{1,0:T(8,128)(2,1)S(1)}, bf16[384,512]{1,0:T(8,128)(2,1)S(1)}, u32[]{:S(2)}, u32[]{:S(2)}) collective-permute-start(bf16[384,512]{1,0:T(8,128)(2,1)S(1)} %get-tuple-element.62.w0), channel_id=1, source_target_pairs={{0,1},{1,0},{2,3},{3,2},{4,5},{5,4},{6,7},{7,6},{8,9},{9,8},{10,11... | collective-permute-start | bytes 1179656 | tf_op jit(solution)/shard_map/ppermute | solution.py:410
  62.9 1.7 %collective-permute-start.32 = (bf16[384,512]{1,0:T(8,128)(2,1)S(1)}, bf16[384,512]{1,0:T(8,128)(2,1)S(1)}, u32[]{:S(2)}, u32[]{:S(2)}) collective-permute-start(bf16[384,512]{1,0:T(8,128)(2,1)S(1)} %collective-permute-done.31.w2), channel_id=1, source_target_pairs={{0,1},{1,0},{2,3},{3,2},{4,5},{5,4},{6,7},{7,6},{8,9},{9,8},{10,11... | collective-permute-start | bytes 1179656 | tf_op jit(solution)/shard_map/ppermute | solution.py:410
  63.0 5.9 %collective-permute-start.29 = (bf16[128,512]{1,0:T(8,128)(2,1)S(1)}, bf16[128,512]{1,0:T(8,128)(2,1)S(1)}, u32[]{:S(2)}, u32[]{:S(2)}) collective-permute-start(bf16[128,512]{1,0:T(8,128)(2,1)S(1)} %get-tuple-element.61), channel_id=1, source_target_pairs={{0,2},{1,3},{2,0},{3,1},{4,6},{5,7},{6,4},{7,5},{8,10},{9,11},{10,... | collective-permute-start | bytes 393224 | tf_op jit(solution)/shard_map/ppermute | solution.py:406

commit v9 on v7

--- a/solution.py
+++ b/solution.py
@@ -158,10 +158,6 @@
             first, place = first + rows, place + half
 
 
-def pair_kernel(first, second, after, out):
-    stack_into(out, (first, second))
-
-
 def hold_kernel(source, after, out):
     out[...] = source[...]
 
@@ -190,13 +186,10 @@
     return jnp.concatenate([stack[k * step + first : k * step + first + rows, :] for k in range(4)], axis=0)
 
 
-def halo_targets(plan, slots, node_rows, width):
-    here = lax.axis_index("dom")
+def halo_targets(firsts, slots, width):
     lane = lax.broadcasted_iota(jnp.int32, (1, width), 1)
     target = jnp.full((1, width), -1, jnp.int32)
-    for place, (pairs, sent, received) in enumerate(plan):
-        region = by_index(received, here)
-        first = jnp.where(region < 0, -4 * node_rows, node_rows + region * slots)
+    for place, first in enumerate(firsts):
         inside = (lane >= place * slots) & (lane < (place + 1) * slots)
         target = jnp.where(inside, lane - place * slots + first, target)
     return target.astype(I16)
@@ -274,7 +267,12 @@
     table[base : base + got, :] = dot(full[halo_first:, :], w_in[d : 2 * d, :]).astype(BF16)
     if base + got < table.shape[0]:
         table[base + got :, :] = jnp.zeros((table.shape[0] - base - got, d), BF16)
-    targets = halo_targets(plan, slots, grid_rows, table.shape[0] - base)
+    here = lax.axis_index("dom")
+    firsts = []
+    for pairs, sent, received in plan:
+        region = by_index(received, here)
+        firsts.append(jnp.where(region < 0, -4 * grid_rows, grid_rows + region * slots))
+    targets = halo_targets(firsts, slots, table.shape[0] - base)
     own = lax.broadcasted_iota(I16, (1, grid_rows), 1)
     mesh = lax.broadcasted_iota(I16, (1, mesh_rows), 1)
 
@@ -305,9 +303,8 @@
 
 
 def node_kernel(
-    plan, k_in, k_out, mesh, mine, theirs, gain, n_in, n_out, w0, w1, w2, w3, w4, w5, send, out, packed, *rest
+    k_in, k_out, mesh, mine, theirs, gain, n_in, n_out, w0, w1, w2, w3, w4, w5, out, packed, stack
 ):
-    outs, stack = rest[:-1], rest[-1]
     put_shard(stack, w0, 0, 0)
     put_shard(stack, w1, 0, 1)
     put_half(stack, k_in, w2, 2, 0)
@@ -317,26 +314,26 @@
     w_in, w_out = joined(stack, 0, k_in), joined(stack, k_in, k_out)
     fresh = node_update(mesh[...], add(mine[...], theirs[...]), w_in, w_out, gain[...])
     out[...] = fresh
-    half = fresh.shape[0] // 2
-    core = lax.rem(lax.axis_index("sub"), 2)
-    place = lax.broadcasted_iota(jnp.int32, (fresh.shape[0], 1), 0)
-    rows = place + core * half + jnp.where(place < half, 0, half)
-    pick_lists(plan, fresh, send, outs, rows.astype(I16))
     stack_into(packed, (n_in, n_out))
 
 
-def proc_first_kernel(
-    k_in, first_row, emb, mine, theirs, edges, w0, w1, pair, pair_beside,
-    table, pre, w_source, w_out, stack, full,
-):
-    d = full.shape[1]
-    node_rows = full.shape[0]
-    rows = node_rows // 4
-    core = lax.rem(lax.axis_index("sub"), 2)
+def middle_kernel(mine, theirs, send, across, round_, full, listed, pair):
+    stack_into(pair, (across, round_))
+    rows = mine.shape[0] // 2
+    quarter = lax.axis_index("sub")
+    core = lax.rem(quarter, 2)
     for half in range(2):
         for part, which in ((mine, core), (theirs, 1 - core)):
             place = pl.multiple_of((2 * half + which) * rows, rows)
             full[pl.ds(place, rows), :] = part[half * rows : (half + 1) * rows, :]
+    listed[...] = pick_rows(full[...], send[0, pl.ds(quarter, 1), :])
+
+
+def proc_first_kernel(
+    k_in, first_row, emb, full, edges, w0, w1, pair, pair_beside, table, pre, w_source, w_out, stack
+):
+    d = full.shape[1]
+    node_rows = full.shape[0]
     put_shard(stack, w0, first_row, 0)
     put_shard(stack, w1, first_row, 1)
     rows = pair.shape[0] // 2
@@ -360,15 +357,17 @@
 
 
 def proc_second_kernel(
-    plan, slots, node_rows, emb, edges, gain, table, pre, w_source, w_out, halo, halo_beside,
+    slots, node_rows, emb, edges, gain, table, pre, w_source, w_out, halo, halo_beside,
     live, keep, give, halo_table, messages, totals,
 ):
     d = pre.shape[1]
-    got = halo[...] + halo_beside[...]
+    got = jnp.concatenate([halo[...], halo_beside[...]], axis=0)
     halo_table[: got.shape[0], :] = dot(got, w_source[...]).astype(BF16)
     if got.shape[0] < halo_table.shape[0]:
         halo_table[got.shape[0] :, :] = jnp.zeros((halo_table.shape[0] - got.shape[0], d), BF16)
-    targets = halo_targets(plan, slots, node_rows, halo_table.shape[0])
+    quarter = lax.axis_index("sub")
+    firsts = [node_rows + (3 - lax.bitwise_xor(quarter, step)) * slots for step in (0, 2, 1, 3)]
+    targets = halo_targets(firsts, slots, halo_table.shape[0])
     lane = lax.broadcasted_iota(I16, (1, node_rows), 1)
 
     def first_stage(first):
@@ -402,6 +401,17 @@
 
 def to_chip(v):
     return lax.ppermute(v, "sub", [(i, i ^ 2) for i in range(4)])
+
+
+def to_offset(v, step):
+    count, parts = lax.axis_size("dom"), lax.axis_size("sub")
+    pairs = [
+        (d * parts + s, (d + offset) * parts + (s ^ step))
+        for d in range(count)
+        for s, offset in enumerate(OFFSETS)
+        if 0 <= d + offset < count
+    ]
+    return lax.ppermute(v, ("dom", "sub"), pairs)
 
 
 def to_core(v):
@@ -524,20 +534,23 @@
     node_round, proc_round = to_group(node_across), to_group(proc_across)
     node_both = to_core(node_across)
     slots = mesh_send.shape[2]
-    mid_half, last_w, *outgoing = call(
-        functools.partial(node_kernel, plan, n_in, n_out),
-        [shape(half, d), shape(n_in + n_out, d)] + [shape(slots, d)] * len(plan),
+    mid_half, last_w = call(
+        functools.partial(node_kernel, n_in, n_out),
+        [shape(half, d), shape(n_in + n_out, d)],
         [
             own_mesh, chip_sum, to_chip(chip_sum), enc_node_gain, proc_node_in, proc_node_out,
-            next_w, next_beside, node_across, node_round, node_both, to_core(node_round), mesh_send,
+            next_w, next_beside, node_across, node_round, node_both, to_core(node_round),
         ],
         scratch=[pltpu.VMEM((4 * (n_in + n_out), d), BF16)],
         flops=2 * half * d * 3 * d,
     )
-    mid_beside = to_core(mid_half)
-    halos = [lax.ppermute(v, "dom", entry[0]) for v, entry in zip(outgoing, plan)]
-    (proc_pair,) = call(pair_kernel, [shape(k_in + k_out, d)], [proc_across, proc_round, halos[0]])
-    (halo,) = call(concat_kernel, [shape(len(plan) * slots, d)], halos)
+    mid, listed, proc_pair = call(
+        middle_kernel,
+        [shape(mesh_rows, d), shape(slots, d), shape(k_in + k_out, d)],
+        [mid_half, to_core(mid_half), mesh_send, proc_across, proc_round],
+        flops=2 * slots * mesh_rows * d,
+    )
+    (halo,) = call(concat_kernel, [shape(2 * slots, d)], [to_offset(listed, 0), to_offset(listed, 2)])
     halo_beside = to_core(halo)
     last_across, last_beside = to_chip(last_w), to_core(last_w)
     early = n_proc // 2
@@ -545,14 +558,14 @@
         functools.partial(proc_first_kernel, k_in, n_in + n_out),
         [shape(d + 2 * mesh_rows, d), shape(early, d, F32), shape(d, d), shape(d, d)],
         [
-            proc_emb, mid_half, mid_beside, proc_edges, next_w, next_beside, proc_pair, to_core(proc_pair),
+            proc_emb, mid, proc_edges, next_w, next_beside, proc_pair, to_core(proc_pair),
         ],
-        scratch=[pltpu.VMEM((4 * (k_in + k_out), d), BF16), pltpu.VMEM((mesh_rows, d), BF16)],
+        scratch=[pltpu.VMEM((4 * (k_in + k_out), d), BF16)],
         flops=2 * early * d * (d + 2 * mesh_rows),
     )
-    halo_rows = padded(len(plan) * slots)
+    halo_rows = padded(4 * slots)
     keep, give = call(
-        functools.partial(proc_second_kernel, plan, slots, mesh_rows),
+        functools.partial(proc_second_kernel, slots, mesh_rows),
         [shape(half, d), shape(half, d)],
         [proc_emb, proc_edges, proc_edge_gain, table, pre, w_source, w_out, halo, halo_beside, proc_blocks],
         scratch=[

time: 71.2 us -> 77 us (1.081)
  the two profiles are of different devices: /device:TPU:12 before, /device:TPU:0 now
where the time goes in v9:
time: 77 us; the launch traced here: 76.8 us
  starting transfers between devices  32.4 us (42%)
  waiting for transfers between devices  23.3 us (30%)
  Pallas kernels  18.3 us (24%)
  between operations  1.71 us (2%)
  local copies, waits for them, and re-layouts  1.1 us (1%)
    pallas_call x16, Pallas kernels, call(): pl.pallas_call(body, out_shape=tuple(outs), in_specs=specs, out_specs=tup...  18.3 us
    ppermute x7, starting transfers between devices, to_chip(): return lax.ppermute(v, 'sub', [(i, i ^ 2) for i in range(4)])  17.5 us
    ppermute x7, waiting for transfers between devices, to_chip(): return lax.ppermute(v, 'sub', [(i, i ^ 2) for i in range(4)])  14.8 us
    ppermute x3, starting transfers between devices, local(): lax.ppermute(v, 'dom', entry[0])  4.81 us
    ppermute x3, waiting for transfers between devices, to_group(): return lax.ppermute(v, 'groups', [(i, count - 1 - i) for i in range(count)])  4.31 us
    ppermute x17, starting transfers between devices, to_core(): return lax.ppermute(v, 'sub', [(i, i ^ 1) for i in range(4)])  4.18 us
    ppermute x3, starting transfers between devices, to_group(): return lax.ppermute(v, 'groups', [(i, count - 1 - i) for i in range(count)])  3.74 us
    ppermute x17, waiting for transfers between devices, to_core(): return lax.ppermute(v, 'sub', [(i, i ^ 1) for i in range(4)])  2.78 us
  transfers between devices with their start and end apart: 32, of which 11 were waited for; matrix products, arithmetic and copies ran while one was open for 0% of the time, Pallas kernels for 21%

profile of v9, /device:TPU:0, one launch (start us, length us, event | category | flops | bytes accessed | tf_op | source)
XLA Modules:
  0.0 76.8 jit_solution(13872203485613933144)
XLA Ops:
  0.1 0.8 %copy-done = bf16[512,128]{1,0:T(8,128)(2,1)S(1)} copy-done((bf16[512,128]{1,0:T(8,128)(2,1)S(1)}, bf16[512,128]{1,0:T(8,128)(2,1)}, u32[]{:S(2)}) %copy-start) | copy-done | bytes 131096
  0.9 0.2 copy-done.1
  1.1 0.0 copy-done.4
  1.1 0.3 shard_map.227
  1.4 3.0 %collective-permute-start.8 = (bf16[256,512]{1,0:T(8,128)(2,1)S(1)}, bf16[256,512]{1,0:T(8,128)(2,1)S(1)}, u32[]{:S(2)}, u32[]{:S(2)}) collective-permute-start(bf16[256,512]{1,0:T(8,128)(2,1)S(1)} %get-tuple-element.38), channel_id=1, source_target_pairs={{0,2},{1,3},{2,0},{3,1},{4,6},{5,7},{6,4},{7,5},{8,10},{9,11},{10,... | collective-permute-start | bytes 786440 | tf_op jit(solution)/shard_map/ppermute | solution.py:403
  4.4 1.6 %collective-permute-start = (bf16[64,128]{1,0:T(8,128)(2,1)S(1)}, bf16[64,128]{1,0:T(8,128)(2,1)S(1)}, u32[]{:S(2)}, u32[]{:S(2)}) collective-permute-start(bf16[64,128]{1,0:T(8,128)(2,1)S(1)} %get-tuple-element.32), channel_id=1, source_target_pairs={{0,4},{4,0},{8,12},{12,8},{1,5},{5,1},{9,13},{13,9},{2,6},{6,2},{1... | collective-permute-start | bytes 49160 | tf_op jit(solution)/shard_map/ppermute | solution.py:483
  6.0 2.6 %collective-permute-start.1 = (bf16[64,128]{1,0:T(8,128)(2,1)S(1)}, bf16[64,128]{1,0:T(8,128)(2,1)S(1)}, u32[]{:S(2)}, u32[]{:S(2)}) collective-permute-start(bf16[64,128]{1,0:T(8,128)(2,1)S(1)} %get-tuple-element.33), channel_id=1, source_target_pairs={{0,8},{4,12},{8,0},{12,4},{1,9},{5,13},{9,1},{13,5},{2,10},{6,14},... | collective-permute-start | bytes 49160 | tf_op jit(solution)/shard_map/ppermute | solution.py:483
  8.6 0.7 collective-permute-start.2
  9.3 1.4 %collective-permute-done.1.refs_3_ = bf16[64,128]{1,0:T(8,128)(2,1)S(1)} collective-permute-done((bf16[64,128]{1,0:T(8,128)(2,1)S(1)}, bf16[64,128]{1,0:T(8,128)(2,1)S(1)}, u32[]{:S(2)}, u32[]{:S(2)}) %collective-permute-start.1) | collective-permute-done | bytes 16416 | tf_op jit(solution)/shard_map/ppermute | solution.py:483
  10.7 0.5 collective-permute-start.3
  11.3 0.0 collective-permute-done.8.across
  11.3 1.6 %collective-permute-start.9 = (bf16[256,512]{1,0:T(8,128)(2,1)S(1)}, bf16[256,512]{1,0:T(8,128)(2,1)S(1)}, u32[]{:S(2)}, u32[]{:S(2)}) collective-permute-start(bf16[256,512]{1,0:T(8,128)(2,1)S(1)} %collective-permute-done.8.across), channel_id=1, source_target_pairs={{0,16},{16,0},{1,17},{17,1},{2,18},{18,2},{3,19},{19,3},{4,20},{20... | collective-permute-start | bytes 786440 | tf_op jit(solution)/shard_map/ppermute | solution.py:423
  12.9 0.5 collective-permute-start.6
  13.4 1.8 %shard_map.229 = (bf16[896,512]{1,0:T(8,128)(2,1)S(1)}, bf16[1024,512]{1,0:T(8,128)(2,1)S(1)}, bf16[2048,512]{1,0:T(8,128)(2,1)S(1)}) custom-call(bf16[256,512]{1,0:T(8,128)(2,1)S(1)} %copy-done.11, bf16[128,512]{1,0:T(8,128)(2,1)S(1)} %copy-done.12, bf16[384,512]{1,0:T(8,128)(2,1)S(1)} %copy-done.10, bf16[128,512]{1,0:T(8,128)(2,1)S(1)} %copy-done.13, ...), custom_call_target="tpu_custom_call" | custom-call | flops 402653184 | bytes 5357568 | tf_op jit(solution)/shard_map/pallas_call | solution.py:62
  15.2 3.1 %collective-permute-done.3.lat.l1 = bf16[1216,128]{1,0:T(8,128)(2,1)S(1)} collective-permute-done((bf16[1216,128]{1,0:T(8,128)(2,1)S(1)}, bf16[1216,128]{1,0:T(8,128)(2,1)S(1)}, u32[]{:S(2)}, u32[]{:S(2)}) %collective-permute-start.3) | collective-permute-done | bytes 311328 | tf_op jit(solution)/shard_map/ppermute | solution.py:403
  18.3 0.1 shard_map.230
  18.4 0.1 collective-permute-start.5
  18.4 0.5 collective-permute-start.10
  18.9 0.0 collective-permute-done.9.round_
  18.9 0.1 collective-permute-start.11
  19.0 0.0 collective-permute-done.4.l2
  19.0 0.4 collective-permute-start.15
  20.1 0.0 collective-permute-done.6.b_in
  20.1 0.9 %collective-permute-start.16 = (bf16[192,512]{1,0:T(8,128)(2,1)S(1)}, bf16[192,512]{1,0:T(8,128)(2,1)S(1)}, u32[]{:S(2)}, u32[]{:S(2)}) collective-permute-start(bf16[192,512]{1,0:T(8,128)(2,1)S(1)} %get-tuple-element.43), channel_id=1, source_target_pairs={{0,2},{1,3},{2,0},{3,1},{4,6},{5,7},{6,4},{7,5},{8,10},{9,11},{10,... | collective-permute-start | bytes 589832 | tf_op jit(solution)/shard_map/ppermute | solution.py:403
  21.0 0.0 collective-permute-done.10.both
  21.1 4.8 %shard_map.231 = (bf16[256,512]{1,0:T(8,128)(2,1)S(1)}, bf16[128,512]{1,0:T(8,128)(2,1)S(1)}, bf16[128,512]{1,0:T(8,128)(2,1)S(1)}, bf16[256,512]{1,0:T(8,128)(2,1)S(1)}) custom-call(bf16[1024,512]{1,0:T(8,128)(2,1)S(1)} %get-tuple-element.35.emb, s32[2,1024]{1,0:T(2,128)S(1)} %copy-done.19, f32[1,512]{1,0:T(1,128)S(1)} %bitcast.6, ...), custom_call_target="tpu_custom_call" | custom-call | flops 2952790016 | bytes 5187588 | tf_op jit(solution)/shard_map/pallas_call | solution.py:62
  25.8 0.0 copy-start.2
  25.8 0.0 copy-start.5
  25.9 0.0 copy-start.6
  25.9 0.1 collective-permute-start.12
  25.9 0.5 collective-permute-start.13
  26.4 0.8 %collective-permute-done.12.first = bf16[128,512]{1,0:T(8,128)(2,1)S(1)} collective-permute-done((bf16[128,512]{1,0:T(8,128)(2,1)S(1)}, bf16[128,512]{1,0:T(8,128)(2,1)S(1)}, u32[]{:S(2)}, u32[]{:S(2)}) %collective-permute-start.12) | collective-permute-done | bytes 131104 | tf_op jit(solution)/shard_map/ppermute | solution.py:418
  27.3 0.2 collective-permute-done.13.second
  27.5 0.1 shard_map.232.after.mine
  27.6 1.6 %collective-permute-start.17 = (bf16[192,512]{1,0:T(8,128)(2,1)S(1)}, bf16[192,512]{1,0:T(8,128)(2,1)S(1)}, u32[]{:S(2)}, u32[]{:S(2)}) collective-permute-start(bf16[192,512]{1,0:T(8,128)(2,1)S(1)} %shard_map.233.w2), channel_id=1, source_target_pairs={{0,16},{16,0},{1,17},{17,1},{2,18},{18,2},{3,19},{19,3},{4,20},{20... | collective-permute-start | bytes 589832 | tf_op jit(solution)/shard_map/ppermute | solution.py:423
  29.2 1.2 %collective-permute-start.21 = (bf16[256,512]{1,0:T(8,128)(2,1)S(1)}, bf16[256,512]{1,0:T(8,128)(2,1)S(1)}, u32[]{:S(2)}, u32[]{:S(2)}) collective-permute-start(bf16[256,512]{1,0:T(8,128)(2,1)S(1)} %get-tuple-element.46), channel_id=1, source_target_pairs={{0,2},{1,3},{2,0},{3,1},{4,6},{5,7},{6,4},{7,5},{8,10},{9,11},{10,... | collective-permute-start | bytes 786440 | tf_op jit(solution)/shard_map/ppermute | solution.py:403
  30.4 0.8 %collective-permute-start.14 = (bf16[256,512]{1,0:T(8,128)(2,1)S(1)}, bf16[256,512]{1,0:T(8,128)(2,1)S(1)}, u32[]{:S(2)}, u32[]{:S(2)}) collective-permute-start(bf16[256,512]{1,0:T(8,128)(2,1)S(1)} %shard_map.232.after.mine), channel_id=1, source_target_pairs={{0,2},{1,3},{2,0},{3,1},{4,6},{5,7},{6,4},{7,5},{8,10},{9,11},{10,... | collective-permute-start | bytes 786440 | tf_op jit(solution)/shard_map/ppermute | solution.py:403
  31.2 3.6 %collective-permute-done.17.w3 = bf16[192,512]{1,0:T(8,128)(2,1)S(1)} collective-permute-done((bf16[192,512]{1,0:T(8,128)(2,1)S(1)}, bf16[192,512]{1,0:T(8,128)(2,1)S(1)}, u32[]{:S(2)}, u32[]{:S(2)}) %collective-permute-start.17) | collective-permute-done | bytes 196640 | tf_op jit(solution)/shard_map/ppermute | solution.py:423
  34.8 3.6 %collective-permute-done.21.source = bf16[256,512]{1,0:T(8,128)(2,1)S(1)} collective-permute-done((bf16[256,512]{1,0:T(8,128)(2,1)S(1)}, bf16[256,512]{1,0:T(8,128)(2,1)S(1)}, u32[]{:S(2)}, u32[]{:S(2)}) %collective-permute-start.21) | collective-permute-done | bytes 262176 | tf_op jit(solution)/shard_map/ppermute | solution.py:403
  38.4 0.0 copy-start.8
  38.4 0.6 collective-permute-start.22
  38.9 4.1 %collective-permute-done.14.theirs = bf16[256,512]{1,0:T(8,128)(2,1)S(1)} collective-permute-done((bf16[256,512]{1,0:T(8,128)(2,1)S(1)}, bf16[256,512]{1,0:T(8,128)(2,1)S(1)}, u32[]{:S(2)}, u32[]{:S(2)}) %collective-permute-start.14) | collective-permute-done | bytes 262176 | tf_op jit(solution)/shard_map/ppermute | solution.py:403
  43.1 0.0 copy-start.16
  43.1 1.0 %shard_map.234 = (bf16[256,512]{1,0:T(8,128)(2,1)S(1)}, bf16[384,512]{1,0:T(8,128)(2,1)S(1)}) custom-call(bf16[256,512]{1,0:T(8,128)(2,1)S(1)} %get-tuple-element.39.mesh, bf16[256,512]{1,0:T(8,128)(2,1)S(1)} %shard_map.232.after.mine, bf16[256,512]{1,0:T(8,128)(2,1)S(1)} %collective-permute-done.14.theirs, f32[1,512]{1,0:T(1,128)S(1)} %bitcast.4, ...), custom_call_target="tpu_custom_call" | custom-call | flops 402653184 | bytes 4458496 | tf_op jit(solution)/shard_map/pallas_call | solution.py:62
  44.1 0.1 collective-permute-start.20
  44.2 0.7 collective-permute-done.22.round_
  44.9 0.8 %collective-permute-done.20.theirs = bf16[256,512]{1,0:T(8,128)(2,1)S(1)} collective-permute-done((bf16[256,512]{1,0:T(8,128)(2,1)S(1)}, bf16[256,512]{1,0:T(8,128)(2,1)S(1)}, u32[]{:S(2)}, u32[]{:S(2)}) %collective-permute-start.20) | collective-permute-done | bytes 262176 | tf_op jit(solution)/shard_map/ppermute | solution.py:418
  45.7 0.3 shard_map.236
  46.0 0.2 collective-permute-start.23
  46.1 1.3 %collective-permute-start.24 = (bf16[32,512]{1,0:T(8,128)(2,1)S(1)}, bf16[32,512]{1,0:T(8,128)(2,1)S(1)}, u32[]{:S(2)}, u32[]{:S(2)}) collective-permute-start(bf16[32,512]{1,0:T(8,128)(2,1)S(1)} %get-tuple-element.53), channel_id=1, source_target_pairs={{2,6},{3,11},{5,1},{6,10},{7,15},{8,0},{9,5},{10,14},{12,4},{13,9}... | collective-permute-start | bytes 98312 | tf_op jit(solution)/shard_map/ppermute | solution.py:414
  47.4 0.8 %collective-permute-start.25 = (bf16[32,512]{1,0:T(8,128)(2,1)S(1)}, bf16[32,512]{1,0:T(8,128)(2,1)S(1)}, u32[]{:S(2)}, u32[]{:S(2)}) collective-permute-start(bf16[32,512]{1,0:T(8,128)(2,1)S(1)} %get-tuple-element.53), channel_id=1, source_target_pairs={{2,4},{3,9},{5,3},{6,8},{7,13},{8,2},{9,7},{10,12},{12,6},{13,11},... | collective-permute-start | bytes 98312 | tf_op jit(solution)/shard_map/ppermute | solution.py:414
  48.9 6.8 %collective-permute-start.30 = (bf16[384,512]{1,0:T(8,128)(2,1)S(1)}, bf16[384,512]{1,0:T(8,128)(2,1)S(1)}, u32[]{:S(2)}, u32[]{:S(2)}) collective-permute-start(bf16[384,512]{1,0:T(8,128)(2,1)S(1)} %get-tuple-element.58.w0), channel_id=1, source_target_pairs={{0,2},{1,3},{2,0},{3,1},{4,6},{5,7},{6,4},{7,5},{8,10},{9,11},{10,... | collective-permute-start | bytes 1179656 | tf_op jit(solution)/shard_map/ppermute | solution.py:403
  55.8 1.1 %collective-permute-start.26 = (bf16[64,512]{1,0:T(8,128)(2,1)S(1)}, bf16[64,512]{1,0:T(8,128)(2,1)S(1)}, u32[]{:S(2)}, u32[]{:S(2)}) collective-permute-start(bf16[64,512]{1,0:T(8,128)(2,1)S(1)} %shard_map.238.halo), channel_id=1, source_target_pairs={{0,1},{1,0},{2,3},{3,2},{4,5},{5,4},{6,7},{7,6},{8,9},{9,8},{10,11... | collective-permute-start | bytes 196616 | tf_op jit(solution)/shard_map/ppermute | solution.py:418
  56.9 2.6 %shard_map.237 = (bf16[1536,512]{1,0:T(8,128)(2,1)S(1)}, f32[1024,512]{1,0:T(8,128)S(1)}, bf16[512,512]{1,0:T(8,128)(2,1)S(1)}, bf16[512,512]{1,0:T(8,128)(2,1)S(1)}) custom-call(bf16[2048,512]{1,0:T(8,128)(2,1)S(1)} %get-tuple-element.45.emb, bf16[512,512]{1,0:T(8,128)(2,1)S(1)} %get-tuple-element.47.full, s32[2,2048]{1,0:T(2,128)S(1)} %copy-done.16, ...), custom_call_target="tpu_custom_call" | custom-call | flops 1610612736 | bytes 10240000 | tf_op jit(solution)/shard_map/pallas_call | solution.py:62
  59.5 0.0 copy-start.9
  59.6 5.9 %shard_map.239 = (bf16[256,512]{1,0:T(8,128)(2,1)S(1)}, bf16[256,512]{1,0:T(8,128)(2,1)S(1)}) custom-call(bf16[2048,512]{1,0:T(8,128)(2,1)S(1)} %get-tuple-element.45.emb, s32[2,2048]{1,0:T(2,128)S(1)} %copy-done.16, f32[1,512]{1,0:T(1,128)S(1)} %bitcast.7, bf16[1536,512]{1,0:T(8,128)(2,1)S(1)} %get-tuple-element.49.table, ...), custom_call_target="tpu_custom_call" | custom-call | flops 3489660928 | bytes 7489540 | tf_op jit(solution)/shard_map/pallas_call | solution.py:62
  65.4 0.1 collective-permute-start.27
  65.5 0.5 collective-permute-start.29
  66.0 0.1 collective-permute-start.31
  66.1 0.9 %collective-permute-done.27.theirs = bf16[256,512]{1,0:T(8,128)(2,1)S(1)} collective-permute-done((bf16[256,512]{1,0:T(8,128)(2,1)S(1)}, bf16[256,512]{1,0:T(8,128)(2,1)S(1)}, u32[]{:S(2)}, u32[]{:S(2)}) %collective-permute-start.27) | collective-permute-done | bytes 262176 | tf_op jit(solution)/shard_map/ppermute | solution.py:418
  67.0 0.1 shard_map.240
  67.1 4.2 %collective-permute-start.28 = (bf16[128,512]{1,0:T(8,128)(2,1)S(1)}, bf16[128,512]{1,0:T(8,128)(2,1)S(1)}, u32[]{:S(2)}, u32[]{:S(2)}) collective-permute-start(bf16[128,512]{1,0:T(8,128)(2,1)S(1)} %get-tuple-element.57), channel_id=1, source_target_pairs={{0,2},{1,3},{2,0},{3,1},{4,6},{5,7},{6,4},{7,5},{8,10},{9,11},{10,... | collective-permute-start | bytes 393224 | tf_op jit(solution)/shard_map/ppermute | solution.py:403
  71.3 4.0 %collective-permute-done.28.theirs = bf16[128,512]{1,0:T(8,128)(2,1)S(1)} collective-permute-done((bf16[128,512]{1,0:T(8,128)(2,1)S(1)}, bf16[128,512]{1,0:T(8,128)(2,1)S(1)}, u32[]{:S(2)}, u32[]{:S(2)}) %collective-permute-start.28) | collective-permute-done | bytes 131104 | tf_op jit(solution)/shard_map/ppermute | solution.py:403
  75.3 1.5 %shard_map.241 = bf16[128,512]{1,0:T(8,128)(2,1)} custom-call(bf16[256,512]{1,0:T(8,128)(2,1)S(1)} %get-tuple-element.44.mine.middle, bf16[128,512]{1,0:T(8,128)(2,1)S(1)} %get-tuple-element.56.mine, bf16[128,512]{1,0:T(8,128)(2,1)S(1)} %collective-permute-done.28.theirs, f32[1,512]{1,0:T(1,128)S(1)} %bitcast.5, bf16[384,512]{1,0:T(8,128)(2,1)S(1)} %get-tuple-element.58.w0, ...), custom_call_target="tpu_custom_call" | custom-call | flops 201326592 | bytes 2230272 | tf_op jit(solution)/shard_map/pallas_call | solution.py:62
  (60 shorter events, 0.2 us)
Async XLA Ops:
  0.0 0.9 %copy-start = (bf16[512,128]{1,0:T(8,128)(2,1)S(1)}, bf16[512,128]{1,0:T(8,128)(2,1)}, u32[]{:S(2)}) copy-start(bf16[512,128]{1,0:T(8,128)(2,1)} %refs_0_.1) | copy-start | bytes 393220
  0.0 0.9 %copy-start.7 = (s32[1,4,64]{2,1,0:T(4,128)S(1)}, s32[1,4,64]{2,1,0:T(4,128)}, u32[]{:S(2)}) copy-start(s32[1,4,64]{2,1,0:T(4,128)} %send.2) | copy-start | bytes 3076
  0.0 1.1 %copy-start.1 = (bf16[384,512]{1,0:T(8,128)(2,1)S(1)}, bf16[384,512]{1,0:T(8,128)(2,1)}, u32[]{:S(2)}) copy-start(bf16[384,512]{1,0:T(8,128)(2,1)} %o_in.1) | copy-start | bytes 1179652
  0.0 1.1 %copy-start.4 = (bf16[128,512]{1,0:T(8,128)(2,1)S(1)}, bf16[128,512]{1,0:T(8,128)(2,1)}, u32[]{:S(2)}) copy-start(bf16[128,512]{1,0:T(8,128)(2,1)} %o_out.1) | copy-start | bytes 393220
  0.0 10.7 %copy-start.3 = (bf16[512,128]{1,0:T(8,128)(2,1)S(1)}, bf16[512,128]{1,0:T(8,128)(2,1)}, u32[]{:S(2)}) copy-start(bf16[512,128]{1,0:T(8,128)(2,1)} %refs_1_.1) | copy-start | bytes 393220
  0.0 13.4 %copy-start.11 = (bf16[256,512]{1,0:T(8,128)(2,1)S(1)}, bf16[256,512]{1,0:T(8,128)(2,1)}, u32[]{:S(2)}) copy-start(bf16[256,512]{1,0:T(8,128)(2,1)} %e_in.1) | copy-start | bytes 786436
  0.0 13.4 %copy-start.12 = (bf16[128,512]{1,0:T(8,128)(2,1)S(1)}, bf16[128,512]{1,0:T(8,128)(2,1)}, u32[]{:S(2)}) copy-start(bf16[128,512]{1,0:T(8,128)(2,1)} %e_out.1) | copy-start | bytes 393220
  0.0 13.3 %copy-start.10 = (bf16[384,512]{1,0:T(8,128)(2,1)S(1)}, bf16[384,512]{1,0:T(8,128)(2,1)}, u32[]{:S(2)}) copy-start(bf16[384,512]{1,0:T(8,128)(2,1)} %p_in.1) | copy-start | bytes 1179652
  0.0 13.3 %copy-start.13 = (bf16[128,512]{1,0:T(8,128)(2,1)S(1)}, bf16[128,512]{1,0:T(8,128)(2,1)}, u32[]{:S(2)}) copy-start(bf16[128,512]{1,0:T(8,128)(2,1)} %p_out.1) | copy-start | bytes 393220
  0.1 13.3 %copy-start.15 = (f32[4,1024]{1,0:T(4,128)S(1)}, f32[4,1024]{1,0:T(4,128)}, u32[]{:S(2)}) copy-start(f32[4,1024]{1,0:T(4,128)} %egeom.1) | copy-start | bytes 49156
  0.1 13.3 %copy-start.17 = (f32[4,512]{1,0:T(4,128)S(1)}, f32[4,512]{1,0:T(4,128)}, u32[]{:S(2)}) copy-start(f32[4,512]{1,0:T(4,128)} %egeo.1) | copy-start | bytes 24580
  0.1 13.3 %copy-start.14 = (f32[4,2048]{1,0:T(4,128)S(1)}, f32[4,2048]{1,0:T(4,128)}, u32[]{:S(2)}) copy-start(f32[4,2048]{1,0:T(4,128)} %pgeom.1) | copy-start | bytes 98308
  0.1 13.3 %copy-start.18 = (f32[4,512]{1,0:T(4,128)S(1)}, f32[4,512]{1,0:T(4,128)}, u32[]{:S(2)}) copy-start(f32[4,512]{1,0:T(4,128)} %pgeo.1) | copy-start | bytes 24580
  1.1 19.9 %copy-start.19 = (s32[2,1024]{1,0:T(2,128)S(1)}, s32[2,1024]{1,0:T(2,128)}, u32[]{:S(2)}) copy-start(s32[2,1024]{1,0:T(2,128)} %edges.3) | copy-start | bytes 24580
  1.1 19.9 %copy-start.20 = (f32[512]{0:T(512)S(1)}, f32[512]{0:T(512)}, u32[]{:S(2)}) copy-start(f32[512]{0:T(512)} %param.44) | copy-start | bytes 6148
  1.4 9.9 %collective-permute-start.8 = (bf16[256,512]{1,0:T(8,128)(2,1)S(1)}, bf16[256,512]{1,0:T(8,128)(2,1)S(1)}, u32[]{:S(2)}, u32[]{:S(2)}) collective-permute-start(bf16[256,512]{1,0:T(8,128)(2,1)S(1)} %get-tuple-element.38), channel_id=1, source_target_pairs={{0,2},{1,3},{2,0},{3,1},{4,6},{5,7},{6,4},{7,5},{8,10},{9,11},{10,... | collective-permute-start | bytes 786440 | tf_op jit(solution)/shard_map/ppermute | solution.py:403
  4.4 4.8 %collective-permute-start = (bf16[64,128]{1,0:T(8,128)(2,1)S(1)}, bf16[64,128]{1,0:T(8,128)(2,1)S(1)}, u32[]{:S(2)}, u32[]{:S(2)}) collective-permute-start(bf16[64,128]{1,0:T(8,128)(2,1)S(1)} %get-tuple-element.32), channel_id=1, source_target_pairs={{0,4},{4,0},{8,12},{12,8},{1,5},{5,1},{9,13},{13,9},{2,6},{6,2},{1... | collective-permute-start | bytes 49160 | tf_op jit(solution)/shard_map/ppermute | solution.py:483
  6.0 4.7 %collective-permute-start.1 = (bf16[64,128]{1,0:T(8,128)(2,1)S(1)}, bf16[64,128]{1,0:T(8,128)(2,1)S(1)}, u32[]{:S(2)}, u32[]{:S(2)}) collective-permute-start(bf16[64,128]{1,0:T(8,128)(2,1)S(1)} %get-tuple-element.33), channel_id=1, source_target_pairs={{0,8},{4,12},{8,0},{12,4},{1,9},{5,13},{9,1},{13,5},{2,10},{6,14},... | collective-permute-start | bytes 49160 | tf_op jit(solution)/shard_map/ppermute | solution.py:483
  8.6 2.1 %collective-permute-start.2 = (bf16[64,128]{1,0:T(8,128)(2,1)S(1)}, bf16[64,128]{1,0:T(8,128)(2,1)S(1)}, u32[]{:S(2)}, u32[]{:S(2)}) collective-permute-start(bf16[64,128]{1,0:T(8,128)(2,1)S(1)} %get-tuple-element.34), channel_id=1, source_target_pairs={{4,8},{8,4},{5,9},{9,5},{6,10},{10,6},{7,11},{11,7},{20,24},{24,20... | collective-permute-start | bytes 49160 | tf_op jit(solution)/shard_map/ppermute | solution.py:483
  10.7 7.6 %collective-permute-start.3 = (bf16[1216,128]{1,0:T(8,128)(2,1)S(1)}, bf16[1216,128]{1,0:T(8,128)(2,1)S(1)}, u32[]{:S(2)}, u32[]{:S(2)}) collective-permute-start(bf16[1216,128]{1,0:T(8,128)(2,1)S(1)} %shard_map.228.after.l0), channel_id=1, source_target_pairs={{0,2},{1,3},{2,0},{3,1},{4,6},{5,7},{6,4},{7,5},{8,10},{9,11},{10,... | collective-permute-start | bytes 933896 | tf_op jit(solution)/shard_map/ppermute | solution.py:403
  11.3 7.7 %collective-permute-start.9 = (bf16[256,512]{1,0:T(8,128)(2,1)S(1)}, bf16[256,512]{1,0:T(8,128)(2,1)S(1)}, u32[]{:S(2)}, u32[]{:S(2)}) collective-permute-start(bf16[256,512]{1,0:T(8,128)(2,1)S(1)} %collective-permute-done.8.across), channel_id=1, source_target_pairs={{0,16},{16,0},{1,17},{17,1},{2,18},{18,2},{3,19},{19,3},{4,20},{20... | collective-permute-start | bytes 786440 | tf_op jit(solution)/shard_map/ppermute | solution.py:423
  12.9 6.2 %collective-permute-start.4 = (bf16[1216,128]{1,0:T(8,128)(2,1)S(1)}, bf16[1216,128]{1,0:T(8,128)(2,1)S(1)}, u32[]{:S(2)}, u32[]{:S(2)}) collective-permute-start(bf16[1216,128]{1,0:T(8,128)(2,1)S(1)} %shard_map.228.after.l0), channel_id=1, source_target_pairs={{0,1},{1,0},{2,3},{3,2},{4,5},{5,4},{6,7},{7,6},{8,9},{9,8},{10,11... | collective-permute-start | bytes 933896 | tf_op jit(solution)/shard_map/ppermute | solution.py:418
  12.9 7.2 %collective-permute-start.6 = (bf16[384,512]{1,0:T(8,128)(2,1)S(1)}, bf16[384,512]{1,0:T(8,128)(2,1)S(1)}, u32[]{:S(2)}, u32[]{:S(2)}) collective-permute-start(bf16[384,512]{1,0:T(8,128)(2,1)S(1)} %copy-done.1), channel_id=1, source_target_pairs={{0,1},{1,0},{2,3},{3,2},{4,5},{5,4},{6,7},{7,6},{8,9},{9,8},{10,11... | collective-permute-start | bytes 1179656 | tf_op jit(solution)/shard_map/ppermute | solution.py:418
  13.4 5.1 %collective-permute-start.7 = (bf16[128,512]{1,0:T(8,128)(2,1)S(1)}, bf16[128,512]{1,0:T(8,128)(2,1)S(1)}, u32[]{:S(2)}, u32[]{:S(2)}) collective-permute-start(bf16[128,512]{1,0:T(8,128)(2,1)S(1)} %copy-done.4), channel_id=1, source_target_pairs={{0,1},{1,0},{2,3},{3,2},{4,5},{5,4},{6,7},{7,6},{8,9},{9,8},{10,11... | collective-permute-start | bytes 393224 | tf_op jit(solution)/shard_map/ppermute | solution.py:418
  18.4 2.7 %collective-permute-start.5 = (bf16[1216,128]{1,0:T(8,128)(2,1)S(1)}, bf16[1216,128]{1,0:T(8,128)(2,1)S(1)}, u32[]{:S(2)}, u32[]{:S(2)}) collective-permute-start(bf16[1216,128]{1,0:T(8,128)(2,1)S(1)} %get-tuple-element.37), channel_id=1, source_target_pairs={{0,1},{1,0},{2,3},{3,2},{4,5},{5,4},{6,7},{7,6},{8,9},{9,8},{10,11... | collective-permute-start | bytes 933896 | tf_op jit(solution)/shard_map/ppermute | solution.py:418
  18.4 2.6 %collective-permute-start.10 = (bf16[256,512]{1,0:T(8,128)(2,1)S(1)}, bf16[256,512]{1,0:T(8,128)(2,1)S(1)}, u32[]{:S(2)}, u32[]{:S(2)}) collective-permute-start(bf16[256,512]{1,0:T(8,128)(2,1)S(1)} %collective-permute-done.8.across), channel_id=1, source_target_pairs={{0,1},{1,0},{2,3},{3,2},{4,5},{5,4},{6,7},{7,6},{8,9},{9,8},{10,11... | collective-permute-start | bytes 786440 | tf_op jit(solution)/shard_map/ppermute | solution.py:418
  18.9 2.1 %collective-permute-start.11 = (bf16[256,512]{1,0:T(8,128)(2,1)S(1)}, bf16[256,512]{1,0:T(8,128)(2,1)S(1)}, u32[]{:S(2)}, u32[]{:S(2)}) collective-permute-start(bf16[256,512]{1,0:T(8,128)(2,1)S(1)} %collective-permute-done.9.round_), channel_id=1, source_target_pairs={{0,1},{1,0},{2,3},{3,2},{4,5},{5,4},{6,7},{7,6},{8,9},{9,8},{10,11... | collective-permute-start | bytes 786440 | tf_op jit(solution)/shard_map/ppermute | solution.py:418
  19.0 19.9 %collective-permute-start.15 = (bf16[896,512]{1,0:T(8,128)(2,1)S(1)}, bf16[896,512]{1,0:T(8,128)(2,1)S(1)}, u32[]{:S(2)}, u32[]{:S(2)}) collective-permute-start(bf16[896,512]{1,0:T(8,128)(2,1)S(1)} %get-tuple-element.36.weights.w0), channel_id=1, source_target_pairs={{0,1},{1,0},{2,3},{3,2},{4,5},{5,4},{6,7},{7,6},{8,9},{9,8},{10,11... | collective-permute-start | bytes 2752520 | tf_op jit(solution)/shard_map/ppermute | solution.py:418
  20.1 7.4 %collective-permute-start.16 = (bf16[192,512]{1,0:T(8,128)(2,1)S(1)}, bf16[192,512]{1,0:T(8,128)(2,1)S(1)}, u32[]{:S(2)}, u32[]{:S(2)}) collective-permute-start(bf16[192,512]{1,0:T(8,128)(2,1)S(1)} %get-tuple-element.43), channel_id=1, source_target_pairs={{0,2},{1,3},{2,0},{3,1},{4,6},{5,7},{6,4},{7,5},{8,10},{9,11},{10,... | collective-permute-start | bytes 589832 | tf_op jit(solution)/shard_map/ppermute | solution.py:403
  25.8 17.2 %copy-start.2 = (bf16[256,512]{1,0:T(8,128)(2,1)S(1)}, bf16[256,512]{1,0:T(8,128)(2,1)}, u32[]{:S(2)}) copy-start(bf16[256,512]{1,0:T(8,128)(2,1)} %n_in.1) | copy-start | bytes 786436
  25.8 17.2 %copy-start.5 = (bf16[128,512]{1,0:T(8,128)(2,1)S(1)}, bf16[128,512]{1,0:T(8,128)(2,1)}, u32[]{:S(2)}) copy-start(bf16[128,512]{1,0:T(8,128)(2,1)} %n_out.1) | copy-start | bytes 393220
  25.9 17.2 %copy-start.6 = (f32[512]{0:T(512)S(1)}, f32[512]{0:T(512)}, u32[]{:S(2)}) copy-start(f32[512]{0:T(512)} %param.45) | copy-start | bytes 6148
  25.9 1.4 %collective-permute-start.12 = (bf16[128,512]{1,0:T(8,128)(2,1)S(1)}, bf16[128,512]{1,0:T(8,128)(2,1)S(1)}, u32[]{:S(2)}, u32[]{:S(2)}) collective-permute-start(bf16[128,512]{1,0:T(8,128)(2,1)S(1)} %get-tuple-element.41), channel_id=1, source_target_pairs={{0,1},{1,0},{2,3},{3,2},{4,5},{5,4},{6,7},{7,6},{8,9},{9,8},{10,11... | collective-permute-start | bytes 393224 | tf_op jit(solution)/shard_map/ppermute | solution.py:418
  25.9 1.5 %collective-permute-start.13 = (bf16[128,512]{1,0:T(8,128)(2,1)S(1)}, bf16[128,512]{1,0:T(8,128)(2,1)S(1)}, u32[]{:S(2)}, u32[]{:S(2)}) collective-permute-start(bf16[128,512]{1,0:T(8,128)(2,1)S(1)} %get-tuple-element.42), channel_id=1, source_target_pairs={{0,1},{1,0},{2,3},{3,2},{4,5},{5,4},{6,7},{7,6},{8,9},{9,8},{10,11... | collective-permute-start | bytes 393224 | tf_op jit(solution)/shard_map/ppermute | solution.py:418
  27.6 7.2 %collective-permute-start.17 = (bf16[192,512]{1,0:T(8,128)(2,1)S(1)}, bf16[192,512]{1,0:T(8,128)(2,1)S(1)}, u32[]{:S(2)}, u32[]{:S(2)}) collective-permute-start(bf16[192,512]{1,0:T(8,128)(2,1)S(1)} %shard_map.233.w2), channel_id=1, source_target_pairs={{0,16},{16,0},{1,17},{17,1},{2,18},{18,2},{3,19},{19,3},{4,20},{20... | collective-permute-start | bytes 589832 | tf_op jit(solution)/shard_map/ppermute | solution.py:423
  29.2 9.2 %collective-permute-start.21 = (bf16[256,512]{1,0:T(8,128)(2,1)S(1)}, bf16[256,512]{1,0:T(8,128)(2,1)S(1)}, u32[]{:S(2)}, u32[]{:S(2)}) collective-permute-start(bf16[256,512]{1,0:T(8,128)(2,1)S(1)} %get-tuple-element.46), channel_id=1, source_target_pairs={{0,2},{1,3},{2,0},{3,1},{4,6},{5,7},{6,4},{7,5},{8,10},{9,11},{10,... | collective-permute-start | bytes 786440 | tf_op jit(solution)/shard_map/ppermute | solution.py:403
  30.4 12.7 %collective-permute-start.14 = (bf16[256,512]{1,0:T(8,128)(2,1)S(1)}, bf16[256,512]{1,0:T(8,128)(2,1)S(1)}, u32[]{:S(2)}, u32[]{:S(2)}) collective-permute-start(bf16[256,512]{1,0:T(8,128)(2,1)S(1)} %shard_map.232.after.mine), channel_id=1, source_target_pairs={{0,2},{1,3},{2,0},{3,1},{4,6},{5,7},{6,4},{7,5},{8,10},{9,11},{10,... | collective-permute-start | bytes 786440 | tf_op jit(solution)/shard_map/ppermute | solution.py:403
  31.2 7.7 %collective-permute-start.18 = (bf16[192,512]{1,0:T(8,128)(2,1)S(1)}, bf16[192,512]{1,0:T(8,128)(2,1)S(1)}, u32[]{:S(2)}, u32[]{:S(2)}) collective-permute-start(bf16[192,512]{1,0:T(8,128)(2,1)S(1)} %shard_map.233.w2), channel_id=1, source_target_pairs={{0,1},{1,0},{2,3},{3,2},{4,5},{5,4},{6,7},{7,6},{8,9},{9,8},{10,11... | collective-permute-start | bytes 589832 | tf_op jit(solution)/shard_map/ppermute | solution.py:418
  34.8 8.3 %collective-permute-start.19 = (bf16[192,512]{1,0:T(8,128)(2,1)S(1)}, bf16[192,512]{1,0:T(8,128)(2,1)S(1)}, u32[]{:S(2)}, u32[]{:S(2)}) collective-permute-start(bf16[192,512]{1,0:T(8,128)(2,1)S(1)} %collective-permute-done.17.w3), channel_id=1, source_target_pairs={{0,1},{1,0},{2,3},{3,2},{4,5},{5,4},{6,7},{7,6},{8,9},{9,8},{10,11... | collective-permute-start | bytes 589832 | tf_op jit(solution)/shard_map/ppermute | solution.py:418
  38.4 7.4 %copy-start.8 = (s32[1,4,32]{2,1,0:T(4,128)S(1)}, s32[1,4,32]{2,1,0:T(4,128)}, u32[]{:S(2)}) copy-start(s32[1,4,32]{2,1,0:T(4,128)} %send.3) | copy-start | bytes 1540
  38.4 6.6 %collective-permute-start.22 = (bf16[256,512]{1,0:T(8,128)(2,1)S(1)}, bf16[256,512]{1,0:T(8,128)(2,1)S(1)}, u32[]{:S(2)}, u32[]{:S(2)}) collective-permute-start(bf16[256,512]{1,0:T(8,128)(2,1)S(1)} %shard_map.235.across), channel_id=1, source_target_pairs={{0,16},{16,0},{1,17},{17,1},{2,18},{18,2},{3,19},{19,3},{4,20},{20... | collective-permute-start | bytes 786440 | tf_op jit(solution)/shard_map/ppermute | solution.py:423
  43.1 13.9 %copy-start.16 = (s32[2,2048]{1,0:T(2,128)S(1)}, s32[2,2048]{1,0:T(2,128)}, u32[]{:S(2)}) copy-start(s32[2,2048]{1,0:T(2,128)} %edges.5) | copy-start | bytes 49156
  44.1 1.6 %collective-permute-start.20 = (bf16[256,512]{1,0:T(8,128)(2,1)S(1)}, bf16[256,512]{1,0:T(8,128)(2,1)S(1)}, u32[]{:S(2)}, u32[]{:S(2)}) collective-permute-start(bf16[256,512]{1,0:T(8,128)(2,1)S(1)} %get-tuple-element.44.mine.middle), channel_id=1, source_target_pairs={{0,1},{1,0},{2,3},{3,2},{4,5},{5,4},{6,7},{7,6},{8,9},{9,8},{10,11... | collective-permute-start | bytes 786440 | tf_op jit(solution)/shard_map/ppermute | solution.py:418
  46.0 11.0 %collective-permute-start.23 = (bf16[512,512]{1,0:T(8,128)(2,1)S(1)}, bf16[512,512]{1,0:T(8,128)(2,1)S(1)}, u32[]{:S(2)}, u32[]{:S(2)}) collective-permute-start(bf16[512,512]{1,0:T(8,128)(2,1)S(1)} %get-tuple-element.48.pair), channel_id=1, source_target_pairs={{0,1},{1,0},{2,3},{3,2},{4,5},{5,4},{6,7},{7,6},{8,9},{9,8},{10,11... | collective-permute-start | bytes 1572872 | tf_op jit(solution)/shard_map/ppermute | solution.py:418
  46.1 9.6 %collective-permute-start.24 = (bf16[32,512]{1,0:T(8,128)(2,1)S(1)}, bf16[32,512]{1,0:T(8,128)(2,1)S(1)}, u32[]{:S(2)}, u32[]{:S(2)}) collective-permute-start(bf16[32,512]{1,0:T(8,128)(2,1)S(1)} %get-tuple-element.53), channel_id=1, source_target_pairs={{2,6},{3,11},{5,1},{6,10},{7,15},{8,0},{9,5},{10,14},{12,4},{13,9}... | collective-permute-start | bytes 98312 | tf_op jit(solution)/shard_map/ppermute | solution.py:414
  47.4 8.4 %collective-permute-start.25 = (bf16[32,512]{1,0:T(8,128)(2,1)S(1)}, bf16[32,512]{1,0:T(8,128)(2,1)S(1)}, u32[]{:S(2)}, u32[]{:S(2)}) collective-permute-start(bf16[32,512]{1,0:T(8,128)(2,1)S(1)} %get-tuple-element.53), channel_id=1, source_target_pairs={{2,4},{3,9},{5,3},{6,8},{7,13},{8,2},{9,7},{10,12},{12,6},{13,11},... | collective-permute-start | bytes 98312 | tf_op jit(solution)/shard_map/ppermute | solution.py:414
  48.9 17.1 %collective-permute-start.30 = (bf16[384,512]{1,0:T(8,128)(2,1)S(1)}, bf16[384,512]{1,0:T(8,128)(2,1)S(1)}, u32[]{:S(2)}, u32[]{:S(2)}) collective-permute-start(bf16[384,512]{1,0:T(8,128)(2,1)S(1)} %get-tuple-element.58.w0), channel_id=1, source_target_pairs={{0,2},{1,3},{2,0},{3,1},{4,6},{5,7},{6,4},{7,5},{8,10},{9,11},{10,... | collective-permute-start | bytes 1179656 | tf_op jit(solution)/shard_map/ppermute | solution.py:403
  55.8 3.7 %collective-permute-start.26 = (bf16[64,512]{1,0:T(8,128)(2,1)S(1)}, bf16[64,512]{1,0:T(8,128)(2,1)S(1)}, u32[]{:S(2)}, u32[]{:S(2)}) collective-permute-start(bf16[64,512]{1,0:T(8,128)(2,1)S(1)} %shard_map.238.halo), channel_id=1, source_target_pairs={{0,1},{1,0},{2,3},{3,2},{4,5},{5,4},{6,7},{7,6},{8,9},{9,8},{10,11... | collective-permute-start | bytes 196616 | tf_op jit(solution)/shard_map/ppermute | solution.py:418
  56.9 2.6 %copy-start.21 = (f32[512]{0:T(512)S(1)}, f32[512]{0:T(512)}, u32[]{:S(2)}) copy-start(f32[512]{0:T(512)} %param.46) | copy-start | bytes 6148
  59.5 15.8 %copy-start.9 = (f32[512]{0:T(512)S(1)}, f32[512]{0:T(512)}, u32[]{:S(2)}) copy-start(f32[512]{0:T(512)} %param.47) | copy-start | bytes 6148
  65.4 1.6 %collective-permute-start.27 = (bf16[256,512]{1,0:T(8,128)(2,1)S(1)}, bf16[256,512]{1,0:T(8,128)(2,1)S(1)}, u32[]{:S(2)}, u32[]{:S(2)}) collective-permute-start(bf16[256,512]{1,0:T(8,128)(2,1)S(1)} %get-tuple-element.55), channel_id=1, source_target_pairs={{0,1},{1,0},{2,3},{3,2},{4,5},{5,4},{6,7},{7,6},{8,9},{9,8},{10,11... | collective-permute-start | bytes 786440 | tf_op jit(solution)/shard_map/ppermute | solution.py:418
  65.5 5.8 %collective-permute-start.29 = (bf16[384,512]{1,0:T(8,128)(2,1)S(1)}, bf16[384,512]{1,0:T(8,128)(2,1)S(1)}, u32[]{:S(2)}, u32[]{:S(2)}) collective-permute-start(bf16[384,512]{1,0:T(8,128)(2,1)S(1)} %get-tuple-element.58.w0), channel_id=1, source_target_pairs={{0,1},{1,0},{2,3},{3,2},{4,5},{5,4},{6,7},{7,6},{8,9},{9,8},{10,11... | collective-permute-start | bytes 1179656 | tf_op jit(solution)/shard_map/ppermute | solution.py:418
  66.0 5.3 %collective-permute-start.31 = (bf16[384,512]{1,0:T(8,128)(2,1)S(1)}, bf16[384,512]{1,0:T(8,128)(2,1)S(1)}, u32[]{:S(2)}, u32[]{:S(2)}) collective-permute-start(bf16[384,512]{1,0:T(8,128)(2,1)S(1)} %collective-permute-done.30.w2), channel_id=1, source_target_pairs={{0,1},{1,0},{2,3},{3,2},{4,5},{5,4},{6,7},{7,6},{8,9},{9,8},{10,11... | collective-permute-start | bytes 1179656 | tf_op jit(solution)/shard_map/ppermute | solution.py:418
  67.1 8.3 %collective-permute-start.28 = (bf16[128,512]{1,0:T(8,128)(2,1)S(1)}, bf16[128,512]{1,0:T(8,128)(2,1)S(1)}, u32[]{:S(2)}, u32[]{:S(2)}) collective-permute-start(bf16[128,512]{1,0:T(8,128)(2,1)S(1)} %get-tuple-element.57), channel_id=1, source_target_pairs={{0,2},{1,3},{2,0},{3,1},{4,6},{5,7},{6,4},{7,5},{8,10},{9,11},{10,... | collective-permute-start | bytes 393224 | tf_op jit(solution)/shard_map/ppermute | solution.py:403

commit v10 on v8

--- a/solution.py
+++ b/solution.py
@@ -129,9 +129,9 @@
     token[...] = jnp.zeros(token.shape, token.dtype)
 
 
-def first_pack_kernel(plan, grid, send, w_in, w_out, token, half, *outs):
+def first_pack_kernel(plan, grid, send, w_in, w_out, n_in, n_out, token, half, *outs):
     place = 0
-    for source in (w_in, w_out):
+    for source in (w_in, w_out, n_in, n_out):
         rows = source.shape[0] // 2
         begin = pl.multiple_of(lax.axis_index("groups") * rows, 64)
         half[place : place + rows, :] = source[pl.ds(begin, rows), :]
@@ -146,31 +146,31 @@
             out[begin : begin + STEP, :] = embed_rows(geom[:, begin : begin + STEP], geo[...])
 
 
-def cross_kernel(parts, weights, lat, lat_out, *crossing):
+def cross_kernel(first, k_in, weights, lat, lat_out, crossing):
     lat_out[...] = lat[...]
-    first = 0
-    for stack, out in zip(parts, crossing):
-        place = 0
-        for rows in stack:
-            half = rows // 2
-            begin = pl.multiple_of(first + lax.axis_index("groups") * half, 64)
-            out[place : place + half, :] = weights[pl.ds(begin, half), :]
-            first, place = first + rows, place + half
-
-
-def relay_kernel(across, round_, w_in, w_out, *refs):
-    *parts, out, pair, packed = refs
+    place = 0
+    for rows in (k_in, weights.shape[0] - first - k_in):
+        half = rows // 2
+        begin = pl.multiple_of(first + lax.axis_index("groups") * half, 64)
+        crossing[place : place + half, :] = weights[pl.ds(begin, half), :]
+        first, place = first + rows, place + half
+
+
+def relay_kernel(w_in, w_out, *refs):
+    *parts, out, packed = refs
     stack_into(out, parts)
-    stack_into(pair, (across, round_))
     stack_into(packed, (w_in, w_out))
-
-
-def hold_kernel(source, after, out):
-    out[...] = source[...]
 
 
 def concat_kernel(*refs):
     stack_into(refs[-1], refs[:-1])
+
+
+def split_kernel(source, *outs):
+    first = 0
+    for out in outs:
+        out[...] = source[first : first + out.shape[0], :]
+        first += out.shape[0]
 
 
 def put_shard(target, source, first, step, part=0, parts=1):
@@ -301,16 +301,19 @@
     return (mine.astype(F32) + theirs.astype(F32)).astype(BF16)
 
 
-def add_kernel(mine, first, second, out):
+def add_kernel(mine, first, second, held_in, node_in, out, held, node):
+    held[...] = held_in[...]
+    node[...] = node_in[...]
     rows = first.shape[0]
     out[:rows, :] = add(mine[:rows, :], first[...])
     out[rows:, :] = add(mine[rows:, :], second[...])
 
 
 def node_kernel(
-    plan, k_in, k_out, mesh, mine, theirs, gain, w0, w1, w2, w3, w4, w5, send, out, *rest
+    plan, k_in, k_out, mesh, mine, theirs, gain, w0, w1, w2, w3, w4, w5, across, round_, send, out, pair, *rest
 ):
     outs, stack = rest[:-1], rest[-1]
+    stack_into(pair, (across, round_))
     put_shard(stack, w0, 0, 0)
     put_shard(stack, w1, 0, 1)
     put_half(stack, k_in, w2, 2, 0)
@@ -417,10 +420,6 @@
 
 def shape(rows, width, dtype=BF16):
     return jax.ShapeDtypeStruct((rows, width), dtype)
-
-
-def call_hold(source, after):
-    return call(hold_kernel, [shape(*source.shape)], [source, after])[0]
 
 
 def padded(rows):
@@ -468,16 +467,17 @@
     (token,) = call(begin_kernel, [shape(16, 128)], [], flops=LONG)
     edge_half, *outgoing = call(
         functools.partial(first_pack_kernel, plan),
-        [shape((k_in + k_out) // 2, d)] + [shape(slots, width)] * len(plan),
-        [grid_lat, grid_send, enc_edge_in, enc_edge_out, token],
-    )
-    edge_across = to_chip(edge_half)
+        [shape((k_in + k_out + n_in + n_out) // 2, d)] + [shape(slots, width)] * len(plan),
+        [grid_lat, grid_send, enc_edge_in, enc_edge_out, enc_node_in, enc_node_out, token],
+    )
+    first_across = to_chip(edge_half)
     halos = [lax.ppermute(v, "dom", entry[0]) for v, entry in zip(outgoing, plan)]
     got = len(plan) * slots
-    (lat,) = call(
-        concat_kernel,
-        [shape(grid_rows + mesh_rows + got, width)],
-        [grid_lat, mesh_lat, *halos],
+    (lat,) = call(concat_kernel, [shape(grid_rows + mesh_rows + got, width)], [grid_lat, mesh_lat, *halos])
+    edge_across, node_across = call(
+        split_kernel,
+        [shape((k_in + k_out) // 2, d), shape((n_in + n_out) // 2, d)],
+        [first_across],
     )
     lat_across = to_chip(lat)
     lat_beside = to_core(lat)
@@ -492,13 +492,13 @@
         ],
         flops=2 * (n_enc + n_proc) * d * 128,
     )
-    lat_sent, node_half, proc_half = call(
-        functools.partial(cross_kernel, ((n_in, n_out), (k_in, k_out))),
-        [shape(lat.shape[0], width), shape((n_in + n_out) // 2, d), shape((k_in + k_out) // 2, d)],
+    lat_sent, proc_half = call(
+        functools.partial(cross_kernel, n_in + n_out, k_in),
+        [shape(lat.shape[0], width), shape((k_in + k_out) // 2, d)],
         [next_w, lat_across],
     )
     lat_both = to_core(lat_sent)
-    node_came, proc_came = to_chip(node_half), to_chip(proc_half)
+    proc_came = to_chip(proc_half)
     next_beside = to_core(next_w)
 
     halo_rows = padded(got)
@@ -521,27 +521,31 @@
         flops=2 * n_enc * d * (3 * d + grid_rows + mesh_rows + halo_rows),
         smem=1,
     )
-    (chip_sum,) = call(add_kernel, [shape(half, d)], [keep, to_core(give), to_core(give_more)])
-    node_across, proc_across = call_hold(node_came, chip_sum), call_hold(proc_came, chip_sum)
-    node_round, proc_round = to_group(node_across), to_group(proc_across)
+    chip_sum, proc_across, node_sent = call(
+        add_kernel,
+        [shape(half, d), shape(*proc_came.shape), shape(*node_across.shape)],
+        [keep, to_core(give), to_core(give_more), proc_came, node_across],
+    )
+    node_round, proc_round = to_group(node_sent), to_group(proc_across)
     node_both = to_core(node_across)
     slots = mesh_send.shape[2]
-    mid_half, *outgoing = call(
+    mid_half, proc_pair, *outgoing = call(
         functools.partial(node_kernel, plan, n_in, n_out),
-        [shape(half, d)] + [shape(slots, d)] * len(plan),
+        [shape(half, d), shape(k_in + k_out, d)] + [shape(slots, d)] * len(plan),
         [
             own_mesh, chip_sum, to_chip(chip_sum), enc_node_gain,
-            next_w, next_beside, node_across, node_round, node_both, to_core(node_round), mesh_send,
+            next_w, next_beside, node_across, node_round, node_both, to_core(node_round),
+            proc_across, proc_round, mesh_send,
         ],
         scratch=[pltpu.VMEM((4 * (n_in + n_out), d), BF16)],
         flops=2 * half * d * 3 * d,
     )
     mid_beside = to_core(mid_half)
     halos = [lax.ppermute(v, "dom", entry[0]) for v, entry in zip(outgoing, plan)]
-    halo, proc_pair, last_w = call(
+    halo, last_w = call(
         relay_kernel,
-        [shape(len(plan) * slots, d), shape(k_in + k_out, d), shape(n_in + n_out, d)],
-        [proc_across, proc_round, proc_node_in, proc_node_out, *halos],
+        [shape(len(plan) * slots, d), shape(n_in + n_out, d)],
+        [proc_node_in, proc_node_out, *halos],
     )
     halo_beside = to_core(halo)
     last_across, last_beside = to_chip(last_w), to_core(last_w)

time: 70.8 us -> 73.7 us (1.041)
  waiting for transfers between devices: 25.1 us -> 28.7 us
    ppermute x3, waiting for transfers between devices: 5.27 us -> 8.55 us  [to_group(): return lax.ppermute(v, 'groups', [(i, count - 1 - i) for i in range(count)])]
    ppermute x7 -> x6, starting transfers between devices: 8.11 us -> 6.63 us  [to_chip(): return lax.ppermute(v, 'sub', [(i, i ^ 2) for i in range(4)])]
    ppermute x3, starting transfers between devices: 1.64 us -> 2.66 us  [to_group(): return lax.ppermute(v, 'groups', [(i, count - 1 - i) for i in range(count)])]
    ppermute x7 -> x6, waiting for transfers between devices: 14.1 us -> 13.3 us  [to_chip(): return lax.ppermute(v, 'sub', [(i, i ^ 2) for i in range(4)])]
    pallas_call x15 -> x14, Pallas kernels: 18.3 us -> 18.3 us  [call(): pl.pallas_call(body, out_shape=tuple(outs), in_specs=specs, out_specs=tup...]
  transfers between devices with their start and end apart: 33 -> 32, of which waited for: 9 -> 12; matrix products, arithmetic and copies ran while one was open for 0% -> 0% of each run, Pallas kernels for 23% -> 21%
where the time goes in v10:
time: 73.7 us; the launch traced here: 73.6 us
  waiting for transfers between devices  28.7 us (39%)
  starting transfers between devices  23.6 us (32%)
  Pallas kernels  18.3 us (25%)
  between operations  1.71 us (2%)
  local copies, waits for them, and re-layouts  1.29 us (2%)
    pallas_call x14, Pallas kernels, call(): pl.pallas_call(body, out_shape=tuple(outs), in_specs=specs, out_specs=tup...  18.3 us
    ppermute x6, waiting for transfers between devices, to_chip(): return lax.ppermute(v, 'sub', [(i, i ^ 2) for i in range(4)])  13.3 us
    ppermute x6, starting transfers between devices, local(): lax.ppermute(v, 'dom', entry[0])  10.9 us
    ppermute x3, waiting for transfers between devices, to_group(): return lax.ppermute(v, 'groups', [(i, count - 1 - i) for i in range(count)])  8.55 us
    ppermute x6, starting transfers between devices, to_chip(): return lax.ppermute(v, 'sub', [(i, i ^ 2) for i in range(4)])  6.63 us
    ppermute x6, waiting for transfers between devices, local(): lax.ppermute(v, 'dom', entry[0])  5.85 us
    ppermute x17, starting transfers between devices, to_core(): return lax.ppermute(v, 'sub', [(i, i ^ 1) for i in range(4)])  3.37 us
    ppermute x3, starting transfers between devices, to_group(): return lax.ppermute(v, 'groups', [(i, count - 1 - i) for i in range(count)])  2.66 us
  transfers between devices with their start and end apart: 32, of which 12 were waited for; matrix products, arithmetic and copies ran while one was open for 0% of the time, Pallas kernels for 21%

profile of v10, /device:TPU:12, one launch (start us, length us, event | category | flops | bytes accessed | tf_op | source)
XLA Modules:
  0.0 73.6 jit_solution(1043030017525833772)
XLA Ops:
  0.1 0.9 %copy-done.3 = bf16[256,512]{1,0:T(8,128)(2,1)S(1)} copy-done((bf16[256,512]{1,0:T(8,128)(2,1)S(1)}, bf16[256,512]{1,0:T(8,128)(2,1)}, u32[]{:S(2)}) %copy-start.3) | copy-done | bytes 262168
  1.0 0.0 copy-done.6
  1.0 0.1 copy-done
  1.0 0.2 copy-done.1
  1.2 0.0 copy-done.7
  1.3 0.0 copy-start.17
  1.3 0.0 copy-start.18
  1.3 0.3 shard_map.227
  1.6 0.0 copy-start.19
  1.6 0.0 copy-start.20
  1.6 1.6 %collective-permute-start.8 = (bf16[448,512]{1,0:T(8,128)(2,1)S(1)}, bf16[448,512]{1,0:T(8,128)(2,1)S(1)}, u32[]{:S(2)}, u32[]{:S(2)}) collective-permute-start(bf16[448,512]{1,0:T(8,128)(2,1)S(1)} %get-tuple-element.44), channel_id=1, source_target_pairs={{0,2},{1,3},{2,0},{3,1},{4,6},{5,7},{6,4},{7,5},{8,10},{9,11},{10,... | collective-permute-start | bytes 1376264 | tf_op jit(solution)/shard_map/ppermute | solution.py:409
  3.2 0.4 collective-permute-start
  3.6 2.6 %collective-permute-start.1 = (bf16[64,128]{1,0:T(8,128)(2,1)S(1)}, bf16[64,128]{1,0:T(8,128)(2,1)S(1)}, u32[]{:S(2)}, u32[]{:S(2)}) collective-permute-start(bf16[64,128]{1,0:T(8,128)(2,1)S(1)} %get-tuple-element.39), channel_id=1, source_target_pairs={{0,8},{4,12},{8,0},{12,4},{1,9},{5,13},{9,1},{13,5},{2,10},{6,14},... | collective-permute-start | bytes 49160 | tf_op jit(solution)/shard_map/ppermute | solution.py:474
  6.2 2.3 %collective-permute-start.2 = (bf16[64,128]{1,0:T(8,128)(2,1)S(1)}, bf16[64,128]{1,0:T(8,128)(2,1)S(1)}, u32[]{:S(2)}, u32[]{:S(2)}) collective-permute-start(bf16[64,128]{1,0:T(8,128)(2,1)S(1)} %get-tuple-element.40), channel_id=1, source_target_pairs={{4,8},{8,4},{5,9},{9,5},{6,10},{10,6},{7,11},{11,7},{20,24},{24,20... | collective-permute-start | bytes 49160 | tf_op jit(solution)/shard_map/ppermute | solution.py:474
  8.6 0.0 collective-permute-done.1.refs_3_
  8.6 3.2 %collective-permute-done.2.refs_4_ = bf16[64,128]{1,0:T(8,128)(2,1)S(1)} collective-permute-done((bf16[64,128]{1,0:T(8,128)(2,1)S(1)}, bf16[64,128]{1,0:T(8,128)(2,1)S(1)}, u32[]{:S(2)}, u32[]{:S(2)}) %collective-permute-start.2) | collective-permute-done | bytes 16416 | tf_op jit(solution)/shard_map/ppermute | solution.py:474
  11.9 0.6 collective-permute-start.3
  12.5 2.6 %collective-permute-done.8.source = bf16[448,512]{1,0:T(8,128)(2,1)S(1)} collective-permute-done((bf16[448,512]{1,0:T(8,128)(2,1)S(1)}, bf16[448,512]{1,0:T(8,128)(2,1)S(1)}, u32[]{:S(2)}, u32[]{:S(2)}) %collective-permute-start.8) | collective-permute-done | bytes 458784 | tf_op jit(solution)/shard_map/ppermute | solution.py:409
  15.1 0.6 collective-permute-start.9
  15.7 0.5 collective-permute-start.6
  16.3 1.8 %shard_map.229 = (bf16[896,512]{1,0:T(8,128)(2,1)S(1)}, bf16[1024,512]{1,0:T(8,128)(2,1)S(1)}, bf16[2048,512]{1,0:T(8,128)(2,1)S(1)}) custom-call(bf16[256,512]{1,0:T(8,128)(2,1)S(1)} %copy-done.3, bf16[128,512]{1,0:T(8,128)(2,1)S(1)} %copy-done.6, bf16[384,512]{1,0:T(8,128)(2,1)S(1)} %copy-done.12, bf16[128,512]{1,0:T(8,128)(2,1)S(1)} %copy-done.13, ...), custom_call_target="tpu_custom_call" | custom-call | flops 402653184 | bytes 5357568 | tf_op jit(solution)/shard_map/pallas_call | solution.py:62
  18.0 2.6 %collective-permute-done.3.lat.l1 = bf16[1216,128]{1,0:T(8,128)(2,1)S(1)} collective-permute-done((bf16[1216,128]{1,0:T(8,128)(2,1)S(1)}, bf16[1216,128]{1,0:T(8,128)(2,1)S(1)}, u32[]{:S(2)}, u32[]{:S(2)}) %collective-permute-start.3) | collective-permute-done | bytes 311328 | tf_op jit(solution)/shard_map/ppermute | solution.py:409
  20.7 0.1 collective-permute-start.5
  20.8 0.5 collective-permute-start.10
  21.3 0.3 collective-permute-done.9.round_
  21.6 0.5 collective-permute-start.16
  22.8 1.6 %collective-permute-start.14 = (bf16[256,512]{1,0:T(8,128)(2,1)S(1)}, bf16[256,512]{1,0:T(8,128)(2,1)S(1)}, u32[]{:S(2)}, u32[]{:S(2)}) collective-permute-start(bf16[256,512]{1,0:T(8,128)(2,1)S(1)} %get-tuple-element.50), channel_id=1, source_target_pairs={{0,2},{1,3},{2,0},{3,1},{4,6},{5,7},{6,4},{7,5},{8,10},{9,11},{10,... | collective-permute-start | bytes 786440 | tf_op jit(solution)/shard_map/ppermute | solution.py:409
  24.4 0.0 copy-start.9
  24.4 0.0 copy-start.10
  24.4 4.8 %shard_map.232 = (bf16[256,512]{1,0:T(8,128)(2,1)S(1)}, bf16[128,512]{1,0:T(8,128)(2,1)S(1)}, bf16[128,512]{1,0:T(8,128)(2,1)S(1)}, bf16[256,512]{1,0:T(8,128)(2,1)S(1)}) custom-call(bf16[1024,512]{1,0:T(8,128)(2,1)S(1)} %get-tuple-element.41.emb, s32[2,1024]{1,0:T(2,128)S(1)} %copy-done.19, f32[1,512]{1,0:T(1,128)S(1)} %bitcast.6, ...), custom_call_target="tpu_custom_call" | custom-call | flops 2952790016 | bytes 5187588 | tf_op jit(solution)/shard_map/pallas_call | solution.py:62
  29.1 0.1 collective-permute-start.12
  29.2 0.5 collective-permute-start.13
  29.7 1.3 %collective-permute-done.14.held_in = bf16[256,512]{1,0:T(8,128)(2,1)S(1)} collective-permute-done((bf16[256,512]{1,0:T(8,128)(2,1)S(1)}, bf16[256,512]{1,0:T(8,128)(2,1)S(1)}, u32[]{:S(2)}, u32[]{:S(2)}) %collective-permute-start.14) | collective-permute-done | bytes 262176 | tf_op jit(solution)/shard_map/ppermute | solution.py:409
  31.0 0.1 shard_map.233
  31.1 0.0 copy-start.2
  31.2 0.0 copy-start.5
  31.2 0.6 collective-permute-start.17
  31.7 1.5 %collective-permute-start.15 = (bf16[256,512]{1,0:T(8,128)(2,1)S(1)}, bf16[256,512]{1,0:T(8,128)(2,1)S(1)}, u32[]{:S(2)}, u32[]{:S(2)}) collective-permute-start(bf16[256,512]{1,0:T(8,128)(2,1)S(1)} %get-tuple-element.52.mine), channel_id=1, source_target_pairs={{0,2},{1,3},{2,0},{3,1},{4,6},{5,7},{6,4},{7,5},{8,10},{9,11},{10,... | collective-permute-start | bytes 786440 | tf_op jit(solution)/shard_map/ppermute | solution.py:409
  33.2 1.5 %collective-permute-start.20 = (bf16[256,512]{1,0:T(8,128)(2,1)S(1)}, bf16[256,512]{1,0:T(8,128)(2,1)S(1)}, u32[]{:S(2)}, u32[]{:S(2)}) collective-permute-start(bf16[256,512]{1,0:T(8,128)(2,1)S(1)} %get-tuple-element.54.across), channel_id=1, source_target_pairs={{0,16},{16,0},{1,17},{17,1},{2,18},{18,2},{3,19},{19,3},{4,20},{20... | collective-permute-start | bytes 786440 | tf_op jit(solution)/shard_map/ppermute | solution.py:418
  34.8 4.2 %collective-permute-done.17.w3 = bf16[192,512]{1,0:T(8,128)(2,1)S(1)} collective-permute-done((bf16[192,512]{1,0:T(8,128)(2,1)S(1)}, bf16[192,512]{1,0:T(8,128)(2,1)S(1)}, u32[]{:S(2)}, u32[]{:S(2)}) %collective-permute-start.17) | collective-permute-done | bytes 196640 | tf_op jit(solution)/shard_map/ppermute | solution.py:418
  39.0 0.7 collective-permute-done.15.theirs
  39.7 4.0 %collective-permute-done.20.round_ = bf16[256,512]{1,0:T(8,128)(2,1)S(1)} collective-permute-done((bf16[256,512]{1,0:T(8,128)(2,1)S(1)}, bf16[256,512]{1,0:T(8,128)(2,1)S(1)}, u32[]{:S(2)}, u32[]{:S(2)}) %collective-permute-start.20) | collective-permute-done | bytes 262176 | tf_op jit(solution)/shard_map/ppermute | solution.py:418
  43.7 0.0 copy-start.16
  43.7 1.3 %shard_map.234 = (bf16[256,512]{1,0:T(8,128)(2,1)S(1)}, bf16[512,512]{1,0:T(8,128)(2,1)S(1)}, bf16[32,512]{1,0:T(8,128)(2,1)S(1)}, bf16[32,512]{1,0:T(8,128)(2,1)S(1)}, bf16[32,512]{1,0:T(8,128)(2,1)S(1)}) custom-call(bf16[256,512]{1,0:T(8,128)(2,1)S(1)} %get-tuple-element.46.mesh, bf16[256,512]{1,0:T(8,128)(2,1)S(1)} %get-tuple-element.52.mine, ...), custom_call_target="tpu_custom_call" | custom-call | flops 402653184 | bytes 4819456 | tf_op jit(solution)/shard_map/pallas_call | solution.py:62
  45.0 0.1 collective-permute-start.22
  45.1 0.5 collective-permute-start.21
  45.6 0.4 collective-permute-start.23
  46.0 2.6 %collective-permute-start.24 = (bf16[32,512]{1,0:T(8,128)(2,1)S(1)}, bf16[32,512]{1,0:T(8,128)(2,1)S(1)}, u32[]{:S(2)}, u32[]{:S(2)}) collective-permute-start(bf16[32,512]{1,0:T(8,128)(2,1)S(1)} %get-tuple-element.63), channel_id=1, source_target_pairs={{0,8},{4,12},{8,0},{12,4},{1,9},{5,13},{9,1},{13,5},{2,10},{6,14},... | collective-permute-start | bytes 98312 | tf_op jit(solution)/shard_map/ppermute | solution.py:544
  48.6 2.5 %collective-permute-start.25 = (bf16[32,512]{1,0:T(8,128)(2,1)S(1)}, bf16[32,512]{1,0:T(8,128)(2,1)S(1)}, u32[]{:S(2)}, u32[]{:S(2)}) collective-permute-start(bf16[32,512]{1,0:T(8,128)(2,1)S(1)} %get-tuple-element.64), channel_id=1, source_target_pairs={{4,8},{8,4},{5,9},{9,5},{6,10},{10,6},{7,11},{11,7},{20,24},{24,20... | collective-permute-start | bytes 98312 | tf_op jit(solution)/shard_map/ppermute | solution.py:544
  51.8 2.6 %collective-permute-done.25.refs_2_ = bf16[32,512]{1,0:T(8,128)(2,1)S(1)} collective-permute-done((bf16[32,512]{1,0:T(8,128)(2,1)S(1)}, bf16[32,512]{1,0:T(8,128)(2,1)S(1)}, u32[]{:S(2)}, u32[]{:S(2)}) %collective-permute-start.25) | collective-permute-done | bytes 32800 | tf_op jit(solution)/shard_map/ppermute | solution.py:544
  54.4 0.1 collective-permute-start.26
  54.5 0.7 collective-permute-start.30
  55.2 0.0 copy-start.21
  55.2 2.6 %shard_map.235 = (bf16[1536,512]{1,0:T(8,128)(2,1)S(1)}, f32[1024,512]{1,0:T(8,128)S(1)}, bf16[512,512]{1,0:T(8,128)(2,1)S(1)}, bf16[512,512]{1,0:T(8,128)(2,1)S(1)}) custom-call(bf16[2048,512]{1,0:T(8,128)(2,1)S(1)} %get-tuple-element.56.emb, bf16[256,512]{1,0:T(8,128)(2,1)S(1)} %get-tuple-element.55.mine.middle, ...), custom_call_target="tpu_custom_call" | custom-call | flops 1610612736 | bytes 10240000 | tf_op jit(solution)/shard_map/pallas_call | solution.py:62
  57.9 0.0 copy-start.11
  57.9 5.8 %shard_map.237 = (bf16[256,512]{1,0:T(8,128)(2,1)S(1)}, bf16[256,512]{1,0:T(8,128)(2,1)S(1)}) custom-call(bf16[2048,512]{1,0:T(8,128)(2,1)S(1)} %get-tuple-element.56.emb, s32[2,2048]{1,0:T(2,128)S(1)} %copy-done.16, f32[1,512]{1,0:T(1,128)S(1)} %bitcast.7, bf16[1536,512]{1,0:T(8,128)(2,1)S(1)} %get-tuple-element.58.table, ...), custom_call_target="tpu_custom_call" | custom-call | flops 3489660928 | bytes 7555076 | tf_op jit(solution)/shard_map/pallas_call | solution.py:62
  63.7 0.2 collective-permute-start.27
  63.9 0.3 collective-permute-start.29
  64.3 1.8 %collective-permute-done.30.w2 = bf16[384,512]{1,0:T(8,128)(2,1)S(1)} collective-permute-done((bf16[384,512]{1,0:T(8,128)(2,1)S(1)}, bf16[384,512]{1,0:T(8,128)(2,1)S(1)}, u32[]{:S(2)}, u32[]{:S(2)}) %collective-permute-start.30) | collective-permute-done | bytes 393248 | tf_op jit(solution)/shard_map/ppermute | solution.py:409
  66.0 0.1 shard_map.238
  66.1 0.7 collective-permute-start.28
  66.8 0.9 %collective-permute-done.31.w3 = bf16[384,512]{1,0:T(8,128)(2,1)S(1)} collective-permute-done((bf16[384,512]{1,0:T(8,128)(2,1)S(1)}, bf16[384,512]{1,0:T(8,128)(2,1)S(1)}, u32[]{:S(2)}, u32[]{:S(2)}) %collective-permute-start.31) | collective-permute-done | bytes 393248 | tf_op jit(solution)/shard_map/ppermute | solution.py:413
  67.8 4.3 %collective-permute-done.28.theirs = bf16[128,512]{1,0:T(8,128)(2,1)S(1)} collective-permute-done((bf16[128,512]{1,0:T(8,128)(2,1)S(1)}, bf16[128,512]{1,0:T(8,128)(2,1)S(1)}, u32[]{:S(2)}, u32[]{:S(2)}) %collective-permute-start.28) | collective-permute-done | bytes 131104 | tf_op jit(solution)/shard_map/ppermute | solution.py:409
  72.1 1.5 %shard_map.239 = bf16[128,512]{1,0:T(8,128)(2,1)} custom-call(bf16[256,512]{1,0:T(8,128)(2,1)S(1)} %get-tuple-element.55.mine.middle, bf16[128,512]{1,0:T(8,128)(2,1)S(1)} %get-tuple-element.68.mine, bf16[128,512]{1,0:T(8,128)(2,1)S(1)} %collective-permute-done.28.theirs, f32[1,512]{1,0:T(1,128)S(1)} %bitcast.5, bf16[384,512]{1,0:T(8,128)(2,1)S(1)} %get-tuple-element.70.w0, ...), custom_call_target="tpu_custom_call" | custom-call | flops 201326592 | bytes 2230272 | tf_op jit(solution)/shard_map/pallas_call | solution.py:62
  (58 shorter events, 0.2 us)
Async XLA Ops:
  0.0 0.9 %copy-start.3 = (bf16[256,512]{1,0:T(8,128)(2,1)S(1)}, bf16[256,512]{1,0:T(8,128)(2,1)}, u32[]{:S(2)}) copy-start(bf16[256,512]{1,0:T(8,128)(2,1)} %e_in.1) | copy-start | bytes 786436
  0.0 1.0 %copy-start.6 = (bf16[128,512]{1,0:T(8,128)(2,1)S(1)}, bf16[128,512]{1,0:T(8,128)(2,1)}, u32[]{:S(2)}) copy-start(bf16[128,512]{1,0:T(8,128)(2,1)} %e_out.1) | copy-start | bytes 393220
  0.0 1.0 %copy-start = (bf16[512,128]{1,0:T(8,128)(2,1)S(1)}, bf16[512,128]{1,0:T(8,128)(2,1)}, u32[]{:S(2)}) copy-start(bf16[512,128]{1,0:T(8,128)(2,1)} %refs_0_.1) | copy-start | bytes 393220
  0.0 1.0 %copy-start.8 = (s32[1,4,64]{2,1,0:T(4,128)S(1)}, s32[1,4,64]{2,1,0:T(4,128)}, u32[]{:S(2)}) copy-start(s32[1,4,64]{2,1,0:T(4,128)} %send.2) | copy-start | bytes 3076
  0.0 1.2 %copy-start.1 = (bf16[384,512]{1,0:T(8,128)(2,1)S(1)}, bf16[384,512]{1,0:T(8,128)(2,1)}, u32[]{:S(2)}) copy-start(bf16[384,512]{1,0:T(8,128)(2,1)} %o_in.1) | copy-start | bytes 1179652
  0.0 1.2 %copy-start.7 = (bf16[128,512]{1,0:T(8,128)(2,1)S(1)}, bf16[128,512]{1,0:T(8,128)(2,1)}, u32[]{:S(2)}) copy-start(bf16[128,512]{1,0:T(8,128)(2,1)} %o_out.1) | copy-start | bytes 393220
  0.0 11.8 %copy-start.4 = (bf16[512,128]{1,0:T(8,128)(2,1)S(1)}, bf16[512,128]{1,0:T(8,128)(2,1)}, u32[]{:S(2)}) copy-start(bf16[512,128]{1,0:T(8,128)(2,1)} %refs_1_.1) | copy-start | bytes 393220
  1.2 15.0 %copy-start.12 = (bf16[384,512]{1,0:T(8,128)(2,1)S(1)}, bf16[384,512]{1,0:T(8,128)(2,1)}, u32[]{:S(2)}) copy-start(bf16[384,512]{1,0:T(8,128)(2,1)} %p_in.1) | copy-start | bytes 1179652
  1.3 15.0 %copy-start.13 = (bf16[128,512]{1,0:T(8,128)(2,1)S(1)}, bf16[128,512]{1,0:T(8,128)(2,1)}, u32[]{:S(2)}) copy-start(bf16[128,512]{1,0:T(8,128)(2,1)} %p_out.1) | copy-start | bytes 393220
  1.3 15.0 %copy-start.14 = (f32[4,2048]{1,0:T(4,128)S(1)}, f32[4,2048]{1,0:T(4,128)}, u32[]{:S(2)}) copy-start(f32[4,2048]{1,0:T(4,128)} %pgeom.1) | copy-start | bytes 98308
  1.3 15.0 %copy-start.15 = (f32[4,1024]{1,0:T(4,128)S(1)}, f32[4,1024]{1,0:T(4,128)}, u32[]{:S(2)}) copy-start(f32[4,1024]{1,0:T(4,128)} %egeom.1) | copy-start | bytes 49156
  1.3 15.0 %copy-start.17 = (f32[4,512]{1,0:T(4,128)S(1)}, f32[4,512]{1,0:T(4,128)}, u32[]{:S(2)}) copy-start(f32[4,512]{1,0:T(4,128)} %egeo.1) | copy-start | bytes 24580
  1.3 15.0 %copy-start.18 = (f32[4,512]{1,0:T(4,128)S(1)}, f32[4,512]{1,0:T(4,128)}, u32[]{:S(2)}) copy-start(f32[4,512]{1,0:T(4,128)} %pgeo.1) | copy-start | bytes 24580
  1.6 22.7 %copy-start.19 = (s32[2,1024]{1,0:T(2,128)S(1)}, s32[2,1024]{1,0:T(2,128)}, u32[]{:S(2)}) copy-start(s32[2,1024]{1,0:T(2,128)} %edges.3) | copy-start | bytes 24580
  1.6 22.7 %copy-start.20 = (f32[512]{0:T(512)S(1)}, f32[512]{0:T(512)}, u32[]{:S(2)}) copy-start(f32[512]{0:T(512)} %param.44) | copy-start | bytes 6148
  1.6 13.5 %collective-permute-start.8 = (bf16[448,512]{1,0:T(8,128)(2,1)S(1)}, bf16[448,512]{1,0:T(8,128)(2,1)S(1)}, u32[]{:S(2)}, u32[]{:S(2)}) collective-permute-start(bf16[448,512]{1,0:T(8,128)(2,1)S(1)} %get-tuple-element.44), channel_id=1, source_target_pairs={{0,2},{1,3},{2,0},{3,1},{4,6},{5,7},{6,4},{7,5},{8,10},{9,11},{10,... | collective-permute-start | bytes 1376264 | tf_op jit(solution)/shard_map/ppermute | solution.py:409
  3.2 5.4 %collective-permute-start = (bf16[64,128]{1,0:T(8,128)(2,1)S(1)}, bf16[64,128]{1,0:T(8,128)(2,1)S(1)}, u32[]{:S(2)}, u32[]{:S(2)}) collective-permute-start(bf16[64,128]{1,0:T(8,128)(2,1)S(1)} %get-tuple-element.38), channel_id=1, source_target_pairs={{0,4},{4,0},{8,12},{12,8},{1,5},{5,1},{9,13},{13,9},{2,6},{6,2},{1... | collective-permute-start | bytes 49160 | tf_op jit(solution)/shard_map/ppermute | solution.py:474
  3.6 5.0 %collective-permute-start.1 = (bf16[64,128]{1,0:T(8,128)(2,1)S(1)}, bf16[64,128]{1,0:T(8,128)(2,1)S(1)}, u32[]{:S(2)}, u32[]{:S(2)}) collective-permute-start(bf16[64,128]{1,0:T(8,128)(2,1)S(1)} %get-tuple-element.39), channel_id=1, source_target_pairs={{0,8},{4,12},{8,0},{12,4},{1,9},{5,13},{9,1},{13,5},{2,10},{6,14},... | collective-permute-start | bytes 49160 | tf_op jit(solution)/shard_map/ppermute | solution.py:474
  6.2 5.6 %collective-permute-start.2 = (bf16[64,128]{1,0:T(8,128)(2,1)S(1)}, bf16[64,128]{1,0:T(8,128)(2,1)S(1)}, u32[]{:S(2)}, u32[]{:S(2)}) collective-permute-start(bf16[64,128]{1,0:T(8,128)(2,1)S(1)} %get-tuple-element.40), channel_id=1, source_target_pairs={{4,8},{8,4},{5,9},{9,5},{6,10},{10,6},{7,11},{11,7},{20,24},{24,20... | collective-permute-start | bytes 49160 | tf_op jit(solution)/shard_map/ppermute | solution.py:474
  11.9 8.7 %collective-permute-start.3 = (bf16[1216,128]{1,0:T(8,128)(2,1)S(1)}, bf16[1216,128]{1,0:T(8,128)(2,1)S(1)}, u32[]{:S(2)}, u32[]{:S(2)}) collective-permute-start(bf16[1216,128]{1,0:T(8,128)(2,1)S(1)} %shard_map.228.after.l0), channel_id=1, source_target_pairs={{0,2},{1,3},{2,0},{3,1},{4,6},{5,7},{6,4},{7,5},{8,10},{9,11},{10,... | collective-permute-start | bytes 933896 | tf_op jit(solution)/shard_map/ppermute | solution.py:409
  15.1 6.4 %collective-permute-start.9 = (bf16[256,512]{1,0:T(8,128)(2,1)S(1)}, bf16[256,512]{1,0:T(8,128)(2,1)S(1)}, u32[]{:S(2)}, u32[]{:S(2)}) collective-permute-start(bf16[256,512]{1,0:T(8,128)(2,1)S(1)} %get-tuple-element.45.across), channel_id=1, source_target_pairs={{0,16},{16,0},{1,17},{17,1},{2,18},{18,2},{3,19},{19,3},{4,20},{20... | collective-permute-start | bytes 786440 | tf_op jit(solution)/shard_map/ppermute | solution.py:418
  15.7 5.9 %collective-permute-start.4 = (bf16[1216,128]{1,0:T(8,128)(2,1)S(1)}, bf16[1216,128]{1,0:T(8,128)(2,1)S(1)}, u32[]{:S(2)}, u32[]{:S(2)}) collective-permute-start(bf16[1216,128]{1,0:T(8,128)(2,1)S(1)} %shard_map.228.after.l0), channel_id=1, source_target_pairs={{0,1},{1,0},{2,3},{3,2},{4,5},{5,4},{6,7},{7,6},{8,9},{9,8},{10,11... | collective-permute-start | bytes 933896 | tf_op jit(solution)/shard_map/ppermute | solution.py:413
  15.7 7.0 %collective-permute-start.6 = (bf16[384,512]{1,0:T(8,128)(2,1)S(1)}, bf16[384,512]{1,0:T(8,128)(2,1)S(1)}, u32[]{:S(2)}, u32[]{:S(2)}) collective-permute-start(bf16[384,512]{1,0:T(8,128)(2,1)S(1)} %copy-done.1), channel_id=1, source_target_pairs={{0,1},{1,0},{2,3},{3,2},{4,5},{5,4},{6,7},{7,6},{8,9},{9,8},{10,11... | collective-permute-start | bytes 1179656 | tf_op jit(solution)/shard_map/ppermute | solution.py:413
  16.2 4.5 %collective-permute-start.7 = (bf16[128,512]{1,0:T(8,128)(2,1)S(1)}, bf16[128,512]{1,0:T(8,128)(2,1)S(1)}, u32[]{:S(2)}, u32[]{:S(2)}) collective-permute-start(bf16[128,512]{1,0:T(8,128)(2,1)S(1)} %copy-done.7), channel_id=1, source_target_pairs={{0,1},{1,0},{2,3},{3,2},{4,5},{5,4},{6,7},{7,6},{8,9},{9,8},{10,11... | collective-permute-start | bytes 393224 | tf_op jit(solution)/shard_map/ppermute | solution.py:413
  20.7 3.6 %collective-permute-start.5 = (bf16[1216,128]{1,0:T(8,128)(2,1)S(1)}, bf16[1216,128]{1,0:T(8,128)(2,1)S(1)}, u32[]{:S(2)}, u32[]{:S(2)}) collective-permute-start(bf16[1216,128]{1,0:T(8,128)(2,1)S(1)} %get-tuple-element.43), channel_id=1, source_target_pairs={{0,1},{1,0},{2,3},{3,2},{4,5},{5,4},{6,7},{7,6},{8,9},{9,8},{10,11... | collective-permute-start | bytes 933896 | tf_op jit(solution)/shard_map/ppermute | solution.py:413
  20.8 3.6 %collective-permute-start.10 = (bf16[256,512]{1,0:T(8,128)(2,1)S(1)}, bf16[256,512]{1,0:T(8,128)(2,1)S(1)}, u32[]{:S(2)}, u32[]{:S(2)}) collective-permute-start(bf16[256,512]{1,0:T(8,128)(2,1)S(1)} %get-tuple-element.45.across), channel_id=1, source_target_pairs={{0,1},{1,0},{2,3},{3,2},{4,5},{5,4},{6,7},{7,6},{8,9},{9,8},{10,11... | collective-permute-start | bytes 786440 | tf_op jit(solution)/shard_map/ppermute | solution.py:413
  21.6 2.7 %collective-permute-start.11 = (bf16[256,512]{1,0:T(8,128)(2,1)S(1)}, bf16[256,512]{1,0:T(8,128)(2,1)S(1)}, u32[]{:S(2)}, u32[]{:S(2)}) collective-permute-start(bf16[256,512]{1,0:T(8,128)(2,1)S(1)} %collective-permute-done.9.round_), channel_id=1, source_target_pairs={{0,1},{1,0},{2,3},{3,2},{4,5},{5,4},{6,7},{7,6},{8,9},{9,8},{10,11... | collective-permute-start | bytes 786440 | tf_op jit(solution)/shard_map/ppermute | solution.py:413
  21.6 17.4 %collective-permute-start.16 = (bf16[896,512]{1,0:T(8,128)(2,1)S(1)}, bf16[896,512]{1,0:T(8,128)(2,1)S(1)}, u32[]{:S(2)}, u32[]{:S(2)}) collective-permute-start(bf16[896,512]{1,0:T(8,128)(2,1)S(1)} %get-tuple-element.42.weights.w0), channel_id=1, source_target_pairs={{0,1},{1,0},{2,3},{3,2},{4,5},{5,4},{6,7},{7,6},{8,9},{9,8},{10,11... | collective-permute-start | bytes 2752520 | tf_op jit(solution)/shard_map/ppermute | solution.py:413
  22.8 8.3 %collective-permute-start.14 = (bf16[256,512]{1,0:T(8,128)(2,1)S(1)}, bf16[256,512]{1,0:T(8,128)(2,1)S(1)}, u32[]{:S(2)}, u32[]{:S(2)}) collective-permute-start(bf16[256,512]{1,0:T(8,128)(2,1)S(1)} %get-tuple-element.50), channel_id=1, source_target_pairs={{0,2},{1,3},{2,0},{3,1},{4,6},{5,7},{6,4},{7,5},{8,10},{9,11},{10,... | collective-permute-start | bytes 786440 | tf_op jit(solution)/shard_map/ppermute | solution.py:409
  24.4 19.3 %copy-start.9 = (f32[512]{0:T(512)S(1)}, f32[512]{0:T(512)}, u32[]{:S(2)}) copy-start(f32[512]{0:T(512)} %param.45) | copy-start | bytes 6148
  24.4 19.3 %copy-start.10 = (s32[1,4,32]{2,1,0:T(4,128)S(1)}, s32[1,4,32]{2,1,0:T(4,128)}, u32[]{:S(2)}) copy-start(s32[1,4,32]{2,1,0:T(4,128)} %send.3) | copy-start | bytes 1540
  29.1 1.9 %collective-permute-start.12 = (bf16[128,512]{1,0:T(8,128)(2,1)S(1)}, bf16[128,512]{1,0:T(8,128)(2,1)S(1)}, u32[]{:S(2)}, u32[]{:S(2)}) collective-permute-start(bf16[128,512]{1,0:T(8,128)(2,1)S(1)} %get-tuple-element.48), channel_id=1, source_target_pairs={{0,1},{1,0},{2,3},{3,2},{4,5},{5,4},{6,7},{7,6},{8,9},{9,8},{10,11... | collective-permute-start | bytes 393224 | tf_op jit(solution)/shard_map/ppermute | solution.py:413
  29.2 1.8 %collective-permute-start.13 = (bf16[128,512]{1,0:T(8,128)(2,1)S(1)}, bf16[128,512]{1,0:T(8,128)(2,1)S(1)}, u32[]{:S(2)}, u32[]{:S(2)}) collective-permute-start(bf16[128,512]{1,0:T(8,128)(2,1)S(1)} %get-tuple-element.49), channel_id=1, source_target_pairs={{0,1},{1,0},{2,3},{3,2},{4,5},{5,4},{6,7},{7,6},{8,9},{9,8},{10,11... | collective-permute-start | bytes 393224 | tf_op jit(solution)/shard_map/ppermute | solution.py:413
  31.1 23.2 %copy-start.2 = (bf16[256,512]{1,0:T(8,128)(2,1)S(1)}, bf16[256,512]{1,0:T(8,128)(2,1)}, u32[]{:S(2)}) copy-start(bf16[256,512]{1,0:T(8,128)(2,1)} %w_in.3) | copy-start | bytes 786436
  31.2 23.2 %copy-start.5 = (bf16[128,512]{1,0:T(8,128)(2,1)S(1)}, bf16[128,512]{1,0:T(8,128)(2,1)}, u32[]{:S(2)}) copy-start(bf16[128,512]{1,0:T(8,128)(2,1)} %w_out.3) | copy-start | bytes 393220
  31.2 7.8 %collective-permute-start.17 = (bf16[192,512]{1,0:T(8,128)(2,1)S(1)}, bf16[192,512]{1,0:T(8,128)(2,1)S(1)}, u32[]{:S(2)}, u32[]{:S(2)}) collective-permute-start(bf16[192,512]{1,0:T(8,128)(2,1)S(1)} %get-tuple-element.53), channel_id=1, source_target_pairs={{0,16},{16,0},{1,17},{17,1},{2,18},{18,2},{3,19},{19,3},{4,20},{20... | collective-permute-start | bytes 589832 | tf_op jit(solution)/shard_map/ppermute | solution.py:418
  31.7 7.9 %collective-permute-start.15 = (bf16[256,512]{1,0:T(8,128)(2,1)S(1)}, bf16[256,512]{1,0:T(8,128)(2,1)S(1)}, u32[]{:S(2)}, u32[]{:S(2)}) collective-permute-start(bf16[256,512]{1,0:T(8,128)(2,1)S(1)} %get-tuple-element.52.mine), channel_id=1, source_target_pairs={{0,2},{1,3},{2,0},{3,1},{4,6},{5,7},{6,4},{7,5},{8,10},{9,11},{10,... | collective-permute-start | bytes 786440 | tf_op jit(solution)/shard_map/ppermute | solution.py:409
  33.2 10.4 %collective-permute-start.20 = (bf16[256,512]{1,0:T(8,128)(2,1)S(1)}, bf16[256,512]{1,0:T(8,128)(2,1)S(1)}, u32[]{:S(2)}, u32[]{:S(2)}) collective-permute-start(bf16[256,512]{1,0:T(8,128)(2,1)S(1)} %get-tuple-element.54.across), channel_id=1, source_target_pairs={{0,16},{16,0},{1,17},{17,1},{2,18},{18,2},{3,19},{19,3},{4,20},{20... | collective-permute-start | bytes 786440 | tf_op jit(solution)/shard_map/ppermute | solution.py:418
  34.8 4.2 %collective-permute-start.18 = (bf16[192,512]{1,0:T(8,128)(2,1)S(1)}, bf16[192,512]{1,0:T(8,128)(2,1)S(1)}, u32[]{:S(2)}, u32[]{:S(2)}) collective-permute-start(bf16[192,512]{1,0:T(8,128)(2,1)S(1)} %get-tuple-element.51.node_in.w2), channel_id=1, source_target_pairs={{0,1},{1,0},{2,3},{3,2},{4,5},{5,4},{6,7},{7,6},{8,9},{9,8},{10,11... | collective-permute-start | bytes 589832 | tf_op jit(solution)/shard_map/ppermute | solution.py:413
  39.0 4.7 %collective-permute-start.19 = (bf16[192,512]{1,0:T(8,128)(2,1)S(1)}, bf16[192,512]{1,0:T(8,128)(2,1)S(1)}, u32[]{:S(2)}, u32[]{:S(2)}) collective-permute-start(bf16[192,512]{1,0:T(8,128)(2,1)S(1)} %collective-permute-done.17.w3), channel_id=1, source_target_pairs={{0,1},{1,0},{2,3},{3,2},{4,5},{5,4},{6,7},{7,6},{8,9},{9,8},{10,11... | collective-permute-start | bytes 589832 | tf_op jit(solution)/shard_map/ppermute | solution.py:413
  43.7 11.5 %copy-start.16 = (s32[2,2048]{1,0:T(2,128)S(1)}, s32[2,2048]{1,0:T(2,128)}, u32[]{:S(2)}) copy-start(s32[2,2048]{1,0:T(2,128)} %edges.5) | copy-start | bytes 49156
  45.0 10.2 %collective-permute-start.22 = (bf16[512,512]{1,0:T(8,128)(2,1)S(1)}, bf16[512,512]{1,0:T(8,128)(2,1)S(1)}, u32[]{:S(2)}, u32[]{:S(2)}) collective-permute-start(bf16[512,512]{1,0:T(8,128)(2,1)S(1)} %get-tuple-element.57.pair), channel_id=1, source_target_pairs={{0,1},{1,0},{2,3},{3,2},{4,5},{5,4},{6,7},{7,6},{8,9},{9,8},{10,11... | collective-permute-start | bytes 1572872 | tf_op jit(solution)/shard_map/ppermute | solution.py:413
  45.1 10.2 %collective-permute-start.21 = (bf16[256,512]{1,0:T(8,128)(2,1)S(1)}, bf16[256,512]{1,0:T(8,128)(2,1)S(1)}, u32[]{:S(2)}, u32[]{:S(2)}) collective-permute-start(bf16[256,512]{1,0:T(8,128)(2,1)S(1)} %get-tuple-element.55.mine.middle), channel_id=1, source_target_pairs={{0,1},{1,0},{2,3},{3,2},{4,5},{5,4},{6,7},{7,6},{8,9},{9,8},{10,11... | collective-permute-start | bytes 786440 | tf_op jit(solution)/shard_map/ppermute | solution.py:413
  45.6 6.2 %collective-permute-start.23 = (bf16[32,512]{1,0:T(8,128)(2,1)S(1)}, bf16[32,512]{1,0:T(8,128)(2,1)S(1)}, u32[]{:S(2)}, u32[]{:S(2)}) collective-permute-start(bf16[32,512]{1,0:T(8,128)(2,1)S(1)} %get-tuple-element.62), channel_id=1, source_target_pairs={{0,4},{4,0},{8,12},{12,8},{1,5},{5,1},{9,13},{13,9},{2,6},{6,2},{1... | collective-permute-start | bytes 98312 | tf_op jit(solution)/shard_map/ppermute | solution.py:544
  46.0 5.8 %collective-permute-start.24 = (bf16[32,512]{1,0:T(8,128)(2,1)S(1)}, bf16[32,512]{1,0:T(8,128)(2,1)S(1)}, u32[]{:S(2)}, u32[]{:S(2)}) collective-permute-start(bf16[32,512]{1,0:T(8,128)(2,1)S(1)} %get-tuple-element.63), channel_id=1, source_target_pairs={{0,8},{4,12},{8,0},{12,4},{1,9},{5,13},{9,1},{13,5},{2,10},{6,14},... | collective-permute-start | bytes 98312 | tf_op jit(solution)/shard_map/ppermute | solution.py:544
  48.6 5.8 %collective-permute-start.25 = (bf16[32,512]{1,0:T(8,128)(2,1)S(1)}, bf16[32,512]{1,0:T(8,128)(2,1)S(1)}, u32[]{:S(2)}, u32[]{:S(2)}) collective-permute-start(bf16[32,512]{1,0:T(8,128)(2,1)S(1)} %get-tuple-element.64), channel_id=1, source_target_pairs={{4,8},{8,4},{5,9},{9,5},{6,10},{10,6},{7,11},{11,7},{20,24},{24,20... | collective-permute-start | bytes 98312 | tf_op jit(solution)/shard_map/ppermute | solution.py:544
  54.4 3.4 %collective-permute-start.26 = (bf16[96,512]{1,0:T(8,128)(2,1)S(1)}, bf16[96,512]{1,0:T(8,128)(2,1)S(1)}, u32[]{:S(2)}, u32[]{:S(2)}) collective-permute-start(bf16[96,512]{1,0:T(8,128)(2,1)S(1)} %get-tuple-element.65.halo), channel_id=1, source_target_pairs={{0,1},{1,0},{2,3},{3,2},{4,5},{5,4},{6,7},{7,6},{8,9},{9,8},{10,11... | collective-permute-start | bytes 294920 | tf_op jit(solution)/shard_map/ppermute | solution.py:413
  54.5 11.5 %collective-permute-start.30 = (bf16[384,512]{1,0:T(8,128)(2,1)S(1)}, bf16[384,512]{1,0:T(8,128)(2,1)S(1)}, u32[]{:S(2)}, u32[]{:S(2)}) collective-permute-start(bf16[384,512]{1,0:T(8,128)(2,1)S(1)} %get-tuple-element.70.w0), channel_id=1, source_target_pairs={{0,2},{1,3},{2,0},{3,1},{4,6},{5,7},{6,4},{7,5},{8,10},{9,11},{10,... | collective-permute-start | bytes 1179656 | tf_op jit(solution)/shard_map/ppermute | solution.py:409
  55.2 2.6 %copy-start.21 = (f32[512]{0:T(512)S(1)}, f32[512]{0:T(512)}, u32[]{:S(2)}) copy-start(f32[512]{0:T(512)} %param.46) | copy-start | bytes 6148
  57.9 14.2 %copy-start.11 = (f32[512]{0:T(512)S(1)}, f32[512]{0:T(512)}, u32[]{:S(2)}) copy-start(f32[512]{0:T(512)} %param.47) | copy-start | bytes 6148
  63.7 2.4 %collective-permute-start.27 = (bf16[256,512]{1,0:T(8,128)(2,1)S(1)}, bf16[256,512]{1,0:T(8,128)(2,1)S(1)}, u32[]{:S(2)}, u32[]{:S(2)}) collective-permute-start(bf16[256,512]{1,0:T(8,128)(2,1)S(1)} %get-tuple-element.67), channel_id=1, source_target_pairs={{0,1},{1,0},{2,3},{3,2},{4,5},{5,4},{6,7},{7,6},{8,9},{9,8},{10,11... | collective-permute-start | bytes 786440 | tf_op jit(solution)/shard_map/ppermute | solution.py:413
  63.9 2.9 %collective-permute-start.29 = (bf16[384,512]{1,0:T(8,128)(2,1)S(1)}, bf16[384,512]{1,0:T(8,128)(2,1)S(1)}, u32[]{:S(2)}, u32[]{:S(2)}) collective-permute-start(bf16[384,512]{1,0:T(8,128)(2,1)S(1)} %get-tuple-element.70.w0), channel_id=1, source_target_pairs={{0,1},{1,0},{2,3},{3,2},{4,5},{5,4},{6,7},{7,6},{8,9},{9,8},{10,11... | collective-permute-start | bytes 1179656 | tf_op jit(solution)/shard_map/ppermute | solution.py:413
  66.0 1.7 %collective-permute-start.31 = (bf16[384,512]{1,0:T(8,128)(2,1)S(1)}, bf16[384,512]{1,0:T(8,128)(2,1)S(1)}, u32[]{:S(2)}, u32[]{:S(2)}) collective-permute-start(bf16[384,512]{1,0:T(8,128)(2,1)S(1)} %collective-permute-done.30.w2), channel_id=1, source_target_pairs={{0,1},{1,0},{2,3},{3,2},{4,5},{5,4},{6,7},{7,6},{8,9},{9,8},{10,11... | collective-permute-start | bytes 1179656 | tf_op jit(solution)/shard_map/ppermute | solution.py:413
  66.1 6.0 %collective-permute-start.28 = (bf16[128,512]{1,0:T(8,128)(2,1)S(1)}, bf16[128,512]{1,0:T(8,128)(2,1)S(1)}, u32[]{:S(2)}, u32[]{:S(2)}) collective-permute-start(bf16[128,512]{1,0:T(8,128)(2,1)S(1)} %get-tuple-element.69), channel_id=1, source_target_pairs={{0,2},{1,3},{2,0},{3,1},{4,6},{5,7},{6,4},{7,5},{8,10},{9,11},{10,... | collective-permute-start | bytes 393224 | tf_op jit(solution)/shard_map/ppermute | solution.py:409

commit v11 on v6

--- a/solution.py
+++ b/solution.py
@@ -12,6 +12,7 @@
 STEP = 512
 GATHERED = 1024
 LONG = 30 * 10**9
+BY_GROUP = ("groups",)
 BY_PART = ("dom",)
 VMEM_BYTES = 24 * 1024 * 1024
 I16 = jnp.int16
@@ -130,11 +131,11 @@
     token[...] = jnp.zeros(token.shape, token.dtype)
 
 
-def first_pack_kernel(plan, grid, send, w_in, w_out, token, half, *outs):
+def first_pack_kernel(plan, grid, send, w_in, w_out, n_out, p_out, token, half, *outs):
     place = 0
-    for source in (w_in, w_out):
+    for source, axes in ((w_in, BY_GROUP), (w_out, BY_GROUP), (n_out, BY_PART), (p_out, BY_GROUP)):
         rows = source.shape[0] // 2
-        begin = pl.multiple_of(lax.axis_index("groups") * rows, 64)
+        begin = pl.multiple_of(parity(axes) * rows, 64)
         half[place : place + rows, :] = source[pl.ds(begin, rows), :]
         place += rows
     pick_lists(plan, grid[...], send, outs)
@@ -149,23 +150,28 @@
 
 def cross_kernel(parts, weights, lat, crossing, lat_out):
     lat_out[...] = lat[...]
-    first, place = 0, 0
-    for rows, axes in parts:
+    place = 0
+    for first, rows, axes in parts:
         half = rows // 2
         begin = pl.multiple_of(first + parity(axes) * half, 64)
         crossing[place : place + half, :] = weights[pl.ds(begin, half), :]
-        first, place = first + rows, place + half
+        place += half
+
+
+def rows_kernel(source, out):
+    out[...] = source[: out.shape[0], :]
 
 
 def pair_kernel(first, second, after, out):
     stack_into(out, (first, second))
 
 
-def split_kernel(source, after, *outs):
-    first = 0
-    for out in outs:
-        out[...] = source[first : first + out.shape[0], :]
-        first += out.shape[0]
+def split_kernel(ins, early, source, after, node, proc):
+    n, p = ins
+    n_rest, p_rest = node.shape[0] - n, proc.shape[0] - p
+    base = early.shape[0] - n_rest - p_rest
+    stack_into(node, (source.at[pl.ds(0, n), :], early.at[pl.ds(base, n_rest), :]))
+    stack_into(proc, (source.at[pl.ds(n, p), :], early.at[pl.ds(base + n_rest, p_rest), :]))
 
 
 def concat_kernel(*refs):
@@ -468,10 +474,11 @@
     (token,) = call(begin_kernel, [shape(16, 128)], [], flops=LONG)
     edge_half, *outgoing = call(
         functools.partial(first_pack_kernel, plan),
-        [shape((k_in + k_out) // 2, d)] + [shape(slots, width)] * len(plan),
-        [grid_lat, grid_send, enc_edge_in, enc_edge_out, token],
-    )
-    edge_across = to_chip(edge_half)
+        [shape((k_in + 2 * k_out + n_out) // 2, d)] + [shape(slots, width)] * len(plan),
+        [grid_lat, grid_send, enc_edge_in, enc_edge_out, enc_node_out, proc_edge_out, token],
+    )
+    first_across = to_chip(edge_half)
+    (edge_across,) = call(rows_kernel, [shape((k_in + k_out) // 2, d)], [first_across])
     halos = [lax.ppermute(v, "dom", entry[0]) for v, entry in zip(outgoing, plan)]
     got = len(plan) * slots
     (lat,) = call(
@@ -493,10 +500,8 @@
         flops=2 * (n_enc + n_proc) * d * 128,
     )
     crossing, lat_sent = call(
-        functools.partial(
-            cross_kernel, ((n_in, BY_PART), (n_out, BY_PART), (k_in, ("groups",)), (k_out, ("groups",)))
-        ),
-        [shape((n_in + n_out + k_in + k_out) // 2, d), shape(lat.shape[0], width)],
+        functools.partial(cross_kernel, ((0, n_in, BY_PART), (n_in + n_out, k_in, BY_GROUP))),
+        [shape((n_in + k_in) // 2, d), shape(lat.shape[0], width)],
         [next_w, lat_across],
     )
     lat_both = to_core(lat_sent)
@@ -525,9 +530,9 @@
     )
     (chip_sum,) = call(add_kernel, [shape(half, d)], [keep, to_core(give)])
     node_across, proc_across = call(
-        split_kernel,
+        functools.partial(split_kernel, (n_in // 2, k_in // 2)),
         [shape((n_in + n_out) // 2, d), shape((k_in + k_out) // 2, d)],
-        [next_across, chip_sum],
+        [first_across, next_across, chip_sum],
     )
     node_round = to_partition(node_across)
     proc_round = to_group(proc_across)

time: 69 us -> 68.6 us (level)
  waiting for transfers between devices: 26.4 us -> 22.1 us
  starting transfers between devices: 21 us -> 25 us
    ppermute x6, waiting for transfers between devices: 15.3 us -> 11.8 us  [to_chip(): return lax.ppermute(v, 'sub', [(i, i ^ 2) for i in range(4)])]
    ppermute x6, starting transfers between devices: 5.48 us -> 8.15 us  [to_chip(): return lax.ppermute(v, 'sub', [(i, i ^ 2) for i in range(4)])]
    ppermute x1, waiting for transfers between devices: 4.79 us -> 3.42 us  [to_partition(): lax.ppermute(v, 'dom', [(i, i ^ 1) for i in range(lax.axis_size('dom'))])]
    pallas_call x15 -> x16, Pallas kernels: 18.3 us -> 18.3 us  [call(): pl.pallas_call(body, out_shape=tuple(outs), in_specs=specs, out_specs=tup...]
  transfers between devices with their start and end apart: 31 -> 31, of which waited for: 9 -> 10; matrix products, arithmetic and copies ran while one was open for 0% -> 0% of each run, Pallas kernels for 24% -> 24%
where the time goes in v11:
time: 68.6 us; the launch traced here: 68.4 us
  starting transfers between devices  25 us (36%)
  waiting for transfers between devices  22.1 us (32%)
  Pallas kernels  18.3 us (27%)
  between operations  1.75 us (3%)
  local copies, waits for them, and re-layouts  1.28 us (2%)
    pallas_call x16, Pallas kernels, call(): pl.pallas_call(body, out_shape=tuple(outs), in_specs=specs, out_specs=tup...  18.3 us
    ppermute x6, waiting for transfers between devices, to_chip(): return lax.ppermute(v, 'sub', [(i, i ^ 2) for i in range(4)])  11.8 us
    ppermute x6, starting transfers between devices, local(): lax.ppermute(v, 'dom', entry[0])  11.6 us
    ppermute x6, starting transfers between devices, to_chip(): return lax.ppermute(v, 'sub', [(i, i ^ 2) for i in range(4)])  8.15 us
    ppermute x6, waiting for transfers between devices, local(): lax.ppermute(v, 'dom', entry[0])  4.74 us
    ppermute x16, starting transfers between devices, to_core(): return lax.ppermute(v, 'sub', [(i, i ^ 1) for i in range(4)])  3.43 us
    ppermute x1, waiting for transfers between devices, to_partition(): lax.ppermute(v, 'dom', [(i, i ^ 1) for i in range(lax.axis_size('dom'))])  3.42 us
    ppermute x16, waiting for transfers between devices, to_core(): return lax.ppermute(v, 'sub', [(i, i ^ 1) for i in range(4)])  2.21 us
  transfers between devices with their start and end apart: 31, of which 10 were waited for; matrix products, arithmetic and copies ran while one was open for 0% of the time, Pallas kernels for 24%

profile of v11, /device:TPU:12, one launch (start us, length us, event | category | flops | bytes accessed | tf_op | source)
XLA Modules:
  0.0 68.4 jit_solution(8458300831029109975)
XLA Ops:
  0.1 0.8 %copy-done.4 = bf16[128,512]{1,0:T(8,128)(2,1)S(1)} copy-done((bf16[128,512]{1,0:T(8,128)(2,1)S(1)}, bf16[128,512]{1,0:T(8,128)(2,1)}, u32[]{:S(2)}) %copy-start.4) | copy-done | bytes 131096
  0.9 0.1 copy-done.5
  1.0 0.1 copy-done
  1.0 0.2 copy-done.1
  1.2 0.0 copy-done.6
  1.3 0.0 copy-start.17
  1.3 0.0 copy-start.18
  1.3 0.3 shard_map.227
  1.6 0.0 copy-start.19
  1.6 0.0 copy-start.20
  1.6 1.6 %collective-permute-start.8 = (bf16[384,512]{1,0:T(8,128)(2,1)S(1)}, bf16[384,512]{1,0:T(8,128)(2,1)S(1)}, u32[]{:S(2)}, u32[]{:S(2)}) collective-permute-start(bf16[384,512]{1,0:T(8,128)(2,1)S(1)} %get-tuple-element.38), channel_id=1, source_target_pairs={{0,2},{1,3},{2,0},{3,1},{4,6},{5,7},{6,4},{7,5},{8,10},{9,11},{10,... | collective-permute-start | bytes 1179656 | tf_op jit(solution)/shard_map/ppermute | solution.py:412
  3.2 0.5 collective-permute-start
  3.6 2.6 %collective-permute-start.1 = (bf16[64,128]{1,0:T(8,128)(2,1)S(1)}, bf16[64,128]{1,0:T(8,128)(2,1)S(1)}, u32[]{:S(2)}, u32[]{:S(2)}) collective-permute-start(bf16[64,128]{1,0:T(8,128)(2,1)S(1)} %get-tuple-element.33), channel_id=1, source_target_pairs={{0,8},{4,12},{8,0},{12,4},{1,9},{5,13},{9,1},{13,5},{2,10},{6,14},... | collective-permute-start | bytes 49160 | tf_op jit(solution)/shard_map/ppermute | solution.py:482
  6.2 2.3 %collective-permute-start.2 = (bf16[64,128]{1,0:T(8,128)(2,1)S(1)}, bf16[64,128]{1,0:T(8,128)(2,1)S(1)}, u32[]{:S(2)}, u32[]{:S(2)}) collective-permute-start(bf16[64,128]{1,0:T(8,128)(2,1)S(1)} %get-tuple-element.34), channel_id=1, source_target_pairs={{4,8},{8,4},{5,9},{9,5},{6,10},{10,6},{7,11},{11,7},{20,24},{24,20... | collective-permute-start | bytes 49160 | tf_op jit(solution)/shard_map/ppermute | solution.py:482
  8.6 0.0 collective-permute-done.1.refs_3_
  8.6 3.2 %collective-permute-done.2.refs_4_ = bf16[64,128]{1,0:T(8,128)(2,1)S(1)} collective-permute-done((bf16[64,128]{1,0:T(8,128)(2,1)S(1)}, bf16[64,128]{1,0:T(8,128)(2,1)S(1)}, u32[]{:S(2)}, u32[]{:S(2)}) %collective-permute-start.2) | collective-permute-done | bytes 16416 | tf_op jit(solution)/shard_map/ppermute | solution.py:482
  11.9 0.6 collective-permute-start.3
  12.5 0.1 collective-permute-done.8.source.early
  12.6 0.6 collective-permute-start.9
  13.1 0.0 collective-permute-start.6
  13.1 0.5 collective-permute-start.7
  13.7 1.8 %shard_map.229 = (bf16[896,512]{1,0:T(8,128)(2,1)S(1)}, bf16[1024,512]{1,0:T(8,128)(2,1)S(1)}, bf16[2048,512]{1,0:T(8,128)(2,1)S(1)}) custom-call(bf16[256,512]{1,0:T(8,128)(2,1)S(1)} %copy-done.13, bf16[128,512]{1,0:T(8,128)(2,1)S(1)} %copy-done.4, bf16[384,512]{1,0:T(8,128)(2,1)S(1)} %copy-done.12, bf16[128,512]{1,0:T(8,128)(2,1)S(1)} %copy-done.5, ...), custom_call_target="tpu_custom_call" | custom-call | flops 402653184 | bytes 5357568 | tf_op jit(solution)/shard_map/pallas_call | solution.py:64
  15.5 3.9 %collective-permute-done.3.lat.l1 = bf16[1216,128]{1,0:T(8,128)(2,1)S(1)} collective-permute-done((bf16[1216,128]{1,0:T(8,128)(2,1)S(1)}, bf16[1216,128]{1,0:T(8,128)(2,1)S(1)}, u32[]{:S(2)}, u32[]{:S(2)}) %collective-permute-start.3) | collective-permute-done | bytes 311328 | tf_op jit(solution)/shard_map/ppermute | solution.py:412
  19.4 0.1 collective-permute-start.5
  19.5 0.5 collective-permute-start.10
  20.0 0.1 collective-permute-start.11
  20.7 0.5 collective-permute-start.14
  21.2 1.4 %collective-permute-start.15 = (bf16[320,512]{1,0:T(8,128)(2,1)S(1)}, bf16[320,512]{1,0:T(8,128)(2,1)S(1)}, u32[]{:S(2)}, u32[]{:S(2)}) collective-permute-start(bf16[320,512]{1,0:T(8,128)(2,1)S(1)} %get-tuple-element.42), channel_id=1, source_target_pairs={{0,2},{1,3},{2,0},{3,1},{4,6},{5,7},{6,4},{7,5},{8,10},{9,11},{10,... | collective-permute-start | bytes 983048 | tf_op jit(solution)/shard_map/ppermute | solution.py:412
  22.6 0.0 copy-start.2
  22.6 0.0 copy-start.7
  22.6 0.0 copy-start.9
  22.6 0.0 copy-start.10
  22.7 4.8 %shard_map.232 = (bf16[256,512]{1,0:T(8,128)(2,1)S(1)}, bf16[256,512]{1,0:T(8,128)(2,1)S(1)}, bf16[256,512]{1,0:T(8,128)(2,1)S(1)}) custom-call(bf16[1024,512]{1,0:T(8,128)(2,1)S(1)} %get-tuple-element.35.emb, s32[2,1024]{1,0:T(2,128)S(1)} %copy-done.19, f32[1,512]{1,0:T(1,128)S(1)} %bitcast.6, bf16[1216,128]{1,0:T(8,128)(2,1)S(1)} %shard_map.228.after.l0, ...), custom_call_target="tpu_custom_call" | custom-call | flops 2952790016 | bytes 5187588 | tf_op jit(solution)/shard_map/pallas_call | solution.py:64
  27.4 0.1 collective-permute-start.12
  27.5 1.5 %collective-permute-done.12.theirs = bf16[256,512]{1,0:T(8,128)(2,1)S(1)} collective-permute-done((bf16[256,512]{1,0:T(8,128)(2,1)S(1)}, bf16[256,512]{1,0:T(8,128)(2,1)S(1)}, u32[]{:S(2)}, u32[]{:S(2)}) %collective-permute-start.12) | collective-permute-done | bytes 262176 | tf_op jit(solution)/shard_map/ppermute | solution.py:416
  29.0 0.1 shard_map.233.after.mine
  29.1 1.8 %collective-permute-done.15.source = bf16[320,512]{1,0:T(8,128)(2,1)S(1)} collective-permute-done((bf16[320,512]{1,0:T(8,128)(2,1)S(1)}, bf16[320,512]{1,0:T(8,128)(2,1)S(1)}, u32[]{:S(2)}, u32[]{:S(2)}) %collective-permute-start.15) | collective-permute-done | bytes 327712 | tf_op jit(solution)/shard_map/ppermute | solution.py:412
  30.9 0.7 %collective-permute-start.16 = (bf16[192,512]{1,0:T(8,128)(2,1)S(1)}, bf16[192,512]{1,0:T(8,128)(2,1)S(1)}, u32[]{:S(2)}, u32[]{:S(2)}) collective-permute-start(bf16[192,512]{1,0:T(8,128)(2,1)S(1)} %get-tuple-element.43.w2), channel_id=1, source_target_pairs={{0,4},{4,0},{8,12},{12,8},{1,5},{5,1},{9,13},{13,9},{2,6},{6,2},{1... | collective-permute-start | bytes 589832 | tf_op jit(solution)/shard_map/ppermute | solution.py:425
  31.6 1.5 %collective-permute-start.13 = (bf16[256,512]{1,0:T(8,128)(2,1)S(1)}, bf16[256,512]{1,0:T(8,128)(2,1)S(1)}, u32[]{:S(2)}, u32[]{:S(2)}) collective-permute-start(bf16[256,512]{1,0:T(8,128)(2,1)S(1)} %shard_map.233.after.mine), channel_id=1, source_target_pairs={{0,2},{1,3},{2,0},{3,1},{4,6},{5,7},{6,4},{7,5},{8,10},{9,11},{10,... | collective-permute-start | bytes 786440 | tf_op jit(solution)/shard_map/ppermute | solution.py:412
  33.1 0.5 collective-permute-start.20
  33.6 3.4 %collective-permute-done.16.w3 = bf16[192,512]{1,0:T(8,128)(2,1)S(1)} collective-permute-done((bf16[192,512]{1,0:T(8,128)(2,1)S(1)}, bf16[192,512]{1,0:T(8,128)(2,1)S(1)}, u32[]{:S(2)}, u32[]{:S(2)}) %collective-permute-start.16) | collective-permute-done | bytes 196640 | tf_op jit(solution)/shard_map/ppermute | solution.py:425
  37.1 1.7 %collective-permute-done.13.theirs = bf16[256,512]{1,0:T(8,128)(2,1)S(1)} collective-permute-done((bf16[256,512]{1,0:T(8,128)(2,1)S(1)}, bf16[256,512]{1,0:T(8,128)(2,1)S(1)}, u32[]{:S(2)}, u32[]{:S(2)}) %collective-permute-start.13) | collective-permute-done | bytes 262176 | tf_op jit(solution)/shard_map/ppermute | solution.py:412
  38.9 0.0 copy-start.16
  38.9 1.2 %shard_map.235 = (bf16[256,512]{1,0:T(8,128)(2,1)S(1)}, bf16[384,512]{1,0:T(8,128)(2,1)S(1)}, bf16[32,512]{1,0:T(8,128)(2,1)S(1)}, bf16[32,512]{1,0:T(8,128)(2,1)S(1)}, bf16[32,512]{1,0:T(8,128)(2,1)S(1)}) custom-call(bf16[256,512]{1,0:T(8,128)(2,1)S(1)} %get-tuple-element.39.mesh, bf16[256,512]{1,0:T(8,128)(2,1)S(1)} %shard_map.233.after.mine, ...), custom_call_target="tpu_custom_call" | custom-call | flops 402653184 | bytes 4557312 | tf_op jit(solution)/shard_map/pallas_call | solution.py:64
  40.2 0.1 collective-permute-start.21
  40.2 0.5 collective-permute-start.19
  40.7 1.4 %collective-permute-start.22 = (bf16[32,512]{1,0:T(8,128)(2,1)S(1)}, bf16[32,512]{1,0:T(8,128)(2,1)S(1)}, u32[]{:S(2)}, u32[]{:S(2)}) collective-permute-start(bf16[32,512]{1,0:T(8,128)(2,1)S(1)} %get-tuple-element.51), channel_id=1, source_target_pairs={{0,4},{4,0},{8,12},{12,8},{1,5},{5,1},{9,13},{13,9},{2,6},{6,2},{1... | collective-permute-start | bytes 98312 | tf_op jit(solution)/shard_map/ppermute | solution.py:552
  42.1 2.8 %collective-permute-start.23 = (bf16[32,512]{1,0:T(8,128)(2,1)S(1)}, bf16[32,512]{1,0:T(8,128)(2,1)S(1)}, u32[]{:S(2)}, u32[]{:S(2)}) collective-permute-start(bf16[32,512]{1,0:T(8,128)(2,1)S(1)} %get-tuple-element.52), channel_id=1, source_target_pairs={{0,8},{4,12},{8,0},{12,4},{1,9},{5,13},{9,1},{13,5},{2,10},{6,14},... | collective-permute-start | bytes 98312 | tf_op jit(solution)/shard_map/ppermute | solution.py:552
  44.9 2.1 %collective-permute-start.24 = (bf16[32,512]{1,0:T(8,128)(2,1)S(1)}, bf16[32,512]{1,0:T(8,128)(2,1)S(1)}, u32[]{:S(2)}, u32[]{:S(2)}) collective-permute-start(bf16[32,512]{1,0:T(8,128)(2,1)S(1)} %get-tuple-element.53), channel_id=1, source_target_pairs={{4,8},{8,4},{5,9},{9,5},{6,10},{10,6},{7,11},{11,7},{20,24},{24,20... | collective-permute-start | bytes 98312 | tf_op jit(solution)/shard_map/ppermute | solution.py:552
  47.7 1.6 %collective-permute-start.29 = (bf16[384,512]{1,0:T(8,128)(2,1)S(1)}, bf16[384,512]{1,0:T(8,128)(2,1)S(1)}, u32[]{:S(2)}, u32[]{:S(2)}) collective-permute-start(bf16[384,512]{1,0:T(8,128)(2,1)S(1)} %get-tuple-element.58.w0), channel_id=1, source_target_pairs={{0,2},{1,3},{2,0},{3,1},{4,6},{5,7},{6,4},{7,5},{8,10},{9,11},{10,... | collective-permute-start | bytes 1179656 | tf_op jit(solution)/shard_map/ppermute | solution.py:412
  49.2 1.5 %collective-permute-done.24.refs_2_ = bf16[32,512]{1,0:T(8,128)(2,1)S(1)} collective-permute-done((bf16[32,512]{1,0:T(8,128)(2,1)S(1)}, bf16[32,512]{1,0:T(8,128)(2,1)S(1)}, u32[]{:S(2)}, u32[]{:S(2)}) %collective-permute-start.24) | collective-permute-done | bytes 32800 | tf_op jit(solution)/shard_map/ppermute | solution.py:552
  50.7 0.1 collective-permute-start.25
  50.8 0.0 copy-start.21
  50.8 2.6 %shard_map.237 = (bf16[1536,512]{1,0:T(8,128)(2,1)S(1)}, f32[1024,512]{1,0:T(8,128)S(1)}, bf16[512,512]{1,0:T(8,128)(2,1)S(1)}, bf16[512,512]{1,0:T(8,128)(2,1)S(1)}) custom-call(bf16[2048,512]{1,0:T(8,128)(2,1)S(1)} %get-tuple-element.45.emb, bf16[256,512]{1,0:T(8,128)(2,1)S(1)} %get-tuple-element.44.after.mine.middle, ...), custom_call_target="tpu_custom_call" | custom-call | flops 1610612736 | bytes 10240000 | tf_op jit(solution)/shard_map/pallas_call | solution.py:64
  53.5 0.0 copy-start.11
  53.5 5.8 %shard_map.239 = (bf16[256,512]{1,0:T(8,128)(2,1)S(1)}, bf16[256,512]{1,0:T(8,128)(2,1)S(1)}) custom-call(bf16[2048,512]{1,0:T(8,128)(2,1)S(1)} %get-tuple-element.45.emb, s32[2,2048]{1,0:T(2,128)S(1)} %copy-done.16, f32[1,512]{1,0:T(1,128)S(1)} %bitcast.7, bf16[1536,512]{1,0:T(8,128)(2,1)S(1)} %get-tuple-element.47.table, ...), custom_call_target="tpu_custom_call" | custom-call | flops 3489660928 | bytes 7555076 | tf_op jit(solution)/shard_map/pallas_call | solution.py:64
  59.3 0.6 collective-permute-start.26
  59.9 0.1 collective-permute-start.28
  60.0 0.4 collective-permute-start.30
  60.4 0.6 collective-permute-done.26.theirs
  61.0 0.1 shard_map.240
  61.1 1.6 %collective-permute-start.27 = (bf16[128,512]{1,0:T(8,128)(2,1)S(1)}, bf16[128,512]{1,0:T(8,128)(2,1)S(1)}, u32[]{:S(2)}, u32[]{:S(2)}) collective-permute-start(bf16[128,512]{1,0:T(8,128)(2,1)S(1)} %get-tuple-element.57), channel_id=1, source_target_pairs={{0,2},{1,3},{2,0},{3,1},{4,6},{5,7},{6,4},{7,5},{8,10},{9,11},{10,... | collective-permute-start | bytes 393224 | tf_op jit(solution)/shard_map/ppermute | solution.py:412
  62.7 4.3 %collective-permute-done.27.theirs = bf16[128,512]{1,0:T(8,128)(2,1)S(1)} collective-permute-done((bf16[128,512]{1,0:T(8,128)(2,1)S(1)}, bf16[128,512]{1,0:T(8,128)(2,1)S(1)}, u32[]{:S(2)}, u32[]{:S(2)}) %collective-permute-start.27) | collective-permute-done | bytes 131104 | tf_op jit(solution)/shard_map/ppermute | solution.py:412
  66.9 1.5 %shard_map.241 = bf16[128,512]{1,0:T(8,128)(2,1)} custom-call(bf16[256,512]{1,0:T(8,128)(2,1)S(1)} %get-tuple-element.44.after.mine.middle, bf16[128,512]{1,0:T(8,128)(2,1)S(1)} %get-tuple-element.56.mine, bf16[128,512]{1,0:T(8,128)(2,1)S(1)} %collective-permute-done.27.theirs, f32[1,512]{1,0:T(1,128)S(1)} %bitcast.5, ...), custom_call_target="tpu_custom_call" | custom-call | flops 201326592 | bytes 2230272 | tf_op jit(solution)/shard_map/pallas_call | solution.py:64
  (58 shorter events, 0.3 us)
Async XLA Ops:
  0.0 0.9 %copy-start.4 = (bf16[128,512]{1,0:T(8,128)(2,1)S(1)}, bf16[128,512]{1,0:T(8,128)(2,1)}, u32[]{:S(2)}) copy-start(bf16[128,512]{1,0:T(8,128)(2,1)} %e_out.1) | copy-start | bytes 393220
  0.0 1.0 %copy-start.5 = (bf16[128,512]{1,0:T(8,128)(2,1)S(1)}, bf16[128,512]{1,0:T(8,128)(2,1)}, u32[]{:S(2)}) copy-start(bf16[128,512]{1,0:T(8,128)(2,1)} %p_out.3) | copy-start | bytes 393220
  0.0 1.0 %copy-start = (bf16[512,128]{1,0:T(8,128)(2,1)S(1)}, bf16[512,128]{1,0:T(8,128)(2,1)}, u32[]{:S(2)}) copy-start(bf16[512,128]{1,0:T(8,128)(2,1)} %refs_0_.1) | copy-start | bytes 393220
  0.0 1.0 %copy-start.8 = (s32[1,4,64]{2,1,0:T(4,128)S(1)}, s32[1,4,64]{2,1,0:T(4,128)}, u32[]{:S(2)}) copy-start(s32[1,4,64]{2,1,0:T(4,128)} %send.2) | copy-start | bytes 3076
  0.0 1.2 %copy-start.1 = (bf16[384,512]{1,0:T(8,128)(2,1)S(1)}, bf16[384,512]{1,0:T(8,128)(2,1)}, u32[]{:S(2)}) copy-start(bf16[384,512]{1,0:T(8,128)(2,1)} %o_in.1) | copy-start | bytes 1179652
  0.0 1.2 %copy-start.6 = (bf16[128,512]{1,0:T(8,128)(2,1)S(1)}, bf16[128,512]{1,0:T(8,128)(2,1)}, u32[]{:S(2)}) copy-start(bf16[128,512]{1,0:T(8,128)(2,1)} %o_out.1) | copy-start | bytes 393220
  0.0 11.8 %copy-start.3 = (bf16[512,128]{1,0:T(8,128)(2,1)S(1)}, bf16[512,128]{1,0:T(8,128)(2,1)}, u32[]{:S(2)}) copy-start(bf16[512,128]{1,0:T(8,128)(2,1)} %refs_1_.1) | copy-start | bytes 393220
  1.2 12.4 %copy-start.12 = (bf16[384,512]{1,0:T(8,128)(2,1)S(1)}, bf16[384,512]{1,0:T(8,128)(2,1)}, u32[]{:S(2)}) copy-start(bf16[384,512]{1,0:T(8,128)(2,1)} %p_in.1) | copy-start | bytes 1179652
  1.2 12.4 %copy-start.13 = (bf16[256,512]{1,0:T(8,128)(2,1)S(1)}, bf16[256,512]{1,0:T(8,128)(2,1)}, u32[]{:S(2)}) copy-start(bf16[256,512]{1,0:T(8,128)(2,1)} %e_in.1) | copy-start | bytes 786436
  1.2 12.4 %copy-start.14 = (f32[4,2048]{1,0:T(4,128)S(1)}, f32[4,2048]{1,0:T(4,128)}, u32[]{:S(2)}) copy-start(f32[4,2048]{1,0:T(4,128)} %pgeom.1) | copy-start | bytes 98308
  1.2 12.4 %copy-start.15 = (f32[4,1024]{1,0:T(4,128)S(1)}, f32[4,1024]{1,0:T(4,128)}, u32[]{:S(2)}) copy-start(f32[4,1024]{1,0:T(4,128)} %egeom.1) | copy-start | bytes 49156
  1.3 12.4 %copy-start.17 = (f32[4,512]{1,0:T(4,128)S(1)}, f32[4,512]{1,0:T(4,128)}, u32[]{:S(2)}) copy-start(f32[4,512]{1,0:T(4,128)} %egeo.1) | copy-start | bytes 24580
  1.3 12.4 %copy-start.18 = (f32[4,512]{1,0:T(4,128)S(1)}, f32[4,512]{1,0:T(4,128)}, u32[]{:S(2)}) copy-start(f32[4,512]{1,0:T(4,128)} %pgeo.1) | copy-start | bytes 24580
  1.6 21.0 %copy-start.19 = (s32[2,1024]{1,0:T(2,128)S(1)}, s32[2,1024]{1,0:T(2,128)}, u32[]{:S(2)}) copy-start(s32[2,1024]{1,0:T(2,128)} %edges.3) | copy-start | bytes 24580
  1.6 21.0 %copy-start.20 = (f32[512]{0:T(512)S(1)}, f32[512]{0:T(512)}, u32[]{:S(2)}) copy-start(f32[512]{0:T(512)} %param.44) | copy-start | bytes 6148
  1.6 10.9 %collective-permute-start.8 = (bf16[384,512]{1,0:T(8,128)(2,1)S(1)}, bf16[384,512]{1,0:T(8,128)(2,1)S(1)}, u32[]{:S(2)}, u32[]{:S(2)}) collective-permute-start(bf16[384,512]{1,0:T(8,128)(2,1)S(1)} %get-tuple-element.38), channel_id=1, source_target_pairs={{0,2},{1,3},{2,0},{3,1},{4,6},{5,7},{6,4},{7,5},{8,10},{9,11},{10,... | collective-permute-start | bytes 1179656 | tf_op jit(solution)/shard_map/ppermute | solution.py:412
  3.2 5.4 %collective-permute-start = (bf16[64,128]{1,0:T(8,128)(2,1)S(1)}, bf16[64,128]{1,0:T(8,128)(2,1)S(1)}, u32[]{:S(2)}, u32[]{:S(2)}) collective-permute-start(bf16[64,128]{1,0:T(8,128)(2,1)S(1)} %get-tuple-element.32), channel_id=1, source_target_pairs={{0,4},{4,0},{8,12},{12,8},{1,5},{5,1},{9,13},{13,9},{2,6},{6,2},{1... | collective-permute-start | bytes 49160 | tf_op jit(solution)/shard_map/ppermute | solution.py:482
  3.6 5.0 %collective-permute-start.1 = (bf16[64,128]{1,0:T(8,128)(2,1)S(1)}, bf16[64,128]{1,0:T(8,128)(2,1)S(1)}, u32[]{:S(2)}, u32[]{:S(2)}) collective-permute-start(bf16[64,128]{1,0:T(8,128)(2,1)S(1)} %get-tuple-element.33), channel_id=1, source_target_pairs={{0,8},{4,12},{8,0},{12,4},{1,9},{5,13},{9,1},{13,5},{2,10},{6,14},... | collective-permute-start | bytes 49160 | tf_op jit(solution)/shard_map/ppermute | solution.py:482
  6.2 5.6 %collective-permute-start.2 = (bf16[64,128]{1,0:T(8,128)(2,1)S(1)}, bf16[64,128]{1,0:T(8,128)(2,1)S(1)}, u32[]{:S(2)}, u32[]{:S(2)}) collective-permute-start(bf16[64,128]{1,0:T(8,128)(2,1)S(1)} %get-tuple-element.34), channel_id=1, source_target_pairs={{4,8},{8,4},{5,9},{9,5},{6,10},{10,6},{7,11},{11,7},{20,24},{24,20... | collective-permute-start | bytes 49160 | tf_op jit(solution)/shard_map/ppermute | solution.py:482
  11.9 7.5 %collective-permute-start.3 = (bf16[1216,128]{1,0:T(8,128)(2,1)S(1)}, bf16[1216,128]{1,0:T(8,128)(2,1)S(1)}, u32[]{:S(2)}, u32[]{:S(2)}) collective-permute-start(bf16[1216,128]{1,0:T(8,128)(2,1)S(1)} %shard_map.228.after.l0), channel_id=1, source_target_pairs={{0,2},{1,3},{2,0},{3,1},{4,6},{5,7},{6,4},{7,5},{8,10},{9,11},{10,... | collective-permute-start | bytes 933896 | tf_op jit(solution)/shard_map/ppermute | solution.py:412
  12.6 7.4 %collective-permute-start.9 = (bf16[256,512]{1,0:T(8,128)(2,1)S(1)}, bf16[256,512]{1,0:T(8,128)(2,1)S(1)}, u32[]{:S(2)}, u32[]{:S(2)}) collective-permute-start(bf16[256,512]{1,0:T(8,128)(2,1)S(1)} %shard_map.231.across), channel_id=1, source_target_pairs={{0,16},{16,0},{1,17},{17,1},{2,18},{18,2},{3,19},{19,3},{4,20},{20... | collective-permute-start | bytes 786440 | tf_op jit(solution)/shard_map/ppermute | solution.py:421
  13.1 8.1 %collective-permute-start.6 = (bf16[384,512]{1,0:T(8,128)(2,1)S(1)}, bf16[384,512]{1,0:T(8,128)(2,1)S(1)}, u32[]{:S(2)}, u32[]{:S(2)}) collective-permute-start(bf16[384,512]{1,0:T(8,128)(2,1)S(1)} %copy-done.1), channel_id=1, source_target_pairs={{0,1},{1,0},{2,3},{3,2},{4,5},{5,4},{6,7},{7,6},{8,9},{9,8},{10,11... | collective-permute-start | bytes 1179656 | tf_op jit(solution)/shard_map/ppermute | solution.py:416
  13.1 6.3 %collective-permute-start.7 = (bf16[128,512]{1,0:T(8,128)(2,1)S(1)}, bf16[128,512]{1,0:T(8,128)(2,1)S(1)}, u32[]{:S(2)}, u32[]{:S(2)}) collective-permute-start(bf16[128,512]{1,0:T(8,128)(2,1)S(1)} %copy-done.6), channel_id=1, source_target_pairs={{0,1},{1,0},{2,3},{3,2},{4,5},{5,4},{6,7},{7,6},{8,9},{9,8},{10,11... | collective-permute-start | bytes 393224 | tf_op jit(solution)/shard_map/ppermute | solution.py:416
  13.7 7.1 %collective-permute-start.4 = (bf16[1216,128]{1,0:T(8,128)(2,1)S(1)}, bf16[1216,128]{1,0:T(8,128)(2,1)S(1)}, u32[]{:S(2)}, u32[]{:S(2)}) collective-permute-start(bf16[1216,128]{1,0:T(8,128)(2,1)S(1)} %shard_map.228.after.l0), channel_id=1, source_target_pairs={{0,1},{1,0},{2,3},{3,2},{4,5},{5,4},{6,7},{7,6},{8,9},{9,8},{10,11... | collective-permute-start | bytes 933896 | tf_op jit(solution)/shard_map/ppermute | solution.py:416
  19.4 3.2 %collective-permute-start.5 = (bf16[1216,128]{1,0:T(8,128)(2,1)S(1)}, bf16[1216,128]{1,0:T(8,128)(2,1)S(1)}, u32[]{:S(2)}, u32[]{:S(2)}) collective-permute-start(bf16[1216,128]{1,0:T(8,128)(2,1)S(1)} %get-tuple-element.37), channel_id=1, source_target_pairs={{0,1},{1,0},{2,3},{3,2},{4,5},{5,4},{6,7},{7,6},{8,9},{9,8},{10,11... | collective-permute-start | bytes 933896 | tf_op jit(solution)/shard_map/ppermute | solution.py:416
  19.5 3.1 %collective-permute-start.10 = (bf16[256,512]{1,0:T(8,128)(2,1)S(1)}, bf16[256,512]{1,0:T(8,128)(2,1)S(1)}, u32[]{:S(2)}, u32[]{:S(2)}) collective-permute-start(bf16[256,512]{1,0:T(8,128)(2,1)S(1)} %shard_map.231.across), channel_id=1, source_target_pairs={{0,1},{1,0},{2,3},{3,2},{4,5},{5,4},{6,7},{7,6},{8,9},{9,8},{10,11... | collective-permute-start | bytes 786440 | tf_op jit(solution)/shard_map/ppermute | solution.py:416
  20.0 2.6 %collective-permute-start.11 = (bf16[256,512]{1,0:T(8,128)(2,1)S(1)}, bf16[256,512]{1,0:T(8,128)(2,1)S(1)}, u32[]{:S(2)}, u32[]{:S(2)}) collective-permute-start(bf16[256,512]{1,0:T(8,128)(2,1)S(1)} %collective-permute-done.9.round_), channel_id=1, source_target_pairs={{0,1},{1,0},{2,3},{3,2},{4,5},{5,4},{6,7},{7,6},{8,9},{9,8},{10,11... | collective-permute-start | bytes 786440 | tf_op jit(solution)/shard_map/ppermute | solution.py:416
  20.7 16.4 %collective-permute-start.14 = (bf16[896,512]{1,0:T(8,128)(2,1)S(1)}, bf16[896,512]{1,0:T(8,128)(2,1)S(1)}, u32[]{:S(2)}, u32[]{:S(2)}) collective-permute-start(bf16[896,512]{1,0:T(8,128)(2,1)S(1)} %get-tuple-element.36.weights.w0), channel_id=1, source_target_pairs={{0,1},{1,0},{2,3},{3,2},{4,5},{5,4},{6,7},{7,6},{8,9},{9,8},{10,11... | collective-permute-start | bytes 2752520 | tf_op jit(solution)/shard_map/ppermute | solution.py:416
  21.2 9.7 %collective-permute-start.15 = (bf16[320,512]{1,0:T(8,128)(2,1)S(1)}, bf16[320,512]{1,0:T(8,128)(2,1)S(1)}, u32[]{:S(2)}, u32[]{:S(2)}) collective-permute-start(bf16[320,512]{1,0:T(8,128)(2,1)S(1)} %get-tuple-element.42), channel_id=1, source_target_pairs={{0,2},{1,3},{2,0},{3,1},{4,6},{5,7},{6,4},{7,5},{8,10},{9,11},{10,... | collective-permute-start | bytes 983048 | tf_op jit(solution)/shard_map/ppermute | solution.py:412
  22.6 16.2 %copy-start.2 = (bf16[256,512]{1,0:T(8,128)(2,1)S(1)}, bf16[256,512]{1,0:T(8,128)(2,1)}, u32[]{:S(2)}) copy-start(bf16[256,512]{1,0:T(8,128)(2,1)} %n_in.1) | copy-start | bytes 786436
  22.6 16.2 %copy-start.7 = (bf16[128,512]{1,0:T(8,128)(2,1)S(1)}, bf16[128,512]{1,0:T(8,128)(2,1)}, u32[]{:S(2)}) copy-start(bf16[128,512]{1,0:T(8,128)(2,1)} %n_out.3) | copy-start | bytes 393220
  22.6 16.2 %copy-start.9 = (f32[512]{0:T(512)S(1)}, f32[512]{0:T(512)}, u32[]{:S(2)}) copy-start(f32[512]{0:T(512)} %param.45) | copy-start | bytes 6148
  22.6 16.2 %copy-start.10 = (s32[1,4,32]{2,1,0:T(4,128)S(1)}, s32[1,4,32]{2,1,0:T(4,128)}, u32[]{:S(2)}) copy-start(s32[1,4,32]{2,1,0:T(4,128)} %send.3) | copy-start | bytes 1540
  27.4 1.6 %collective-permute-start.12 = (bf16[256,512]{1,0:T(8,128)(2,1)S(1)}, bf16[256,512]{1,0:T(8,128)(2,1)S(1)}, u32[]{:S(2)}, u32[]{:S(2)}) collective-permute-start(bf16[256,512]{1,0:T(8,128)(2,1)S(1)} %get-tuple-element.41), channel_id=1, source_target_pairs={{0,1},{1,0},{2,3},{3,2},{4,5},{5,4},{6,7},{7,6},{8,9},{9,8},{10,11... | collective-permute-start | bytes 786440 | tf_op jit(solution)/shard_map/ppermute | solution.py:416
  30.9 6.1 %collective-permute-start.16 = (bf16[192,512]{1,0:T(8,128)(2,1)S(1)}, bf16[192,512]{1,0:T(8,128)(2,1)S(1)}, u32[]{:S(2)}, u32[]{:S(2)}) collective-permute-start(bf16[192,512]{1,0:T(8,128)(2,1)S(1)} %get-tuple-element.43.w2), channel_id=1, source_target_pairs={{0,4},{4,0},{8,12},{12,8},{1,5},{5,1},{9,13},{13,9},{2,6},{6,2},{1... | collective-permute-start | bytes 589832 | tf_op jit(solution)/shard_map/ppermute | solution.py:425
  31.6 7.2 %collective-permute-start.13 = (bf16[256,512]{1,0:T(8,128)(2,1)S(1)}, bf16[256,512]{1,0:T(8,128)(2,1)S(1)}, u32[]{:S(2)}, u32[]{:S(2)}) collective-permute-start(bf16[256,512]{1,0:T(8,128)(2,1)S(1)} %shard_map.233.after.mine), channel_id=1, source_target_pairs={{0,2},{1,3},{2,0},{3,1},{4,6},{5,7},{6,4},{7,5},{8,10},{9,11},{10,... | collective-permute-start | bytes 786440 | tf_op jit(solution)/shard_map/ppermute | solution.py:412
  33.1 7.0 %collective-permute-start.20 = (bf16[256,512]{1,0:T(8,128)(2,1)S(1)}, bf16[256,512]{1,0:T(8,128)(2,1)S(1)}, u32[]{:S(2)}, u32[]{:S(2)}) collective-permute-start(bf16[256,512]{1,0:T(8,128)(2,1)S(1)} %get-tuple-element.46.first), channel_id=1, source_target_pairs={{0,16},{16,0},{1,17},{17,1},{2,18},{18,2},{3,19},{19,3},{4,20},{20... | collective-permute-start | bytes 786440 | tf_op jit(solution)/shard_map/ppermute | solution.py:421
  33.6 3.4 %collective-permute-start.17 = (bf16[192,512]{1,0:T(8,128)(2,1)S(1)}, bf16[192,512]{1,0:T(8,128)(2,1)S(1)}, u32[]{:S(2)}, u32[]{:S(2)}) collective-permute-start(bf16[192,512]{1,0:T(8,128)(2,1)S(1)} %get-tuple-element.43.w2), channel_id=1, source_target_pairs={{0,1},{1,0},{2,3},{3,2},{4,5},{5,4},{6,7},{7,6},{8,9},{9,8},{10,11... | collective-permute-start | bytes 589832 | tf_op jit(solution)/shard_map/ppermute | solution.py:416
  37.1 1.8 %collective-permute-start.18 = (bf16[192,512]{1,0:T(8,128)(2,1)S(1)}, bf16[192,512]{1,0:T(8,128)(2,1)S(1)}, u32[]{:S(2)}, u32[]{:S(2)}) collective-permute-start(bf16[192,512]{1,0:T(8,128)(2,1)S(1)} %collective-permute-done.16.w3), channel_id=1, source_target_pairs={{0,1},{1,0},{2,3},{3,2},{4,5},{5,4},{6,7},{7,6},{8,9},{9,8},{10,11... | collective-permute-start | bytes 589832 | tf_op jit(solution)/shard_map/ppermute | solution.py:416
  38.9 12.0 %copy-start.16 = (s32[2,2048]{1,0:T(2,128)S(1)}, s32[2,2048]{1,0:T(2,128)}, u32[]{:S(2)}) copy-start(s32[2,2048]{1,0:T(2,128)} %edges.5) | copy-start | bytes 49156
  40.2 10.6 %collective-permute-start.21 = (bf16[512,512]{1,0:T(8,128)(2,1)S(1)}, bf16[512,512]{1,0:T(8,128)(2,1)S(1)}, u32[]{:S(2)}, u32[]{:S(2)}) collective-permute-start(bf16[512,512]{1,0:T(8,128)(2,1)S(1)} %shard_map.236.pair), channel_id=1, source_target_pairs={{0,1},{1,0},{2,3},{3,2},{4,5},{5,4},{6,7},{7,6},{8,9},{9,8},{10,11... | collective-permute-start | bytes 1572872 | tf_op jit(solution)/shard_map/ppermute | solution.py:416
  40.2 10.6 %collective-permute-start.19 = (bf16[256,512]{1,0:T(8,128)(2,1)S(1)}, bf16[256,512]{1,0:T(8,128)(2,1)S(1)}, u32[]{:S(2)}, u32[]{:S(2)}) collective-permute-start(bf16[256,512]{1,0:T(8,128)(2,1)S(1)} %get-tuple-element.44.after.mine.middle), channel_id=1, source_target_pairs={{0,1},{1,0},{2,3},{3,2},{4,5},{5,4},{6,7},{7,6},{8,9},{9,8},{10,11... | collective-permute-start | bytes 786440 | tf_op jit(solution)/shard_map/ppermute | solution.py:416
  40.7 6.9 %collective-permute-start.22 = (bf16[32,512]{1,0:T(8,128)(2,1)S(1)}, bf16[32,512]{1,0:T(8,128)(2,1)S(1)}, u32[]{:S(2)}, u32[]{:S(2)}) collective-permute-start(bf16[32,512]{1,0:T(8,128)(2,1)S(1)} %get-tuple-element.51), channel_id=1, source_target_pairs={{0,4},{4,0},{8,12},{12,8},{1,5},{5,1},{9,13},{13,9},{2,6},{6,2},{1... | collective-permute-start | bytes 98312 | tf_op jit(solution)/shard_map/ppermute | solution.py:552
  42.1 7.1 %collective-permute-start.23 = (bf16[32,512]{1,0:T(8,128)(2,1)S(1)}, bf16[32,512]{1,0:T(8,128)(2,1)S(1)}, u32[]{:S(2)}, u32[]{:S(2)}) collective-permute-start(bf16[32,512]{1,0:T(8,128)(2,1)S(1)} %get-tuple-element.52), channel_id=1, source_target_pairs={{0,8},{4,12},{8,0},{12,4},{1,9},{5,13},{9,1},{13,5},{2,10},{6,14},... | collective-permute-start | bytes 98312 | tf_op jit(solution)/shard_map/ppermute | solution.py:552
  44.9 5.8 %collective-permute-start.24 = (bf16[32,512]{1,0:T(8,128)(2,1)S(1)}, bf16[32,512]{1,0:T(8,128)(2,1)S(1)}, u32[]{:S(2)}, u32[]{:S(2)}) collective-permute-start(bf16[32,512]{1,0:T(8,128)(2,1)S(1)} %get-tuple-element.53), channel_id=1, source_target_pairs={{4,8},{8,4},{5,9},{9,5},{6,10},{10,6},{7,11},{11,7},{20,24},{24,20... | collective-permute-start | bytes 98312 | tf_op jit(solution)/shard_map/ppermute | solution.py:552
  47.7 12.3 %collective-permute-start.29 = (bf16[384,512]{1,0:T(8,128)(2,1)S(1)}, bf16[384,512]{1,0:T(8,128)(2,1)S(1)}, u32[]{:S(2)}, u32[]{:S(2)}) collective-permute-start(bf16[384,512]{1,0:T(8,128)(2,1)S(1)} %get-tuple-element.58.w0), channel_id=1, source_target_pairs={{0,2},{1,3},{2,0},{3,1},{4,6},{5,7},{6,4},{7,5},{8,10},{9,11},{10,... | collective-permute-start | bytes 1179656 | tf_op jit(solution)/shard_map/ppermute | solution.py:412
  50.7 2.7 %collective-permute-start.25 = (bf16[96,512]{1,0:T(8,128)(2,1)S(1)}, bf16[96,512]{1,0:T(8,128)(2,1)S(1)}, u32[]{:S(2)}, u32[]{:S(2)}) collective-permute-start(bf16[96,512]{1,0:T(8,128)(2,1)S(1)} %shard_map.238.halo), channel_id=1, source_target_pairs={{0,1},{1,0},{2,3},{3,2},{4,5},{5,4},{6,7},{7,6},{8,9},{9,8},{10,11... | collective-permute-start | bytes 294920 | tf_op jit(solution)/shard_map/ppermute | solution.py:416
  50.8 2.6 %copy-start.21 = (f32[512]{0:T(512)S(1)}, f32[512]{0:T(512)}, u32[]{:S(2)}) copy-start(f32[512]{0:T(512)} %param.46) | copy-start | bytes 6148
  53.5 13.5 %copy-start.11 = (f32[512]{0:T(512)S(1)}, f32[512]{0:T(512)}, u32[]{:S(2)}) copy-start(f32[512]{0:T(512)} %param.47) | copy-start | bytes 6148
  59.3 1.7 %collective-permute-start.26 = (bf16[256,512]{1,0:T(8,128)(2,1)S(1)}, bf16[256,512]{1,0:T(8,128)(2,1)S(1)}, u32[]{:S(2)}, u32[]{:S(2)}) collective-permute-start(bf16[256,512]{1,0:T(8,128)(2,1)S(1)} %get-tuple-element.55), channel_id=1, source_target_pairs={{0,1},{1,0},{2,3},{3,2},{4,5},{5,4},{6,7},{7,6},{8,9},{9,8},{10,11... | collective-permute-start | bytes 786440 | tf_op jit(solution)/shard_map/ppermute | solution.py:416
  59.9 2.8 %collective-permute-start.28 = (bf16[384,512]{1,0:T(8,128)(2,1)S(1)}, bf16[384,512]{1,0:T(8,128)(2,1)S(1)}, u32[]{:S(2)}, u32[]{:S(2)}) collective-permute-start(bf16[384,512]{1,0:T(8,128)(2,1)S(1)} %get-tuple-element.58.w0), channel_id=1, source_target_pairs={{0,1},{1,0},{2,3},{3,2},{4,5},{5,4},{6,7},{7,6},{8,9},{9,8},{10,11... | collective-permute-start | bytes 1179656 | tf_op jit(solution)/shard_map/ppermute | solution.py:416
  60.0 2.7 %collective-permute-start.30 = (bf16[384,512]{1,0:T(8,128)(2,1)S(1)}, bf16[384,512]{1,0:T(8,128)(2,1)S(1)}, u32[]{:S(2)}, u32[]{:S(2)}) collective-permute-start(bf16[384,512]{1,0:T(8,128)(2,1)S(1)} %collective-permute-done.29.w2), channel_id=1, source_target_pairs={{0,1},{1,0},{2,3},{3,2},{4,5},{5,4},{6,7},{7,6},{8,9},{9,8},{10,11... | collective-permute-start | bytes 1179656 | tf_op jit(solution)/shard_map/ppermute | solution.py:416
  61.1 5.8 %collective-permute-start.27 = (bf16[128,512]{1,0:T(8,128)(2,1)S(1)}, bf16[128,512]{1,0:T(8,128)(2,1)S(1)}, u32[]{:S(2)}, u32[]{:S(2)}) collective-permute-start(bf16[128,512]{1,0:T(8,128)(2,1)S(1)} %get-tuple-element.57), channel_id=1, source_target_pairs={{0,2},{1,3},{2,0},{3,1},{4,6},{5,7},{6,4},{7,5},{8,10},{9,11},{10,... | collective-permute-start | bytes 393224 | tf_op jit(solution)/shard_map/ppermute | solution.py:412

commit v12 on v11

--- a/solution.py
+++ b/solution.py
@@ -20,9 +20,16 @@
 F32 = jnp.float32
 
 
+def silu_of_half(h):
+    return h + h * jnp.tanh(h)
+
+
 def silu(v):
-    h = 0.5 * v
-    return h + h * jnp.tanh(h)
+    return silu_of_half(0.5 * v)
+
+
+def halved(v):
+    return (v.astype(F32) * 0.5).astype(BF16)
 
 
 def region_of(delta):
@@ -96,11 +103,14 @@
     return silu(dot_first(left, right)).astype(BF16)
 
 
-def layer_norm(v):
+def layer_norm(v, live=None):
     width = v.shape[-1]
     centered = v - jnp.sum(v, axis=-1, keepdims=True) * (1.0 / width)
     spread = jnp.sum(centered * centered, axis=-1, keepdims=True) * (1.0 / width)
-    return centered * lax.rsqrt(spread + 1e-05)
+    factor = lax.rsqrt(spread + 1e-05)
+    if live is not None:
+        factor = jnp.where(live, factor, 0.0)
+    return centered * factor
 
 
 def hot(cond):
@@ -223,13 +233,21 @@
 
 def edge_blocks(edges, live_edges, first_stage, w_out, messages, totals):
     count = edges.shape[1]
+    steps = count // STEP
     row = lax.broadcasted_iota(I16, (totals.shape[0], 1), 0)
     quarter = lax.axis_index("sub")
-    for first in range(0, count, STEP):
-        hidden = silu(first_stage(first)).astype(BF16)
-        message = layer_norm(dot(hidden, w_out))
+    sums, raw = {}, {}
+    for turn in range(steps + 2):
+        if turn < steps:
+            sums[turn] = first_stage(turn * STEP)
+        if 0 <= turn - 1 < steps:
+            raw[turn - 1] = dot(silu_of_half(sums.pop(turn - 1)).astype(BF16), w_out)
+        if turn < 2:
+            continue
+        first = (turn - 2) * STEP
         place = lax.broadcasted_iota(jnp.int32, (STEP, 1), 0) + (first + quarter * count)
-        messages[first : first + STEP, :] = jnp.where(place < live_edges, message, 0.0).astype(BF16)
+        message = layer_norm(raw.pop(turn - 2), place < live_edges)
+        messages[first : first + STEP, :] = message.astype(BF16)
         done = first + STEP
         if done % GATHERED == 0 or done == count:
             begin = (first // GATHERED) * GATHERED
@@ -277,11 +295,11 @@
 
     w_in = joined(stack, 0, k_in)
     halo_first, got = grid_rows + mesh_rows, full.shape[0] - grid_rows - mesh_rows
-    table[:d, :] = w_in[:d, :]
-    table[d : d + grid_rows, :] = dot(full[:grid_rows, :], w_in[d : 2 * d, :]).astype(BF16)
+    table[:d, :] = halved(w_in[:d, :])
+    table[d : d + grid_rows, :] = halved(dot(full[:grid_rows, :], w_in[d : 2 * d, :]))
     base = d + grid_rows + mesh_rows
-    table[d + grid_rows : base, :] = dot(full[grid_rows:halo_first, :], w_in[2 * d :, :]).astype(BF16)
-    table[base : base + got, :] = dot(full[halo_first:, :], w_in[d : 2 * d, :]).astype(BF16)
+    table[d + grid_rows : base, :] = halved(dot(full[grid_rows:halo_first, :], w_in[2 * d :, :]))
+    table[base : base + got, :] = halved(dot(full[halo_first:, :], w_in[d : 2 * d, :]))
     if base + got < table.shape[0]:
         table[base + got :, :] = jnp.zeros((table.shape[0] - base - got, d), BF16)
     targets = halo_targets(plan, slots, grid_rows, table.shape[0] - base)
@@ -354,9 +372,9 @@
     w_in = joined(stack, 0, k_in)
     w_out[...] = joined(stack, k_in, d // 4)
     w_source[...] = w_in[d : 2 * d, :]
-    table[:d, :] = w_in[:d, :]
-    table[d : d + node_rows, :] = dot(full[...], w_in[d : 2 * d, :]).astype(BF16)
-    table[d + node_rows :, :] = dot(full[...], w_in[2 * d :, :]).astype(BF16)
+    table[:d, :] = halved(w_in[:d, :])
+    table[d : d + node_rows, :] = halved(dot(full[...], w_in[d : 2 * d, :]))
+    table[d + node_rows :, :] = halved(dot(full[...], w_in[2 * d :, :]))
     lane = lax.broadcasted_iota(I16, (1, node_rows), 1)
     for first in range(0, pre.shape[0], STEP):
         pre[first : first + STEP, :] = dot(own_chosen(emb, edges, lane, first), table[...])
@@ -373,7 +391,7 @@
 ):
     d = pre.shape[1]
     got = halo[...] + halo_beside[...]
-    halo_table[: got.shape[0], :] = dot(got, w_source[...]).astype(BF16)
+    halo_table[: got.shape[0], :] = halved(dot(got, w_source[...]))
     if got.shape[0] < halo_table.shape[0]:
         halo_table[got.shape[0] :, :] = jnp.zeros((halo_table.shape[0] - got.shape[0], d), BF16)
     targets = halo_targets(plan, slots, node_rows, halo_table.shape[0])

time: 68.6 us -> 68.4 us (level)
  no operation moved by 1% of the time
where the time goes in v12:
time: 68.4 us; the launch traced here: 68.2 us
  starting transfers between devices  25 us (37%)
  waiting for transfers between devices  22.2 us (32%)
  Pallas kernels  18.1 us (26%)
  between operations  1.75 us (3%)
  local copies, waits for them, and re-layouts  1.28 us (2%)
    pallas_call x16, Pallas kernels, call(): pl.pallas_call(body, out_shape=tuple(outs), in_specs=specs, out_specs=tup...  18.1 us
    ppermute x6, waiting for transfers between devices, to_chip(): return lax.ppermute(v, 'sub', [(i, i ^ 2) for i in range(4)])  11.8 us
    ppermute x6, starting transfers between devices, local(): lax.ppermute(v, 'dom', entry[0])  11.6 us
    ppermute x6, starting transfers between devices, to_chip(): return lax.ppermute(v, 'sub', [(i, i ^ 2) for i in range(4)])  8.15 us
    ppermute x6, waiting for transfers between devices, local(): lax.ppermute(v, 'dom', entry[0])  4.74 us
    ppermute x16, starting transfers between devices, to_core(): return lax.ppermute(v, 'sub', [(i, i ^ 1) for i in range(4)])  3.43 us
    ppermute x1, waiting for transfers between devices, to_partition(): lax.ppermute(v, 'dom', [(i, i ^ 1) for i in range(lax.axis_size('dom'))])  3.42 us
    ppermute x16, waiting for transfers between devices, to_core(): return lax.ppermute(v, 'sub', [(i, i ^ 1) for i in range(4)])  2.21 us
  transfers between devices with their start and end apart: 31, of which 10 were waited for; matrix products, arithmetic and copies ran while one was open for 0% of the time, Pallas kernels for 24%

profile of v12, /device:TPU:12, one launch (start us, length us, event | category | flops | bytes accessed | tf_op | source)
XLA Modules:
  0.0 68.2 jit_solution(15852855766704684960)
XLA Ops:
  0.1 0.8 %copy-done.4 = bf16[128,512]{1,0:T(8,128)(2,1)S(1)} copy-done((bf16[128,512]{1,0:T(8,128)(2,1)S(1)}, bf16[128,512]{1,0:T(8,128)(2,1)}, u32[]{:S(2)}) %copy-start.4) | copy-done | bytes 131096
  0.9 0.1 copy-done.5
  1.0 0.1 copy-done
  1.0 0.2 copy-done.1
  1.2 0.0 copy-done.6
  1.3 0.0 copy-start.17
  1.3 0.0 copy-start.18
  1.3 0.3 shard_map.227
  1.6 0.0 copy-start.19
  1.6 0.0 copy-start.20
  1.6 1.6 %collective-permute-start.8 = (bf16[384,512]{1,0:T(8,128)(2,1)S(1)}, bf16[384,512]{1,0:T(8,128)(2,1)S(1)}, u32[]{:S(2)}, u32[]{:S(2)}) collective-permute-start(bf16[384,512]{1,0:T(8,128)(2,1)S(1)} %get-tuple-element.38), channel_id=1, source_target_pairs={{0,2},{1,3},{2,0},{3,1},{4,6},{5,7},{6,4},{7,5},{8,10},{9,11},{10,... | collective-permute-start | bytes 1179656 | tf_op jit(solution)/shard_map/ppermute | solution.py:430
  3.2 0.5 collective-permute-start
  3.6 2.6 %collective-permute-start.1 = (bf16[64,128]{1,0:T(8,128)(2,1)S(1)}, bf16[64,128]{1,0:T(8,128)(2,1)S(1)}, u32[]{:S(2)}, u32[]{:S(2)}) collective-permute-start(bf16[64,128]{1,0:T(8,128)(2,1)S(1)} %get-tuple-element.33), channel_id=1, source_target_pairs={{0,8},{4,12},{8,0},{12,4},{1,9},{5,13},{9,1},{13,5},{2,10},{6,14},... | collective-permute-start | bytes 49160 | tf_op jit(solution)/shard_map/ppermute | solution.py:500
  6.2 2.3 %collective-permute-start.2 = (bf16[64,128]{1,0:T(8,128)(2,1)S(1)}, bf16[64,128]{1,0:T(8,128)(2,1)S(1)}, u32[]{:S(2)}, u32[]{:S(2)}) collective-permute-start(bf16[64,128]{1,0:T(8,128)(2,1)S(1)} %get-tuple-element.34), channel_id=1, source_target_pairs={{4,8},{8,4},{5,9},{9,5},{6,10},{10,6},{7,11},{11,7},{20,24},{24,20... | collective-permute-start | bytes 49160 | tf_op jit(solution)/shard_map/ppermute | solution.py:500
  8.6 0.0 collective-permute-done.refs_2_
  8.6 3.2 %collective-permute-done.2.refs_4_ = bf16[64,128]{1,0:T(8,128)(2,1)S(1)} collective-permute-done((bf16[64,128]{1,0:T(8,128)(2,1)S(1)}, bf16[64,128]{1,0:T(8,128)(2,1)S(1)}, u32[]{:S(2)}, u32[]{:S(2)}) %collective-permute-start.2) | collective-permute-done | bytes 16416 | tf_op jit(solution)/shard_map/ppermute | solution.py:500
  11.9 0.6 collective-permute-start.3
  12.5 0.1 collective-permute-done.8.source.early
  12.6 0.6 collective-permute-start.9
  13.1 0.5 collective-permute-start.7
  13.7 0.0 collective-permute-start.4
  13.7 1.8 %shard_map.229 = (bf16[896,512]{1,0:T(8,128)(2,1)S(1)}, bf16[1024,512]{1,0:T(8,128)(2,1)S(1)}, bf16[2048,512]{1,0:T(8,128)(2,1)S(1)}) custom-call(bf16[256,512]{1,0:T(8,128)(2,1)S(1)} %copy-done.13, bf16[128,512]{1,0:T(8,128)(2,1)S(1)} %copy-done.4, bf16[384,512]{1,0:T(8,128)(2,1)S(1)} %copy-done.12, bf16[128,512]{1,0:T(8,128)(2,1)S(1)} %copy-done.5, ...), custom_call_target="tpu_custom_call" | custom-call | flops 402653184 | bytes 5357568 | tf_op jit(solution)/shard_map/pallas_call | solution.py:71
  15.5 3.9 %collective-permute-done.3.lat.l1 = bf16[1216,128]{1,0:T(8,128)(2,1)S(1)} collective-permute-done((bf16[1216,128]{1,0:T(8,128)(2,1)S(1)}, bf16[1216,128]{1,0:T(8,128)(2,1)S(1)}, u32[]{:S(2)}, u32[]{:S(2)}) %collective-permute-start.3) | collective-permute-done | bytes 311328 | tf_op jit(solution)/shard_map/ppermute | solution.py:430
  19.4 0.1 collective-permute-start.5
  19.5 0.5 collective-permute-start.10
  20.0 0.1 collective-permute-start.11
  20.7 0.5 collective-permute-start.14
  21.2 1.4 %collective-permute-start.15 = (bf16[320,512]{1,0:T(8,128)(2,1)S(1)}, bf16[320,512]{1,0:T(8,128)(2,1)S(1)}, u32[]{:S(2)}, u32[]{:S(2)}) collective-permute-start(bf16[320,512]{1,0:T(8,128)(2,1)S(1)} %get-tuple-element.42), channel_id=1, source_target_pairs={{0,2},{1,3},{2,0},{3,1},{4,6},{5,7},{6,4},{7,5},{8,10},{9,11},{10,... | collective-permute-start | bytes 983048 | tf_op jit(solution)/shard_map/ppermute | solution.py:430
  22.6 0.0 copy-start.2
  22.6 0.0 copy-start.7
  22.6 0.0 copy-start.9
  22.6 0.0 copy-start.10
  22.7 4.7 %shard_map.232 = (bf16[256,512]{1,0:T(8,128)(2,1)S(1)}, bf16[256,512]{1,0:T(8,128)(2,1)S(1)}, bf16[256,512]{1,0:T(8,128)(2,1)S(1)}) custom-call(bf16[1024,512]{1,0:T(8,128)(2,1)S(1)} %get-tuple-element.35.emb, s32[2,1024]{1,0:T(2,128)S(1)} %copy-done.19, f32[1,512]{1,0:T(1,128)S(1)} %bitcast.6, bf16[1216,128]{1,0:T(8,128)(2,1)S(1)} %shard_map.228.after.l0, ...), custom_call_target="tpu_custom_call" | custom-call | flops 2952790016 | bytes 5187588 | tf_op jit(solution)/shard_map/pallas_call | solution.py:71
  27.4 0.1 collective-permute-start.12
  27.5 1.5 %collective-permute-done.12.theirs = bf16[256,512]{1,0:T(8,128)(2,1)S(1)} collective-permute-done((bf16[256,512]{1,0:T(8,128)(2,1)S(1)}, bf16[256,512]{1,0:T(8,128)(2,1)S(1)}, u32[]{:S(2)}, u32[]{:S(2)}) %collective-permute-start.12) | collective-permute-done | bytes 262176 | tf_op jit(solution)/shard_map/ppermute | solution.py:434
  29.0 0.1 shard_map.233.after.mine
  29.1 1.9 %collective-permute-done.15.source = bf16[320,512]{1,0:T(8,128)(2,1)S(1)} collective-permute-done((bf16[320,512]{1,0:T(8,128)(2,1)S(1)}, bf16[320,512]{1,0:T(8,128)(2,1)S(1)}, u32[]{:S(2)}, u32[]{:S(2)}) %collective-permute-start.15) | collective-permute-done | bytes 327712 | tf_op jit(solution)/shard_map/ppermute | solution.py:430
  30.9 0.7 %collective-permute-start.16 = (bf16[192,512]{1,0:T(8,128)(2,1)S(1)}, bf16[192,512]{1,0:T(8,128)(2,1)S(1)}, u32[]{:S(2)}, u32[]{:S(2)}) collective-permute-start(bf16[192,512]{1,0:T(8,128)(2,1)S(1)} %get-tuple-element.43.w2), channel_id=1, source_target_pairs={{0,4},{4,0},{8,12},{12,8},{1,5},{5,1},{9,13},{13,9},{2,6},{6,2},{1... | collective-permute-start | bytes 589832 | tf_op jit(solution)/shard_map/ppermute | solution.py:443
  31.6 1.5 %collective-permute-start.13 = (bf16[256,512]{1,0:T(8,128)(2,1)S(1)}, bf16[256,512]{1,0:T(8,128)(2,1)S(1)}, u32[]{:S(2)}, u32[]{:S(2)}) collective-permute-start(bf16[256,512]{1,0:T(8,128)(2,1)S(1)} %shard_map.233.after.mine), channel_id=1, source_target_pairs={{0,2},{1,3},{2,0},{3,1},{4,6},{5,7},{6,4},{7,5},{8,10},{9,11},{10,... | collective-permute-start | bytes 786440 | tf_op jit(solution)/shard_map/ppermute | solution.py:430
  33.1 0.5 collective-permute-start.20
  33.6 3.4 %collective-permute-done.16.w3 = bf16[192,512]{1,0:T(8,128)(2,1)S(1)} collective-permute-done((bf16[192,512]{1,0:T(8,128)(2,1)S(1)}, bf16[192,512]{1,0:T(8,128)(2,1)S(1)}, u32[]{:S(2)}, u32[]{:S(2)}) %collective-permute-start.16) | collective-permute-done | bytes 196640 | tf_op jit(solution)/shard_map/ppermute | solution.py:443
  37.1 1.7 %collective-permute-done.13.theirs = bf16[256,512]{1,0:T(8,128)(2,1)S(1)} collective-permute-done((bf16[256,512]{1,0:T(8,128)(2,1)S(1)}, bf16[256,512]{1,0:T(8,128)(2,1)S(1)}, u32[]{:S(2)}, u32[]{:S(2)}) %collective-permute-start.13) | collective-permute-done | bytes 262176 | tf_op jit(solution)/shard_map/ppermute | solution.py:430
  38.9 0.0 copy-start.16
  38.9 1.2 %shard_map.235 = (bf16[256,512]{1,0:T(8,128)(2,1)S(1)}, bf16[384,512]{1,0:T(8,128)(2,1)S(1)}, bf16[32,512]{1,0:T(8,128)(2,1)S(1)}, bf16[32,512]{1,0:T(8,128)(2,1)S(1)}, bf16[32,512]{1,0:T(8,128)(2,1)S(1)}) custom-call(bf16[256,512]{1,0:T(8,128)(2,1)S(1)} %get-tuple-element.39.mesh, bf16[256,512]{1,0:T(8,128)(2,1)S(1)} %shard_map.233.after.mine, ...), custom_call_target="tpu_custom_call" | custom-call | flops 402653184 | bytes 4557312 | tf_op jit(solution)/shard_map/pallas_call | solution.py:71
  40.2 0.1 collective-permute-start.21
  40.2 0.5 collective-permute-start.19
  40.7 1.4 %collective-permute-start.22 = (bf16[32,512]{1,0:T(8,128)(2,1)S(1)}, bf16[32,512]{1,0:T(8,128)(2,1)S(1)}, u32[]{:S(2)}, u32[]{:S(2)}) collective-permute-start(bf16[32,512]{1,0:T(8,128)(2,1)S(1)} %get-tuple-element.51), channel_id=1, source_target_pairs={{0,4},{4,0},{8,12},{12,8},{1,5},{5,1},{9,13},{13,9},{2,6},{6,2},{1... | collective-permute-start | bytes 98312 | tf_op jit(solution)/shard_map/ppermute | solution.py:570
  42.1 2.8 %collective-permute-start.23 = (bf16[32,512]{1,0:T(8,128)(2,1)S(1)}, bf16[32,512]{1,0:T(8,128)(2,1)S(1)}, u32[]{:S(2)}, u32[]{:S(2)}) collective-permute-start(bf16[32,512]{1,0:T(8,128)(2,1)S(1)} %get-tuple-element.52), channel_id=1, source_target_pairs={{0,8},{4,12},{8,0},{12,4},{1,9},{5,13},{9,1},{13,5},{2,10},{6,14},... | collective-permute-start | bytes 98312 | tf_op jit(solution)/shard_map/ppermute | solution.py:570
  44.9 2.1 %collective-permute-start.24 = (bf16[32,512]{1,0:T(8,128)(2,1)S(1)}, bf16[32,512]{1,0:T(8,128)(2,1)S(1)}, u32[]{:S(2)}, u32[]{:S(2)}) collective-permute-start(bf16[32,512]{1,0:T(8,128)(2,1)S(1)} %get-tuple-element.53), channel_id=1, source_target_pairs={{4,8},{8,4},{5,9},{9,5},{6,10},{10,6},{7,11},{11,7},{20,24},{24,20... | collective-permute-start | bytes 98312 | tf_op jit(solution)/shard_map/ppermute | solution.py:570
  47.7 1.6 %collective-permute-start.29 = (bf16[384,512]{1,0:T(8,128)(2,1)S(1)}, bf16[384,512]{1,0:T(8,128)(2,1)S(1)}, u32[]{:S(2)}, u32[]{:S(2)}) collective-permute-start(bf16[384,512]{1,0:T(8,128)(2,1)S(1)} %get-tuple-element.58.w0), channel_id=1, source_target_pairs={{0,2},{1,3},{2,0},{3,1},{4,6},{5,7},{6,4},{7,5},{8,10},{9,11},{10,... | collective-permute-start | bytes 1179656 | tf_op jit(solution)/shard_map/ppermute | solution.py:430
  49.2 1.5 %collective-permute-done.24.refs_2_ = bf16[32,512]{1,0:T(8,128)(2,1)S(1)} collective-permute-done((bf16[32,512]{1,0:T(8,128)(2,1)S(1)}, bf16[32,512]{1,0:T(8,128)(2,1)S(1)}, u32[]{:S(2)}, u32[]{:S(2)}) %collective-permute-start.24) | collective-permute-done | bytes 32800 | tf_op jit(solution)/shard_map/ppermute | solution.py:570
  50.7 0.1 collective-permute-start.25
  50.8 0.0 copy-start.21
  50.8 2.6 %shard_map.237 = (bf16[1536,512]{1,0:T(8,128)(2,1)S(1)}, f32[1024,512]{1,0:T(8,128)S(1)}, bf16[512,512]{1,0:T(8,128)(2,1)S(1)}, bf16[512,512]{1,0:T(8,128)(2,1)S(1)}) custom-call(bf16[2048,512]{1,0:T(8,128)(2,1)S(1)} %get-tuple-element.45.emb, bf16[256,512]{1,0:T(8,128)(2,1)S(1)} %get-tuple-element.44.after.mine.middle, ...), custom_call_target="tpu_custom_call" | custom-call | flops 1610612736 | bytes 10240000 | tf_op jit(solution)/shard_map/pallas_call | solution.py:71
  53.5 0.0 copy-start.11
  53.5 5.7 %shard_map.239 = (bf16[256,512]{1,0:T(8,128)(2,1)S(1)}, bf16[256,512]{1,0:T(8,128)(2,1)S(1)}) custom-call(bf16[2048,512]{1,0:T(8,128)(2,1)S(1)} %get-tuple-element.45.emb, s32[2,2048]{1,0:T(2,128)S(1)} %copy-done.16, f32[1,512]{1,0:T(1,128)S(1)} %bitcast.7, bf16[1536,512]{1,0:T(8,128)(2,1)S(1)} %get-tuple-element.47.table, ...), custom_call_target="tpu_custom_call" | custom-call | flops 3489660928 | bytes 7555076 | tf_op jit(solution)/shard_map/pallas_call | solution.py:71
  59.2 0.6 collective-permute-start.26
  59.7 0.1 collective-permute-start.28
  59.8 0.4 collective-permute-start.30
  60.2 0.6 collective-permute-done.26.theirs
  60.9 0.1 shard_map.240
  60.9 1.6 %collective-permute-start.27 = (bf16[128,512]{1,0:T(8,128)(2,1)S(1)}, bf16[128,512]{1,0:T(8,128)(2,1)S(1)}, u32[]{:S(2)}, u32[]{:S(2)}) collective-permute-start(bf16[128,512]{1,0:T(8,128)(2,1)S(1)} %get-tuple-element.57), channel_id=1, source_target_pairs={{0,2},{1,3},{2,0},{3,1},{4,6},{5,7},{6,4},{7,5},{8,10},{9,11},{10,... | collective-permute-start | bytes 393224 | tf_op jit(solution)/shard_map/ppermute | solution.py:430
  62.5 4.3 %collective-permute-done.27.theirs = bf16[128,512]{1,0:T(8,128)(2,1)S(1)} collective-permute-done((bf16[128,512]{1,0:T(8,128)(2,1)S(1)}, bf16[128,512]{1,0:T(8,128)(2,1)S(1)}, u32[]{:S(2)}, u32[]{:S(2)}) %collective-permute-start.27) | collective-permute-done | bytes 131104 | tf_op jit(solution)/shard_map/ppermute | solution.py:430
  66.8 1.5 %shard_map.241 = bf16[128,512]{1,0:T(8,128)(2,1)} custom-call(bf16[256,512]{1,0:T(8,128)(2,1)S(1)} %get-tuple-element.44.after.mine.middle, bf16[128,512]{1,0:T(8,128)(2,1)S(1)} %get-tuple-element.56.mine, bf16[128,512]{1,0:T(8,128)(2,1)S(1)} %collective-permute-done.27.theirs, f32[1,512]{1,0:T(1,128)S(1)} %bitcast.5, ...), custom_call_target="tpu_custom_call" | custom-call | flops 201326592 | bytes 2230272 | tf_op jit(solution)/shard_map/pallas_call | solution.py:71
  (58 shorter events, 0.3 us)
Async XLA Ops:
  0.0 0.9 %copy-start.4 = (bf16[128,512]{1,0:T(8,128)(2,1)S(1)}, bf16[128,512]{1,0:T(8,128)(2,1)}, u32[]{:S(2)}) copy-start(bf16[128,512]{1,0:T(8,128)(2,1)} %e_out.1) | copy-start | bytes 393220
  0.0 1.0 %copy-start.5 = (bf16[128,512]{1,0:T(8,128)(2,1)S(1)}, bf16[128,512]{1,0:T(8,128)(2,1)}, u32[]{:S(2)}) copy-start(bf16[128,512]{1,0:T(8,128)(2,1)} %p_out.3) | copy-start | bytes 393220
  0.0 1.0 %copy-start = (bf16[512,128]{1,0:T(8,128)(2,1)S(1)}, bf16[512,128]{1,0:T(8,128)(2,1)}, u32[]{:S(2)}) copy-start(bf16[512,128]{1,0:T(8,128)(2,1)} %refs_0_.1) | copy-start | bytes 393220
  0.0 1.0 %copy-start.8 = (s32[1,4,64]{2,1,0:T(4,128)S(1)}, s32[1,4,64]{2,1,0:T(4,128)}, u32[]{:S(2)}) copy-start(s32[1,4,64]{2,1,0:T(4,128)} %send.2) | copy-start | bytes 3076
  0.0 1.2 %copy-start.1 = (bf16[384,512]{1,0:T(8,128)(2,1)S(1)}, bf16[384,512]{1,0:T(8,128)(2,1)}, u32[]{:S(2)}) copy-start(bf16[384,512]{1,0:T(8,128)(2,1)} %o_in.1) | copy-start | bytes 1179652
  0.0 1.2 %copy-start.6 = (bf16[128,512]{1,0:T(8,128)(2,1)S(1)}, bf16[128,512]{1,0:T(8,128)(2,1)}, u32[]{:S(2)}) copy-start(bf16[128,512]{1,0:T(8,128)(2,1)} %o_out.1) | copy-start | bytes 393220
  0.0 11.8 %copy-start.3 = (bf16[512,128]{1,0:T(8,128)(2,1)S(1)}, bf16[512,128]{1,0:T(8,128)(2,1)}, u32[]{:S(2)}) copy-start(bf16[512,128]{1,0:T(8,128)(2,1)} %refs_1_.1) | copy-start | bytes 393220
  1.2 12.4 %copy-start.12 = (bf16[384,512]{1,0:T(8,128)(2,1)S(1)}, bf16[384,512]{1,0:T(8,128)(2,1)}, u32[]{:S(2)}) copy-start(bf16[384,512]{1,0:T(8,128)(2,1)} %p_in.1) | copy-start | bytes 1179652
  1.2 12.4 %copy-start.13 = (bf16[256,512]{1,0:T(8,128)(2,1)S(1)}, bf16[256,512]{1,0:T(8,128)(2,1)}, u32[]{:S(2)}) copy-start(bf16[256,512]{1,0:T(8,128)(2,1)} %e_in.1) | copy-start | bytes 786436
  1.2 12.4 %copy-start.14 = (f32[4,2048]{1,0:T(4,128)S(1)}, f32[4,2048]{1,0:T(4,128)}, u32[]{:S(2)}) copy-start(f32[4,2048]{1,0:T(4,128)} %pgeom.1) | copy-start | bytes 98308
  1.2 12.4 %copy-start.15 = (f32[4,1024]{1,0:T(4,128)S(1)}, f32[4,1024]{1,0:T(4,128)}, u32[]{:S(2)}) copy-start(f32[4,1024]{1,0:T(4,128)} %egeom.1) | copy-start | bytes 49156
  1.3 12.4 %copy-start.17 = (f32[4,512]{1,0:T(4,128)S(1)}, f32[4,512]{1,0:T(4,128)}, u32[]{:S(2)}) copy-start(f32[4,512]{1,0:T(4,128)} %egeo.1) | copy-start | bytes 24580
  1.3 12.4 %copy-start.18 = (f32[4,512]{1,0:T(4,128)S(1)}, f32[4,512]{1,0:T(4,128)}, u32[]{:S(2)}) copy-start(f32[4,512]{1,0:T(4,128)} %pgeo.1) | copy-start | bytes 24580
  1.6 21.0 %copy-start.19 = (s32[2,1024]{1,0:T(2,128)S(1)}, s32[2,1024]{1,0:T(2,128)}, u32[]{:S(2)}) copy-start(s32[2,1024]{1,0:T(2,128)} %edges.3) | copy-start | bytes 24580
  1.6 21.0 %copy-start.20 = (f32[512]{0:T(512)S(1)}, f32[512]{0:T(512)}, u32[]{:S(2)}) copy-start(f32[512]{0:T(512)} %param.44) | copy-start | bytes 6148
  1.6 10.9 %collective-permute-start.8 = (bf16[384,512]{1,0:T(8,128)(2,1)S(1)}, bf16[384,512]{1,0:T(8,128)(2,1)S(1)}, u32[]{:S(2)}, u32[]{:S(2)}) collective-permute-start(bf16[384,512]{1,0:T(8,128)(2,1)S(1)} %get-tuple-element.38), channel_id=1, source_target_pairs={{0,2},{1,3},{2,0},{3,1},{4,6},{5,7},{6,4},{7,5},{8,10},{9,11},{10,... | collective-permute-start | bytes 1179656 | tf_op jit(solution)/shard_map/ppermute | solution.py:430
  3.2 5.4 %collective-permute-start = (bf16[64,128]{1,0:T(8,128)(2,1)S(1)}, bf16[64,128]{1,0:T(8,128)(2,1)S(1)}, u32[]{:S(2)}, u32[]{:S(2)}) collective-permute-start(bf16[64,128]{1,0:T(8,128)(2,1)S(1)} %get-tuple-element.32), channel_id=1, source_target_pairs={{0,4},{4,0},{8,12},{12,8},{1,5},{5,1},{9,13},{13,9},{2,6},{6,2},{1... | collective-permute-start | bytes 49160 | tf_op jit(solution)/shard_map/ppermute | solution.py:500
  3.6 5.0 %collective-permute-start.1 = (bf16[64,128]{1,0:T(8,128)(2,1)S(1)}, bf16[64,128]{1,0:T(8,128)(2,1)S(1)}, u32[]{:S(2)}, u32[]{:S(2)}) collective-permute-start(bf16[64,128]{1,0:T(8,128)(2,1)S(1)} %get-tuple-element.33), channel_id=1, source_target_pairs={{0,8},{4,12},{8,0},{12,4},{1,9},{5,13},{9,1},{13,5},{2,10},{6,14},... | collective-permute-start | bytes 49160 | tf_op jit(solution)/shard_map/ppermute | solution.py:500
  6.2 5.6 %collective-permute-start.2 = (bf16[64,128]{1,0:T(8,128)(2,1)S(1)}, bf16[64,128]{1,0:T(8,128)(2,1)S(1)}, u32[]{:S(2)}, u32[]{:S(2)}) collective-permute-start(bf16[64,128]{1,0:T(8,128)(2,1)S(1)} %get-tuple-element.34), channel_id=1, source_target_pairs={{4,8},{8,4},{5,9},{9,5},{6,10},{10,6},{7,11},{11,7},{20,24},{24,20... | collective-permute-start | bytes 49160 | tf_op jit(solution)/shard_map/ppermute | solution.py:500
  11.9 7.5 %collective-permute-start.3 = (bf16[1216,128]{1,0:T(8,128)(2,1)S(1)}, bf16[1216,128]{1,0:T(8,128)(2,1)S(1)}, u32[]{:S(2)}, u32[]{:S(2)}) collective-permute-start(bf16[1216,128]{1,0:T(8,128)(2,1)S(1)} %shard_map.228.after.l0), channel_id=1, source_target_pairs={{0,2},{1,3},{2,0},{3,1},{4,6},{5,7},{6,4},{7,5},{8,10},{9,11},{10,... | collective-permute-start | bytes 933896 | tf_op jit(solution)/shard_map/ppermute | solution.py:430
  12.6 7.4 %collective-permute-start.9 = (bf16[256,512]{1,0:T(8,128)(2,1)S(1)}, bf16[256,512]{1,0:T(8,128)(2,1)S(1)}, u32[]{:S(2)}, u32[]{:S(2)}) collective-permute-start(bf16[256,512]{1,0:T(8,128)(2,1)S(1)} %shard_map.231.across), channel_id=1, source_target_pairs={{0,16},{16,0},{1,17},{17,1},{2,18},{18,2},{3,19},{19,3},{4,20},{20... | collective-permute-start | bytes 786440 | tf_op jit(solution)/shard_map/ppermute | solution.py:439
  13.1 8.1 %collective-permute-start.6 = (bf16[384,512]{1,0:T(8,128)(2,1)S(1)}, bf16[384,512]{1,0:T(8,128)(2,1)S(1)}, u32[]{:S(2)}, u32[]{:S(2)}) collective-permute-start(bf16[384,512]{1,0:T(8,128)(2,1)S(1)} %copy-done.1), channel_id=1, source_target_pairs={{0,1},{1,0},{2,3},{3,2},{4,5},{5,4},{6,7},{7,6},{8,9},{9,8},{10,11... | collective-permute-start | bytes 1179656 | tf_op jit(solution)/shard_map/ppermute | solution.py:434
  13.1 6.3 %collective-permute-start.7 = (bf16[128,512]{1,0:T(8,128)(2,1)S(1)}, bf16[128,512]{1,0:T(8,128)(2,1)S(1)}, u32[]{:S(2)}, u32[]{:S(2)}) collective-permute-start(bf16[128,512]{1,0:T(8,128)(2,1)S(1)} %copy-done.6), channel_id=1, source_target_pairs={{0,1},{1,0},{2,3},{3,2},{4,5},{5,4},{6,7},{7,6},{8,9},{9,8},{10,11... | collective-permute-start | bytes 393224 | tf_op jit(solution)/shard_map/ppermute | solution.py:434
  13.7 7.1 %collective-permute-start.4 = (bf16[1216,128]{1,0:T(8,128)(2,1)S(1)}, bf16[1216,128]{1,0:T(8,128)(2,1)S(1)}, u32[]{:S(2)}, u32[]{:S(2)}) collective-permute-start(bf16[1216,128]{1,0:T(8,128)(2,1)S(1)} %shard_map.228.after.l0), channel_id=1, source_target_pairs={{0,1},{1,0},{2,3},{3,2},{4,5},{5,4},{6,7},{7,6},{8,9},{9,8},{10,11... | collective-permute-start | bytes 933896 | tf_op jit(solution)/shard_map/ppermute | solution.py:434
  19.4 3.2 %collective-permute-start.5 = (bf16[1216,128]{1,0:T(8,128)(2,1)S(1)}, bf16[1216,128]{1,0:T(8,128)(2,1)S(1)}, u32[]{:S(2)}, u32[]{:S(2)}) collective-permute-start(bf16[1216,128]{1,0:T(8,128)(2,1)S(1)} %get-tuple-element.37), channel_id=1, source_target_pairs={{0,1},{1,0},{2,3},{3,2},{4,5},{5,4},{6,7},{7,6},{8,9},{9,8},{10,11... | collective-permute-start | bytes 933896 | tf_op jit(solution)/shard_map/ppermute | solution.py:434
  19.5 3.1 %collective-permute-start.10 = (bf16[256,512]{1,0:T(8,128)(2,1)S(1)}, bf16[256,512]{1,0:T(8,128)(2,1)S(1)}, u32[]{:S(2)}, u32[]{:S(2)}) collective-permute-start(bf16[256,512]{1,0:T(8,128)(2,1)S(1)} %shard_map.231.across), channel_id=1, source_target_pairs={{0,1},{1,0},{2,3},{3,2},{4,5},{5,4},{6,7},{7,6},{8,9},{9,8},{10,11... | collective-permute-start | bytes 786440 | tf_op jit(solution)/shard_map/ppermute | solution.py:434
  20.0 2.6 %collective-permute-start.11 = (bf16[256,512]{1,0:T(8,128)(2,1)S(1)}, bf16[256,512]{1,0:T(8,128)(2,1)S(1)}, u32[]{:S(2)}, u32[]{:S(2)}) collective-permute-start(bf16[256,512]{1,0:T(8,128)(2,1)S(1)} %collective-permute-done.9.round_), channel_id=1, source_target_pairs={{0,1},{1,0},{2,3},{3,2},{4,5},{5,4},{6,7},{7,6},{8,9},{9,8},{10,11... | collective-permute-start | bytes 786440 | tf_op jit(solution)/shard_map/ppermute | solution.py:434
  20.7 16.4 %collective-permute-start.14 = (bf16[896,512]{1,0:T(8,128)(2,1)S(1)}, bf16[896,512]{1,0:T(8,128)(2,1)S(1)}, u32[]{:S(2)}, u32[]{:S(2)}) collective-permute-start(bf16[896,512]{1,0:T(8,128)(2,1)S(1)} %get-tuple-element.36.weights.w0), channel_id=1, source_target_pairs={{0,1},{1,0},{2,3},{3,2},{4,5},{5,4},{6,7},{7,6},{8,9},{9,8},{10,11... | collective-permute-start | bytes 2752520 | tf_op jit(solution)/shard_map/ppermute | solution.py:434
  21.2 9.7 %collective-permute-start.15 = (bf16[320,512]{1,0:T(8,128)(2,1)S(1)}, bf16[320,512]{1,0:T(8,128)(2,1)S(1)}, u32[]{:S(2)}, u32[]{:S(2)}) collective-permute-start(bf16[320,512]{1,0:T(8,128)(2,1)S(1)} %get-tuple-element.42), channel_id=1, source_target_pairs={{0,2},{1,3},{2,0},{3,1},{4,6},{5,7},{6,4},{7,5},{8,10},{9,11},{10,... | collective-permute-start | bytes 983048 | tf_op jit(solution)/shard_map/ppermute | solution.py:430
  22.6 16.2 %copy-start.2 = (bf16[256,512]{1,0:T(8,128)(2,1)S(1)}, bf16[256,512]{1,0:T(8,128)(2,1)}, u32[]{:S(2)}) copy-start(bf16[256,512]{1,0:T(8,128)(2,1)} %n_in.1) | copy-start | bytes 786436
  22.6 16.2 %copy-start.7 = (bf16[128,512]{1,0:T(8,128)(2,1)S(1)}, bf16[128,512]{1,0:T(8,128)(2,1)}, u32[]{:S(2)}) copy-start(bf16[128,512]{1,0:T(8,128)(2,1)} %n_out.3) | copy-start | bytes 393220
  22.6 16.2 %copy-start.9 = (f32[512]{0:T(512)S(1)}, f32[512]{0:T(512)}, u32[]{:S(2)}) copy-start(f32[512]{0:T(512)} %param.45) | copy-start | bytes 6148
  22.6 16.2 %copy-start.10 = (s32[1,4,32]{2,1,0:T(4,128)S(1)}, s32[1,4,32]{2,1,0:T(4,128)}, u32[]{:S(2)}) copy-start(s32[1,4,32]{2,1,0:T(4,128)} %send.3) | copy-start | bytes 1540
  27.4 1.6 %collective-permute-start.12 = (bf16[256,512]{1,0:T(8,128)(2,1)S(1)}, bf16[256,512]{1,0:T(8,128)(2,1)S(1)}, u32[]{:S(2)}, u32[]{:S(2)}) collective-permute-start(bf16[256,512]{1,0:T(8,128)(2,1)S(1)} %get-tuple-element.41), channel_id=1, source_target_pairs={{0,1},{1,0},{2,3},{3,2},{4,5},{5,4},{6,7},{7,6},{8,9},{9,8},{10,11... | collective-permute-start | bytes 786440 | tf_op jit(solution)/shard_map/ppermute | solution.py:434
  30.9 6.1 %collective-permute-start.16 = (bf16[192,512]{1,0:T(8,128)(2,1)S(1)}, bf16[192,512]{1,0:T(8,128)(2,1)S(1)}, u32[]{:S(2)}, u32[]{:S(2)}) collective-permute-start(bf16[192,512]{1,0:T(8,128)(2,1)S(1)} %get-tuple-element.43.w2), channel_id=1, source_target_pairs={{0,4},{4,0},{8,12},{12,8},{1,5},{5,1},{9,13},{13,9},{2,6},{6,2},{1... | collective-permute-start | bytes 589832 | tf_op jit(solution)/shard_map/ppermute | solution.py:443
  31.6 7.2 %collective-permute-start.13 = (bf16[256,512]{1,0:T(8,128)(2,1)S(1)}, bf16[256,512]{1,0:T(8,128)(2,1)S(1)}, u32[]{:S(2)}, u32[]{:S(2)}) collective-permute-start(bf16[256,512]{1,0:T(8,128)(2,1)S(1)} %shard_map.233.after.mine), channel_id=1, source_target_pairs={{0,2},{1,3},{2,0},{3,1},{4,6},{5,7},{6,4},{7,5},{8,10},{9,11},{10,... | collective-permute-start | bytes 786440 | tf_op jit(solution)/shard_map/ppermute | solution.py:430
  33.1 7.0 %collective-permute-start.20 = (bf16[256,512]{1,0:T(8,128)(2,1)S(1)}, bf16[256,512]{1,0:T(8,128)(2,1)S(1)}, u32[]{:S(2)}, u32[]{:S(2)}) collective-permute-start(bf16[256,512]{1,0:T(8,128)(2,1)S(1)} %get-tuple-element.46.first), channel_id=1, source_target_pairs={{0,16},{16,0},{1,17},{17,1},{2,18},{18,2},{3,19},{19,3},{4,20},{20... | collective-permute-start | bytes 786440 | tf_op jit(solution)/shard_map/ppermute | solution.py:439
  33.6 3.4 %collective-permute-start.17 = (bf16[192,512]{1,0:T(8,128)(2,1)S(1)}, bf16[192,512]{1,0:T(8,128)(2,1)S(1)}, u32[]{:S(2)}, u32[]{:S(2)}) collective-permute-start(bf16[192,512]{1,0:T(8,128)(2,1)S(1)} %get-tuple-element.43.w2), channel_id=1, source_target_pairs={{0,1},{1,0},{2,3},{3,2},{4,5},{5,4},{6,7},{7,6},{8,9},{9,8},{10,11... | collective-permute-start | bytes 589832 | tf_op jit(solution)/shard_map/ppermute | solution.py:434
  37.1 1.8 %collective-permute-start.18 = (bf16[192,512]{1,0:T(8,128)(2,1)S(1)}, bf16[192,512]{1,0:T(8,128)(2,1)S(1)}, u32[]{:S(2)}, u32[]{:S(2)}) collective-permute-start(bf16[192,512]{1,0:T(8,128)(2,1)S(1)} %collective-permute-done.16.w3), channel_id=1, source_target_pairs={{0,1},{1,0},{2,3},{3,2},{4,5},{5,4},{6,7},{7,6},{8,9},{9,8},{10,11... | collective-permute-start | bytes 589832 | tf_op jit(solution)/shard_map/ppermute | solution.py:434
  38.9 12.0 %copy-start.16 = (s32[2,2048]{1,0:T(2,128)S(1)}, s32[2,2048]{1,0:T(2,128)}, u32[]{:S(2)}) copy-start(s32[2,2048]{1,0:T(2,128)} %edges.5) | copy-start | bytes 49156
  40.2 10.6 %collective-permute-start.21 = (bf16[512,512]{1,0:T(8,128)(2,1)S(1)}, bf16[512,512]{1,0:T(8,128)(2,1)S(1)}, u32[]{:S(2)}, u32[]{:S(2)}) collective-permute-start(bf16[512,512]{1,0:T(8,128)(2,1)S(1)} %shard_map.236.pair), channel_id=1, source_target_pairs={{0,1},{1,0},{2,3},{3,2},{4,5},{5,4},{6,7},{7,6},{8,9},{9,8},{10,11... | collective-permute-start | bytes 1572872 | tf_op jit(solution)/shard_map/ppermute | solution.py:434
  40.2 10.6 %collective-permute-start.19 = (bf16[256,512]{1,0:T(8,128)(2,1)S(1)}, bf16[256,512]{1,0:T(8,128)(2,1)S(1)}, u32[]{:S(2)}, u32[]{:S(2)}) collective-permute-start(bf16[256,512]{1,0:T(8,128)(2,1)S(1)} %get-tuple-element.44.after.mine.middle), channel_id=1, source_target_pairs={{0,1},{1,0},{2,3},{3,2},{4,5},{5,4},{6,7},{7,6},{8,9},{9,8},{10,11... | collective-permute-start | bytes 786440 | tf_op jit(solution)/shard_map/ppermute | solution.py:434
  40.7 6.9 %collective-permute-start.22 = (bf16[32,512]{1,0:T(8,128)(2,1)S(1)}, bf16[32,512]{1,0:T(8,128)(2,1)S(1)}, u32[]{:S(2)}, u32[]{:S(2)}) collective-permute-start(bf16[32,512]{1,0:T(8,128)(2,1)S(1)} %get-tuple-element.51), channel_id=1, source_target_pairs={{0,4},{4,0},{8,12},{12,8},{1,5},{5,1},{9,13},{13,9},{2,6},{6,2},{1... | collective-permute-start | bytes 98312 | tf_op jit(solution)/shard_map/ppermute | solution.py:570
  42.1 7.1 %collective-permute-start.23 = (bf16[32,512]{1,0:T(8,128)(2,1)S(1)}, bf16[32,512]{1,0:T(8,128)(2,1)S(1)}, u32[]{:S(2)}, u32[]{:S(2)}) collective-permute-start(bf16[32,512]{1,0:T(8,128)(2,1)S(1)} %get-tuple-element.52), channel_id=1, source_target_pairs={{0,8},{4,12},{8,0},{12,4},{1,9},{5,13},{9,1},{13,5},{2,10},{6,14},... | collective-permute-start | bytes 98312 | tf_op jit(solution)/shard_map/ppermute | solution.py:570
  44.9 5.8 %collective-permute-start.24 = (bf16[32,512]{1,0:T(8,128)(2,1)S(1)}, bf16[32,512]{1,0:T(8,128)(2,1)S(1)}, u32[]{:S(2)}, u32[]{:S(2)}) collective-permute-start(bf16[32,512]{1,0:T(8,128)(2,1)S(1)} %get-tuple-element.53), channel_id=1, source_target_pairs={{4,8},{8,4},{5,9},{9,5},{6,10},{10,6},{7,11},{11,7},{20,24},{24,20... | collective-permute-start | bytes 98312 | tf_op jit(solution)/shard_map/ppermute | solution.py:570
  47.7 12.1 %collective-permute-start.29 = (bf16[384,512]{1,0:T(8,128)(2,1)S(1)}, bf16[384,512]{1,0:T(8,128)(2,1)S(1)}, u32[]{:S(2)}, u32[]{:S(2)}) collective-permute-start(bf16[384,512]{1,0:T(8,128)(2,1)S(1)} %get-tuple-element.58.w0), channel_id=1, source_target_pairs={{0,2},{1,3},{2,0},{3,1},{4,6},{5,7},{6,4},{7,5},{8,10},{9,11},{10,... | collective-permute-start | bytes 1179656 | tf_op jit(solution)/shard_map/ppermute | solution.py:430
  50.7 2.7 %collective-permute-start.25 = (bf16[96,512]{1,0:T(8,128)(2,1)S(1)}, bf16[96,512]{1,0:T(8,128)(2,1)S(1)}, u32[]{:S(2)}, u32[]{:S(2)}) collective-permute-start(bf16[96,512]{1,0:T(8,128)(2,1)S(1)} %shard_map.238.halo), channel_id=1, source_target_pairs={{0,1},{1,0},{2,3},{3,2},{4,5},{5,4},{6,7},{7,6},{8,9},{9,8},{10,11... | collective-permute-start | bytes 294920 | tf_op jit(solution)/shard_map/ppermute | solution.py:434
  50.8 2.6 %copy-start.21 = (f32[512]{0:T(512)S(1)}, f32[512]{0:T(512)}, u32[]{:S(2)}) copy-start(f32[512]{0:T(512)} %param.46) | copy-start | bytes 6148
  53.5 13.3 %copy-start.11 = (f32[512]{0:T(512)S(1)}, f32[512]{0:T(512)}, u32[]{:S(2)}) copy-start(f32[512]{0:T(512)} %param.47) | copy-start | bytes 6148
  59.2 1.7 %collective-permute-start.26 = (bf16[256,512]{1,0:T(8,128)(2,1)S(1)}, bf16[256,512]{1,0:T(8,128)(2,1)S(1)}, u32[]{:S(2)}, u32[]{:S(2)}) collective-permute-start(bf16[256,512]{1,0:T(8,128)(2,1)S(1)} %get-tuple-element.55), channel_id=1, source_target_pairs={{0,1},{1,0},{2,3},{3,2},{4,5},{5,4},{6,7},{7,6},{8,9},{9,8},{10,11... | collective-permute-start | bytes 786440 | tf_op jit(solution)/shard_map/ppermute | solution.py:434
  59.7 2.8 %collective-permute-start.28 = (bf16[384,512]{1,0:T(8,128)(2,1)S(1)}, bf16[384,512]{1,0:T(8,128)(2,1)S(1)}, u32[]{:S(2)}, u32[]{:S(2)}) collective-permute-start(bf16[384,512]{1,0:T(8,128)(2,1)S(1)} %get-tuple-element.58.w0), channel_id=1, source_target_pairs={{0,1},{1,0},{2,3},{3,2},{4,5},{5,4},{6,7},{7,6},{8,9},{9,8},{10,11... | collective-permute-start | bytes 1179656 | tf_op jit(solution)/shard_map/ppermute | solution.py:434
  59.8 2.7 %collective-permute-start.30 = (bf16[384,512]{1,0:T(8,128)(2,1)S(1)}, bf16[384,512]{1,0:T(8,128)(2,1)S(1)}, u32[]{:S(2)}, u32[]{:S(2)}) collective-permute-start(bf16[384,512]{1,0:T(8,128)(2,1)S(1)} %collective-permute-done.29.w2), channel_id=1, source_target_pairs={{0,1},{1,0},{2,3},{3,2},{4,5},{5,4},{6,7},{7,6},{8,9},{9,8},{10,11... | collective-permute-start | bytes 1179656 | tf_op jit(solution)/shard_map/ppermute | solution.py:434
  60.9 5.8 %collective-permute-start.27 = (bf16[128,512]{1,0:T(8,128)(2,1)S(1)}, bf16[128,512]{1,0:T(8,128)(2,1)S(1)}, u32[]{:S(2)}, u32[]{:S(2)}) collective-permute-start(bf16[128,512]{1,0:T(8,128)(2,1)S(1)} %get-tuple-element.57), channel_id=1, source_target_pairs={{0,2},{1,3},{2,0},{3,1},{4,6},{5,7},{6,4},{7,5},{8,10},{9,11},{10,... | collective-permute-start | bytes 393224 | tf_op jit(solution)/shard_map/ppermute | solution.py:430

commit v13 on v12

--- a/solution.py
+++ b/solution.py
@@ -151,20 +151,21 @@
     pick_lists(plan, grid[...], send, outs)
 
 
-def embed_kernel(e_in, e_out, p_in, p_out, egeom, egeo, pgeom, pgeo, after, weights, eout, pout):
-    stack_into(weights, (e_in, e_out, p_in, p_out))
+def embed_kernel(e_in, e_out, p_in, p_out, egeom, egeo, pgeom, pgeo, after, node, proc, eout, pout):
+    stack_into(node, (e_in, e_out))
+    stack_into(proc, (p_in, p_out))
     for geom, geo, out in ((egeom, egeo, eout), (pgeom, pgeo, pout)):
         for begin in range(0, out.shape[0], STEP):
             out[begin : begin + STEP, :] = embed_rows(geom[:, begin : begin + STEP], geo[...])
 
 
-def cross_kernel(parts, weights, lat, crossing, lat_out):
+def cross_kernel(counts, node, proc, lat, crossing, lat_out):
     lat_out[...] = lat[...]
     place = 0
-    for first, rows, axes in parts:
+    for stack, rows, axes in ((node, counts[0], BY_PART), (proc, counts[1], BY_GROUP)):
         half = rows // 2
-        begin = pl.multiple_of(first + parity(axes) * half, 64)
-        crossing[place : place + half, :] = weights[pl.ds(begin, half), :]
+        begin = pl.multiple_of(parity(axes) * half, 64)
+        crossing[place : place + half, :] = stack[pl.ds(begin, half), :]
         place += half
 
 
@@ -331,7 +332,7 @@
 
 
 def node_kernel(
-    plan, k_in, k_out, mesh, mine, theirs, gain, n_in, n_out, w0, w1, w2, w3, w4, w5, send, out, packed, *rest
+    plan, k_in, k_out, mesh, mine, theirs, gain, n_in, n_out, w0, w1, w2, w3, w4, w5, send, after, out, packed, *rest
 ):
     outs, stack = rest[:-1], rest[-1]
     put_shard(stack, w0, 0, 0)
@@ -352,7 +353,7 @@
 
 
 def proc_first_kernel(
-    k_in, first_row, emb, mine, theirs, edges, w0, w1, pair, pair_beside,
+    k_in, emb, mine, theirs, edges, w0, w1, pair, pair_beside,
     table, pre, w_source, w_out, stack, full,
 ):
     d = full.shape[1]
@@ -363,8 +364,8 @@
         for part, which in ((mine, core), (theirs, 1 - core)):
             place = pl.multiple_of((2 * half + which) * rows, rows)
             full[pl.ds(place, rows), :] = part[half * rows : (half + 1) * rows, :]
-    put_shard(stack, w0, first_row, 0)
-    put_shard(stack, w1, first_row, 1)
+    put_shard(stack, w0, 0, 0)
+    put_shard(stack, w1, 0, 1)
     rows = pair.shape[0] // 2
     for other in range(2):
         put_half(stack, k_in, pair.at[pl.ds(other * rows, rows), :], 2, other)
@@ -416,14 +417,25 @@
         out[...] = add(mine[pl.ds(place, rows), :], theirs[pl.ds(place, rows), :])
 
 
-def out_kernel(k_in, k_out, middle, mine, theirs, gain, w0, w1, w2, w3, out, stack):
-    rows = mine.shape[0]
-    chip = lax.div(lax.axis_index("sub"), 2)
+def out_kernel(k_in, k_out, middle, mine, theirs, gain, w0, w1, w2, w3, out, stacked, hidden):
+    rows, d = out.shape
+    quarter = lax.axis_index("sub")
+    chip = lax.div(quarter, 2)
     mesh = middle[pl.ds(pl.multiple_of(chip * rows, rows), rows), :]
-    for shard, bit in zip((w0, w1, w2, w3), (0, 1, 2, 3)):
-        put_shard(stack, shard, 0, bit)
-    w_in, w_out = joined(stack, 0, k_in), joined(stack, k_in, k_out)
-    out[...] = node_update(mesh, add(mine[...], theirs[...]), w_in, w_out, gain[...])
+    stacked[:, :d] = mesh
+    stacked[:, d:] = add(mine[...], theirs[...])
+    shards = (w0, w1, w2, w3)
+
+    def columns_of(ref, step, count):
+        return ref[:, pl.ds(pl.multiple_of(lax.bitwise_xor(quarter, step) * count, count), count)]
+
+    left = jnp.concatenate([columns_of(stacked, step, k_in) for step in range(4)], axis=1)
+    right = jnp.concatenate([w[:k_in, :] for w in shards], axis=0)
+    hidden[...] = silu(dot(left, right)).astype(BF16)
+    left = jnp.concatenate([columns_of(hidden, step, k_out) for step in range(4)], axis=1)
+    right = jnp.concatenate([w[k_in:, :] for w in shards], axis=0)
+    update = layer_norm(dot(left, right)) * gain[...]
+    out[...] = (mesh.astype(F32) + update).astype(BF16)
 
 
 def to_chip(v):
@@ -508,9 +520,9 @@
     lat_beside = to_core(lat)
     edge_beside = [to_core(enc_edge_in), to_core(enc_edge_out)]
     edge_round = to_group(edge_across)
-    next_w, enc_emb, proc_emb = call(
+    node_w, proc_w, enc_emb, proc_emb = call(
         embed_kernel,
-        [shape(n_in + n_out + k_in + k_out, d), shape(n_enc, d), shape(n_proc, d)],
+        [shape(n_in + n_out, d), shape(k_in + k_out, d), shape(n_enc, d), shape(n_proc, d)],
         [
             enc_node_in, enc_node_out, proc_edge_in, proc_edge_out,
             enc_geom, enc_geo, proc_geom, proc_geo, lat,
@@ -518,13 +530,13 @@
         flops=2 * (n_enc + n_proc) * d * 128,
     )
     crossing, lat_sent = call(
-        functools.partial(cross_kernel, ((0, n_in, BY_PART), (n_in + n_out, k_in, BY_GROUP))),
+        functools.partial(cross_kernel, (n_in, k_in)),
         [shape((n_in + k_in) // 2, d), shape(lat.shape[0], width)],
-        [next_w, lat_across],
+        [node_w, proc_w, lat_across],
     )
     lat_both = to_core(lat_sent)
     next_across = to_chip(crossing)
-    next_beside = to_core(next_w)
+    node_beside, proc_beside = to_core(node_w), to_core(proc_w)
 
     halo_rows = padded(got)
     half = mesh_rows // 2
@@ -561,7 +573,7 @@
         [shape(half, d), shape(n_in + n_out, d)] + [shape(slots, d)] * len(plan),
         [
             own_mesh, chip_sum, to_chip(chip_sum), enc_node_gain, proc_node_in, proc_node_out,
-            next_w, next_beside, node_across, node_round, node_both, to_core(node_round), mesh_send,
+            node_w, node_beside, node_across, node_round, node_both, to_core(node_round), mesh_send, proc_beside,
         ],
         scratch=[pltpu.VMEM((4 * (n_in + n_out), d), BF16)],
         flops=2 * half * d * 3 * d,
@@ -573,10 +585,10 @@
     last_across, last_beside = to_chip(last_w), to_core(last_w)
     early = n_proc // 2
     table, pre, w_source, w_out = call(
-        functools.partial(proc_first_kernel, k_in, n_in + n_out),
+        functools.partial(proc_first_kernel, k_in),
         [shape(d + 2 * mesh_rows, d), shape(early, d, F32), shape(d, d), shape(d, d)],
         [
-            proc_emb, mid_half, to_core(mid_half), proc_edges, next_w, next_beside, proc_pair, to_core(proc_pair),
+            proc_emb, mid_half, to_core(mid_half), proc_edges, proc_w, proc_beside, proc_pair, to_core(proc_pair),
         ],
         scratch=[pltpu.VMEM((4 * (k_in + k_out), d), BF16), pltpu.VMEM((mesh_rows, d), BF16)],
         flops=2 * early * d * (d + 2 * mesh_rows),
@@ -600,7 +612,7 @@
         functools.partial(out_kernel, n_in, n_out),
         [shape(quarter, d)],
         [mid_half, mine, to_chip(other), proc_node_gain, last_w, last_beside, last_across, to_core(last_across)],
-        scratch=[pltpu.VMEM((4 * (n_in + n_out), d), BF16)],
+        scratch=[pltpu.VMEM((quarter, 4 * n_in), BF16), pltpu.VMEM((quarter, 4 * n_out), BF16)],
         flops=2 * quarter * d * 3 * d,
     )
     return result

time: 68.4 us -> 68.6 us (level)
    ppermute x16 -> x17, waiting for transfers between devices: 2.21 us -> 1.55 us  [to_core(): return lax.ppermute(v, 'sub', [(i, i ^ 1) for i in range(4)])]
    ppermute x16 -> x17, starting transfers between devices: 3.43 us -> 3.6 us  [to_core(): return lax.ppermute(v, 'sub', [(i, i ^ 1) for i in range(4)])]
  transfers between devices with their start and end apart: 31 -> 32, of which waited for: 10 -> 10; matrix products, arithmetic and copies ran while one was open for 0% -> 0% of each run, Pallas kernels for 24% -> 24%
where the time goes in v13:
time: 68.6 us; the launch traced here: 68.5 us
  starting transfers between devices  25.2 us (37%)
  waiting for transfers between devices  22.3 us (33%)
  Pallas kernels  17.9 us (26%)
  between operations  1.75 us (3%)
  local copies, waits for them, and re-layouts  1.28 us (2%)
    pallas_call x16, Pallas kernels, call(): pl.pallas_call(body, out_shape=tuple(outs), in_specs=specs, out_specs=tup...  17.9 us
    ppermute x6, waiting for transfers between devices, to_chip(): return lax.ppermute(v, 'sub', [(i, i ^ 2) for i in range(4)])  12.2 us
    ppermute x6, starting transfers between devices, local(): lax.ppermute(v, 'dom', entry[0])  11.6 us
    ppermute x6, starting transfers between devices, to_chip(): return lax.ppermute(v, 'sub', [(i, i ^ 2) for i in range(4)])  8.21 us
    ppermute x6, waiting for transfers between devices, local(): lax.ppermute(v, 'dom', entry[0])  4.74 us
    ppermute x1, waiting for transfers between devices, to_partition(): lax.ppermute(v, 'dom', [(i, i ^ 1) for i in range(lax.axis_size('dom'))])  3.83 us
    ppermute x17, starting transfers between devices, to_core(): return lax.ppermute(v, 'sub', [(i, i ^ 1) for i in range(4)])  3.6 us
    ppermute x17, waiting for transfers between devices, to_core(): return lax.ppermute(v, 'sub', [(i, i ^ 1) for i in range(4)])  1.55 us
  transfers between devices with their start and end apart: 32, of which 10 were waited for; matrix products, arithmetic and copies ran while one was open for 0% of the time, Pallas kernels for 24%

profile of v13, /device:TPU:12, one launch (start us, length us, event | category | flops | bytes accessed | tf_op | source)
XLA Modules:
  0.0 68.5 jit_solution(6264124229656865615)
XLA Ops:
  0.1 0.8 %copy-done.4 = bf16[128,512]{1,0:T(8,128)(2,1)S(1)} copy-done((bf16[128,512]{1,0:T(8,128)(2,1)S(1)}, bf16[128,512]{1,0:T(8,128)(2,1)}, u32[]{:S(2)}) %copy-start.4) | copy-done | bytes 131096
  0.9 0.1 copy-done.5
  1.0 0.1 copy-done
  1.0 0.2 copy-done.1
  1.2 0.0 copy-done.6
  1.3 0.0 copy-start.17
  1.3 0.0 copy-start.18
  1.3 0.3 shard_map.227
  1.6 0.0 copy-start.19
  1.6 0.0 copy-start.20
  1.6 1.6 %collective-permute-start.8 = (bf16[384,512]{1,0:T(8,128)(2,1)S(1)}, bf16[384,512]{1,0:T(8,128)(2,1)S(1)}, u32[]{:S(2)}, u32[]{:S(2)}) collective-permute-start(bf16[384,512]{1,0:T(8,128)(2,1)S(1)} %get-tuple-element.40), channel_id=1, source_target_pairs={{0,2},{1,3},{2,0},{3,1},{4,6},{5,7},{6,4},{7,5},{8,10},{9,11},{10,... | collective-permute-start | bytes 1179656 | tf_op jit(solution)/shard_map/ppermute | solution.py:442
  3.2 0.5 collective-permute-start
  3.6 2.6 %collective-permute-start.1 = (bf16[64,128]{1,0:T(8,128)(2,1)S(1)}, bf16[64,128]{1,0:T(8,128)(2,1)S(1)}, u32[]{:S(2)}, u32[]{:S(2)}) collective-permute-start(bf16[64,128]{1,0:T(8,128)(2,1)S(1)} %get-tuple-element.34), channel_id=1, source_target_pairs={{0,8},{4,12},{8,0},{12,4},{1,9},{5,13},{9,1},{13,5},{2,10},{6,14},... | collective-permute-start | bytes 49160 | tf_op jit(solution)/shard_map/ppermute | solution.py:512
  6.2 2.3 %collective-permute-start.2 = (bf16[64,128]{1,0:T(8,128)(2,1)S(1)}, bf16[64,128]{1,0:T(8,128)(2,1)S(1)}, u32[]{:S(2)}, u32[]{:S(2)}) collective-permute-start(bf16[64,128]{1,0:T(8,128)(2,1)S(1)} %get-tuple-element.35), channel_id=1, source_target_pairs={{4,8},{8,4},{5,9},{9,5},{6,10},{10,6},{7,11},{11,7},{20,24},{24,20... | collective-permute-start | bytes 49160 | tf_op jit(solution)/shard_map/ppermute | solution.py:512
  8.6 3.2 %collective-permute-done.2.refs_4_ = bf16[64,128]{1,0:T(8,128)(2,1)S(1)} collective-permute-done((bf16[64,128]{1,0:T(8,128)(2,1)S(1)}, bf16[64,128]{1,0:T(8,128)(2,1)S(1)}, u32[]{:S(2)}, u32[]{:S(2)}) %collective-permute-start.2) | collective-permute-done | bytes 16416 | tf_op jit(solution)/shard_map/ppermute | solution.py:512
  11.9 0.6 collective-permute-start.3
  12.5 0.1 collective-permute-done.8.source.early
  12.6 0.6 collective-permute-start.9
  13.1 0.0 collective-permute-start.6
  13.1 0.5 collective-permute-start.7
  13.7 1.8 %shard_map.229 = (bf16[384,512]{1,0:T(8,128)(2,1)S(1)}, bf16[512,512]{1,0:T(8,128)(2,1)S(1)}, bf16[1024,512]{1,0:T(8,128)(2,1)S(1)}, bf16[2048,512]{1,0:T(8,128)(2,1)S(1)}) custom-call(bf16[256,512]{1,0:T(8,128)(2,1)S(1)} %copy-done.13, bf16[128,512]{1,0:T(8,128)(2,1)S(1)} %copy-done.4, bf16[384,512]{1,0:T(8,128)(2,1)S(1)} %copy-done.12, ...), custom_call_target="tpu_custom_call" | custom-call | flops 402653184 | bytes 5357568 | tf_op jit(solution)/shard_map/pallas_call | solution.py:71
  15.5 3.9 %collective-permute-done.3.lat.l1 = bf16[1216,128]{1,0:T(8,128)(2,1)S(1)} collective-permute-done((bf16[1216,128]{1,0:T(8,128)(2,1)S(1)}, bf16[1216,128]{1,0:T(8,128)(2,1)S(1)}, u32[]{:S(2)}, u32[]{:S(2)}) %collective-permute-start.3) | collective-permute-done | bytes 311328 | tf_op jit(solution)/shard_map/ppermute | solution.py:442
  19.4 0.1 collective-permute-start.5
  19.5 0.5 collective-permute-start.10
  20.0 0.1 collective-permute-start.11
  20.7 1.4 %collective-permute-start.15 = (bf16[320,512]{1,0:T(8,128)(2,1)S(1)}, bf16[320,512]{1,0:T(8,128)(2,1)S(1)}, u32[]{:S(2)}, u32[]{:S(2)}) collective-permute-start(bf16[320,512]{1,0:T(8,128)(2,1)S(1)} %get-tuple-element.44), channel_id=1, source_target_pairs={{0,2},{1,3},{2,0},{3,1},{4,6},{5,7},{6,4},{7,5},{8,10},{9,11},{10,... | collective-permute-start | bytes 983048 | tf_op jit(solution)/shard_map/ppermute | solution.py:442
  22.2 0.0 copy-start.2
  22.2 0.0 copy-start.7
  22.2 0.0 copy-start.9
  22.2 0.0 copy-start.10
  22.2 4.7 %shard_map.232 = (bf16[256,512]{1,0:T(8,128)(2,1)S(1)}, bf16[256,512]{1,0:T(8,128)(2,1)S(1)}, bf16[256,512]{1,0:T(8,128)(2,1)S(1)}) custom-call(bf16[1024,512]{1,0:T(8,128)(2,1)S(1)} %get-tuple-element.36.emb, s32[2,1024]{1,0:T(2,128)S(1)} %copy-done.19, f32[1,512]{1,0:T(1,128)S(1)} %bitcast.6, bf16[1216,128]{1,0:T(8,128)(2,1)S(1)} %shard_map.228.after.l0, ...), custom_call_target="tpu_custom_call" | custom-call | flops 2952790016 | bytes 5187588 | tf_op jit(solution)/shard_map/pallas_call | solution.py:71
  27.0 0.2 collective-permute-start.12
  27.2 0.3 collective-permute-start.14
  27.6 0.2 collective-permute-start.19
  27.7 0.9 %collective-permute-done.12.theirs = bf16[256,512]{1,0:T(8,128)(2,1)S(1)} collective-permute-done((bf16[256,512]{1,0:T(8,128)(2,1)S(1)}, bf16[256,512]{1,0:T(8,128)(2,1)S(1)}, u32[]{:S(2)}, u32[]{:S(2)}) %collective-permute-start.12) | collective-permute-done | bytes 262176 | tf_op jit(solution)/shard_map/ppermute | solution.py:446
  28.6 0.1 shard_map.233.after.mine
  28.6 2.2 %collective-permute-done.15.source = bf16[320,512]{1,0:T(8,128)(2,1)S(1)} collective-permute-done((bf16[320,512]{1,0:T(8,128)(2,1)S(1)}, bf16[320,512]{1,0:T(8,128)(2,1)S(1)}, u32[]{:S(2)}, u32[]{:S(2)}) %collective-permute-start.15) | collective-permute-done | bytes 327712 | tf_op jit(solution)/shard_map/ppermute | solution.py:442
  30.9 0.7 collective-permute-start.16
  31.6 1.5 %collective-permute-start.13 = (bf16[256,512]{1,0:T(8,128)(2,1)S(1)}, bf16[256,512]{1,0:T(8,128)(2,1)S(1)}, u32[]{:S(2)}, u32[]{:S(2)}) collective-permute-start(bf16[256,512]{1,0:T(8,128)(2,1)S(1)} %shard_map.233.after.mine), channel_id=1, source_target_pairs={{0,2},{1,3},{2,0},{3,1},{4,6},{5,7},{6,4},{7,5},{8,10},{9,11},{10,... | collective-permute-start | bytes 786440 | tf_op jit(solution)/shard_map/ppermute | solution.py:442
  33.1 0.5 collective-permute-start.21
  33.6 3.8 %collective-permute-done.16.w3 = bf16[192,512]{1,0:T(8,128)(2,1)S(1)} collective-permute-done((bf16[192,512]{1,0:T(8,128)(2,1)S(1)}, bf16[192,512]{1,0:T(8,128)(2,1)S(1)}, u32[]{:S(2)}, u32[]{:S(2)}) %collective-permute-start.16) | collective-permute-done | bytes 196640 | tf_op jit(solution)/shard_map/ppermute | solution.py:455
  37.4 1.8 %collective-permute-done.13.theirs = bf16[256,512]{1,0:T(8,128)(2,1)S(1)} collective-permute-done((bf16[256,512]{1,0:T(8,128)(2,1)S(1)}, bf16[256,512]{1,0:T(8,128)(2,1)S(1)}, u32[]{:S(2)}, u32[]{:S(2)}) %collective-permute-start.13) | collective-permute-done | bytes 262176 | tf_op jit(solution)/shard_map/ppermute | solution.py:442
  39.2 0.0 copy-start.16
  39.3 1.2 %shard_map.235 = (bf16[256,512]{1,0:T(8,128)(2,1)S(1)}, bf16[384,512]{1,0:T(8,128)(2,1)S(1)}, bf16[32,512]{1,0:T(8,128)(2,1)S(1)}, bf16[32,512]{1,0:T(8,128)(2,1)S(1)}, bf16[32,512]{1,0:T(8,128)(2,1)S(1)}) custom-call(bf16[256,512]{1,0:T(8,128)(2,1)S(1)} %get-tuple-element.41.mesh, bf16[256,512]{1,0:T(8,128)(2,1)S(1)} %shard_map.233.after.mine, ...), custom_call_target="tpu_custom_call" | custom-call | flops 402653184 | bytes 4033024 | tf_op jit(solution)/shard_map/pallas_call | solution.py:71
  40.6 0.1 collective-permute-start.22
  40.6 0.5 collective-permute-start.20
  41.1 1.3 %collective-permute-start.23 = (bf16[32,512]{1,0:T(8,128)(2,1)S(1)}, bf16[32,512]{1,0:T(8,128)(2,1)S(1)}, u32[]{:S(2)}, u32[]{:S(2)}) collective-permute-start(bf16[32,512]{1,0:T(8,128)(2,1)S(1)} %get-tuple-element.53), channel_id=1, source_target_pairs={{0,4},{4,0},{8,12},{12,8},{1,5},{5,1},{9,13},{13,9},{2,6},{6,2},{1... | collective-permute-start | bytes 98312 | tf_op jit(solution)/shard_map/ppermute | solution.py:582
  42.5 2.8 %collective-permute-start.24 = (bf16[32,512]{1,0:T(8,128)(2,1)S(1)}, bf16[32,512]{1,0:T(8,128)(2,1)S(1)}, u32[]{:S(2)}, u32[]{:S(2)}) collective-permute-start(bf16[32,512]{1,0:T(8,128)(2,1)S(1)} %get-tuple-element.54), channel_id=1, source_target_pairs={{0,8},{4,12},{8,0},{12,4},{1,9},{5,13},{9,1},{13,5},{2,10},{6,14},... | collective-permute-start | bytes 98312 | tf_op jit(solution)/shard_map/ppermute | solution.py:582
  45.3 2.1 %collective-permute-start.25 = (bf16[32,512]{1,0:T(8,128)(2,1)S(1)}, bf16[32,512]{1,0:T(8,128)(2,1)S(1)}, u32[]{:S(2)}, u32[]{:S(2)}) collective-permute-start(bf16[32,512]{1,0:T(8,128)(2,1)S(1)} %get-tuple-element.55), channel_id=1, source_target_pairs={{4,8},{8,4},{5,9},{9,5},{6,10},{10,6},{7,11},{11,7},{20,24},{24,20... | collective-permute-start | bytes 98312 | tf_op jit(solution)/shard_map/ppermute | solution.py:582
  48.1 1.6 %collective-permute-start.30 = (bf16[384,512]{1,0:T(8,128)(2,1)S(1)}, bf16[384,512]{1,0:T(8,128)(2,1)S(1)}, u32[]{:S(2)}, u32[]{:S(2)}) collective-permute-start(bf16[384,512]{1,0:T(8,128)(2,1)S(1)} %get-tuple-element.60.w0), channel_id=1, source_target_pairs={{0,2},{1,3},{2,0},{3,1},{4,6},{5,7},{6,4},{7,5},{8,10},{9,11},{10,... | collective-permute-start | bytes 1179656 | tf_op jit(solution)/shard_map/ppermute | solution.py:442
  49.6 1.5 %collective-permute-done.25.refs_2_ = bf16[32,512]{1,0:T(8,128)(2,1)S(1)} collective-permute-done((bf16[32,512]{1,0:T(8,128)(2,1)S(1)}, bf16[32,512]{1,0:T(8,128)(2,1)S(1)}, u32[]{:S(2)}, u32[]{:S(2)}) %collective-permute-start.25) | collective-permute-done | bytes 32800 | tf_op jit(solution)/shard_map/ppermute | solution.py:582
  51.1 0.1 collective-permute-start.26
  51.2 0.0 copy-start.21
  51.2 2.6 %shard_map.237 = (bf16[1536,512]{1,0:T(8,128)(2,1)S(1)}, f32[1024,512]{1,0:T(8,128)S(1)}, bf16[512,512]{1,0:T(8,128)(2,1)S(1)}, bf16[512,512]{1,0:T(8,128)(2,1)S(1)}) custom-call(bf16[2048,512]{1,0:T(8,128)(2,1)S(1)} %get-tuple-element.47.emb, bf16[256,512]{1,0:T(8,128)(2,1)S(1)} %get-tuple-element.46.after.mine.middle, ...), custom_call_target="tpu_custom_call" | custom-call | flops 1610612736 | bytes 9453568 | tf_op jit(solution)/shard_map/pallas_call | solution.py:71
  53.9 0.0 copy-start.11
  53.9 5.6 %shard_map.239 = (bf16[256,512]{1,0:T(8,128)(2,1)S(1)}, bf16[256,512]{1,0:T(8,128)(2,1)S(1)}) custom-call(bf16[2048,512]{1,0:T(8,128)(2,1)S(1)} %get-tuple-element.47.emb, s32[2,2048]{1,0:T(2,128)S(1)} %copy-done.16, f32[1,512]{1,0:T(1,128)S(1)} %bitcast.7, bf16[1536,512]{1,0:T(8,128)(2,1)S(1)} %get-tuple-element.49.table, ...), custom_call_target="tpu_custom_call" | custom-call | flops 3489660928 | bytes 7555076 | tf_op jit(solution)/shard_map/pallas_call | solution.py:71
  59.5 0.6 collective-permute-start.27
  60.0 0.1 collective-permute-start.29
  60.1 0.4 collective-permute-start.31
  60.5 0.6 collective-permute-done.27.theirs
  61.2 0.1 shard_map.240
  61.2 1.6 %collective-permute-start.28 = (bf16[128,512]{1,0:T(8,128)(2,1)S(1)}, bf16[128,512]{1,0:T(8,128)(2,1)S(1)}, u32[]{:S(2)}, u32[]{:S(2)}) collective-permute-start(bf16[128,512]{1,0:T(8,128)(2,1)S(1)} %get-tuple-element.59), channel_id=1, source_target_pairs={{0,2},{1,3},{2,0},{3,1},{4,6},{5,7},{6,4},{7,5},{8,10},{9,11},{10,... | collective-permute-start | bytes 393224 | tf_op jit(solution)/shard_map/ppermute | solution.py:442
  62.8 4.3 %collective-permute-done.28.theirs = bf16[128,512]{1,0:T(8,128)(2,1)S(1)} collective-permute-done((bf16[128,512]{1,0:T(8,128)(2,1)S(1)}, bf16[128,512]{1,0:T(8,128)(2,1)S(1)}, u32[]{:S(2)}, u32[]{:S(2)}) %collective-permute-start.28) | collective-permute-done | bytes 131104 | tf_op jit(solution)/shard_map/ppermute | solution.py:442
  67.1 1.4 %shard_map.241 = bf16[128,512]{1,0:T(8,128)(2,1)} custom-call(bf16[256,512]{1,0:T(8,128)(2,1)S(1)} %get-tuple-element.46.after.mine.middle, bf16[128,512]{1,0:T(8,128)(2,1)S(1)} %get-tuple-element.58.mine, bf16[128,512]{1,0:T(8,128)(2,1)S(1)} %collective-permute-done.28.theirs, f32[1,512]{1,0:T(1,128)S(1)} %bitcast.5, ...), custom_call_target="tpu_custom_call" | custom-call | flops 201326592 | bytes 2230272 | tf_op jit(solution)/shard_map/pallas_call | solution.py:71
  (60 shorter events, 0.3 us)
Async XLA Ops:
  0.0 0.9 %copy-start.4 = (bf16[128,512]{1,0:T(8,128)(2,1)S(1)}, bf16[128,512]{1,0:T(8,128)(2,1)}, u32[]{:S(2)}) copy-start(bf16[128,512]{1,0:T(8,128)(2,1)} %e_out.1) | copy-start | bytes 393220
  0.0 1.0 %copy-start.5 = (bf16[128,512]{1,0:T(8,128)(2,1)S(1)}, bf16[128,512]{1,0:T(8,128)(2,1)}, u32[]{:S(2)}) copy-start(bf16[128,512]{1,0:T(8,128)(2,1)} %p_out.3) | copy-start | bytes 393220
  0.0 1.0 %copy-start = (bf16[512,128]{1,0:T(8,128)(2,1)S(1)}, bf16[512,128]{1,0:T(8,128)(2,1)}, u32[]{:S(2)}) copy-start(bf16[512,128]{1,0:T(8,128)(2,1)} %refs_0_.1) | copy-start | bytes 393220
  0.0 1.0 %copy-start.8 = (s32[1,4,64]{2,1,0:T(4,128)S(1)}, s32[1,4,64]{2,1,0:T(4,128)}, u32[]{:S(2)}) copy-start(s32[1,4,64]{2,1,0:T(4,128)} %send.2) | copy-start | bytes 3076
  0.0 1.2 %copy-start.1 = (bf16[384,512]{1,0:T(8,128)(2,1)S(1)}, bf16[384,512]{1,0:T(8,128)(2,1)}, u32[]{:S(2)}) copy-start(bf16[384,512]{1,0:T(8,128)(2,1)} %o_in.1) | copy-start | bytes 1179652
  0.0 1.2 %copy-start.6 = (bf16[128,512]{1,0:T(8,128)(2,1)S(1)}, bf16[128,512]{1,0:T(8,128)(2,1)}, u32[]{:S(2)}) copy-start(bf16[128,512]{1,0:T(8,128)(2,1)} %o_out.1) | copy-start | bytes 393220
  0.0 11.8 %copy-start.3 = (bf16[512,128]{1,0:T(8,128)(2,1)S(1)}, bf16[512,128]{1,0:T(8,128)(2,1)}, u32[]{:S(2)}) copy-start(bf16[512,128]{1,0:T(8,128)(2,1)} %refs_1_.1) | copy-start | bytes 393220
  1.2 12.4 %copy-start.12 = (bf16[384,512]{1,0:T(8,128)(2,1)S(1)}, bf16[384,512]{1,0:T(8,128)(2,1)}, u32[]{:S(2)}) copy-start(bf16[384,512]{1,0:T(8,128)(2,1)} %p_in.1) | copy-start | bytes 1179652
  1.2 12.4 %copy-start.13 = (bf16[256,512]{1,0:T(8,128)(2,1)S(1)}, bf16[256,512]{1,0:T(8,128)(2,1)}, u32[]{:S(2)}) copy-start(bf16[256,512]{1,0:T(8,128)(2,1)} %e_in.1) | copy-start | bytes 786436
  1.2 12.4 %copy-start.14 = (f32[4,2048]{1,0:T(4,128)S(1)}, f32[4,2048]{1,0:T(4,128)}, u32[]{:S(2)}) copy-start(f32[4,2048]{1,0:T(4,128)} %pgeom.1) | copy-start | bytes 98308
  1.2 12.4 %copy-start.15 = (f32[4,1024]{1,0:T(4,128)S(1)}, f32[4,1024]{1,0:T(4,128)}, u32[]{:S(2)}) copy-start(f32[4,1024]{1,0:T(4,128)} %egeom.1) | copy-start | bytes 49156
  1.3 12.4 %copy-start.17 = (f32[4,512]{1,0:T(4,128)S(1)}, f32[4,512]{1,0:T(4,128)}, u32[]{:S(2)}) copy-start(f32[4,512]{1,0:T(4,128)} %egeo.1) | copy-start | bytes 24580
  1.3 12.4 %copy-start.18 = (f32[4,512]{1,0:T(4,128)S(1)}, f32[4,512]{1,0:T(4,128)}, u32[]{:S(2)}) copy-start(f32[4,512]{1,0:T(4,128)} %pgeo.1) | copy-start | bytes 24580
  1.6 20.6 %copy-start.19 = (s32[2,1024]{1,0:T(2,128)S(1)}, s32[2,1024]{1,0:T(2,128)}, u32[]{:S(2)}) copy-start(s32[2,1024]{1,0:T(2,128)} %edges.3) | copy-start | bytes 24580
  1.6 20.6 %copy-start.20 = (f32[512]{0:T(512)S(1)}, f32[512]{0:T(512)}, u32[]{:S(2)}) copy-start(f32[512]{0:T(512)} %param.44) | copy-start | bytes 6148
  1.6 10.9 %collective-permute-start.8 = (bf16[384,512]{1,0:T(8,128)(2,1)S(1)}, bf16[384,512]{1,0:T(8,128)(2,1)S(1)}, u32[]{:S(2)}, u32[]{:S(2)}) collective-permute-start(bf16[384,512]{1,0:T(8,128)(2,1)S(1)} %get-tuple-element.40), channel_id=1, source_target_pairs={{0,2},{1,3},{2,0},{3,1},{4,6},{5,7},{6,4},{7,5},{8,10},{9,11},{10,... | collective-permute-start | bytes 1179656 | tf_op jit(solution)/shard_map/ppermute | solution.py:442
  3.2 5.4 %collective-permute-start = (bf16[64,128]{1,0:T(8,128)(2,1)S(1)}, bf16[64,128]{1,0:T(8,128)(2,1)S(1)}, u32[]{:S(2)}, u32[]{:S(2)}) collective-permute-start(bf16[64,128]{1,0:T(8,128)(2,1)S(1)} %get-tuple-element.33), channel_id=1, source_target_pairs={{0,4},{4,0},{8,12},{12,8},{1,5},{5,1},{9,13},{13,9},{2,6},{6,2},{1... | collective-permute-start | bytes 49160 | tf_op jit(solution)/shard_map/ppermute | solution.py:512
  3.6 5.0 %collective-permute-start.1 = (bf16[64,128]{1,0:T(8,128)(2,1)S(1)}, bf16[64,128]{1,0:T(8,128)(2,1)S(1)}, u32[]{:S(2)}, u32[]{:S(2)}) collective-permute-start(bf16[64,128]{1,0:T(8,128)(2,1)S(1)} %get-tuple-element.34), channel_id=1, source_target_pairs={{0,8},{4,12},{8,0},{12,4},{1,9},{5,13},{9,1},{13,5},{2,10},{6,14},... | collective-permute-start | bytes 49160 | tf_op jit(solution)/shard_map/ppermute | solution.py:512
  6.2 5.6 %collective-permute-start.2 = (bf16[64,128]{1,0:T(8,128)(2,1)S(1)}, bf16[64,128]{1,0:T(8,128)(2,1)S(1)}, u32[]{:S(2)}, u32[]{:S(2)}) collective-permute-start(bf16[64,128]{1,0:T(8,128)(2,1)S(1)} %get-tuple-element.35), channel_id=1, source_target_pairs={{4,8},{8,4},{5,9},{9,5},{6,10},{10,6},{7,11},{11,7},{20,24},{24,20... | collective-permute-start | bytes 49160 | tf_op jit(solution)/shard_map/ppermute | solution.py:512
  11.9 7.5 %collective-permute-start.3 = (bf16[1216,128]{1,0:T(8,128)(2,1)S(1)}, bf16[1216,128]{1,0:T(8,128)(2,1)S(1)}, u32[]{:S(2)}, u32[]{:S(2)}) collective-permute-start(bf16[1216,128]{1,0:T(8,128)(2,1)S(1)} %shard_map.228.after.l0), channel_id=1, source_target_pairs={{0,2},{1,3},{2,0},{3,1},{4,6},{5,7},{6,4},{7,5},{8,10},{9,11},{10,... | collective-permute-start | bytes 933896 | tf_op jit(solution)/shard_map/ppermute | solution.py:442
  12.6 7.4 %collective-permute-start.9 = (bf16[256,512]{1,0:T(8,128)(2,1)S(1)}, bf16[256,512]{1,0:T(8,128)(2,1)S(1)}, u32[]{:S(2)}, u32[]{:S(2)}) collective-permute-start(bf16[256,512]{1,0:T(8,128)(2,1)S(1)} %shard_map.231.across), channel_id=1, source_target_pairs={{0,16},{16,0},{1,17},{17,1},{2,18},{18,2},{3,19},{19,3},{4,20},{20... | collective-permute-start | bytes 786440 | tf_op jit(solution)/shard_map/ppermute | solution.py:451
  13.1 9.0 %collective-permute-start.6 = (bf16[384,512]{1,0:T(8,128)(2,1)S(1)}, bf16[384,512]{1,0:T(8,128)(2,1)S(1)}, u32[]{:S(2)}, u32[]{:S(2)}) collective-permute-start(bf16[384,512]{1,0:T(8,128)(2,1)S(1)} %copy-done.1), channel_id=1, source_target_pairs={{0,1},{1,0},{2,3},{3,2},{4,5},{5,4},{6,7},{7,6},{8,9},{9,8},{10,11... | collective-permute-start | bytes 1179656 | tf_op jit(solution)/shard_map/ppermute | solution.py:446
  13.1 6.3 %collective-permute-start.7 = (bf16[128,512]{1,0:T(8,128)(2,1)S(1)}, bf16[128,512]{1,0:T(8,128)(2,1)S(1)}, u32[]{:S(2)}, u32[]{:S(2)}) collective-permute-start(bf16[128,512]{1,0:T(8,128)(2,1)S(1)} %copy-done.6), channel_id=1, source_target_pairs={{0,1},{1,0},{2,3},{3,2},{4,5},{5,4},{6,7},{7,6},{8,9},{9,8},{10,11... | collective-permute-start | bytes 393224 | tf_op jit(solution)/shard_map/ppermute | solution.py:446
  13.7 7.1 %collective-permute-start.4 = (bf16[1216,128]{1,0:T(8,128)(2,1)S(1)}, bf16[1216,128]{1,0:T(8,128)(2,1)S(1)}, u32[]{:S(2)}, u32[]{:S(2)}) collective-permute-start(bf16[1216,128]{1,0:T(8,128)(2,1)S(1)} %shard_map.228.after.l0), channel_id=1, source_target_pairs={{0,1},{1,0},{2,3},{3,2},{4,5},{5,4},{6,7},{7,6},{8,9},{9,8},{10,11... | collective-permute-start | bytes 933896 | tf_op jit(solution)/shard_map/ppermute | solution.py:446
  19.4 2.8 %collective-permute-start.5 = (bf16[1216,128]{1,0:T(8,128)(2,1)S(1)}, bf16[1216,128]{1,0:T(8,128)(2,1)S(1)}, u32[]{:S(2)}, u32[]{:S(2)}) collective-permute-start(bf16[1216,128]{1,0:T(8,128)(2,1)S(1)} %get-tuple-element.39), channel_id=1, source_target_pairs={{0,1},{1,0},{2,3},{3,2},{4,5},{5,4},{6,7},{7,6},{8,9},{9,8},{10,11... | collective-permute-start | bytes 933896 | tf_op jit(solution)/shard_map/ppermute | solution.py:446
  19.5 2.7 %collective-permute-start.10 = (bf16[256,512]{1,0:T(8,128)(2,1)S(1)}, bf16[256,512]{1,0:T(8,128)(2,1)S(1)}, u32[]{:S(2)}, u32[]{:S(2)}) collective-permute-start(bf16[256,512]{1,0:T(8,128)(2,1)S(1)} %shard_map.231.across), channel_id=1, source_target_pairs={{0,1},{1,0},{2,3},{3,2},{4,5},{5,4},{6,7},{7,6},{8,9},{9,8},{10,11... | collective-permute-start | bytes 786440 | tf_op jit(solution)/shard_map/ppermute | solution.py:446
  20.0 2.2 %collective-permute-start.11 = (bf16[256,512]{1,0:T(8,128)(2,1)S(1)}, bf16[256,512]{1,0:T(8,128)(2,1)S(1)}, u32[]{:S(2)}, u32[]{:S(2)}) collective-permute-start(bf16[256,512]{1,0:T(8,128)(2,1)S(1)} %collective-permute-done.9.round_), channel_id=1, source_target_pairs={{0,1},{1,0},{2,3},{3,2},{4,5},{5,4},{6,7},{7,6},{8,9},{9,8},{10,11... | collective-permute-start | bytes 786440 | tf_op jit(solution)/shard_map/ppermute | solution.py:446
  20.7 10.1 %collective-permute-start.15 = (bf16[320,512]{1,0:T(8,128)(2,1)S(1)}, bf16[320,512]{1,0:T(8,128)(2,1)S(1)}, u32[]{:S(2)}, u32[]{:S(2)}) collective-permute-start(bf16[320,512]{1,0:T(8,128)(2,1)S(1)} %get-tuple-element.44), channel_id=1, source_target_pairs={{0,2},{1,3},{2,0},{3,1},{4,6},{5,7},{6,4},{7,5},{8,10},{9,11},{10,... | collective-permute-start | bytes 983048 | tf_op jit(solution)/shard_map/ppermute | solution.py:442
  22.2 17.0 %copy-start.2 = (bf16[256,512]{1,0:T(8,128)(2,1)S(1)}, bf16[256,512]{1,0:T(8,128)(2,1)}, u32[]{:S(2)}) copy-start(bf16[256,512]{1,0:T(8,128)(2,1)} %n_in.1) | copy-start | bytes 786436
  22.2 17.0 %copy-start.7 = (bf16[128,512]{1,0:T(8,128)(2,1)S(1)}, bf16[128,512]{1,0:T(8,128)(2,1)}, u32[]{:S(2)}) copy-start(bf16[128,512]{1,0:T(8,128)(2,1)} %n_out.3) | copy-start | bytes 393220
  22.2 17.0 %copy-start.9 = (f32[512]{0:T(512)S(1)}, f32[512]{0:T(512)}, u32[]{:S(2)}) copy-start(f32[512]{0:T(512)} %param.45) | copy-start | bytes 6148
  22.2 17.0 %copy-start.10 = (s32[1,4,32]{2,1,0:T(4,128)S(1)}, s32[1,4,32]{2,1,0:T(4,128)}, u32[]{:S(2)}) copy-start(s32[1,4,32]{2,1,0:T(4,128)} %send.3) | copy-start | bytes 1540
  27.0 1.6 %collective-permute-start.12 = (bf16[256,512]{1,0:T(8,128)(2,1)S(1)}, bf16[256,512]{1,0:T(8,128)(2,1)S(1)}, u32[]{:S(2)}, u32[]{:S(2)}) collective-permute-start(bf16[256,512]{1,0:T(8,128)(2,1)S(1)} %get-tuple-element.43), channel_id=1, source_target_pairs={{0,1},{1,0},{2,3},{3,2},{4,5},{5,4},{6,7},{7,6},{8,9},{9,8},{10,11... | collective-permute-start | bytes 786440 | tf_op jit(solution)/shard_map/ppermute | solution.py:446
  27.2 6.3 %collective-permute-start.14 = (bf16[384,512]{1,0:T(8,128)(2,1)S(1)}, bf16[384,512]{1,0:T(8,128)(2,1)S(1)}, u32[]{:S(2)}, u32[]{:S(2)}) collective-permute-start(bf16[384,512]{1,0:T(8,128)(2,1)S(1)} %get-tuple-element.37.node.w0), channel_id=1, source_target_pairs={{0,1},{1,0},{2,3},{3,2},{4,5},{5,4},{6,7},{7,6},{8,9},{9,8},{10,11... | collective-permute-start | bytes 1179656 | tf_op jit(solution)/shard_map/ppermute | solution.py:446
  27.6 9.8 %collective-permute-start.19 = (bf16[512,512]{1,0:T(8,128)(2,1)S(1)}, bf16[512,512]{1,0:T(8,128)(2,1)S(1)}, u32[]{:S(2)}, u32[]{:S(2)}) collective-permute-start(bf16[512,512]{1,0:T(8,128)(2,1)S(1)} %get-tuple-element.38.proc.w0), channel_id=1, source_target_pairs={{0,1},{1,0},{2,3},{3,2},{4,5},{5,4},{6,7},{7,6},{8,9},{9,8},{10,11... | collective-permute-start | bytes 1572872 | tf_op jit(solution)/shard_map/ppermute | solution.py:446
  30.9 6.5 %collective-permute-start.16 = (bf16[192,512]{1,0:T(8,128)(2,1)S(1)}, bf16[192,512]{1,0:T(8,128)(2,1)S(1)}, u32[]{:S(2)}, u32[]{:S(2)}) collective-permute-start(bf16[192,512]{1,0:T(8,128)(2,1)S(1)} %get-tuple-element.45.w2), channel_id=1, source_target_pairs={{0,4},{4,0},{8,12},{12,8},{1,5},{5,1},{9,13},{13,9},{2,6},{6,2},{1... | collective-permute-start | bytes 589832 | tf_op jit(solution)/shard_map/ppermute | solution.py:455
  31.6 7.7 %collective-permute-start.13 = (bf16[256,512]{1,0:T(8,128)(2,1)S(1)}, bf16[256,512]{1,0:T(8,128)(2,1)S(1)}, u32[]{:S(2)}, u32[]{:S(2)}) collective-permute-start(bf16[256,512]{1,0:T(8,128)(2,1)S(1)} %shard_map.233.after.mine), channel_id=1, source_target_pairs={{0,2},{1,3},{2,0},{3,1},{4,6},{5,7},{6,4},{7,5},{8,10},{9,11},{10,... | collective-permute-start | bytes 786440 | tf_op jit(solution)/shard_map/ppermute | solution.py:442
  33.1 7.5 %collective-permute-start.21 = (bf16[256,512]{1,0:T(8,128)(2,1)S(1)}, bf16[256,512]{1,0:T(8,128)(2,1)S(1)}, u32[]{:S(2)}, u32[]{:S(2)}) collective-permute-start(bf16[256,512]{1,0:T(8,128)(2,1)S(1)} %get-tuple-element.48.first), channel_id=1, source_target_pairs={{0,16},{16,0},{1,17},{17,1},{2,18},{18,2},{3,19},{19,3},{4,20},{20... | collective-permute-start | bytes 786440 | tf_op jit(solution)/shard_map/ppermute | solution.py:451
  33.6 3.8 %collective-permute-start.17 = (bf16[192,512]{1,0:T(8,128)(2,1)S(1)}, bf16[192,512]{1,0:T(8,128)(2,1)S(1)}, u32[]{:S(2)}, u32[]{:S(2)}) collective-permute-start(bf16[192,512]{1,0:T(8,128)(2,1)S(1)} %get-tuple-element.45.w2), channel_id=1, source_target_pairs={{0,1},{1,0},{2,3},{3,2},{4,5},{5,4},{6,7},{7,6},{8,9},{9,8},{10,11... | collective-permute-start | bytes 589832 | tf_op jit(solution)/shard_map/ppermute | solution.py:446
  37.4 1.8 %collective-permute-start.18 = (bf16[192,512]{1,0:T(8,128)(2,1)S(1)}, bf16[192,512]{1,0:T(8,128)(2,1)S(1)}, u32[]{:S(2)}, u32[]{:S(2)}) collective-permute-start(bf16[192,512]{1,0:T(8,128)(2,1)S(1)} %collective-permute-done.16.w3), channel_id=1, source_target_pairs={{0,1},{1,0},{2,3},{3,2},{4,5},{5,4},{6,7},{7,6},{8,9},{9,8},{10,11... | collective-permute-start | bytes 589832 | tf_op jit(solution)/shard_map/ppermute | solution.py:446
  39.2 12.0 %copy-start.16 = (s32[2,2048]{1,0:T(2,128)S(1)}, s32[2,2048]{1,0:T(2,128)}, u32[]{:S(2)}) copy-start(s32[2,2048]{1,0:T(2,128)} %edges.5) | copy-start | bytes 49156
  40.6 10.6 %collective-permute-start.22 = (bf16[512,512]{1,0:T(8,128)(2,1)S(1)}, bf16[512,512]{1,0:T(8,128)(2,1)S(1)}, u32[]{:S(2)}, u32[]{:S(2)}) collective-permute-start(bf16[512,512]{1,0:T(8,128)(2,1)S(1)} %shard_map.236.pair), channel_id=1, source_target_pairs={{0,1},{1,0},{2,3},{3,2},{4,5},{5,4},{6,7},{7,6},{8,9},{9,8},{10,11... | collective-permute-start | bytes 1572872 | tf_op jit(solution)/shard_map/ppermute | solution.py:446
  40.6 10.6 %collective-permute-start.20 = (bf16[256,512]{1,0:T(8,128)(2,1)S(1)}, bf16[256,512]{1,0:T(8,128)(2,1)S(1)}, u32[]{:S(2)}, u32[]{:S(2)}) collective-permute-start(bf16[256,512]{1,0:T(8,128)(2,1)S(1)} %get-tuple-element.46.after.mine.middle), channel_id=1, source_target_pairs={{0,1},{1,0},{2,3},{3,2},{4,5},{5,4},{6,7},{7,6},{8,9},{9,8},{10,11... | collective-permute-start | bytes 786440 | tf_op jit(solution)/shard_map/ppermute | solution.py:446
  41.1 6.9 %collective-permute-start.23 = (bf16[32,512]{1,0:T(8,128)(2,1)S(1)}, bf16[32,512]{1,0:T(8,128)(2,1)S(1)}, u32[]{:S(2)}, u32[]{:S(2)}) collective-permute-start(bf16[32,512]{1,0:T(8,128)(2,1)S(1)} %get-tuple-element.53), channel_id=1, source_target_pairs={{0,4},{4,0},{8,12},{12,8},{1,5},{5,1},{9,13},{13,9},{2,6},{6,2},{1... | collective-permute-start | bytes 98312 | tf_op jit(solution)/shard_map/ppermute | solution.py:582
  42.5 7.1 %collective-permute-start.24 = (bf16[32,512]{1,0:T(8,128)(2,1)S(1)}, bf16[32,512]{1,0:T(8,128)(2,1)S(1)}, u32[]{:S(2)}, u32[]{:S(2)}) collective-permute-start(bf16[32,512]{1,0:T(8,128)(2,1)S(1)} %get-tuple-element.54), channel_id=1, source_target_pairs={{0,8},{4,12},{8,0},{12,4},{1,9},{5,13},{9,1},{13,5},{2,10},{6,14},... | collective-permute-start | bytes 98312 | tf_op jit(solution)/shard_map/ppermute | solution.py:582
  45.3 5.8 %collective-permute-start.25 = (bf16[32,512]{1,0:T(8,128)(2,1)S(1)}, bf16[32,512]{1,0:T(8,128)(2,1)S(1)}, u32[]{:S(2)}, u32[]{:S(2)}) collective-permute-start(bf16[32,512]{1,0:T(8,128)(2,1)S(1)} %get-tuple-element.55), channel_id=1, source_target_pairs={{4,8},{8,4},{5,9},{9,5},{6,10},{10,6},{7,11},{11,7},{20,24},{24,20... | collective-permute-start | bytes 98312 | tf_op jit(solution)/shard_map/ppermute | solution.py:582
  48.1 12.0 %collective-permute-start.30 = (bf16[384,512]{1,0:T(8,128)(2,1)S(1)}, bf16[384,512]{1,0:T(8,128)(2,1)S(1)}, u32[]{:S(2)}, u32[]{:S(2)}) collective-permute-start(bf16[384,512]{1,0:T(8,128)(2,1)S(1)} %get-tuple-element.60.w0), channel_id=1, source_target_pairs={{0,2},{1,3},{2,0},{3,1},{4,6},{5,7},{6,4},{7,5},{8,10},{9,11},{10,... | collective-permute-start | bytes 1179656 | tf_op jit(solution)/shard_map/ppermute | solution.py:442
  51.1 2.7 %collective-permute-start.26 = (bf16[96,512]{1,0:T(8,128)(2,1)S(1)}, bf16[96,512]{1,0:T(8,128)(2,1)S(1)}, u32[]{:S(2)}, u32[]{:S(2)}) collective-permute-start(bf16[96,512]{1,0:T(8,128)(2,1)S(1)} %shard_map.238.halo), channel_id=1, source_target_pairs={{0,1},{1,0},{2,3},{3,2},{4,5},{5,4},{6,7},{7,6},{8,9},{9,8},{10,11... | collective-permute-start | bytes 294920 | tf_op jit(solution)/shard_map/ppermute | solution.py:446
  51.2 2.6 %copy-start.21 = (f32[512]{0:T(512)S(1)}, f32[512]{0:T(512)}, u32[]{:S(2)}) copy-start(f32[512]{0:T(512)} %param.46) | copy-start | bytes 6148
  53.9 13.2 %copy-start.11 = (f32[512]{0:T(512)S(1)}, f32[512]{0:T(512)}, u32[]{:S(2)}) copy-start(f32[512]{0:T(512)} %param.47) | copy-start | bytes 6148
  59.5 1.7 %collective-permute-start.27 = (bf16[256,512]{1,0:T(8,128)(2,1)S(1)}, bf16[256,512]{1,0:T(8,128)(2,1)S(1)}, u32[]{:S(2)}, u32[]{:S(2)}) collective-permute-start(bf16[256,512]{1,0:T(8,128)(2,1)S(1)} %get-tuple-element.57), channel_id=1, source_target_pairs={{0,1},{1,0},{2,3},{3,2},{4,5},{5,4},{6,7},{7,6},{8,9},{9,8},{10,11... | collective-permute-start | bytes 786440 | tf_op jit(solution)/shard_map/ppermute | solution.py:446
  60.0 2.8 %collective-permute-start.29 = (bf16[384,512]{1,0:T(8,128)(2,1)S(1)}, bf16[384,512]{1,0:T(8,128)(2,1)S(1)}, u32[]{:S(2)}, u32[]{:S(2)}) collective-permute-start(bf16[384,512]{1,0:T(8,128)(2,1)S(1)} %get-tuple-element.60.w0), channel_id=1, source_target_pairs={{0,1},{1,0},{2,3},{3,2},{4,5},{5,4},{6,7},{7,6},{8,9},{9,8},{10,11... | collective-permute-start | bytes 1179656 | tf_op jit(solution)/shard_map/ppermute | solution.py:446
  60.1 2.7 %collective-permute-start.31 = (bf16[384,512]{1,0:T(8,128)(2,1)S(1)}, bf16[384,512]{1,0:T(8,128)(2,1)S(1)}, u32[]{:S(2)}, u32[]{:S(2)}) collective-permute-start(bf16[384,512]{1,0:T(8,128)(2,1)S(1)} %collective-permute-done.30.w2), channel_id=1, source_target_pairs={{0,1},{1,0},{2,3},{3,2},{4,5},{5,4},{6,7},{7,6},{8,9},{9,8},{10,11... | collective-permute-start | bytes 1179656 | tf_op jit(solution)/shard_map/ppermute | solution.py:446
  61.2 5.8 %collective-permute-start.28 = (bf16[128,512]{1,0:T(8,128)(2,1)S(1)}, bf16[128,512]{1,0:T(8,128)(2,1)S(1)}, u32[]{:S(2)}, u32[]{:S(2)}) collective-permute-start(bf16[128,512]{1,0:T(8,128)(2,1)S(1)} %get-tuple-element.59), channel_id=1, source_target_pairs={{0,2},{1,3},{2,0},{3,1},{4,6},{5,7},{6,4},{7,5},{8,10},{9,11},{10,... | collective-permute-start | bytes 393224 | tf_op jit(solution)/shard_map/ppermute | solution.py:442

commit v14 on v13

--- a/solution.py
+++ b/solution.py
@@ -141,13 +141,16 @@
     token[...] = jnp.zeros(token.shape, token.dtype)
 
 
-def first_pack_kernel(plan, grid, send, w_in, w_out, n_out, p_out, token, half, *outs):
+def first_pack_kernel(plan, grid, send, w_in, w_out, n_out, p_out, p_in, token, half, *outs):
     place = 0
     for source, axes in ((w_in, BY_GROUP), (w_out, BY_GROUP), (n_out, BY_PART), (p_out, BY_GROUP)):
         rows = source.shape[0] // 2
         begin = pl.multiple_of(parity(axes) * rows, 64)
         half[place : place + rows, :] = source[pl.ds(begin, rows), :]
         place += rows
+    rows = half.shape[0] - place
+    begin = pl.multiple_of(lax.axis_index("groups") * (p_in.shape[0] // 2), 64)
+    half[place:, :] = p_in[pl.ds(begin, rows), :]
     pick_lists(plan, grid[...], send, outs)
 
 
@@ -159,14 +162,14 @@
             out[begin : begin + STEP, :] = embed_rows(geom[:, begin : begin + STEP], geo[...])
 
 
-def cross_kernel(counts, node, proc, lat, crossing, lat_out):
+def cross_kernel(counts, skipped, node, proc, lat, crossing, lat_out):
     lat_out[...] = lat[...]
     place = 0
-    for stack, rows, axes in ((node, counts[0], BY_PART), (proc, counts[1], BY_GROUP)):
+    for stack, rows, axes, gone in ((node, counts[0], BY_PART, 0), (proc, counts[1], BY_GROUP, skipped)):
         half = rows // 2
-        begin = pl.multiple_of(parity(axes) * half, 64)
-        crossing[place : place + half, :] = stack[pl.ds(begin, half), :]
-        place += half
+        begin = pl.multiple_of(parity(axes) * half + gone, 32)
+        crossing[place : place + half - gone, :] = stack[pl.ds(begin, half - gone), :]
+        place += half - gone
 
 
 def rows_kernel(source, out):
@@ -177,12 +180,14 @@
     stack_into(out, (first, second))
 
 
-def split_kernel(ins, early, source, after, node, proc):
-    n, p = ins
-    n_rest, p_rest = node.shape[0] - n, proc.shape[0] - p
-    base = early.shape[0] - n_rest - p_rest
-    stack_into(node, (source.at[pl.ds(0, n), :], early.at[pl.ds(base, n_rest), :]))
-    stack_into(proc, (source.at[pl.ds(n, p), :], early.at[pl.ds(base + n_rest, p_rest), :]))
+def split_kernel(n, early_rows, early, source, after, node, proc):
+    rest = source.shape[0] - n
+    n_out = node.shape[0] - n
+    p_out = proc.shape[0] - rest - early_rows
+    base = early.shape[0] - n_out - p_out - early_rows
+    stack_into(node, (source.at[pl.ds(0, n), :], early.at[pl.ds(base, n_out), :]))
+    first = early.at[pl.ds(base + n_out + p_out, early_rows), :]
+    stack_into(proc, (first, source.at[pl.ds(n, rest), :], early.at[pl.ds(base + n_out, p_out), :]))
 
 
 def concat_kernel(*refs):
@@ -260,18 +265,20 @@
                 totals[...] += part
 
 
-def hand_out(totals, gain, keep, give):
+def hand_out(totals, gain, keep, *give):
     rows = totals.shape[0] // 4
     core = lax.rem(lax.axis_index("sub"), 2)
     for half in range(2):
-        for out, which in ((keep, core), (give, 1 - core)):
+        kept = keep.at[pl.ds(half * rows, rows), :]
+        given = give[0].at[pl.ds(half * rows, rows), :] if len(give) == 1 else give[half]
+        for out, which in ((kept, core), (given, 1 - core)):
             place = pl.multiple_of((2 * half + which) * rows, rows)
-            out[half * rows : (half + 1) * rows, :] = (totals[pl.ds(place, rows), :] * gain[...]).astype(BF16)
+            out[...] = (totals[pl.ds(place, rows), :] * gain[...]).astype(BF16)
 
 
 def enc_kernel(
     plan, slots, grid_rows, mesh_rows, k_in, emb, edges, gain, l0, l1, l2, l3, o_in, o_out, b_in, b_out,
-    across, round_, both, round_both, live, keep, give, own_mesh, full, stack, table, messages, totals,
+    across, round_, both, round_both, live, keep, give, give_more, own_mesh, full, stack, table, messages, totals,
 ):
     d = gain.shape[1]
     quarter = lax.axis_index("sub")
@@ -313,7 +320,7 @@
         return dot(jnp.concatenate(chosen, axis=1), table[...])
 
     edge_blocks(edges, live[0] * BLOCK, first_stage, joined(stack, k_in, d // 4), messages, totals)
-    hand_out(totals, gain, keep, give)
+    hand_out(totals, gain, keep, give, give_more)
 
 
 def node_update(mesh, shares, w_in, w_out, gain):
@@ -327,8 +334,10 @@
     return (mine.astype(F32) + theirs.astype(F32)).astype(BF16)
 
 
-def add_kernel(mine, theirs, out):
-    out[...] = add(mine[...], theirs[...])
+def add_kernel(mine, first, second, out):
+    rows = first.shape[0]
+    out[:rows, :] = add(mine[:rows, :], first[...])
+    out[rows:, :] = add(mine[rows:, :], second[...])
 
 
 def node_kernel(
@@ -501,11 +510,12 @@
     width = grid_lat.shape[1]
 
     slots = grid_send.shape[2]
+    early_rows = k_in // 4
     (token,) = call(begin_kernel, [shape(16, 128)], [], flops=LONG)
     edge_half, *outgoing = call(
         functools.partial(first_pack_kernel, plan),
-        [shape((k_in + 2 * k_out + n_out) // 2, d)] + [shape(slots, width)] * len(plan),
-        [grid_lat, grid_send, enc_edge_in, enc_edge_out, enc_node_out, proc_edge_out, token],
+        [shape((k_in + 2 * k_out + n_out) // 2 + early_rows, d)] + [shape(slots, width)] * len(plan),
+        [grid_lat, grid_send, enc_edge_in, enc_edge_out, enc_node_out, proc_edge_out, proc_edge_in, token],
     )
     first_across = to_chip(edge_half)
     (edge_across,) = call(rows_kernel, [shape((k_in + k_out) // 2, d)], [first_across])
@@ -530,8 +540,8 @@
         flops=2 * (n_enc + n_proc) * d * 128,
     )
     crossing, lat_sent = call(
-        functools.partial(cross_kernel, (n_in, k_in)),
-        [shape((n_in + k_in) // 2, d), shape(lat.shape[0], width)],
+        functools.partial(cross_kernel, (n_in, k_in), early_rows),
+        [shape((n_in + k_in) // 2 - early_rows, d), shape(lat.shape[0], width)],
         [node_w, proc_w, lat_across],
     )
     lat_both = to_core(lat_sent)
@@ -540,9 +550,9 @@
 
     halo_rows = padded(got)
     half = mesh_rows // 2
-    keep, give, own_mesh = call(
+    keep, give, give_more, own_mesh = call(
         functools.partial(enc_kernel, plan, slots, grid_rows, mesh_rows, k_in),
-        [shape(half, d)] * 3,
+        [shape(half, d), shape(half // 2, d), shape(half // 2, d), shape(half, d)],
         [
             enc_emb, enc_edges, enc_edge_gain, lat, lat_across, lat_beside, lat_both,
             enc_edge_in, enc_edge_out, *edge_beside,
@@ -558,9 +568,9 @@
         flops=2 * n_enc * d * (3 * d + grid_rows + mesh_rows + halo_rows),
         smem=1,
     )
-    (chip_sum,) = call(add_kernel, [shape(half, d)], [keep, to_core(give)])
+    (chip_sum,) = call(add_kernel, [shape(half, d)], [keep, to_core(give), to_core(give_more)])
     node_across, proc_across = call(
-        functools.partial(split_kernel, (n_in // 2, k_in // 2)),
+        functools.partial(split_kernel, n_in // 2, early_rows),
         [shape((n_in + n_out) // 2, d), shape((k_in + k_out) // 2, d)],
         [first_across, next_across, chip_sum],
     )

time: 68.6 us -> 69.8 us (1.017)
  waiting for transfers between devices: 22.3 us -> 25.4 us
  starting transfers between devices: 25.2 us -> 23.2 us
    ppermute x6, starting transfers between devices: 8.21 us -> 5.96 us  [to_chip(): return lax.ppermute(v, 'sub', [(i, i ^ 2) for i in range(4)])]
    ppermute x1, waiting for transfers between devices: 3.83 us -> 5.08 us  [to_partition(): lax.ppermute(v, 'dom', [(i, i ^ 1) for i in range(lax.axis_size('dom'))])]
    ppermute x6, waiting for transfers between devices: 4.74 us -> 5.69 us  [local(): lax.ppermute(v, 'dom', entry[0])]
    ppermute x17 -> x18, waiting for transfers between devices: 1.55 us -> 2.07 us  [to_core(): return lax.ppermute(v, 'sub', [(i, i ^ 1) for i in range(4)])]
    ppermute x17 -> x18, starting transfers between devices: 3.6 us -> 3.99 us  [to_core(): return lax.ppermute(v, 'sub', [(i, i ^ 1) for i in range(4)])]
  transfers between devices with their start and end apart: 32 -> 33, of which waited for: 10 -> 12; matrix products, arithmetic and copies ran while one was open for 0% -> 0% of each run, Pallas kernels for 24% -> 23%
where the time goes in v14:
time: 69.8 us; the launch traced here: 69.6 us
  waiting for transfers between devices  25.4 us (36%)
  starting transfers between devices  23.2 us (33%)
  Pallas kernels  17.9 us (26%)
  between operations  1.76 us (3%)
  local copies, waits for them, and re-layouts  1.33 us (2%)
    pallas_call x16, Pallas kernels, call(): pl.pallas_call(body, out_shape=tuple(outs), in_specs=specs, out_specs=tup...  17.9 us
    ppermute x6, waiting for transfers between devices, to_chip(): return lax.ppermute(v, 'sub', [(i, i ^ 2) for i in range(4)])  12.3 us
    ppermute x6, starting transfers between devices, local(): lax.ppermute(v, 'dom', entry[0])  11.6 us
    ppermute x6, starting transfers between devices, to_chip(): return lax.ppermute(v, 'sub', [(i, i ^ 2) for i in range(4)])  5.96 us
    ppermute x6, waiting for transfers between devices, local(): lax.ppermute(v, 'dom', entry[0])  5.69 us
    ppermute x1, waiting for transfers between devices, to_partition(): lax.ppermute(v, 'dom', [(i, i ^ 1) for i in range(lax.axis_size('dom'))])  5.08 us
    ppermute x18, starting transfers between devices, to_core(): return lax.ppermute(v, 'sub', [(i, i ^ 1) for i in range(4)])  3.99 us
    ppermute x18, waiting for transfers between devices, to_core(): return lax.ppermute(v, 'sub', [(i, i ^ 1) for i in range(4)])  2.07 us
  transfers between devices with their start and end apart: 33, of which 12 were waited for; matrix products, arithmetic and copies ran while one was open for 0% of the time, Pallas kernels for 23%

profile of v14, /device:TPU:12, one launch (start us, length us, event | category | flops | bytes accessed | tf_op | source)
XLA Modules:
  0.0 69.6 jit_solution(5093836159124405248)
XLA Ops:
  0.1 0.8 %copy-done.5 = bf16[128,512]{1,0:T(8,128)(2,1)S(1)} copy-done((bf16[128,512]{1,0:T(8,128)(2,1)S(1)}, bf16[128,512]{1,0:T(8,128)(2,1)}, u32[]{:S(2)}) %copy-start.5) | copy-done | bytes 131096
  0.9 0.2 copy-done.1
  1.1 0.0 copy-done.6
  1.1 0.0 copy-done
  1.1 0.1 copy-done.2
  1.3 0.0 copy-done.7
  1.3 0.0 copy-start.18
  1.3 0.3 shard_map.227
  1.7 0.0 copy-start.19
  1.7 0.0 copy-start.20
  1.7 1.6 %collective-permute-start.8 = (bf16[480,512]{1,0:T(8,128)(2,1)S(1)}, bf16[480,512]{1,0:T(8,128)(2,1)S(1)}, u32[]{:S(2)}, u32[]{:S(2)}) collective-permute-start(bf16[480,512]{1,0:T(8,128)(2,1)S(1)} %get-tuple-element.41), channel_id=1, source_target_pairs={{0,2},{1,3},{2,0},{3,1},{4,6},{5,7},{6,4},{7,5},{8,10},{9,11},{10,... | collective-permute-start | bytes 1474568 | tf_op jit(solution)/shard_map/ppermute | solution.py:451
  3.2 0.5 collective-permute-start
  3.7 2.6 %collective-permute-start.1 = (bf16[64,128]{1,0:T(8,128)(2,1)S(1)}, bf16[64,128]{1,0:T(8,128)(2,1)S(1)}, u32[]{:S(2)}, u32[]{:S(2)}) collective-permute-start(bf16[64,128]{1,0:T(8,128)(2,1)S(1)} %get-tuple-element.35), channel_id=1, source_target_pairs={{0,8},{4,12},{8,0},{12,4},{1,9},{5,13},{9,1},{13,5},{2,10},{6,14},... | collective-permute-start | bytes 49160 | tf_op jit(solution)/shard_map/ppermute | solution.py:522
  6.3 2.3 %collective-permute-start.2 = (bf16[64,128]{1,0:T(8,128)(2,1)S(1)}, bf16[64,128]{1,0:T(8,128)(2,1)S(1)}, u32[]{:S(2)}, u32[]{:S(2)}) collective-permute-start(bf16[64,128]{1,0:T(8,128)(2,1)S(1)} %get-tuple-element.36), channel_id=1, source_target_pairs={{4,8},{8,4},{5,9},{9,5},{6,10},{10,6},{7,11},{11,7},{20,24},{24,20... | collective-permute-start | bytes 49160 | tf_op jit(solution)/shard_map/ppermute | solution.py:522
  8.7 3.2 %collective-permute-done.2.refs_4_ = bf16[64,128]{1,0:T(8,128)(2,1)S(1)} collective-permute-done((bf16[64,128]{1,0:T(8,128)(2,1)S(1)}, bf16[64,128]{1,0:T(8,128)(2,1)S(1)}, u32[]{:S(2)}, u32[]{:S(2)}) %collective-permute-start.2) | collective-permute-done | bytes 16416 | tf_op jit(solution)/shard_map/ppermute | solution.py:522
  11.9 0.6 collective-permute-start.3
  12.5 3.3 %collective-permute-done.8.source.early = bf16[480,512]{1,0:T(8,128)(2,1)S(1)} collective-permute-done((bf16[480,512]{1,0:T(8,128)(2,1)S(1)}, bf16[480,512]{1,0:T(8,128)(2,1)S(1)}, u32[]{:S(2)}, u32[]{:S(2)}) %collective-permute-start.8) | collective-permute-done | bytes 491552 | tf_op jit(solution)/shard_map/ppermute | solution.py:451
  15.9 0.6 collective-permute-start.9
  16.5 0.5 collective-permute-start.7
  17.0 1.8 %shard_map.229 = (bf16[384,512]{1,0:T(8,128)(2,1)S(1)}, bf16[512,512]{1,0:T(8,128)(2,1)S(1)}, bf16[1024,512]{1,0:T(8,128)(2,1)S(1)}, bf16[2048,512]{1,0:T(8,128)(2,1)S(1)}) custom-call(bf16[256,512]{1,0:T(8,128)(2,1)S(1)} %copy-done.13, bf16[128,512]{1,0:T(8,128)(2,1)S(1)} %copy-done.5, bf16[384,512]{1,0:T(8,128)(2,1)S(1)} %copy-done.1, ...), custom_call_target="tpu_custom_call" | custom-call | flops 402653184 | bytes 5357568 | tf_op jit(solution)/shard_map/pallas_call | solution.py:71
  18.8 2.6 %collective-permute-done.3.lat.l1 = bf16[1216,128]{1,0:T(8,128)(2,1)S(1)} collective-permute-done((bf16[1216,128]{1,0:T(8,128)(2,1)S(1)}, bf16[1216,128]{1,0:T(8,128)(2,1)S(1)}, u32[]{:S(2)}, u32[]{:S(2)}) %collective-permute-start.3) | collective-permute-done | bytes 311328 | tf_op jit(solution)/shard_map/ppermute | solution.py:451
  21.4 0.1 collective-permute-start.5
  21.5 0.5 collective-permute-start.10
  22.0 0.3 collective-permute-done.9.round_
  23.0 0.6 collective-permute-start.15
  23.6 1.5 %collective-permute-start.16 = (bf16[224,512]{1,0:T(8,128)(2,1)S(1)}, bf16[224,512]{1,0:T(8,128)(2,1)S(1)}, u32[]{:S(2)}, u32[]{:S(2)}) collective-permute-start(bf16[224,512]{1,0:T(8,128)(2,1)S(1)} %get-tuple-element.46), channel_id=1, source_target_pairs={{0,2},{1,3},{2,0},{3,1},{4,6},{5,7},{6,4},{7,5},{8,10},{9,11},{10,... | collective-permute-start | bytes 688136 | tf_op jit(solution)/shard_map/ppermute | solution.py:451
  25.1 0.0 copy-start.3
  25.1 0.0 copy-start.8
  25.1 0.0 copy-start.10
  25.1 0.0 copy-start.11
  25.1 4.7 %shard_map.232 = (bf16[256,512]{1,0:T(8,128)(2,1)S(1)}, bf16[128,512]{1,0:T(8,128)(2,1)S(1)}, bf16[128,512]{1,0:T(8,128)(2,1)S(1)}, bf16[256,512]{1,0:T(8,128)(2,1)S(1)}) custom-call(bf16[1024,512]{1,0:T(8,128)(2,1)S(1)} %get-tuple-element.37.emb, s32[2,1024]{1,0:T(2,128)S(1)} %copy-done.19, f32[1,512]{1,0:T(1,128)S(1)} %bitcast.6, ...), custom_call_target="tpu_custom_call" | custom-call | flops 2952790016 | bytes 5187588 | tf_op jit(solution)/shard_map/pallas_call | solution.py:71
  29.9 0.1 collective-permute-start.12
  30.0 0.5 collective-permute-start.13
  30.5 0.1 collective-permute-start.20
  30.5 0.8 %collective-permute-done.12.first = bf16[128,512]{1,0:T(8,128)(2,1)S(1)} collective-permute-done((bf16[128,512]{1,0:T(8,128)(2,1)S(1)}, bf16[128,512]{1,0:T(8,128)(2,1)S(1)}, u32[]{:S(2)}, u32[]{:S(2)}) %collective-permute-start.12) | collective-permute-done | bytes 131104 | tf_op jit(solution)/shard_map/ppermute | solution.py:455
  31.3 0.2 collective-permute-done.13.second
  31.5 0.1 shard_map.233.after.mine
  31.6 0.5 collective-permute-start.17
  32.1 1.1 %collective-permute-start.14 = (bf16[256,512]{1,0:T(8,128)(2,1)S(1)}, bf16[256,512]{1,0:T(8,128)(2,1)S(1)}, u32[]{:S(2)}, u32[]{:S(2)}) collective-permute-start(bf16[256,512]{1,0:T(8,128)(2,1)S(1)} %shard_map.233.after.mine), channel_id=1, source_target_pairs={{0,2},{1,3},{2,0},{3,1},{4,6},{5,7},{6,4},{7,5},{8,10},{9,11},{10,... | collective-permute-start | bytes 786440 | tf_op jit(solution)/shard_map/ppermute | solution.py:451
  33.2 0.5 collective-permute-start.22
  33.7 5.1 %collective-permute-done.17.w3 = bf16[192,512]{1,0:T(8,128)(2,1)S(1)} collective-permute-done((bf16[192,512]{1,0:T(8,128)(2,1)S(1)}, bf16[192,512]{1,0:T(8,128)(2,1)S(1)}, u32[]{:S(2)}, u32[]{:S(2)}) %collective-permute-start.17) | collective-permute-done | bytes 196640 | tf_op jit(solution)/shard_map/ppermute | solution.py:464
  38.8 1.6 %collective-permute-done.14.theirs = bf16[256,512]{1,0:T(8,128)(2,1)S(1)} collective-permute-done((bf16[256,512]{1,0:T(8,128)(2,1)S(1)}, bf16[256,512]{1,0:T(8,128)(2,1)S(1)}, u32[]{:S(2)}, u32[]{:S(2)}) %collective-permute-start.14) | collective-permute-done | bytes 262176 | tf_op jit(solution)/shard_map/ppermute | solution.py:451
  40.4 1.2 %shard_map.235 = (bf16[256,512]{1,0:T(8,128)(2,1)S(1)}, bf16[384,512]{1,0:T(8,128)(2,1)S(1)}, bf16[32,512]{1,0:T(8,128)(2,1)S(1)}, bf16[32,512]{1,0:T(8,128)(2,1)S(1)}, bf16[32,512]{1,0:T(8,128)(2,1)S(1)}) custom-call(bf16[256,512]{1,0:T(8,128)(2,1)S(1)} %get-tuple-element.42.mesh, bf16[256,512]{1,0:T(8,128)(2,1)S(1)} %shard_map.233.after.mine, ...), custom_call_target="tpu_custom_call" | custom-call | flops 402653184 | bytes 4033024 | tf_op jit(solution)/shard_map/pallas_call | solution.py:71
  41.7 0.1 collective-permute-start.23
  41.8 0.5 collective-permute-start.21
  42.3 1.6 %collective-permute-start.24 = (bf16[32,512]{1,0:T(8,128)(2,1)S(1)}, bf16[32,512]{1,0:T(8,128)(2,1)S(1)}, u32[]{:S(2)}, u32[]{:S(2)}) collective-permute-start(bf16[32,512]{1,0:T(8,128)(2,1)S(1)} %get-tuple-element.55), channel_id=1, source_target_pairs={{0,4},{4,0},{8,12},{12,8},{1,5},{5,1},{9,13},{13,9},{2,6},{6,2},{1... | collective-permute-start | bytes 98312 | tf_op jit(solution)/shard_map/ppermute | solution.py:592
  43.9 2.6 %collective-permute-start.25 = (bf16[32,512]{1,0:T(8,128)(2,1)S(1)}, bf16[32,512]{1,0:T(8,128)(2,1)S(1)}, u32[]{:S(2)}, u32[]{:S(2)}) collective-permute-start(bf16[32,512]{1,0:T(8,128)(2,1)S(1)} %get-tuple-element.56), channel_id=1, source_target_pairs={{0,8},{4,12},{8,0},{12,4},{1,9},{5,13},{9,1},{13,5},{2,10},{6,14},... | collective-permute-start | bytes 98312 | tf_op jit(solution)/shard_map/ppermute | solution.py:592
  46.5 2.1 %collective-permute-start.26 = (bf16[32,512]{1,0:T(8,128)(2,1)S(1)}, bf16[32,512]{1,0:T(8,128)(2,1)S(1)}, u32[]{:S(2)}, u32[]{:S(2)}) collective-permute-start(bf16[32,512]{1,0:T(8,128)(2,1)S(1)} %get-tuple-element.57), channel_id=1, source_target_pairs={{4,8},{8,4},{5,9},{9,5},{6,10},{10,6},{7,11},{11,7},{20,24},{24,20... | collective-permute-start | bytes 98312 | tf_op jit(solution)/shard_map/ppermute | solution.py:592
  49.2 0.6 collective-permute-start.31
  49.8 2.4 %collective-permute-done.26.refs_2_ = bf16[32,512]{1,0:T(8,128)(2,1)S(1)} collective-permute-done((bf16[32,512]{1,0:T(8,128)(2,1)S(1)}, bf16[32,512]{1,0:T(8,128)(2,1)S(1)}, u32[]{:S(2)}, u32[]{:S(2)}) %collective-permute-start.26) | collective-permute-done | bytes 32800 | tf_op jit(solution)/shard_map/ppermute | solution.py:592
  52.3 0.1 collective-permute-start.27
  52.4 0.0 copy-start.21
  52.4 2.6 %shard_map.237 = (bf16[1536,512]{1,0:T(8,128)(2,1)S(1)}, f32[1024,512]{1,0:T(8,128)S(1)}, bf16[512,512]{1,0:T(8,128)(2,1)S(1)}, bf16[512,512]{1,0:T(8,128)(2,1)S(1)}) custom-call(bf16[2048,512]{1,0:T(8,128)(2,1)S(1)} %get-tuple-element.49.emb, bf16[256,512]{1,0:T(8,128)(2,1)S(1)} %get-tuple-element.48.after.mine.middle, ...), custom_call_target="tpu_custom_call" | custom-call | flops 1610612736 | bytes 9453568 | tf_op jit(solution)/shard_map/pallas_call | solution.py:71
  55.0 0.0 copy-start.12
  55.0 5.6 %shard_map.239 = (bf16[256,512]{1,0:T(8,128)(2,1)S(1)}, bf16[256,512]{1,0:T(8,128)(2,1)S(1)}) custom-call(bf16[2048,512]{1,0:T(8,128)(2,1)S(1)} %get-tuple-element.49.emb, s32[2,2048]{1,0:T(2,128)S(1)} %copy-done.16, f32[1,512]{1,0:T(1,128)S(1)} %bitcast.7, bf16[1536,512]{1,0:T(8,128)(2,1)S(1)} %get-tuple-element.51.table, ...), custom_call_target="tpu_custom_call" | custom-call | flops 3489660928 | bytes 7555076 | tf_op jit(solution)/shard_map/pallas_call | solution.py:71
  60.6 0.5 collective-permute-start.28
  61.2 0.1 collective-permute-start.30
  61.2 0.4 collective-permute-start.32
  61.7 0.6 collective-permute-done.28.theirs
  62.3 0.1 shard_map.240
  62.4 0.6 collective-permute-start.29
  63.0 0.4 collective-permute-done.32.w3
  63.5 4.8 %collective-permute-done.29.theirs = bf16[128,512]{1,0:T(8,128)(2,1)S(1)} collective-permute-done((bf16[128,512]{1,0:T(8,128)(2,1)S(1)}, bf16[128,512]{1,0:T(8,128)(2,1)S(1)}, u32[]{:S(2)}, u32[]{:S(2)}) %collective-permute-start.29) | collective-permute-done | bytes 131104 | tf_op jit(solution)/shard_map/ppermute | solution.py:451
  68.2 1.4 %shard_map.241 = bf16[128,512]{1,0:T(8,128)(2,1)} custom-call(bf16[256,512]{1,0:T(8,128)(2,1)S(1)} %get-tuple-element.48.after.mine.middle, bf16[128,512]{1,0:T(8,128)(2,1)S(1)} %get-tuple-element.60.mine, bf16[128,512]{1,0:T(8,128)(2,1)S(1)} %collective-permute-done.29.theirs, f32[1,512]{1,0:T(1,128)S(1)} %bitcast.5, ...), custom_call_target="tpu_custom_call" | custom-call | flops 201326592 | bytes 2230272 | tf_op jit(solution)/shard_map/pallas_call | solution.py:71
  (62 shorter events, 0.3 us)
Async XLA Ops:
  0.0 0.9 %copy-start.5 = (bf16[128,512]{1,0:T(8,128)(2,1)S(1)}, bf16[128,512]{1,0:T(8,128)(2,1)}, u32[]{:S(2)}) copy-start(bf16[128,512]{1,0:T(8,128)(2,1)} %e_out.1) | copy-start | bytes 393220
  0.0 1.1 %copy-start.1 = (bf16[384,512]{1,0:T(8,128)(2,1)S(1)}, bf16[384,512]{1,0:T(8,128)(2,1)}, u32[]{:S(2)}) copy-start(bf16[384,512]{1,0:T(8,128)(2,1)} %p_in.3) | copy-start | bytes 1179652
  0.0 1.1 %copy-start.6 = (bf16[128,512]{1,0:T(8,128)(2,1)S(1)}, bf16[128,512]{1,0:T(8,128)(2,1)}, u32[]{:S(2)}) copy-start(bf16[128,512]{1,0:T(8,128)(2,1)} %p_out.3) | copy-start | bytes 393220
  0.0 1.1 %copy-start = (bf16[512,128]{1,0:T(8,128)(2,1)S(1)}, bf16[512,128]{1,0:T(8,128)(2,1)}, u32[]{:S(2)}) copy-start(bf16[512,128]{1,0:T(8,128)(2,1)} %refs_0_.1) | copy-start | bytes 393220
  0.0 1.1 %copy-start.9 = (s32[1,4,64]{2,1,0:T(4,128)S(1)}, s32[1,4,64]{2,1,0:T(4,128)}, u32[]{:S(2)}) copy-start(s32[1,4,64]{2,1,0:T(4,128)} %send.2) | copy-start | bytes 3076
  0.0 1.3 %copy-start.2 = (bf16[384,512]{1,0:T(8,128)(2,1)S(1)}, bf16[384,512]{1,0:T(8,128)(2,1)}, u32[]{:S(2)}) copy-start(bf16[384,512]{1,0:T(8,128)(2,1)} %o_in.1) | copy-start | bytes 1179652
  0.0 1.3 %copy-start.7 = (bf16[128,512]{1,0:T(8,128)(2,1)S(1)}, bf16[128,512]{1,0:T(8,128)(2,1)}, u32[]{:S(2)}) copy-start(bf16[128,512]{1,0:T(8,128)(2,1)} %o_out.1) | copy-start | bytes 393220
  0.0 11.9 %copy-start.4 = (bf16[512,128]{1,0:T(8,128)(2,1)S(1)}, bf16[512,128]{1,0:T(8,128)(2,1)}, u32[]{:S(2)}) copy-start(bf16[512,128]{1,0:T(8,128)(2,1)} %refs_1_.1) | copy-start | bytes 393220
  1.3 15.7 %copy-start.13 = (bf16[256,512]{1,0:T(8,128)(2,1)S(1)}, bf16[256,512]{1,0:T(8,128)(2,1)}, u32[]{:S(2)}) copy-start(bf16[256,512]{1,0:T(8,128)(2,1)} %e_in.1) | copy-start | bytes 786436
  1.3 15.7 %copy-start.14 = (f32[4,2048]{1,0:T(4,128)S(1)}, f32[4,2048]{1,0:T(4,128)}, u32[]{:S(2)}) copy-start(f32[4,2048]{1,0:T(4,128)} %pgeom.1) | copy-start | bytes 98308
  1.3 15.7 %copy-start.15 = (f32[4,1024]{1,0:T(4,128)S(1)}, f32[4,1024]{1,0:T(4,128)}, u32[]{:S(2)}) copy-start(f32[4,1024]{1,0:T(4,128)} %egeom.1) | copy-start | bytes 49156
  1.3 15.7 %copy-start.17 = (f32[4,512]{1,0:T(4,128)S(1)}, f32[4,512]{1,0:T(4,128)}, u32[]{:S(2)}) copy-start(f32[4,512]{1,0:T(4,128)} %egeo.1) | copy-start | bytes 24580
  1.3 15.7 %copy-start.18 = (f32[4,512]{1,0:T(4,128)S(1)}, f32[4,512]{1,0:T(4,128)}, u32[]{:S(2)}) copy-start(f32[4,512]{1,0:T(4,128)} %pgeo.1) | copy-start | bytes 24580
  1.7 23.4 %copy-start.19 = (s32[2,1024]{1,0:T(2,128)S(1)}, s32[2,1024]{1,0:T(2,128)}, u32[]{:S(2)}) copy-start(s32[2,1024]{1,0:T(2,128)} %edges.3) | copy-start | bytes 24580
  1.7 23.4 %copy-start.20 = (f32[512]{0:T(512)S(1)}, f32[512]{0:T(512)}, u32[]{:S(2)}) copy-start(f32[512]{0:T(512)} %param.44) | copy-start | bytes 6148
  1.7 14.2 %collective-permute-start.8 = (bf16[480,512]{1,0:T(8,128)(2,1)S(1)}, bf16[480,512]{1,0:T(8,128)(2,1)S(1)}, u32[]{:S(2)}, u32[]{:S(2)}) collective-permute-start(bf16[480,512]{1,0:T(8,128)(2,1)S(1)} %get-tuple-element.41), channel_id=1, source_target_pairs={{0,2},{1,3},{2,0},{3,1},{4,6},{5,7},{6,4},{7,5},{8,10},{9,11},{10,... | collective-permute-start | bytes 1474568 | tf_op jit(solution)/shard_map/ppermute | solution.py:451
  3.2 5.4 %collective-permute-start = (bf16[64,128]{1,0:T(8,128)(2,1)S(1)}, bf16[64,128]{1,0:T(8,128)(2,1)S(1)}, u32[]{:S(2)}, u32[]{:S(2)}) collective-permute-start(bf16[64,128]{1,0:T(8,128)(2,1)S(1)} %get-tuple-element.34), channel_id=1, source_target_pairs={{0,4},{4,0},{8,12},{12,8},{1,5},{5,1},{9,13},{13,9},{2,6},{6,2},{1... | collective-permute-start | bytes 49160 | tf_op jit(solution)/shard_map/ppermute | solution.py:522
  3.7 5.0 %collective-permute-start.1 = (bf16[64,128]{1,0:T(8,128)(2,1)S(1)}, bf16[64,128]{1,0:T(8,128)(2,1)S(1)}, u32[]{:S(2)}, u32[]{:S(2)}) collective-permute-start(bf16[64,128]{1,0:T(8,128)(2,1)S(1)} %get-tuple-element.35), channel_id=1, source_target_pairs={{0,8},{4,12},{8,0},{12,4},{1,9},{5,13},{9,1},{13,5},{2,10},{6,14},... | collective-permute-start | bytes 49160 | tf_op jit(solution)/shard_map/ppermute | solution.py:522
  6.3 5.6 %collective-permute-start.2 = (bf16[64,128]{1,0:T(8,128)(2,1)S(1)}, bf16[64,128]{1,0:T(8,128)(2,1)S(1)}, u32[]{:S(2)}, u32[]{:S(2)}) collective-permute-start(bf16[64,128]{1,0:T(8,128)(2,1)S(1)} %get-tuple-element.36), channel_id=1, source_target_pairs={{4,8},{8,4},{5,9},{9,5},{6,10},{10,6},{7,11},{11,7},{20,24},{24,20... | collective-permute-start | bytes 49160 | tf_op jit(solution)/shard_map/ppermute | solution.py:522
  11.9 9.5 %collective-permute-start.3 = (bf16[1216,128]{1,0:T(8,128)(2,1)S(1)}, bf16[1216,128]{1,0:T(8,128)(2,1)S(1)}, u32[]{:S(2)}, u32[]{:S(2)}) collective-permute-start(bf16[1216,128]{1,0:T(8,128)(2,1)S(1)} %shard_map.228.after.l0), channel_id=1, source_target_pairs={{0,2},{1,3},{2,0},{3,1},{4,6},{5,7},{6,4},{7,5},{8,10},{9,11},{10,... | collective-permute-start | bytes 933896 | tf_op jit(solution)/shard_map/ppermute | solution.py:451
  15.9 6.4 %collective-permute-start.9 = (bf16[256,512]{1,0:T(8,128)(2,1)S(1)}, bf16[256,512]{1,0:T(8,128)(2,1)S(1)}, u32[]{:S(2)}, u32[]{:S(2)}) collective-permute-start(bf16[256,512]{1,0:T(8,128)(2,1)S(1)} %shard_map.231.across), channel_id=1, source_target_pairs={{0,16},{16,0},{1,17},{17,1},{2,18},{18,2},{3,19},{19,3},{4,20},{20... | collective-permute-start | bytes 786440 | tf_op jit(solution)/shard_map/ppermute | solution.py:460
  16.5 7.1 %collective-permute-start.6 = (bf16[384,512]{1,0:T(8,128)(2,1)S(1)}, bf16[384,512]{1,0:T(8,128)(2,1)S(1)}, u32[]{:S(2)}, u32[]{:S(2)}) collective-permute-start(bf16[384,512]{1,0:T(8,128)(2,1)S(1)} %copy-done.2), channel_id=1, source_target_pairs={{0,1},{1,0},{2,3},{3,2},{4,5},{5,4},{6,7},{7,6},{8,9},{9,8},{10,11... | collective-permute-start | bytes 1179656 | tf_op jit(solution)/shard_map/ppermute | solution.py:455
  16.5 5.0 %collective-permute-start.7 = (bf16[128,512]{1,0:T(8,128)(2,1)S(1)}, bf16[128,512]{1,0:T(8,128)(2,1)S(1)}, u32[]{:S(2)}, u32[]{:S(2)}) collective-permute-start(bf16[128,512]{1,0:T(8,128)(2,1)S(1)} %copy-done.7), channel_id=1, source_target_pairs={{0,1},{1,0},{2,3},{3,2},{4,5},{5,4},{6,7},{7,6},{8,9},{9,8},{10,11... | collective-permute-start | bytes 393224 | tf_op jit(solution)/shard_map/ppermute | solution.py:455
  17.0 6.0 %collective-permute-start.4 = (bf16[1216,128]{1,0:T(8,128)(2,1)S(1)}, bf16[1216,128]{1,0:T(8,128)(2,1)S(1)}, u32[]{:S(2)}, u32[]{:S(2)}) collective-permute-start(bf16[1216,128]{1,0:T(8,128)(2,1)S(1)} %shard_map.228.after.l0), channel_id=1, source_target_pairs={{0,1},{1,0},{2,3},{3,2},{4,5},{5,4},{6,7},{7,6},{8,9},{9,8},{10,11... | collective-permute-start | bytes 933896 | tf_op jit(solution)/shard_map/ppermute | solution.py:455
  21.4 3.6 %collective-permute-start.5 = (bf16[1216,128]{1,0:T(8,128)(2,1)S(1)}, bf16[1216,128]{1,0:T(8,128)(2,1)S(1)}, u32[]{:S(2)}, u32[]{:S(2)}) collective-permute-start(bf16[1216,128]{1,0:T(8,128)(2,1)S(1)} %get-tuple-element.40), channel_id=1, source_target_pairs={{0,1},{1,0},{2,3},{3,2},{4,5},{5,4},{6,7},{7,6},{8,9},{9,8},{10,11... | collective-permute-start | bytes 933896 | tf_op jit(solution)/shard_map/ppermute | solution.py:455
  21.5 3.5 %collective-permute-start.10 = (bf16[256,512]{1,0:T(8,128)(2,1)S(1)}, bf16[256,512]{1,0:T(8,128)(2,1)S(1)}, u32[]{:S(2)}, u32[]{:S(2)}) collective-permute-start(bf16[256,512]{1,0:T(8,128)(2,1)S(1)} %shard_map.231.across), channel_id=1, source_target_pairs={{0,1},{1,0},{2,3},{3,2},{4,5},{5,4},{6,7},{7,6},{8,9},{9,8},{10,11... | collective-permute-start | bytes 786440 | tf_op jit(solution)/shard_map/ppermute | solution.py:455
  22.3 2.7 %collective-permute-start.11 = (bf16[256,512]{1,0:T(8,128)(2,1)S(1)}, bf16[256,512]{1,0:T(8,128)(2,1)S(1)}, u32[]{:S(2)}, u32[]{:S(2)}) collective-permute-start(bf16[256,512]{1,0:T(8,128)(2,1)S(1)} %collective-permute-done.9.round_), channel_id=1, source_target_pairs={{0,1},{1,0},{2,3},{3,2},{4,5},{5,4},{6,7},{7,6},{8,9},{9,8},{10,11... | collective-permute-start | bytes 786440 | tf_op jit(solution)/shard_map/ppermute | solution.py:455
  23.0 10.7 %collective-permute-start.15 = (bf16[384,512]{1,0:T(8,128)(2,1)S(1)}, bf16[384,512]{1,0:T(8,128)(2,1)S(1)}, u32[]{:S(2)}, u32[]{:S(2)}) collective-permute-start(bf16[384,512]{1,0:T(8,128)(2,1)S(1)} %get-tuple-element.38.node.w0), channel_id=1, source_target_pairs={{0,1},{1,0},{2,3},{3,2},{4,5},{5,4},{6,7},{7,6},{8,9},{9,8},{10,11... | collective-permute-start | bytes 1179656 | tf_op jit(solution)/shard_map/ppermute | solution.py:455
  23.6 8.0 %collective-permute-start.16 = (bf16[224,512]{1,0:T(8,128)(2,1)S(1)}, bf16[224,512]{1,0:T(8,128)(2,1)S(1)}, u32[]{:S(2)}, u32[]{:S(2)}) collective-permute-start(bf16[224,512]{1,0:T(8,128)(2,1)S(1)} %get-tuple-element.46), channel_id=1, source_target_pairs={{0,2},{1,3},{2,0},{3,1},{4,6},{5,7},{6,4},{7,5},{8,10},{9,11},{10,... | collective-permute-start | bytes 688136 | tf_op jit(solution)/shard_map/ppermute | solution.py:451
  25.1 15.3 %copy-start.3 = (bf16[256,512]{1,0:T(8,128)(2,1)S(1)}, bf16[256,512]{1,0:T(8,128)(2,1)}, u32[]{:S(2)}) copy-start(bf16[256,512]{1,0:T(8,128)(2,1)} %n_in.1) | copy-start | bytes 786436
  25.1 15.3 %copy-start.8 = (bf16[128,512]{1,0:T(8,128)(2,1)S(1)}, bf16[128,512]{1,0:T(8,128)(2,1)}, u32[]{:S(2)}) copy-start(bf16[128,512]{1,0:T(8,128)(2,1)} %n_out.3) | copy-start | bytes 393220
  25.1 15.3 %copy-start.10 = (f32[512]{0:T(512)S(1)}, f32[512]{0:T(512)}, u32[]{:S(2)}) copy-start(f32[512]{0:T(512)} %param.45) | copy-start | bytes 6148
  25.1 15.3 %copy-start.11 = (s32[1,4,32]{2,1,0:T(4,128)S(1)}, s32[1,4,32]{2,1,0:T(4,128)}, u32[]{:S(2)}) copy-start(s32[1,4,32]{2,1,0:T(4,128)} %send.3) | copy-start | bytes 1540
  29.9 1.4 %collective-permute-start.12 = (bf16[128,512]{1,0:T(8,128)(2,1)S(1)}, bf16[128,512]{1,0:T(8,128)(2,1)S(1)}, u32[]{:S(2)}, u32[]{:S(2)}) collective-permute-start(bf16[128,512]{1,0:T(8,128)(2,1)S(1)} %get-tuple-element.44), channel_id=1, source_target_pairs={{0,1},{1,0},{2,3},{3,2},{4,5},{5,4},{6,7},{7,6},{8,9},{9,8},{10,11... | collective-permute-start | bytes 393224 | tf_op jit(solution)/shard_map/ppermute | solution.py:455
  30.0 1.5 %collective-permute-start.13 = (bf16[128,512]{1,0:T(8,128)(2,1)S(1)}, bf16[128,512]{1,0:T(8,128)(2,1)S(1)}, u32[]{:S(2)}, u32[]{:S(2)}) collective-permute-start(bf16[128,512]{1,0:T(8,128)(2,1)S(1)} %get-tuple-element.45), channel_id=1, source_target_pairs={{0,1},{1,0},{2,3},{3,2},{4,5},{5,4},{6,7},{7,6},{8,9},{9,8},{10,11... | collective-permute-start | bytes 393224 | tf_op jit(solution)/shard_map/ppermute | solution.py:455
  30.5 8.3 %collective-permute-start.20 = (bf16[512,512]{1,0:T(8,128)(2,1)S(1)}, bf16[512,512]{1,0:T(8,128)(2,1)S(1)}, u32[]{:S(2)}, u32[]{:S(2)}) collective-permute-start(bf16[512,512]{1,0:T(8,128)(2,1)S(1)} %get-tuple-element.39.proc.w0), channel_id=1, source_target_pairs={{0,1},{1,0},{2,3},{3,2},{4,5},{5,4},{6,7},{7,6},{8,9},{9,8},{10,11... | collective-permute-start | bytes 1572872 | tf_op jit(solution)/shard_map/ppermute | solution.py:455
  31.6 7.2 %collective-permute-start.17 = (bf16[192,512]{1,0:T(8,128)(2,1)S(1)}, bf16[192,512]{1,0:T(8,128)(2,1)S(1)}, u32[]{:S(2)}, u32[]{:S(2)}) collective-permute-start(bf16[192,512]{1,0:T(8,128)(2,1)S(1)} %get-tuple-element.47.w2), channel_id=1, source_target_pairs={{0,4},{4,0},{8,12},{12,8},{1,5},{5,1},{9,13},{13,9},{2,6},{6,2},{1... | collective-permute-start | bytes 589832 | tf_op jit(solution)/shard_map/ppermute | solution.py:464
  32.1 8.3 %collective-permute-start.14 = (bf16[256,512]{1,0:T(8,128)(2,1)S(1)}, bf16[256,512]{1,0:T(8,128)(2,1)S(1)}, u32[]{:S(2)}, u32[]{:S(2)}) collective-permute-start(bf16[256,512]{1,0:T(8,128)(2,1)S(1)} %shard_map.233.after.mine), channel_id=1, source_target_pairs={{0,2},{1,3},{2,0},{3,1},{4,6},{5,7},{6,4},{7,5},{8,10},{9,11},{10,... | collective-permute-start | bytes 786440 | tf_op jit(solution)/shard_map/ppermute | solution.py:451
  33.2 8.5 %collective-permute-start.22 = (bf16[256,512]{1,0:T(8,128)(2,1)S(1)}, bf16[256,512]{1,0:T(8,128)(2,1)S(1)}, u32[]{:S(2)}, u32[]{:S(2)}) collective-permute-start(bf16[256,512]{1,0:T(8,128)(2,1)S(1)} %get-tuple-element.50.first), channel_id=1, source_target_pairs={{0,16},{16,0},{1,17},{17,1},{2,18},{18,2},{3,19},{19,3},{4,20},{20... | collective-permute-start | bytes 786440 | tf_op jit(solution)/shard_map/ppermute | solution.py:460
  33.7 5.1 %collective-permute-start.18 = (bf16[192,512]{1,0:T(8,128)(2,1)S(1)}, bf16[192,512]{1,0:T(8,128)(2,1)S(1)}, u32[]{:S(2)}, u32[]{:S(2)}) collective-permute-start(bf16[192,512]{1,0:T(8,128)(2,1)S(1)} %get-tuple-element.47.w2), channel_id=1, source_target_pairs={{0,1},{1,0},{2,3},{3,2},{4,5},{5,4},{6,7},{7,6},{8,9},{9,8},{10,11... | collective-permute-start | bytes 589832 | tf_op jit(solution)/shard_map/ppermute | solution.py:455
  38.8 1.6 %collective-permute-start.19 = (bf16[192,512]{1,0:T(8,128)(2,1)S(1)}, bf16[192,512]{1,0:T(8,128)(2,1)S(1)}, u32[]{:S(2)}, u32[]{:S(2)}) collective-permute-start(bf16[192,512]{1,0:T(8,128)(2,1)S(1)} %collective-permute-done.17.w3), channel_id=1, source_target_pairs={{0,1},{1,0},{2,3},{3,2},{4,5},{5,4},{6,7},{7,6},{8,9},{9,8},{10,11... | collective-permute-start | bytes 589832 | tf_op jit(solution)/shard_map/ppermute | solution.py:455
  40.4 12.0 %copy-start.16 = (s32[2,2048]{1,0:T(2,128)S(1)}, s32[2,2048]{1,0:T(2,128)}, u32[]{:S(2)}) copy-start(s32[2,2048]{1,0:T(2,128)} %edges.5) | copy-start | bytes 49156
  41.7 10.6 %collective-permute-start.23 = (bf16[512,512]{1,0:T(8,128)(2,1)S(1)}, bf16[512,512]{1,0:T(8,128)(2,1)S(1)}, u32[]{:S(2)}, u32[]{:S(2)}) collective-permute-start(bf16[512,512]{1,0:T(8,128)(2,1)S(1)} %shard_map.236.pair), channel_id=1, source_target_pairs={{0,1},{1,0},{2,3},{3,2},{4,5},{5,4},{6,7},{7,6},{8,9},{9,8},{10,11... | collective-permute-start | bytes 1572872 | tf_op jit(solution)/shard_map/ppermute | solution.py:455
  41.8 10.6 %collective-permute-start.21 = (bf16[256,512]{1,0:T(8,128)(2,1)S(1)}, bf16[256,512]{1,0:T(8,128)(2,1)S(1)}, u32[]{:S(2)}, u32[]{:S(2)}) collective-permute-start(bf16[256,512]{1,0:T(8,128)(2,1)S(1)} %get-tuple-element.48.after.mine.middle), channel_id=1, source_target_pairs={{0,1},{1,0},{2,3},{3,2},{4,5},{5,4},{6,7},{7,6},{8,9},{9,8},{10,11... | collective-permute-start | bytes 786440 | tf_op jit(solution)/shard_map/ppermute | solution.py:455
  42.3 6.9 %collective-permute-start.24 = (bf16[32,512]{1,0:T(8,128)(2,1)S(1)}, bf16[32,512]{1,0:T(8,128)(2,1)S(1)}, u32[]{:S(2)}, u32[]{:S(2)}) collective-permute-start(bf16[32,512]{1,0:T(8,128)(2,1)S(1)} %get-tuple-element.55), channel_id=1, source_target_pairs={{0,4},{4,0},{8,12},{12,8},{1,5},{5,1},{9,13},{13,9},{2,6},{6,2},{1... | collective-permute-start | bytes 98312 | tf_op jit(solution)/shard_map/ppermute | solution.py:592
  43.9 5.9 %collective-permute-start.25 = (bf16[32,512]{1,0:T(8,128)(2,1)S(1)}, bf16[32,512]{1,0:T(8,128)(2,1)S(1)}, u32[]{:S(2)}, u32[]{:S(2)}) collective-permute-start(bf16[32,512]{1,0:T(8,128)(2,1)S(1)} %get-tuple-element.56), channel_id=1, source_target_pairs={{0,8},{4,12},{8,0},{12,4},{1,9},{5,13},{9,1},{13,5},{2,10},{6,14},... | collective-permute-start | bytes 98312 | tf_op jit(solution)/shard_map/ppermute | solution.py:592
  46.5 5.8 %collective-permute-start.26 = (bf16[32,512]{1,0:T(8,128)(2,1)S(1)}, bf16[32,512]{1,0:T(8,128)(2,1)S(1)}, u32[]{:S(2)}, u32[]{:S(2)}) collective-permute-start(bf16[32,512]{1,0:T(8,128)(2,1)S(1)} %get-tuple-element.57), channel_id=1, source_target_pairs={{4,8},{8,4},{5,9},{9,5},{6,10},{10,6},{7,11},{11,7},{20,24},{24,20... | collective-permute-start | bytes 98312 | tf_op jit(solution)/shard_map/ppermute | solution.py:592
  49.2 12.0 %collective-permute-start.31 = (bf16[384,512]{1,0:T(8,128)(2,1)S(1)}, bf16[384,512]{1,0:T(8,128)(2,1)S(1)}, u32[]{:S(2)}, u32[]{:S(2)}) collective-permute-start(bf16[384,512]{1,0:T(8,128)(2,1)S(1)} %get-tuple-element.62.w0), channel_id=1, source_target_pairs={{0,2},{1,3},{2,0},{3,1},{4,6},{5,7},{6,4},{7,5},{8,10},{9,11},{10,... | collective-permute-start | bytes 1179656 | tf_op jit(solution)/shard_map/ppermute | solution.py:451
  52.3 2.7 %collective-permute-start.27 = (bf16[96,512]{1,0:T(8,128)(2,1)S(1)}, bf16[96,512]{1,0:T(8,128)(2,1)S(1)}, u32[]{:S(2)}, u32[]{:S(2)}) collective-permute-start(bf16[96,512]{1,0:T(8,128)(2,1)S(1)} %shard_map.238.halo), channel_id=1, source_target_pairs={{0,1},{1,0},{2,3},{3,2},{4,5},{5,4},{6,7},{7,6},{8,9},{9,8},{10,11... | collective-permute-start | bytes 294920 | tf_op jit(solution)/shard_map/ppermute | solution.py:455
  52.4 2.6 %copy-start.21 = (f32[512]{0:T(512)S(1)}, f32[512]{0:T(512)}, u32[]{:S(2)}) copy-start(f32[512]{0:T(512)} %param.46) | copy-start | bytes 6148
  55.0 13.2 %copy-start.12 = (f32[512]{0:T(512)S(1)}, f32[512]{0:T(512)}, u32[]{:S(2)}) copy-start(f32[512]{0:T(512)} %param.47) | copy-start | bytes 6148
  60.6 1.7 %collective-permute-start.28 = (bf16[256,512]{1,0:T(8,128)(2,1)S(1)}, bf16[256,512]{1,0:T(8,128)(2,1)S(1)}, u32[]{:S(2)}, u32[]{:S(2)}) collective-permute-start(bf16[256,512]{1,0:T(8,128)(2,1)S(1)} %get-tuple-element.59), channel_id=1, source_target_pairs={{0,1},{1,0},{2,3},{3,2},{4,5},{5,4},{6,7},{7,6},{8,9},{9,8},{10,11... | collective-permute-start | bytes 786440 | tf_op jit(solution)/shard_map/ppermute | solution.py:455
  61.2 1.8 %collective-permute-start.30 = (bf16[384,512]{1,0:T(8,128)(2,1)S(1)}, bf16[384,512]{1,0:T(8,128)(2,1)S(1)}, u32[]{:S(2)}, u32[]{:S(2)}) collective-permute-start(bf16[384,512]{1,0:T(8,128)(2,1)S(1)} %get-tuple-element.62.w0), channel_id=1, source_target_pairs={{0,1},{1,0},{2,3},{3,2},{4,5},{5,4},{6,7},{7,6},{8,9},{9,8},{10,11... | collective-permute-start | bytes 1179656 | tf_op jit(solution)/shard_map/ppermute | solution.py:455
  61.2 2.2 %collective-permute-start.32 = (bf16[384,512]{1,0:T(8,128)(2,1)S(1)}, bf16[384,512]{1,0:T(8,128)(2,1)S(1)}, u32[]{:S(2)}, u32[]{:S(2)}) collective-permute-start(bf16[384,512]{1,0:T(8,128)(2,1)S(1)} %collective-permute-done.31.w2), channel_id=1, source_target_pairs={{0,1},{1,0},{2,3},{3,2},{4,5},{5,4},{6,7},{7,6},{8,9},{9,8},{10,11... | collective-permute-start | bytes 1179656 | tf_op jit(solution)/shard_map/ppermute | solution.py:455
  62.4 5.8 %collective-permute-start.29 = (bf16[128,512]{1,0:T(8,128)(2,1)S(1)}, bf16[128,512]{1,0:T(8,128)(2,1)S(1)}, u32[]{:S(2)}, u32[]{:S(2)}) collective-permute-start(bf16[128,512]{1,0:T(8,128)(2,1)S(1)} %get-tuple-element.61), channel_id=1, source_target_pairs={{0,2},{1,3},{2,0},{3,1},{4,6},{5,7},{6,4},{7,5},{8,10},{9,11},{10,... | collective-permute-start | bytes 393224 | tf_op jit(solution)/shard_map/ppermute | solution.py:451

commit v15 on v13

--- a/solution.py
+++ b/solution.py
@@ -63,11 +63,11 @@
     return [pl.BlockSpec(memory_space=pltpu.VMEM)] * count
 
 
-def call(body, outs, args, scratch=(), flops=0, smem=0):
+def call(body, outs, args, scratch=(), flops=0):
     moved = sum(a.size * a.dtype.itemsize for a in args) + sum(
         o.size * jnp.dtype(o.dtype).itemsize for o in outs
     )
-    specs = whole_refs(len(args) - smem) + [pl.BlockSpec(memory_space=pltpu.SMEM)] * smem
+    specs = whole_refs(len(args))
     return pl.pallas_call(
         body,
         out_shape=tuple(outs),
@@ -151,7 +151,9 @@
     pick_lists(plan, grid[...], send, outs)
 
 
-def embed_kernel(e_in, e_out, p_in, p_out, egeom, egeo, pgeom, pgeo, after, node, proc, eout, pout):
+def embed_kernel(e_in, e_out, p_in, p_out, egeom, egeo, pgeom, pgeo, elive, plive, after, node, proc, eout, pout, lives):
+    lives[0:1, :] = jnp.broadcast_to(elive[...], (1, lives.shape[1]))
+    lives[1:2, :] = jnp.broadcast_to(plive[...], (1, lives.shape[1]))
     stack_into(node, (e_in, e_out))
     stack_into(proc, (p_in, p_out))
     for geom, geo, out in ((egeom, egeo, eout), (pgeom, pgeo, pout)):
@@ -312,7 +314,7 @@
         chosen = [emb[first : first + STEP, :], hot(own == senders), hot(mesh == receivers), hot(targets == senders)]
         return dot(jnp.concatenate(chosen, axis=1), table[...])
 
-    edge_blocks(edges, live[0] * BLOCK, first_stage, joined(stack, k_in, d // 4), messages, totals)
+    edge_blocks(edges, live[0:1, 0:1] * BLOCK, first_stage, joined(stack, k_in, d // 4), messages, totals)
     hand_out(totals, gain, keep, give)
 
 
@@ -405,7 +407,7 @@
             return pre[first : first + STEP, :] + remote
         return dot(own_chosen(emb, edges, lane, first), table[...]) + remote
 
-    edge_blocks(edges, live[0] * BLOCK, first_stage, w_out[...], messages, totals)
+    edge_blocks(edges, live[1:2, 0:1] * BLOCK, first_stage, w_out[...], messages, totals)
     hand_out(totals, gain, keep, give)
 
 
@@ -520,12 +522,15 @@
     lat_beside = to_core(lat)
     edge_beside = [to_core(enc_edge_in), to_core(enc_edge_out)]
     edge_round = to_group(edge_across)
-    node_w, proc_w, enc_emb, proc_emb = call(
+    node_w, proc_w, enc_emb, proc_emb, lives = call(
         embed_kernel,
-        [shape(n_in + n_out, d), shape(k_in + k_out, d), shape(n_enc, d), shape(n_proc, d)],
+        [
+            shape(n_in + n_out, d), shape(k_in + k_out, d), shape(n_enc, d), shape(n_proc, d),
+            shape(8, 128, jnp.int32),
+        ],
         [
             enc_node_in, enc_node_out, proc_edge_in, proc_edge_out,
-            enc_geom, enc_geo, proc_geom, proc_geo, lat,
+            enc_geom, enc_geo, proc_geom, proc_geo, enc_blocks.reshape(1, 1), proc_blocks.reshape(1, 1), lat,
         ],
         flops=2 * (n_enc + n_proc) * d * 128,
     )
@@ -546,7 +551,7 @@
         [
             enc_emb, enc_edges, enc_edge_gain, lat, lat_across, lat_beside, lat_both,
             enc_edge_in, enc_edge_out, *edge_beside,
-            edge_across, edge_round, to_core(edge_across), to_core(edge_round), enc_blocks,
+            edge_across, edge_round, to_core(edge_across), to_core(edge_round), lives,
         ],
         scratch=[
             pltpu.VMEM((grid_rows + mesh_rows + got, d), BF16),
@@ -556,7 +561,6 @@
             pltpu.VMEM((mesh_rows, d), F32),
         ],
         flops=2 * n_enc * d * (3 * d + grid_rows + mesh_rows + halo_rows),
-        smem=1,
     )
     (chip_sum,) = call(add_kernel, [shape(half, d)], [keep, to_core(give)])
     node_across, proc_across = call(
@@ -597,14 +601,13 @@
     keep, give = call(
         functools.partial(proc_second_kernel, plan, slots, mesh_rows),
         [shape(half, d), shape(half, d)],
-        [proc_emb, proc_edges, proc_edge_gain, table, pre, w_source, w_out, halo, halo_beside, proc_blocks],
+        [proc_emb, proc_edges, proc_edge_gain, table, pre, w_source, w_out, halo, halo_beside, lives],
         scratch=[
             pltpu.VMEM((halo_rows, d), BF16),
             pltpu.VMEM((n_proc, d), BF16),
             pltpu.VMEM((mesh_rows, d), F32),
         ],
         flops=2 * n_proc * d * (2 * d + mesh_rows + halo_rows),
-        smem=1,
     )
     quarter = mesh_rows // 4
     mine, other = call(fold_kernel, [shape(quarter, d)] * 2, [keep, to_core(give)])

time: 68.6 us -> 67.9 us (0.990)
  waiting for transfers between devices: 22.3 us -> 21.4 us
    ppermute x6, waiting for transfers between devices: 12.2 us -> 10.2 us  [to_chip(): return lax.ppermute(v, 'sub', [(i, i ^ 2) for i in range(4)])]
  transfers between devices with their start and end apart: 32 -> 32, of which waited for: 10 -> 11; matrix products, arithmetic and copies ran while one was open for 0% -> 0% of each run, Pallas kernels for 24% -> 24%
where the time goes in v15:
time: 67.9 us; the launch traced here: 67.8 us
  starting transfers between devices  25.2 us (37%)
  waiting for transfers between devices  21.4 us (32%)
  Pallas kernels  18.2 us (27%)
  between operations  1.73 us (3%)
  local copies, waits for them, and re-layouts  1.27 us (2%)
    pallas_call x16, Pallas kernels, call(): pl.pallas_call(body, out_shape=tuple(outs), in_specs=specs, out_specs=tup...  18.2 us
    ppermute x6, starting transfers between devices, local(): lax.ppermute(v, 'dom', entry[0])  11.6 us
    ppermute x6, waiting for transfers between devices, to_chip(): return lax.ppermute(v, 'sub', [(i, i ^ 2) for i in range(4)])  10.2 us
    ppermute x6, starting transfers between devices, to_chip(): return lax.ppermute(v, 'sub', [(i, i ^ 2) for i in range(4)])  8.15 us
    ppermute x6, waiting for transfers between devices, local(): lax.ppermute(v, 'dom', entry[0])  5.38 us
    ppermute x1, waiting for transfers between devices, to_partition(): lax.ppermute(v, 'dom', [(i, i ^ 1) for i in range(lax.axis_size('dom'))])  3.83 us
    ppermute x17, starting transfers between devices, to_core(): return lax.ppermute(v, 'sub', [(i, i ^ 1) for i in range(4)])  3.63 us
    ppermute x17, waiting for transfers between devices, to_core(): return lax.ppermute(v, 'sub', [(i, i ^ 1) for i in range(4)])  1.95 us
  transfers between devices with their start and end apart: 32, of which 11 were waited for; matrix products, arithmetic and copies ran while one was open for 0% of the time, Pallas kernels for 24%

profile of v15, /device:TPU:12, one launch (start us, length us, event | category | flops | bytes accessed | tf_op | source)
XLA Modules:
  0.0 67.8 jit_solution(17592278682730224716)
XLA Ops:
  0.1 0.8 %copy-done.4 = bf16[128,512]{1,0:T(8,128)(2,1)S(1)} copy-done((bf16[128,512]{1,0:T(8,128)(2,1)S(1)}, bf16[128,512]{1,0:T(8,128)(2,1)}, u32[]{:S(2)}) %copy-start.4) | copy-done | bytes 131096
  0.9 0.1 copy-done.5
  1.0 0.1 copy-done
  1.0 0.2 copy-done.1
  1.2 0.0 copy-done.6
  1.3 0.0 copy-start.17
  1.3 0.0 copy-start.18
  1.3 0.3 shard_map.227
  1.6 0.0 copy-start.19
  1.6 0.0 copy-start.20
  1.6 1.6 %collective-permute-start.8 = (bf16[384,512]{1,0:T(8,128)(2,1)S(1)}, bf16[384,512]{1,0:T(8,128)(2,1)S(1)}, u32[]{:S(2)}, u32[]{:S(2)}) collective-permute-start(bf16[384,512]{1,0:T(8,128)(2,1)S(1)} %get-tuple-element.41), channel_id=1, source_target_pairs={{0,2},{1,3},{2,0},{3,1},{4,6},{5,7},{6,4},{7,5},{8,10},{9,11},{10,... | collective-permute-start | bytes 1179656 | tf_op jit(solution)/shard_map/ppermute | solution.py:444
  3.2 0.5 collective-permute-start
  3.6 2.6 %collective-permute-start.1 = (bf16[64,128]{1,0:T(8,128)(2,1)S(1)}, bf16[64,128]{1,0:T(8,128)(2,1)S(1)}, u32[]{:S(2)}, u32[]{:S(2)}) collective-permute-start(bf16[64,128]{1,0:T(8,128)(2,1)S(1)} %get-tuple-element.35), channel_id=1, source_target_pairs={{0,8},{4,12},{8,0},{12,4},{1,9},{5,13},{9,1},{13,5},{2,10},{6,14},... | collective-permute-start | bytes 49160 | tf_op jit(solution)/shard_map/ppermute | solution.py:514
  6.2 2.3 %collective-permute-start.2 = (bf16[64,128]{1,0:T(8,128)(2,1)S(1)}, bf16[64,128]{1,0:T(8,128)(2,1)S(1)}, u32[]{:S(2)}, u32[]{:S(2)}) collective-permute-start(bf16[64,128]{1,0:T(8,128)(2,1)S(1)} %get-tuple-element.36), channel_id=1, source_target_pairs={{4,8},{8,4},{5,9},{9,5},{6,10},{10,6},{7,11},{11,7},{20,24},{24,20... | collective-permute-start | bytes 49160 | tf_op jit(solution)/shard_map/ppermute | solution.py:514
  8.6 0.0 collective-permute-done.refs_2_
  8.6 3.2 %collective-permute-done.2.refs_4_ = bf16[64,128]{1,0:T(8,128)(2,1)S(1)} collective-permute-done((bf16[64,128]{1,0:T(8,128)(2,1)S(1)}, bf16[64,128]{1,0:T(8,128)(2,1)S(1)}, u32[]{:S(2)}, u32[]{:S(2)}) %collective-permute-start.2) | collective-permute-done | bytes 16416 | tf_op jit(solution)/shard_map/ppermute | solution.py:514
  11.9 0.6 collective-permute-start.3
  12.5 0.1 collective-permute-done.8.source.early
  12.6 0.6 collective-permute-start.9
  13.1 0.5 collective-permute-start.7
  14.9 0.1 collective-permute-start.4
  15.1 1.8 %shard_map.229 = (bf16[384,512]{1,0:T(8,128)(2,1)S(1)}, bf16[512,512]{1,0:T(8,128)(2,1)S(1)}, bf16[1024,512]{1,0:T(8,128)(2,1)S(1)}, bf16[2048,512]{1,0:T(8,128)(2,1)S(1)}, s32[8,128]{1,0:T(8,128)S(1)}) custom-call(bf16[256,512]{1,0:T(8,128)(2,1)S(1)} %copy-done.13, bf16[128,512]{1,0:T(8,128)(2,1)S(1)} %copy-done.4, bf16[384,512]{1,0:T(8,128)(2,1)S(1)} %copy-done.12, ...), custom_call_target="tpu_custom_call" | custom-call | flops 402653184 | bytes 5361672 | tf_op jit(solution)/shard_map/pallas_call | solution.py:71
  16.9 2.4 %collective-permute-done.3.lat.l1 = bf16[1216,128]{1,0:T(8,128)(2,1)S(1)} collective-permute-done((bf16[1216,128]{1,0:T(8,128)(2,1)S(1)}, bf16[1216,128]{1,0:T(8,128)(2,1)S(1)}, u32[]{:S(2)}, u32[]{:S(2)}) %collective-permute-start.3) | collective-permute-done | bytes 311328 | tf_op jit(solution)/shard_map/ppermute | solution.py:444
  19.4 0.1 collective-permute-start.5
  19.5 0.5 collective-permute-start.10
  20.0 0.1 collective-permute-start.11
  20.1 1.4 %collective-permute-start.15 = (bf16[320,512]{1,0:T(8,128)(2,1)S(1)}, bf16[320,512]{1,0:T(8,128)(2,1)S(1)}, u32[]{:S(2)}, u32[]{:S(2)}) collective-permute-start(bf16[320,512]{1,0:T(8,128)(2,1)S(1)} %get-tuple-element.46), channel_id=1, source_target_pairs={{0,2},{1,3},{2,0},{3,1},{4,6},{5,7},{6,4},{7,5},{8,10},{9,11},{10,... | collective-permute-start | bytes 983048 | tf_op jit(solution)/shard_map/ppermute | solution.py:444
  21.4 0.4 collective-permute-done.11.round_both
  21.8 0.0 copy-start.9
  21.8 0.0 copy-start.10
  21.8 4.9 %shard_map.232 = (bf16[256,512]{1,0:T(8,128)(2,1)S(1)}, bf16[256,512]{1,0:T(8,128)(2,1)S(1)}, bf16[256,512]{1,0:T(8,128)(2,1)S(1)}) custom-call(bf16[1024,512]{1,0:T(8,128)(2,1)S(1)} %get-tuple-element.37.emb, s32[2,1024]{1,0:T(2,128)S(1)} %copy-done.19, f32[1,512]{1,0:T(1,128)S(1)} %bitcast.10, bf16[1216,128]{1,0:T(8,128)(2,1)S(1)} %shard_map.228.after.l0, ...), custom_call_target="tpu_custom_call" | custom-call | flops 2952790016 | bytes 5191680 | tf_op jit(solution)/shard_map/pallas_call | solution.py:71
  26.8 0.2 collective-permute-start.12
  27.0 0.4 collective-permute-start.14
  27.3 0.1 collective-permute-start.19
  27.5 0.9 %collective-permute-done.12.theirs = bf16[256,512]{1,0:T(8,128)(2,1)S(1)} collective-permute-done((bf16[256,512]{1,0:T(8,128)(2,1)S(1)}, bf16[256,512]{1,0:T(8,128)(2,1)S(1)}, u32[]{:S(2)}, u32[]{:S(2)}) %collective-permute-start.12) | collective-permute-done | bytes 262176 | tf_op jit(solution)/shard_map/ppermute | solution.py:448
  28.4 0.1 shard_map.233.after.mine
  28.4 1.7 %collective-permute-done.15.source = bf16[320,512]{1,0:T(8,128)(2,1)S(1)} collective-permute-done((bf16[320,512]{1,0:T(8,128)(2,1)S(1)}, bf16[320,512]{1,0:T(8,128)(2,1)S(1)}, u32[]{:S(2)}, u32[]{:S(2)}) %collective-permute-start.15) | collective-permute-done | bytes 327712 | tf_op jit(solution)/shard_map/ppermute | solution.py:444
  30.2 0.7 %collective-permute-start.16 = (bf16[192,512]{1,0:T(8,128)(2,1)S(1)}, bf16[192,512]{1,0:T(8,128)(2,1)S(1)}, u32[]{:S(2)}, u32[]{:S(2)}) collective-permute-start(bf16[192,512]{1,0:T(8,128)(2,1)S(1)} %get-tuple-element.47.w2), channel_id=1, source_target_pairs={{0,4},{4,0},{8,12},{12,8},{1,5},{5,1},{9,13},{13,9},{2,6},{6,2},{1... | collective-permute-start | bytes 589832 | tf_op jit(solution)/shard_map/ppermute | solution.py:457
  30.8 1.5 %collective-permute-start.13 = (bf16[256,512]{1,0:T(8,128)(2,1)S(1)}, bf16[256,512]{1,0:T(8,128)(2,1)S(1)}, u32[]{:S(2)}, u32[]{:S(2)}) collective-permute-start(bf16[256,512]{1,0:T(8,128)(2,1)S(1)} %shard_map.233.after.mine), channel_id=1, source_target_pairs={{0,2},{1,3},{2,0},{3,1},{4,6},{5,7},{6,4},{7,5},{8,10},{9,11},{10,... | collective-permute-start | bytes 786440 | tf_op jit(solution)/shard_map/ppermute | solution.py:444
  32.3 0.5 collective-permute-start.21
  32.8 3.8 %collective-permute-done.16.w3 = bf16[192,512]{1,0:T(8,128)(2,1)S(1)} collective-permute-done((bf16[192,512]{1,0:T(8,128)(2,1)S(1)}, bf16[192,512]{1,0:T(8,128)(2,1)S(1)}, u32[]{:S(2)}, u32[]{:S(2)}) %collective-permute-start.16) | collective-permute-done | bytes 196640 | tf_op jit(solution)/shard_map/ppermute | solution.py:457
  36.7 1.8 %collective-permute-done.13.theirs = bf16[256,512]{1,0:T(8,128)(2,1)S(1)} collective-permute-done((bf16[256,512]{1,0:T(8,128)(2,1)S(1)}, bf16[256,512]{1,0:T(8,128)(2,1)S(1)}, u32[]{:S(2)}, u32[]{:S(2)}) %collective-permute-start.13) | collective-permute-done | bytes 262176 | tf_op jit(solution)/shard_map/ppermute | solution.py:444
  38.5 0.0 copy-start.16
  38.5 1.2 %shard_map.235 = (bf16[256,512]{1,0:T(8,128)(2,1)S(1)}, bf16[384,512]{1,0:T(8,128)(2,1)S(1)}, bf16[32,512]{1,0:T(8,128)(2,1)S(1)}, bf16[32,512]{1,0:T(8,128)(2,1)S(1)}, bf16[32,512]{1,0:T(8,128)(2,1)S(1)}) custom-call(bf16[256,512]{1,0:T(8,128)(2,1)S(1)} %get-tuple-element.43.mesh, bf16[256,512]{1,0:T(8,128)(2,1)S(1)} %shard_map.233.after.mine, ...), custom_call_target="tpu_custom_call" | custom-call | flops 402653184 | bytes 4033024 | tf_op jit(solution)/shard_map/pallas_call | solution.py:71
  39.8 0.1 collective-permute-start.22
  39.9 0.5 collective-permute-start.20
  40.4 1.3 %collective-permute-start.23 = (bf16[32,512]{1,0:T(8,128)(2,1)S(1)}, bf16[32,512]{1,0:T(8,128)(2,1)S(1)}, u32[]{:S(2)}, u32[]{:S(2)}) collective-permute-start(bf16[32,512]{1,0:T(8,128)(2,1)S(1)} %get-tuple-element.55), channel_id=1, source_target_pairs={{0,4},{4,0},{8,12},{12,8},{1,5},{5,1},{9,13},{13,9},{2,6},{6,2},{1... | collective-permute-start | bytes 98312 | tf_op jit(solution)/shard_map/ppermute | solution.py:586
  41.7 2.8 %collective-permute-start.24 = (bf16[32,512]{1,0:T(8,128)(2,1)S(1)}, bf16[32,512]{1,0:T(8,128)(2,1)S(1)}, u32[]{:S(2)}, u32[]{:S(2)}) collective-permute-start(bf16[32,512]{1,0:T(8,128)(2,1)S(1)} %get-tuple-element.56), channel_id=1, source_target_pairs={{0,8},{4,12},{8,0},{12,4},{1,9},{5,13},{9,1},{13,5},{2,10},{6,14},... | collective-permute-start | bytes 98312 | tf_op jit(solution)/shard_map/ppermute | solution.py:586
  44.6 2.1 %collective-permute-start.25 = (bf16[32,512]{1,0:T(8,128)(2,1)S(1)}, bf16[32,512]{1,0:T(8,128)(2,1)S(1)}, u32[]{:S(2)}, u32[]{:S(2)}) collective-permute-start(bf16[32,512]{1,0:T(8,128)(2,1)S(1)} %get-tuple-element.57), channel_id=1, source_target_pairs={{4,8},{8,4},{5,9},{9,5},{6,10},{10,6},{7,11},{11,7},{20,24},{24,20... | collective-permute-start | bytes 98312 | tf_op jit(solution)/shard_map/ppermute | solution.py:586
  46.7 1.6 %collective-permute-start.30 = (bf16[384,512]{1,0:T(8,128)(2,1)S(1)}, bf16[384,512]{1,0:T(8,128)(2,1)S(1)}, u32[]{:S(2)}, u32[]{:S(2)}) collective-permute-start(bf16[384,512]{1,0:T(8,128)(2,1)S(1)} %get-tuple-element.62.w0), channel_id=1, source_target_pairs={{0,2},{1,3},{2,0},{3,1},{4,6},{5,7},{6,4},{7,5},{8,10},{9,11},{10,... | collective-permute-start | bytes 1179656 | tf_op jit(solution)/shard_map/ppermute | solution.py:444
  48.2 2.1 %collective-permute-done.25.refs_2_ = bf16[32,512]{1,0:T(8,128)(2,1)S(1)} collective-permute-done((bf16[32,512]{1,0:T(8,128)(2,1)S(1)}, bf16[32,512]{1,0:T(8,128)(2,1)S(1)}, u32[]{:S(2)}, u32[]{:S(2)}) %collective-permute-start.25) | collective-permute-done | bytes 32800 | tf_op jit(solution)/shard_map/ppermute | solution.py:586
  50.4 0.1 collective-permute-start.26
  50.5 0.0 copy-start.21
  50.5 2.6 %shard_map.237 = (bf16[1536,512]{1,0:T(8,128)(2,1)S(1)}, f32[1024,512]{1,0:T(8,128)S(1)}, bf16[512,512]{1,0:T(8,128)(2,1)S(1)}, bf16[512,512]{1,0:T(8,128)(2,1)S(1)}) custom-call(bf16[2048,512]{1,0:T(8,128)(2,1)S(1)} %get-tuple-element.49.emb, bf16[256,512]{1,0:T(8,128)(2,1)S(1)} %get-tuple-element.48.after.mine.middle, ...), custom_call_target="tpu_custom_call" | custom-call | flops 1610612736 | bytes 9453568 | tf_op jit(solution)/shard_map/pallas_call | solution.py:71
  53.1 0.0 copy-start.11
  53.1 5.6 %shard_map.239 = (bf16[256,512]{1,0:T(8,128)(2,1)S(1)}, bf16[256,512]{1,0:T(8,128)(2,1)S(1)}) custom-call(bf16[2048,512]{1,0:T(8,128)(2,1)S(1)} %get-tuple-element.49.emb, s32[2,2048]{1,0:T(2,128)S(1)} %copy-done.16, f32[1,512]{1,0:T(1,128)S(1)} %bitcast.11, bf16[1536,512]{1,0:T(8,128)(2,1)S(1)} %get-tuple-element.51.table, ...), custom_call_target="tpu_custom_call" | custom-call | flops 3489660928 | bytes 7559168 | tf_op jit(solution)/shard_map/pallas_call | solution.py:71
  58.8 0.5 collective-permute-start.27
  59.3 0.1 collective-permute-start.29
  59.4 0.4 collective-permute-start.31
  59.8 0.6 collective-permute-done.27.theirs
  60.5 0.1 shard_map.240
  60.5 1.6 %collective-permute-start.28 = (bf16[128,512]{1,0:T(8,128)(2,1)S(1)}, bf16[128,512]{1,0:T(8,128)(2,1)S(1)}, u32[]{:S(2)}, u32[]{:S(2)}) collective-permute-start(bf16[128,512]{1,0:T(8,128)(2,1)S(1)} %get-tuple-element.61), channel_id=1, source_target_pairs={{0,2},{1,3},{2,0},{3,1},{4,6},{5,7},{6,4},{7,5},{8,10},{9,11},{10,... | collective-permute-start | bytes 393224 | tf_op jit(solution)/shard_map/ppermute | solution.py:444
  62.1 4.3 %collective-permute-done.28.theirs = bf16[128,512]{1,0:T(8,128)(2,1)S(1)} collective-permute-done((bf16[128,512]{1,0:T(8,128)(2,1)S(1)}, bf16[128,512]{1,0:T(8,128)(2,1)S(1)}, u32[]{:S(2)}, u32[]{:S(2)}) %collective-permute-start.28) | collective-permute-done | bytes 131104 | tf_op jit(solution)/shard_map/ppermute | solution.py:444
  66.4 1.4 %shard_map.241 = bf16[128,512]{1,0:T(8,128)(2,1)} custom-call(bf16[256,512]{1,0:T(8,128)(2,1)S(1)} %get-tuple-element.48.after.mine.middle, bf16[128,512]{1,0:T(8,128)(2,1)S(1)} %get-tuple-element.60.mine, bf16[128,512]{1,0:T(8,128)(2,1)S(1)} %collective-permute-done.28.theirs, f32[1,512]{1,0:T(1,128)S(1)} %bitcast.9, ...), custom_call_target="tpu_custom_call" | custom-call | flops 201326592 | bytes 2230272 | tf_op jit(solution)/shard_map/pallas_call | solution.py:71
  (60 shorter events, 0.3 us)
Async XLA Ops:
  0.0 0.9 %copy-start.4 = (bf16[128,512]{1,0:T(8,128)(2,1)S(1)}, bf16[128,512]{1,0:T(8,128)(2,1)}, u32[]{:S(2)}) copy-start(bf16[128,512]{1,0:T(8,128)(2,1)} %e_out.1) | copy-start | bytes 393220
  0.0 1.0 %copy-start.5 = (bf16[128,512]{1,0:T(8,128)(2,1)S(1)}, bf16[128,512]{1,0:T(8,128)(2,1)}, u32[]{:S(2)}) copy-start(bf16[128,512]{1,0:T(8,128)(2,1)} %p_out.3) | copy-start | bytes 393220
  0.0 1.0 %copy-start = (bf16[512,128]{1,0:T(8,128)(2,1)S(1)}, bf16[512,128]{1,0:T(8,128)(2,1)}, u32[]{:S(2)}) copy-start(bf16[512,128]{1,0:T(8,128)(2,1)} %refs_0_.1) | copy-start | bytes 393220
  0.0 1.0 %copy-start.8 = (s32[1,4,64]{2,1,0:T(4,128)S(1)}, s32[1,4,64]{2,1,0:T(4,128)}, u32[]{:S(2)}) copy-start(s32[1,4,64]{2,1,0:T(4,128)} %send.2) | copy-start | bytes 3076
  0.0 1.2 %copy-start.1 = (bf16[384,512]{1,0:T(8,128)(2,1)S(1)}, bf16[384,512]{1,0:T(8,128)(2,1)}, u32[]{:S(2)}) copy-start(bf16[384,512]{1,0:T(8,128)(2,1)} %o_in.1) | copy-start | bytes 1179652
  0.0 1.2 %copy-start.6 = (bf16[128,512]{1,0:T(8,128)(2,1)S(1)}, bf16[128,512]{1,0:T(8,128)(2,1)}, u32[]{:S(2)}) copy-start(bf16[128,512]{1,0:T(8,128)(2,1)} %o_out.1) | copy-start | bytes 393220
  0.0 11.8 %copy-start.3 = (bf16[512,128]{1,0:T(8,128)(2,1)S(1)}, bf16[512,128]{1,0:T(8,128)(2,1)}, u32[]{:S(2)}) copy-start(bf16[512,128]{1,0:T(8,128)(2,1)} %refs_1_.1) | copy-start | bytes 393220
  1.2 13.8 %copy-start.12 = (bf16[384,512]{1,0:T(8,128)(2,1)S(1)}, bf16[384,512]{1,0:T(8,128)(2,1)}, u32[]{:S(2)}) copy-start(bf16[384,512]{1,0:T(8,128)(2,1)} %p_in.1) | copy-start | bytes 1179652
  1.2 13.8 %copy-start.13 = (bf16[256,512]{1,0:T(8,128)(2,1)S(1)}, bf16[256,512]{1,0:T(8,128)(2,1)}, u32[]{:S(2)}) copy-start(bf16[256,512]{1,0:T(8,128)(2,1)} %e_in.1) | copy-start | bytes 786436
  1.2 13.8 %copy-start.14 = (f32[4,2048]{1,0:T(4,128)S(1)}, f32[4,2048]{1,0:T(4,128)}, u32[]{:S(2)}) copy-start(f32[4,2048]{1,0:T(4,128)} %pgeom.1) | copy-start | bytes 98308
  1.2 13.8 %copy-start.15 = (f32[4,1024]{1,0:T(4,128)S(1)}, f32[4,1024]{1,0:T(4,128)}, u32[]{:S(2)}) copy-start(f32[4,1024]{1,0:T(4,128)} %egeom.1) | copy-start | bytes 49156
  1.3 13.8 %copy-start.17 = (f32[4,512]{1,0:T(4,128)S(1)}, f32[4,512]{1,0:T(4,128)}, u32[]{:S(2)}) copy-start(f32[4,512]{1,0:T(4,128)} %egeo.1) | copy-start | bytes 24580
  1.3 13.8 %copy-start.18 = (f32[4,512]{1,0:T(4,128)S(1)}, f32[4,512]{1,0:T(4,128)}, u32[]{:S(2)}) copy-start(f32[4,512]{1,0:T(4,128)} %pgeo.1) | copy-start | bytes 24580
  1.6 20.2 %copy-start.19 = (s32[2,1024]{1,0:T(2,128)S(1)}, s32[2,1024]{1,0:T(2,128)}, u32[]{:S(2)}) copy-start(s32[2,1024]{1,0:T(2,128)} %edges.3) | copy-start | bytes 24580
  1.6 20.2 %copy-start.20 = (f32[512]{0:T(512)S(1)}, f32[512]{0:T(512)}, u32[]{:S(2)}) copy-start(f32[512]{0:T(512)} %param.44) | copy-start | bytes 6148
  1.6 10.9 %collective-permute-start.8 = (bf16[384,512]{1,0:T(8,128)(2,1)S(1)}, bf16[384,512]{1,0:T(8,128)(2,1)S(1)}, u32[]{:S(2)}, u32[]{:S(2)}) collective-permute-start(bf16[384,512]{1,0:T(8,128)(2,1)S(1)} %get-tuple-element.41), channel_id=1, source_target_pairs={{0,2},{1,3},{2,0},{3,1},{4,6},{5,7},{6,4},{7,5},{8,10},{9,11},{10,... | collective-permute-start | bytes 1179656 | tf_op jit(solution)/shard_map/ppermute | solution.py:444
  3.2 5.4 %collective-permute-start = (bf16[64,128]{1,0:T(8,128)(2,1)S(1)}, bf16[64,128]{1,0:T(8,128)(2,1)S(1)}, u32[]{:S(2)}, u32[]{:S(2)}) collective-permute-start(bf16[64,128]{1,0:T(8,128)(2,1)S(1)} %get-tuple-element.34), channel_id=1, source_target_pairs={{0,4},{4,0},{8,12},{12,8},{1,5},{5,1},{9,13},{13,9},{2,6},{6,2},{1... | collective-permute-start | bytes 49160 | tf_op jit(solution)/shard_map/ppermute | solution.py:514
  3.6 5.0 %collective-permute-start.1 = (bf16[64,128]{1,0:T(8,128)(2,1)S(1)}, bf16[64,128]{1,0:T(8,128)(2,1)S(1)}, u32[]{:S(2)}, u32[]{:S(2)}) collective-permute-start(bf16[64,128]{1,0:T(8,128)(2,1)S(1)} %get-tuple-element.35), channel_id=1, source_target_pairs={{0,8},{4,12},{8,0},{12,4},{1,9},{5,13},{9,1},{13,5},{2,10},{6,14},... | collective-permute-start | bytes 49160 | tf_op jit(solution)/shard_map/ppermute | solution.py:514
  6.2 5.6 %collective-permute-start.2 = (bf16[64,128]{1,0:T(8,128)(2,1)S(1)}, bf16[64,128]{1,0:T(8,128)(2,1)S(1)}, u32[]{:S(2)}, u32[]{:S(2)}) collective-permute-start(bf16[64,128]{1,0:T(8,128)(2,1)S(1)} %get-tuple-element.36), channel_id=1, source_target_pairs={{4,8},{8,4},{5,9},{9,5},{6,10},{10,6},{7,11},{11,7},{20,24},{24,20... | collective-permute-start | bytes 49160 | tf_op jit(solution)/shard_map/ppermute | solution.py:514
  11.9 7.5 %collective-permute-start.3 = (bf16[1216,128]{1,0:T(8,128)(2,1)S(1)}, bf16[1216,128]{1,0:T(8,128)(2,1)S(1)}, u32[]{:S(2)}, u32[]{:S(2)}) collective-permute-start(bf16[1216,128]{1,0:T(8,128)(2,1)S(1)} %shard_map.228.after.l0), channel_id=1, source_target_pairs={{0,2},{1,3},{2,0},{3,1},{4,6},{5,7},{6,4},{7,5},{8,10},{9,11},{10,... | collective-permute-start | bytes 933896 | tf_op jit(solution)/shard_map/ppermute | solution.py:444
  12.6 7.4 %collective-permute-start.9 = (bf16[256,512]{1,0:T(8,128)(2,1)S(1)}, bf16[256,512]{1,0:T(8,128)(2,1)S(1)}, u32[]{:S(2)}, u32[]{:S(2)}) collective-permute-start(bf16[256,512]{1,0:T(8,128)(2,1)S(1)} %shard_map.231.across), channel_id=1, source_target_pairs={{0,16},{16,0},{1,17},{17,1},{2,18},{18,2},{3,19},{19,3},{4,20},{20... | collective-permute-start | bytes 786440 | tf_op jit(solution)/shard_map/ppermute | solution.py:453
  13.1 8.3 %collective-permute-start.6 = (bf16[384,512]{1,0:T(8,128)(2,1)S(1)}, bf16[384,512]{1,0:T(8,128)(2,1)S(1)}, u32[]{:S(2)}, u32[]{:S(2)}) collective-permute-start(bf16[384,512]{1,0:T(8,128)(2,1)S(1)} %copy-done.1), channel_id=1, source_target_pairs={{0,1},{1,0},{2,3},{3,2},{4,5},{5,4},{6,7},{7,6},{8,9},{9,8},{10,11... | collective-permute-start | bytes 1179656 | tf_op jit(solution)/shard_map/ppermute | solution.py:448
  13.1 6.3 %collective-permute-start.7 = (bf16[128,512]{1,0:T(8,128)(2,1)S(1)}, bf16[128,512]{1,0:T(8,128)(2,1)S(1)}, u32[]{:S(2)}, u32[]{:S(2)}) collective-permute-start(bf16[128,512]{1,0:T(8,128)(2,1)S(1)} %copy-done.6), channel_id=1, source_target_pairs={{0,1},{1,0},{2,3},{3,2},{4,5},{5,4},{6,7},{7,6},{8,9},{9,8},{10,11... | collective-permute-start | bytes 393224 | tf_op jit(solution)/shard_map/ppermute | solution.py:448
  14.9 5.1 %collective-permute-start.4 = (bf16[1216,128]{1,0:T(8,128)(2,1)S(1)}, bf16[1216,128]{1,0:T(8,128)(2,1)S(1)}, u32[]{:S(2)}, u32[]{:S(2)}) collective-permute-start(bf16[1216,128]{1,0:T(8,128)(2,1)S(1)} %shard_map.228.after.l0), channel_id=1, source_target_pairs={{0,1},{1,0},{2,3},{3,2},{4,5},{5,4},{6,7},{7,6},{8,9},{9,8},{10,11... | collective-permute-start | bytes 933896 | tf_op jit(solution)/shard_map/ppermute | solution.py:448
  19.4 2.0 %collective-permute-start.5 = (bf16[1216,128]{1,0:T(8,128)(2,1)S(1)}, bf16[1216,128]{1,0:T(8,128)(2,1)S(1)}, u32[]{:S(2)}, u32[]{:S(2)}) collective-permute-start(bf16[1216,128]{1,0:T(8,128)(2,1)S(1)} %get-tuple-element.40), channel_id=1, source_target_pairs={{0,1},{1,0},{2,3},{3,2},{4,5},{5,4},{6,7},{7,6},{8,9},{9,8},{10,11... | collective-permute-start | bytes 933896 | tf_op jit(solution)/shard_map/ppermute | solution.py:448
  19.5 2.0 %collective-permute-start.10 = (bf16[256,512]{1,0:T(8,128)(2,1)S(1)}, bf16[256,512]{1,0:T(8,128)(2,1)S(1)}, u32[]{:S(2)}, u32[]{:S(2)}) collective-permute-start(bf16[256,512]{1,0:T(8,128)(2,1)S(1)} %shard_map.231.across), channel_id=1, source_target_pairs={{0,1},{1,0},{2,3},{3,2},{4,5},{5,4},{6,7},{7,6},{8,9},{9,8},{10,11... | collective-permute-start | bytes 786440 | tf_op jit(solution)/shard_map/ppermute | solution.py:448
  20.0 1.8 %collective-permute-start.11 = (bf16[256,512]{1,0:T(8,128)(2,1)S(1)}, bf16[256,512]{1,0:T(8,128)(2,1)S(1)}, u32[]{:S(2)}, u32[]{:S(2)}) collective-permute-start(bf16[256,512]{1,0:T(8,128)(2,1)S(1)} %collective-permute-done.9.round_), channel_id=1, source_target_pairs={{0,1},{1,0},{2,3},{3,2},{4,5},{5,4},{6,7},{7,6},{8,9},{9,8},{10,11... | collective-permute-start | bytes 786440 | tf_op jit(solution)/shard_map/ppermute | solution.py:448
  20.1 10.1 %collective-permute-start.15 = (bf16[320,512]{1,0:T(8,128)(2,1)S(1)}, bf16[320,512]{1,0:T(8,128)(2,1)S(1)}, u32[]{:S(2)}, u32[]{:S(2)}) collective-permute-start(bf16[320,512]{1,0:T(8,128)(2,1)S(1)} %get-tuple-element.46), channel_id=1, source_target_pairs={{0,2},{1,3},{2,0},{3,1},{4,6},{5,7},{6,4},{7,5},{8,10},{9,11},{10,... | collective-permute-start | bytes 983048 | tf_op jit(solution)/shard_map/ppermute | solution.py:444
  21.8 16.7 %copy-start.2 = (bf16[256,512]{1,0:T(8,128)(2,1)S(1)}, bf16[256,512]{1,0:T(8,128)(2,1)}, u32[]{:S(2)}) copy-start(bf16[256,512]{1,0:T(8,128)(2,1)} %n_in.1) | copy-start | bytes 786436
  21.8 16.7 %copy-start.7 = (bf16[128,512]{1,0:T(8,128)(2,1)S(1)}, bf16[128,512]{1,0:T(8,128)(2,1)}, u32[]{:S(2)}) copy-start(bf16[128,512]{1,0:T(8,128)(2,1)} %n_out.3) | copy-start | bytes 393220
  21.8 16.7 %copy-start.9 = (f32[512]{0:T(512)S(1)}, f32[512]{0:T(512)}, u32[]{:S(2)}) copy-start(f32[512]{0:T(512)} %param.45) | copy-start | bytes 6148
  21.8 16.7 %copy-start.10 = (s32[1,4,32]{2,1,0:T(4,128)S(1)}, s32[1,4,32]{2,1,0:T(4,128)}, u32[]{:S(2)}) copy-start(s32[1,4,32]{2,1,0:T(4,128)} %send.3) | copy-start | bytes 1540
  26.8 1.6 %collective-permute-start.12 = (bf16[256,512]{1,0:T(8,128)(2,1)S(1)}, bf16[256,512]{1,0:T(8,128)(2,1)S(1)}, u32[]{:S(2)}, u32[]{:S(2)}) collective-permute-start(bf16[256,512]{1,0:T(8,128)(2,1)S(1)} %get-tuple-element.45), channel_id=1, source_target_pairs={{0,1},{1,0},{2,3},{3,2},{4,5},{5,4},{6,7},{7,6},{8,9},{9,8},{10,11... | collective-permute-start | bytes 786440 | tf_op jit(solution)/shard_map/ppermute | solution.py:448
  27.0 5.9 %collective-permute-start.14 = (bf16[384,512]{1,0:T(8,128)(2,1)S(1)}, bf16[384,512]{1,0:T(8,128)(2,1)S(1)}, u32[]{:S(2)}, u32[]{:S(2)}) collective-permute-start(bf16[384,512]{1,0:T(8,128)(2,1)S(1)} %get-tuple-element.38.node.w0), channel_id=1, source_target_pairs={{0,1},{1,0},{2,3},{3,2},{4,5},{5,4},{6,7},{7,6},{8,9},{9,8},{10,11... | collective-permute-start | bytes 1179656 | tf_op jit(solution)/shard_map/ppermute | solution.py:448
  27.3 9.3 %collective-permute-start.19 = (bf16[512,512]{1,0:T(8,128)(2,1)S(1)}, bf16[512,512]{1,0:T(8,128)(2,1)S(1)}, u32[]{:S(2)}, u32[]{:S(2)}) collective-permute-start(bf16[512,512]{1,0:T(8,128)(2,1)S(1)} %get-tuple-element.39.proc.w0), channel_id=1, source_target_pairs={{0,1},{1,0},{2,3},{3,2},{4,5},{5,4},{6,7},{7,6},{8,9},{9,8},{10,11... | collective-permute-start | bytes 1572872 | tf_op jit(solution)/shard_map/ppermute | solution.py:448
  30.2 6.5 %collective-permute-start.16 = (bf16[192,512]{1,0:T(8,128)(2,1)S(1)}, bf16[192,512]{1,0:T(8,128)(2,1)S(1)}, u32[]{:S(2)}, u32[]{:S(2)}) collective-permute-start(bf16[192,512]{1,0:T(8,128)(2,1)S(1)} %get-tuple-element.47.w2), channel_id=1, source_target_pairs={{0,4},{4,0},{8,12},{12,8},{1,5},{5,1},{9,13},{13,9},{2,6},{6,2},{1... | collective-permute-start | bytes 589832 | tf_op jit(solution)/shard_map/ppermute | solution.py:457
  30.8 7.7 %collective-permute-start.13 = (bf16[256,512]{1,0:T(8,128)(2,1)S(1)}, bf16[256,512]{1,0:T(8,128)(2,1)S(1)}, u32[]{:S(2)}, u32[]{:S(2)}) collective-permute-start(bf16[256,512]{1,0:T(8,128)(2,1)S(1)} %shard_map.233.after.mine), channel_id=1, source_target_pairs={{0,2},{1,3},{2,0},{3,1},{4,6},{5,7},{6,4},{7,5},{8,10},{9,11},{10,... | collective-permute-start | bytes 786440 | tf_op jit(solution)/shard_map/ppermute | solution.py:444
  32.3 7.4 %collective-permute-start.21 = (bf16[256,512]{1,0:T(8,128)(2,1)S(1)}, bf16[256,512]{1,0:T(8,128)(2,1)S(1)}, u32[]{:S(2)}, u32[]{:S(2)}) collective-permute-start(bf16[256,512]{1,0:T(8,128)(2,1)S(1)} %get-tuple-element.50.first), channel_id=1, source_target_pairs={{0,16},{16,0},{1,17},{17,1},{2,18},{18,2},{3,19},{19,3},{4,20},{20... | collective-permute-start | bytes 786440 | tf_op jit(solution)/shard_map/ppermute | solution.py:453
  32.8 3.8 %collective-permute-start.17 = (bf16[192,512]{1,0:T(8,128)(2,1)S(1)}, bf16[192,512]{1,0:T(8,128)(2,1)S(1)}, u32[]{:S(2)}, u32[]{:S(2)}) collective-permute-start(bf16[192,512]{1,0:T(8,128)(2,1)S(1)} %get-tuple-element.47.w2), channel_id=1, source_target_pairs={{0,1},{1,0},{2,3},{3,2},{4,5},{5,4},{6,7},{7,6},{8,9},{9,8},{10,11... | collective-permute-start | bytes 589832 | tf_op jit(solution)/shard_map/ppermute | solution.py:448
  36.7 1.8 %collective-permute-start.18 = (bf16[192,512]{1,0:T(8,128)(2,1)S(1)}, bf16[192,512]{1,0:T(8,128)(2,1)S(1)}, u32[]{:S(2)}, u32[]{:S(2)}) collective-permute-start(bf16[192,512]{1,0:T(8,128)(2,1)S(1)} %collective-permute-done.16.w3), channel_id=1, source_target_pairs={{0,1},{1,0},{2,3},{3,2},{4,5},{5,4},{6,7},{7,6},{8,9},{9,8},{10,11... | collective-permute-start | bytes 589832 | tf_op jit(solution)/shard_map/ppermute | solution.py:448
  38.5 12.0 %copy-start.16 = (s32[2,2048]{1,0:T(2,128)S(1)}, s32[2,2048]{1,0:T(2,128)}, u32[]{:S(2)}) copy-start(s32[2,2048]{1,0:T(2,128)} %edges.5) | copy-start | bytes 49156
  39.8 10.6 %collective-permute-start.22 = (bf16[512,512]{1,0:T(8,128)(2,1)S(1)}, bf16[512,512]{1,0:T(8,128)(2,1)S(1)}, u32[]{:S(2)}, u32[]{:S(2)}) collective-permute-start(bf16[512,512]{1,0:T(8,128)(2,1)S(1)} %shard_map.236.pair), channel_id=1, source_target_pairs={{0,1},{1,0},{2,3},{3,2},{4,5},{5,4},{6,7},{7,6},{8,9},{9,8},{10,11... | collective-permute-start | bytes 1572872 | tf_op jit(solution)/shard_map/ppermute | solution.py:448
  39.9 10.6 %collective-permute-start.20 = (bf16[256,512]{1,0:T(8,128)(2,1)S(1)}, bf16[256,512]{1,0:T(8,128)(2,1)S(1)}, u32[]{:S(2)}, u32[]{:S(2)}) collective-permute-start(bf16[256,512]{1,0:T(8,128)(2,1)S(1)} %get-tuple-element.48.after.mine.middle), channel_id=1, source_target_pairs={{0,1},{1,0},{2,3},{3,2},{4,5},{5,4},{6,7},{7,6},{8,9},{9,8},{10,11... | collective-permute-start | bytes 786440 | tf_op jit(solution)/shard_map/ppermute | solution.py:448
  40.4 6.3 %collective-permute-start.23 = (bf16[32,512]{1,0:T(8,128)(2,1)S(1)}, bf16[32,512]{1,0:T(8,128)(2,1)S(1)}, u32[]{:S(2)}, u32[]{:S(2)}) collective-permute-start(bf16[32,512]{1,0:T(8,128)(2,1)S(1)} %get-tuple-element.55), channel_id=1, source_target_pairs={{0,4},{4,0},{8,12},{12,8},{1,5},{5,1},{9,13},{13,9},{2,6},{6,2},{1... | collective-permute-start | bytes 98312 | tf_op jit(solution)/shard_map/ppermute | solution.py:586
  41.7 6.5 %collective-permute-start.24 = (bf16[32,512]{1,0:T(8,128)(2,1)S(1)}, bf16[32,512]{1,0:T(8,128)(2,1)S(1)}, u32[]{:S(2)}, u32[]{:S(2)}) collective-permute-start(bf16[32,512]{1,0:T(8,128)(2,1)S(1)} %get-tuple-element.56), channel_id=1, source_target_pairs={{0,8},{4,12},{8,0},{12,4},{1,9},{5,13},{9,1},{13,5},{2,10},{6,14},... | collective-permute-start | bytes 98312 | tf_op jit(solution)/shard_map/ppermute | solution.py:586
  44.6 5.8 %collective-permute-start.25 = (bf16[32,512]{1,0:T(8,128)(2,1)S(1)}, bf16[32,512]{1,0:T(8,128)(2,1)S(1)}, u32[]{:S(2)}, u32[]{:S(2)}) collective-permute-start(bf16[32,512]{1,0:T(8,128)(2,1)S(1)} %get-tuple-element.57), channel_id=1, source_target_pairs={{4,8},{8,4},{5,9},{9,5},{6,10},{10,6},{7,11},{11,7},{20,24},{24,20... | collective-permute-start | bytes 98312 | tf_op jit(solution)/shard_map/ppermute | solution.py:586
  46.7 12.7 %collective-permute-start.30 = (bf16[384,512]{1,0:T(8,128)(2,1)S(1)}, bf16[384,512]{1,0:T(8,128)(2,1)S(1)}, u32[]{:S(2)}, u32[]{:S(2)}) collective-permute-start(bf16[384,512]{1,0:T(8,128)(2,1)S(1)} %get-tuple-element.62.w0), channel_id=1, source_target_pairs={{0,2},{1,3},{2,0},{3,1},{4,6},{5,7},{6,4},{7,5},{8,10},{9,11},{10,... | collective-permute-start | bytes 1179656 | tf_op jit(solution)/shard_map/ppermute | solution.py:444
  50.4 2.7 %collective-permute-start.26 = (bf16[96,512]{1,0:T(8,128)(2,1)S(1)}, bf16[96,512]{1,0:T(8,128)(2,1)S(1)}, u32[]{:S(2)}, u32[]{:S(2)}) collective-permute-start(bf16[96,512]{1,0:T(8,128)(2,1)S(1)} %shard_map.238.halo), channel_id=1, source_target_pairs={{0,1},{1,0},{2,3},{3,2},{4,5},{5,4},{6,7},{7,6},{8,9},{9,8},{10,11... | collective-permute-start | bytes 294920 | tf_op jit(solution)/shard_map/ppermute | solution.py:448
  50.5 2.6 %copy-start.21 = (f32[512]{0:T(512)S(1)}, f32[512]{0:T(512)}, u32[]{:S(2)}) copy-start(f32[512]{0:T(512)} %param.46) | copy-start | bytes 6148
  53.1 13.3 %copy-start.11 = (f32[512]{0:T(512)S(1)}, f32[512]{0:T(512)}, u32[]{:S(2)}) copy-start(f32[512]{0:T(512)} %param.47) | copy-start | bytes 6148
  58.8 1.7 %collective-permute-start.27 = (bf16[256,512]{1,0:T(8,128)(2,1)S(1)}, bf16[256,512]{1,0:T(8,128)(2,1)S(1)}, u32[]{:S(2)}, u32[]{:S(2)}) collective-permute-start(bf16[256,512]{1,0:T(8,128)(2,1)S(1)} %get-tuple-element.59), channel_id=1, source_target_pairs={{0,1},{1,0},{2,3},{3,2},{4,5},{5,4},{6,7},{7,6},{8,9},{9,8},{10,11... | collective-permute-start | bytes 786440 | tf_op jit(solution)/shard_map/ppermute | solution.py:448
  59.3 2.8 %collective-permute-start.29 = (bf16[384,512]{1,0:T(8,128)(2,1)S(1)}, bf16[384,512]{1,0:T(8,128)(2,1)S(1)}, u32[]{:S(2)}, u32[]{:S(2)}) collective-permute-start(bf16[384,512]{1,0:T(8,128)(2,1)S(1)} %get-tuple-element.62.w0), channel_id=1, source_target_pairs={{0,1},{1,0},{2,3},{3,2},{4,5},{5,4},{6,7},{7,6},{8,9},{9,8},{10,11... | collective-permute-start | bytes 1179656 | tf_op jit(solution)/shard_map/ppermute | solution.py:448
  59.4 2.7 %collective-permute-start.31 = (bf16[384,512]{1,0:T(8,128)(2,1)S(1)}, bf16[384,512]{1,0:T(8,128)(2,1)S(1)}, u32[]{:S(2)}, u32[]{:S(2)}) collective-permute-start(bf16[384,512]{1,0:T(8,128)(2,1)S(1)} %collective-permute-done.30.w2), channel_id=1, source_target_pairs={{0,1},{1,0},{2,3},{3,2},{4,5},{5,4},{6,7},{7,6},{8,9},{9,8},{10,11... | collective-permute-start | bytes 1179656 | tf_op jit(solution)/shard_map/ppermute | solution.py:448
  60.5 5.8 %collective-permute-start.28 = (bf16[128,512]{1,0:T(8,128)(2,1)S(1)}, bf16[128,512]{1,0:T(8,128)(2,1)S(1)}, u32[]{:S(2)}, u32[]{:S(2)}) collective-permute-start(bf16[128,512]{1,0:T(8,128)(2,1)S(1)} %get-tuple-element.61), channel_id=1, source_target_pairs={{0,2},{1,3},{2,0},{3,1},{4,6},{5,7},{6,4},{7,5},{8,10},{9,11},{10,... | collective-permute-start | bytes 393224 | tf_op jit(solution)/shard_map/ppermute | solution.py:444

commit v16 on v15

--- a/solution.py
+++ b/solution.py
@@ -10,7 +10,7 @@
 BLOCK = 128
 OFFSETS = (-2, -1, 1, 2)
 STEP = 512
-GATHERED = 1024
+GATHERED = 2048
 LONG = 30 * 10**9
 BY_GROUP = ("groups",)
 BY_PART = ("dom",)

time: 67.9 us -> 68 us (level)
  no operation moved by 1% of the time
where the time goes in v16:
time: 68 us; the launch traced here: 67.8 us
  starting transfers between devices  25.2 us (37%)
  waiting for transfers between devices  21.4 us (31%)
  Pallas kernels  18.2 us (27%)
  between operations  1.73 us (3%)
  local copies, waits for them, and re-layouts  1.27 us (2%)
    pallas_call x16, Pallas kernels, call(): pl.pallas_call(body, out_shape=tuple(outs), in_specs=specs, out_specs=tup...  18.2 us
    ppermute x6, starting transfers between devices, local(): lax.ppermute(v, 'dom', entry[0])  11.6 us
    ppermute x6, waiting for transfers between devices, to_chip(): return lax.ppermute(v, 'sub', [(i, i ^ 2) for i in range(4)])  10.2 us
    ppermute x6, starting transfers between devices, to_chip(): return lax.ppermute(v, 'sub', [(i, i ^ 2) for i in range(4)])  8.15 us
    ppermute x6, waiting for transfers between devices, local(): lax.ppermute(v, 'dom', entry[0])  5.38 us
    ppermute x1, waiting for transfers between devices, to_partition(): lax.ppermute(v, 'dom', [(i, i ^ 1) for i in range(lax.axis_size('dom'))])  3.83 us
    ppermute x17, starting transfers between devices, to_core(): return lax.ppermute(v, 'sub', [(i, i ^ 1) for i in range(4)])  3.63 us
    ppermute x17, waiting for transfers between devices, to_core(): return lax.ppermute(v, 'sub', [(i, i ^ 1) for i in range(4)])  1.95 us
  transfers between devices with their start and end apart: 32, of which 11 were waited for; matrix products, arithmetic and copies ran while one was open for 0% of the time, Pallas kernels for 24%

profile of v16, /device:TPU:12, one launch (start us, length us, event | category | flops | bytes accessed | tf_op | source)
XLA Modules:
  0.0 67.8 jit_solution(4275513012709391817)
XLA Ops:
  0.1 0.8 %copy-done.4 = bf16[128,512]{1,0:T(8,128)(2,1)S(1)} copy-done((bf16[128,512]{1,0:T(8,128)(2,1)S(1)}, bf16[128,512]{1,0:T(8,128)(2,1)}, u32[]{:S(2)}) %copy-start.4) | copy-done | bytes 131096
  0.9 0.1 copy-done.5
  1.0 0.1 copy-done
  1.0 0.2 copy-done.1
  1.2 0.0 copy-done.6
  1.3 0.0 copy-start.17
  1.3 0.0 copy-start.18
  1.3 0.3 shard_map.227
  1.6 0.0 copy-start.19
  1.6 0.0 copy-start.20
  1.6 1.6 %collective-permute-start.8 = (bf16[384,512]{1,0:T(8,128)(2,1)S(1)}, bf16[384,512]{1,0:T(8,128)(2,1)S(1)}, u32[]{:S(2)}, u32[]{:S(2)}) collective-permute-start(bf16[384,512]{1,0:T(8,128)(2,1)S(1)} %get-tuple-element.41), channel_id=1, source_target_pairs={{0,2},{1,3},{2,0},{3,1},{4,6},{5,7},{6,4},{7,5},{8,10},{9,11},{10,... | collective-permute-start | bytes 1179656 | tf_op jit(solution)/shard_map/ppermute | solution.py:444
  3.2 0.5 collective-permute-start
  3.6 2.6 %collective-permute-start.1 = (bf16[64,128]{1,0:T(8,128)(2,1)S(1)}, bf16[64,128]{1,0:T(8,128)(2,1)S(1)}, u32[]{:S(2)}, u32[]{:S(2)}) collective-permute-start(bf16[64,128]{1,0:T(8,128)(2,1)S(1)} %get-tuple-element.35), channel_id=1, source_target_pairs={{0,8},{4,12},{8,0},{12,4},{1,9},{5,13},{9,1},{13,5},{2,10},{6,14},... | collective-permute-start | bytes 49160 | tf_op jit(solution)/shard_map/ppermute | solution.py:514
  6.2 2.3 %collective-permute-start.2 = (bf16[64,128]{1,0:T(8,128)(2,1)S(1)}, bf16[64,128]{1,0:T(8,128)(2,1)S(1)}, u32[]{:S(2)}, u32[]{:S(2)}) collective-permute-start(bf16[64,128]{1,0:T(8,128)(2,1)S(1)} %get-tuple-element.36), channel_id=1, source_target_pairs={{4,8},{8,4},{5,9},{9,5},{6,10},{10,6},{7,11},{11,7},{20,24},{24,20... | collective-permute-start | bytes 49160 | tf_op jit(solution)/shard_map/ppermute | solution.py:514
  8.6 0.0 collective-permute-done.1.refs_3_
  8.6 3.2 %collective-permute-done.2.refs_4_ = bf16[64,128]{1,0:T(8,128)(2,1)S(1)} collective-permute-done((bf16[64,128]{1,0:T(8,128)(2,1)S(1)}, bf16[64,128]{1,0:T(8,128)(2,1)S(1)}, u32[]{:S(2)}, u32[]{:S(2)}) %collective-permute-start.2) | collective-permute-done | bytes 16416 | tf_op jit(solution)/shard_map/ppermute | solution.py:514
  11.9 0.6 collective-permute-start.3
  12.5 0.1 collective-permute-done.8.source.early
  12.6 0.6 collective-permute-start.9
  13.1 0.5 collective-permute-start.7
  14.9 0.1 collective-permute-start.4
  15.1 1.8 %shard_map.229 = (bf16[384,512]{1,0:T(8,128)(2,1)S(1)}, bf16[512,512]{1,0:T(8,128)(2,1)S(1)}, bf16[1024,512]{1,0:T(8,128)(2,1)S(1)}, bf16[2048,512]{1,0:T(8,128)(2,1)S(1)}, s32[8,128]{1,0:T(8,128)S(1)}) custom-call(bf16[256,512]{1,0:T(8,128)(2,1)S(1)} %copy-done.13, bf16[128,512]{1,0:T(8,128)(2,1)S(1)} %copy-done.4, bf16[384,512]{1,0:T(8,128)(2,1)S(1)} %copy-done.12, ...), custom_call_target="tpu_custom_call" | custom-call | flops 402653184 | bytes 5361672 | tf_op jit(solution)/shard_map/pallas_call | solution.py:71
  16.9 2.4 %collective-permute-done.3.lat.l1 = bf16[1216,128]{1,0:T(8,128)(2,1)S(1)} collective-permute-done((bf16[1216,128]{1,0:T(8,128)(2,1)S(1)}, bf16[1216,128]{1,0:T(8,128)(2,1)S(1)}, u32[]{:S(2)}, u32[]{:S(2)}) %collective-permute-start.3) | collective-permute-done | bytes 311328 | tf_op jit(solution)/shard_map/ppermute | solution.py:444
  19.4 0.1 collective-permute-start.5
  19.5 0.5 collective-permute-start.10
  20.0 0.1 collective-permute-start.11
  20.1 1.4 %collective-permute-start.15 = (bf16[320,512]{1,0:T(8,128)(2,1)S(1)}, bf16[320,512]{1,0:T(8,128)(2,1)S(1)}, u32[]{:S(2)}, u32[]{:S(2)}) collective-permute-start(bf16[320,512]{1,0:T(8,128)(2,1)S(1)} %get-tuple-element.46), channel_id=1, source_target_pairs={{0,2},{1,3},{2,0},{3,1},{4,6},{5,7},{6,4},{7,5},{8,10},{9,11},{10,... | collective-permute-start | bytes 983048 | tf_op jit(solution)/shard_map/ppermute | solution.py:444
  21.4 0.4 collective-permute-done.11.round_both
  21.8 0.0 copy-start.9
  21.8 0.0 copy-start.10
  21.8 4.9 %shard_map.232 = (bf16[256,512]{1,0:T(8,128)(2,1)S(1)}, bf16[256,512]{1,0:T(8,128)(2,1)S(1)}, bf16[256,512]{1,0:T(8,128)(2,1)S(1)}) custom-call(bf16[1024,512]{1,0:T(8,128)(2,1)S(1)} %get-tuple-element.37.emb, s32[2,1024]{1,0:T(2,128)S(1)} %copy-done.19, f32[1,512]{1,0:T(1,128)S(1)} %bitcast.10, bf16[1216,128]{1,0:T(8,128)(2,1)S(1)} %shard_map.228.after.l0, ...), custom_call_target="tpu_custom_call" | custom-call | flops 2952790016 | bytes 5191680 | tf_op jit(solution)/shard_map/pallas_call | solution.py:71
  26.8 0.2 collective-permute-start.12
  27.0 0.4 collective-permute-start.14
  27.3 0.1 collective-permute-start.19
  27.5 0.9 %collective-permute-done.12.theirs = bf16[256,512]{1,0:T(8,128)(2,1)S(1)} collective-permute-done((bf16[256,512]{1,0:T(8,128)(2,1)S(1)}, bf16[256,512]{1,0:T(8,128)(2,1)S(1)}, u32[]{:S(2)}, u32[]{:S(2)}) %collective-permute-start.12) | collective-permute-done | bytes 262176 | tf_op jit(solution)/shard_map/ppermute | solution.py:448
  28.4 0.1 shard_map.233.after.mine
  28.4 1.7 %collective-permute-done.15.source = bf16[320,512]{1,0:T(8,128)(2,1)S(1)} collective-permute-done((bf16[320,512]{1,0:T(8,128)(2,1)S(1)}, bf16[320,512]{1,0:T(8,128)(2,1)S(1)}, u32[]{:S(2)}, u32[]{:S(2)}) %collective-permute-start.15) | collective-permute-done | bytes 327712 | tf_op jit(solution)/shard_map/ppermute | solution.py:444
  30.2 0.7 %collective-permute-start.16 = (bf16[192,512]{1,0:T(8,128)(2,1)S(1)}, bf16[192,512]{1,0:T(8,128)(2,1)S(1)}, u32[]{:S(2)}, u32[]{:S(2)}) collective-permute-start(bf16[192,512]{1,0:T(8,128)(2,1)S(1)} %get-tuple-element.47.w2), channel_id=1, source_target_pairs={{0,4},{4,0},{8,12},{12,8},{1,5},{5,1},{9,13},{13,9},{2,6},{6,2},{1... | collective-permute-start | bytes 589832 | tf_op jit(solution)/shard_map/ppermute | solution.py:457
  30.8 1.5 %collective-permute-start.13 = (bf16[256,512]{1,0:T(8,128)(2,1)S(1)}, bf16[256,512]{1,0:T(8,128)(2,1)S(1)}, u32[]{:S(2)}, u32[]{:S(2)}) collective-permute-start(bf16[256,512]{1,0:T(8,128)(2,1)S(1)} %shard_map.233.after.mine), channel_id=1, source_target_pairs={{0,2},{1,3},{2,0},{3,1},{4,6},{5,7},{6,4},{7,5},{8,10},{9,11},{10,... | collective-permute-start | bytes 786440 | tf_op jit(solution)/shard_map/ppermute | solution.py:444
  32.3 0.5 collective-permute-start.21
  32.8 3.8 %collective-permute-done.16.w3 = bf16[192,512]{1,0:T(8,128)(2,1)S(1)} collective-permute-done((bf16[192,512]{1,0:T(8,128)(2,1)S(1)}, bf16[192,512]{1,0:T(8,128)(2,1)S(1)}, u32[]{:S(2)}, u32[]{:S(2)}) %collective-permute-start.16) | collective-permute-done | bytes 196640 | tf_op jit(solution)/shard_map/ppermute | solution.py:457
  36.7 1.8 %collective-permute-done.13.theirs = bf16[256,512]{1,0:T(8,128)(2,1)S(1)} collective-permute-done((bf16[256,512]{1,0:T(8,128)(2,1)S(1)}, bf16[256,512]{1,0:T(8,128)(2,1)S(1)}, u32[]{:S(2)}, u32[]{:S(2)}) %collective-permute-start.13) | collective-permute-done | bytes 262176 | tf_op jit(solution)/shard_map/ppermute | solution.py:444
  38.5 0.0 copy-start.16
  38.5 1.2 %shard_map.235 = (bf16[256,512]{1,0:T(8,128)(2,1)S(1)}, bf16[384,512]{1,0:T(8,128)(2,1)S(1)}, bf16[32,512]{1,0:T(8,128)(2,1)S(1)}, bf16[32,512]{1,0:T(8,128)(2,1)S(1)}, bf16[32,512]{1,0:T(8,128)(2,1)S(1)}) custom-call(bf16[256,512]{1,0:T(8,128)(2,1)S(1)} %get-tuple-element.43.mesh, bf16[256,512]{1,0:T(8,128)(2,1)S(1)} %shard_map.233.after.mine, ...), custom_call_target="tpu_custom_call" | custom-call | flops 402653184 | bytes 4033024 | tf_op jit(solution)/shard_map/pallas_call | solution.py:71
  39.8 0.1 collective-permute-start.22
  39.9 0.5 collective-permute-start.20
  40.4 1.3 %collective-permute-start.23 = (bf16[32,512]{1,0:T(8,128)(2,1)S(1)}, bf16[32,512]{1,0:T(8,128)(2,1)S(1)}, u32[]{:S(2)}, u32[]{:S(2)}) collective-permute-start(bf16[32,512]{1,0:T(8,128)(2,1)S(1)} %get-tuple-element.55), channel_id=1, source_target_pairs={{0,4},{4,0},{8,12},{12,8},{1,5},{5,1},{9,13},{13,9},{2,6},{6,2},{1... | collective-permute-start | bytes 98312 | tf_op jit(solution)/shard_map/ppermute | solution.py:586
  41.7 2.8 %collective-permute-start.24 = (bf16[32,512]{1,0:T(8,128)(2,1)S(1)}, bf16[32,512]{1,0:T(8,128)(2,1)S(1)}, u32[]{:S(2)}, u32[]{:S(2)}) collective-permute-start(bf16[32,512]{1,0:T(8,128)(2,1)S(1)} %get-tuple-element.56), channel_id=1, source_target_pairs={{0,8},{4,12},{8,0},{12,4},{1,9},{5,13},{9,1},{13,5},{2,10},{6,14},... | collective-permute-start | bytes 98312 | tf_op jit(solution)/shard_map/ppermute | solution.py:586
  44.6 2.1 %collective-permute-start.25 = (bf16[32,512]{1,0:T(8,128)(2,1)S(1)}, bf16[32,512]{1,0:T(8,128)(2,1)S(1)}, u32[]{:S(2)}, u32[]{:S(2)}) collective-permute-start(bf16[32,512]{1,0:T(8,128)(2,1)S(1)} %get-tuple-element.57), channel_id=1, source_target_pairs={{4,8},{8,4},{5,9},{9,5},{6,10},{10,6},{7,11},{11,7},{20,24},{24,20... | collective-permute-start | bytes 98312 | tf_op jit(solution)/shard_map/ppermute | solution.py:586
  46.7 1.6 %collective-permute-start.30 = (bf16[384,512]{1,0:T(8,128)(2,1)S(1)}, bf16[384,512]{1,0:T(8,128)(2,1)S(1)}, u32[]{:S(2)}, u32[]{:S(2)}) collective-permute-start(bf16[384,512]{1,0:T(8,128)(2,1)S(1)} %get-tuple-element.62.w0), channel_id=1, source_target_pairs={{0,2},{1,3},{2,0},{3,1},{4,6},{5,7},{6,4},{7,5},{8,10},{9,11},{10,... | collective-permute-start | bytes 1179656 | tf_op jit(solution)/shard_map/ppermute | solution.py:444
  48.2 2.1 %collective-permute-done.25.refs_2_ = bf16[32,512]{1,0:T(8,128)(2,1)S(1)} collective-permute-done((bf16[32,512]{1,0:T(8,128)(2,1)S(1)}, bf16[32,512]{1,0:T(8,128)(2,1)S(1)}, u32[]{:S(2)}, u32[]{:S(2)}) %collective-permute-start.25) | collective-permute-done | bytes 32800 | tf_op jit(solution)/shard_map/ppermute | solution.py:586
  50.4 0.1 collective-permute-start.26
  50.5 0.0 copy-start.21
  50.5 2.6 %shard_map.237 = (bf16[1536,512]{1,0:T(8,128)(2,1)S(1)}, f32[1024,512]{1,0:T(8,128)S(1)}, bf16[512,512]{1,0:T(8,128)(2,1)S(1)}, bf16[512,512]{1,0:T(8,128)(2,1)S(1)}) custom-call(bf16[2048,512]{1,0:T(8,128)(2,1)S(1)} %get-tuple-element.49.emb, bf16[256,512]{1,0:T(8,128)(2,1)S(1)} %get-tuple-element.48.after.mine.middle, ...), custom_call_target="tpu_custom_call" | custom-call | flops 1610612736 | bytes 9453568 | tf_op jit(solution)/shard_map/pallas_call | solution.py:71
  53.1 0.0 copy-start.11
  53.1 5.6 %shard_map.239 = (bf16[256,512]{1,0:T(8,128)(2,1)S(1)}, bf16[256,512]{1,0:T(8,128)(2,1)S(1)}) custom-call(bf16[2048,512]{1,0:T(8,128)(2,1)S(1)} %get-tuple-element.49.emb, s32[2,2048]{1,0:T(2,128)S(1)} %copy-done.16, f32[1,512]{1,0:T(1,128)S(1)} %bitcast.11, bf16[1536,512]{1,0:T(8,128)(2,1)S(1)} %get-tuple-element.51.table, ...), custom_call_target="tpu_custom_call" | custom-call | flops 3489660928 | bytes 7559168 | tf_op jit(solution)/shard_map/pallas_call | solution.py:71
  58.8 0.5 collective-permute-start.27
  59.3 0.1 collective-permute-start.29
  59.4 0.4 collective-permute-start.31
  59.8 0.6 collective-permute-done.27.theirs
  60.5 0.1 shard_map.240
  60.6 1.6 %collective-permute-start.28 = (bf16[128,512]{1,0:T(8,128)(2,1)S(1)}, bf16[128,512]{1,0:T(8,128)(2,1)S(1)}, u32[]{:S(2)}, u32[]{:S(2)}) collective-permute-start(bf16[128,512]{1,0:T(8,128)(2,1)S(1)} %get-tuple-element.61), channel_id=1, source_target_pairs={{0,2},{1,3},{2,0},{3,1},{4,6},{5,7},{6,4},{7,5},{8,10},{9,11},{10,... | collective-permute-start | bytes 393224 | tf_op jit(solution)/shard_map/ppermute | solution.py:444
  62.1 4.3 %collective-permute-done.28.theirs = bf16[128,512]{1,0:T(8,128)(2,1)S(1)} collective-permute-done((bf16[128,512]{1,0:T(8,128)(2,1)S(1)}, bf16[128,512]{1,0:T(8,128)(2,1)S(1)}, u32[]{:S(2)}, u32[]{:S(2)}) %collective-permute-start.28) | collective-permute-done | bytes 131104 | tf_op jit(solution)/shard_map/ppermute | solution.py:444
  66.4 1.4 %shard_map.241 = bf16[128,512]{1,0:T(8,128)(2,1)} custom-call(bf16[256,512]{1,0:T(8,128)(2,1)S(1)} %get-tuple-element.48.after.mine.middle, bf16[128,512]{1,0:T(8,128)(2,1)S(1)} %get-tuple-element.60.mine, bf16[128,512]{1,0:T(8,128)(2,1)S(1)} %collective-permute-done.28.theirs, f32[1,512]{1,0:T(1,128)S(1)} %bitcast.9, ...), custom_call_target="tpu_custom_call" | custom-call | flops 201326592 | bytes 2230272 | tf_op jit(solution)/shard_map/pallas_call | solution.py:71
  (60 shorter events, 0.3 us)
Async XLA Ops:
  0.0 0.9 %copy-start.4 = (bf16[128,512]{1,0:T(8,128)(2,1)S(1)}, bf16[128,512]{1,0:T(8,128)(2,1)}, u32[]{:S(2)}) copy-start(bf16[128,512]{1,0:T(8,128)(2,1)} %e_out.1) | copy-start | bytes 393220
  0.0 1.0 %copy-start.5 = (bf16[128,512]{1,0:T(8,128)(2,1)S(1)}, bf16[128,512]{1,0:T(8,128)(2,1)}, u32[]{:S(2)}) copy-start(bf16[128,512]{1,0:T(8,128)(2,1)} %p_out.3) | copy-start | bytes 393220
  0.0 1.0 %copy-start = (bf16[512,128]{1,0:T(8,128)(2,1)S(1)}, bf16[512,128]{1,0:T(8,128)(2,1)}, u32[]{:S(2)}) copy-start(bf16[512,128]{1,0:T(8,128)(2,1)} %refs_0_.1) | copy-start | bytes 393220
  0.0 1.0 %copy-start.8 = (s32[1,4,64]{2,1,0:T(4,128)S(1)}, s32[1,4,64]{2,1,0:T(4,128)}, u32[]{:S(2)}) copy-start(s32[1,4,64]{2,1,0:T(4,128)} %send.2) | copy-start | bytes 3076
  0.0 1.2 %copy-start.1 = (bf16[384,512]{1,0:T(8,128)(2,1)S(1)}, bf16[384,512]{1,0:T(8,128)(2,1)}, u32[]{:S(2)}) copy-start(bf16[384,512]{1,0:T(8,128)(2,1)} %o_in.1) | copy-start | bytes 1179652
  0.0 1.2 %copy-start.6 = (bf16[128,512]{1,0:T(8,128)(2,1)S(1)}, bf16[128,512]{1,0:T(8,128)(2,1)}, u32[]{:S(2)}) copy-start(bf16[128,512]{1,0:T(8,128)(2,1)} %o_out.1) | copy-start | bytes 393220
  0.0 11.8 %copy-start.3 = (bf16[512,128]{1,0:T(8,128)(2,1)S(1)}, bf16[512,128]{1,0:T(8,128)(2,1)}, u32[]{:S(2)}) copy-start(bf16[512,128]{1,0:T(8,128)(2,1)} %refs_1_.1) | copy-start | bytes 393220
  1.2 13.8 %copy-start.12 = (bf16[384,512]{1,0:T(8,128)(2,1)S(1)}, bf16[384,512]{1,0:T(8,128)(2,1)}, u32[]{:S(2)}) copy-start(bf16[384,512]{1,0:T(8,128)(2,1)} %p_in.1) | copy-start | bytes 1179652
  1.2 13.8 %copy-start.13 = (bf16[256,512]{1,0:T(8,128)(2,1)S(1)}, bf16[256,512]{1,0:T(8,128)(2,1)}, u32[]{:S(2)}) copy-start(bf16[256,512]{1,0:T(8,128)(2,1)} %e_in.1) | copy-start | bytes 786436
  1.2 13.8 %copy-start.14 = (f32[4,2048]{1,0:T(4,128)S(1)}, f32[4,2048]{1,0:T(4,128)}, u32[]{:S(2)}) copy-start(f32[4,2048]{1,0:T(4,128)} %pgeom.1) | copy-start | bytes 98308
  1.2 13.8 %copy-start.15 = (f32[4,1024]{1,0:T(4,128)S(1)}, f32[4,1024]{1,0:T(4,128)}, u32[]{:S(2)}) copy-start(f32[4,1024]{1,0:T(4,128)} %egeom.1) | copy-start | bytes 49156
  1.3 13.8 %copy-start.17 = (f32[4,512]{1,0:T(4,128)S(1)}, f32[4,512]{1,0:T(4,128)}, u32[]{:S(2)}) copy-start(f32[4,512]{1,0:T(4,128)} %egeo.1) | copy-start | bytes 24580
  1.3 13.8 %copy-start.18 = (f32[4,512]{1,0:T(4,128)S(1)}, f32[4,512]{1,0:T(4,128)}, u32[]{:S(2)}) copy-start(f32[4,512]{1,0:T(4,128)} %pgeo.1) | copy-start | bytes 24580
  1.6 20.2 %copy-start.19 = (s32[2,1024]{1,0:T(2,128)S(1)}, s32[2,1024]{1,0:T(2,128)}, u32[]{:S(2)}) copy-start(s32[2,1024]{1,0:T(2,128)} %edges.3) | copy-start | bytes 24580
  1.6 20.2 %copy-start.20 = (f32[512]{0:T(512)S(1)}, f32[512]{0:T(512)}, u32[]{:S(2)}) copy-start(f32[512]{0:T(512)} %param.44) | copy-start | bytes 6148
  1.6 10.9 %collective-permute-start.8 = (bf16[384,512]{1,0:T(8,128)(2,1)S(1)}, bf16[384,512]{1,0:T(8,128)(2,1)S(1)}, u32[]{:S(2)}, u32[]{:S(2)}) collective-permute-start(bf16[384,512]{1,0:T(8,128)(2,1)S(1)} %get-tuple-element.41), channel_id=1, source_target_pairs={{0,2},{1,3},{2,0},{3,1},{4,6},{5,7},{6,4},{7,5},{8,10},{9,11},{10,... | collective-permute-start | bytes 1179656 | tf_op jit(solution)/shard_map/ppermute | solution.py:444
  3.2 5.4 %collective-permute-start = (bf16[64,128]{1,0:T(8,128)(2,1)S(1)}, bf16[64,128]{1,0:T(8,128)(2,1)S(1)}, u32[]{:S(2)}, u32[]{:S(2)}) collective-permute-start(bf16[64,128]{1,0:T(8,128)(2,1)S(1)} %get-tuple-element.34), channel_id=1, source_target_pairs={{0,4},{4,0},{8,12},{12,8},{1,5},{5,1},{9,13},{13,9},{2,6},{6,2},{1... | collective-permute-start | bytes 49160 | tf_op jit(solution)/shard_map/ppermute | solution.py:514
  3.6 5.0 %collective-permute-start.1 = (bf16[64,128]{1,0:T(8,128)(2,1)S(1)}, bf16[64,128]{1,0:T(8,128)(2,1)S(1)}, u32[]{:S(2)}, u32[]{:S(2)}) collective-permute-start(bf16[64,128]{1,0:T(8,128)(2,1)S(1)} %get-tuple-element.35), channel_id=1, source_target_pairs={{0,8},{4,12},{8,0},{12,4},{1,9},{5,13},{9,1},{13,5},{2,10},{6,14},... | collective-permute-start | bytes 49160 | tf_op jit(solution)/shard_map/ppermute | solution.py:514
  6.2 5.6 %collective-permute-start.2 = (bf16[64,128]{1,0:T(8,128)(2,1)S(1)}, bf16[64,128]{1,0:T(8,128)(2,1)S(1)}, u32[]{:S(2)}, u32[]{:S(2)}) collective-permute-start(bf16[64,128]{1,0:T(8,128)(2,1)S(1)} %get-tuple-element.36), channel_id=1, source_target_pairs={{4,8},{8,4},{5,9},{9,5},{6,10},{10,6},{7,11},{11,7},{20,24},{24,20... | collective-permute-start | bytes 49160 | tf_op jit(solution)/shard_map/ppermute | solution.py:514
  11.9 7.5 %collective-permute-start.3 = (bf16[1216,128]{1,0:T(8,128)(2,1)S(1)}, bf16[1216,128]{1,0:T(8,128)(2,1)S(1)}, u32[]{:S(2)}, u32[]{:S(2)}) collective-permute-start(bf16[1216,128]{1,0:T(8,128)(2,1)S(1)} %shard_map.228.after.l0), channel_id=1, source_target_pairs={{0,2},{1,3},{2,0},{3,1},{4,6},{5,7},{6,4},{7,5},{8,10},{9,11},{10,... | collective-permute-start | bytes 933896 | tf_op jit(solution)/shard_map/ppermute | solution.py:444
  12.6 7.4 %collective-permute-start.9 = (bf16[256,512]{1,0:T(8,128)(2,1)S(1)}, bf16[256,512]{1,0:T(8,128)(2,1)S(1)}, u32[]{:S(2)}, u32[]{:S(2)}) collective-permute-start(bf16[256,512]{1,0:T(8,128)(2,1)S(1)} %shard_map.231.across), channel_id=1, source_target_pairs={{0,16},{16,0},{1,17},{17,1},{2,18},{18,2},{3,19},{19,3},{4,20},{20... | collective-permute-start | bytes 786440 | tf_op jit(solution)/shard_map/ppermute | solution.py:453
  13.1 8.3 %collective-permute-start.6 = (bf16[384,512]{1,0:T(8,128)(2,1)S(1)}, bf16[384,512]{1,0:T(8,128)(2,1)S(1)}, u32[]{:S(2)}, u32[]{:S(2)}) collective-permute-start(bf16[384,512]{1,0:T(8,128)(2,1)S(1)} %copy-done.1), channel_id=1, source_target_pairs={{0,1},{1,0},{2,3},{3,2},{4,5},{5,4},{6,7},{7,6},{8,9},{9,8},{10,11... | collective-permute-start | bytes 1179656 | tf_op jit(solution)/shard_map/ppermute | solution.py:448
  13.1 6.3 %collective-permute-start.7 = (bf16[128,512]{1,0:T(8,128)(2,1)S(1)}, bf16[128,512]{1,0:T(8,128)(2,1)S(1)}, u32[]{:S(2)}, u32[]{:S(2)}) collective-permute-start(bf16[128,512]{1,0:T(8,128)(2,1)S(1)} %copy-done.6), channel_id=1, source_target_pairs={{0,1},{1,0},{2,3},{3,2},{4,5},{5,4},{6,7},{7,6},{8,9},{9,8},{10,11... | collective-permute-start | bytes 393224 | tf_op jit(solution)/shard_map/ppermute | solution.py:448
  14.9 5.1 %collective-permute-start.4 = (bf16[1216,128]{1,0:T(8,128)(2,1)S(1)}, bf16[1216,128]{1,0:T(8,128)(2,1)S(1)}, u32[]{:S(2)}, u32[]{:S(2)}) collective-permute-start(bf16[1216,128]{1,0:T(8,128)(2,1)S(1)} %shard_map.228.after.l0), channel_id=1, source_target_pairs={{0,1},{1,0},{2,3},{3,2},{4,5},{5,4},{6,7},{7,6},{8,9},{9,8},{10,11... | collective-permute-start | bytes 933896 | tf_op jit(solution)/shard_map/ppermute | solution.py:448
  19.4 2.0 %collective-permute-start.5 = (bf16[1216,128]{1,0:T(8,128)(2,1)S(1)}, bf16[1216,128]{1,0:T(8,128)(2,1)S(1)}, u32[]{:S(2)}, u32[]{:S(2)}) collective-permute-start(bf16[1216,128]{1,0:T(8,128)(2,1)S(1)} %get-tuple-element.40), channel_id=1, source_target_pairs={{0,1},{1,0},{2,3},{3,2},{4,5},{5,4},{6,7},{7,6},{8,9},{9,8},{10,11... | collective-permute-start | bytes 933896 | tf_op jit(solution)/shard_map/ppermute | solution.py:448
  19.5 2.0 %collective-permute-start.10 = (bf16[256,512]{1,0:T(8,128)(2,1)S(1)}, bf16[256,512]{1,0:T(8,128)(2,1)S(1)}, u32[]{:S(2)}, u32[]{:S(2)}) collective-permute-start(bf16[256,512]{1,0:T(8,128)(2,1)S(1)} %shard_map.231.across), channel_id=1, source_target_pairs={{0,1},{1,0},{2,3},{3,2},{4,5},{5,4},{6,7},{7,6},{8,9},{9,8},{10,11... | collective-permute-start | bytes 786440 | tf_op jit(solution)/shard_map/ppermute | solution.py:448
  20.0 1.8 %collective-permute-start.11 = (bf16[256,512]{1,0:T(8,128)(2,1)S(1)}, bf16[256,512]{1,0:T(8,128)(2,1)S(1)}, u32[]{:S(2)}, u32[]{:S(2)}) collective-permute-start(bf16[256,512]{1,0:T(8,128)(2,1)S(1)} %collective-permute-done.9.round_), channel_id=1, source_target_pairs={{0,1},{1,0},{2,3},{3,2},{4,5},{5,4},{6,7},{7,6},{8,9},{9,8},{10,11... | collective-permute-start | bytes 786440 | tf_op jit(solution)/shard_map/ppermute | solution.py:448
  20.1 10.1 %collective-permute-start.15 = (bf16[320,512]{1,0:T(8,128)(2,1)S(1)}, bf16[320,512]{1,0:T(8,128)(2,1)S(1)}, u32[]{:S(2)}, u32[]{:S(2)}) collective-permute-start(bf16[320,512]{1,0:T(8,128)(2,1)S(1)} %get-tuple-element.46), channel_id=1, source_target_pairs={{0,2},{1,3},{2,0},{3,1},{4,6},{5,7},{6,4},{7,5},{8,10},{9,11},{10,... | collective-permute-start | bytes 983048 | tf_op jit(solution)/shard_map/ppermute | solution.py:444
  21.8 16.7 %copy-start.2 = (bf16[256,512]{1,0:T(8,128)(2,1)S(1)}, bf16[256,512]{1,0:T(8,128)(2,1)}, u32[]{:S(2)}) copy-start(bf16[256,512]{1,0:T(8,128)(2,1)} %n_in.1) | copy-start | bytes 786436
  21.8 16.7 %copy-start.7 = (bf16[128,512]{1,0:T(8,128)(2,1)S(1)}, bf16[128,512]{1,0:T(8,128)(2,1)}, u32[]{:S(2)}) copy-start(bf16[128,512]{1,0:T(8,128)(2,1)} %n_out.3) | copy-start | bytes 393220
  21.8 16.7 %copy-start.9 = (f32[512]{0:T(512)S(1)}, f32[512]{0:T(512)}, u32[]{:S(2)}) copy-start(f32[512]{0:T(512)} %param.45) | copy-start | bytes 6148
  21.8 16.7 %copy-start.10 = (s32[1,4,32]{2,1,0:T(4,128)S(1)}, s32[1,4,32]{2,1,0:T(4,128)}, u32[]{:S(2)}) copy-start(s32[1,4,32]{2,1,0:T(4,128)} %send.3) | copy-start | bytes 1540
  26.8 1.6 %collective-permute-start.12 = (bf16[256,512]{1,0:T(8,128)(2,1)S(1)}, bf16[256,512]{1,0:T(8,128)(2,1)S(1)}, u32[]{:S(2)}, u32[]{:S(2)}) collective-permute-start(bf16[256,512]{1,0:T(8,128)(2,1)S(1)} %get-tuple-element.45), channel_id=1, source_target_pairs={{0,1},{1,0},{2,3},{3,2},{4,5},{5,4},{6,7},{7,6},{8,9},{9,8},{10,11... | collective-permute-start | bytes 786440 | tf_op jit(solution)/shard_map/ppermute | solution.py:448
  27.0 5.9 %collective-permute-start.14 = (bf16[384,512]{1,0:T(8,128)(2,1)S(1)}, bf16[384,512]{1,0:T(8,128)(2,1)S(1)}, u32[]{:S(2)}, u32[]{:S(2)}) collective-permute-start(bf16[384,512]{1,0:T(8,128)(2,1)S(1)} %get-tuple-element.38.node.w0), channel_id=1, source_target_pairs={{0,1},{1,0},{2,3},{3,2},{4,5},{5,4},{6,7},{7,6},{8,9},{9,8},{10,11... | collective-permute-start | bytes 1179656 | tf_op jit(solution)/shard_map/ppermute | solution.py:448
  27.3 9.3 %collective-permute-start.19 = (bf16[512,512]{1,0:T(8,128)(2,1)S(1)}, bf16[512,512]{1,0:T(8,128)(2,1)S(1)}, u32[]{:S(2)}, u32[]{:S(2)}) collective-permute-start(bf16[512,512]{1,0:T(8,128)(2,1)S(1)} %get-tuple-element.39.proc.w0), channel_id=1, source_target_pairs={{0,1},{1,0},{2,3},{3,2},{4,5},{5,4},{6,7},{7,6},{8,9},{9,8},{10,11... | collective-permute-start | bytes 1572872 | tf_op jit(solution)/shard_map/ppermute | solution.py:448
  30.2 6.5 %collective-permute-start.16 = (bf16[192,512]{1,0:T(8,128)(2,1)S(1)}, bf16[192,512]{1,0:T(8,128)(2,1)S(1)}, u32[]{:S(2)}, u32[]{:S(2)}) collective-permute-start(bf16[192,512]{1,0:T(8,128)(2,1)S(1)} %get-tuple-element.47.w2), channel_id=1, source_target_pairs={{0,4},{4,0},{8,12},{12,8},{1,5},{5,1},{9,13},{13,9},{2,6},{6,2},{1... | collective-permute-start | bytes 589832 | tf_op jit(solution)/shard_map/ppermute | solution.py:457
  30.8 7.7 %collective-permute-start.13 = (bf16[256,512]{1,0:T(8,128)(2,1)S(1)}, bf16[256,512]{1,0:T(8,128)(2,1)S(1)}, u32[]{:S(2)}, u32[]{:S(2)}) collective-permute-start(bf16[256,512]{1,0:T(8,128)(2,1)S(1)} %shard_map.233.after.mine), channel_id=1, source_target_pairs={{0,2},{1,3},{2,0},{3,1},{4,6},{5,7},{6,4},{7,5},{8,10},{9,11},{10,... | collective-permute-start | bytes 786440 | tf_op jit(solution)/shard_map/ppermute | solution.py:444
  32.3 7.4 %collective-permute-start.21 = (bf16[256,512]{1,0:T(8,128)(2,1)S(1)}, bf16[256,512]{1,0:T(8,128)(2,1)S(1)}, u32[]{:S(2)}, u32[]{:S(2)}) collective-permute-start(bf16[256,512]{1,0:T(8,128)(2,1)S(1)} %get-tuple-element.50.first), channel_id=1, source_target_pairs={{0,16},{16,0},{1,17},{17,1},{2,18},{18,2},{3,19},{19,3},{4,20},{20... | collective-permute-start | bytes 786440 | tf_op jit(solution)/shard_map/ppermute | solution.py:453
  32.8 3.8 %collective-permute-start.17 = (bf16[192,512]{1,0:T(8,128)(2,1)S(1)}, bf16[192,512]{1,0:T(8,128)(2,1)S(1)}, u32[]{:S(2)}, u32[]{:S(2)}) collective-permute-start(bf16[192,512]{1,0:T(8,128)(2,1)S(1)} %get-tuple-element.47.w2), channel_id=1, source_target_pairs={{0,1},{1,0},{2,3},{3,2},{4,5},{5,4},{6,7},{7,6},{8,9},{9,8},{10,11... | collective-permute-start | bytes 589832 | tf_op jit(solution)/shard_map/ppermute | solution.py:448
  36.7 1.8 %collective-permute-start.18 = (bf16[192,512]{1,0:T(8,128)(2,1)S(1)}, bf16[192,512]{1,0:T(8,128)(2,1)S(1)}, u32[]{:S(2)}, u32[]{:S(2)}) collective-permute-start(bf16[192,512]{1,0:T(8,128)(2,1)S(1)} %collective-permute-done.16.w3), channel_id=1, source_target_pairs={{0,1},{1,0},{2,3},{3,2},{4,5},{5,4},{6,7},{7,6},{8,9},{9,8},{10,11... | collective-permute-start | bytes 589832 | tf_op jit(solution)/shard_map/ppermute | solution.py:448
  38.5 12.0 %copy-start.16 = (s32[2,2048]{1,0:T(2,128)S(1)}, s32[2,2048]{1,0:T(2,128)}, u32[]{:S(2)}) copy-start(s32[2,2048]{1,0:T(2,128)} %edges.5) | copy-start | bytes 49156
  39.8 10.6 %collective-permute-start.22 = (bf16[512,512]{1,0:T(8,128)(2,1)S(1)}, bf16[512,512]{1,0:T(8,128)(2,1)S(1)}, u32[]{:S(2)}, u32[]{:S(2)}) collective-permute-start(bf16[512,512]{1,0:T(8,128)(2,1)S(1)} %shard_map.236.pair), channel_id=1, source_target_pairs={{0,1},{1,0},{2,3},{3,2},{4,5},{5,4},{6,7},{7,6},{8,9},{9,8},{10,11... | collective-permute-start | bytes 1572872 | tf_op jit(solution)/shard_map/ppermute | solution.py:448
  39.9 10.6 %collective-permute-start.20 = (bf16[256,512]{1,0:T(8,128)(2,1)S(1)}, bf16[256,512]{1,0:T(8,128)(2,1)S(1)}, u32[]{:S(2)}, u32[]{:S(2)}) collective-permute-start(bf16[256,512]{1,0:T(8,128)(2,1)S(1)} %get-tuple-element.48.after.mine.middle), channel_id=1, source_target_pairs={{0,1},{1,0},{2,3},{3,2},{4,5},{5,4},{6,7},{7,6},{8,9},{9,8},{10,11... | collective-permute-start | bytes 786440 | tf_op jit(solution)/shard_map/ppermute | solution.py:448
  40.4 6.3 %collective-permute-start.23 = (bf16[32,512]{1,0:T(8,128)(2,1)S(1)}, bf16[32,512]{1,0:T(8,128)(2,1)S(1)}, u32[]{:S(2)}, u32[]{:S(2)}) collective-permute-start(bf16[32,512]{1,0:T(8,128)(2,1)S(1)} %get-tuple-element.55), channel_id=1, source_target_pairs={{0,4},{4,0},{8,12},{12,8},{1,5},{5,1},{9,13},{13,9},{2,6},{6,2},{1... | collective-permute-start | bytes 98312 | tf_op jit(solution)/shard_map/ppermute | solution.py:586
  41.7 6.5 %collective-permute-start.24 = (bf16[32,512]{1,0:T(8,128)(2,1)S(1)}, bf16[32,512]{1,0:T(8,128)(2,1)S(1)}, u32[]{:S(2)}, u32[]{:S(2)}) collective-permute-start(bf16[32,512]{1,0:T(8,128)(2,1)S(1)} %get-tuple-element.56), channel_id=1, source_target_pairs={{0,8},{4,12},{8,0},{12,4},{1,9},{5,13},{9,1},{13,5},{2,10},{6,14},... | collective-permute-start | bytes 98312 | tf_op jit(solution)/shard_map/ppermute | solution.py:586
  44.6 5.8 %collective-permute-start.25 = (bf16[32,512]{1,0:T(8,128)(2,1)S(1)}, bf16[32,512]{1,0:T(8,128)(2,1)S(1)}, u32[]{:S(2)}, u32[]{:S(2)}) collective-permute-start(bf16[32,512]{1,0:T(8,128)(2,1)S(1)} %get-tuple-element.57), channel_id=1, source_target_pairs={{4,8},{8,4},{5,9},{9,5},{6,10},{10,6},{7,11},{11,7},{20,24},{24,20... | collective-permute-start | bytes 98312 | tf_op jit(solution)/shard_map/ppermute | solution.py:586
  46.7 12.7 %collective-permute-start.30 = (bf16[384,512]{1,0:T(8,128)(2,1)S(1)}, bf16[384,512]{1,0:T(8,128)(2,1)S(1)}, u32[]{:S(2)}, u32[]{:S(2)}) collective-permute-start(bf16[384,512]{1,0:T(8,128)(2,1)S(1)} %get-tuple-element.62.w0), channel_id=1, source_target_pairs={{0,2},{1,3},{2,0},{3,1},{4,6},{5,7},{6,4},{7,5},{8,10},{9,11},{10,... | collective-permute-start | bytes 1179656 | tf_op jit(solution)/shard_map/ppermute | solution.py:444
  50.4 2.7 %collective-permute-start.26 = (bf16[96,512]{1,0:T(8,128)(2,1)S(1)}, bf16[96,512]{1,0:T(8,128)(2,1)S(1)}, u32[]{:S(2)}, u32[]{:S(2)}) collective-permute-start(bf16[96,512]{1,0:T(8,128)(2,1)S(1)} %shard_map.238.halo), channel_id=1, source_target_pairs={{0,1},{1,0},{2,3},{3,2},{4,5},{5,4},{6,7},{7,6},{8,9},{9,8},{10,11... | collective-permute-start | bytes 294920 | tf_op jit(solution)/shard_map/ppermute | solution.py:448
  50.5 2.6 %copy-start.21 = (f32[512]{0:T(512)S(1)}, f32[512]{0:T(512)}, u32[]{:S(2)}) copy-start(f32[512]{0:T(512)} %param.46) | copy-start | bytes 6148
  53.1 13.3 %copy-start.11 = (f32[512]{0:T(512)S(1)}, f32[512]{0:T(512)}, u32[]{:S(2)}) copy-start(f32[512]{0:T(512)} %param.47) | copy-start | bytes 6148
  58.8 1.7 %collective-permute-start.27 = (bf16[256,512]{1,0:T(8,128)(2,1)S(1)}, bf16[256,512]{1,0:T(8,128)(2,1)S(1)}, u32[]{:S(2)}, u32[]{:S(2)}) collective-permute-start(bf16[256,512]{1,0:T(8,128)(2,1)S(1)} %get-tuple-element.59), channel_id=1, source_target_pairs={{0,1},{1,0},{2,3},{3,2},{4,5},{5,4},{6,7},{7,6},{8,9},{9,8},{10,11... | collective-permute-start | bytes 786440 | tf_op jit(solution)/shard_map/ppermute | solution.py:448
  59.3 2.8 %collective-permute-start.29 = (bf16[384,512]{1,0:T(8,128)(2,1)S(1)}, bf16[384,512]{1,0:T(8,128)(2,1)S(1)}, u32[]{:S(2)}, u32[]{:S(2)}) collective-permute-start(bf16[384,512]{1,0:T(8,128)(2,1)S(1)} %get-tuple-element.62.w0), channel_id=1, source_target_pairs={{0,1},{1,0},{2,3},{3,2},{4,5},{5,4},{6,7},{7,6},{8,9},{9,8},{10,11... | collective-permute-start | bytes 1179656 | tf_op jit(solution)/shard_map/ppermute | solution.py:448
  59.4 2.7 %collective-permute-start.31 = (bf16[384,512]{1,0:T(8,128)(2,1)S(1)}, bf16[384,512]{1,0:T(8,128)(2,1)S(1)}, u32[]{:S(2)}, u32[]{:S(2)}) collective-permute-start(bf16[384,512]{1,0:T(8,128)(2,1)S(1)} %collective-permute-done.30.w2), channel_id=1, source_target_pairs={{0,1},{1,0},{2,3},{3,2},{4,5},{5,4},{6,7},{7,6},{8,9},{9,8},{10,11... | collective-permute-start | bytes 1179656 | tf_op jit(solution)/shard_map/ppermute | solution.py:448
  60.6 5.8 %collective-permute-start.28 = (bf16[128,512]{1,0:T(8,128)(2,1)S(1)}, bf16[128,512]{1,0:T(8,128)(2,1)S(1)}, u32[]{:S(2)}, u32[]{:S(2)}) collective-permute-start(bf16[128,512]{1,0:T(8,128)(2,1)S(1)} %get-tuple-element.61), channel_id=1, source_target_pairs={{0,2},{1,3},{2,0},{3,1},{4,6},{5,7},{6,4},{7,5},{8,10},{9,11},{10,... | collective-permute-start | bytes 393224 | tf_op jit(solution)/shard_map/ppermute | solution.py:444
